TPU v7x, 32 devices: a whole 2x2x4 slice. The times are simulated.
32 devices in a mesh: groups: 2 (over y), row: 4 (over x, core), col: 4 (over z).
Axes of the slice: x: 2, y: 2, z: 4, core: 2. Of those that a mesh axis runs over, the one named last changes fastest.
Arguments:
- inputs: bfloat16 [1536, 4096], P(('groups', 'col'), 'row'), parts along dimension 0, may hold values from -6 to 6
- cotangent: bfloat16 [1536, 4096], P(('groups', 'col'), 'row'), parts along dimension 0, may hold values from -6 to 6
- preactivation: bfloat16 [1536, 8192], P(('groups', 'row'), 'col'), parts along dimension 0, may hold values from -8 to 8
- up_weight: bfloat16 [4096, 8192], P('row', 'col'), may hold values from -0.09375 to 0.09375
- down_weight: bfloat16 [8192, 4096], P('col', 'row'), may hold values from -0.0625 to 0.0625
Outputs:
- grad_input: bfloat16 [1536, 4096], P(('groups', 'col'), 'row'), parts along dimension 0
- grad_up: float32 [8192, 8192], P(('groups', 'row'), 'col'), parts along dimension 0
- grad_down: float32 [16384, 4096], P(('groups', 'col'), 'row'), parts along dimension 0
There are 2 independent parts, one for each index of `groups`. A program takes and returns all parts, laid end to end along the dimension named above; an argument that names none is the same for every part. Nothing has to cross between parts.
All inputs are finite; a program needn't handle non-finite values.
Results may differ from a plain program's by a relative error of at most 0.0049.
Values may be sent and summed in bfloat16 or wider, within the bound.
No kernel may reach another device: no remote copies, remote signals or barrier semaphores. Data moves between devices by JAX's collectives and lax.ppermute only.
A program may use at most 128 MiB of HBM per device.

v0:
```python
import math

import jax
import jax.numpy as jnp
from jax import lax
from jax.sharding import PartitionSpec as P


def gelu_pair(values):
    v = values.astype(jnp.float32)
    tanh_arg = 0.7978845608 * (v + 0.044715 * v * v * v)
    tanh_val = jnp.tanh(tanh_arg)
    gelu_value = 0.5 * v * (1.0 + tanh_val)
    gelu_slope = 0.5 * (1.0 + tanh_val) + 0.5 * v * (1.0 - tanh_val * tanh_val) * 0.7978845608 * (
        1.0 + 3.0 * 0.044715 * v * v
    )
    return (gelu_value, gelu_slope)


def per_device(inputs, cotangent, preactivation, up_weight, down_weight):
    inputs_all, cotangent_all = (
        lax.all_gather(inputs, "col", axis=0, tiled=True),
        lax.all_gather(cotangent, "col", axis=0, tiled=True),
    )
    total_tokens = inputs_all.shape[0]
    token_scale = 1.0 / math.sqrt(total_tokens)
    last_dims = (((1,), (1,)), ((), ()))
    first_dims = (((0,), (0,)), ((), ()))
    piece = cotangent_all
    hidden_grad = lax.psum_scatter(
        lax.dot_general(piece, down_weight, last_dims, preferred_element_type=jnp.float32),
        "row",
        scatter_dimension=0,
        tiled=True,
    )
    gelu_value, gelu_slope = gelu_pair(preactivation)
    activation = gelu_value.astype(jnp.bfloat16)
    pre_grad = (hidden_grad * gelu_slope).astype(jnp.bfloat16)
    activation_all, pre_grad_all = (
        lax.all_gather(activation, "row", axis=0, tiled=True),
        lax.all_gather(pre_grad, "row", axis=0, tiled=True),
    )
    piece = pre_grad_all
    grad_input = lax.psum_scatter(
        lax.dot_general(piece, up_weight, last_dims, preferred_element_type=jnp.float32),
        "col",
        scatter_dimension=0,
        tiled=True,
    ).astype(jnp.bfloat16)
    grad_up = (
        lax.dot_general(inputs_all, pre_grad_all, first_dims, preferred_element_type=jnp.float32)
        * token_scale
    )
    grad_down = (
        lax.dot_general(
            activation_all, cotangent_all, first_dims, preferred_element_type=jnp.float32
        )
        * token_scale
    )
    return (grad_input, grad_up, grad_down)


def solution(mesh):
    placed = (
        P(("groups", "col"), "row"),
        P(("groups", "col"), "row"),
        P(("groups", "row"), "col"),
        P("row", "col"),
        P("col", "row"),
    )
    return jax.shard_map(
        per_device,
        mesh=mesh,
        in_specs=placed,
        out_specs=(
            P(("groups", "col"), "row"),
            P(("groups", "row"), "col"),
            P(("groups", "col"), "row"),
        ),
        check_vma=False,
    )
```

profile of v0, /device:TPU:0, one launch (start us, length us, event | category | flops | bytes accessed | tf_op | source)
XLA Modules:
  0.0 286.9 jit_solution(9059382792913873849)
XLA Ops:
  7.2 0.0 all-gather.5.cloned.1.call-start
  7.2 0.7 all-gather.5.cloned.1.call-update
  7.9 0.0 reduce-scatter.3.cloned.1.call-start
  7.9 41.4 %all-gather.5.cloned.1.call-done = bf16[768,1024]{1,0:T(8,128)(2,1)} async-done(((bf16[192,1024]{1,0:T(8,128)(2,1)}), bf16[768,1024]{1,0:T(8,128)(2,1)}) %all-gather.5.cloned.1.call-update) | async-done | bytes 1572880 | tf_op jit(solution)/shard_map/all_gather | solution.py:23
  49.4 8.8 %fusion.11 = f32[768,2048]{1,0:T(8,128)} fusion(bf16[768,1024]{1,0:T(8,128)(2,1)} %all-gather.5.cloned.1.call-done, bf16[2048,1024]{1,0:T(8,128)(2,1)} %param.9), kind=kOutput, calls=%fused_computation.20 | convolution fusion | flops 3221225472 | bytes 12058624 | tf_op jit(solution)/shard_map/dot_general | solution.py:31
  58.2 0.0 copy-start
  58.2 0.0 reduce-scatter.3.cloned.1.call-update
  58.2 0.0 all-gather.7.cloned.1.call-start
  58.3 57.3 %reduce-scatter.3.cloned.1.call-done = f32[192,2048]{1,0:T(8,128)} async-done(((f32[768,2048]{1,0:T(8,128)}), f32[192,2048]{1,0:T(8,128)}) %reduce-scatter.3.cloned.1.call-update) | async-done | bytes 1572880 | tf_op jit(solution)/shard_map/reduce_scatter | solution.py:30
  115.6 0.0 copy-done
  115.6 3.7 %fusion.7 = (bf16[192,2048]{1,0:T(8,128)(2,1)}, bf16[192,2048]{1,0:T(8,128)(2,1)}) fusion(bf16[192,2048]{1,0:T(8,128)(2,1)S(1)} %copy-done, f32[192,2048]{1,0:T(8,128)} %reduce-scatter.3.cloned.1.call-done), kind=kLoop, calls=%fused_computation.16 | loop fusion | flops 8650752 | bytes 3932160 | tf_op jit(solution)/shard_map/convert_element_type | solution.py:37
  119.3 0.0 all-gather.7.cloned.1.call-update
  119.3 0.0 all-gather.9.cloned.1.call-start
  119.4 0.5 all-gather.9.cloned.1.call-update
  119.9 0.0 all-gather.11.cloned.1.call-start
  119.9 0.5 all-gather.11.cloned.1.call-update
  120.5 0.0 reduce-scatter.5.cloned.1.call-start
  120.5 27.5 %all-gather.7.cloned.1.call-done = bf16[768,2048]{1,0:T(8,128)(2,1)} async-done(((bf16[192,2048]{1,0:T(8,128)(2,1)}), bf16[768,2048]{1,0:T(8,128)(2,1)}) %all-gather.7.cloned.1.call-update) | async-done | bytes 3145744 | tf_op jit(solution)/shard_map/all_gather | solution.py:41
  148.0 8.3 %fusion.12 = f32[768,1024]{1,0:T(8,128)} fusion(bf16[768,2048]{1,0:T(8,128)(2,1)} %all-gather.7.cloned.1.call-done, bf16[1024,2048]{1,0:T(8,128)(2,1)} %param.8), kind=kOutput, calls=%fused_computation.21 | convolution fusion | flops 3221225472 | bytes 10485760 | tf_op jit(solution)/shard_map/dot_general | solution.py:45
  156.3 0.0 copy-start.1
  156.3 0.0 reduce-scatter.5.cloned.1.call-update
  156.3 30.3 %all-gather.9.cloned.1.call-done = bf16[768,1024]{1,0:T(8,128)(2,1)} async-done(((bf16[192,1024]{1,0:T(8,128)(2,1)}), bf16[768,1024]{1,0:T(8,128)(2,1)}) %all-gather.9.cloned.1.call-update) | async-done | bytes 1572880 | tf_op jit(solution)/shard_map/all_gather | solution.py:22
  186.6 0.0 copy-done.1
  186.6 7.1 %multiply_bitcast_fusion = f32[1024,2048]{0,1:T(8,128)} fusion(bf16[768,2048]{1,0:T(8,128)(2,1)S(1)} %copy-done.1, bf16[768,1024]{1,0:T(8,128)(2,1)} %all-gather.9.cloned.1.call-done), kind=kOutput, calls=%fused_computation | convolution fusion | flops 3223322624 | bytes 13107200 | tf_op jit(solution)/shard_map/dot_general | solution.py:51
  193.8 0.0 copy-start.2
  193.8 9.4 %copy.8 = f32[1024,2048]{1,0:T(8,128)} copy(f32[1024,2048]{0,1:T(8,128)} %multiply_bitcast_fusion) | data formatting | bytes 16777216
  203.2 12.4 %all-gather.11.cloned.1.call-done = bf16[768,2048]{1,0:T(8,128)(2,1)} async-done(((bf16[192,2048]{1,0:T(8,128)(2,1)}), bf16[768,2048]{1,0:T(8,128)(2,1)}) %all-gather.11.cloned.1.call-update) | async-done | bytes 3145744 | tf_op jit(solution)/shard_map/all_gather | solution.py:40
  215.5 0.0 copy-done.2
  215.6 7.6 %convolution_multiply_fusion = f32[2048,1024]{1,0:T(8,128)} fusion(bf16[768,2048]{1,0:T(8,128)(2,1)} %all-gather.11.cloned.1.call-done, bf16[768,1024]{1,0:T(8,128)(2,1)S(1)} %copy-done.2), kind=kOutput, calls=%fused_computation.1 | convolution fusion | flops 3223322624 | bytes 13107200 | tf_op jit(solution)/shard_map/dot_general | solution.py:55
  223.2 55.0 %reduce-scatter.5.cloned.1.call-done = f32[192,1024]{1,0:T(8,128)} async-done(((f32[768,1024]{1,0:T(8,128)}), f32[192,1024]{1,0:T(8,128)}) %reduce-scatter.5.cloned.1.call-update) | async-done | bytes 786448 | tf_op jit(solution)/shard_map/reduce_scatter | solution.py:44
  278.1 1.9 convert_element_type.14
Async XLA Ops:
  7.2 42.2 %all-gather.5.cloned.1.call-start = ((), (), s32[]{:S(2)}) async-start(), calls=%async_computation.2 | async-start | bytes 1966080 | tf_op jit(solution)/shard_map/all_gather | solution.py:23
  7.9 107.7 %reduce-scatter.3.cloned.1.call-start = ((), (), s32[]{:S(2)}) async-start(), calls=%async_computation.3 | async-start | bytes 7864320 | tf_op jit(solution)/shard_map/reduce_scatter | solution.py:30
  58.2 57.4 %copy-start = (bf16[192,2048]{1,0:T(8,128)(2,1)S(1)}, bf16[192,2048]{1,0:T(8,128)(2,1)}, u32[]{:S(2)}) copy-start(bf16[192,2048]{1,0:T(8,128)(2,1)} %param.7) | copy-start | bytes 2359300
  58.2 89.8 %all-gather.7.cloned.1.call-start = ((), (), s32[]{:S(2)}) async-start(), calls=%async_computation.4 | async-start | bytes 3932160 | tf_op jit(solution)/shard_map/all_gather | solution.py:41
  119.3 67.3 %all-gather.9.cloned.1.call-start = ((), (), s32[]{:S(2)}) async-start(), calls=%async_computation.6 | async-start | bytes 1966080 | tf_op jit(solution)/shard_map/all_gather | solution.py:22
  119.9 95.7 %all-gather.11.cloned.1.call-start = ((), (), s32[]{:S(2)}) async-start(), calls=%async_computation.7 | async-start | bytes 3932160 | tf_op jit(solution)/shard_map/all_gather | solution.py:40
  120.5 157.6 %reduce-scatter.5.cloned.1.call-start = ((), (), s32[]{:S(2)}) async-start(), calls=%async_computation.5 | async-start | bytes 3932160 | tf_op jit(solution)/shard_map/reduce_scatter | solution.py:44
  156.3 30.4 %copy-start.1 = (bf16[768,2048]{1,0:T(8,128)(2,1)S(1)}, bf16[768,2048]{1,0:T(8,128)(2,1)}, u32[]{:S(2)}) copy-start(bf16[768,2048]{1,0:T(8,128)(2,1)} %all-gather.7.cloned.1.call-done) | copy-start | bytes 9437188
  193.8 21.8 %copy-start.2 = (bf16[768,1024]{1,0:T(8,128)(2,1)S(1)}, bf16[768,1024]{1,0:T(8,128)(2,1)}, u32[]{:S(2)}) copy-start(bf16[768,1024]{1,0:T(8,128)(2,1)} %all-gather.5.cloned.1.call-done) | copy-start | bytes 4718596
Sparse Core Ops, SparseCore 0:
  9.6 39.7 all-gather.4
  58.4 57.1 reduce-scatter.2
  119.4 28.5 all-gather.6
  149.5 37.0 all-gather.8
  188.1 27.3 all-gather.10
  217.8 60.2 reduce-scatter.4
where the time goes:
time: 287 us
  waiting for transfers between devices  226 us (79%)
  matrix products  31.8 us (11%)
  between operations  14.1 us (5%)
  local copies, waits for them, and re-layouts  9.43 us (3%)
  other arithmetic  5.61 us (2%)
    reduce_scatter x1, waiting for transfers between devices, per_device(): lax.psum_scatter(lax.dot_general(piece, down_weight, last_dims, preferred...  57.3 us
    reduce_scatter x1, waiting for transfers between devices, per_device(): lax.psum_scatter(lax.dot_general(piece, up_weight, last_dims, preferred_e...  55 us
    all_gather x1, waiting for transfers between devices, per_device(): lax.all_gather(cotangent, 'col', axis=0, tiled=True)  41.4 us
    all_gather x1, waiting for transfers between devices, per_device(): lax.all_gather(inputs, 'col', axis=0, tiled=True)  30.3 us
    all_gather x1, waiting for transfers between devices, per_device(): lax.all_gather(pre_grad, 'row', axis=0, tiled=True)  27.5 us
    all_gather x1, waiting for transfers between devices, per_device(): lax.all_gather(activation, 'row', axis=0, tiled=True)  12.4 us
    unnamed x7, local copies, waits for them, and re-layouts  9.43 us
    dot_general x1, matrix products, per_device(): lax.dot_general(piece, down_weight, last_dims, preferred_element_type=jnp...  8.82 us
  transfers between devices with their start and end apart: 6, of which 6 were waited for; matrix products, arithmetic and copies ran while one was open for 11% of the time, Pallas kernels for 0%

commit v1 on v0

v1 whole, which is shorter than its diff:
```python
import math

import jax
import jax.numpy as jnp
from jax import lax
from jax.sharding import PartitionSpec as P

LAST = (((1,), (1,)), ((), ()))
FIRST = (((0,), (0,)), ((), ()))


def gelu_parts(values):
    v = values.astype(jnp.float32)
    tanh_val = jnp.tanh(0.7978845608 * (v + 0.044715 * v * v * v))
    return v, tanh_val


def gelu(values):
    v, tanh_val = gelu_parts(values)
    return 0.5 * v * (1.0 + tanh_val)


def gelu_slope(values):
    v, tanh_val = gelu_parts(values)
    return 0.5 * (1.0 + tanh_val) + 0.5 * v * (1.0 - tanh_val * tanh_val) * 0.7978845608 * (
        1.0 + 3.0 * 0.044715 * v * v
    )


def dot(a, b, dims):
    return lax.dot_general(a, b, dims, preferred_element_type=jnp.float32)


def per_device(inputs, cotangent, preactivation, up_weight, down_weight):
    cols, rows = lax.axis_size("col"), lax.axis_size("row")
    z, r = lax.axis_index("col"), lax.axis_index("row")
    core = lax.rem(r, 2)
    tokens, features = cotangent.shape
    hidden = down_weight.shape[0]
    half = hidden // 2
    ring = [(i, (i + 1) % cols) for i in range(cols)]
    pair = [(i, i ^ 1) for i in range(rows)]
    total_tokens = tokens * cols
    token_scale = 1.0 / math.sqrt(total_tokens)

    pre_all = lax.all_gather(preactivation, "row", axis=0, tiled=True)

    down_mine = lax.dynamic_slice(down_weight, (core * half, 0), (half, features))
    down_other = lax.dynamic_slice(down_weight, ((1 - core) * half, 0), (half, features))
    down_pair = lax.ppermute(down_other, "row", pair)
    up_mine = lax.dynamic_slice(up_weight, (0, core * half), (features, half))
    up_other = lax.dynamic_slice(up_weight, (0, (1 - core) * half), (features, half))

    cots = [cotangent]
    for _ in range(cols - 1):
        cots.append(lax.ppermute(cots[-1], "col", ring))
    inputs_all = lax.all_gather(inputs, "col", axis=0, tiled=True)

    order = list(range(1, cols)) + [0]
    sums = None
    pre_grad_all = jnp.zeros((total_tokens, hidden), jnp.bfloat16)
    cot_all = jnp.zeros((total_tokens, features), jnp.bfloat16)
    for s in order:
        at = lax.rem(z - s + cols, cols) * tokens
        cot = cots[s]
        cot_all = lax.dynamic_update_slice(cot_all, cot, (at, 0))
        cot_pair = lax.ppermute(cot, "row", pair)
        part = dot(cot, down_mine, LAST) + dot(cot_pair, down_pair, LAST)
        sent = part.astype(jnp.bfloat16)
        for shift in range(2, rows, 2):
            part = part + lax.ppermute(
                sent, "row", [(i, (i + shift) % rows) for i in range(rows)]
            ).astype(jnp.float32)
        v = lax.dynamic_slice(pre_all, (at, core * half), (tokens, half))
        pre_grad = (part * gelu_slope(v)).astype(jnp.bfloat16)
        pre_grad_pair = lax.ppermute(pre_grad, "row", pair)
        pre_grad_all = lax.dynamic_update_slice(pre_grad_all, pre_grad, (at, core * half))
        pre_grad_all = lax.dynamic_update_slice(
            pre_grad_all, pre_grad_pair, (at, (1 - core) * half)
        )
        share = dot(pre_grad, up_mine, LAST) + dot(pre_grad_pair, up_other, LAST)
        if sums is not None:
            share = share + lax.ppermute(sums, "col", ring).astype(jnp.float32)
        sums = share.astype(jnp.bfloat16)
    activation = gelu(pre_all).astype(jnp.bfloat16)
    grad_down = dot(activation, cot_all, FIRST) * token_scale
    grad_up = dot(inputs_all, pre_grad_all, FIRST) * token_scale
    return (sums, grad_up, grad_down)


def solution(mesh):
    placed = (
        P(("groups", "col"), "row"),
        P(("groups", "col"), "row"),
        P(("groups", "row"), "col"),
        P("row", "col"),
        P("col", "row"),
    )
    return jax.shard_map(
        per_device,
        mesh=mesh,
        in_specs=placed,
        out_specs=(
            P(("groups", "col"), "row"),
            P(("groups", "row"), "col"),
            P(("groups", "col"), "row"),
        ),
        check_vma=False,
    )
```

time: 287 us -> 158 us (0.55)
  waiting for transfers between devices: 226 us -> 51.4 us
  local copies, waits for them, and re-layouts: 9.43 us -> 31.2 us
  starting transfers between devices: 0.24 us -> 12.9 us
  matrix products: 31.8 us -> 40.9 us
    reduce_scatter x2 -> x0, waiting for transfers between devices: 112 us -> none  [the longest x1 57.3 us: per_device(): lax.psum_scatter(lax.dot_general(piece, down_weight, last_dims, preferred...]
    all_gather x4 -> x2, waiting for transfers between devices: 112 us -> 0.02 us  [the longest x1 0.02 us: per_device(): inputs_all = lax.all_gather(inputs, 'col', axis=0, tiled=True)]
    ppermute x0 -> x19, waiting for transfers between devices: none -> 50.7 us  [the longest x3 29.8 us: per_device(): cots.append(lax.ppermute(cots[-1], 'col', ring))]
    dynamic_update_slice x0 -> x8, local copies, waits for them, and re-layouts: none -> 15.3 us  [the longest x4 15.2 us: per_device(): lax.dynamic_update_slice(pre_grad_all, pre_grad_pair, (at, (1 - core) * h...]
    ppermute x0 -> x19, starting transfers between devices: none -> 12.8 us  [the longest x4 5.05 us: per_device(): pre_grad_pair = lax.ppermute(pre_grad, 'row', pair)]
    dot_general x4 -> x18, matrix products: 31.8 us -> 40.9 us  [dot(): return lax.dot_general(a, b, dims, preferred_element_type=jnp.float32)]
    dynamic_update_slice x0 -> x4, other arithmetic: none -> 6.64 us  [per_device(): lax.dynamic_update_slice(pre_grad_all, pre_grad, (at, core * half))]
    convert_element_type x2 -> x0, other arithmetic: 5.61 us -> none  [the longest x1 3.67 us: per_device(): activation = gelu_value.astype(jnp.bfloat16)]
  transfers between devices with their start and end apart: 6 -> 21, of which waited for: 6 -> 7; matrix products, arithmetic and copies ran while one was open for 11% -> 46% of each run, Pallas kernels for 0% -> 0%
where the time goes in v1:
time: 158 us; the launch traced here: 157 us
  waiting for transfers between devices  51.4 us (33%)
  matrix products  40.9 us (26%)
  local copies, waits for them, and re-layouts  31.2 us (20%)
  between operations  14.4 us (9%)
  starting transfers between devices  12.9 us (8%)
  other arithmetic  6.64 us (4%)
    dot_general x18, matrix products, dot(): return lax.dot_general(a, b, dims, preferred_element_type=jnp.float32)  40.9 us
    ppermute x3, waiting for transfers between devices, per_device(): cots.append(lax.ppermute(cots[-1], 'col', ring))  29.8 us
    dynamic_update_slice x4, local copies, waits for them, and re-layouts, per_device(): lax.dynamic_update_slice(pre_grad_all, pre_grad_pair, (at, (1 - core) * h...  15.2 us
    unnamed x23, local copies, waits for them, and re-layouts  12.2 us
    ppermute x4, waiting for transfers between devices, per_device(): lax.ppermute(sent, 'row', [(i, (i + shift) % rows) for i in range(rows)])  11.2 us
    ppermute x3, waiting for transfers between devices, per_device(): share = share + lax.ppermute(sums, 'col', ring).astype(jnp.float32)  8.89 us
    dynamic_update_slice x4, other arithmetic, per_device(): lax.dynamic_update_slice(pre_grad_all, pre_grad, (at, core * half))  6.64 us
    ppermute x4, starting transfers between devices, per_device(): pre_grad_pair = lax.ppermute(pre_grad, 'row', pair)  5.05 us
  transfers between devices with their start and end apart: 21, of which 7 were waited for; matrix products, arithmetic and copies ran while one was open for 46% of the time, Pallas kernels for 0%

profile of v1, /device:TPU:0, one launch (start us, length us, event | category | flops | bytes accessed | tf_op | source)
XLA Modules:
  0.0 157.4 jit_solution(5135276442834647441)
XLA Ops:
  8.0 3.1 %constant_dynamic-slice_fusion = bf16[1024,1024]{1,0:T(8,128)(2,1)} fusion(bf16[2048,1024]{1,0:T(8,128)(2,1)} %param.9, s32[]{:T(128)S(6)} %select_n.13), kind=kLoop, calls=%fused_computation.138 | loop fusion | bytes 4194308 | tf_op jit(solution)/shard_map/dynamic_slice | solution.py:49
  11.5 2.6 %collective-permute-start.4 = (bf16[192,1024]{1,0:T(8,128)(2,1)S(1)}, bf16[192,1024]{1,0:T(8,128)(2,1)S(1)}, u32[]{:S(2)}, u32[]{:S(2)}) collective-permute-start(bf16[192,1024]{1,0:T(8,128)(2,1)S(1)} %copy-done.8), channel_id=1, source_target_pairs={{0,1},{1,2},{2,3},{3,0},{4,5},{5,6},{6,7},{7,4},{8,9},{9,10},{10,1... | collective-permute-start | bytes 1179656 | tf_op jit(solution)/shard_map/ppermute | solution.py:56
  14.4 11.5 %collective-permute-done.4 = bf16[192,1024]{1,0:T(8,128)(2,1)S(1)} collective-permute-done((bf16[192,1024]{1,0:T(8,128)(2,1)S(1)}, bf16[192,1024]{1,0:T(8,128)(2,1)S(1)}, u32[]{:S(2)}, u32[]{:S(2)}) %collective-permute-start.4) | collective-permute-done | bytes 393248 | tf_op jit(solution)/shard_map/ppermute | solution.py:56
  25.9 2.4 %fusion.32 = f32[1024,192]{0,1:T(8,128)S(1)} fusion(bf16[192,1024]{1,0:T(8,128)(2,1)S(1)} %copy-done.8, bf16[2048,1024]{1,0:T(8,128)(2,1)} %param.9, s32[]{:T(128)S(6)} %select_n.12), kind=kOutput, calls=%fused_computation.66 | convolution fusion | flops 402653184 | bytes 3276804 | tf_op jit(solution)/shard_map/dot_general | solution.py:31
  28.4 2.6 %fusion.26 = f32[1024,192]{0,1:T(8,128)S(1)} fusion(bf16[192,1024]{1,0:T(8,128)(2,1)S(1)} %collective-permute-done.4, bf16[2048,1024]{1,0:T(8,128)(2,1)} %param.9, s32[]{:T(128)S(6)} %select_n.12), kind=kOutput, calls=%fused_computation.60 | convolution fusion | flops 402653184 | bytes 3276804 | tf_op jit(solution)/shard_map/dot_general | solution.py:31
  31.0 7.6 %collective-permute-done.5 = bf16[192,1024]{1,0:T(8,128)(2,1)S(1)} collective-permute-done((bf16[192,1024]{1,0:T(8,128)(2,1)S(1)}, bf16[192,1024]{1,0:T(8,128)(2,1)S(1)}, u32[]{:S(2)}, u32[]{:S(2)}) %collective-permute-start.5) | collective-permute-done | bytes 393248 | tf_op jit(solution)/shard_map/ppermute | solution.py:56
  39.9 10.7 %collective-permute-done.6 = bf16[192,1024]{1,0:T(8,128)(2,1)S(1)} collective-permute-done((bf16[192,1024]{1,0:T(8,128)(2,1)S(1)}, bf16[192,1024]{1,0:T(8,128)(2,1)S(1)}, u32[]{:S(2)}, u32[]{:S(2)}) %collective-permute-start.6) | collective-permute-done | bytes 393248 | tf_op jit(solution)/shard_map/ppermute | solution.py:56
  52.2 1.9 %fusion.133 = (bf16[192,1024]{1,0:T(8,128)(2,1)}, f32[192,1024]{1,0:T(8,128)}) fusion(f32[1024,192]{0,1:T(8,128)S(1)} %fusion.30, bf16[1024,1024]{1,0:T(8,128)(2,1)S(1)} %collective-permute-done, bf16[192,1024]{1,0:T(8,128)(2,1)S(1)} %collective-permute-done.7), kind=kOutput, calls=%fused_computation.150 | convolution fusion | flops 403046400 | bytes 4456448 | tf_op jit(solution)/shard_map/dot_general | solution.py:31
  54.1 1.2 collective-permute-start.8
  55.3 1.7 %fusion.131 = (bf16[192,1024]{1,0:T(8,128)(2,1)S(1)}, f32[192,1024]{1,0:T(8,128)}) fusion(f32[1024,192]{0,1:T(8,128)S(1)} %fusion.26, bf16[1024,1024]{1,0:T(8,128)(2,1)S(1)} %collective-permute-done, bf16[192,1024]{1,0:T(8,128)(2,1)S(1)} %collective-permute-done.13), kind=kOutput, calls=%fused_computation.148 | convolution fusion | flops 403046400 | bytes 4456448 | tf_op jit(solution)/shard_map/dot_general | solution.py:31
  57.9 1.9 %fusion.134 = (bf16[192,1024]{1,0:T(8,128)(2,1)}, f32[192,1024]{1,0:T(8,128)}) fusion(f32[1024,192]{0,1:T(8,128)S(1)} %fusion.32, bf16[1024,1024]{1,0:T(8,128)(2,1)S(1)} %collective-permute-done, bf16[192,1024]{1,0:T(8,128)(2,1)S(1)} %collective-permute-done.1), kind=kOutput, calls=%fused_computation.151 | convolution fusion | flops 403046400 | bytes 4456448 | tf_op jit(solution)/shard_map/dot_general | solution.py:31
  61.0 1.8 %fusion.132 = (bf16[192,1024]{1,0:T(8,128)(2,1)S(1)}, f32[192,1024]{1,0:T(8,128)}) fusion(f32[1024,192]{0,1:T(8,128)S(1)} %fusion.28, bf16[1024,1024]{1,0:T(8,128)(2,1)S(1)} %collective-permute-done, bf16[192,1024]{1,0:T(8,128)(2,1)S(1)} %collective-permute-done.10), kind=kOutput, calls=%fused_computation.149 | convolution fusion | flops 403046400 | bytes 4456448 | tf_op jit(solution)/shard_map/dot_general | solution.py:31
  63.5 11.2 %collective-permute-done.14 = bf16[192,1024]{1,0:T(8,128)(2,1)S(1)} collective-permute-done((bf16[192,1024]{1,0:T(8,128)(2,1)S(1)}, bf16[192,1024]{1,0:T(8,128)(2,1)S(1)}, u32[]{:S(2)}, u32[]{:S(2)}) %collective-permute-start.14) | collective-permute-done | bytes 393248 | tf_op jit(solution)/shard_map/ppermute | solution.py:71
  75.9 1.5 copy-done.9
  77.4 1.8 %fusion.129 = (bf16[768,2048]{1,0:T(8,128)(2,1)S(1)}, bf16[192,1024]{1,0:T(8,128)(2,1)S(1)}) fusion(bf16[768,2048]{1,0:T(8,128)(2,1)S(1)} %broadcast_in_dim.6, s32[]{:T(128)S(6)} %select_n.17, s32[]{:T(128)S(6)} %select_n.12, bf16[768,2048]{1,0:T(8,128)(2,1)S(1)} %copy-done.9, f32[192,1024]{1,0:T(8,128)} %get-tuple-element.15, bf16[192,1024]{1,0:T(8,128)(2,1)} %copy-done.10), kind=kLoop, calls=%fused_computation.147 | loop fusion | flops 4325376 | bytes 2359304 | tf_op jit(solution)/shard_map/dynamic_update_slice | solution.py:77
  79.3 8.2 %convolution_multiply_fusion = f32[2048,1024]{1,0:T(8,128)} fusion(bf16[768,1024]{1,0:T(8,128)(2,1)} %copy-done.5, bf16[768,2048]{1,0:T(8,128)(2,1)S(1)} %copy-done.9), kind=kOutput, calls=%fused_computation.11 | convolution fusion | flops 3239051264 | bytes 13107200 | tf_op jit(solution)/shard_map/dot_general | solution.py:31
  87.5 3.4 %dynamic_update_slice.37 = bf16[768,2048]{1,0:T(8,128)(2,1)S(1)} dynamic-update-slice(bf16[768,2048]{1,0:T(8,128)(2,1)S(1)} %get-tuple-element.12, bf16[192,1024]{1,0:T(8,128)(2,1)S(1)} %collective-permute-done.15, s32[]{:T(128)S(6)} %select_n.17, s32[]{:T(128)S(6)} %select_n.13) | dynamic-update-slice | bytes 786436 | tf_op jit(solution)/shard_map/dynamic_update_slice | solution.py:78
  91.0 1.6 %fusion.127 = (bf16[768,2048]{1,0:T(8,128)(2,1)S(1)}, bf16[192,1024]{1,0:T(8,128)(2,1)S(1)}) fusion(bf16[768,2048]{1,0:T(8,128)(2,1)S(1)} %dynamic_update_slice.37, s32[]{:T(128)S(6)} %select_n.16, s32[]{:T(128)S(6)} %select_n.12, bf16[768,2048]{1,0:T(8,128)(2,1)S(1)} %copy-done.9, f32[192,1024]{1,0:T(8,128)S(1)} %copy-done.4, ...), kind=kLoop, calls=%fused_computation.146 | loop fusion | flops 4325376 | bytes 2359304 | tf_op jit(solution)/shard_map/dynamic_update_slice | solution.py:77
  92.6 1.9 %collective-permute-start.12 = (bf16[192,1024]{1,0:T(8,128)(2,1)S(1)}, bf16[192,1024]{1,0:T(8,128)(2,1)S(1)}, u32[]{:S(2)}, u32[]{:S(2)}) collective-permute-start(bf16[192,1024]{1,0:T(8,128)(2,1)S(1)} %get-tuple-element.11), channel_id=1, source_target_pairs={{0,4},{4,0},{8,12},{12,8},{1,5},{5,1},{9,13},{13,9},{2,6},{6,2},{1... | collective-permute-start | bytes 1179656 | tf_op jit(solution)/shard_map/ppermute | solution.py:76
  96.5 3.9 %dynamic_update_slice.39 = bf16[768,2048]{1,0:T(8,128)(2,1)S(1)} dynamic-update-slice(bf16[768,2048]{1,0:T(8,128)(2,1)S(1)} %get-tuple-element.10, bf16[192,1024]{1,0:T(8,128)(2,1)S(1)} %collective-permute-done.12, s32[]{:T(128)S(6)} %select_n.16, s32[]{:T(128)S(6)} %select_n.13) | dynamic-update-slice | bytes 786436 | tf_op jit(solution)/shard_map/dynamic_update_slice | solution.py:78
  100.4 1.6 %fusion.125 = (bf16[768,2048]{1,0:T(8,128)(2,1)S(1)}, bf16[192,1024]{1,0:T(8,128)(2,1)S(1)}) fusion(bf16[768,2048]{1,0:T(8,128)(2,1)S(1)} %dynamic_update_slice.39, s32[]{:T(128)S(6)} %select_n.15, s32[]{:T(128)S(6)} %select_n.12, bf16[768,2048]{1,0:T(8,128)(2,1)S(1)} %copy-done.9, f32[192,1024]{1,0:T(8,128)S(1)} %copy-done.3, ...), kind=kLoop, calls=%fused_computation.145 | loop fusion | flops 4325376 | bytes 2359304 | tf_op jit(solution)/shard_map/dynamic_update_slice | solution.py:77
  102.0 1.9 %collective-permute-start.9 = (bf16[192,1024]{1,0:T(8,128)(2,1)S(1)}, bf16[192,1024]{1,0:T(8,128)(2,1)S(1)}, u32[]{:S(2)}, u32[]{:S(2)}) collective-permute-start(bf16[192,1024]{1,0:T(8,128)(2,1)S(1)} %get-tuple-element.9), channel_id=1, source_target_pairs={{0,4},{4,0},{8,12},{12,8},{1,5},{5,1},{9,13},{13,9},{2,6},{6,2},{1... | collective-permute-start | bytes 1179656 | tf_op jit(solution)/shard_map/ppermute | solution.py:76
  104.8 4.4 %collective-permute-done.16 = bf16[192,1024]{1,0:T(8,128)(2,1)S(1)} collective-permute-done((bf16[192,1024]{1,0:T(8,128)(2,1)S(1)}, bf16[192,1024]{1,0:T(8,128)(2,1)S(1)}, u32[]{:S(2)}, u32[]{:S(2)}) %collective-permute-start.16) | collective-permute-done | bytes 393248 | tf_op jit(solution)/shard_map/ppermute | solution.py:83
  110.2 3.9 %dynamic_update_slice.41 = bf16[768,2048]{1,0:T(8,128)(2,1)S(1)} dynamic-update-slice(bf16[768,2048]{1,0:T(8,128)(2,1)S(1)} %get-tuple-element.8, bf16[192,1024]{1,0:T(8,128)(2,1)S(1)} %collective-permute-done.9, s32[]{:T(128)S(6)} %select_n.15, s32[]{:T(128)S(6)} %select_n.13) | dynamic-update-slice | bytes 786436 | tf_op jit(solution)/shard_map/dynamic_update_slice | solution.py:78
  114.2 1.6 %fusion.123 = (bf16[768,2048]{1,0:T(8,128)(2,1)S(1)}, bf16[192,1024]{1,0:T(8,128)(2,1)S(1)}) fusion(bf16[768,2048]{1,0:T(8,128)(2,1)S(1)} %dynamic_update_slice.41, s32[]{:T(128)S(6)} %select_n.14, s32[]{:T(128)S(6)} %select_n.12, bf16[768,2048]{1,0:T(8,128)(2,1)S(1)} %copy-done.9, f32[192,1024]{1,0:T(8,128)S(1)} %copy-done.2, ...), kind=kLoop, calls=%fused_computation.144 | loop fusion | flops 4325376 | bytes 2359304 | tf_op jit(solution)/shard_map/dynamic_update_slice | solution.py:77
  117.8 4.5 %collective-permute-done.17 = bf16[192,1024]{1,0:T(8,128)(2,1)S(1)} collective-permute-done((bf16[192,1024]{1,0:T(8,128)(2,1)S(1)}, bf16[192,1024]{1,0:T(8,128)(2,1)S(1)}, u32[]{:S(2)}, u32[]{:S(2)}) %collective-permute-start.17) | collective-permute-done | bytes 393248 | tf_op jit(solution)/shard_map/ppermute | solution.py:83
  122.2 1.6 %fusion.65 = bf16[192,1024]{1,0:T(8,128)(2,1)} fusion(f32[192,1024]{1,0:T(8,128)S(1)} %fusion.14, bf16[192,1024]{1,0:T(8,128)(2,1)S(1)} %get-tuple-element.9, bf16[1024,2048]{1,0:T(8,128)(2,1)S(1)} %copy-done, s32[]{:T(128)S(6)} %select_n.12, bf16[192,1024]{1,0:T(8,128)(2,1)S(1)} %collective-permute-done.17), kind=kOutput, calls=%fused_computation.85 | convolution fusion | flops 403439616 | bytes 4063236 | tf_op jit(solution)/shard_map/dot_general | solution.py:31
  124.6 3.9 %dynamic_update_slice.43 = bf16[768,2048]{1,0:T(8,128)(2,1)S(1)} dynamic-update-slice(bf16[768,2048]{1,0:T(8,128)(2,1)S(1)} %get-tuple-element.6, bf16[192,1024]{1,0:T(8,128)(2,1)S(1)} %collective-permute-done.3, s32[]{:T(128)S(6)} %select_n.14, s32[]{:T(128)S(6)} %select_n.13) | dynamic-update-slice | bytes 786436 | tf_op jit(solution)/shard_map/dynamic_update_slice | solution.py:78
  128.5 7.2 %multiply_bitcast_fusion = f32[1024,2048]{0,1:T(8,128)} fusion(bf16[768,2048]{1,0:T(8,128)(2,1)S(1)} %dynamic_update_slice.43, bf16[768,1024]{1,0:T(8,128)(2,1)} %all-gather.5.cloned.1.call-done), kind=kOutput, calls=%fused_computation.5 | convolution fusion | flops 3223322624 | bytes 13107200 | tf_op jit(solution)/shard_map/dot_general | solution.py:31
  135.7 9.2 %copy.8 = f32[1024,2048]{1,0:T(8,128)} copy(f32[1024,2048]{0,1:T(8,128)} %multiply_bitcast_fusion) | data formatting | bytes 16777216
  144.8 2.4 %fusion.16 = f32[192,1024]{1,0:T(8,128)S(1)} fusion(bf16[192,1024]{1,0:T(8,128)(2,1)S(1)} %copy-done.7, bf16[1024,2048]{1,0:T(8,128)(2,1)} %param.8, s32[]{:T(128)S(6)} %select_n.13), kind=kOutput, calls=%fused_computation.50 | convolution fusion | flops 402653184 | bytes 3276804 | tf_op jit(solution)/shard_map/dot_general | solution.py:31
  147.3 3.2 %fusion.68 = bf16[192,1024]{1,0:T(8,128)(2,1)} fusion(f32[192,1024]{1,0:T(8,128)S(1)} %fusion.16, bf16[192,1024]{1,0:T(8,128)(2,1)S(1)} %get-tuple-element.7, bf16[1024,2048]{1,0:T(8,128)(2,1)} %param.8, s32[]{:T(128)S(6)} %select_n.12, bf16[192,1024]{1,0:T(8,128)(2,1)} %collective-permute-done.18), kind=kOutput, calls=%fused_computation.86 | convolution fusion | flops 403439616 | bytes 4063236 | tf_op jit(solution)/shard_map/dot_general | solution.py:31
  (68 shorter events, 14.9 us)
Async XLA Ops:
  7.2 4.3 %copy-start.8 = (bf16[192,1024]{1,0:T(8,128)(2,1)S(1)}, bf16[192,1024]{1,0:T(8,128)(2,1)}, u32[]{:S(2)}) copy-start(bf16[192,1024]{1,0:T(8,128)(2,1)} %param.6) | copy-start | bytes 1179652
  7.2 67.5 %all-gather.3.cloned.1.call-start = ((), (), s32[]{:S(2)}) async-start(), calls=%async_computation | async-start | bytes 3932160 | tf_op jit(solution)/shard_map/all_gather | solution.py:46
  7.9 120.6 %all-gather.5.cloned.1.call-start = ((), (), s32[]{:S(2)}) async-start(), calls=%async_computation.1 | async-start | bytes 1966080 | tf_op jit(solution)/shard_map/all_gather | solution.py:57
  11.0 41.2 %collective-permute-start = (bf16[1024,1024]{1,0:T(8,128)(2,1)}, bf16[1024,1024]{1,0:T(8,128)(2,1)S(1)}, u32[]{:S(2)}, u32[]{:S(2)}) collective-permute-start(bf16[1024,1024]{1,0:T(8,128)(2,1)} %constant_dynamic-slice_fusion), channel_id=1, source_target_pairs={{0,4},{4,0},{8,12},{12,8},{1,5},{5,1},{9,13},{13,9},{2,6},{6,2},{1... | collective-permute-start | bytes 6291464 | tf_op jit(solution)/shard_map/ppermute | solution.py:50
  11.5 14.4 %collective-permute-start.4 = (bf16[192,1024]{1,0:T(8,128)(2,1)S(1)}, bf16[192,1024]{1,0:T(8,128)(2,1)S(1)}, u32[]{:S(2)}, u32[]{:S(2)}) collective-permute-start(bf16[192,1024]{1,0:T(8,128)(2,1)S(1)} %copy-done.8), channel_id=1, source_target_pairs={{0,1},{1,2},{2,3},{3,0},{4,5},{5,6},{6,7},{7,4},{8,9},{9,10},{10,1... | collective-permute-start | bytes 1179656 | tf_op jit(solution)/shard_map/ppermute | solution.py:56
  14.1 43.8 %collective-permute-start.1 = (bf16[192,1024]{1,0:T(8,128)(2,1)S(1)}, bf16[192,1024]{1,0:T(8,128)(2,1)S(1)}, u32[]{:S(2)}, u32[]{:S(2)}) collective-permute-start(bf16[192,1024]{1,0:T(8,128)(2,1)S(1)} %copy-done.8), channel_id=1, source_target_pairs={{0,4},{4,0},{8,12},{12,8},{1,5},{5,1},{9,13},{13,9},{2,6},{6,2},{1... | collective-permute-start | bytes 1179656 | tf_op jit(solution)/shard_map/ppermute | solution.py:67
  25.9 12.7 %collective-permute-start.5 = (bf16[192,1024]{1,0:T(8,128)(2,1)S(1)}, bf16[192,1024]{1,0:T(8,128)(2,1)S(1)}, u32[]{:S(2)}, u32[]{:S(2)}) collective-permute-start(bf16[192,1024]{1,0:T(8,128)(2,1)S(1)} %collective-permute-done.4), channel_id=1, source_target_pairs={{0,1},{1,2},{2,3},{3,0},{4,5},{5,6},{6,7},{7,4},{8,9},{9,10},{10,1... | collective-permute-start | bytes 1179656 | tf_op jit(solution)/shard_map/ppermute | solution.py:56
  28.3 10.7 %copy-start.1 = (bf16[2048,1024]{1,0:T(8,128)(2,1)S(1)}, bf16[2048,1024]{1,0:T(8,128)(2,1)}, u32[]{:S(2)}) copy-start(bf16[2048,1024]{1,0:T(8,128)(2,1)} %param.9) | copy-start | bytes 12582916
  28.3 27.0 %collective-permute-start.13 = (bf16[192,1024]{1,0:T(8,128)(2,1)S(1)}, bf16[192,1024]{1,0:T(8,128)(2,1)S(1)}, u32[]{:S(2)}, u32[]{:S(2)}) collective-permute-start(bf16[192,1024]{1,0:T(8,128)(2,1)S(1)} %collective-permute-done.4), channel_id=1, source_target_pairs={{0,4},{4,0},{8,12},{12,8},{1,5},{5,1},{9,13},{13,9},{2,6},{6,2},{1... | collective-permute-start | bytes 1179656 | tf_op jit(solution)/shard_map/ppermute | solution.py:67
  38.6 11.9 %collective-permute-start.6 = (bf16[192,1024]{1,0:T(8,128)(2,1)S(1)}, bf16[192,1024]{1,0:T(8,128)(2,1)S(1)}, u32[]{:S(2)}, u32[]{:S(2)}) collective-permute-start(bf16[192,1024]{1,0:T(8,128)(2,1)S(1)} %collective-permute-done.5), channel_id=1, source_target_pairs={{0,1},{1,2},{2,3},{3,0},{4,5},{5,6},{6,7},{7,4},{8,9},{9,10},{10,1... | collective-permute-start | bytes 1179656 | tf_op jit(solution)/shard_map/ppermute | solution.py:56
  38.9 22.1 %collective-permute-start.10 = (bf16[192,1024]{1,0:T(8,128)(2,1)S(1)}, bf16[192,1024]{1,0:T(8,128)(2,1)S(1)}, u32[]{:S(2)}, u32[]{:S(2)}) collective-permute-start(bf16[192,1024]{1,0:T(8,128)(2,1)S(1)} %collective-permute-done.5), channel_id=1, source_target_pairs={{0,4},{4,0},{8,12},{12,8},{1,5},{5,1},{9,13},{13,9},{2,6},{6,2},{1... | collective-permute-start | bytes 1179656 | tf_op jit(solution)/shard_map/ppermute | solution.py:67
  50.5 1.7 %collective-permute-start.7 = (bf16[192,1024]{1,0:T(8,128)(2,1)S(1)}, bf16[192,1024]{1,0:T(8,128)(2,1)S(1)}, u32[]{:S(2)}, u32[]{:S(2)}) collective-permute-start(bf16[192,1024]{1,0:T(8,128)(2,1)S(1)} %collective-permute-done.6), channel_id=1, source_target_pairs={{0,4},{4,0},{8,12},{12,8},{1,5},{5,1},{9,13},{13,9},{2,6},{6,2},{1... | collective-permute-start | bytes 1179656 | tf_op jit(solution)/shard_map/ppermute | solution.py:67
  51.5 5.6 %copy-start.5 = (bf16[768,1024]{1,0:T(8,128)(2,1)}, bf16[768,1024]{1,0:T(8,128)(2,1)S(1)}, u32[]{:S(2)}) copy-start(bf16[768,1024]{1,0:T(8,128)(2,1)S(1)} %constant_dynamic-update-slice_fusion) | copy-start | bytes 4718596
  54.1 46.3 %collective-permute-start.8 = (bf16[192,1024]{1,0:T(8,128)(2,1)}, bf16[192,1024]{1,0:T(8,128)(2,1)}, u32[]{:S(2)}, u32[]{:S(2)}) collective-permute-start(bf16[192,1024]{1,0:T(8,128)(2,1)} %get-tuple-element.18), channel_id=1, source_target_pairs={{0,8},{4,12},{8,0},{12,4},{1,9},{5,13},{9,1},{13,5},{2,10},{6,14},... | collective-permute-start | bytes 1179656 | tf_op jit(solution)/shard_map/ppermute | solution.py:71
  57.1 17.7 %collective-permute-start.14 = (bf16[192,1024]{1,0:T(8,128)(2,1)S(1)}, bf16[192,1024]{1,0:T(8,128)(2,1)S(1)}, u32[]{:S(2)}, u32[]{:S(2)}) collective-permute-start(bf16[192,1024]{1,0:T(8,128)(2,1)S(1)} %get-tuple-element.14), channel_id=1, source_target_pairs={{0,8},{4,12},{8,0},{12,4},{1,9},{5,13},{9,1},{13,5},{2,10},{6,14},... | collective-permute-start | bytes 1179656 | tf_op jit(solution)/shard_map/ppermute | solution.py:71
  59.7 54.4 %collective-permute-start.2 = (bf16[192,1024]{1,0:T(8,128)(2,1)}, bf16[192,1024]{1,0:T(8,128)(2,1)}, u32[]{:S(2)}, u32[]{:S(2)}) collective-permute-start(bf16[192,1024]{1,0:T(8,128)(2,1)} %get-tuple-element.20), channel_id=1, source_target_pairs={{0,8},{4,12},{8,0},{12,4},{1,9},{5,13},{9,1},{13,5},{2,10},{6,14},... | collective-permute-start | bytes 1179656 | tf_op jit(solution)/shard_map/ppermute | solution.py:71
  62.7 28.2 %collective-permute-start.11 = (bf16[192,1024]{1,0:T(8,128)(2,1)S(1)}, bf16[192,1024]{1,0:T(8,128)(2,1)}, u32[]{:S(2)}, u32[]{:S(2)}) collective-permute-start(bf16[192,1024]{1,0:T(8,128)(2,1)S(1)} %get-tuple-element.16), channel_id=1, source_target_pairs={{0,8},{4,12},{8,0},{12,4},{1,9},{5,13},{9,1},{13,5},{2,10},{6,14},... | collective-permute-start | bytes 1179656 | tf_op jit(solution)/shard_map/ppermute | solution.py:71
  74.7 0.7 copy-start.10
  75.5 1.9 %copy-start.9 = (bf16[768,2048]{1,0:T(8,128)(2,1)S(1)}, bf16[768,2048]{1,0:T(8,128)(2,1)}, u32[]{:S(2)}) copy-start(bf16[768,2048]{1,0:T(8,128)(2,1)} %all-gather.3.cloned.1.call-done) | copy-start | bytes 9437188
  79.2 11.8 %copy-start.4 = (f32[192,1024]{1,0:T(8,128)S(1)}, f32[192,1024]{1,0:T(8,128)}, u32[]{:S(2)}) copy-start(f32[192,1024]{1,0:T(8,128)} %get-tuple-element.17) | copy-start | bytes 2359300
  79.2 8.3 %collective-permute-start.15 = (bf16[192,1024]{1,0:T(8,128)(2,1)S(1)}, bf16[192,1024]{1,0:T(8,128)(2,1)S(1)}, u32[]{:S(2)}, u32[]{:S(2)}) collective-permute-start(bf16[192,1024]{1,0:T(8,128)(2,1)S(1)} %get-tuple-element.13), channel_id=1, source_target_pairs={{0,4},{4,0},{8,12},{12,8},{1,5},{5,1},{9,13},{13,9},{2,6},{6,2},{1... | collective-permute-start | bytes 1179656 | tf_op jit(solution)/shard_map/ppermute | solution.py:76
  79.3 15.2 %copy-start = (bf16[1024,2048]{1,0:T(8,128)(2,1)S(1)}, bf16[1024,2048]{1,0:T(8,128)(2,1)}, u32[]{:S(2)}) copy-start(bf16[1024,2048]{1,0:T(8,128)(2,1)} %param.8) | copy-start | bytes 12582916
  92.6 7.9 %copy-start.3 = (f32[192,1024]{1,0:T(8,128)S(1)}, f32[192,1024]{1,0:T(8,128)}, u32[]{:S(2)}) copy-start(f32[192,1024]{1,0:T(8,128)} %get-tuple-element.19) | copy-start | bytes 2359300
  92.6 3.9 %collective-permute-start.12 = (bf16[192,1024]{1,0:T(8,128)(2,1)S(1)}, bf16[192,1024]{1,0:T(8,128)(2,1)S(1)}, u32[]{:S(2)}, u32[]{:S(2)}) collective-permute-start(bf16[192,1024]{1,0:T(8,128)(2,1)S(1)} %get-tuple-element.11), channel_id=1, source_target_pairs={{0,4},{4,0},{8,12},{12,8},{1,5},{5,1},{9,13},{13,9},{2,6},{6,2},{1... | collective-permute-start | bytes 1179656 | tf_op jit(solution)/shard_map/ppermute | solution.py:76
  96.2 13.1 %collective-permute-start.16 = (bf16[192,1024]{1,0:T(8,128)(2,1)S(1)}, bf16[192,1024]{1,0:T(8,128)(2,1)S(1)}, u32[]{:S(2)}, u32[]{:S(2)}) collective-permute-start(bf16[192,1024]{1,0:T(8,128)(2,1)S(1)} %fusion.59), channel_id=1, source_target_pairs={{0,1},{1,2},{2,3},{3,0},{4,5},{5,6},{6,7},{7,4},{8,9},{9,10},{10,1... | collective-permute-start | bytes 1179656 | tf_op jit(solution)/shard_map/ppermute | solution.py:83
  102.0 8.2 %collective-permute-start.9 = (bf16[192,1024]{1,0:T(8,128)(2,1)S(1)}, bf16[192,1024]{1,0:T(8,128)(2,1)S(1)}, u32[]{:S(2)}, u32[]{:S(2)}) collective-permute-start(bf16[192,1024]{1,0:T(8,128)(2,1)S(1)} %get-tuple-element.9), channel_id=1, source_target_pairs={{0,4},{4,0},{8,12},{12,8},{1,5},{5,1},{9,13},{13,9},{2,6},{6,2},{1... | collective-permute-start | bytes 1179656 | tf_op jit(solution)/shard_map/ppermute | solution.py:76
  104.8 9.4 %copy-start.2 = (f32[192,1024]{1,0:T(8,128)S(1)}, f32[192,1024]{1,0:T(8,128)}, u32[]{:S(2)}) copy-start(f32[192,1024]{1,0:T(8,128)} %get-tuple-element.21) | copy-start | bytes 2359300
  110.2 12.1 %collective-permute-start.17 = (bf16[192,1024]{1,0:T(8,128)(2,1)S(1)}, bf16[192,1024]{1,0:T(8,128)(2,1)S(1)}, u32[]{:S(2)}, u32[]{:S(2)}) collective-permute-start(bf16[192,1024]{1,0:T(8,128)(2,1)S(1)} %fusion.62), channel_id=1, source_target_pairs={{0,1},{1,2},{2,3},{3,0},{4,5},{5,6},{6,7},{7,4},{8,9},{9,10},{10,1... | collective-permute-start | bytes 1179656 | tf_op jit(solution)/shard_map/ppermute | solution.py:83
  115.8 8.0 %collective-permute-start.3 = (bf16[192,1024]{1,0:T(8,128)(2,1)S(1)}, bf16[192,1024]{1,0:T(8,128)(2,1)S(1)}, u32[]{:S(2)}, u32[]{:S(2)}) collective-permute-start(bf16[192,1024]{1,0:T(8,128)(2,1)S(1)} %get-tuple-element.7), channel_id=1, source_target_pairs={{0,4},{4,0},{8,12},{12,8},{1,5},{5,1},{9,13},{13,9},{2,6},{6,2},{1... | collective-permute-start | bytes 1179656 | tf_op jit(solution)/shard_map/ppermute | solution.py:76
  123.8 23.4 %collective-permute-start.18 = (bf16[192,1024]{1,0:T(8,128)(2,1)}, bf16[192,1024]{1,0:T(8,128)(2,1)}, u32[]{:S(2)}, u32[]{:S(2)}) collective-permute-start(bf16[192,1024]{1,0:T(8,128)(2,1)} %fusion.65), channel_id=1, source_target_pairs={{0,1},{1,2},{2,3},{3,0},{4,5},{5,6},{6,7},{7,4},{8,9},{9,10},{10,1... | collective-permute-start | bytes 1179656 | tf_op jit(solution)/shard_map/ppermute | solution.py:83
  123.9 0.7 copy-start.6
  135.7 9.2 %copy-start.7 = (bf16[192,1024]{1,0:T(8,128)(2,1)S(1)}, bf16[192,1024]{1,0:T(8,128)(2,1)}, u32[]{:S(2)}) copy-start(bf16[192,1024]{1,0:T(8,128)(2,1)} %copy-done.6) | copy-start | bytes 1179652
Sparse Core Ops, SparseCore 0:
  9.6 31.2 all-gather.2
  42.4 37.3 all-gather.4

commit v2 on v1

v2 whole, which is shorter than its diff:
```python
import functools
import math

import jax
import jax.numpy as jnp
from jax import lax
from jax.experimental import pallas as pl
from jax.experimental.pallas import tpu as pltpu
from jax.sharding import PartitionSpec as P

LAST = (((1,), (1,)), ((), ()))
FIRST = (((0,), (0,)), ((), ()))
MIB = 1024 * 1024


def gelu_parts(values):
    v = values.astype(jnp.float32)
    tanh_val = jnp.tanh(0.7978845608 * (v + 0.044715 * v * v * v))
    return v, tanh_val


def gelu(values):
    v, tanh_val = gelu_parts(values)
    return 0.5 * v * (1.0 + tanh_val)


def gelu_slope(values):
    v, tanh_val = gelu_parts(values)
    return 0.5 * (1.0 + tanh_val) + 0.5 * v * (1.0 - tanh_val * tanh_val) * 0.7978845608 * (
        1.0 + 3.0 * 0.044715 * v * v
    )


def dot(a, b, dims):
    return lax.dot_general(a, b, dims, preferred_element_type=jnp.float32)


def tile_of(extent):
    return next(t for t in (256, 128, extent) if extent % t == 0)


def in_vmem():
    return pl.BlockSpec(memory_space=pltpu.VMEM)


def grad_down_kernel(blocks, scale, at_ref, pre_ref, *refs):
    cot_refs, out_ref, cots = refs[:blocks], refs[blocks], refs[blocks + 1]
    tokens = cot_refs[0].shape[0]

    @pl.when(pl.program_id(0) == 0)
    def _():
        for s in range(blocks):
            cots[pl.ds(pl.multiple_of(at_ref[s] * tokens, tokens), tokens), :] = cot_refs[s][...]

    activation = gelu(pre_ref[...]).astype(jnp.bfloat16)
    out_ref[...] = dot(activation, cots[...], FIRST) * scale


def grad_down_call(at, pre_all, cots, scale):
    total, hidden = pre_all.shape
    features = cots[0].shape[1]
    tile = tile_of(hidden)
    return pl.pallas_call(
        functools.partial(grad_down_kernel, len(cots), scale),
        out_shape=jax.ShapeDtypeStruct((hidden, features), jnp.float32),
        grid_spec=pltpu.PrefetchScalarGridSpec(
            num_scalar_prefetch=1,
            grid=(hidden // tile,),
            in_specs=[pl.BlockSpec((total, tile), lambda i, at: (0, i))]
            + [in_vmem() for _ in cots],
            out_specs=pl.BlockSpec((tile, features), lambda i, at: (i, 0)),
            scratch_shapes=[pltpu.VMEM((total, features), jnp.bfloat16)],
        ),
        compiler_params=pltpu.CompilerParams(vmem_limit_bytes=24 * MIB),
        cost_estimate=pl.CostEstimate(
            flops=2 * total * hidden * features,
            bytes_accessed=4 * hidden * features + 2 * total * (hidden + features),
            transcendentals=total * hidden,
        ),
    )(at, pre_all, *cots)


def grad_up_kernel(blocks, scale, at_ref, in_ref, *refs):
    mine, pair = refs[:blocks], refs[blocks : 2 * blocks]
    out_ref, grads = refs[2 * blocks], refs[2 * blocks + 1]
    tokens, half = mine[0].shape

    @pl.when(pl.program_id(0) == 0)
    def _():
        core = at_ref[blocks]
        left = pl.ds(pl.multiple_of(core * half, half), half)
        right = pl.ds(pl.multiple_of((1 - core) * half, half), half)
        for s in range(blocks):
            here = pl.ds(pl.multiple_of(at_ref[s] * tokens, tokens), tokens)
            grads[here, left] = mine[s][...]
            grads[here, right] = pair[s][...]

    out_ref[...] = dot(in_ref[...], grads[...], FIRST) * scale


def grad_up_call(at, inputs_all, mine, pair, scale):
    total, features = inputs_all.shape
    hidden = 2 * mine[0].shape[1]
    tile = tile_of(features)
    return pl.pallas_call(
        functools.partial(grad_up_kernel, len(mine), scale),
        out_shape=jax.ShapeDtypeStruct((features, hidden), jnp.float32),
        grid_spec=pltpu.PrefetchScalarGridSpec(
            num_scalar_prefetch=1,
            grid=(features // tile,),
            in_specs=[pl.BlockSpec((total, tile), lambda i, at: (0, i))]
            + [in_vmem() for _ in mine + pair],
            out_specs=pl.BlockSpec((tile, hidden), lambda i, at: (i, 0)),
            scratch_shapes=[pltpu.VMEM((total, hidden), jnp.bfloat16)],
        ),
        compiler_params=pltpu.CompilerParams(vmem_limit_bytes=24 * MIB),
        cost_estimate=pl.CostEstimate(
            flops=2 * total * hidden * features,
            bytes_accessed=4 * hidden * features + 2 * total * (hidden + features),
            transcendentals=0,
        ),
    )(at, inputs_all, *mine, *pair)


def pre_grad_kernel(at_ref, pre_ref, part_ref, *refs):
    out_ref = refs[-1]
    rows = 64
    for first in range(0, part_ref.shape[0], rows):
        here = pl.ds(first, rows)
        total = part_ref[here, :]
        for other in refs[:-1]:
            total = total + other[here, :].astype(jnp.float32)
        out_ref[here, :] = (total * gelu_slope(pre_ref[here, :])).astype(jnp.bfloat16)


def pre_grad_call(at, core, pre_all, part, others):
    tokens, half = part.shape
    return pl.pallas_call(
        pre_grad_kernel,
        out_shape=jax.ShapeDtypeStruct((tokens, half), jnp.bfloat16),
        grid_spec=pltpu.PrefetchScalarGridSpec(
            num_scalar_prefetch=1,
            grid=(1,),
            in_specs=[pl.BlockSpec((tokens, half), lambda i, at: (at[0], at[1]))]
            + [in_vmem() for _ in [part] + others],
            out_specs=in_vmem(),
        ),
        compiler_params=pltpu.CompilerParams(vmem_limit_bytes=8 * MIB),
        cost_estimate=pl.CostEstimate(
            flops=20 * tokens * half,
            bytes_accessed=10 * tokens * half,
            transcendentals=tokens * half,
        ),
    )(jnp.stack([at, core]).astype(jnp.int32), pre_all, part, *others)


def per_device(inputs, cotangent, preactivation, up_weight, down_weight):
    cols, rows = lax.axis_size("col"), lax.axis_size("row")
    z, r = lax.axis_index("col"), lax.axis_index("row")
    core = lax.rem(r, 2)
    tokens, features = cotangent.shape
    hidden = down_weight.shape[0]
    half = hidden // 2
    ring = [(i, (i + 1) % cols) for i in range(cols)]
    pair = [(i, i ^ 1) for i in range(rows)]
    scale = 1.0 / math.sqrt(tokens * cols)
    at = jnp.stack([lax.rem(z - s + cols, cols) for s in range(cols)] + [core]).astype(jnp.int32)

    pre_all = lax.all_gather(preactivation, "row", axis=0, tiled=True)

    down_mine = lax.dynamic_slice(down_weight, (core * half, 0), (half, features))
    down_other = lax.dynamic_slice(down_weight, ((1 - core) * half, 0), (half, features))
    up_mine = lax.dynamic_slice(up_weight, (0, core * half), (features, half))
    up_other = lax.dynamic_slice(up_weight, (0, (1 - core) * half), (features, half))

    cots, parts, sent = [cotangent], [None] * cols, [None] * cols

    def hidden_part(s):
        cot_pair = lax.ppermute(cots[s], "row", pair)
        parts[s] = dot(cots[s], down_mine, LAST) + dot(cot_pair, down_pair, LAST)
        sent[s] = parts[s].astype(jnp.bfloat16)

    arriving = lax.ppermute(cotangent, "col", ring)
    down_pair = lax.ppermute(down_other, "row", pair)
    for s in range(cols):
        hidden_part(s)
        if s < cols - 1:
            arriving, _ = lax.optimization_barrier((arriving, sent[s]))
            cots.append(arriving)
        if s < cols - 2:
            arriving = lax.ppermute(arriving, "col", ring)
    inputs_all = lax.all_gather(inputs, "col", axis=0, tiled=True)

    sums, mine, theirs = None, [None] * cols, [None] * cols
    for s in list(range(1, cols)) + [0]:
        others = [
            lax.ppermute(sent[s], "row", [(i, (i + shift) % rows) for i in range(rows)])
            for shift in range(2, rows, 2)
        ]
        mine[s] = pre_grad_call(at[s], core, pre_all, parts[s], others)
        theirs[s] = lax.ppermute(mine[s], "row", pair)
        share = dot(mine[s], up_mine, LAST) + dot(theirs[s], up_other, LAST)
        if sums is not None:
            share = share + lax.ppermute(sums, "col", ring).astype(jnp.float32)
        sums = share.astype(jnp.bfloat16)
    grad_down = grad_down_call(at, pre_all, cots, scale)
    grad_up = grad_up_call(at, inputs_all, mine, theirs, scale)
    return (sums, grad_up, grad_down)


def solution(mesh):
    placed = (
        P(("groups", "col"), "row"),
        P(("groups", "col"), "row"),
        P(("groups", "row"), "col"),
        P("row", "col"),
        P("col", "row"),
    )
    return jax.shard_map(
        per_device,
        mesh=mesh,
        in_specs=placed,
        out_specs=(
            P(("groups", "col"), "row"),
            P(("groups", "row"), "col"),
            P(("groups", "col"), "row"),
        ),
        check_vma=False,
    )
```

time: 158 us -> 135 us (0.85)
  Pallas kernels: 0 us -> 24.8 us
  local copies, waits for them, and re-layouts: 31.2 us -> 10.6 us
  matrix products: 40.9 us -> 22.6 us
  other arithmetic: 6.64 us -> 0.3 us
  starting transfers between devices: 12.9 us -> 8.68 us
  waiting for transfers between devices: 51.4 us -> 53 us
    pallas_call x0 -> x6, Pallas kernels: none -> 24.8 us  [the longest x1 8.8 us: grad_down_call(): pl.pallas_call(functools.partial(grad_down_kernel, len(cots), scale), out...]
    dot_general x18 -> x16, matrix products: 40.9 us -> 22.6 us  [dot(): return lax.dot_general(a, b, dims, preferred_element_type=jnp.float32)]
    dynamic_update_slice x8 -> x0, local copies, waits for them, and re-layouts: 15.3 us -> none  [the longest x4 15.2 us: per_device(): lax.dynamic_update_slice(pre_grad_all, pre_grad_pair, (at, (1 - core) * h...]
    dynamic_update_slice x4 -> x0, other arithmetic: 6.64 us -> none  [per_device(): lax.dynamic_update_slice(pre_grad_all, pre_grad, (at, core * half))]
    unnamed x23 -> x68, local copies, waits for them, and re-layouts: 12.2 us -> 7.41 us
    ppermute x15, starting transfers between devices: 12 us -> 7.86 us  [the longest x4 4.06 us: per_device(): lax.ppermute(sent[s], 'row', [(i, (i + shift) % rows) for i in range(rows)])]
  transfers between devices with their start and end apart: 21 -> 21, of which waited for: 7 -> 10; matrix products, arithmetic and copies ran while one was open for 46% -> 18% of each run, Pallas kernels for 0% -> 18%
where the time goes in v2:
time: 135 us
  waiting for transfers between devices  53 us (39%)
  Pallas kernels  24.8 us (18%)
  matrix products  22.6 us (17%)
  between operations  14.5 us (11%)
  local copies, waits for them, and re-layouts  10.6 us (8%)
  starting transfers between devices  8.68 us (6%)
    dot_general x16, matrix products, dot(): return lax.dot_general(a, b, dims, preferred_element_type=jnp.float32)  22.6 us
    ppermute x2, waiting for transfers between devices, per_device(): arriving = lax.ppermute(arriving, 'col', ring)  19.9 us
    ppermute x4, waiting for transfers between devices, per_device(): lax.ppermute(sent[s], 'row', [(i, (i + shift) % rows) for i in range(rows)])  13.9 us
    ppermute x3, waiting for transfers between devices, per_device(): share = share + lax.ppermute(sums, 'col', ring).astype(jnp.float32)  9.67 us
    pallas_call x1, Pallas kernels, grad_down_call(): pl.pallas_call(functools.partial(grad_down_kernel, len(cots), scale), out...  8.8 us
    pallas_call x4, Pallas kernels, pre_grad_call(): pl.pallas_call(pre_grad_kernel, out_shape=jax.ShapeDtypeStruct((tokens, h...  8.09 us
    pallas_call x1, Pallas kernels, grad_up_call(): pl.pallas_call(functools.partial(grad_up_kernel, len(mine), scale), out_s...  7.9 us
    unnamed x68, local copies, waits for them, and re-layouts  7.41 us
  transfers between devices with their start and end apart: 21, of which 10 were waited for; matrix products, arithmetic and copies ran while one was open for 18% of the time, Pallas kernels for 18%

profile of v2, /device:TPU:0, one launch (start us, length us, event | category | flops | bytes accessed | tf_op | source)
XLA Modules:
  0.0 134.5 jit_solution(7422282588940920619)
XLA Ops:
  8.0 3.1 %constant_dynamic-slice_fusion = bf16[1024,1024]{1,0:T(8,128)(2,1)} fusion(bf16[2048,1024]{1,0:T(8,128)(2,1)} %param.9, s32[]{:T(128)S(6)} %select_n.9), kind=kLoop, calls=%fused_computation.51 | loop fusion | bytes 4194308 | tf_op jit(solution)/shard_map/dynamic_slice | solution.py:172
  11.6 3.0 %collective-permute-start.4 = (bf16[192,1024]{1,0:T(8,128)(2,1)S(1)}, bf16[192,1024]{1,0:T(8,128)(2,1)S(1)}, u32[]{:S(2)}, u32[]{:S(2)}) collective-permute-start(bf16[192,1024]{1,0:T(8,128)(2,1)S(1)} %copy-done.17), channel_id=1, source_target_pairs={{0,1},{1,2},{2,3},{3,0},{4,5},{5,6},{6,7},{7,4},{8,9},{9,10},{10,1... | collective-permute-start | bytes 1179656 | tf_op jit(solution)/shard_map/ppermute | solution.py:183
  14.6 2.4 %fusion.22 = f32[1024,192]{0,1:T(8,128)S(1)} fusion(bf16[192,1024]{1,0:T(8,128)(2,1)S(1)} %copy-done.17, bf16[2048,1024]{1,0:T(8,128)(2,1)} %param.9, s32[]{:T(128)S(6)} %select_n.8), kind=kOutput, calls=%fused_computation.22 | convolution fusion | flops 402653184 | bytes 3276804 | tf_op jit(solution)/shard_map/dot_general | solution.py:35
  17.1 1.9 %fusion.79 = (bf16[192,1024]{1,0:T(8,128)(2,1)}, f32[192,1024]{1,0:T(8,128)}) fusion(f32[1024,192]{0,1:T(8,128)S(1)} %fusion.22, bf16[1024,1024]{1,0:T(8,128)(2,1)S(1)} %collective-permute-done, bf16[192,1024]{1,0:T(8,128)(2,1)S(1)} %collective-permute-done.1), kind=kOutput, calls=%fused_computation.57 | convolution fusion | flops 403046400 | bytes 4456448 | tf_op jit(solution)/shard_map/dot_general | solution.py:35
  19.0 7.0 %collective-permute-done.4.refs_1_ = bf16[192,1024]{1,0:T(8,128)(2,1)S(1)} collective-permute-done((bf16[192,1024]{1,0:T(8,128)(2,1)S(1)}, bf16[192,1024]{1,0:T(8,128)(2,1)S(1)}, u32[]{:S(2)}, u32[]{:S(2)}) %collective-permute-start.4) | collective-permute-done | bytes 393248 | tf_op jit(solution)/shard_map/ppermute | solution.py:183
  26.0 1.7 %collective-permute-done.6 = bf16[192,1024]{1,0:T(8,128)(2,1)S(1)} collective-permute-done((bf16[192,1024]{1,0:T(8,128)(2,1)S(1)}, bf16[192,1024]{1,0:T(8,128)(2,1)S(1)}, u32[]{:S(2)}, u32[]{:S(2)}) %collective-permute-start.6) | collective-permute-done | bytes 393248 | tf_op jit(solution)/shard_map/ppermute | solution.py:179
  28.5 0.9 fusion.80
  29.4 9.8 %collective-permute-done.5.refs_2_ = bf16[192,1024]{1,0:T(8,128)(2,1)S(1)} collective-permute-done((bf16[192,1024]{1,0:T(8,128)(2,1)S(1)}, bf16[192,1024]{1,0:T(8,128)(2,1)S(1)}, u32[]{:S(2)}, u32[]{:S(2)}) %collective-permute-start.5) | collective-permute-done | bytes 393248 | tf_op jit(solution)/shard_map/ppermute | solution.py:191
  39.3 1.5 %collective-permute-start.14 = (bf16[192,1024]{1,0:T(8,128)(2,1)S(1)}, bf16[192,1024]{1,0:T(8,128)(2,1)S(1)}, u32[]{:S(2)}, u32[]{:S(2)}) collective-permute-start(bf16[192,1024]{1,0:T(8,128)(2,1)S(1)} %get-tuple-element.11), channel_id=1, source_target_pairs={{0,8},{4,12},{8,0},{12,4},{1,9},{5,13},{9,1},{13,5},{2,10},{6,14},... | collective-permute-start | bytes 1179656 | tf_op jit(solution)/shard_map/ppermute | solution.py:197
  41.9 1.9 %fusion.81 = (bf16[192,1024]{1,0:T(8,128)(2,1)}, f32[192,1024]{1,0:T(8,128)}) fusion(f32[192,1024]{1,0:T(8,128)S(1)} %fusion.84, bf16[192,1024]{1,0:T(8,128)(2,1)S(1)} %collective-permute-done.5.refs_2_, bf16[2048,1024]{1,0:T(8,128)(2,1)S(1)} %copy-done.32, s32[]{:T(128)S(6)} %select_n.8), kind=kOutput, calls=%fused_computation.59 | convolution fusion | flops 403046400 | bytes 4456452 | tf_op jit(solution)/shard_map/dot_general | solution.py:35
  43.8 10.0 %collective-permute-done.7.refs_3_ = bf16[192,1024]{1,0:T(8,128)(2,1)S(1)} collective-permute-done((bf16[192,1024]{1,0:T(8,128)(2,1)S(1)}, bf16[192,1024]{1,0:T(8,128)(2,1)S(1)}, u32[]{:S(2)}, u32[]{:S(2)}) %collective-permute-start.7) | collective-permute-done | bytes 393248 | tf_op jit(solution)/shard_map/ppermute | solution.py:191
  54.5 1.5 %collective-permute-start.12 = (bf16[192,1024]{1,0:T(8,128)(2,1)}, bf16[192,1024]{1,0:T(8,128)(2,1)}, u32[]{:S(2)}, u32[]{:S(2)}) collective-permute-start(bf16[192,1024]{1,0:T(8,128)(2,1)} %get-tuple-element.13), channel_id=1, source_target_pairs={{0,8},{4,12},{8,0},{12,4},{1,9},{5,13},{9,1},{13,5},{2,10},{6,14},... | collective-permute-start | bytes 1179656 | tf_op jit(solution)/shard_map/ppermute | solution.py:197
  56.0 1.9 %copy-done = bf16[768,2048]{1,0:T(8,128)(2,1)S(1)} copy-done((bf16[768,2048]{1,0:T(8,128)(2,1)S(1)}, bf16[768,2048]{1,0:T(8,128)(2,1)}, u32[]{:S(2)}) %copy-start) | copy-done | bytes 3145752
  58.0 1.1 shard_map.79.refs_1_
  61.1 1.9 %fusion.82 = (bf16[192,1024]{1,0:T(8,128)(2,1)}, f32[192,1024]{1,0:T(8,128)}) fusion(f32[192,1024]{1,0:T(8,128)S(1)} %fusion.85, bf16[192,1024]{1,0:T(8,128)(2,1)S(1)} %collective-permute-done.7.refs_3_, bf16[2048,1024]{1,0:T(8,128)(2,1)S(1)} %copy-done.33, s32[]{:T(128)S(6)} %select_n.8), kind=kOutput, calls=%fused_computation.60 | convolution fusion | flops 403046400 | bytes 4456452 | tf_op jit(solution)/shard_map/dot_general | solution.py:35
  63.6 11.0 %collective-permute-done.12.refs_0_ = bf16[192,1024]{1,0:T(8,128)(2,1)} collective-permute-done((bf16[192,1024]{1,0:T(8,128)(2,1)}, bf16[192,1024]{1,0:T(8,128)(2,1)}, u32[]{:S(2)}, u32[]{:S(2)}) %collective-permute-start.12) | collective-permute-done | bytes 393248 | tf_op jit(solution)/shard_map/ppermute | solution.py:197
  74.7 2.4 %shard_map.78.refs_2_ = bf16[192,1024]{1,0:T(8,128)(2,1)S(1)} custom-call(s32[2]{0:T(128)S(1)} %pad_add_fusion.2.at_ref, bf16[768,2048]{1,0:T(8,128)(2,1)S(1)} %copy-done.1, f32[192,1024]{1,0:T(8,128)S(1)} %copy-done.8, bf16[192,1024]{1,0:T(8,128)(2,1)} %collective-permute-done.12.refs_0_), custom_call_target="tpu_custom_call" | custom-call | flops 3932160 | bytes 1966080 | tf_op jit(solution)/shard_map/pallas_call | solution.py:138
  78.0 1.6 %fusion.55 = bf16[192,1024]{1,0:T(8,128)(2,1)} fusion(f32[192,1024]{1,0:T(8,128)S(1)} %fusion, bf16[192,1024]{1,0:T(8,128)(2,1)S(1)} %shard_map.79.refs_1_, bf16[1024,2048]{1,0:T(8,128)(2,1)S(1)} %copy-done.26, s32[]{:T(128)S(6)} %select_n.8), kind=kOutput, calls=%fused_computation.36 | convolution fusion | flops 403046400 | bytes 3670020 | tf_op jit(solution)/shard_map/dot_general | solution.py:35
  79.9 2.8 %collective-permute-done.10.refs_0_ = bf16[192,1024]{1,0:T(8,128)(2,1)} collective-permute-done((bf16[192,1024]{1,0:T(8,128)(2,1)}, bf16[192,1024]{1,0:T(8,128)(2,1)}, u32[]{:S(2)}, u32[]{:S(2)}) %collective-permute-start.10) | collective-permute-done | bytes 393248 | tf_op jit(solution)/shard_map/ppermute | solution.py:197
  82.7 1.1 copy-done.9
  83.8 2.1 %shard_map.77.refs_3_ = bf16[192,1024]{1,0:T(8,128)(2,1)S(1)} custom-call(s32[2]{0:T(128)S(1)} %pad_add_fusion.1.at_ref, bf16[768,2048]{1,0:T(8,128)(2,1)S(1)} %copy-done.1, f32[192,1024]{1,0:T(8,128)S(1)} %copy-done.9, bf16[192,1024]{1,0:T(8,128)(2,1)} %collective-permute-done.10.refs_0_), custom_call_target="tpu_custom_call" | custom-call | flops 3932160 | bytes 1966080 | tf_op jit(solution)/shard_map/pallas_call | solution.py:138
  86.1 2.4 %shard_map.76.refs_0_ = bf16[192,1024]{1,0:T(8,128)(2,1)S(1)} custom-call(s32[2]{0:T(128)S(1)} %pad_add_fusion.at_ref, bf16[768,2048]{1,0:T(8,128)(2,1)S(1)} %copy-done.1, f32[192,1024]{1,0:T(8,128)S(1)} %copy-done.10, bf16[192,1024]{1,0:T(8,128)(2,1)} %collective-permute-done.2.refs_0_), custom_call_target="tpu_custom_call" | custom-call | flops 3932160 | bytes 1966080 | tf_op jit(solution)/shard_map/pallas_call | solution.py:138
  89.0 1.8 %fusion.2 = f32[192,1024]{1,0:T(8,128)S(1)} fusion(bf16[192,1024]{1,0:T(8,128)(2,1)} %collective-permute-done.13.refs_6_, bf16[1024,2048]{1,0:T(8,128)(2,1)S(1)} %copy-done.27, s32[]{:T(128)S(6)} %select_n.9), kind=kOutput, calls=%fused_computation.2 | convolution fusion | flops 402653184 | bytes 3276804 | tf_op jit(solution)/shard_map/dot_general | solution.py:35
  90.9 6.5 %collective-permute-done.16 = bf16[192,1024]{1,0:T(8,128)(2,1)} collective-permute-done((bf16[192,1024]{1,0:T(8,128)(2,1)}, bf16[192,1024]{1,0:T(8,128)(2,1)}, u32[]{:S(2)}, u32[]{:S(2)}) %collective-permute-start.16) | collective-permute-done | bytes 393248 | tf_op jit(solution)/shard_map/ppermute | solution.py:204
  97.4 1.9 %fusion.58 = bf16[192,1024]{1,0:T(8,128)(2,1)S(1)} fusion(f32[192,1024]{1,0:T(8,128)S(1)} %fusion.2, bf16[192,1024]{1,0:T(8,128)(2,1)S(1)} %shard_map.78.refs_2_, bf16[1024,2048]{1,0:T(8,128)(2,1)S(1)} %copy-done.27, s32[]{:T(128)S(6)} %select_n.8, bf16[192,1024]{1,0:T(8,128)(2,1)} %collective-permute-done.16), kind=kOutput, calls=%fused_computation.37 | convolution fusion | flops 403439616 | bytes 4063236 | tf_op jit(solution)/shard_map/dot_general | solution.py:35
  99.6 8.8 %shard_map.81 = f32[2048,1024]{1,0:T(8,128)} custom-call(s32[5]{0:T(128)S(1)} %stack.43.at_ref, bf16[768,2048]{1,0:T(8,128)(2,1)S(1)} %copy-done.1, bf16[192,1024]{1,0:T(8,128)(2,1)S(1)} %copy-done.18, bf16[192,1024]{1,0:T(8,128)(2,1)S(1)} %copy-done.12, bf16[192,1024]{1,0:T(8,128)(2,1)S(1)} %copy-done.14, bf16[192,1024]{1,0:T(8,128)(2,1)S(1)} %copy-done.16), custom_call_target="tpu_custom_call" | custom-call | flops 3221225472 | bytes 13107200 | tf_op jit(solution)/shard_map/pallas_call | solution.py:63
  109.2 3.0 %collective-permute-done.17 = bf16[192,1024]{1,0:T(8,128)(2,1)S(1)} collective-permute-done((bf16[192,1024]{1,0:T(8,128)(2,1)S(1)}, bf16[192,1024]{1,0:T(8,128)(2,1)S(1)}, u32[]{:S(2)}, u32[]{:S(2)}) %collective-permute-start.17) | collective-permute-done | bytes 393248 | tf_op jit(solution)/shard_map/ppermute | solution.py:204
  112.3 1.6 %fusion.61 = bf16[192,1024]{1,0:T(8,128)(2,1)} fusion(f32[192,1024]{1,0:T(8,128)S(1)} %fusion.4, bf16[192,1024]{1,0:T(8,128)(2,1)S(1)} %shard_map.77.refs_3_, bf16[1024,2048]{1,0:T(8,128)(2,1)S(1)} %copy-done.27, s32[]{:T(128)S(6)} %select_n.8, bf16[192,1024]{1,0:T(8,128)(2,1)S(1)} %collective-permute-done.17), kind=kOutput, calls=%fused_computation.38 | convolution fusion | flops 403439616 | bytes 4063236 | tf_op jit(solution)/shard_map/dot_general | solution.py:35
  115.6 1.0 copy-done.24
  116.6 1.4 %copy-done.25 = bf16[768,1024]{1,0:T(8,128)(2,1)S(1)} copy-done((bf16[768,1024]{1,0:T(8,128)(2,1)S(1)}, bf16[768,1024]{1,0:T(8,128)(2,1)}, u32[]{:S(2)}) %copy-start.25) | copy-done | bytes 1572888
  118.0 7.9 %shard_map.80 = f32[1024,2048]{1,0:T(8,128)} custom-call(s32[5]{0:T(128)S(1)} %stack.43.at_ref, bf16[768,1024]{1,0:T(8,128)(2,1)S(1)} %copy-done.25, bf16[192,1024]{1,0:T(8,128)(2,1)S(1)} %copy-done.5, bf16[192,1024]{1,0:T(8,128)(2,1)S(1)} %copy-done.7, bf16[192,1024]{1,0:T(8,128)(2,1)S(1)} %shard_map.78.refs_2_, bf16[192,1024]{1,0:T(8,128)(2,1)S(1)} %copy-done.3, ...), custom_call_target="tpu_custom_call" | custom-call | flops 3221225472 | bytes 13107200 | tf_op jit(solution)/shard_map/pallas_call | solution.py:105
  126.1 1.6 %fusion.64 = bf16[192,1024]{1,0:T(8,128)(2,1)} fusion(f32[192,1024]{1,0:T(8,128)S(1)} %fusion.6, bf16[192,1024]{1,0:T(8,128)(2,1)S(1)} %copy-done.5, bf16[1024,2048]{1,0:T(8,128)(2,1)S(1)} %copy-done.28, s32[]{:T(128)S(6)} %select_n.8, bf16[192,1024]{1,0:T(8,128)(2,1)S(1)} %collective-permute-done.18), kind=kOutput, calls=%fused_computation.39 | convolution fusion | flops 403439616 | bytes 4063236 | tf_op jit(solution)/shard_map/dot_general | solution.py:35
  (108 shorter events, 11.2 us)
Async XLA Ops:
  7.2 48.9 %all-gather.3.cloned.1.call-start = ((), (), s32[]{:S(2)}) async-start(), calls=%async_computation | async-start | bytes 3932160 | tf_op jit(solution)/shard_map/all_gather | solution.py:169
  7.9 107.7 %all-gather.5.cloned.1.call-start = ((), (), s32[]{:S(2)}) async-start(), calls=%async_computation.1 | async-start | bytes 1966080 | tf_op jit(solution)/shard_map/all_gather | solution.py:192
  11.1 6.0 %collective-permute-start = (bf16[1024,1024]{1,0:T(8,128)(2,1)}, bf16[1024,1024]{1,0:T(8,128)(2,1)S(1)}, u32[]{:S(2)}, u32[]{:S(2)}) collective-permute-start(bf16[1024,1024]{1,0:T(8,128)(2,1)} %constant_dynamic-slice_fusion), channel_id=1, source_target_pairs={{0,4},{4,0},{8,12},{12,8},{1,5},{5,1},{9,13},{13,9},{2,6},{6,2},{1... | collective-permute-start | bytes 6291464 | tf_op jit(solution)/shard_map/ppermute | solution.py:184
  11.6 5.5 %collective-permute-start.1 = (bf16[192,1024]{1,0:T(8,128)(2,1)S(1)}, bf16[192,1024]{1,0:T(8,128)(2,1)S(1)}, u32[]{:S(2)}, u32[]{:S(2)}) collective-permute-start(bf16[192,1024]{1,0:T(8,128)(2,1)S(1)} %copy-done.17), channel_id=1, source_target_pairs={{0,4},{4,0},{8,12},{12,8},{1,5},{5,1},{9,13},{13,9},{2,6},{6,2},{1... | collective-permute-start | bytes 1179656 | tf_op jit(solution)/shard_map/ppermute | solution.py:179
  11.6 14.3 %collective-permute-start.4 = (bf16[192,1024]{1,0:T(8,128)(2,1)S(1)}, bf16[192,1024]{1,0:T(8,128)(2,1)S(1)}, u32[]{:S(2)}, u32[]{:S(2)}) collective-permute-start(bf16[192,1024]{1,0:T(8,128)(2,1)S(1)} %copy-done.17), channel_id=1, source_target_pairs={{0,1},{1,2},{2,3},{3,0},{4,5},{5,6},{6,7},{7,4},{8,9},{9,10},{10,1... | collective-permute-start | bytes 1179656 | tf_op jit(solution)/shard_map/ppermute | solution.py:183
  17.1 10.6 %copy-start.29 = (bf16[1024,1024]{1,0:T(8,128)(2,1)}, bf16[1024,1024]{1,0:T(8,128)(2,1)S(1)}, u32[]{:S(2)}) copy-start(bf16[1024,1024]{1,0:T(8,128)(2,1)S(1)} %collective-permute-done) | copy-start | bytes 6291460
  17.1 11.4 %copy-start.32 = (bf16[2048,1024]{1,0:T(8,128)(2,1)S(1)}, bf16[2048,1024]{1,0:T(8,128)(2,1)}, u32[]{:S(2)}) copy-start(bf16[2048,1024]{1,0:T(8,128)(2,1)} %param.9) | copy-start | bytes 12582916
  25.9 1.7 %collective-permute-start.6 = (bf16[192,1024]{1,0:T(8,128)(2,1)S(1)}, bf16[192,1024]{1,0:T(8,128)(2,1)S(1)}, u32[]{:S(2)}, u32[]{:S(2)}) collective-permute-start(bf16[192,1024]{1,0:T(8,128)(2,1)S(1)} %collective-permute-done.4.refs_1_), channel_id=1, source_target_pairs={{0,4},{4,0},{8,12},{12,8},{1,5},{5,1},{9,13},{13,9},{2,6},{6,2},{1... | collective-permute-start | bytes 1179656 | tf_op jit(solution)/shard_map/ppermute | solution.py:179
  25.9 13.3 %collective-permute-start.5 = (bf16[192,1024]{1,0:T(8,128)(2,1)S(1)}, bf16[192,1024]{1,0:T(8,128)(2,1)S(1)}, u32[]{:S(2)}, u32[]{:S(2)}) collective-permute-start(bf16[192,1024]{1,0:T(8,128)(2,1)S(1)} %collective-permute-done.4.refs_1_), channel_id=1, source_target_pairs={{0,1},{1,2},{2,3},{3,0},{4,5},{5,6},{6,7},{7,4},{8,9},{9,10},{10,1... | collective-permute-start | bytes 1179656 | tf_op jit(solution)/shard_map/ppermute | solution.py:191
  28.5 12.5 %copy-start.30 = (bf16[1024,1024]{1,0:T(8,128)(2,1)S(1)}, bf16[1024,1024]{1,0:T(8,128)(2,1)}, u32[]{:S(2)}) copy-start(bf16[1024,1024]{1,0:T(8,128)(2,1)} %copy-done.29) | copy-start | bytes 6291460
  39.3 1.7 %collective-permute-start.8 = (bf16[192,1024]{1,0:T(8,128)(2,1)S(1)}, bf16[192,1024]{1,0:T(8,128)(2,1)S(1)}, u32[]{:S(2)}, u32[]{:S(2)}) collective-permute-start(bf16[192,1024]{1,0:T(8,128)(2,1)S(1)} %collective-permute-done.5.refs_2_), channel_id=1, source_target_pairs={{0,4},{4,0},{8,12},{12,8},{1,5},{5,1},{9,13},{13,9},{2,6},{6,2},{1... | collective-permute-start | bytes 1179656 | tf_op jit(solution)/shard_map/ppermute | solution.py:179
  39.3 16.8 %collective-permute-start.14 = (bf16[192,1024]{1,0:T(8,128)(2,1)S(1)}, bf16[192,1024]{1,0:T(8,128)(2,1)S(1)}, u32[]{:S(2)}, u32[]{:S(2)}) collective-permute-start(bf16[192,1024]{1,0:T(8,128)(2,1)S(1)} %get-tuple-element.11), channel_id=1, source_target_pairs={{0,8},{4,12},{8,0},{12,4},{1,9},{5,13},{9,1},{13,5},{2,10},{6,14},... | collective-permute-start | bytes 1179656 | tf_op jit(solution)/shard_map/ppermute | solution.py:197
  40.8 13.0 %collective-permute-start.7 = (bf16[192,1024]{1,0:T(8,128)(2,1)S(1)}, bf16[192,1024]{1,0:T(8,128)(2,1)S(1)}, u32[]{:S(2)}, u32[]{:S(2)}) collective-permute-start(bf16[192,1024]{1,0:T(8,128)(2,1)S(1)} %collective-permute-done.5.refs_2_), channel_id=1, source_target_pairs={{0,1},{1,2},{2,3},{3,0},{4,5},{5,6},{6,7},{7,4},{8,9},{9,10},{10,1... | collective-permute-start | bytes 1179656 | tf_op jit(solution)/shard_map/ppermute | solution.py:191
  53.8 5.4 %collective-permute-start.9 = (bf16[192,1024]{1,0:T(8,128)(2,1)S(1)}, bf16[192,1024]{1,0:T(8,128)(2,1)S(1)}, u32[]{:S(2)}, u32[]{:S(2)}) collective-permute-start(bf16[192,1024]{1,0:T(8,128)(2,1)S(1)} %collective-permute-done.7.refs_3_), channel_id=1, source_target_pairs={{0,4},{4,0},{8,12},{12,8},{1,5},{5,1},{9,13},{13,9},{2,6},{6,2},{1... | collective-permute-start | bytes 1179656 | tf_op jit(solution)/shard_map/ppermute | solution.py:179
  54.0 32.1 %collective-permute-start.2 = (bf16[192,1024]{1,0:T(8,128)(2,1)}, bf16[192,1024]{1,0:T(8,128)(2,1)}, u32[]{:S(2)}, u32[]{:S(2)}) collective-permute-start(bf16[192,1024]{1,0:T(8,128)(2,1)} %get-tuple-element.9), channel_id=1, source_target_pairs={{0,8},{4,12},{8,0},{12,4},{1,9},{5,13},{9,1},{13,5},{2,10},{6,14},... | collective-permute-start | bytes 1179656 | tf_op jit(solution)/shard_map/ppermute | solution.py:197
  54.5 20.1 %collective-permute-start.12 = (bf16[192,1024]{1,0:T(8,128)(2,1)}, bf16[192,1024]{1,0:T(8,128)(2,1)}, u32[]{:S(2)}, u32[]{:S(2)}) collective-permute-start(bf16[192,1024]{1,0:T(8,128)(2,1)} %get-tuple-element.13), channel_id=1, source_target_pairs={{0,8},{4,12},{8,0},{12,4},{1,9},{5,13},{9,1},{13,5},{2,10},{6,14},... | collective-permute-start | bytes 1179656 | tf_op jit(solution)/shard_map/ppermute | solution.py:197
  59.1 18.9 %copy-start.6 = (bf16[192,1024]{1,0:T(8,128)(2,1)}, bf16[192,1024]{1,0:T(8,128)(2,1)S(1)}, u32[]{:S(2)}) copy-start(bf16[192,1024]{1,0:T(8,128)(2,1)S(1)} %shard_map.79.refs_1_) | copy-start | bytes 1179652
  59.1 18.1 %collective-permute-start.15 = (bf16[192,1024]{1,0:T(8,128)(2,1)S(1)}, bf16[192,1024]{1,0:T(8,128)(2,1)S(1)}, u32[]{:S(2)}, u32[]{:S(2)}) collective-permute-start(bf16[192,1024]{1,0:T(8,128)(2,1)S(1)} %shard_map.79.refs_1_), channel_id=1, source_target_pairs={{0,4},{4,0},{8,12},{12,8},{1,5},{5,1},{9,13},{13,9},{2,6},{6,2},{1... | collective-permute-start | bytes 1179656 | tf_op jit(solution)/shard_map/ppermute | solution.py:201
  61.1 13.5 %copy-start.1 = (bf16[768,2048]{1,0:T(8,128)(2,1)S(1)}, bf16[768,2048]{1,0:T(8,128)(2,1)}, u32[]{:S(2)}) copy-start(bf16[768,2048]{1,0:T(8,128)(2,1)} %all-gather.3.cloned.1.call-done.pre_ref) | copy-start | bytes 9437188
  61.1 13.5 %copy-start.8 = (f32[192,1024]{1,0:T(8,128)S(1)}, f32[192,1024]{1,0:T(8,128)}, u32[]{:S(2)}) copy-start(f32[192,1024]{1,0:T(8,128)} %get-tuple-element.14.part_ref) | copy-start | bytes 2359300
  63.1 19.6 %collective-permute-start.10 = (bf16[192,1024]{1,0:T(8,128)(2,1)}, bf16[192,1024]{1,0:T(8,128)(2,1)}, u32[]{:S(2)}, u32[]{:S(2)}) collective-permute-start(bf16[192,1024]{1,0:T(8,128)(2,1)} %get-tuple-element.15), channel_id=1, source_target_pairs={{0,8},{4,12},{8,0},{12,4},{1,9},{5,13},{9,1},{13,5},{2,10},{6,14},... | collective-permute-start | bytes 1179656 | tf_op jit(solution)/shard_map/ppermute | solution.py:197
  77.1 12.0 %collective-permute-start.13 = (bf16[192,1024]{1,0:T(8,128)(2,1)S(1)}, bf16[192,1024]{1,0:T(8,128)(2,1)}, u32[]{:S(2)}, u32[]{:S(2)}) collective-permute-start(bf16[192,1024]{1,0:T(8,128)(2,1)S(1)} %shard_map.78.refs_2_), channel_id=1, source_target_pairs={{0,4},{4,0},{8,12},{12,8},{1,5},{5,1},{9,13},{13,9},{2,6},{6,2},{1... | collective-permute-start | bytes 1179656 | tf_op jit(solution)/shard_map/ppermute | solution.py:201
  79.6 17.8 %collective-permute-start.16 = (bf16[192,1024]{1,0:T(8,128)(2,1)}, bf16[192,1024]{1,0:T(8,128)(2,1)}, u32[]{:S(2)}, u32[]{:S(2)}) collective-permute-start(bf16[192,1024]{1,0:T(8,128)(2,1)} %fusion.55), channel_id=1, source_target_pairs={{0,1},{1,2},{2,3},{3,0},{4,5},{5,6},{6,7},{7,4},{8,9},{9,10},{10,1... | collective-permute-start | bytes 1179656 | tf_op jit(solution)/shard_map/ppermute | solution.py:204
  86.0 26.3 %copy-start.2 = (bf16[192,1024]{1,0:T(8,128)(2,1)}, bf16[192,1024]{1,0:T(8,128)(2,1)S(1)}, u32[]{:S(2)}) copy-start(bf16[192,1024]{1,0:T(8,128)(2,1)S(1)} %shard_map.77.refs_3_) | copy-start | bytes 1179652
  86.0 22.4 %collective-permute-start.11 = (bf16[192,1024]{1,0:T(8,128)(2,1)S(1)}, bf16[192,1024]{1,0:T(8,128)(2,1)S(1)}, u32[]{:S(2)}, u32[]{:S(2)}) collective-permute-start(bf16[192,1024]{1,0:T(8,128)(2,1)S(1)} %shard_map.77.refs_3_), channel_id=1, source_target_pairs={{0,4},{4,0},{8,12},{12,8},{1,5},{5,1},{9,13},{13,9},{2,6},{6,2},{1... | collective-permute-start | bytes 1179656 | tf_op jit(solution)/shard_map/ppermute | solution.py:201
  88.5 10.7 %copy-start.4 = (bf16[192,1024]{1,0:T(8,128)(2,1)}, bf16[192,1024]{1,0:T(8,128)(2,1)S(1)}, u32[]{:S(2)}) copy-start(bf16[192,1024]{1,0:T(8,128)(2,1)S(1)} %shard_map.76.refs_0_) | copy-start | bytes 1179652
  88.6 25.4 %collective-permute-start.3 = (bf16[192,1024]{1,0:T(8,128)(2,1)S(1)}, bf16[192,1024]{1,0:T(8,128)(2,1)S(1)}, u32[]{:S(2)}, u32[]{:S(2)}) collective-permute-start(bf16[192,1024]{1,0:T(8,128)(2,1)S(1)} %shard_map.76.refs_0_), channel_id=1, source_target_pairs={{0,4},{4,0},{8,12},{12,8},{1,5},{5,1},{9,13},{13,9},{2,6},{6,2},{1... | collective-permute-start | bytes 1179656 | tf_op jit(solution)/shard_map/ppermute | solution.py:201
  90.9 8.6 %copy-start.12 = (bf16[192,1024]{1,0:T(8,128)(2,1)S(1)}, bf16[192,1024]{1,0:T(8,128)(2,1)}, u32[]{:S(2)}) copy-start(bf16[192,1024]{1,0:T(8,128)(2,1)} %copy-done.11) | copy-start | bytes 1179652
  90.9 8.6 %copy-start.14 = (bf16[192,1024]{1,0:T(8,128)(2,1)S(1)}, bf16[192,1024]{1,0:T(8,128)(2,1)}, u32[]{:S(2)}) copy-start(bf16[192,1024]{1,0:T(8,128)(2,1)} %copy-done.13) | copy-start | bytes 1179652
  90.9 8.6 %copy-start.16 = (bf16[192,1024]{1,0:T(8,128)(2,1)S(1)}, bf16[192,1024]{1,0:T(8,128)(2,1)}, u32[]{:S(2)}) copy-start(bf16[192,1024]{1,0:T(8,128)(2,1)} %copy-done.15) | copy-start | bytes 1179652
  99.3 13.0 %collective-permute-start.17 = (bf16[192,1024]{1,0:T(8,128)(2,1)S(1)}, bf16[192,1024]{1,0:T(8,128)(2,1)S(1)}, u32[]{:S(2)}, u32[]{:S(2)}) collective-permute-start(bf16[192,1024]{1,0:T(8,128)(2,1)S(1)} %fusion.58), channel_id=1, source_target_pairs={{0,1},{1,2},{2,3},{3,0},{4,5},{5,6},{6,7},{7,4},{8,9},{9,10},{10,1... | collective-permute-start | bytes 1179656 | tf_op jit(solution)/shard_map/ppermute | solution.py:204
  113.9 12.2 %collective-permute-start.18 = (bf16[192,1024]{1,0:T(8,128)(2,1)}, bf16[192,1024]{1,0:T(8,128)(2,1)S(1)}, u32[]{:S(2)}, u32[]{:S(2)}) collective-permute-start(bf16[192,1024]{1,0:T(8,128)(2,1)} %fusion.61), channel_id=1, source_target_pairs={{0,1},{1,2},{2,3},{3,0},{4,5},{5,6},{6,7},{7,4},{8,9},{9,10},{10,1... | collective-permute-start | bytes 1179656 | tf_op jit(solution)/shard_map/ppermute | solution.py:204
  (23 other events, 70.3 us)
Sparse Core Ops, SparseCore 0:
  9.6 31.4 all-gather.2
  54.0 37.8 all-gather.4

commit v3 on v2

--- a/solution.py
+++ b/solution.py
@@ -33,6 +33,10 @@
 
 def dot(a, b, dims):
     return lax.dot_general(a, b, dims, preferred_element_type=jnp.float32)
+
+
+def after(value, *first):
+    return lax.optimization_barrier((value, *first))[0]
 
 
 def tile_of(extent):
@@ -168,43 +172,58 @@
 
     pre_all = lax.all_gather(preactivation, "row", axis=0, tiled=True)
 
+    down_pair = lax.ppermute(down_weight, "row", pair)
     down_mine = lax.dynamic_slice(down_weight, (core * half, 0), (half, features))
-    down_other = lax.dynamic_slice(down_weight, ((1 - core) * half, 0), (half, features))
+    down_pair = lax.dynamic_slice(down_pair, (core * half, 0), (half, features))
     up_mine = lax.dynamic_slice(up_weight, (0, core * half), (features, half))
     up_other = lax.dynamic_slice(up_weight, (0, (1 - core) * half), (features, half))
 
-    cots, parts, sent = [cotangent], [None] * cols, [None] * cols
-
-    def hidden_part(s):
-        cot_pair = lax.ppermute(cots[s], "row", pair)
-        parts[s] = dot(cots[s], down_mine, LAST) + dot(cot_pair, down_pair, LAST)
-        sent[s] = parts[s].astype(jnp.bfloat16)
-
-    arriving = lax.ppermute(cotangent, "col", ring)
-    down_pair = lax.ppermute(down_other, "row", pair)
-    for s in range(cols):
-        hidden_part(s)
-        if s < cols - 1:
-            arriving, _ = lax.optimization_barrier((arriving, sent[s]))
-            cots.append(arriving)
-        if s < cols - 2:
-            arriving = lax.ppermute(arriving, "col", ring)
-    inputs_all = lax.all_gather(inputs, "col", axis=0, tiled=True)
-
-    sums, mine, theirs = None, [None] * cols, [None] * cols
-    for s in list(range(1, cols)) + [0]:
-        others = [
-            lax.ppermute(sent[s], "row", [(i, (i + shift) % rows) for i in range(rows)])
+    parts, others, mine, theirs = ([None] * cols for _ in range(4))
+
+    def hidden_part(s, cot, first):
+        cot_pair = lax.ppermute(after(cot, *first), "row", pair)
+        parts[s] = dot(cot, down_mine, LAST) + dot(cot_pair, down_pair, LAST)
+        sent = parts[s].astype(jnp.bfloat16)
+        others[s] = [
+            lax.ppermute(sent, "row", [(i, (i + shift) % rows) for i in range(rows)])
             for shift in range(2, rows, 2)
         ]
-        mine[s] = pre_grad_call(at[s], core, pre_all, parts[s], others)
+        return sent
+
+    def pre_grad(s, first):
+        others[s][0] = after(others[s][0], *first)
+        mine[s] = pre_grad_call(at[s], core, pre_all, parts[s], others[s])
         theirs[s] = lax.ppermute(mine[s], "row", pair)
-        share = dot(mine[s], up_mine, LAST) + dot(theirs[s], up_other, LAST)
-        if sums is not None:
-            share = share + lax.ppermute(sums, "col", ring).astype(jnp.float32)
-        sums = share.astype(jnp.bfloat16)
-    grad_down = grad_down_call(at, pre_all, cots, scale)
-    grad_up = grad_up_call(at, inputs_all, mine, theirs, scale)
+
+    def share(s, first):
+        return dot(after(mine[s], *first), up_mine, LAST) + dot(theirs[s], up_other, LAST)
+
+    cots = [cotangent]
+    sent = hidden_part(0, cotangent, [])
+    arriving = lax.ppermute(cotangent, "col", ring)
+    for s in range(1, cols):
+        first = [sent]
+        if s == cols - 1:
+            pre_grad(1, [sent])
+            first = [sent, mine[1]]
+        cots.append(after(arriving, *first))
+        if s < cols - 1:
+            arriving = lax.ppermute(cots[s], "col", ring)
+        sent = hidden_part(s, cots[s], others[s - 2] if s >= 2 else [])
+    inputs_all = lax.all_gather(inputs, "col", axis=0, tiled=True)
+
+    sums = share(1, []).astype(jnp.bfloat16)
+    grad_down = grad_down_call(after(at, sums), pre_all, cots, scale)
+    for s in range(2, cols):
+        pre_grad(s, [sums, sent])
+        if s == cols - 1:
+            pre_grad(0, [mine[s]])
+        arrived = lax.ppermute(sums, "col", ring)
+        first = [grad_down] if s == 2 else []
+        sums = (share(s, first) + arrived.astype(jnp.float32)).astype(jnp.bfloat16)
+    arrived = lax.ppermute(sums, "col", ring)
+    grad_up = grad_up_call(after(at, sums), inputs_all, mine, theirs, scale)
+    sums = (share(0, [grad_up]) + arrived.astype(jnp.float32)).astype(jnp.bfloat16)
     return (sums, grad_up, grad_down)
 
 

time: 135 us -> 133 us (0.985)
  waiting for transfers between devices: 53 us -> 42.7 us
  starting transfers between devices: 8.68 us -> 17.9 us
  matrix products: 22.6 us -> 30.8 us
  local copies, waits for them, and re-layouts: 10.6 us -> 5.31 us
  Pallas kernels: 24.8 us -> 21.3 us
    ppermute x18, starting transfers between devices: 5.58 us -> 15.2 us  [the longest x3 7.43 us: per_device(): arrived = lax.ppermute(sums, 'col', ring)]
    ppermute x18, waiting for transfers between devices: 45.4 us -> 37.2 us  [the longest x3 16.5 us: per_device(): arrived = lax.ppermute(sums, 'col', ring)]
    dot_general x16, matrix products: 22.6 us -> 30.8 us  [dot(): return lax.dot_general(a, b, dims, preferred_element_type=jnp.float32)]
    pallas_call x4, Pallas kernels: 8.09 us -> 4.49 us  [pre_grad_call(): pl.pallas_call(pre_grad_kernel, out_shape=jax.ShapeDtypeStruct((tokens, h...]
    dynamic_slice x1 -> x0, local copies, waits for them, and re-layouts: 3.13 us -> none  [per_device(): lax.dynamic_slice(down_weight, ((1 - core) * half, 0), (half, features))]
    unnamed x68 -> x28, local copies, waits for them, and re-layouts: 7.41 us -> 5.23 us
    ppermute x1, waiting for transfers between devices: 6.97 us -> 5.32 us  [per_device(): arriving = lax.ppermute(cotangent, 'col', ring)]
  transfers between devices with their start and end apart: 21 -> 21, of which waited for: 10 -> 9; matrix products, arithmetic and copies ran while one was open for 18% -> 22% of each run, Pallas kernels for 18% -> 16%
where the time goes in v3:
time: 133 us
  waiting for transfers between devices  42.7 us (32%)
  matrix products  30.8 us (23%)
  Pallas kernels  21.3 us (16%)
  starting transfers between devices  17.9 us (13%)
  between operations  14.3 us (11%)
  local copies, waits for them, and re-layouts  5.31 us (4%)
    dot_general x16, matrix products, dot(): return lax.dot_general(a, b, dims, preferred_element_type=jnp.float32)  30.8 us
    ppermute x3, waiting for transfers between devices, per_device(): arrived = lax.ppermute(sums, 'col', ring)  16.5 us
    ppermute x4, waiting for transfers between devices, hidden_part(): lax.ppermute(sent, 'row', [(i, (i + shift) % rows) for i in range(rows)])  11.2 us
    pallas_call x1, Pallas kernels, grad_down_call(): pl.pallas_call(functools.partial(grad_down_kernel, len(cots), scale), out...  10.1 us
    ppermute x2, waiting for transfers between devices, per_device(): arriving = lax.ppermute(cots[s], 'col', ring)  7.49 us
    ppermute x3, starting transfers between devices, per_device(): arrived = lax.ppermute(sums, 'col', ring)  7.43 us
    pallas_call x1, Pallas kernels, grad_up_call(): pl.pallas_call(functools.partial(grad_up_kernel, len(mine), scale), out_s...  6.65 us
    ppermute x1, waiting for transfers between devices, per_device(): arriving = lax.ppermute(cotangent, 'col', ring)  5.32 us
  transfers between devices with their start and end apart: 21, of which 9 were waited for; matrix products, arithmetic and copies ran while one was open for 22% of the time, Pallas kernels for 16%

profile of v3, /device:TPU:0, one launch (start us, length us, event | category | flops | bytes accessed | tf_op | source)
XLA Modules:
  0.0 132.6 jit_solution(8382164306152466885)
XLA Ops:
  8.5 2.6 %collective-permute-start.3 = (bf16[192,1024]{1,0:T(8,128)(2,1)}, bf16[192,1024]{1,0:T(8,128)(2,1)S(1)}, u32[]{:S(2)}, u32[]{:S(2)}) collective-permute-start(bf16[192,1024]{1,0:T(8,128)(2,1)} %refs_0_.1), channel_id=1, source_target_pairs={{0,1},{1,2},{2,3},{3,0},{4,5},{5,6},{6,7},{7,4},{8,9},{9,10},{10,1... | collective-permute-start | bytes 1179656 | tf_op jit(solution)/shard_map/ppermute | solution.py:203
  11.1 2.5 %fusion.30 = f32[1024,192]{0,1:T(8,128)S(1)} fusion(bf16[192,1024]{1,0:T(8,128)(2,1)} %refs_0_.1, bf16[2048,1024]{1,0:T(8,128)(2,1)} %param.9, s32[]{:T(128)S(6)} %select_n.8), kind=kOutput, calls=%fused_computation.30 | convolution fusion | flops 402653184 | bytes 3276804 | tf_op jit(solution)/shard_map/dot_general | solution.py:35
  13.6 1.7 %collective-permute-done.1 = bf16[192,1024]{1,0:T(8,128)(2,1)S(1)} collective-permute-done((bf16[192,1024]{1,0:T(8,128)(2,1)}, bf16[192,1024]{1,0:T(8,128)(2,1)S(1)}, u32[]{:S(2)}, u32[]{:S(2)}) %collective-permute-start.1) | collective-permute-done | bytes 393248 | tf_op jit(solution)/shard_map/ppermute | solution.py:184
  15.3 2.4 %fusion.96 = (bf16[192,1024]{1,0:T(8,128)(2,1)S(1)}, f32[192,1024]{1,0:T(8,128)S(1)}) fusion(f32[1024,192]{0,1:T(8,128)S(1)} %fusion.30, bf16[192,1024]{1,0:T(8,128)(2,1)S(1)} %collective-permute-done.1, bf16[2048,1024]{1,0:T(8,128)(2,1)} %collective-permute-done, s32[]{:T(128)S(6)} %select_n.8), kind=kOutput, calls=%fused_computation.68 | convolution fusion | flops 403046400 | bytes 4456452 | tf_op jit(solution)/shard_map/dot_general | solution.py:35
  17.7 5.3 %collective-permute-done.3.refs_1_ = bf16[192,1024]{1,0:T(8,128)(2,1)S(1)} collective-permute-done((bf16[192,1024]{1,0:T(8,128)(2,1)}, bf16[192,1024]{1,0:T(8,128)(2,1)S(1)}, u32[]{:S(2)}, u32[]{:S(2)}) %collective-permute-start.3) | collective-permute-done | bytes 393248 | tf_op jit(solution)/shard_map/ppermute | solution.py:203
  23.1 1.5 %collective-permute-start.2 = (bf16[192,1024]{1,0:T(8,128)(2,1)S(1)}, bf16[192,1024]{1,0:T(8,128)(2,1)S(1)}, u32[]{:S(2)}, u32[]{:S(2)}) collective-permute-start(bf16[192,1024]{1,0:T(8,128)(2,1)S(1)} %get-tuple-element.29), channel_id=1, source_target_pairs={{0,8},{4,12},{8,0},{12,4},{1,9},{5,13},{9,1},{13,5},{2,10},{6,14},... | collective-permute-start | bytes 1179656 | tf_op jit(solution)/shard_map/ppermute | solution.py:188
  24.8 2.5 %fusion.20 = f32[192,1024]{1,0:T(8,128)S(1)} fusion(bf16[192,1024]{1,0:T(8,128)(2,1)S(1)} %collective-permute-done.5, bf16[2048,1024]{1,0:T(8,128)(2,1)} %collective-permute-done, s32[]{:T(128)S(6)} %select_n.8), kind=kOutput, calls=%fused_computation.20 | convolution fusion | flops 402653184 | bytes 3276804 | tf_op jit(solution)/shard_map/dot_general | solution.py:35
  27.3 1.6 %fusion.97 = (bf16[192,1024]{1,0:T(8,128)(2,1)}, f32[192,1024]{1,0:T(8,128)S(1)}) fusion(f32[192,1024]{1,0:T(8,128)S(1)} %fusion.20, bf16[192,1024]{1,0:T(8,128)(2,1)S(1)} %collective-permute-done.3.refs_1_, bf16[2048,1024]{1,0:T(8,128)(2,1)S(1)} %copy-done.12, s32[]{:T(128)S(6)} %select_n.8), kind=kOutput, calls=%fused_computation.69 | convolution fusion | flops 403046400 | bytes 4456452 | tf_op jit(solution)/shard_map/dot_general | solution.py:35
  28.9 7.5 %collective-permute-done.4.refs_2_ = bf16[192,1024]{1,0:T(8,128)(2,1)S(1)} collective-permute-done((bf16[192,1024]{1,0:T(8,128)(2,1)S(1)}, bf16[192,1024]{1,0:T(8,128)(2,1)S(1)}, u32[]{:S(2)}, u32[]{:S(2)}) %collective-permute-start.4) | collective-permute-done | bytes 393248 | tf_op jit(solution)/shard_map/ppermute | solution.py:211
  36.4 6.9 %collective-permute-done.2.refs_0_ = bf16[192,1024]{1,0:T(8,128)(2,1)S(1)} collective-permute-done((bf16[192,1024]{1,0:T(8,128)(2,1)S(1)}, bf16[192,1024]{1,0:T(8,128)(2,1)S(1)}, u32[]{:S(2)}, u32[]{:S(2)}) %collective-permute-start.2) | collective-permute-done | bytes 393248 | tf_op jit(solution)/shard_map/ppermute | solution.py:188
  43.4 1.5 %collective-permute-start.8 = (bf16[192,1024]{1,0:T(8,128)(2,1)}, bf16[192,1024]{1,0:T(8,128)(2,1)S(1)}, u32[]{:S(2)}, u32[]{:S(2)}) collective-permute-start(bf16[192,1024]{1,0:T(8,128)(2,1)} %get-tuple-element.31), channel_id=1, source_target_pairs={{0,8},{4,12},{8,0},{12,4},{1,9},{5,13},{9,1},{13,5},{2,10},{6,14},... | collective-permute-start | bytes 1179656 | tf_op jit(solution)/shard_map/ppermute | solution.py:188
  44.9 1.2 collective-permute-start.6
  46.1 2.5 %fusion.18 = f32[192,1024]{1,0:T(8,128)S(1)} fusion(bf16[192,1024]{1,0:T(8,128)(2,1)S(1)} %collective-permute-done.7, bf16[2048,1024]{1,0:T(8,128)(2,1)} %collective-permute-done, s32[]{:T(128)S(6)} %select_n.8), kind=kOutput, calls=%fused_computation.18 | convolution fusion | flops 402653184 | bytes 3276804 | tf_op jit(solution)/shard_map/dot_general | solution.py:35
  48.6 3.2 %fusion.98 = (bf16[192,1024]{1,0:T(8,128)(2,1)}, f32[192,1024]{1,0:T(8,128)S(1)}) fusion(f32[192,1024]{1,0:T(8,128)S(1)} %fusion.18, bf16[192,1024]{1,0:T(8,128)(2,1)S(1)} %collective-permute-done.4.refs_2_, bf16[2048,1024]{1,0:T(8,128)(2,1)} %param.9, s32[]{:T(128)S(6)} %select_n.8), kind=kOutput, calls=%fused_computation.70 | convolution fusion | flops 403046400 | bytes 4456452 | tf_op jit(solution)/shard_map/dot_general | solution.py:35
  51.8 4.3 %collective-permute-done.8.refs_0_ = bf16[192,1024]{1,0:T(8,128)(2,1)S(1)} collective-permute-done((bf16[192,1024]{1,0:T(8,128)(2,1)}, bf16[192,1024]{1,0:T(8,128)(2,1)S(1)}, u32[]{:S(2)}, u32[]{:S(2)}) %collective-permute-start.8) | collective-permute-done | bytes 393248 | tf_op jit(solution)/shard_map/ppermute | solution.py:188
  56.9 2.0 %copy-done = bf16[768,2048]{1,0:T(8,128)(2,1)S(1)} copy-done((bf16[768,2048]{1,0:T(8,128)(2,1)S(1)}, bf16[768,2048]{1,0:T(8,128)(2,1)}, u32[]{:S(2)}) %copy-start) | copy-done | bytes 3145752
  61.9 2.4 %fusion.14 = f32[192,1024]{1,0:T(8,128)S(1)} fusion(bf16[192,1024]{1,0:T(8,128)(2,1)S(1)} %shard_map.76.refs_1_, bf16[1024,2048]{1,0:T(8,128)(2,1)} %param.8, s32[]{:T(128)S(6)} %select_n.8), kind=kOutput, calls=%fused_computation.14 | convolution fusion | flops 402653184 | bytes 3276804 | tf_op jit(solution)/shard_map/dot_general | solution.py:35
  64.4 2.6 %fusion.74 = bf16[192,1024]{1,0:T(8,128)(2,1)S(1)} fusion(f32[192,1024]{1,0:T(8,128)S(1)} %fusion.14, bf16[192,1024]{1,0:T(8,128)(2,1)S(1)} %collective-permute-done.12.refs_5_, bf16[1024,2048]{1,0:T(8,128)(2,1)} %param.8, s32[]{:T(128)S(6)} %select_n.9), kind=kOutput, calls=%fused_computation.46 | convolution fusion | flops 403046400 | bytes 3670020 | tf_op jit(solution)/shard_map/dot_general | solution.py:35
  67.1 1.6 %collective-permute-start.14 = (bf16[192,1024]{1,0:T(8,128)(2,1)S(1)}, bf16[192,1024]{1,0:T(8,128)(2,1)S(1)}, u32[]{:S(2)}, u32[]{:S(2)}) collective-permute-start(bf16[192,1024]{1,0:T(8,128)(2,1)S(1)} %fusion.74), channel_id=1, source_target_pairs={{0,1},{1,2},{2,3},{3,0},{4,5},{5,6},{6,7},{7,4},{8,9},{9,10},{10,1... | collective-permute-start | bytes 1179656 | tf_op jit(solution)/shard_map/ppermute | solution.py:221
  68.7 2.5 %fusion.16 = f32[192,1024]{1,0:T(8,128)S(1)} fusion(bf16[192,1024]{1,0:T(8,128)(2,1)S(1)} %collective-permute-done.9, bf16[2048,1024]{1,0:T(8,128)(2,1)} %collective-permute-done, s32[]{:T(128)S(6)} %select_n.8), kind=kOutput, calls=%fused_computation.16 | convolution fusion | flops 402653184 | bytes 3276804 | tf_op jit(solution)/shard_map/dot_general | solution.py:35
  71.1 1.9 %fusion.99 = (bf16[192,1024]{1,0:T(8,128)(2,1)S(1)}, f32[192,1024]{1,0:T(8,128)S(1)}) fusion(f32[192,1024]{1,0:T(8,128)S(1)} %fusion.16, bf16[192,1024]{1,0:T(8,128)(2,1)} %collective-permute-done.6.refs_3_, bf16[2048,1024]{1,0:T(8,128)(2,1)S(1)} %copy-done.13, s32[]{:T(128)S(6)} %select_n.8), kind=kOutput, calls=%fused_computation.71 | convolution fusion | flops 403046400 | bytes 4456452 | tf_op jit(solution)/shard_map/dot_general | solution.py:35
  73.1 1.6 %collective-permute-start.10 = (bf16[192,1024]{1,0:T(8,128)(2,1)S(1)}, bf16[192,1024]{1,0:T(8,128)(2,1)S(1)}, u32[]{:S(2)}, u32[]{:S(2)}) collective-permute-start(bf16[192,1024]{1,0:T(8,128)(2,1)S(1)} %get-tuple-element.35), channel_id=1, source_target_pairs={{0,8},{4,12},{8,0},{12,4},{1,9},{5,13},{9,1},{13,5},{2,10},{6,14},... | collective-permute-start | bytes 1179656 | tf_op jit(solution)/shard_map/ppermute | solution.py:188
  75.9 10.1 %shard_map.78 = f32[2048,1024]{1,0:T(8,128)} custom-call(s32[5]{0:T(128)S(1)} %stack.43.at_ref, bf16[768,2048]{1,0:T(8,128)(2,1)S(1)} %copy-done.1, bf16[192,1024]{1,0:T(8,128)(2,1)S(1)} %copy-done.2, bf16[192,1024]{1,0:T(8,128)(2,1)S(1)} %collective-permute-done.3.refs_1_, bf16[192,1024]{1,0:T(8,128)(2,1)S(1)} %collective-permute-done.4.refs_2_, ...), custom_call_target="tpu_custom_call" | custom-call | flops 3221225472 | bytes 13107200 | tf_op jit(solution)/shard_map/pallas_call | solution.py:67
  86.9 2.2 %collective-permute-done.14 = bf16[192,1024]{1,0:T(8,128)(2,1)S(1)} collective-permute-done((bf16[192,1024]{1,0:T(8,128)(2,1)S(1)}, bf16[192,1024]{1,0:T(8,128)(2,1)S(1)}, u32[]{:S(2)}, u32[]{:S(2)}) %collective-permute-start.14) | collective-permute-done | bytes 393248 | tf_op jit(solution)/shard_map/ppermute | solution.py:221
  91.2 5.8 %collective-permute-start.16 = (bf16[192,1024]{1,0:T(8,128)(2,1)S(1)}, bf16[192,1024]{1,0:T(8,128)(2,1)S(1)}, u32[]{:S(2)}, u32[]{:S(2)}) collective-permute-start(bf16[192,1024]{1,0:T(8,128)(2,1)S(1)} %fusion.71), channel_id=1, source_target_pairs={{0,1},{1,2},{2,3},{3,0},{4,5},{5,6},{6,7},{7,4},{8,9},{9,10},{10,1... | collective-permute-start | bytes 1179656 | tf_op jit(solution)/shard_map/ppermute | solution.py:221
  97.2 1.1 shard_map.80.refs_0_
  99.2 10.5 %collective-permute-done.16 = bf16[192,1024]{1,0:T(8,128)(2,1)S(1)} collective-permute-done((bf16[192,1024]{1,0:T(8,128)(2,1)S(1)}, bf16[192,1024]{1,0:T(8,128)(2,1)S(1)}, u32[]{:S(2)}, u32[]{:S(2)}) %collective-permute-start.16) | collective-permute-done | bytes 393248 | tf_op jit(solution)/shard_map/ppermute | solution.py:221
  109.7 1.6 %fusion.68 = bf16[192,1024]{1,0:T(8,128)(2,1)} fusion(f32[192,1024]{1,0:T(8,128)S(1)} %fusion.10, bf16[192,1024]{1,0:T(8,128)(2,1)S(1)} %collective-permute-done.15.refs_7_, bf16[1024,2048]{1,0:T(8,128)(2,1)S(1)} %copy-done.10, s32[]{:T(128)S(6)} %select_n.9, bf16[192,1024]{1,0:T(8,128)(2,1)S(1)} %collective-permute-done.16), kind=kOutput, calls=%fused_computation.44 | convolution fusion | flops 403439616 | bytes 4063236 | tf_op jit(solution)/shard_map/dot_general | solution.py:35
  111.4 1.4 %copy-done.5 = bf16[768,1024]{1,0:T(8,128)(2,1)S(1)} copy-done((bf16[768,1024]{1,0:T(8,128)(2,1)S(1)}, bf16[768,1024]{1,0:T(8,128)(2,1)}, u32[]{:S(2)}) %copy-start.5) | copy-done | bytes 1572888
  112.8 6.6 %shard_map.81 = f32[1024,2048]{1,0:T(8,128)} custom-call(s32[5]{0:T(128)S(1)} %stack.43.at_ref, bf16[768,1024]{1,0:T(8,128)(2,1)S(1)} %copy-done.5, bf16[192,1024]{1,0:T(8,128)(2,1)S(1)} %shard_map.80.refs_0_, bf16[192,1024]{1,0:T(8,128)(2,1)S(1)} %shard_map.76.refs_1_, bf16[192,1024]{1,0:T(8,128)(2,1)S(1)} %shard_map.77.refs_2_, ...), custom_call_target="tpu_custom_call" | custom-call | flops 3221225472 | bytes 13107200 | tf_op jit(solution)/shard_map/pallas_call | solution.py:109
  120.3 3.9 %collective-permute-done.18 = bf16[192,1024]{1,0:T(8,128)(2,1)S(1)} collective-permute-done((bf16[192,1024]{1,0:T(8,128)(2,1)}, bf16[192,1024]{1,0:T(8,128)(2,1)S(1)}, u32[]{:S(2)}, u32[]{:S(2)}) %collective-permute-start.18) | collective-permute-done | bytes 393248 | tf_op jit(solution)/shard_map/ppermute | solution.py:224
  124.1 1.6 %fusion.77 = bf16[192,1024]{1,0:T(8,128)(2,1)} fusion(f32[192,1024]{1,0:T(8,128)S(1)} %fusion, bf16[192,1024]{1,0:T(8,128)(2,1)S(1)} %shard_map.80.refs_0_, bf16[1024,2048]{1,0:T(8,128)(2,1)S(1)} %copy-done.11, s32[]{:T(128)S(6)} %select_n.8, bf16[192,1024]{1,0:T(8,128)(2,1)S(1)} %collective-permute-done.18), kind=kOutput, calls=%fused_computation.47 | convolution fusion | flops 403439616 | bytes 4063236 | tf_op jit(solution)/shard_map/dot_general | solution.py:35
  (67 shorter events, 11.4 us)
Async XLA Ops:
  7.2 49.7 %all-gather.3.cloned.1.call-start = ((), (), s32[]{:S(2)}) async-start(), calls=%async_computation | async-start | bytes 3932160 | tf_op jit(solution)/shard_map/all_gather | solution.py:173
  7.2 8.1 %collective-permute-start = (bf16[2048,1024]{1,0:T(8,128)(2,1)}, bf16[2048,1024]{1,0:T(8,128)(2,1)}, u32[]{:S(2)}, u32[]{:S(2)}) collective-permute-start(bf16[2048,1024]{1,0:T(8,128)(2,1)} %param.9), channel_id=1, source_target_pairs={{0,4},{4,0},{8,12},{12,8},{1,5},{5,1},{9,13},{13,9},{2,6},{6,2},{1... | collective-permute-start | bytes 12582920 | tf_op jit(solution)/shard_map/ppermute | solution.py:175
  7.9 103.4 %all-gather.5.cloned.1.call-start = ((), (), s32[]{:S(2)}) async-start(), calls=%async_computation.1 | async-start | bytes 1966080 | tf_op jit(solution)/shard_map/all_gather | solution.py:213
  7.9 7.3 %collective-permute-start.1 = (bf16[192,1024]{1,0:T(8,128)(2,1)}, bf16[192,1024]{1,0:T(8,128)(2,1)S(1)}, u32[]{:S(2)}, u32[]{:S(2)}) collective-permute-start(bf16[192,1024]{1,0:T(8,128)(2,1)} %refs_0_.1), channel_id=1, source_target_pairs={{0,4},{4,0},{8,12},{12,8},{1,5},{5,1},{9,13},{13,9},{2,6},{6,2},{1... | collective-permute-start | bytes 1179656 | tf_op jit(solution)/shard_map/ppermute | solution.py:184
  8.5 14.6 %collective-permute-start.3 = (bf16[192,1024]{1,0:T(8,128)(2,1)}, bf16[192,1024]{1,0:T(8,128)(2,1)S(1)}, u32[]{:S(2)}, u32[]{:S(2)}) collective-permute-start(bf16[192,1024]{1,0:T(8,128)(2,1)} %refs_0_.1), channel_id=1, source_target_pairs={{0,1},{1,2},{2,3},{3,0},{4,5},{5,6},{6,7},{7,4},{8,9},{9,10},{10,1... | collective-permute-start | bytes 1179656 | tf_op jit(solution)/shard_map/ppermute | solution.py:203
  13.6 13.7 %copy-start.12 = (bf16[2048,1024]{1,0:T(8,128)(2,1)S(1)}, bf16[2048,1024]{1,0:T(8,128)(2,1)}, u32[]{:S(2)}) copy-start(bf16[2048,1024]{1,0:T(8,128)(2,1)} %param.9) | copy-start | bytes 12582916
  23.1 1.7 %collective-permute-start.5 = (bf16[192,1024]{1,0:T(8,128)(2,1)S(1)}, bf16[192,1024]{1,0:T(8,128)(2,1)S(1)}, u32[]{:S(2)}, u32[]{:S(2)}) collective-permute-start(bf16[192,1024]{1,0:T(8,128)(2,1)S(1)} %collective-permute-done.3.refs_1_), channel_id=1, source_target_pairs={{0,4},{4,0},{8,12},{12,8},{1,5},{5,1},{9,13},{13,9},{2,6},{6,2},{1... | collective-permute-start | bytes 1179656 | tf_op jit(solution)/shard_map/ppermute | solution.py:184
  23.1 13.3 %collective-permute-start.4 = (bf16[192,1024]{1,0:T(8,128)(2,1)S(1)}, bf16[192,1024]{1,0:T(8,128)(2,1)S(1)}, u32[]{:S(2)}, u32[]{:S(2)}) collective-permute-start(bf16[192,1024]{1,0:T(8,128)(2,1)S(1)} %collective-permute-done.3.refs_1_), channel_id=1, source_target_pairs={{0,1},{1,2},{2,3},{3,0},{4,5},{5,6},{6,7},{7,4},{8,9},{9,10},{10,1... | collective-permute-start | bytes 1179656 | tf_op jit(solution)/shard_map/ppermute | solution.py:211
  23.1 20.2 %collective-permute-start.2 = (bf16[192,1024]{1,0:T(8,128)(2,1)S(1)}, bf16[192,1024]{1,0:T(8,128)(2,1)S(1)}, u32[]{:S(2)}, u32[]{:S(2)}) collective-permute-start(bf16[192,1024]{1,0:T(8,128)(2,1)S(1)} %get-tuple-element.29), channel_id=1, source_target_pairs={{0,8},{4,12},{8,0},{12,4},{1,9},{5,13},{9,1},{13,5},{2,10},{6,14},... | collective-permute-start | bytes 1179656 | tf_op jit(solution)/shard_map/ppermute | solution.py:188
  43.3 13.6 %copy-start.6 = (bf16[192,1024]{1,0:T(8,128)(2,1)}, bf16[192,1024]{1,0:T(8,128)(2,1)S(1)}, u32[]{:S(2)}) copy-start(bf16[192,1024]{1,0:T(8,128)(2,1)S(1)} %collective-permute-done.2.refs_0_) | copy-start | bytes 1179652
  43.3 2.8 %collective-permute-start.7 = (bf16[192,1024]{1,0:T(8,128)(2,1)S(1)}, bf16[192,1024]{1,0:T(8,128)(2,1)S(1)}, u32[]{:S(2)}, u32[]{:S(2)}) collective-permute-start(bf16[192,1024]{1,0:T(8,128)(2,1)S(1)} %collective-permute-done.4.refs_2_), channel_id=1, source_target_pairs={{0,4},{4,0},{8,12},{12,8},{1,5},{5,1},{9,13},{13,9},{2,6},{6,2},{1... | collective-permute-start | bytes 1179656 | tf_op jit(solution)/shard_map/ppermute | solution.py:184
  43.4 12.7 %collective-permute-start.8 = (bf16[192,1024]{1,0:T(8,128)(2,1)}, bf16[192,1024]{1,0:T(8,128)(2,1)S(1)}, u32[]{:S(2)}, u32[]{:S(2)}) collective-permute-start(bf16[192,1024]{1,0:T(8,128)(2,1)} %get-tuple-element.31), channel_id=1, source_target_pairs={{0,8},{4,12},{8,0},{12,4},{1,9},{5,13},{9,1},{13,5},{2,10},{6,14},... | collective-permute-start | bytes 1179656 | tf_op jit(solution)/shard_map/ppermute | solution.py:188
  44.9 16.8 %collective-permute-start.6 = (bf16[192,1024]{1,0:T(8,128)(2,1)S(1)}, bf16[192,1024]{1,0:T(8,128)(2,1)}, u32[]{:S(2)}, u32[]{:S(2)}) collective-permute-start(bf16[192,1024]{1,0:T(8,128)(2,1)S(1)} %collective-permute-done.4.refs_2_), channel_id=1, source_target_pairs={{0,1},{1,2},{2,3},{3,0},{4,5},{5,6},{6,7},{7,4},{8,9},{9,10},{10,1... | collective-permute-start | bytes 1179656 | tf_op jit(solution)/shard_map/ppermute | solution.py:211
  56.9 2.0 %copy-start = (bf16[768,2048]{1,0:T(8,128)(2,1)S(1)}, bf16[768,2048]{1,0:T(8,128)(2,1)}, u32[]{:S(2)}) copy-start(bf16[768,2048]{1,0:T(8,128)(2,1)} %all-gather.3.cloned.1.call-done.pre_ref) | copy-start | bytes 9437188
  61.0 3.4 %collective-permute-start.12 = (bf16[192,1024]{1,0:T(8,128)(2,1)S(1)}, bf16[192,1024]{1,0:T(8,128)(2,1)S(1)}, u32[]{:S(2)}, u32[]{:S(2)}) collective-permute-start(bf16[192,1024]{1,0:T(8,128)(2,1)S(1)} %shard_map.76.refs_1_), channel_id=1, source_target_pairs={{0,4},{4,0},{8,12},{12,8},{1,5},{5,1},{9,13},{13,9},{2,6},{6,2},{1... | collective-permute-start | bytes 1179656 | tf_op jit(solution)/shard_map/ppermute | solution.py:196
  61.4 13.3 %collective-permute-start.11 = (bf16[192,1024]{1,0:T(8,128)(2,1)}, bf16[192,1024]{1,0:T(8,128)(2,1)S(1)}, u32[]{:S(2)}, u32[]{:S(2)}) collective-permute-start(bf16[192,1024]{1,0:T(8,128)(2,1)} %get-tuple-element.33), channel_id=1, source_target_pairs={{0,8},{4,12},{8,0},{12,4},{1,9},{5,13},{9,1},{13,5},{2,10},{6,14},... | collective-permute-start | bytes 1179656 | tf_op jit(solution)/shard_map/ppermute | solution.py:188
  61.7 6.9 %collective-permute-start.9 = (bf16[192,1024]{1,0:T(8,128)(2,1)}, bf16[192,1024]{1,0:T(8,128)(2,1)S(1)}, u32[]{:S(2)}, u32[]{:S(2)}) collective-permute-start(bf16[192,1024]{1,0:T(8,128)(2,1)} %collective-permute-done.6.refs_3_), channel_id=1, source_target_pairs={{0,4},{4,0},{8,12},{12,8},{1,5},{5,1},{9,13},{13,9},{2,6},{6,2},{1... | collective-permute-start | bytes 1179656 | tf_op jit(solution)/shard_map/ppermute | solution.py:184
  64.4 6.7 %copy-start.13 = (bf16[2048,1024]{1,0:T(8,128)(2,1)S(1)}, bf16[2048,1024]{1,0:T(8,128)(2,1)}, u32[]{:S(2)}) copy-start(bf16[2048,1024]{1,0:T(8,128)(2,1)} %param.9) | copy-start | bytes 12582916
  64.4 8.7 %copy-start.3 = (bf16[192,1024]{1,0:T(8,128)(2,1)}, bf16[192,1024]{1,0:T(8,128)(2,1)S(1)}, u32[]{:S(2)}) copy-start(bf16[192,1024]{1,0:T(8,128)(2,1)S(1)} %collective-permute-done.12.refs_5_) | copy-start | bytes 1179652
  67.1 7.6 %copy-start.1 = (bf16[768,2048]{1,0:T(8,128)(2,1)S(1)}, bf16[768,2048]{1,0:T(8,128)(2,1)}, u32[]{:S(2)}) copy-start(bf16[768,2048]{1,0:T(8,128)(2,1)} %all-gather.3.cloned.1.call-done.pre_ref) | copy-start | bytes 9437188
  67.1 22.1 %collective-permute-start.14 = (bf16[192,1024]{1,0:T(8,128)(2,1)S(1)}, bf16[192,1024]{1,0:T(8,128)(2,1)S(1)}, u32[]{:S(2)}, u32[]{:S(2)}) collective-permute-start(bf16[192,1024]{1,0:T(8,128)(2,1)S(1)} %fusion.74), channel_id=1, source_target_pairs={{0,1},{1,2},{2,3},{3,0},{4,5},{5,6},{6,7},{7,4},{8,9},{9,10},{10,1... | collective-permute-start | bytes 1179656 | tf_op jit(solution)/shard_map/ppermute | solution.py:221
  71.1 4.8 %copy-start.2 = (bf16[192,1024]{1,0:T(8,128)(2,1)S(1)}, bf16[192,1024]{1,0:T(8,128)(2,1)}, u32[]{:S(2)}) copy-start(bf16[192,1024]{1,0:T(8,128)(2,1)} %refs_0_.1) | copy-start | bytes 1179652
  73.1 16.9 %collective-permute-start.10 = (bf16[192,1024]{1,0:T(8,128)(2,1)S(1)}, bf16[192,1024]{1,0:T(8,128)(2,1)S(1)}, u32[]{:S(2)}, u32[]{:S(2)}) collective-permute-start(bf16[192,1024]{1,0:T(8,128)(2,1)S(1)} %get-tuple-element.35), channel_id=1, source_target_pairs={{0,8},{4,12},{8,0},{12,4},{1,9},{5,13},{9,1},{13,5},{2,10},{6,14},... | collective-permute-start | bytes 1179656 | tf_op jit(solution)/shard_map/ppermute | solution.py:188
  75.8 10.2 %copy-start.10 = (bf16[1024,2048]{1,0:T(8,128)(2,1)S(1)}, bf16[1024,2048]{1,0:T(8,128)(2,1)}, u32[]{:S(2)}) copy-start(bf16[1024,2048]{1,0:T(8,128)(2,1)} %param.8) | copy-start | bytes 12582916
  75.8 11.1 %collective-permute-start.13 = (bf16[192,1024]{1,0:T(8,128)(2,1)S(1)}, bf16[192,1024]{1,0:T(8,128)(2,1)S(1)}, u32[]{:S(2)}, u32[]{:S(2)}) collective-permute-start(bf16[192,1024]{1,0:T(8,128)(2,1)S(1)} %shard_map.77.refs_2_), channel_id=1, source_target_pairs={{0,4},{4,0},{8,12},{12,8},{1,5},{5,1},{9,13},{13,9},{2,6},{6,2},{1... | collective-permute-start | bytes 1179656 | tf_op jit(solution)/shard_map/ppermute | solution.py:196
  86.9 10.2 %copy-start.7 = (bf16[192,1024]{1,0:T(8,128)(2,1)S(1)}, bf16[192,1024]{1,0:T(8,128)(2,1)}, u32[]{:S(2)}) copy-start(bf16[192,1024]{1,0:T(8,128)(2,1)} %copy-done.6) | copy-start | bytes 1179652
  91.2 8.1 %collective-permute-start.15 = (bf16[192,1024]{1,0:T(8,128)(2,1)S(1)}, bf16[192,1024]{1,0:T(8,128)(2,1)S(1)}, u32[]{:S(2)}, u32[]{:S(2)}) collective-permute-start(bf16[192,1024]{1,0:T(8,128)(2,1)S(1)} %shard_map.79.refs_3_), channel_id=1, source_target_pairs={{0,4},{4,0},{8,12},{12,8},{1,5},{5,1},{9,13},{13,9},{2,6},{6,2},{1... | collective-permute-start | bytes 1179656 | tf_op jit(solution)/shard_map/ppermute | solution.py:196
  91.2 18.5 %collective-permute-start.16 = (bf16[192,1024]{1,0:T(8,128)(2,1)S(1)}, bf16[192,1024]{1,0:T(8,128)(2,1)S(1)}, u32[]{:S(2)}, u32[]{:S(2)}) collective-permute-start(bf16[192,1024]{1,0:T(8,128)(2,1)S(1)} %fusion.71), channel_id=1, source_target_pairs={{0,1},{1,2},{2,3},{3,0},{4,5},{5,6},{6,7},{7,4},{8,9},{9,10},{10,1... | collective-permute-start | bytes 1179656 | tf_op jit(solution)/shard_map/ppermute | solution.py:221
  98.3 13.0 %copy-start.4 = (bf16[192,1024]{1,0:T(8,128)(2,1)S(1)}, bf16[192,1024]{1,0:T(8,128)(2,1)}, u32[]{:S(2)}) copy-start(bf16[192,1024]{1,0:T(8,128)(2,1)} %copy-done.3) | copy-start | bytes 1179652
  98.3 13.0 %collective-permute-start.17 = (bf16[192,1024]{1,0:T(8,128)(2,1)S(1)}, bf16[192,1024]{1,0:T(8,128)(2,1)S(1)}, u32[]{:S(2)}, u32[]{:S(2)}) collective-permute-start(bf16[192,1024]{1,0:T(8,128)(2,1)S(1)} %shard_map.80.refs_0_), channel_id=1, source_target_pairs={{0,4},{4,0},{8,12},{12,8},{1,5},{5,1},{9,13},{13,9},{2,6},{6,2},{1... | collective-permute-start | bytes 1179656 | tf_op jit(solution)/shard_map/ppermute | solution.py:196
  111.3 12.8 %collective-permute-start.18 = (bf16[192,1024]{1,0:T(8,128)(2,1)}, bf16[192,1024]{1,0:T(8,128)(2,1)S(1)}, u32[]{:S(2)}, u32[]{:S(2)}) collective-permute-start(bf16[192,1024]{1,0:T(8,128)(2,1)} %fusion.68), channel_id=1, source_target_pairs={{0,1},{1,2},{2,3},{3,0},{4,5},{5,6},{6,7},{7,4},{8,9},{9,10},{10,1... | collective-permute-start | bytes 1179656 | tf_op jit(solution)/shard_map/ppermute | solution.py:224
  112.8 6.7 %copy-start.11 = (bf16[1024,2048]{1,0:T(8,128)(2,1)S(1)}, bf16[1024,2048]{1,0:T(8,128)(2,1)}, u32[]{:S(2)}) copy-start(bf16[1024,2048]{1,0:T(8,128)(2,1)} %param.8) | copy-start | bytes 12582916
  (3 other events, 3.2 us)
Sparse Core Ops, SparseCore 0:
  9.6 40.6 all-gather.2
  51.9 45.0 all-gather.4

commit v4 on v3

v4 whole, which is shorter than its diff:
```python
import functools
import math

import jax
import jax.numpy as jnp
from jax import lax
from jax.experimental import pallas as pl
from jax.experimental.pallas import tpu as pltpu
from jax.sharding import PartitionSpec as P

LAST = (((1,), (1,)), ((), ()))
FIRST = (((0,), (0,)), ((), ()))
MIB = 1024 * 1024
LITTLE = pl.CostEstimate(flops=1024, bytes_accessed=1024, transcendentals=0)


def gelu_parts(values):
    v = values.astype(jnp.float32)
    tanh_val = jnp.tanh(0.7978845608 * (v + 0.044715 * v * v * v))
    return v, tanh_val


def gelu(values):
    v, tanh_val = gelu_parts(values)
    return 0.5 * v * (1.0 + tanh_val)


def gelu_slope(values):
    v, tanh_val = gelu_parts(values)
    return 0.5 * (1.0 + tanh_val) + 0.5 * v * (1.0 - tanh_val * tanh_val) * 0.7978845608 * (
        1.0 + 3.0 * 0.044715 * v * v
    )


def dot(a, b, dims):
    return lax.dot_general(a, b, dims, preferred_element_type=jnp.float32)


def after(value, *first):
    return lax.optimization_barrier((value, *first))[0]


def tile_of(extent):
    return next(t for t in (256, 128, extent) if extent % t == 0)


def in_vmem():
    return pl.BlockSpec(memory_space=pltpu.VMEM)


def grad_down_kernel(blocks, scale, at_ref, pre_ref, *refs):
    cot_refs, out_ref, cots = refs[:blocks], refs[-2], refs[-1]
    tokens = cot_refs[0].shape[0]

    @pl.when(pl.program_id(0) == 0)
    def _():
        for s in range(blocks):
            cots[pl.ds(pl.multiple_of(at_ref[s] * tokens, tokens), tokens), :] = cot_refs[s][...]

    activation = gelu(pre_ref[...]).astype(jnp.bfloat16)
    out_ref[...] = dot(activation, cots[...], FIRST) * scale


def grad_down_call(at, pre_all, cots, scale, second=None):
    total, hidden = pre_all.shape
    features = cots[0].shape[1]
    tile = tile_of(hidden // 2)
    steps = hidden // 2 // tile
    skip = 0 if second is None else steps
    rest = [] if second is None else [second]
    return pl.pallas_call(
        functools.partial(grad_down_kernel, len(cots), scale),
        out_shape=jax.ShapeDtypeStruct((hidden, features), jnp.float32),
        grid_spec=pltpu.PrefetchScalarGridSpec(
            num_scalar_prefetch=1,
            grid=(steps,),
            in_specs=[pl.BlockSpec((total, tile), lambda i, at: (0, i + skip))]
            + [in_vmem() for _ in cots]
            + [pl.BlockSpec(memory_space=pl.ANY) for _ in rest],
            out_specs=pl.BlockSpec((tile, features), lambda i, at: (i + skip, 0)),
            scratch_shapes=[pltpu.VMEM((total, features), jnp.bfloat16)],
        ),
        input_output_aliases={2 + len(cots): 0} if rest else {},
        compiler_params=pltpu.CompilerParams(vmem_limit_bytes=16 * MIB),
        cost_estimate=LITTLE,
    )(at, pre_all, *cots, *rest)


def grad_up_kernel(blocks, scale, at_ref, *refs):
    ins, mine, pair = (refs[i * blocks : (i + 1) * blocks] for i in range(3))
    out_ref, inputs, grads = refs[3 * blocks :]
    tokens, half = mine[0].shape
    tile = out_ref.shape[0]

    @pl.when(pl.program_id(0) == 0)
    def _():
        core = at_ref[blocks]
        left = pl.ds(pl.multiple_of(core * half, half), half)
        right = pl.ds(pl.multiple_of((1 - core) * half, half), half)
        for s in range(blocks):
            here = pl.ds(s * tokens, tokens)
            inputs[here, :] = ins[s][...]
            grads[here, left] = mine[s][...]
            grads[here, right] = pair[s][...]

    columns = pl.ds(pl.multiple_of(pl.program_id(0) * tile, tile), tile)
    out_ref[...] = dot(inputs[:, columns], grads[...], FIRST) * scale


def grad_up_call(at, ins, mine, pair, scale):
    tokens, features = ins[0].shape
    total = tokens * len(ins)
    hidden = 2 * mine[0].shape[1]
    tile = tile_of(features)
    return pl.pallas_call(
        functools.partial(grad_up_kernel, len(mine), scale),
        out_shape=jax.ShapeDtypeStruct((features, hidden), jnp.float32),
        grid_spec=pltpu.PrefetchScalarGridSpec(
            num_scalar_prefetch=1,
            grid=(features // tile,),
            in_specs=[in_vmem() for _ in ins + mine + pair],
            out_specs=pl.BlockSpec((tile, hidden), lambda i, at: (i, 0)),
            scratch_shapes=[
                pltpu.VMEM((total, features), jnp.bfloat16),
                pltpu.VMEM((total, hidden), jnp.bfloat16),
            ],
        ),
        compiler_params=pltpu.CompilerParams(vmem_limit_bytes=20 * MIB),
        cost_estimate=LITTLE,
    )(at, *ins, *mine, *pair)


def lay_out_kernel(at_ref, *refs):
    out_ref = refs[-1]
    tokens = refs[0].shape[0]
    for i, ref in enumerate(refs[:-1]):
        out_ref[pl.ds(pl.multiple_of(at_ref[i] * tokens, tokens), tokens), :] = ref[...]


def lay_out_call(places, blocks):
    tokens, hidden = blocks[0].shape
    return pl.pallas_call(
        lay_out_kernel,
        out_shape=jax.ShapeDtypeStruct((tokens * len(blocks), hidden), jnp.bfloat16),
        grid_spec=pltpu.PrefetchScalarGridSpec(
            num_scalar_prefetch=1,
            grid=(1,),
            in_specs=[in_vmem() for _ in blocks],
            out_specs=in_vmem(),
        ),
        compiler_params=pltpu.CompilerParams(vmem_limit_bytes=8 * MIB),
        cost_estimate=LITTLE,
    )(places, *blocks)


def pre_grad_kernel(at_ref, pre_ref, part_ref, *refs):
    out_ref = refs[-1]
    tokens, half = part_ref.shape
    rows = 64
    columns = pl.ds(pl.multiple_of(at_ref[1] * half, half), half)
    for first in range(0, tokens, rows):
        here = pl.ds(first, rows)
        total = part_ref[here, :]
        for other in refs[:-1]:
            total = total + other[here, :].astype(jnp.float32)
        place = pl.ds(pl.multiple_of(at_ref[0] * tokens + first, rows), rows)
        out_ref[here, :] = (total * gelu_slope(pre_ref[place, columns])).astype(jnp.bfloat16)


def pre_grad_call(at, core, pre_all, part, others):
    tokens, half = part.shape
    return pl.pallas_call(
        pre_grad_kernel,
        out_shape=jax.ShapeDtypeStruct((tokens, half), jnp.bfloat16),
        grid_spec=pltpu.PrefetchScalarGridSpec(
            num_scalar_prefetch=1,
            grid=(1,),
            in_specs=[in_vmem() for _ in [pre_all, part] + others],
            out_specs=in_vmem(),
        ),
        compiler_params=pltpu.CompilerParams(vmem_limit_bytes=8 * MIB),
        cost_estimate=LITTLE,
    )(jnp.stack([at, core]).astype(jnp.int32), pre_all, part, *others)


def hidden_kernel(core_ref, cot_ref, pair_ref, mine_ref, theirs_ref, part_ref, sent_ref):
    half = part_ref.shape[1]
    tile = tile_of(half)
    for first in range(0, half, tile):
        rows = pl.ds(pl.multiple_of(core_ref[0] * half + first, tile), tile)
        part = dot(cot_ref[...], mine_ref[rows, :], LAST)
        part = part + dot(pair_ref[...], theirs_ref[rows, :], LAST)
        part_ref[:, pl.ds(first, tile)] = part
        sent_ref[:, pl.ds(first, tile)] = part.astype(jnp.bfloat16)


def hidden_call(core, cot, cot_pair, down_mine, down_pair):
    shape = (cot.shape[0], down_mine.shape[0] // 2)
    return pl.pallas_call(
        hidden_kernel,
        out_shape=[
            jax.ShapeDtypeStruct(shape, jnp.float32),
            jax.ShapeDtypeStruct(shape, jnp.bfloat16),
        ],
        grid_spec=pltpu.PrefetchScalarGridSpec(
            num_scalar_prefetch=1,
            grid=(1,),
            in_specs=[in_vmem() for _ in range(4)],
            out_specs=[in_vmem(), in_vmem()],
        ),
        compiler_params=pltpu.CompilerParams(vmem_limit_bytes=20 * MIB),
        cost_estimate=LITTLE,
    )(core, cot, cot_pair, down_mine, down_pair)


def share_kernel(core_ref, mine_ref, theirs_ref, up_ref, *refs):
    out_ref = refs[-1]
    features, half = up_ref.shape[0], mine_ref.shape[1]
    tile = tile_of(features)
    left = pl.ds(pl.multiple_of(core_ref[0] * half, half), half)
    right = pl.ds(pl.multiple_of((1 - core_ref[0]) * half, half), half)
    for first in range(0, features, tile):
        here = pl.ds(first, tile)
        total = dot(mine_ref[...], up_ref[here, left], LAST)
        total = total + dot(theirs_ref[...], up_ref[here, right], LAST)
        for arrived in refs[:-1]:
            total = total + arrived[:, here].astype(jnp.float32)
        out_ref[:, here] = total.astype(jnp.bfloat16)


def share_call(core, mine, theirs, up_weight, arrived):
    return pl.pallas_call(
        share_kernel,
        out_shape=jax.ShapeDtypeStruct((mine.shape[0], up_weight.shape[0]), jnp.bfloat16),
        grid_spec=pltpu.PrefetchScalarGridSpec(
            num_scalar_prefetch=1,
            grid=(1,),
            in_specs=[in_vmem() for _ in [mine, theirs, up_weight] + arrived],
            out_specs=in_vmem(),
        ),
        compiler_params=pltpu.CompilerParams(vmem_limit_bytes=16 * MIB),
        cost_estimate=LITTLE,
    )(core, mine, theirs, up_weight, *arrived)


def per_device(inputs, cotangent, preactivation, up_weight, down_weight):
    cols, rows = lax.axis_size("col"), lax.axis_size("row")
    z, r = lax.axis_index("col"), lax.axis_index("row")
    core = lax.rem(r, 2)
    tokens, features = cotangent.shape
    hidden = down_weight.shape[0]
    half = hidden // 2
    ring = [(i, (i + 1) % cols) for i in range(cols)]
    pair = [(i, i ^ 1) for i in range(rows)]
    scale = 1.0 / math.sqrt(tokens * cols)
    at = jnp.stack([lax.rem(z - s + cols, cols) for s in range(cols)] + [core]).astype(jnp.int32)

    shifts = range(2, rows, 2)
    over_x = [[(i, (i + shift) % rows) for i in range(rows)] for shift in shifts]
    places = [r] + [lax.rem(r - shift + rows, rows) for shift in shifts]
    places = jnp.stack(places + [p + 1 - 2 * lax.rem(p, 2) for p in places]).astype(jnp.int32)
    pres = [preactivation] + [lax.ppermute(preactivation, "row", to) for to in over_x]

    down_pair = lax.ppermute(down_weight, "row", pair)
    parts, others, mine, theirs = ([None] * cols for _ in range(4))

    def hidden_part(s, cot, first):
        cot_pair = after(lax.ppermute(cot, "row", pair), *first)
        parts[s], sent = hidden_call(at[cols:], cot, cot_pair, down_weight, down_pair)
        if s != 0:
            exchange(s, sent)
        return sent

    def exchange(s, sent):
        others[s] = [lax.ppermute(sent, "row", to) for to in over_x]

    def pre_grad(s, first):
        others[s][0] = after(others[s][0], *first)
        mine[s] = pre_grad_call(at[s], core, pre_all, parts[s], others[s])
        theirs[s] = lax.ppermute(mine[s], "row", pair)

    def share(s, first, arrived):
        return share_call(at[cols:], after(mine[s], *first), theirs[s], up_weight, arrived)

    cots, ins = [cotangent], [inputs]
    sent = own = hidden_part(0, cotangent, [])
    arriving = lax.ppermute(cotangent, "col", ring)
    for s in range(1, cols):
        first = [sent]
        if s == cols - 1:
            pre_all = lay_out_call(after(places, sent), pres)
            pre_grad(1, [sent])
            first = [sent, mine[1]]
        cots.append(after(arriving, *first))
        sent = hidden_part(s, cots[s], pres[1:] if s == 1 else [])
        if s == 1:
            pres = pres + [lax.ppermute(after(p, cots[1]), "row", pair) for p in pres]
        if s < cols - 1:
            arriving = lax.ppermute(cots[s], "col", ring)
        else:
            ins.append(lax.ppermute(after(inputs, cots[cols - 2]), "col", ring))
    exchange(0, after(own, sent))

    sums = share(1, [ins[1]], [])
    grad_down = grad_down_call(after(at, sums, sent), pre_all, cots, scale)
    for s in range(2, cols):
        pre_grad(s, [sums, grad_down])
        if s == 2:
            grad_down = grad_down_call(after(at, mine[s]), pre_all, cots, scale, grad_down)
        if s == cols - 1:
            pre_grad(0, [mine[s]])
        arrived = lax.ppermute(sums, "col", ring)
        ins.append(lax.ppermute(ins[-1], "col", ring))
        first = [ins[-1]] + ([grad_down] if s == 2 else [])
        sums = share(s, first, [arrived])
    arrived = lax.ppermute(sums, "col", ring)
    grad_up = grad_up_call(after(at, sums), ins, mine, theirs, scale)
    sums = share(0, [grad_up], [arrived])
    return (sums, grad_up, grad_down)


def solution(mesh):
    placed = (
        P(("groups", "col"), "row"),
        P(("groups", "col"), "row"),
        P(("groups", "row"), "col"),
        P("row", "col"),
        P("col", "row"),
    )
    return jax.shard_map(
        per_device,
        mesh=mesh,
        in_specs=placed,
        out_specs=(
            P(("groups", "col"), "row"),
            P(("groups", "row"), "col"),
            P(("groups", "col"), "row"),
        ),
        check_vma=False,
    )
```

time: 133 us -> 120 us (0.902)
  Pallas kernels: 21.3 us -> 53.7 us
  matrix products: 30.8 us -> 0 us
  between operations: 14.3 us -> 0.87 us
  local copies, waits for them, and re-layouts: 5.31 us -> 13.5 us
  waiting for transfers between devices: 42.7 us -> 35.9 us
  starting transfers between devices: 17.9 us -> 14.8 us
    dot_general x16 -> x0, matrix products: 30.8 us -> none  [dot(): return lax.dot_general(a, b, dims, preferred_element_type=jnp.float32)]
    pallas_call x0 -> x9, Pallas kernels: none -> 26.1 us  [the longest x4 17.3 us: hidden_call(): pl.pallas_call(hidden_kernel, out_shape=[jax.ShapeDtypeStruct(shape, jnp....]
    unnamed x28 -> x48, local copies, waits for them, and re-layouts: 5.23 us -> 13.5 us
    ppermute x3, starting transfers between devices: 7.43 us -> 0.32 us  [per_device(): arrived = lax.ppermute(sums, 'col', ring)]
    ppermute x1, waiting for transfers between devices: 5.32 us -> 0.64 us  [per_device(): arriving = lax.ppermute(cotangent, 'col', ring)]
    ppermute x2, waiting for transfers between devices: 7.49 us -> 3.56 us  [per_device(): arriving = lax.ppermute(cots[s], 'col', ring)]
    ppermute x8 -> x14, starting transfers between devices: 5.72 us -> 9.33 us  [the longest x4 4.34 us: exchange(): others[s] = [lax.ppermute(sent, 'row', to) for to in over_x]]
    pallas_call x4, Pallas kernels: 4.49 us -> 7.22 us  [pre_grad_call(): pl.pallas_call(pre_grad_kernel, out_shape=jax.ShapeDtypeStruct((tokens, h...]
  transfers between devices with their start and end apart: 21 -> 25, of which waited for: 9 -> 11; matrix products, arithmetic and copies ran while one was open for 22% -> 0% of each run, Pallas kernels for 16% -> 43%
where the time goes in v4:
time: 120 us; the launch traced here: 119 us
  Pallas kernels  53.7 us (45%)
  waiting for transfers between devices  35.9 us (30%)
  starting transfers between devices  14.8 us (12%)
  local copies, waits for them, and re-layouts  13.5 us (11%)
    pallas_call x4, Pallas kernels, hidden_call(): pl.pallas_call(hidden_kernel, out_shape=[jax.ShapeDtypeStruct(shape, jnp....  17.3 us
    ppermute x3, waiting for transfers between devices, per_device(): arrived = lax.ppermute(sums, 'col', ring)  16.9 us
    unnamed x48, local copies, waits for them, and re-layouts  13.5 us
    pallas_call x2, Pallas kernels, grad_down_call(): pl.pallas_call(functools.partial(grad_down_kernel, len(cots), scale), out...  12.4 us
    pallas_call x4, Pallas kernels, share_call(): pl.pallas_call(share_kernel, out_shape=jax.ShapeDtypeStruct((mine.shape[0...  8.04 us
    pallas_call x1, Pallas kernels, grad_up_call(): pl.pallas_call(functools.partial(grad_up_kernel, len(mine), scale), out_s...  7.88 us
    pallas_call x4, Pallas kernels, pre_grad_call(): pl.pallas_call(pre_grad_kernel, out_shape=jax.ShapeDtypeStruct((tokens, h...  7.22 us
    ppermute x4, starting transfers between devices, exchange(): others[s] = [lax.ppermute(sent, 'row', to) for to in over_x]  4.34 us
  transfers between devices with their start and end apart: 25, of which 11 were waited for; matrix products, arithmetic and copies ran while one was open for 0% of the time, Pallas kernels for 43%

profile of v4, /device:TPU:0, one launch (start us, length us, event | category | flops | bytes accessed | tf_op | source)
XLA Modules:
  0.0 119.2 jit_solution(6345715236340102102)
XLA Ops:
  1.1 2.6 %collective-permute-start.5 = (bf16[192,2048]{1,0:T(8,128)(2,1)}, bf16[192,2048]{1,0:T(8,128)(2,1)S(1)}, u32[]{:S(2)}, u32[]{:S(2)}) collective-permute-start(bf16[192,2048]{1,0:T(8,128)(2,1)} %refs_0_.4), channel_id=1, source_target_pairs={{0,8},{4,12},{8,0},{12,4},{1,9},{5,13},{9,1},{13,5},{2,10},{6,14},... | collective-permute-start | bytes 2359304 | tf_op jit(solution)/shard_map/ppermute | solution.py:262
  3.9 1.6 %collective-permute-start = (bf16[192,1024]{1,0:T(8,128)(2,1)}, bf16[192,1024]{1,0:T(8,128)(2,1)S(1)}, u32[]{:S(2)}, u32[]{:S(2)}) collective-permute-start(bf16[192,1024]{1,0:T(8,128)(2,1)} %refs_0_.6), channel_id=1, source_target_pairs={{0,1},{1,2},{2,3},{3,0},{4,5},{5,6},{6,7},{7,4},{8,9},{9,10},{10,1... | collective-permute-start | bytes 1179656 | tf_op jit(solution)/shard_map/ppermute | solution.py:287
  5.5 3.3 %collective-permute-done.1.pair_ref = bf16[192,1024]{1,0:T(8,128)(2,1)S(1)} collective-permute-done((bf16[192,1024]{1,0:T(8,128)(2,1)}, bf16[192,1024]{1,0:T(8,128)(2,1)S(1)}, u32[]{:S(2)}, u32[]{:S(2)}) %collective-permute-start.1) | collective-permute-done | bytes 393248 | tf_op jit(solution)/shard_map/ppermute | solution.py:268
  8.7 2.2 %copy-done = bf16[2048,1024]{1,0:T(8,128)(2,1)S(1)} copy-done((bf16[2048,1024]{1,0:T(8,128)(2,1)S(1)}, bf16[2048,1024]{1,0:T(8,128)(2,1)}, u32[]{:S(2)}) %copy-start) | copy-done | bytes 4194328
  11.9 3.9 %shard_map.76 = (f32[192,1024]{1,0:T(8,128)S(1)}, bf16[192,1024]{1,0:T(8,128)(2,1)S(1)}) custom-call(s32[1]{0:T(128)} %bitcast.core_ref, bf16[192,1024]{1,0:T(8,128)(2,1)S(1)} %copy-done.5, bf16[192,1024]{1,0:T(8,128)(2,1)S(1)} %collective-permute-done.1.pair_ref, bf16[2048,1024]{1,0:T(8,128)(2,1)S(1)} %copy-done, ...), custom_call_target="tpu_custom_call" | custom-call | flops 1024 | bytes 1024 | tf_op jit(solution)/shard_map/pallas_call | solution.py:199
  17.3 2.5 %collective-permute-start.3 = (bf16[192,1024]{1,0:T(8,128)(2,1)S(1)}, bf16[192,1024]{1,0:T(8,128)(2,1)}, u32[]{:S(2)}, u32[]{:S(2)}) collective-permute-start(bf16[192,1024]{1,0:T(8,128)(2,1)S(1)} %collective-permute-done.cot_ref.refs_1_), channel_id=1, source_target_pairs={{0,1},{1,2},{2,3},{3,0},{4,5},{5,6},{6,7},{7,4},{8,9},{9,10},{10,1... | collective-permute-start | bytes 1179656 | tf_op jit(solution)/shard_map/ppermute | solution.py:299
  19.8 2.3 %collective-permute-done.5.refs_1_ = bf16[192,2048]{1,0:T(8,128)(2,1)S(1)} collective-permute-done((bf16[192,2048]{1,0:T(8,128)(2,1)}, bf16[192,2048]{1,0:T(8,128)(2,1)S(1)}, u32[]{:S(2)}, u32[]{:S(2)}) %collective-permute-start.5) | collective-permute-done | bytes 786464 | tf_op jit(solution)/shard_map/ppermute | solution.py:262
  22.6 4.5 %shard_map.77 = (f32[192,1024]{1,0:T(8,128)S(1)}, bf16[192,1024]{1,0:T(8,128)(2,1)}) custom-call(s32[1]{0:T(128)} %bitcast.core_ref, bf16[192,1024]{1,0:T(8,128)(2,1)S(1)} %collective-permute-done.cot_ref.refs_1_, bf16[192,1024]{1,0:T(8,128)(2,1)S(1)} %collective-permute-done.4.pair_ref, bf16[2048,1024]{1,0:T(8,128)(2,1)S(1)} %copy-done.1, ...), custom_call_target="tpu_custom_call" | custom-call | flops 1024 | bytes 1024 | tf_op jit(solution)/shard_map/pallas_call | solution.py:199
  28.0 3.6 %collective-permute-done.3.cot_ref.refs_2_ = bf16[192,1024]{1,0:T(8,128)(2,1)} collective-permute-done((bf16[192,1024]{1,0:T(8,128)(2,1)S(1)}, bf16[192,1024]{1,0:T(8,128)(2,1)}, u32[]{:S(2)}, u32[]{:S(2)}) %collective-permute-start.3) | collective-permute-done | bytes 393248 | tf_op jit(solution)/shard_map/ppermute | solution.py:299
  31.5 1.6 %collective-permute-start.10 = (bf16[192,1024]{1,0:T(8,128)(2,1)}, bf16[192,1024]{1,0:T(8,128)(2,1)}, u32[]{:S(2)}, u32[]{:S(2)}) collective-permute-start(bf16[192,1024]{1,0:T(8,128)(2,1)} %get-tuple-element.34), channel_id=1, source_target_pairs={{0,8},{4,12},{8,0},{12,4},{1,9},{5,13},{9,1},{13,5},{2,10},{6,14},... | collective-permute-start | bytes 1179656 | tf_op jit(solution)/shard_map/ppermute | solution.py:275
  34.5 2.2 %copy-done.2 = bf16[2048,1024]{1,0:T(8,128)(2,1)S(1)} copy-done((bf16[2048,1024]{1,0:T(8,128)(2,1)S(1)}, bf16[2048,1024]{1,0:T(8,128)(2,1)}, u32[]{:S(2)}) %copy-start.2) | copy-done | bytes 4194328
  36.7 4.8 %shard_map.78 = (f32[192,1024]{1,0:T(8,128)S(1)}, bf16[192,1024]{1,0:T(8,128)(2,1)}) custom-call(s32[1]{0:T(128)} %bitcast.core_ref, bf16[192,1024]{1,0:T(8,128)(2,1)} %collective-permute-done.3.cot_ref.refs_2_, bf16[192,1024]{1,0:T(8,128)(2,1)} %collective-permute-done.6.pair_ref, bf16[2048,1024]{1,0:T(8,128)(2,1)S(1)} %copy-done.2, ...), custom_call_target="tpu_custom_call" | custom-call | flops 1024 | bytes 1024 | tf_op jit(solution)/shard_map/pallas_call | solution.py:199
  43.4 1.1 copy-done.16
  44.5 1.1 copy-done.20
  46.4 2.9 %shard_map.80.mine_ref.refs_5_ = bf16[192,1024]{1,0:T(8,128)(2,1)} custom-call(s32[2]{0:T(128)S(1)} %pad_add_fusion.2.at_ref, bf16[768,2048]{1,0:T(8,128)(2,1)S(1)} %shard_map.79.pre_ref, f32[192,1024]{1,0:T(8,128)S(1)} %copy-done.18, bf16[192,1024]{1,0:T(8,128)(2,1)} %collective-permute-done.10.refs_0_), custom_call_target="tpu_custom_call" | custom-call | flops 1024 | bytes 1024 | tf_op jit(solution)/shard_map/pallas_call | solution.py:172
  50.6 4.3 %collective-permute-done.15.refs_1_ = bf16[192,1024]{1,0:T(8,128)(2,1)} collective-permute-done((bf16[192,1024]{1,0:T(8,128)(2,1)}, bf16[192,1024]{1,0:T(8,128)(2,1)}, u32[]{:S(2)}, u32[]{:S(2)}) %collective-permute-start.15) | collective-permute-done | bytes 393248 | tf_op jit(solution)/shard_map/ppermute | solution.py:301
  54.9 2.2 %copy-done.3 = bf16[2048,1024]{1,0:T(8,128)(2,1)S(1)} copy-done((bf16[2048,1024]{1,0:T(8,128)(2,1)S(1)}, bf16[2048,1024]{1,0:T(8,128)(2,1)}, u32[]{:S(2)}) %copy-start.3) | copy-done | bytes 4194328
  57.1 4.1 %shard_map.81 = (f32[192,1024]{1,0:T(8,128)S(1)}, bf16[192,1024]{1,0:T(8,128)(2,1)S(1)}) custom-call(s32[1]{0:T(128)} %bitcast.core_ref, bf16[192,1024]{1,0:T(8,128)(2,1)} %collective-permute-done.9.cot_ref.refs_3_, bf16[192,1024]{1,0:T(8,128)(2,1)} %collective-permute-done.11.pair_ref, bf16[2048,1024]{1,0:T(8,128)(2,1)S(1)} %copy-done.3, ...), custom_call_target="tpu_custom_call" | custom-call | flops 1024 | bytes 1024 | tf_op jit(solution)/shard_map/pallas_call | solution.py:199
  61.2 2.7 %shard_map.82 = bf16[192,1024]{1,0:T(8,128)(2,1)S(1)} custom-call(s32[1]{0:T(128)} %bitcast.core_ref, bf16[192,1024]{1,0:T(8,128)(2,1)} %shard_map.80.mine_ref.refs_5_, bf16[192,1024]{1,0:T(8,128)(2,1)} %collective-permute-done.16.theirs_ref.refs_9_, bf16[1024,2048]{1,0:T(8,128)(2,1)S(1)} %copy-done.4), custom_call_target="tpu_custom_call" | custom-call | flops 1024 | bytes 1024 | tf_op jit(solution)/shard_map/pallas_call | solution.py:232
  64.0 6.2 %shard_map.83.refs_4_ = f32[2048,1024]{1,0:T(8,128)} custom-call(s32[5]{0:T(128)S(1)} %stack.63.at_ref, bf16[768,2048]{1,0:T(8,128)(2,1)S(1)} %shard_map.79.pre_ref, bf16[192,1024]{1,0:T(8,128)(2,1)S(1)} %copy-done.6, bf16[192,1024]{1,0:T(8,128)(2,1)S(1)} %collective-permute-done.cot_ref.refs_1_, bf16[192,1024]{1,0:T(8,128)(2,1)} %collective-permute-done.3.cot_ref.refs_2_, ...), custom_call_target="tpu_custom_call" | custom-call | flops 1024 | bytes 1024 | tf_op jit(solution)/shard_map/pallas_call | solution.py:71
  70.2 2.1 %shard_map.84.mine_ref.refs_6_ = bf16[192,1024]{1,0:T(8,128)(2,1)S(1)} custom-call(s32[2]{0:T(128)S(1)} %pad_add_fusion.4.at_ref, bf16[768,2048]{1,0:T(8,128)(2,1)S(1)} %shard_map.79.pre_ref, f32[192,1024]{1,0:T(8,128)S(1)} %copy-done.14, bf16[192,1024]{1,0:T(8,128)(2,1)} %collective-permute-done.14.refs_0_), custom_call_target="tpu_custom_call" | custom-call | flops 1024 | bytes 1024 | tf_op jit(solution)/shard_map/pallas_call | solution.py:172
  73.3 6.2 %shard_map.85 = f32[2048,1024]{1,0:T(8,128)} custom-call(s32[5]{0:T(128)S(1)} %stack.63.at_ref, bf16[768,2048]{1,0:T(8,128)(2,1)S(1)} %shard_map.79.pre_ref, bf16[192,1024]{1,0:T(8,128)(2,1)S(1)} %copy-done.6, bf16[192,1024]{1,0:T(8,128)(2,1)S(1)} %collective-permute-done.cot_ref.refs_1_, ...), custom_call_target="tpu_custom_call", output_to_operand_aliasing={{}: (6, {})} | custom-call | flops 1024 | bytes 1024 | tf_op jit(solution)/shard_map/pallas_call | solution.py:71
  79.5 1.5 %collective-permute-start.12 = (bf16[192,1024]{1,0:T(8,128)(2,1)S(1)}, bf16[192,1024]{1,0:T(8,128)(2,1)S(1)}, u32[]{:S(2)}, u32[]{:S(2)}) collective-permute-start(bf16[192,1024]{1,0:T(8,128)(2,1)S(1)} %copy-done.23), channel_id=1, source_target_pairs={{0,8},{4,12},{8,0},{12,4},{1,9},{5,13},{9,1},{13,5},{2,10},{6,14},... | collective-permute-start | bytes 1179656 | tf_op jit(solution)/shard_map/ppermute | solution.py:275
  81.9 4.4 %collective-permute-done.19.refs_0_ = bf16[192,1024]{1,0:T(8,128)(2,1)S(1)} collective-permute-done((bf16[192,1024]{1,0:T(8,128)(2,1)S(1)}, bf16[192,1024]{1,0:T(8,128)(2,1)S(1)}, u32[]{:S(2)}, u32[]{:S(2)}) %collective-permute-start.19) | collective-permute-done | bytes 393248 | tf_op jit(solution)/shard_map/ppermute | solution.py:312
  86.2 1.5 %shard_map.86 = bf16[192,1024]{1,0:T(8,128)(2,1)S(1)} custom-call(s32[1]{0:T(128)} %bitcast.core_ref, bf16[192,1024]{1,0:T(8,128)(2,1)S(1)} %shard_map.84.mine_ref.refs_6_, bf16[192,1024]{1,0:T(8,128)(2,1)S(1)} %collective-permute-done.18.theirs_ref.refs_10_, bf16[1024,2048]{1,0:T(8,128)(2,1)S(1)} %copy-done.4, ...), custom_call_target="tpu_custom_call" | custom-call | flops 1024 | bytes 1024 | tf_op jit(solution)/shard_map/pallas_call | solution.py:232
  89.1 3.2 %collective-permute-done.12.refs_0_ = bf16[192,1024]{1,0:T(8,128)(2,1)S(1)} collective-permute-done((bf16[192,1024]{1,0:T(8,128)(2,1)S(1)}, bf16[192,1024]{1,0:T(8,128)(2,1)S(1)}, u32[]{:S(2)}, u32[]{:S(2)}) %collective-permute-start.12) | collective-permute-done | bytes 393248 | tf_op jit(solution)/shard_map/ppermute | solution.py:275
  93.5 1.4 %collective-permute-done.20.refs_3_ = bf16[192,1024]{1,0:T(8,128)(2,1)S(1)} collective-permute-done((bf16[192,1024]{1,0:T(8,128)(2,1)S(1)}, bf16[192,1024]{1,0:T(8,128)(2,1)S(1)}, u32[]{:S(2)}, u32[]{:S(2)}) %collective-permute-start.20) | collective-permute-done | bytes 393248 | tf_op jit(solution)/shard_map/ppermute | solution.py:313
  94.9 8.0 %collective-permute-done.22.refs_0_ = bf16[192,1024]{1,0:T(8,128)(2,1)S(1)} collective-permute-done((bf16[192,1024]{1,0:T(8,128)(2,1)S(1)}, bf16[192,1024]{1,0:T(8,128)(2,1)S(1)}, u32[]{:S(2)}, u32[]{:S(2)}) %collective-permute-start.22) | collective-permute-done | bytes 393248 | tf_op jit(solution)/shard_map/ppermute | solution.py:312
  102.8 1.5 %shard_map.89 = bf16[192,1024]{1,0:T(8,128)(2,1)S(1)} custom-call(s32[1]{0:T(128)} %bitcast.core_ref, bf16[192,1024]{1,0:T(8,128)(2,1)S(1)} %shard_map.87.mine_ref.refs_7_, bf16[192,1024]{1,0:T(8,128)(2,1)S(1)} %collective-permute-done.21.theirs_ref.refs_11_, bf16[1024,2048]{1,0:T(8,128)(2,1)S(1)} %copy-done.4, ...), custom_call_target="tpu_custom_call" | custom-call | flops 1024 | bytes 1024 | tf_op jit(solution)/shard_map/pallas_call | solution.py:232
  104.5 7.9 %shard_map.90 = f32[1024,2048]{1,0:T(8,128)} custom-call(s32[5]{0:T(128)S(1)} %stack.63.at_ref, bf16[192,1024]{1,0:T(8,128)(2,1)S(1)} %copy-done.21, bf16[192,1024]{1,0:T(8,128)(2,1)} %collective-permute-done.15.refs_1_, bf16[192,1024]{1,0:T(8,128)(2,1)S(1)} %collective-permute-done.17.refs_2_, bf16[192,1024]{1,0:T(8,128)(2,1)S(1)} %collective-permute-done.20.refs_3_, ...), custom_call_target="tpu_custom_call" | custom-call | flops 1024 | bytes 1024 | tf_op jit(solution)/shard_map/pallas_call | solution.py:115
  112.3 4.6 %collective-permute-done.24.refs_0_ = bf16[192,1024]{1,0:T(8,128)(2,1)S(1)} collective-permute-done((bf16[192,1024]{1,0:T(8,128)(2,1)S(1)}, bf16[192,1024]{1,0:T(8,128)(2,1)S(1)}, u32[]{:S(2)}, u32[]{:S(2)}) %collective-permute-start.24) | collective-permute-done | bytes 393248 | tf_op jit(solution)/shard_map/ppermute | solution.py:316
  116.9 2.3 %shard_map.91 = bf16[192,1024]{1,0:T(8,128)(2,1)} custom-call(s32[1]{0:T(128)} %bitcast.core_ref, bf16[192,1024]{1,0:T(8,128)(2,1)S(1)} %shard_map.88.refs_4_.mine_ref, bf16[192,1024]{1,0:T(8,128)(2,1)S(1)} %collective-permute-done.23.refs_8_.theirs_ref, bf16[1024,2048]{1,0:T(8,128)(2,1)S(1)} %copy-done.4, bf16[192,1024]{1,0:T(8,128)(2,1)S(1)} %collective-permute-done.24.refs_0_), custom_call_target="tpu_custom_call" | custom-call | flops 1024 | bytes 1024 | tf_op jit(solution)/shard_map/pallas_call | solution.py:232
  (88 shorter events, 14.3 us)
Async XLA Ops:
  0.6 8.1 %collective-permute-start.2 = (bf16[2048,1024]{1,0:T(8,128)(2,1)}, bf16[2048,1024]{1,0:T(8,128)(2,1)}, u32[]{:S(2)}, u32[]{:S(2)}) collective-permute-start(bf16[2048,1024]{1,0:T(8,128)(2,1)} %mine_ref.7), channel_id=1, source_target_pairs={{0,4},{4,0},{8,12},{12,8},{1,5},{5,1},{9,13},{13,9},{2,6},{6,2},{1... | collective-permute-start | bytes 12582920 | tf_op jit(solution)/shard_map/ppermute | solution.py:264
  1.1 20.9 %collective-permute-start.5 = (bf16[192,2048]{1,0:T(8,128)(2,1)}, bf16[192,2048]{1,0:T(8,128)(2,1)S(1)}, u32[]{:S(2)}, u32[]{:S(2)}) collective-permute-start(bf16[192,2048]{1,0:T(8,128)(2,1)} %refs_0_.4), channel_id=1, source_target_pairs={{0,8},{4,12},{8,0},{12,4},{1,9},{5,13},{9,1},{13,5},{2,10},{6,14},... | collective-permute-start | bytes 2359304 | tf_op jit(solution)/shard_map/ppermute | solution.py:262
  3.7 5.0 %collective-permute-start.1 = (bf16[192,1024]{1,0:T(8,128)(2,1)}, bf16[192,1024]{1,0:T(8,128)(2,1)S(1)}, u32[]{:S(2)}, u32[]{:S(2)}) collective-permute-start(bf16[192,1024]{1,0:T(8,128)(2,1)} %refs_0_.6), channel_id=1, source_target_pairs={{0,4},{4,0},{8,12},{12,8},{1,5},{5,1},{9,13},{13,9},{2,6},{6,2},{1... | collective-permute-start | bytes 1179656 | tf_op jit(solution)/shard_map/ppermute | solution.py:268
  3.9 13.4 %collective-permute-start = (bf16[192,1024]{1,0:T(8,128)(2,1)}, bf16[192,1024]{1,0:T(8,128)(2,1)S(1)}, u32[]{:S(2)}, u32[]{:S(2)}) collective-permute-start(bf16[192,1024]{1,0:T(8,128)(2,1)} %refs_0_.6), channel_id=1, source_target_pairs={{0,1},{1,2},{2,3},{3,0},{4,5},{5,6},{6,7},{7,4},{8,9},{9,10},{10,1... | collective-permute-start | bytes 1179656 | tf_op jit(solution)/shard_map/ppermute | solution.py:287
  11.9 10.2 %copy-start.7 = (bf16[192,2048]{1,0:T(8,128)(2,1)S(1)}, bf16[192,2048]{1,0:T(8,128)(2,1)}, u32[]{:S(2)}) copy-start(bf16[192,2048]{1,0:T(8,128)(2,1)} %refs_0_.4) | copy-start | bytes 2359300
  11.9 10.7 %copy-start.1 = (bf16[2048,1024]{1,0:T(8,128)(2,1)S(1)}, bf16[2048,1024]{1,0:T(8,128)(2,1)}, u32[]{:S(2)}) copy-start(bf16[2048,1024]{1,0:T(8,128)(2,1)} %mine_ref.7) | copy-start | bytes 12582916
  16.7 10.4 %copy-start.22 = (bf16[192,1024]{1,0:T(8,128)(2,1)}, bf16[192,1024]{1,0:T(8,128)(2,1)S(1)}, u32[]{:S(2)}) copy-start(bf16[192,1024]{1,0:T(8,128)(2,1)S(1)} %get-tuple-element.45) | copy-start | bytes 1179652
  17.3 5.3 %collective-permute-start.4 = (bf16[192,1024]{1,0:T(8,128)(2,1)S(1)}, bf16[192,1024]{1,0:T(8,128)(2,1)S(1)}, u32[]{:S(2)}, u32[]{:S(2)}) collective-permute-start(bf16[192,1024]{1,0:T(8,128)(2,1)S(1)} %collective-permute-done.cot_ref.refs_1_), channel_id=1, source_target_pairs={{0,4},{4,0},{8,12},{12,8},{1,5},{5,1},{9,13},{13,9},{2,6},{6,2},{1... | collective-permute-start | bytes 1179656 | tf_op jit(solution)/shard_map/ppermute | solution.py:268
  17.3 14.2 %collective-permute-start.3 = (bf16[192,1024]{1,0:T(8,128)(2,1)S(1)}, bf16[192,1024]{1,0:T(8,128)(2,1)}, u32[]{:S(2)}, u32[]{:S(2)}) collective-permute-start(bf16[192,1024]{1,0:T(8,128)(2,1)S(1)} %collective-permute-done.cot_ref.refs_1_), channel_id=1, source_target_pairs={{0,1},{1,2},{2,3},{3,0},{4,5},{5,6},{6,7},{7,4},{8,9},{9,10},{10,1... | collective-permute-start | bytes 1179656 | tf_op jit(solution)/shard_map/ppermute | solution.py:299
  22.1 19.5 %collective-permute-start.8 = (bf16[192,2048]{1,0:T(8,128)(2,1)S(1)}, bf16[192,2048]{1,0:T(8,128)(2,1)S(1)}, u32[]{:S(2)}, u32[]{:S(2)}) collective-permute-start(bf16[192,2048]{1,0:T(8,128)(2,1)S(1)} %collective-permute-done.5.refs_1_), channel_id=1, source_target_pairs={{0,4},{4,0},{8,12},{12,8},{1,5},{5,1},{9,13},{13,9},{2,6},{6,2},{1... | collective-permute-start | bytes 2359304 | tf_op jit(solution)/shard_map/ppermute | solution.py:297
  22.1 20.4 %collective-permute-start.7 = (bf16[192,2048]{1,0:T(8,128)(2,1)S(1)}, bf16[192,2048]{1,0:T(8,128)(2,1)S(1)}, u32[]{:S(2)}, u32[]{:S(2)}) collective-permute-start(bf16[192,2048]{1,0:T(8,128)(2,1)S(1)} %copy-done.7), channel_id=1, source_target_pairs={{0,4},{4,0},{8,12},{12,8},{1,5},{5,1},{9,13},{13,9},{2,6},{6,2},{1... | collective-permute-start | bytes 2359304 | tf_op jit(solution)/shard_map/ppermute | solution.py:297
  31.5 2.1 %collective-permute-start.6 = (bf16[192,1024]{1,0:T(8,128)(2,1)}, bf16[192,1024]{1,0:T(8,128)(2,1)}, u32[]{:S(2)}, u32[]{:S(2)}) collective-permute-start(bf16[192,1024]{1,0:T(8,128)(2,1)} %collective-permute-done.3.cot_ref.refs_2_), channel_id=1, source_target_pairs={{0,4},{4,0},{8,12},{12,8},{1,5},{5,1},{9,13},{13,9},{2,6},{6,2},{1... | collective-permute-start | bytes 1179656 | tf_op jit(solution)/shard_map/ppermute | solution.py:268
  31.5 14.8 %collective-permute-start.10 = (bf16[192,1024]{1,0:T(8,128)(2,1)}, bf16[192,1024]{1,0:T(8,128)(2,1)}, u32[]{:S(2)}, u32[]{:S(2)}) collective-permute-start(bf16[192,1024]{1,0:T(8,128)(2,1)} %get-tuple-element.34), channel_id=1, source_target_pairs={{0,8},{4,12},{8,0},{12,4},{1,9},{5,13},{9,1},{13,5},{2,10},{6,14},... | collective-permute-start | bytes 1179656 | tf_op jit(solution)/shard_map/ppermute | solution.py:275
  33.1 16.2 %collective-permute-start.9 = (bf16[192,1024]{1,0:T(8,128)(2,1)}, bf16[192,1024]{1,0:T(8,128)(2,1)}, u32[]{:S(2)}, u32[]{:S(2)}) collective-permute-start(bf16[192,1024]{1,0:T(8,128)(2,1)} %collective-permute-done.3.cot_ref.refs_2_), channel_id=1, source_target_pairs={{0,1},{1,2},{2,3},{3,0},{4,5},{5,6},{6,7},{7,4},{8,9},{9,10},{10,1... | collective-permute-start | bytes 1179656 | tf_op jit(solution)/shard_map/ppermute | solution.py:299
  33.6 21.3 %collective-permute-start.15 = (bf16[192,1024]{1,0:T(8,128)(2,1)}, bf16[192,1024]{1,0:T(8,128)(2,1)}, u32[]{:S(2)}, u32[]{:S(2)}) collective-permute-start(bf16[192,1024]{1,0:T(8,128)(2,1)} %refs_0_.7), channel_id=1, source_target_pairs={{0,1},{1,2},{2,3},{3,0},{4,5},{5,6},{6,7},{7,4},{8,9},{9,10},{10,1... | collective-permute-start | bytes 1179656 | tf_op jit(solution)/shard_map/ppermute | solution.py:301
  36.7 9.7 %copy-start.18 = (f32[192,1024]{1,0:T(8,128)S(1)}, f32[192,1024]{1,0:T(8,128)}, u32[]{:S(2)}) copy-start(f32[192,1024]{1,0:T(8,128)} %copy-done.17) | copy-start | bytes 2359300
  41.5 7.7 %copy-start.13 = (f32[192,1024]{1,0:T(8,128)}, f32[192,1024]{1,0:T(8,128)S(1)}, u32[]{:S(2)}) copy-start(f32[192,1024]{1,0:T(8,128)S(1)} %get-tuple-element.47.part_ref) | copy-start | bytes 2359300
  49.3 5.6 %collective-permute-start.11 = (bf16[192,1024]{1,0:T(8,128)(2,1)}, bf16[192,1024]{1,0:T(8,128)(2,1)}, u32[]{:S(2)}, u32[]{:S(2)}) collective-permute-start(bf16[192,1024]{1,0:T(8,128)(2,1)} %collective-permute-done.9.cot_ref.refs_3_), channel_id=1, source_target_pairs={{0,4},{4,0},{8,12},{12,8},{1,5},{5,1},{9,13},{13,9},{2,6},{6,2},{1... | collective-permute-start | bytes 1179656 | tf_op jit(solution)/shard_map/ppermute | solution.py:268
  49.3 11.9 %collective-permute-start.16 = (bf16[192,1024]{1,0:T(8,128)(2,1)}, bf16[192,1024]{1,0:T(8,128)(2,1)}, u32[]{:S(2)}, u32[]{:S(2)}) collective-permute-start(bf16[192,1024]{1,0:T(8,128)(2,1)} %shard_map.80.mine_ref.refs_5_), channel_id=1, source_target_pairs={{0,4},{4,0},{8,12},{12,8},{1,5},{5,1},{9,13},{13,9},{2,6},{6,2},{1... | collective-permute-start | bytes 1179656 | tf_op jit(solution)/shard_map/ppermute | solution.py:280
  49.8 20.4 %collective-permute-start.14 = (bf16[192,1024]{1,0:T(8,128)(2,1)}, bf16[192,1024]{1,0:T(8,128)(2,1)}, u32[]{:S(2)}, u32[]{:S(2)}) collective-permute-start(bf16[192,1024]{1,0:T(8,128)(2,1)} %get-tuple-element.36), channel_id=1, source_target_pairs={{0,8},{4,12},{8,0},{12,4},{1,9},{5,13},{9,1},{13,5},{2,10},{6,14},... | collective-permute-start | bytes 1179656 | tf_op jit(solution)/shard_map/ppermute | solution.py:275
  54.9 24.6 %collective-permute-start.17 = (bf16[192,1024]{1,0:T(8,128)(2,1)}, bf16[192,1024]{1,0:T(8,128)(2,1)S(1)}, u32[]{:S(2)}, u32[]{:S(2)}) collective-permute-start(bf16[192,1024]{1,0:T(8,128)(2,1)} %collective-permute-done.15.refs_1_), channel_id=1, source_target_pairs={{0,1},{1,2},{2,3},{3,0},{4,5},{5,6},{6,7},{7,4},{8,9},{9,10},{10,1... | collective-permute-start | bytes 1179656 | tf_op jit(solution)/shard_map/ppermute | solution.py:313
  72.3 9.5 %collective-permute-start.18 = (bf16[192,1024]{1,0:T(8,128)(2,1)S(1)}, bf16[192,1024]{1,0:T(8,128)(2,1)S(1)}, u32[]{:S(2)}, u32[]{:S(2)}) collective-permute-start(bf16[192,1024]{1,0:T(8,128)(2,1)S(1)} %shard_map.84.mine_ref.refs_6_), channel_id=1, source_target_pairs={{0,4},{4,0},{8,12},{12,8},{1,5},{5,1},{9,13},{13,9},{2,6},{6,2},{1... | collective-permute-start | bytes 1179656 | tf_op jit(solution)/shard_map/ppermute | solution.py:280
  72.4 13.8 %collective-permute-start.19 = (bf16[192,1024]{1,0:T(8,128)(2,1)S(1)}, bf16[192,1024]{1,0:T(8,128)(2,1)S(1)}, u32[]{:S(2)}, u32[]{:S(2)}) collective-permute-start(bf16[192,1024]{1,0:T(8,128)(2,1)S(1)} %shard_map.82), channel_id=1, source_target_pairs={{0,1},{1,2},{2,3},{3,0},{4,5},{5,6},{6,7},{7,4},{8,9},{9,10},{10,1... | collective-permute-start | bytes 1179656 | tf_op jit(solution)/shard_map/ppermute | solution.py:312
  72.6 15.2 %collective-permute-start.13 = (bf16[192,1024]{1,0:T(8,128)(2,1)S(1)}, bf16[192,1024]{1,0:T(8,128)(2,1)S(1)}, u32[]{:S(2)}, u32[]{:S(2)}) collective-permute-start(bf16[192,1024]{1,0:T(8,128)(2,1)S(1)} %get-tuple-element.44), channel_id=1, source_target_pairs={{0,8},{4,12},{8,0},{12,4},{1,9},{5,13},{9,1},{13,5},{2,10},{6,14},... | collective-permute-start | bytes 1179656 | tf_op jit(solution)/shard_map/ppermute | solution.py:275
  79.5 12.8 %copy-start.10 = (f32[192,1024]{1,0:T(8,128)S(1)}, f32[192,1024]{1,0:T(8,128)}, u32[]{:S(2)}) copy-start(f32[192,1024]{1,0:T(8,128)} %copy-done.9) | copy-start | bytes 2359300
  79.5 12.8 %collective-permute-start.12 = (bf16[192,1024]{1,0:T(8,128)(2,1)S(1)}, bf16[192,1024]{1,0:T(8,128)(2,1)S(1)}, u32[]{:S(2)}, u32[]{:S(2)}) collective-permute-start(bf16[192,1024]{1,0:T(8,128)(2,1)S(1)} %copy-done.23), channel_id=1, source_target_pairs={{0,8},{4,12},{8,0},{12,4},{1,9},{5,13},{9,1},{13,5},{2,10},{6,14},... | collective-permute-start | bytes 1179656 | tf_op jit(solution)/shard_map/ppermute | solution.py:275
  81.0 13.9 %collective-permute-start.20 = (bf16[192,1024]{1,0:T(8,128)(2,1)S(1)}, bf16[192,1024]{1,0:T(8,128)(2,1)S(1)}, u32[]{:S(2)}, u32[]{:S(2)}) collective-permute-start(bf16[192,1024]{1,0:T(8,128)(2,1)S(1)} %collective-permute-done.17.refs_2_), channel_id=1, source_target_pairs={{0,1},{1,2},{2,3},{3,0},{4,5},{5,6},{6,7},{7,4},{8,9},{9,10},{10,1... | collective-permute-start | bytes 1179656 | tf_op jit(solution)/shard_map/ppermute | solution.py:313
  88.9 6.0 %collective-permute-start.21 = (bf16[192,1024]{1,0:T(8,128)(2,1)S(1)}, bf16[192,1024]{1,0:T(8,128)(2,1)S(1)}, u32[]{:S(2)}, u32[]{:S(2)}) collective-permute-start(bf16[192,1024]{1,0:T(8,128)(2,1)S(1)} %shard_map.87.mine_ref.refs_7_), channel_id=1, source_target_pairs={{0,4},{4,0},{8,12},{12,8},{1,5},{5,1},{9,13},{13,9},{2,6},{6,2},{1... | collective-permute-start | bytes 1179656 | tf_op jit(solution)/shard_map/ppermute | solution.py:280
  89.0 13.9 %collective-permute-start.22 = (bf16[192,1024]{1,0:T(8,128)(2,1)S(1)}, bf16[192,1024]{1,0:T(8,128)(2,1)S(1)}, u32[]{:S(2)}, u32[]{:S(2)}) collective-permute-start(bf16[192,1024]{1,0:T(8,128)(2,1)S(1)} %shard_map.86), channel_id=1, source_target_pairs={{0,1},{1,2},{2,3},{3,0},{4,5},{5,6},{6,7},{7,4},{8,9},{9,10},{10,1... | collective-permute-start | bytes 1179656 | tf_op jit(solution)/shard_map/ppermute | solution.py:312
  92.3 12.1 %copy-start.21 = (bf16[192,1024]{1,0:T(8,128)(2,1)S(1)}, bf16[192,1024]{1,0:T(8,128)(2,1)}, u32[]{:S(2)}) copy-start(bf16[192,1024]{1,0:T(8,128)(2,1)} %refs_0_.7) | copy-start | bytes 1179652
  94.9 9.6 %collective-permute-start.23 = (bf16[192,1024]{1,0:T(8,128)(2,1)S(1)}, bf16[192,1024]{1,0:T(8,128)(2,1)S(1)}, u32[]{:S(2)}, u32[]{:S(2)}) collective-permute-start(bf16[192,1024]{1,0:T(8,128)(2,1)S(1)} %shard_map.88.refs_4_.mine_ref), channel_id=1, source_target_pairs={{0,4},{4,0},{8,12},{12,8},{1,5},{5,1},{9,13},{13,9},{2,6},{6,2},{1... | collective-permute-start | bytes 1179656 | tf_op jit(solution)/shard_map/ppermute | solution.py:280
  104.4 12.5 %collective-permute-start.24 = (bf16[192,1024]{1,0:T(8,128)(2,1)S(1)}, bf16[192,1024]{1,0:T(8,128)(2,1)S(1)}, u32[]{:S(2)}, u32[]{:S(2)}) collective-permute-start(bf16[192,1024]{1,0:T(8,128)(2,1)S(1)} %shard_map.89), channel_id=1, source_target_pairs={{0,1},{1,2},{2,3},{3,0},{4,5},{5,6},{6,7},{7,4},{8,9},{9,10},{10,1... | collective-permute-start | bytes 1179656 | tf_op jit(solution)/shard_map/ppermute | solution.py:316
  (17 other events, 51.1 us)

commit v5 on v4

--- a/solution.py
+++ b/solution.py
@@ -61,29 +61,24 @@
     out_ref[...] = dot(activation, cots[...], FIRST) * scale
 
 
-def grad_down_call(at, pre_all, cots, scale, second=None):
+def grad_down_call(at, pre_all, cots, scale):
     total, hidden = pre_all.shape
     features = cots[0].shape[1]
-    tile = tile_of(hidden // 2)
-    steps = hidden // 2 // tile
-    skip = 0 if second is None else steps
-    rest = [] if second is None else [second]
+    tile = tile_of(hidden)
     return pl.pallas_call(
         functools.partial(grad_down_kernel, len(cots), scale),
         out_shape=jax.ShapeDtypeStruct((hidden, features), jnp.float32),
         grid_spec=pltpu.PrefetchScalarGridSpec(
             num_scalar_prefetch=1,
-            grid=(steps,),
-            in_specs=[pl.BlockSpec((total, tile), lambda i, at: (0, i + skip))]
-            + [in_vmem() for _ in cots]
-            + [pl.BlockSpec(memory_space=pl.ANY) for _ in rest],
-            out_specs=pl.BlockSpec((tile, features), lambda i, at: (i + skip, 0)),
+            grid=(hidden // tile,),
+            in_specs=[pl.BlockSpec((total, tile), lambda i, at: (0, i))]
+            + [in_vmem() for _ in cots],
+            out_specs=pl.BlockSpec((tile, features), lambda i, at: (i, 0)),
             scratch_shapes=[pltpu.VMEM((total, features), jnp.bfloat16)],
         ),
-        input_output_aliases={2 + len(cots): 0} if rest else {},
         compiler_params=pltpu.CompilerParams(vmem_limit_bytes=16 * MIB),
         cost_estimate=LITTLE,
-    )(at, pre_all, *cots, *rest)
+    )(at, pre_all, *cots)
 
 
 def grad_up_kernel(blocks, scale, at_ref, *refs):
@@ -184,61 +179,65 @@
 
 
 def hidden_kernel(core_ref, cot_ref, pair_ref, mine_ref, theirs_ref, part_ref, sent_ref):
-    half = part_ref.shape[1]
+    tile = mine_ref.shape[0]
+    part = dot(cot_ref[...], mine_ref[...], LAST) + dot(pair_ref[...], theirs_ref[...], LAST)
+    here = pl.ds(pl.multiple_of(pl.program_id(0) * tile, tile), tile)
+    part_ref[:, here] = part
+    sent_ref[:, here] = part.astype(jnp.bfloat16)
+
+
+def hidden_call(core, cot, cot_pair, down_mine, down_pair):
+    (tokens, features), half = cot.shape, down_mine.shape[0] // 2
     tile = tile_of(half)
-    for first in range(0, half, tile):
-        rows = pl.ds(pl.multiple_of(core_ref[0] * half + first, tile), tile)
-        part = dot(cot_ref[...], mine_ref[rows, :], LAST)
-        part = part + dot(pair_ref[...], theirs_ref[rows, :], LAST)
-        part_ref[:, pl.ds(first, tile)] = part
-        sent_ref[:, pl.ds(first, tile)] = part.astype(jnp.bfloat16)
-
-
-def hidden_call(core, cot, cot_pair, down_mine, down_pair):
-    shape = (cot.shape[0], down_mine.shape[0] // 2)
+    weight = pl.BlockSpec((tile, features), lambda i, core: (core[0] * (half // tile) + i, 0))
     return pl.pallas_call(
         hidden_kernel,
         out_shape=[
-            jax.ShapeDtypeStruct(shape, jnp.float32),
-            jax.ShapeDtypeStruct(shape, jnp.bfloat16),
+            jax.ShapeDtypeStruct((tokens, half), jnp.float32),
+            jax.ShapeDtypeStruct((tokens, half), jnp.bfloat16),
         ],
         grid_spec=pltpu.PrefetchScalarGridSpec(
             num_scalar_prefetch=1,
-            grid=(1,),
-            in_specs=[in_vmem() for _ in range(4)],
+            grid=(half // tile,),
+            in_specs=[in_vmem(), in_vmem(), weight, weight],
             out_specs=[in_vmem(), in_vmem()],
         ),
-        compiler_params=pltpu.CompilerParams(vmem_limit_bytes=20 * MIB),
+        compiler_params=pltpu.CompilerParams(vmem_limit_bytes=10 * MIB),
         cost_estimate=LITTLE,
     )(core, cot, cot_pair, down_mine, down_pair)
 
 
 def share_kernel(core_ref, mine_ref, theirs_ref, up_ref, *refs):
     out_ref = refs[-1]
-    features, half = up_ref.shape[0], mine_ref.shape[1]
-    tile = tile_of(features)
+    tile, half = up_ref.shape[0], mine_ref.shape[1]
     left = pl.ds(pl.multiple_of(core_ref[0] * half, half), half)
     right = pl.ds(pl.multiple_of((1 - core_ref[0]) * half, half), half)
-    for first in range(0, features, tile):
-        here = pl.ds(first, tile)
-        total = dot(mine_ref[...], up_ref[here, left], LAST)
-        total = total + dot(theirs_ref[...], up_ref[here, right], LAST)
-        for arrived in refs[:-1]:
-            total = total + arrived[:, here].astype(jnp.float32)
-        out_ref[:, here] = total.astype(jnp.bfloat16)
+    here = pl.ds(pl.multiple_of(pl.program_id(0) * tile, tile), tile)
+    total = dot(mine_ref[...], up_ref[:, left], LAST)
+    total = total + dot(theirs_ref[...], up_ref[:, right], LAST)
+    for arrived in refs[:-1]:
+        total = total + arrived[:, here].astype(jnp.float32)
+    out_ref[:, here] = total.astype(jnp.bfloat16)
 
 
 def share_call(core, mine, theirs, up_weight, arrived):
+    features, hidden = up_weight.shape
+    tile = tile_of(features)
     return pl.pallas_call(
         share_kernel,
-        out_shape=jax.ShapeDtypeStruct((mine.shape[0], up_weight.shape[0]), jnp.bfloat16),
-        grid_spec=pltpu.PrefetchScalarGridSpec(
-            num_scalar_prefetch=1,
-            grid=(1,),
-            in_specs=[in_vmem() for _ in [mine, theirs, up_weight] + arrived],
+        out_shape=jax.ShapeDtypeStruct((mine.shape[0], features), jnp.bfloat16),
+        grid_spec=pltpu.PrefetchScalarGridSpec(
+            num_scalar_prefetch=1,
+            grid=(features // tile,),
+            in_specs=[
+                in_vmem(),
+                in_vmem(),
+                pl.BlockSpec((tile, hidden), lambda i, core: (i, 0)),
+                *[in_vmem() for _ in arrived],
+            ],
             out_specs=in_vmem(),
         ),
-        compiler_params=pltpu.CompilerParams(vmem_limit_bytes=16 * MIB),
+        compiler_params=pltpu.CompilerParams(vmem_limit_bytes=10 * MIB),
         cost_estimate=LITTLE,
     )(core, mine, theirs, up_weight, *arrived)
 
@@ -283,36 +282,37 @@
         return share_call(at[cols:], after(mine[s], *first), theirs[s], up_weight, arrived)
 
     cots, ins = [cotangent], [inputs]
-    sent = own = hidden_part(0, cotangent, [])
     arriving = lax.ppermute(cotangent, "col", ring)
     for s in range(1, cols):
-        first = [sent]
-        if s == cols - 1:
+        first = [sent] if s > 1 else []
+        if s > 1 and s == cols - 1:
             pre_all = lay_out_call(after(places, sent), pres)
             pre_grad(1, [sent])
             first = [sent, mine[1]]
         cots.append(after(arriving, *first))
-        sent = hidden_part(s, cots[s], pres[1:] if s == 1 else [])
-        if s == 1:
-            pres = pres + [lax.ppermute(after(p, cots[1]), "row", pair) for p in pres]
         if s < cols - 1:
             arriving = lax.ppermute(cots[s], "col", ring)
+        if s == 1:
+            own = hidden_part(0, cotangent, [cots[1]])
+            sent = hidden_part(1, cots[1], pres[1:] + [own])
+            pres = pres + [lax.ppermute(after(p, cots[1]), "row", pair) for p in pres]
         else:
-            ins.append(lax.ppermute(after(inputs, cots[cols - 2]), "col", ring))
+            sent = hidden_part(s, cots[s], [])
     exchange(0, after(own, sent))
-
-    sums = share(1, [ins[1]], [])
-    grad_down = grad_down_call(after(at, sums, sent), pre_all, cots, scale)
-    for s in range(2, cols):
-        pre_grad(s, [sums, grad_down])
-        if s == 2:
-            grad_down = grad_down_call(after(at, mine[s]), pre_all, cots, scale, grad_down)
-        if s == cols - 1:
-            pre_grad(0, [mine[s]])
-        arrived = lax.ppermute(sums, "col", ring)
-        ins.append(lax.ppermute(ins[-1], "col", ring))
-        first = [ins[-1]] + ([grad_down] if s == 2 else [])
-        sums = share(s, first, [arrived])
+    ins.append(lax.ppermute(after(inputs, cots[cols - 2]), "col", ring))
+
+    late = []
+    for s in range(1, cols):
+        following = (s + 1) % cols
+        pre_grad(following, [sent, *late])
+        arrived = [lax.ppermute(sums, "col", ring)] if s > 1 else []
+        if s > 1:
+            ins.append(lax.ppermute(ins[-1], "col", ring))
+        sums = share(s, [mine[following], ins[s]], arrived)
+        late = [sums]
+        if s == 1:
+            grad_down = grad_down_call(after(at, sums), pre_all, cots, scale)
+            late = [grad_down]
     arrived = lax.ppermute(sums, "col", ring)
     grad_up = grad_up_call(after(at, sums), ins, mine, theirs, scale)
     sums = share(0, [grad_up], [arrived])

time: 120 us -> 138 us (1.15)
  waiting for transfers between devices: 35.9 us -> 42.4 us
  local copies, waits for them, and re-layouts: 13.5 us -> 18.3 us
  Pallas kernels: 53.7 us -> 57.4 us
  starting transfers between devices: 14.8 us -> 17.8 us
    ppermute x3 -> x1, waiting for transfers between devices: 16.9 us -> 3.6 us  [per_device(): arrived = lax.ppermute(sums, 'col', ring)]
    ppermute x1, waiting for transfers between devices: 0.64 us -> 11.7 us  [per_device(): arriving = lax.ppermute(cotangent, 'col', ring)]
    ppermute x0 -> x2, waiting for transfers between devices: none -> 7.38 us  [per_device(): arrived = [lax.ppermute(sums, 'col', ring)] if s > 1 else []]
    ppermute x1, waiting for transfers between devices: 4.27 us -> 11.4 us  [per_device(): ins.append(lax.ppermute(after(inputs, cots[cols - 2]), 'col', ring))]
    unnamed x48 -> x56, local copies, waits for them, and re-layouts: 13.5 us -> 18.2 us
    ppermute x0 -> x2, starting transfers between devices: none -> 4.3 us  [per_device(): arrived = [lax.ppermute(sums, 'col', ring)] if s > 1 else []]
    pallas_call x4, Pallas kernels: 8.04 us -> 12.1 us  [share_call(): pl.pallas_call(share_kernel, out_shape=jax.ShapeDtypeStruct((mine.shape[0...]
    ppermute x4, waiting for transfers between devices: 3.6 us -> 0.01 us  [hidden_part(): cot_pair = after(lax.ppermute(cot, 'row', pair), *first)]
  transfers between devices with their start and end apart: 25 -> 25, of which waited for: 11 -> 6; matrix products, arithmetic and copies ran while one was open for 0% -> 0% of each run, Pallas kernels for 43% -> 40%
where the time goes in v5:
time: 138 us; the launch traced here: 137 us
  Pallas kernels  57.4 us (42%)
  waiting for transfers between devices  42.4 us (31%)
  local copies, waits for them, and re-layouts  18.3 us (13%)
  starting transfers between devices  17.8 us (13%)
    unnamed x56, local copies, waits for them, and re-layouts  18.2 us
    pallas_call x4, Pallas kernels, hidden_call(): pl.pallas_call(hidden_kernel, out_shape=[jax.ShapeDtypeStruct((tokens, ha...  17.8 us
    pallas_call x4, Pallas kernels, share_call(): pl.pallas_call(share_kernel, out_shape=jax.ShapeDtypeStruct((mine.shape[0...  12.1 us
    ppermute x1, waiting for transfers between devices, per_device(): arriving = lax.ppermute(cotangent, 'col', ring)  11.7 us
    ppermute x1, waiting for transfers between devices, per_device(): ins.append(lax.ppermute(after(inputs, cots[cols - 2]), 'col', ring))  11.4 us
    pallas_call x1, Pallas kernels, grad_down_call(): pl.pallas_call(functools.partial(grad_down_kernel, len(cots), scale), out...  9.73 us
    pallas_call x4, Pallas kernels, pre_grad_call(): pl.pallas_call(pre_grad_kernel, out_shape=jax.ShapeDtypeStruct((tokens, h...  8.83 us
    pallas_call x1, Pallas kernels, grad_up_call(): pl.pallas_call(functools.partial(grad_up_kernel, len(mine), scale), out_s...  8.25 us
  transfers between devices with their start and end apart: 25, of which 6 were waited for; matrix products, arithmetic and copies ran while one was open for 0% of the time, Pallas kernels for 40%

profile of v5, /device:TPU:0, one launch (start us, length us, event | category | flops | bytes accessed | tf_op | source)
XLA Modules:
  0.0 137.1 jit_solution(17079113281535396981)
XLA Ops:
  1.1 2.6 %collective-permute-start.3 = (bf16[192,2048]{1,0:T(8,128)(2,1)}, bf16[192,2048]{1,0:T(8,128)(2,1)S(1)}, u32[]{:S(2)}, u32[]{:S(2)}) collective-permute-start(bf16[192,2048]{1,0:T(8,128)(2,1)} %refs_0_.3), channel_id=1, source_target_pairs={{0,8},{4,12},{8,0},{12,4},{1,9},{5,13},{9,1},{13,5},{2,10},{6,14},... | collective-permute-start | bytes 2359304 | tf_op jit(solution)/shard_map/ppermute | solution.py:261
  3.7 1.6 %collective-permute-start = (bf16[192,1024]{1,0:T(8,128)(2,1)}, bf16[192,1024]{1,0:T(8,128)(2,1)S(1)}, u32[]{:S(2)}, u32[]{:S(2)}) collective-permute-start(bf16[192,1024]{1,0:T(8,128)(2,1)} %refs_0_.4), channel_id=1, source_target_pairs={{0,1},{1,2},{2,3},{3,0},{4,5},{5,6},{6,7},{7,4},{8,9},{9,10},{10,1... | collective-permute-start | bytes 1179656 | tf_op jit(solution)/shard_map/ppermute | solution.py:285
  5.3 11.7 %collective-permute-done.cot_ref.refs_1_ = bf16[192,1024]{1,0:T(8,128)(2,1)S(1)} collective-permute-done((bf16[192,1024]{1,0:T(8,128)(2,1)}, bf16[192,1024]{1,0:T(8,128)(2,1)S(1)}, u32[]{:S(2)}, u32[]{:S(2)}) %collective-permute-start) | collective-permute-done | bytes 393248 | tf_op jit(solution)/shard_map/ppermute | solution.py:285
  17.0 5.1 %collective-permute-done.3.refs_1_ = bf16[192,2048]{1,0:T(8,128)(2,1)S(1)} collective-permute-done((bf16[192,2048]{1,0:T(8,128)(2,1)}, bf16[192,2048]{1,0:T(8,128)(2,1)S(1)}, u32[]{:S(2)}, u32[]{:S(2)}) %collective-permute-start.3) | collective-permute-done | bytes 786464 | tf_op jit(solution)/shard_map/ppermute | solution.py:261
  22.6 2.2 %copy-done = bf16[2048,1024]{1,0:T(8,128)(2,1)S(1)} copy-done((bf16[2048,1024]{1,0:T(8,128)(2,1)S(1)}, bf16[2048,1024]{1,0:T(8,128)(2,1)}, u32[]{:S(2)}) %copy-start) | copy-done | bytes 4194328
  25.8 3.8 %shard_map.76 = (f32[192,1024]{1,0:T(8,128)S(1)}, bf16[192,1024]{1,0:T(8,128)(2,1)S(1)}) custom-call(s32[1]{0:T(128)} %bitcast.core_ref, bf16[192,1024]{1,0:T(8,128)(2,1)S(1)} %copy-done.6, bf16[192,1024]{1,0:T(8,128)(2,1)S(1)} %collective-permute-done.4.pair_ref, bf16[2048,1024]{1,0:T(8,128)(2,1)S(1)} %copy-done, ...), custom_call_target="tpu_custom_call" | custom-call | flops 1024 | bytes 1024 | tf_op jit(solution)/shard_map/pallas_call | solution.py:193
  30.5 4.7 %shard_map.77 = (f32[192,1024]{1,0:T(8,128)S(1)}, bf16[192,1024]{1,0:T(8,128)(2,1)}) custom-call(s32[1]{0:T(128)} %bitcast.core_ref, bf16[192,1024]{1,0:T(8,128)(2,1)S(1)} %collective-permute-done.cot_ref.refs_1_, bf16[192,1024]{1,0:T(8,128)(2,1)} %collective-permute-done.2.pair_ref, bf16[2048,1024]{1,0:T(8,128)(2,1)S(1)} %copy-done.1, ...), custom_call_target="tpu_custom_call" | custom-call | flops 1024 | bytes 1024 | tf_op jit(solution)/shard_map/pallas_call | solution.py:193
  36.2 1.8 %collective-permute-start.10 = (bf16[192,1024]{1,0:T(8,128)(2,1)}, bf16[192,1024]{1,0:T(8,128)(2,1)}, u32[]{:S(2)}, u32[]{:S(2)}) collective-permute-start(bf16[192,1024]{1,0:T(8,128)(2,1)} %get-tuple-element.33), channel_id=1, source_target_pairs={{0,8},{4,12},{8,0},{12,4},{1,9},{5,13},{9,1},{13,5},{2,10},{6,14},... | collective-permute-start | bytes 1179656 | tf_op jit(solution)/shard_map/ppermute | solution.py:274
  38.0 1.6 %collective-permute-start.9 = (bf16[192,1024]{1,0:T(8,128)(2,1)S(1)}, bf16[192,1024]{1,0:T(8,128)(2,1)}, u32[]{:S(2)}, u32[]{:S(2)}) collective-permute-start(bf16[192,1024]{1,0:T(8,128)(2,1)S(1)} %collective-permute-done.1.cot_ref.refs_2_), channel_id=1, source_target_pairs={{0,1},{1,2},{2,3},{3,0},{4,5},{5,6},{6,7},{7,4},{8,9},{9,10},{10,1... | collective-permute-start | bytes 1179656 | tf_op jit(solution)/shard_map/ppermute | solution.py:294
  39.7 2.2 %copy-done.2 = bf16[2048,1024]{1,0:T(8,128)(2,1)S(1)} copy-done((bf16[2048,1024]{1,0:T(8,128)(2,1)S(1)}, bf16[2048,1024]{1,0:T(8,128)(2,1)}, u32[]{:S(2)}) %copy-start.2) | copy-done | bytes 4194328
  41.9 4.6 %shard_map.78 = (f32[192,1024]{1,0:T(8,128)S(1)}, bf16[192,1024]{1,0:T(8,128)(2,1)}) custom-call(s32[1]{0:T(128)} %bitcast.core_ref, bf16[192,1024]{1,0:T(8,128)(2,1)S(1)} %collective-permute-done.1.cot_ref.refs_2_, bf16[192,1024]{1,0:T(8,128)(2,1)S(1)} %collective-permute-done.6.pair_ref, bf16[2048,1024]{1,0:T(8,128)(2,1)S(1)} %copy-done.2, ...), custom_call_target="tpu_custom_call" | custom-call | flops 1024 | bytes 1024 | tf_op jit(solution)/shard_map/pallas_call | solution.py:193
  49.2 1.1 copy-done.18
  50.3 1.1 copy-done.20
  52.2 2.9 %shard_map.80.mine_ref.refs_5_ = bf16[192,1024]{1,0:T(8,128)(2,1)} custom-call(s32[2]{0:T(128)S(1)} %pad_add_fusion.2.at_ref, bf16[768,2048]{1,0:T(8,128)(2,1)S(1)} %shard_map.79.pre_ref, f32[192,1024]{1,0:T(8,128)S(1)} %copy-done.22, bf16[192,1024]{1,0:T(8,128)(2,1)} %collective-permute-done.10.refs_0_), custom_call_target="tpu_custom_call" | custom-call | flops 1024 | bytes 1024 | tf_op jit(solution)/shard_map/pallas_call | solution.py:167
  55.1 1.6 %collective-permute-start.15 = (bf16[192,1024]{1,0:T(8,128)(2,1)}, bf16[192,1024]{1,0:T(8,128)(2,1)}, u32[]{:S(2)}, u32[]{:S(2)}) collective-permute-start(bf16[192,1024]{1,0:T(8,128)(2,1)} %refs_0_.5), channel_id=1, source_target_pairs={{0,1},{1,2},{2,3},{3,0},{4,5},{5,6},{6,7},{7,4},{8,9},{9,10},{10,1... | collective-permute-start | bytes 1179656 | tf_op jit(solution)/shard_map/ppermute | solution.py:302
  57.3 11.4 %collective-permute-done.15.refs_1_ = bf16[192,1024]{1,0:T(8,128)(2,1)} collective-permute-done((bf16[192,1024]{1,0:T(8,128)(2,1)}, bf16[192,1024]{1,0:T(8,128)(2,1)}, u32[]{:S(2)}, u32[]{:S(2)}) %collective-permute-start.15) | collective-permute-done | bytes 393248 | tf_op jit(solution)/shard_map/ppermute | solution.py:302
  68.8 2.2 %copy-done.3 = bf16[2048,1024]{1,0:T(8,128)(2,1)S(1)} copy-done((bf16[2048,1024]{1,0:T(8,128)(2,1)S(1)}, bf16[2048,1024]{1,0:T(8,128)(2,1)}, u32[]{:S(2)}) %copy-start.3) | copy-done | bytes 4194328
  71.0 4.6 %shard_map.81 = (f32[192,1024]{1,0:T(8,128)S(1)}, bf16[192,1024]{1,0:T(8,128)(2,1)}) custom-call(s32[1]{0:T(128)} %bitcast.core_ref, bf16[192,1024]{1,0:T(8,128)(2,1)} %collective-permute-done.9.cot_ref.refs_3_, bf16[192,1024]{1,0:T(8,128)(2,1)S(1)} %collective-permute-done.11.pair_ref, bf16[2048,1024]{1,0:T(8,128)(2,1)S(1)} %copy-done.3, ...), custom_call_target="tpu_custom_call" | custom-call | flops 1024 | bytes 1024 | tf_op jit(solution)/shard_map/pallas_call | solution.py:193
  77.0 2.3 %shard_map.82.mine_ref.refs_6_ = bf16[192,1024]{1,0:T(8,128)(2,1)S(1)} custom-call(s32[2]{0:T(128)S(1)} %pad_add_fusion.3.at_ref, bf16[768,2048]{1,0:T(8,128)(2,1)S(1)} %shard_map.79.pre_ref, f32[192,1024]{1,0:T(8,128)S(1)} %copy-done.26, bf16[192,1024]{1,0:T(8,128)(2,1)} %collective-permute-done.13.refs_0_), custom_call_target="tpu_custom_call" | custom-call | flops 1024 | bytes 1024 | tf_op jit(solution)/shard_map/pallas_call | solution.py:167
  79.4 4.0 %shard_map.83 = bf16[192,1024]{1,0:T(8,128)(2,1)} custom-call(s32[1]{0:T(128)} %bitcast.core_ref, bf16[192,1024]{1,0:T(8,128)(2,1)} %shard_map.80.mine_ref.refs_5_, bf16[192,1024]{1,0:T(8,128)(2,1)} %collective-permute-done.16.theirs_ref.refs_9_, bf16[1024,2048]{1,0:T(8,128)(2,1)S(1)} %copy-done.4), custom_call_target="tpu_custom_call" | custom-call | flops 1024 | bytes 1024 | tf_op jit(solution)/shard_map/pallas_call | solution.py:226
  83.4 1.3 collective-permute-start.19
  84.9 1.3 collective-permute-start.12
  89.2 9.7 %shard_map.84 = f32[2048,1024]{1,0:T(8,128)} custom-call(s32[5]{0:T(128)S(1)} %stack.63.at_ref, bf16[768,2048]{1,0:T(8,128)(2,1)S(1)} %shard_map.79.pre_ref, bf16[192,1024]{1,0:T(8,128)(2,1)S(1)} %copy-done.7, bf16[192,1024]{1,0:T(8,128)(2,1)S(1)} %copy-done.9, bf16[192,1024]{1,0:T(8,128)(2,1)S(1)} %copy-done.11, ...), custom_call_target="tpu_custom_call" | custom-call | flops 1024 | bytes 1024 | tf_op jit(solution)/shard_map/pallas_call | solution.py:68
  99.2 2.5 %shard_map.85.mine_ref.refs_7_ = bf16[192,1024]{1,0:T(8,128)(2,1)S(1)} custom-call(s32[2]{0:T(128)S(1)} %pad_add_fusion.4.at_ref, bf16[768,2048]{1,0:T(8,128)(2,1)S(1)} %shard_map.79.pre_ref, f32[192,1024]{1,0:T(8,128)S(1)} %copy-done.24, bf16[192,1024]{1,0:T(8,128)(2,1)} %collective-permute-done.14.refs_0_), custom_call_target="tpu_custom_call" | custom-call | flops 1024 | bytes 1024 | tf_op jit(solution)/shard_map/pallas_call | solution.py:167
  101.8 3.2 %shard_map.86 = bf16[192,1024]{1,0:T(8,128)(2,1)S(1)} custom-call(s32[1]{0:T(128)} %bitcast.core_ref, bf16[192,1024]{1,0:T(8,128)(2,1)S(1)} %shard_map.82.mine_ref.refs_6_, bf16[192,1024]{1,0:T(8,128)(2,1)} %collective-permute-done.18.theirs_ref.refs_10_, bf16[1024,2048]{1,0:T(8,128)(2,1)S(1)} %copy-done.5, bf16[192,1024]{1,0:T(8,128)(2,1)} %collective-permute-done.19.refs_0_), custom_call_target="tpu_custom_call" | custom-call | flops 1024 | bytes 1024 | tf_op jit(solution)/shard_map/pallas_call | solution.py:226
  105.0 3.0 %collective-permute-start.22 = (bf16[192,1024]{1,0:T(8,128)(2,1)S(1)}, bf16[192,1024]{1,0:T(8,128)(2,1)S(1)}, u32[]{:S(2)}, u32[]{:S(2)}) collective-permute-start(bf16[192,1024]{1,0:T(8,128)(2,1)S(1)} %shard_map.86), channel_id=1, source_target_pairs={{0,1},{1,2},{2,3},{3,0},{4,5},{5,6},{6,7},{7,4},{8,9},{9,10},{10,1... | collective-permute-start | bytes 1179656 | tf_op jit(solution)/shard_map/ppermute | solution.py:308
  109.7 3.2 %collective-permute-done.20.refs_3_ = bf16[192,1024]{1,0:T(8,128)(2,1)S(1)} collective-permute-done((bf16[192,1024]{1,0:T(8,128)(2,1)}, bf16[192,1024]{1,0:T(8,128)(2,1)S(1)}, u32[]{:S(2)}, u32[]{:S(2)}) %collective-permute-start.20) | collective-permute-done | bytes 393248 | tf_op jit(solution)/shard_map/ppermute | solution.py:310
  112.9 7.4 %collective-permute-done.22.refs_0_ = bf16[192,1024]{1,0:T(8,128)(2,1)S(1)} collective-permute-done((bf16[192,1024]{1,0:T(8,128)(2,1)S(1)}, bf16[192,1024]{1,0:T(8,128)(2,1)S(1)}, u32[]{:S(2)}, u32[]{:S(2)}) %collective-permute-start.22) | collective-permute-done | bytes 393248 | tf_op jit(solution)/shard_map/ppermute | solution.py:308
  120.3 2.1 %shard_map.88 = bf16[192,1024]{1,0:T(8,128)(2,1)S(1)} custom-call(s32[1]{0:T(128)} %bitcast.core_ref, bf16[192,1024]{1,0:T(8,128)(2,1)S(1)} %shard_map.85.mine_ref.refs_7_, bf16[192,1024]{1,0:T(8,128)(2,1)S(1)} %collective-permute-done.21.theirs_ref.refs_11_, bf16[1024,2048]{1,0:T(8,128)(2,1)S(1)} %copy-done.5, ...), custom_call_target="tpu_custom_call" | custom-call | flops 1024 | bytes 1024 | tf_op jit(solution)/shard_map/pallas_call | solution.py:226
  122.4 8.2 %shard_map.89 = f32[1024,2048]{1,0:T(8,128)} custom-call(s32[5]{0:T(128)S(1)} %stack.63.at_ref, bf16[192,1024]{1,0:T(8,128)(2,1)} %refs_0_.5, bf16[192,1024]{1,0:T(8,128)(2,1)} %collective-permute-done.15.refs_1_, bf16[192,1024]{1,0:T(8,128)(2,1)} %collective-permute-done.17.refs_2_, bf16[192,1024]{1,0:T(8,128)(2,1)S(1)} %collective-permute-done.20.refs_3_, ...), custom_call_target="tpu_custom_call" | custom-call | flops 1024 | bytes 1024 | tf_op jit(solution)/shard_map/pallas_call | solution.py:110
  130.7 3.6 %collective-permute-done.24.refs_0_ = bf16[192,1024]{1,0:T(8,128)(2,1)S(1)} collective-permute-done((bf16[192,1024]{1,0:T(8,128)(2,1)S(1)}, bf16[192,1024]{1,0:T(8,128)(2,1)S(1)}, u32[]{:S(2)}, u32[]{:S(2)}) %collective-permute-start.24) | collective-permute-done | bytes 393248 | tf_op jit(solution)/shard_map/ppermute | solution.py:316
  134.3 2.8 %shard_map.90 = bf16[192,1024]{1,0:T(8,128)(2,1)} custom-call(s32[1]{0:T(128)} %bitcast.core_ref, bf16[192,1024]{1,0:T(8,128)(2,1)S(1)} %shard_map.87.refs_4_.mine_ref, bf16[192,1024]{1,0:T(8,128)(2,1)S(1)} %collective-permute-done.23.refs_8_.theirs_ref, bf16[1024,2048]{1,0:T(8,128)(2,1)S(1)} %copy-done.5, bf16[192,1024]{1,0:T(8,128)(2,1)S(1)} %collective-permute-done.24.refs_0_), custom_call_target="tpu_custom_call" | custom-call | flops 1024 | bytes 1024 | tf_op jit(solution)/shard_map/pallas_call | solution.py:226
  (95 shorter events, 14.9 us)
Async XLA Ops:
  0.6 21.9 %collective-permute-start.5 = (bf16[2048,1024]{1,0:T(8,128)(2,1)}, bf16[2048,1024]{1,0:T(8,128)(2,1)}, u32[]{:S(2)}, u32[]{:S(2)}) collective-permute-start(bf16[2048,1024]{1,0:T(8,128)(2,1)} %mine_ref.7), channel_id=1, source_target_pairs={{0,4},{4,0},{8,12},{12,8},{1,5},{5,1},{9,13},{13,9},{2,6},{6,2},{1... | collective-permute-start | bytes 12582920 | tf_op jit(solution)/shard_map/ppermute | solution.py:263
  1.1 20.9 %collective-permute-start.3 = (bf16[192,2048]{1,0:T(8,128)(2,1)}, bf16[192,2048]{1,0:T(8,128)(2,1)S(1)}, u32[]{:S(2)}, u32[]{:S(2)}) collective-permute-start(bf16[192,2048]{1,0:T(8,128)(2,1)} %refs_0_.3), channel_id=1, source_target_pairs={{0,8},{4,12},{8,0},{12,4},{1,9},{5,13},{9,1},{13,5},{2,10},{6,14},... | collective-permute-start | bytes 2359304 | tf_op jit(solution)/shard_map/ppermute | solution.py:261
  3.7 13.3 %collective-permute-start = (bf16[192,1024]{1,0:T(8,128)(2,1)}, bf16[192,1024]{1,0:T(8,128)(2,1)S(1)}, u32[]{:S(2)}, u32[]{:S(2)}) collective-permute-start(bf16[192,1024]{1,0:T(8,128)(2,1)} %refs_0_.4), channel_id=1, source_target_pairs={{0,1},{1,2},{2,3},{3,0},{4,5},{5,6},{6,7},{7,4},{8,9},{9,10},{10,1... | collective-permute-start | bytes 1179656 | tf_op jit(solution)/shard_map/ppermute | solution.py:285
  5.3 16.8 %collective-permute-start.4 = (bf16[192,1024]{1,0:T(8,128)(2,1)}, bf16[192,1024]{1,0:T(8,128)(2,1)S(1)}, u32[]{:S(2)}, u32[]{:S(2)}) collective-permute-start(bf16[192,1024]{1,0:T(8,128)(2,1)} %refs_0_.4), channel_id=1, source_target_pairs={{0,4},{4,0},{8,12},{12,8},{1,5},{5,1},{9,13},{13,9},{2,6},{6,2},{1... | collective-permute-start | bytes 1179656 | tf_op jit(solution)/shard_map/ppermute | solution.py:267
  17.0 13.6 %copy-start.8 = (bf16[192,1024]{1,0:T(8,128)(2,1)}, bf16[192,1024]{1,0:T(8,128)(2,1)S(1)}, u32[]{:S(2)}) copy-start(bf16[192,1024]{1,0:T(8,128)(2,1)S(1)} %collective-permute-done.cot_ref.refs_1_) | copy-start | bytes 1179652
  17.0 13.6 %collective-permute-start.2 = (bf16[192,1024]{1,0:T(8,128)(2,1)S(1)}, bf16[192,1024]{1,0:T(8,128)(2,1)}, u32[]{:S(2)}, u32[]{:S(2)}) collective-permute-start(bf16[192,1024]{1,0:T(8,128)(2,1)S(1)} %collective-permute-done.cot_ref.refs_1_), channel_id=1, source_target_pairs={{0,4},{4,0},{8,12},{12,8},{1,5},{5,1},{9,13},{13,9},{2,6},{6,2},{1... | collective-permute-start | bytes 1179656 | tf_op jit(solution)/shard_map/ppermute | solution.py:267
  17.0 19.2 %collective-permute-start.1 = (bf16[192,1024]{1,0:T(8,128)(2,1)S(1)}, bf16[192,1024]{1,0:T(8,128)(2,1)S(1)}, u32[]{:S(2)}, u32[]{:S(2)}) collective-permute-start(bf16[192,1024]{1,0:T(8,128)(2,1)S(1)} %collective-permute-done.cot_ref.refs_1_), channel_id=1, source_target_pairs={{0,1},{1,2},{2,3},{3,0},{4,5},{5,6},{6,7},{7,4},{8,9},{9,10},{10,1... | collective-permute-start | bytes 1179656 | tf_op jit(solution)/shard_map/ppermute | solution.py:294
  22.1 7.6 %copy-start.15 = (bf16[192,2048]{1,0:T(8,128)(2,1)}, bf16[192,2048]{1,0:T(8,128)(2,1)S(1)}, u32[]{:S(2)}) copy-start(bf16[192,2048]{1,0:T(8,128)(2,1)S(1)} %collective-permute-done.3.refs_1_) | copy-start | bytes 2359300
  22.1 25.4 %collective-permute-start.7 = (bf16[192,2048]{1,0:T(8,128)(2,1)}, bf16[192,2048]{1,0:T(8,128)(2,1)S(1)}, u32[]{:S(2)}, u32[]{:S(2)}) collective-permute-start(bf16[192,2048]{1,0:T(8,128)(2,1)} %refs_0_.3), channel_id=1, source_target_pairs={{0,4},{4,0},{8,12},{12,8},{1,5},{5,1},{9,13},{13,9},{2,6},{6,2},{1... | collective-permute-start | bytes 2359304 | tf_op jit(solution)/shard_map/ppermute | solution.py:298
  22.1 26.2 %collective-permute-start.8 = (bf16[192,2048]{1,0:T(8,128)(2,1)S(1)}, bf16[192,2048]{1,0:T(8,128)(2,1)S(1)}, u32[]{:S(2)}, u32[]{:S(2)}) collective-permute-start(bf16[192,2048]{1,0:T(8,128)(2,1)S(1)} %collective-permute-done.3.refs_1_), channel_id=1, source_target_pairs={{0,4},{4,0},{8,12},{12,8},{1,5},{5,1},{9,13},{13,9},{2,6},{6,2},{1... | collective-permute-start | bytes 2359304 | tf_op jit(solution)/shard_map/ppermute | solution.py:298
  36.1 10.4 %copy-start.10 = (bf16[192,1024]{1,0:T(8,128)(2,1)}, bf16[192,1024]{1,0:T(8,128)(2,1)S(1)}, u32[]{:S(2)}) copy-start(bf16[192,1024]{1,0:T(8,128)(2,1)S(1)} %collective-permute-done.1.cot_ref.refs_2_) | copy-start | bytes 1179652
  36.1 3.6 %collective-permute-start.6 = (bf16[192,1024]{1,0:T(8,128)(2,1)S(1)}, bf16[192,1024]{1,0:T(8,128)(2,1)S(1)}, u32[]{:S(2)}, u32[]{:S(2)}) collective-permute-start(bf16[192,1024]{1,0:T(8,128)(2,1)S(1)} %collective-permute-done.1.cot_ref.refs_2_), channel_id=1, source_target_pairs={{0,4},{4,0},{8,12},{12,8},{1,5},{5,1},{9,13},{13,9},{2,6},{6,2},{1... | collective-permute-start | bytes 1179656 | tf_op jit(solution)/shard_map/ppermute | solution.py:267
  36.2 16.0 %collective-permute-start.10 = (bf16[192,1024]{1,0:T(8,128)(2,1)}, bf16[192,1024]{1,0:T(8,128)(2,1)}, u32[]{:S(2)}, u32[]{:S(2)}) collective-permute-start(bf16[192,1024]{1,0:T(8,128)(2,1)} %get-tuple-element.33), channel_id=1, source_target_pairs={{0,8},{4,12},{8,0},{12,4},{1,9},{5,13},{9,1},{13,5},{2,10},{6,14},... | collective-permute-start | bytes 1179656 | tf_op jit(solution)/shard_map/ppermute | solution.py:274
  38.0 17.1 %collective-permute-start.9 = (bf16[192,1024]{1,0:T(8,128)(2,1)S(1)}, bf16[192,1024]{1,0:T(8,128)(2,1)}, u32[]{:S(2)}, u32[]{:S(2)}) collective-permute-start(bf16[192,1024]{1,0:T(8,128)(2,1)S(1)} %collective-permute-done.1.cot_ref.refs_2_), channel_id=1, source_target_pairs={{0,1},{1,2},{2,3},{3,0},{4,5},{5,6},{6,7},{7,4},{8,9},{9,10},{10,1... | collective-permute-start | bytes 1179656 | tf_op jit(solution)/shard_map/ppermute | solution.py:294
  41.9 7.3 %copy-start.16 = (bf16[192,2048]{1,0:T(8,128)(2,1)S(1)}, bf16[192,2048]{1,0:T(8,128)(2,1)}, u32[]{:S(2)}) copy-start(bf16[192,2048]{1,0:T(8,128)(2,1)} %copy-done.15) | copy-start | bytes 2359300
  41.9 10.3 %copy-start.22 = (f32[192,1024]{1,0:T(8,128)S(1)}, f32[192,1024]{1,0:T(8,128)}, u32[]{:S(2)}) copy-start(f32[192,1024]{1,0:T(8,128)} %copy-done.21) | copy-start | bytes 2359300
  55.1 2.2 %collective-permute-start.11 = (bf16[192,1024]{1,0:T(8,128)(2,1)}, bf16[192,1024]{1,0:T(8,128)(2,1)S(1)}, u32[]{:S(2)}, u32[]{:S(2)}) collective-permute-start(bf16[192,1024]{1,0:T(8,128)(2,1)} %collective-permute-done.9.cot_ref.refs_3_), channel_id=1, source_target_pairs={{0,4},{4,0},{8,12},{12,8},{1,5},{5,1},{9,13},{13,9},{2,6},{6,2},{1... | collective-permute-start | bytes 1179656 | tf_op jit(solution)/shard_map/ppermute | solution.py:267
  55.1 13.6 %collective-permute-start.15 = (bf16[192,1024]{1,0:T(8,128)(2,1)}, bf16[192,1024]{1,0:T(8,128)(2,1)}, u32[]{:S(2)}, u32[]{:S(2)}) collective-permute-start(bf16[192,1024]{1,0:T(8,128)(2,1)} %refs_0_.5), channel_id=1, source_target_pairs={{0,1},{1,2},{2,3},{3,0},{4,5},{5,6},{6,7},{7,4},{8,9},{9,10},{10,1... | collective-permute-start | bytes 1179656 | tf_op jit(solution)/shard_map/ppermute | solution.py:302
  56.7 20.3 %collective-permute-start.13 = (bf16[192,1024]{1,0:T(8,128)(2,1)}, bf16[192,1024]{1,0:T(8,128)(2,1)}, u32[]{:S(2)}, u32[]{:S(2)}) collective-permute-start(bf16[192,1024]{1,0:T(8,128)(2,1)} %get-tuple-element.35), channel_id=1, source_target_pairs={{0,8},{4,12},{8,0},{12,4},{1,9},{5,13},{9,1},{13,5},{2,10},{6,14},... | collective-permute-start | bytes 1179656 | tf_op jit(solution)/shard_map/ppermute | solution.py:274
  57.2 22.1 %collective-permute-start.16 = (bf16[192,1024]{1,0:T(8,128)(2,1)}, bf16[192,1024]{1,0:T(8,128)(2,1)}, u32[]{:S(2)}, u32[]{:S(2)}) collective-permute-start(bf16[192,1024]{1,0:T(8,128)(2,1)} %shard_map.80.mine_ref.refs_5_), channel_id=1, source_target_pairs={{0,4},{4,0},{8,12},{12,8},{1,5},{5,1},{9,13},{13,9},{2,6},{6,2},{1... | collective-permute-start | bytes 1179656 | tf_op jit(solution)/shard_map/ppermute | solution.py:279
  68.8 30.1 %collective-permute-start.17 = (bf16[192,1024]{1,0:T(8,128)(2,1)}, bf16[192,1024]{1,0:T(8,128)(2,1)}, u32[]{:S(2)}, u32[]{:S(2)}) collective-permute-start(bf16[192,1024]{1,0:T(8,128)(2,1)} %collective-permute-done.15.refs_1_), channel_id=1, source_target_pairs={{0,1},{1,2},{2,3},{3,0},{4,5},{5,6},{6,7},{7,4},{8,9},{9,10},{10,1... | collective-permute-start | bytes 1179656 | tf_op jit(solution)/shard_map/ppermute | solution.py:310
  76.5 22.7 %collective-permute-start.14 = (bf16[192,1024]{1,0:T(8,128)(2,1)}, bf16[192,1024]{1,0:T(8,128)(2,1)}, u32[]{:S(2)}, u32[]{:S(2)}) collective-permute-start(bf16[192,1024]{1,0:T(8,128)(2,1)} %get-tuple-element.43), channel_id=1, source_target_pairs={{0,8},{4,12},{8,0},{12,4},{1,9},{5,13},{9,1},{13,5},{2,10},{6,14},... | collective-permute-start | bytes 1179656 | tf_op jit(solution)/shard_map/ppermute | solution.py:274
  79.3 22.4 %collective-permute-start.18 = (bf16[192,1024]{1,0:T(8,128)(2,1)S(1)}, bf16[192,1024]{1,0:T(8,128)(2,1)}, u32[]{:S(2)}, u32[]{:S(2)}) collective-permute-start(bf16[192,1024]{1,0:T(8,128)(2,1)S(1)} %shard_map.82.mine_ref.refs_6_), channel_id=1, source_target_pairs={{0,4},{4,0},{8,12},{12,8},{1,5},{5,1},{9,13},{13,9},{2,6},{6,2},{1... | collective-permute-start | bytes 1179656 | tf_op jit(solution)/shard_map/ppermute | solution.py:279
  83.4 18.4 %collective-permute-start.19 = (bf16[192,1024]{1,0:T(8,128)(2,1)}, bf16[192,1024]{1,0:T(8,128)(2,1)}, u32[]{:S(2)}, u32[]{:S(2)}) collective-permute-start(bf16[192,1024]{1,0:T(8,128)(2,1)} %shard_map.83), channel_id=1, source_target_pairs={{0,1},{1,2},{2,3},{3,0},{4,5},{5,6},{6,7},{7,4},{8,9},{9,10},{10,1... | collective-permute-start | bytes 1179656 | tf_op jit(solution)/shard_map/ppermute | solution.py:308
  84.9 23.2 %collective-permute-start.12 = (bf16[192,1024]{1,0:T(8,128)(2,1)}, bf16[192,1024]{1,0:T(8,128)(2,1)S(1)}, u32[]{:S(2)}, u32[]{:S(2)}) collective-permute-start(bf16[192,1024]{1,0:T(8,128)(2,1)} %copy-done.27), channel_id=1, source_target_pairs={{0,8},{4,12},{8,0},{12,4},{1,9},{5,13},{9,1},{13,5},{2,10},{6,14},... | collective-permute-start | bytes 1179656 | tf_op jit(solution)/shard_map/ppermute | solution.py:274
  89.2 10.0 %copy-start.24 = (f32[192,1024]{1,0:T(8,128)S(1)}, f32[192,1024]{1,0:T(8,128)}, u32[]{:S(2)}) copy-start(f32[192,1024]{1,0:T(8,128)} %copy-done.23) | copy-start | bytes 2359300
  98.9 14.0 %collective-permute-start.20 = (bf16[192,1024]{1,0:T(8,128)(2,1)}, bf16[192,1024]{1,0:T(8,128)(2,1)S(1)}, u32[]{:S(2)}, u32[]{:S(2)}) collective-permute-start(bf16[192,1024]{1,0:T(8,128)(2,1)} %collective-permute-done.17.refs_2_), channel_id=1, source_target_pairs={{0,1},{1,2},{2,3},{3,0},{4,5},{5,6},{6,7},{7,4},{8,9},{9,10},{10,1... | collective-permute-start | bytes 1179656 | tf_op jit(solution)/shard_map/ppermute | solution.py:310
  99.2 8.8 %copy-start.14 = (f32[192,1024]{1,0:T(8,128)S(1)}, f32[192,1024]{1,0:T(8,128)}, u32[]{:S(2)}) copy-start(f32[192,1024]{1,0:T(8,128)} %copy-done.13) | copy-start | bytes 2359300
  105.0 15.3 %collective-permute-start.22 = (bf16[192,1024]{1,0:T(8,128)(2,1)S(1)}, bf16[192,1024]{1,0:T(8,128)(2,1)S(1)}, u32[]{:S(2)}, u32[]{:S(2)}) collective-permute-start(bf16[192,1024]{1,0:T(8,128)(2,1)S(1)} %shard_map.86), channel_id=1, source_target_pairs={{0,1},{1,2},{2,3},{3,0},{4,5},{5,6},{6,7},{7,4},{8,9},{9,10},{10,1... | collective-permute-start | bytes 1179656 | tf_op jit(solution)/shard_map/ppermute | solution.py:308
  108.0 12.3 %collective-permute-start.21 = (bf16[192,1024]{1,0:T(8,128)(2,1)S(1)}, bf16[192,1024]{1,0:T(8,128)(2,1)S(1)}, u32[]{:S(2)}, u32[]{:S(2)}) collective-permute-start(bf16[192,1024]{1,0:T(8,128)(2,1)S(1)} %shard_map.85.mine_ref.refs_7_), channel_id=1, source_target_pairs={{0,4},{4,0},{8,12},{12,8},{1,5},{5,1},{9,13},{13,9},{2,6},{6,2},{1... | collective-permute-start | bytes 1179656 | tf_op jit(solution)/shard_map/ppermute | solution.py:279
  109.2 13.3 %collective-permute-start.23 = (bf16[192,1024]{1,0:T(8,128)(2,1)S(1)}, bf16[192,1024]{1,0:T(8,128)(2,1)S(1)}, u32[]{:S(2)}, u32[]{:S(2)}) collective-permute-start(bf16[192,1024]{1,0:T(8,128)(2,1)S(1)} %shard_map.87.refs_4_.mine_ref), channel_id=1, source_target_pairs={{0,4},{4,0},{8,12},{12,8},{1,5},{5,1},{9,13},{13,9},{2,6},{6,2},{1... | collective-permute-start | bytes 1179656 | tf_op jit(solution)/shard_map/ppermute | solution.py:279
  122.4 11.9 %collective-permute-start.24 = (bf16[192,1024]{1,0:T(8,128)(2,1)S(1)}, bf16[192,1024]{1,0:T(8,128)(2,1)S(1)}, u32[]{:S(2)}, u32[]{:S(2)}) collective-permute-start(bf16[192,1024]{1,0:T(8,128)(2,1)S(1)} %shard_map.88), channel_id=1, source_target_pairs={{0,1},{1,2},{2,3},{3,0},{4,5},{5,6},{6,7},{7,4},{8,9},{9,10},{10,1... | collective-permute-start | bytes 1179656 | tf_op jit(solution)/shard_map/ppermute | solution.py:316
  (21 other events, 47.7 us)

commit v6 on v1

v6 whole, which is shorter than its diff:
```python
import functools
import math

import jax
import jax.numpy as jnp
from jax import lax
from jax.experimental import pallas as pl
from jax.experimental.pallas import tpu as pltpu
from jax.sharding import PartitionSpec as P

LAST = (((1,), (1,)), ((), ()))
FIRST = (((0,), (0,)), ((), ()))
MIB = 1024 * 1024
LITTLE = pl.CostEstimate(flops=1024, bytes_accessed=1024, transcendentals=0)


def gelu_parts(values):
    v = values.astype(jnp.float32)
    tanh_val = jnp.tanh(0.7978845608 * (v + 0.044715 * v * v * v))
    return v, tanh_val


def gelu(values):
    v, tanh_val = gelu_parts(values)
    return 0.5 * v * (1.0 + tanh_val)


def gelu_slope(values):
    v, tanh_val = gelu_parts(values)
    return 0.5 * (1.0 + tanh_val) + 0.5 * v * (1.0 - tanh_val * tanh_val) * 0.7978845608 * (
        1.0 + 3.0 * 0.044715 * v * v
    )


def dot(a, b, dims):
    return lax.dot_general(a, b, dims, preferred_element_type=jnp.float32)


def after(value, *first):
    return lax.optimization_barrier((value, *first))[0] if first else value


def tile_of(extent):
    return next(t for t in (256, 128, extent) if extent % t == 0)


def in_vmem():
    return pl.BlockSpec(memory_space=pltpu.VMEM)


def block(index, size, first=0):
    return pl.ds(pl.multiple_of(index * size + first, math.gcd(size, first)), size - first)


def block_at(place_ref, step, cols):
    return lax.rem(place_ref[0] - step + cols, cols)


def core_of(place_ref):
    return lax.rem(place_ref[1], 2)


def call(kernel, place, operands, outs, mib, grid=(1,), in_specs=None, out_specs=None, scratch=()):
    return pl.pallas_call(
        kernel,
        out_shape=outs,
        grid_spec=pltpu.PrefetchScalarGridSpec(
            num_scalar_prefetch=1,
            grid=grid,
            in_specs=in_specs or [in_vmem() for _ in operands],
            out_specs=out_specs or jax.tree.map(lambda _: in_vmem(), outs),
            scratch_shapes=scratch,
        ),
        compiler_params=pltpu.CompilerParams(vmem_limit_bytes=mib * MIB),
        cost_estimate=LITTLE,
    )(place, *operands)


def lay_out_kernel(shifts, rows, place_ref, *refs):
    out_ref = refs[-1]
    tokens = refs[0].shape[0]
    for i, ref in enumerate(refs[:-1]):
        owner = lax.rem(place_ref[1] - shifts[i % len(shifts)] + rows, rows)
        if i >= len(shifts):
            owner = owner + 1 - 2 * lax.rem(owner, 2)
        out_ref[block(owner, tokens), :] = ref[...]


def lay_out_call(place, blocks, shifts, rows):
    tokens, hidden = blocks[0].shape
    out = jax.ShapeDtypeStruct((tokens * len(blocks), hidden), jnp.bfloat16)
    return call(functools.partial(lay_out_kernel, shifts, rows), place, blocks, out, 8)


def hidden_kernel(place_ref, cot_ref, pair_ref, mine_ref, theirs_ref, part_ref, sent_ref):
    half = part_ref.shape[1]
    tile = tile_of(half)
    for first in range(0, half, tile):
        rows = pl.ds(pl.multiple_of(core_of(place_ref) * half + first, tile), tile)
        part = dot(cot_ref[...], mine_ref[rows, :], LAST)
        part = part + dot(pair_ref[...], theirs_ref[rows, :], LAST)
        part_ref[:, pl.ds(first, tile)] = part
        sent_ref[:, pl.ds(first, tile)] = part.astype(jnp.bfloat16)


def hidden_call(place, cot, cot_pair, down_mine, down_pair):
    shape = (cot.shape[0], down_mine.shape[0] // 2)
    outs = [jax.ShapeDtypeStruct(shape, jnp.float32), jax.ShapeDtypeStruct(shape, jnp.bfloat16)]
    return call(hidden_kernel, place, [cot, cot_pair, down_mine, down_pair], outs, 12)


def pre_grad_kernel(step, cols, place_ref, pre_ref, part_ref, *refs):
    out_ref = refs[-1]
    tokens, half = part_ref.shape
    rows = 64 if tokens % 64 == 0 else tokens
    columns = block(core_of(place_ref), half)
    start = block_at(place_ref, step, cols) * tokens
    for first in range(0, tokens, rows):
        here = pl.ds(first, rows)
        total = part_ref[here, :]
        for other in refs[:-1]:
            total = total + other[here, :].astype(jnp.float32)
        v = pre_ref[pl.ds(pl.multiple_of(start + first, rows), rows), columns]
        out_ref[here, :] = (total * gelu_slope(v)).astype(jnp.bfloat16)


def pre_grad_call(place, step, cols, pre_all, part, others):
    out = jax.ShapeDtypeStruct(part.shape, jnp.bfloat16)
    kernel = functools.partial(pre_grad_kernel, step, cols)
    return call(kernel, place, [pre_all, part, *others], out, 8)


def share_kernel(place_ref, mine_ref, theirs_ref, up_ref, *refs):
    out_ref = refs[-1]
    features, half = up_ref.shape[0], mine_ref.shape[1]
    tile = tile_of(features)
    left, right = block(core_of(place_ref), half), block(1 - core_of(place_ref), half)
    for first in range(0, features, tile):
        here = pl.ds(first, tile)
        total = dot(mine_ref[...], up_ref[here, left], LAST)
        total = total + dot(theirs_ref[...], up_ref[here, right], LAST)
        for arrived in refs[:-1]:
            total = total + arrived[:, here].astype(jnp.float32)
        out_ref[:, here] = total.astype(jnp.bfloat16)


def share_call(place, mine, theirs, up_weight, arrived):
    out = jax.ShapeDtypeStruct((mine.shape[0], up_weight.shape[0]), jnp.bfloat16)
    return call(share_kernel, place, [mine, theirs, up_weight, *arrived], out, 12)


def grad_down_kernel(blocks, scale, place_ref, pre_ref, *refs):
    cot_refs, out_ref, cots = refs[:blocks], refs[-2], refs[-1]
    tokens = cot_refs[0].shape[0]

    @pl.when(pl.program_id(0) == 0)
    def _():
        for s in range(blocks):
            cots[block(block_at(place_ref, s, blocks), tokens), :] = cot_refs[s][...]

    activation = gelu(pre_ref[...]).astype(jnp.bfloat16)
    out_ref[...] = dot(activation, cots[...], FIRST) * scale


def grad_down_call(place, pre_all, cots, scale):
    total, hidden = pre_all.shape
    features = cots[0].shape[1]
    tile = tile_of(hidden)
    return call(
        functools.partial(grad_down_kernel, len(cots), scale),
        place,
        [pre_all, *cots],
        jax.ShapeDtypeStruct((hidden, features), jnp.float32),
        14,
        grid=(hidden // tile,),
        in_specs=[pl.BlockSpec((total, tile), lambda i, place: (0, i))]
        + [in_vmem() for _ in cots],
        out_specs=pl.BlockSpec((tile, features), lambda i, place: (i, 0)),
        scratch=[pltpu.VMEM((total, features), jnp.bfloat16)],
    )


def grad_up_kernel(blocks, scale, place_ref, *refs):
    ins, mine, pair = (refs[i * blocks : (i + 1) * blocks] for i in range(3))
    out_ref, inputs, grads = refs[3 * blocks :]
    tokens, half = mine[0].shape
    tile = out_ref.shape[0]

    @pl.when(pl.program_id(0) == 0)
    def _():
        left, right = block(core_of(place_ref), half), block(1 - core_of(place_ref), half)
        for s in range(blocks):
            here = pl.ds(s * tokens, tokens)
            inputs[here, :] = ins[s][...]
            grads[here, left] = mine[s][...]
            grads[here, right] = pair[s][...]

    out_ref[...] = dot(inputs[:, block(pl.program_id(0), tile)], grads[...], FIRST) * scale


def grad_up_call(place, ins, mine, pair, scale):
    tokens, features = ins[0].shape
    total = tokens * len(ins)
    hidden = 2 * mine[0].shape[1]
    tile = tile_of(features)
    return call(
        functools.partial(grad_up_kernel, len(mine), scale),
        place,
        [*ins, *mine, *pair],
        jax.ShapeDtypeStruct((features, hidden), jnp.float32),
        18,
        grid=(features // tile,),
        out_specs=pl.BlockSpec((tile, hidden), lambda i, place: (i, 0)),
        scratch=[
            pltpu.VMEM((total, features), jnp.bfloat16),
            pltpu.VMEM((total, hidden), jnp.bfloat16),
        ],
    )


def per_device(inputs, cotangent, preactivation, up_weight, down_weight):
    cols, rows = lax.axis_size("col"), lax.axis_size("row")
    place = jnp.stack([lax.axis_index("col"), lax.axis_index("row")]).astype(jnp.int32)
    cotangent, preactivation, down_weight = (
        after(x, place) for x in (cotangent, preactivation, down_weight)
    )
    ring = [(i, (i + 1) % cols) for i in range(cols)]
    pair = [(i, i ^ 1) for i in range(rows)]
    shifts = range(0, rows, 2)
    over_x = [[(i, (i + shift) % rows) for i in range(rows)] for shift in shifts[1:]]
    scale = 1.0 / math.sqrt(cotangent.shape[0] * cols)

    pres = [preactivation] + [lax.ppermute(preactivation, "row", to) for to in over_x]
    down_pair = lax.ppermute(down_weight, "row", pair)
    parts, sent, others, mine, theirs = ([None] * cols for _ in range(5))

    def hidden_part(s, *first):
        cot_pair = after(lax.ppermute(cots[s], "row", pair), *first)
        parts[s], sent[s] = hidden_call(place, cots[s], cot_pair, down_weight, down_pair)

    def exchange(s, *first):
        values = after(sent[s], *first)
        others[s] = [lax.ppermute(values, "row", to) for to in over_x]

    def pre_grad(s, *first):
        mine[s] = pre_grad_call(after(place, *first), s, cols, pre_all, parts[s], others[s])
        theirs[s] = lax.ppermute(mine[s], "row", pair)

    def share(s, arrived, *first):
        return share_call(after(place, *first), mine[s], theirs[s], up_weight, arrived)

    cots, ins = [cotangent], [inputs]
    arriving = lax.ppermute(cotangent, "col", ring)
    for s in range(1, cols):
        if s == 2:
            arriving = after(arriving, sent[0])
        elif s > 2:
            arriving = after(arriving, sent[s - 1])
        cots.append(arriving)
        if s < cols - 1:
            arriving = lax.ppermute(arriving, "col", ring)
            hidden_part(s)
            exchange(s)
        if s == 1:
            hidden_part(0, sent[1], *pres[1:])
            pres = pres + [lax.ppermute(after(p, sent[1]), "row", pair) for p in pres]

    last = cols - 1
    pre_all = lay_out_call(after(place, sent[last - 1]), pres, shifts, rows)
    pre_grad(1, sent[last - 1])
    ins.append(lax.ppermute(after(inputs, cots[last - 1]), "col", ring))
    sums = share(1, [], mine[1])
    pre_grad(2, sums)
    hidden_part(last, mine[2], ins[1])
    exchange(last)
    exchange(0, sent[last])
    grad_down = grad_down_call(after(place, sums, sent[last]), pre_all, cots, scale)
    late = grad_down
    for s in range(2, cols):
        following = (s + 1) % cols
        pre_grad(following, late)
        arrived = lax.ppermute(sums, "col", ring)
        ins.append(lax.ppermute(ins[-1], "col", ring))
        sums = late = share(s, [arrived], mine[following], ins[s])
    arrived = lax.ppermute(sums, "col", ring)
    grad_up = grad_up_call(after(place, sums), ins, mine, theirs, scale)
    sums = share(0, [arrived], grad_up)
    return (sums, grad_up, grad_down)


def solution(mesh):
    placed = (
        P(("groups", "col"), "row"),
        P(("groups", "col"), "row"),
        P(("groups", "row"), "col"),
        P("row", "col"),
        P("col", "row"),
    )
    return jax.shard_map(
        per_device,
        mesh=mesh,
        in_specs=placed,
        out_specs=(
            P(("groups", "col"), "row"),
            P(("groups", "row"), "col"),
            P(("groups", "col"), "row"),
        ),
        check_vma=False,
    )
```

time: 158 us -> 106 us (0.67)
  matrix products: 40.9 us -> 0 us
  Pallas kernels: 0 us -> 38 us
  local copies, waits for them, and re-layouts: 31.2 us -> 2.22 us
  between operations: 14.4 us -> 0.87 us
  other arithmetic: 6.64 us -> 0.08 us
  waiting for transfers between devices: 51.4 us -> 53.8 us
  starting transfers between devices: 12.9 us -> 10.6 us
    dot_general x18 -> x0, matrix products: 40.9 us -> none  [dot(): return lax.dot_general(a, b, dims, preferred_element_type=jnp.float32)]
    pallas_call x0 -> x15, Pallas kernels: none -> 38 us  [call(): pl.pallas_call(kernel, out_shape=outs, grid_spec=pltpu.PrefetchScalarGrid...]
    dynamic_update_slice x8 -> x0, local copies, waits for them, and re-layouts: 15.3 us -> none  [the longest x4 15.2 us: per_device(): lax.dynamic_update_slice(pre_grad_all, pre_grad_pair, (at, (1 - core) * h...]
    unnamed x23 -> x12, local copies, waits for them, and re-layouts: 12.2 us -> 2.22 us
    dynamic_update_slice x4 -> x0, other arithmetic: 6.64 us -> none  [per_device(): lax.dynamic_update_slice(pre_grad_all, pre_grad, (at, core * half))]
    ppermute x19 -> x25, waiting for transfers between devices: 50.7 us -> 53.8 us  [the longest x3 11.8 us: per_device(): arrived = lax.ppermute(sums, 'col', ring)]
    dynamic_slice x1 -> x0, local copies, waits for them, and re-layouts: 3.08 us -> none  [per_device(): lax.dynamic_slice(down_weight, ((1 - core) * half, 0), (half, features))]
    ppermute x19 -> x25, starting transfers between devices: 12.8 us -> 10.6 us  [the longest x4 3.81 us: exchange(): others[s] = [lax.ppermute(values, 'row', to) for to in over_x]]
  transfers between devices with their start and end apart: 21 -> 25, of which waited for: 7 -> 12; matrix products, arithmetic and copies ran while one was open for 46% -> 0% of each run, Pallas kernels for 0% -> 33%
where the time goes in v6:
time: 106 us
  waiting for transfers between devices  53.8 us (51%)
  Pallas kernels  38 us (36%)
  starting transfers between devices  10.6 us (10%)
  local copies, waits for them, and re-layouts  2.22 us (2%)
    pallas_call x15, Pallas kernels, call(): pl.pallas_call(kernel, out_shape=outs, grid_spec=pltpu.PrefetchScalarGrid...  38 us
    ppermute x3, waiting for transfers between devices, per_device(): arrived = lax.ppermute(sums, 'col', ring)  11.8 us
    ppermute x1, waiting for transfers between devices, per_device(): arriving = lax.ppermute(cotangent, 'col', ring)  10.5 us
    ppermute x2, waiting for transfers between devices, per_device(): ins.append(lax.ppermute(ins[-1], 'col', ring))  9.92 us
    ppermute x1, waiting for transfers between devices, per_device(): ins.append(lax.ppermute(after(inputs, cots[last - 1]), 'col', ring))  7.7 us
    ppermute x4, waiting for transfers between devices, exchange(): others[s] = [lax.ppermute(values, 'row', to) for to in over_x]  6.75 us
    ppermute x2, waiting for transfers between devices, per_device(): arriving = lax.ppermute(arriving, 'col', ring)  3.83 us
    ppermute x4, starting transfers between devices, exchange(): others[s] = [lax.ppermute(values, 'row', to) for to in over_x]  3.81 us
  transfers between devices with their start and end apart: 25, of which 12 were waited for; matrix products, arithmetic and copies ran while one was open for 0% of the time, Pallas kernels for 33%

profile of v6, /device:TPU:0, one launch (start us, length us, event | category | flops | bytes accessed | tf_op | source)
XLA Modules:
  0.0 105.6 jit_solution(746526717607025463)
XLA Ops:
  1.2 2.6 %collective-permute-start = (bf16[192,1024]{1,0:T(8,128)(2,1)}, bf16[192,1024]{1,0:T(8,128)(2,1)S(1)}, u32[]{:S(2)}, u32[]{:S(2)}) collective-permute-start(bf16[192,1024]{1,0:T(8,128)(2,1)} %refs_0_.2), channel_id=1, source_target_pairs={{0,1},{1,2},{2,3},{3,0},{4,5},{5,6},{6,7},{7,4},{8,9},{9,10},{10,1... | collective-permute-start | bytes 1179656 | tf_op jit(solution)/shard_map/ppermute | solution.py:253
  3.8 1.5 %collective-permute-start.5 = (bf16[192,2048]{1,0:T(8,128)(2,1)}, bf16[192,2048]{1,0:T(8,128)(2,1)S(1)}, u32[]{:S(2)}, u32[]{:S(2)}) collective-permute-start(bf16[192,2048]{1,0:T(8,128)(2,1)} %refs_0_.1), channel_id=1, source_target_pairs={{0,8},{4,12},{8,0},{12,4},{1,9},{5,13},{9,1},{13,5},{2,10},{6,14},... | collective-permute-start | bytes 2359304 | tf_op jit(solution)/shard_map/ppermute | solution.py:233
  5.3 10.5 %collective-permute-done.cot_ref.refs_1_ = bf16[192,1024]{1,0:T(8,128)(2,1)S(1)} collective-permute-done((bf16[192,1024]{1,0:T(8,128)(2,1)}, bf16[192,1024]{1,0:T(8,128)(2,1)S(1)}, u32[]{:S(2)}, u32[]{:S(2)}) %collective-permute-start) | collective-permute-done | bytes 393248 | tf_op jit(solution)/shard_map/ppermute | solution.py:253
  16.3 1.7 %collective-permute-done.3.pair_ref = bf16[192,1024]{1,0:T(8,128)(2,1)S(1)} collective-permute-done((bf16[192,1024]{1,0:T(8,128)(2,1)S(1)}, bf16[192,1024]{1,0:T(8,128)(2,1)S(1)}, u32[]{:S(2)}, u32[]{:S(2)}) %collective-permute-start.3) | collective-permute-done | bytes 393248 | tf_op jit(solution)/shard_map/ppermute | solution.py:238
  18.0 2.2 %copy-done = bf16[2048,1024]{1,0:T(8,128)(2,1)S(1)} copy-done((bf16[2048,1024]{1,0:T(8,128)(2,1)S(1)}, bf16[2048,1024]{1,0:T(8,128)(2,1)}, u32[]{:S(2)}) %copy-start) | copy-done | bytes 4194328
  20.2 2.1 %shard_map.76 = (f32[192,1024]{1,0:T(8,128)S(1)}, bf16[192,1024]{1,0:T(8,128)(2,1)S(1)}) custom-call(s32[2]{0:T(128)S(1)} %pad_add_fusion.place_ref, bf16[192,1024]{1,0:T(8,128)(2,1)S(1)} %collective-permute-done.cot_ref.refs_1_, bf16[192,1024]{1,0:T(8,128)(2,1)S(1)} %collective-permute-done.3.pair_ref, bf16[2048,1024]{1,0:T(8,128)(2,1)S(1)} %copy-done, ...), custom_call_target="tpu_custom_call" | custom-call | flops 1024 | bytes 1024 | tf_op jit(solution)/shard_map/pallas_call | solution.py:64
  22.3 1.3 %collective-permute-done.5.refs_1_ = bf16[192,2048]{1,0:T(8,128)(2,1)S(1)} collective-permute-done((bf16[192,2048]{1,0:T(8,128)(2,1)}, bf16[192,2048]{1,0:T(8,128)(2,1)S(1)}, u32[]{:S(2)}, u32[]{:S(2)}) %collective-permute-start.5) | collective-permute-done | bytes 786464 | tf_op jit(solution)/shard_map/ppermute | solution.py:233
  24.1 2.1 %shard_map.77 = (f32[192,1024]{1,0:T(8,128)S(1)}, bf16[192,1024]{1,0:T(8,128)(2,1)S(1)}) custom-call(s32[2]{0:T(128)S(1)} %pad_add_fusion.place_ref, bf16[192,1024]{1,0:T(8,128)(2,1)S(1)} %copy-done.3, bf16[192,1024]{1,0:T(8,128)(2,1)S(1)} %collective-permute-done.2.pair_ref, bf16[2048,1024]{1,0:T(8,128)(2,1)S(1)} %copy-done, ...), custom_call_target="tpu_custom_call" | custom-call | flops 1024 | bytes 1024 | tf_op jit(solution)/shard_map/pallas_call | solution.py:64
  26.2 2.9 %collective-permute-done.1.cot_ref.refs_2_ = bf16[192,1024]{1,0:T(8,128)(2,1)S(1)} collective-permute-done((bf16[192,1024]{1,0:T(8,128)(2,1)S(1)}, bf16[192,1024]{1,0:T(8,128)(2,1)S(1)}, u32[]{:S(2)}, u32[]{:S(2)}) %collective-permute-start.1) | collective-permute-done | bytes 393248 | tf_op jit(solution)/shard_map/ppermute | solution.py:261
  29.1 1.5 %collective-permute-start.9 = (bf16[192,1024]{1,0:T(8,128)(2,1)S(1)}, bf16[192,1024]{1,0:T(8,128)(2,1)S(1)}, u32[]{:S(2)}, u32[]{:S(2)}) collective-permute-start(bf16[192,1024]{1,0:T(8,128)(2,1)S(1)} %get-tuple-element.34), channel_id=1, source_target_pairs={{0,8},{4,12},{8,0},{12,4},{1,9},{5,13},{9,1},{13,5},{2,10},{6,14},... | collective-permute-start | bytes 1179656 | tf_op jit(solution)/shard_map/ppermute | solution.py:243
  31.0 2.1 %shard_map.78 = (f32[192,1024]{1,0:T(8,128)S(1)}, bf16[192,1024]{1,0:T(8,128)(2,1)S(1)}) custom-call(s32[2]{0:T(128)S(1)} %pad_add_fusion.place_ref, bf16[192,1024]{1,0:T(8,128)(2,1)S(1)} %collective-permute-done.1.cot_ref.refs_2_, bf16[192,1024]{1,0:T(8,128)(2,1)S(1)} %collective-permute-done.6.pair_ref, bf16[2048,1024]{1,0:T(8,128)(2,1)S(1)} %copy-done, ...), custom_call_target="tpu_custom_call" | custom-call | flops 1024 | bytes 1024 | tf_op jit(solution)/shard_map/pallas_call | solution.py:64
  33.1 0.8 shard_map.79.pre_ref
  33.9 6.7 %collective-permute-done.9.refs_0_ = bf16[192,1024]{1,0:T(8,128)(2,1)S(1)} collective-permute-done((bf16[192,1024]{1,0:T(8,128)(2,1)S(1)}, bf16[192,1024]{1,0:T(8,128)(2,1)S(1)}, u32[]{:S(2)}, u32[]{:S(2)}) %collective-permute-start.9) | collective-permute-done | bytes 393248 | tf_op jit(solution)/shard_map/ppermute | solution.py:243
  40.6 1.1 %shard_map.80.mine_ref.refs_5_ = bf16[192,1024]{1,0:T(8,128)(2,1)S(1)} custom-call(s32[2]{0:T(128)S(1)} %pad_add_fusion.place_ref, bf16[768,2048]{1,0:T(8,128)(2,1)S(1)} %shard_map.79.pre_ref, f32[192,1024]{1,0:T(8,128)S(1)} %get-tuple-element.43.part_ref, bf16[192,1024]{1,0:T(8,128)(2,1)S(1)} %collective-permute-done.9.refs_0_), custom_call_target="tpu_custom_call" | custom-call | flops 1024 | bytes 1024 | tf_op jit(solution)/shard_map/pallas_call | solution.py:64
  41.8 1.6 %collective-permute-start.13 = (bf16[192,1024]{1,0:T(8,128)(2,1)S(1)}, bf16[192,1024]{1,0:T(8,128)(2,1)S(1)}, u32[]{:S(2)}, u32[]{:S(2)}) collective-permute-start(bf16[192,1024]{1,0:T(8,128)(2,1)S(1)} %get-tuple-element.39), channel_id=1, source_target_pairs={{0,8},{4,12},{8,0},{12,4},{1,9},{5,13},{9,1},{13,5},{2,10},{6,14},... | collective-permute-start | bytes 1179656 | tf_op jit(solution)/shard_map/ppermute | solution.py:243
  43.4 1.0 collective-permute-done.11.cot_ref.refs_3_
  44.4 7.7 %collective-permute-done.14.refs_1_ = bf16[192,1024]{1,0:T(8,128)(2,1)S(1)} collective-permute-done((bf16[192,1024]{1,0:T(8,128)(2,1)S(1)}, bf16[192,1024]{1,0:T(8,128)(2,1)S(1)}, u32[]{:S(2)}, u32[]{:S(2)}) %collective-permute-start.14) | collective-permute-done | bytes 393248 | tf_op jit(solution)/shard_map/ppermute | solution.py:271
  52.1 2.1 %shard_map.81 = bf16[192,1024]{1,0:T(8,128)(2,1)S(1)} custom-call(s32[2]{0:T(128)S(1)} %pad_add_fusion.place_ref, bf16[192,1024]{1,0:T(8,128)(2,1)S(1)} %shard_map.80.mine_ref.refs_5_, bf16[192,1024]{1,0:T(8,128)(2,1)S(1)} %collective-permute-done.10.theirs_ref.refs_9_, bf16[1024,2048]{1,0:T(8,128)(2,1)S(1)} %copy-done.2), custom_call_target="tpu_custom_call" | custom-call | flops 1024 | bytes 1024 | tf_op jit(solution)/shard_map/pallas_call | solution.py:64
  54.2 1.1 %shard_map.82.mine_ref.refs_6_ = bf16[192,1024]{1,0:T(8,128)(2,1)S(1)} custom-call(s32[2]{0:T(128)S(1)} %pad_add_fusion.place_ref, bf16[768,2048]{1,0:T(8,128)(2,1)S(1)} %shard_map.79.pre_ref, f32[192,1024]{1,0:T(8,128)S(1)} %get-tuple-element.47.part_ref, bf16[192,1024]{1,0:T(8,128)(2,1)S(1)} %collective-permute-done.13.refs_0_), custom_call_target="tpu_custom_call" | custom-call | flops 1024 | bytes 1024 | tf_op jit(solution)/shard_map/pallas_call | solution.py:64
  55.3 2.1 %shard_map.83 = (f32[192,1024]{1,0:T(8,128)S(1)}, bf16[192,1024]{1,0:T(8,128)(2,1)S(1)}) custom-call(s32[2]{0:T(128)S(1)} %pad_add_fusion.place_ref, bf16[192,1024]{1,0:T(8,128)(2,1)S(1)} %collective-permute-done.11.cot_ref.refs_3_, bf16[192,1024]{1,0:T(8,128)(2,1)S(1)} %collective-permute-done.12.pair_ref, bf16[2048,1024]{1,0:T(8,128)(2,1)S(1)} %copy-done.1, ...), custom_call_target="tpu_custom_call" | custom-call | flops 1024 | bytes 1024 | tf_op jit(solution)/shard_map/pallas_call | solution.py:64
  57.4 0.8 collective-permute-start.15
  58.2 7.1 %collective-permute-done.16.refs_2_ = bf16[192,1024]{1,0:T(8,128)(2,1)S(1)} collective-permute-done((bf16[192,1024]{1,0:T(8,128)(2,1)S(1)}, bf16[192,1024]{1,0:T(8,128)(2,1)S(1)}, u32[]{:S(2)}, u32[]{:S(2)}) %collective-permute-start.16) | collective-permute-done | bytes 393248 | tf_op jit(solution)/shard_map/ppermute | solution.py:283
  65.3 8.8 %shard_map.84 = f32[2048,1024]{1,0:T(8,128)} custom-call(s32[2]{0:T(128)S(1)} %pad_add_fusion.place_ref, bf16[768,2048]{1,0:T(8,128)(2,1)S(1)} %shard_map.79.pre_ref, bf16[192,1024]{1,0:T(8,128)(2,1)S(1)} %copy-done.3, bf16[192,1024]{1,0:T(8,128)(2,1)S(1)} %collective-permute-done.cot_ref.refs_1_, ...), custom_call_target="tpu_custom_call" | custom-call | flops 1024 | bytes 1024 | tf_op jit(solution)/shard_map/pallas_call | solution.py:64
  74.1 1.1 %shard_map.85.mine_ref.refs_7_ = bf16[192,1024]{1,0:T(8,128)(2,1)S(1)} custom-call(s32[2]{0:T(128)S(1)} %pad_add_fusion.place_ref, bf16[768,2048]{1,0:T(8,128)(2,1)S(1)} %shard_map.79.pre_ref, f32[192,1024]{1,0:T(8,128)S(1)} %get-tuple-element.53.part_ref, bf16[192,1024]{1,0:T(8,128)(2,1)S(1)} %collective-permute-done.15.refs_0_), custom_call_target="tpu_custom_call" | custom-call | flops 1024 | bytes 1024 | tf_op jit(solution)/shard_map/pallas_call | solution.py:64
  75.3 2.1 %shard_map.86 = bf16[192,1024]{1,0:T(8,128)(2,1)S(1)} custom-call(s32[2]{0:T(128)S(1)} %pad_add_fusion.place_ref, bf16[192,1024]{1,0:T(8,128)(2,1)S(1)} %shard_map.82.mine_ref.refs_6_, bf16[192,1024]{1,0:T(8,128)(2,1)S(1)} %collective-permute-done.17.theirs_ref.refs_10_, bf16[1024,2048]{1,0:T(8,128)(2,1)S(1)} %copy-done.2, ...), custom_call_target="tpu_custom_call" | custom-call | flops 1024 | bytes 1024 | tf_op jit(solution)/shard_map/pallas_call | solution.py:64
  77.7 1.1 %shard_map.87.refs_4_.mine_ref = bf16[192,1024]{1,0:T(8,128)(2,1)S(1)} custom-call(s32[2]{0:T(128)S(1)} %pad_add_fusion.place_ref, bf16[768,2048]{1,0:T(8,128)(2,1)S(1)} %shard_map.79.pre_ref, f32[192,1024]{1,0:T(8,128)S(1)} %get-tuple-element.56.part_ref, bf16[192,1024]{1,0:T(8,128)(2,1)S(1)} %collective-permute-done.19.refs_0_), custom_call_target="tpu_custom_call" | custom-call | flops 1024 | bytes 1024 | tf_op jit(solution)/shard_map/pallas_call | solution.py:64
  79.4 2.8 %collective-permute-done.20.refs_3_ = bf16[192,1024]{1,0:T(8,128)(2,1)S(1)} collective-permute-done((bf16[192,1024]{1,0:T(8,128)(2,1)S(1)}, bf16[192,1024]{1,0:T(8,128)(2,1)S(1)}, u32[]{:S(2)}, u32[]{:S(2)}) %collective-permute-start.20) | collective-permute-done | bytes 393248 | tf_op jit(solution)/shard_map/ppermute | solution.py:283
  82.2 7.4 %collective-permute-done.22.refs_0_ = bf16[192,1024]{1,0:T(8,128)(2,1)S(1)} collective-permute-done((bf16[192,1024]{1,0:T(8,128)(2,1)S(1)}, bf16[192,1024]{1,0:T(8,128)(2,1)S(1)}, u32[]{:S(2)}, u32[]{:S(2)}) %collective-permute-start.22) | collective-permute-done | bytes 393248 | tf_op jit(solution)/shard_map/ppermute | solution.py:282
  89.6 2.1 %shard_map.88 = bf16[192,1024]{1,0:T(8,128)(2,1)S(1)} custom-call(s32[2]{0:T(128)S(1)} %pad_add_fusion.place_ref, bf16[192,1024]{1,0:T(8,128)(2,1)S(1)} %shard_map.85.mine_ref.refs_7_, bf16[192,1024]{1,0:T(8,128)(2,1)S(1)} %collective-permute-done.21.theirs_ref.refs_11_, bf16[1024,2048]{1,0:T(8,128)(2,1)S(1)} %copy-done.2, ...), custom_call_target="tpu_custom_call" | custom-call | flops 1024 | bytes 1024 | tf_op jit(solution)/shard_map/pallas_call | solution.py:64
  91.7 6.6 %shard_map.89 = f32[1024,2048]{1,0:T(8,128)} custom-call(s32[2]{0:T(128)S(1)} %pad_add_fusion.place_ref, bf16[192,1024]{1,0:T(8,128)(2,1)S(1)} %copy-done.5, bf16[192,1024]{1,0:T(8,128)(2,1)S(1)} %collective-permute-done.14.refs_1_, bf16[192,1024]{1,0:T(8,128)(2,1)S(1)} %collective-permute-done.16.refs_2_, ...), custom_call_target="tpu_custom_call" | custom-call | flops 1024 | bytes 1024 | tf_op jit(solution)/shard_map/pallas_call | solution.py:64
  98.4 4.4 %collective-permute-done.24.refs_0_ = bf16[192,1024]{1,0:T(8,128)(2,1)S(1)} collective-permute-done((bf16[192,1024]{1,0:T(8,128)(2,1)S(1)}, bf16[192,1024]{1,0:T(8,128)(2,1)S(1)}, u32[]{:S(2)}, u32[]{:S(2)}) %collective-permute-start.24) | collective-permute-done | bytes 393248 | tf_op jit(solution)/shard_map/ppermute | solution.py:285
  102.7 2.8 %shard_map.90 = bf16[192,1024]{1,0:T(8,128)(2,1)} custom-call(s32[2]{0:T(128)S(1)} %pad_add_fusion.place_ref, bf16[192,1024]{1,0:T(8,128)(2,1)S(1)} %shard_map.87.refs_4_.mine_ref, bf16[192,1024]{1,0:T(8,128)(2,1)S(1)} %collective-permute-done.23.refs_8_.theirs_ref, bf16[1024,2048]{1,0:T(8,128)(2,1)S(1)} %copy-done.2, ...), custom_call_target="tpu_custom_call" | custom-call | flops 1024 | bytes 1024 | tf_op jit(solution)/shard_map/pallas_call | solution.py:64
  (46 shorter events, 3.1 us)
Async XLA Ops:
  0.7 17.3 %collective-permute-start.4 = (bf16[2048,1024]{1,0:T(8,128)(2,1)}, bf16[2048,1024]{1,0:T(8,128)(2,1)S(1)}, u32[]{:S(2)}, u32[]{:S(2)}) collective-permute-start(bf16[2048,1024]{1,0:T(8,128)(2,1)} %mine_ref.3), channel_id=1, source_target_pairs={{0,4},{4,0},{8,12},{12,8},{1,5},{5,1},{9,13},{13,9},{2,6},{6,2},{1... | collective-permute-start | bytes 12582920 | tf_op jit(solution)/shard_map/ppermute | solution.py:234
  1.2 14.6 %collective-permute-start = (bf16[192,1024]{1,0:T(8,128)(2,1)}, bf16[192,1024]{1,0:T(8,128)(2,1)S(1)}, u32[]{:S(2)}, u32[]{:S(2)}) collective-permute-start(bf16[192,1024]{1,0:T(8,128)(2,1)} %refs_0_.2), channel_id=1, source_target_pairs={{0,1},{1,2},{2,3},{3,0},{4,5},{5,6},{6,7},{7,4},{8,9},{9,10},{10,1... | collective-permute-start | bytes 1179656 | tf_op jit(solution)/shard_map/ppermute | solution.py:253
  3.8 19.8 %collective-permute-start.5 = (bf16[192,2048]{1,0:T(8,128)(2,1)}, bf16[192,2048]{1,0:T(8,128)(2,1)S(1)}, u32[]{:S(2)}, u32[]{:S(2)}) collective-permute-start(bf16[192,2048]{1,0:T(8,128)(2,1)} %refs_0_.1), channel_id=1, source_target_pairs={{0,8},{4,12},{8,0},{12,4},{1,9},{5,13},{9,1},{13,5},{2,10},{6,14},... | collective-permute-start | bytes 2359304 | tf_op jit(solution)/shard_map/ppermute | solution.py:233
  15.8 2.2 %collective-permute-start.3 = (bf16[192,1024]{1,0:T(8,128)(2,1)S(1)}, bf16[192,1024]{1,0:T(8,128)(2,1)S(1)}, u32[]{:S(2)}, u32[]{:S(2)}) collective-permute-start(bf16[192,1024]{1,0:T(8,128)(2,1)S(1)} %collective-permute-done.cot_ref.refs_1_), channel_id=1, source_target_pairs={{0,4},{4,0},{8,12},{12,8},{1,5},{5,1},{9,13},{13,9},{2,6},{6,2},{1... | collective-permute-start | bytes 1179656 | tf_op jit(solution)/shard_map/ppermute | solution.py:238
  15.8 8.4 %collective-permute-start.2 = (bf16[192,1024]{1,0:T(8,128)(2,1)}, bf16[192,1024]{1,0:T(8,128)(2,1)S(1)}, u32[]{:S(2)}, u32[]{:S(2)}) collective-permute-start(bf16[192,1024]{1,0:T(8,128)(2,1)} %refs_0_.2), channel_id=1, source_target_pairs={{0,4},{4,0},{8,12},{12,8},{1,5},{5,1},{9,13},{13,9},{2,6},{6,2},{1... | collective-permute-start | bytes 1179656 | tf_op jit(solution)/shard_map/ppermute | solution.py:238
  16.3 12.8 %collective-permute-start.1 = (bf16[192,1024]{1,0:T(8,128)(2,1)S(1)}, bf16[192,1024]{1,0:T(8,128)(2,1)S(1)}, u32[]{:S(2)}, u32[]{:S(2)}) collective-permute-start(bf16[192,1024]{1,0:T(8,128)(2,1)S(1)} %collective-permute-done.cot_ref.refs_1_), channel_id=1, source_target_pairs={{0,1},{1,2},{2,3},{3,0},{4,5},{5,6},{6,7},{7,4},{8,9},{9,10},{10,1... | collective-permute-start | bytes 1179656 | tf_op jit(solution)/shard_map/ppermute | solution.py:261
  18.0 2.2 %copy-start = (bf16[2048,1024]{1,0:T(8,128)(2,1)S(1)}, bf16[2048,1024]{1,0:T(8,128)(2,1)}, u32[]{:S(2)}) copy-start(bf16[2048,1024]{1,0:T(8,128)(2,1)} %mine_ref.3) | copy-start | bytes 12582916
  20.2 3.4 %copy-start.4 = (bf16[192,2048]{1,0:T(8,128)(2,1)S(1)}, bf16[192,2048]{1,0:T(8,128)(2,1)}, u32[]{:S(2)}) copy-start(bf16[192,2048]{1,0:T(8,128)(2,1)} %refs_0_.1) | copy-start | bytes 2359300
  20.2 3.9 %copy-start.3 = (bf16[192,1024]{1,0:T(8,128)(2,1)S(1)}, bf16[192,1024]{1,0:T(8,128)(2,1)}, u32[]{:S(2)}) copy-start(bf16[192,1024]{1,0:T(8,128)(2,1)} %refs_0_.2) | copy-start | bytes 1179652
  22.3 8.5 %copy-start.5 = (bf16[192,1024]{1,0:T(8,128)(2,1)S(1)}, bf16[192,1024]{1,0:T(8,128)(2,1)}, u32[]{:S(2)}) copy-start(bf16[192,1024]{1,0:T(8,128)(2,1)} %refs_0_.3) | copy-start | bytes 1179652
  23.6 9.5 %collective-permute-start.7 = (bf16[192,2048]{1,0:T(8,128)(2,1)S(1)}, bf16[192,2048]{1,0:T(8,128)(2,1)S(1)}, u32[]{:S(2)}, u32[]{:S(2)}) collective-permute-start(bf16[192,2048]{1,0:T(8,128)(2,1)S(1)} %copy-done.4), channel_id=1, source_target_pairs={{0,4},{4,0},{8,12},{12,8},{1,5},{5,1},{9,13},{13,9},{2,6},{6,2},{1... | collective-permute-start | bytes 2359304 | tf_op jit(solution)/shard_map/ppermute | solution.py:266
  23.6 9.5 %collective-permute-start.8 = (bf16[192,2048]{1,0:T(8,128)(2,1)S(1)}, bf16[192,2048]{1,0:T(8,128)(2,1)S(1)}, u32[]{:S(2)}, u32[]{:S(2)}) collective-permute-start(bf16[192,2048]{1,0:T(8,128)(2,1)S(1)} %collective-permute-done.5.refs_1_), channel_id=1, source_target_pairs={{0,4},{4,0},{8,12},{12,8},{1,5},{5,1},{9,13},{13,9},{2,6},{6,2},{1... | collective-permute-start | bytes 2359304 | tf_op jit(solution)/shard_map/ppermute | solution.py:266
  29.1 1.7 %collective-permute-start.6 = (bf16[192,1024]{1,0:T(8,128)(2,1)S(1)}, bf16[192,1024]{1,0:T(8,128)(2,1)S(1)}, u32[]{:S(2)}, u32[]{:S(2)}) collective-permute-start(bf16[192,1024]{1,0:T(8,128)(2,1)S(1)} %collective-permute-done.1.cot_ref.refs_2_), channel_id=1, source_target_pairs={{0,4},{4,0},{8,12},{12,8},{1,5},{5,1},{9,13},{13,9},{2,6},{6,2},{1... | collective-permute-start | bytes 1179656 | tf_op jit(solution)/shard_map/ppermute | solution.py:238
  29.1 11.5 %collective-permute-start.9 = (bf16[192,1024]{1,0:T(8,128)(2,1)S(1)}, bf16[192,1024]{1,0:T(8,128)(2,1)S(1)}, u32[]{:S(2)}, u32[]{:S(2)}) collective-permute-start(bf16[192,1024]{1,0:T(8,128)(2,1)S(1)} %get-tuple-element.34), channel_id=1, source_target_pairs={{0,8},{4,12},{8,0},{12,4},{1,9},{5,13},{9,1},{13,5},{2,10},{6,14},... | collective-permute-start | bytes 1179656 | tf_op jit(solution)/shard_map/ppermute | solution.py:243
  30.6 13.8 %collective-permute-start.11 = (bf16[192,1024]{1,0:T(8,128)(2,1)S(1)}, bf16[192,1024]{1,0:T(8,128)(2,1)S(1)}, u32[]{:S(2)}, u32[]{:S(2)}) collective-permute-start(bf16[192,1024]{1,0:T(8,128)(2,1)S(1)} %collective-permute-done.1.cot_ref.refs_2_), channel_id=1, source_target_pairs={{0,1},{1,2},{2,3},{3,0},{4,5},{5,6},{6,7},{7,4},{8,9},{9,10},{10,1... | collective-permute-start | bytes 1179656 | tf_op jit(solution)/shard_map/ppermute | solution.py:261
  30.8 21.2 %collective-permute-start.14 = (bf16[192,1024]{1,0:T(8,128)(2,1)S(1)}, bf16[192,1024]{1,0:T(8,128)(2,1)S(1)}, u32[]{:S(2)}, u32[]{:S(2)}) collective-permute-start(bf16[192,1024]{1,0:T(8,128)(2,1)S(1)} %copy-done.5), channel_id=1, source_target_pairs={{0,1},{1,2},{2,3},{3,0},{4,5},{5,6},{6,7},{7,4},{8,9},{9,10},{10,1... | collective-permute-start | bytes 1179656 | tf_op jit(solution)/shard_map/ppermute | solution.py:271
  33.1 19.0 %copy-start.2 = (bf16[1024,2048]{1,0:T(8,128)(2,1)S(1)}, bf16[1024,2048]{1,0:T(8,128)(2,1)}, u32[]{:S(2)}) copy-start(bf16[1024,2048]{1,0:T(8,128)(2,1)} %up_ref.7) | copy-start | bytes 12582916
  41.8 13.6 %copy-start.1 = (bf16[2048,1024]{1,0:T(8,128)(2,1)S(1)}, bf16[2048,1024]{1,0:T(8,128)(2,1)}, u32[]{:S(2)}) copy-start(bf16[2048,1024]{1,0:T(8,128)(2,1)} %mine_ref.3) | copy-start | bytes 12582916
  41.8 10.3 %collective-permute-start.10 = (bf16[192,1024]{1,0:T(8,128)(2,1)S(1)}, bf16[192,1024]{1,0:T(8,128)(2,1)S(1)}, u32[]{:S(2)}, u32[]{:S(2)}) collective-permute-start(bf16[192,1024]{1,0:T(8,128)(2,1)S(1)} %shard_map.80.mine_ref.refs_5_), channel_id=1, source_target_pairs={{0,4},{4,0},{8,12},{12,8},{1,5},{5,1},{9,13},{13,9},{2,6},{6,2},{1... | collective-permute-start | bytes 1179656 | tf_op jit(solution)/shard_map/ppermute | solution.py:247
  41.8 12.3 %collective-permute-start.13 = (bf16[192,1024]{1,0:T(8,128)(2,1)S(1)}, bf16[192,1024]{1,0:T(8,128)(2,1)S(1)}, u32[]{:S(2)}, u32[]{:S(2)}) collective-permute-start(bf16[192,1024]{1,0:T(8,128)(2,1)S(1)} %get-tuple-element.39), channel_id=1, source_target_pairs={{0,8},{4,12},{8,0},{12,4},{1,9},{5,13},{9,1},{13,5},{2,10},{6,14},... | collective-permute-start | bytes 1179656 | tf_op jit(solution)/shard_map/ppermute | solution.py:243
  44.4 10.9 %collective-permute-start.12 = (bf16[192,1024]{1,0:T(8,128)(2,1)S(1)}, bf16[192,1024]{1,0:T(8,128)(2,1)S(1)}, u32[]{:S(2)}, u32[]{:S(2)}) collective-permute-start(bf16[192,1024]{1,0:T(8,128)(2,1)S(1)} %collective-permute-done.11.cot_ref.refs_3_), channel_id=1, source_target_pairs={{0,4},{4,0},{8,12},{12,8},{1,5},{5,1},{9,13},{13,9},{2,6},{6,2},{1... | collective-permute-start | bytes 1179656 | tf_op jit(solution)/shard_map/ppermute | solution.py:238
  52.1 13.2 %collective-permute-start.16 = (bf16[192,1024]{1,0:T(8,128)(2,1)S(1)}, bf16[192,1024]{1,0:T(8,128)(2,1)S(1)}, u32[]{:S(2)}, u32[]{:S(2)}) collective-permute-start(bf16[192,1024]{1,0:T(8,128)(2,1)S(1)} %collective-permute-done.14.refs_1_), channel_id=1, source_target_pairs={{0,1},{1,2},{2,3},{3,0},{4,5},{5,6},{6,7},{7,4},{8,9},{9,10},{10,1... | collective-permute-start | bytes 1179656 | tf_op jit(solution)/shard_map/ppermute | solution.py:283
  57.4 16.7 %collective-permute-start.15 = (bf16[192,1024]{1,0:T(8,128)(2,1)S(1)}, bf16[192,1024]{1,0:T(8,128)(2,1)S(1)}, u32[]{:S(2)}, u32[]{:S(2)}) collective-permute-start(bf16[192,1024]{1,0:T(8,128)(2,1)S(1)} %get-tuple-element.50), channel_id=1, source_target_pairs={{0,8},{4,12},{8,0},{12,4},{1,9},{5,13},{9,1},{13,5},{2,10},{6,14},... | collective-permute-start | bytes 1179656 | tf_op jit(solution)/shard_map/ppermute | solution.py:243
  58.2 17.1 %collective-permute-start.17 = (bf16[192,1024]{1,0:T(8,128)(2,1)S(1)}, bf16[192,1024]{1,0:T(8,128)(2,1)S(1)}, u32[]{:S(2)}, u32[]{:S(2)}) collective-permute-start(bf16[192,1024]{1,0:T(8,128)(2,1)S(1)} %shard_map.82.mine_ref.refs_6_), channel_id=1, source_target_pairs={{0,4},{4,0},{8,12},{12,8},{1,5},{5,1},{9,13},{13,9},{2,6},{6,2},{1... | collective-permute-start | bytes 1179656 | tf_op jit(solution)/shard_map/ppermute | solution.py:247
  58.2 17.1 %collective-permute-start.18 = (bf16[192,1024]{1,0:T(8,128)(2,1)S(1)}, bf16[192,1024]{1,0:T(8,128)(2,1)S(1)}, u32[]{:S(2)}, u32[]{:S(2)}) collective-permute-start(bf16[192,1024]{1,0:T(8,128)(2,1)S(1)} %shard_map.81), channel_id=1, source_target_pairs={{0,1},{1,2},{2,3},{3,0},{4,5},{5,6},{6,7},{7,4},{8,9},{9,10},{10,1... | collective-permute-start | bytes 1179656 | tf_op jit(solution)/shard_map/ppermute | solution.py:282
  65.3 16.9 %collective-permute-start.20 = (bf16[192,1024]{1,0:T(8,128)(2,1)S(1)}, bf16[192,1024]{1,0:T(8,128)(2,1)S(1)}, u32[]{:S(2)}, u32[]{:S(2)}) collective-permute-start(bf16[192,1024]{1,0:T(8,128)(2,1)S(1)} %collective-permute-done.16.refs_2_), channel_id=1, source_target_pairs={{0,1},{1,2},{2,3},{3,0},{4,5},{5,6},{6,7},{7,4},{8,9},{9,10},{10,1... | collective-permute-start | bytes 1179656 | tf_op jit(solution)/shard_map/ppermute | solution.py:283
  65.3 12.4 %collective-permute-start.19 = (bf16[192,1024]{1,0:T(8,128)(2,1)S(1)}, bf16[192,1024]{1,0:T(8,128)(2,1)S(1)}, u32[]{:S(2)}, u32[]{:S(2)}) collective-permute-start(bf16[192,1024]{1,0:T(8,128)(2,1)S(1)} %get-tuple-element.57), channel_id=1, source_target_pairs={{0,8},{4,12},{8,0},{12,4},{1,9},{5,13},{9,1},{13,5},{2,10},{6,14},... | collective-permute-start | bytes 1179656 | tf_op jit(solution)/shard_map/ppermute | solution.py:243
  77.4 12.2 %collective-permute-start.22 = (bf16[192,1024]{1,0:T(8,128)(2,1)S(1)}, bf16[192,1024]{1,0:T(8,128)(2,1)S(1)}, u32[]{:S(2)}, u32[]{:S(2)}) collective-permute-start(bf16[192,1024]{1,0:T(8,128)(2,1)S(1)} %shard_map.86), channel_id=1, source_target_pairs={{0,1},{1,2},{2,3},{3,0},{4,5},{5,6},{6,7},{7,4},{8,9},{9,10},{10,1... | collective-permute-start | bytes 1179656 | tf_op jit(solution)/shard_map/ppermute | solution.py:282
  77.6 12.0 %collective-permute-start.21 = (bf16[192,1024]{1,0:T(8,128)(2,1)S(1)}, bf16[192,1024]{1,0:T(8,128)(2,1)S(1)}, u32[]{:S(2)}, u32[]{:S(2)}) collective-permute-start(bf16[192,1024]{1,0:T(8,128)(2,1)S(1)} %shard_map.85.mine_ref.refs_7_), channel_id=1, source_target_pairs={{0,4},{4,0},{8,12},{12,8},{1,5},{5,1},{9,13},{13,9},{2,6},{6,2},{1... | collective-permute-start | bytes 1179656 | tf_op jit(solution)/shard_map/ppermute | solution.py:247
  78.8 12.9 %collective-permute-start.23 = (bf16[192,1024]{1,0:T(8,128)(2,1)S(1)}, bf16[192,1024]{1,0:T(8,128)(2,1)S(1)}, u32[]{:S(2)}, u32[]{:S(2)}) collective-permute-start(bf16[192,1024]{1,0:T(8,128)(2,1)S(1)} %shard_map.87.refs_4_.mine_ref), channel_id=1, source_target_pairs={{0,4},{4,0},{8,12},{12,8},{1,5},{5,1},{9,13},{13,9},{2,6},{6,2},{1... | collective-permute-start | bytes 1179656 | tf_op jit(solution)/shard_map/ppermute | solution.py:247
  91.6 11.1 %collective-permute-start.24 = (bf16[192,1024]{1,0:T(8,128)(2,1)S(1)}, bf16[192,1024]{1,0:T(8,128)(2,1)S(1)}, u32[]{:S(2)}, u32[]{:S(2)}) collective-permute-start(bf16[192,1024]{1,0:T(8,128)(2,1)S(1)} %shard_map.88), channel_id=1, source_target_pairs={{0,1},{1,2},{2,3},{3,0},{4,5},{5,6},{6,7},{7,4},{8,9},{9,10},{10,1... | collective-permute-start | bytes 1179656 | tf_op jit(solution)/shard_map/ppermute | solution.py:285

commit v7 on v6

--- a/solution.py
+++ b/solution.py
@@ -11,7 +11,8 @@
 LAST = (((1,), (1,)), ((), ()))
 FIRST = (((0,), (0,)), ((), ()))
 MIB = 1024 * 1024
-LITTLE = pl.CostEstimate(flops=1024, bytes_accessed=1024, transcendentals=0)
+PART = 16
+EARLY = 9 * 10**9
 
 
 def gelu_parts(values):
@@ -60,7 +61,7 @@
     return lax.rem(place_ref[1], 2)
 
 
-def call(kernel, place, operands, outs, mib, grid=(1,), in_specs=None, out_specs=None, scratch=()):
+def call(kernel, place, operands, outs, mib, flops, grid=(1,), in_specs=None, out_specs=None, scratch=()):
     return pl.pallas_call(
         kernel,
         out_shape=outs,
@@ -72,24 +73,51 @@
             scratch_shapes=scratch,
         ),
         compiler_params=pltpu.CompilerParams(vmem_limit_bytes=mib * MIB),
-        cost_estimate=LITTLE,
+        cost_estimate=pl.CostEstimate(flops=flops // PART, bytes_accessed=1024, transcendentals=0),
     )(place, *operands)
 
 
-def lay_out_kernel(shifts, rows, place_ref, *refs):
-    out_ref = refs[-1]
-    tokens = refs[0].shape[0]
-    for i, ref in enumerate(refs[:-1]):
-        owner = lax.rem(place_ref[1] - shifts[i % len(shifts)] + rows, rows)
-        if i >= len(shifts):
-            owner = owner + 1 - 2 * lax.rem(owner, 2)
+def go_on_kernel(place_ref, out_ref):
+    for i in range(2):
+        out_ref[i] = place_ref[i]
+
+
+def go_on_call(place, declared):
+    return pl.pallas_call(
+        go_on_kernel,
+        out_shape=jax.ShapeDtypeStruct(place.shape, place.dtype),
+        in_specs=[pl.BlockSpec(memory_space=pltpu.SMEM)],
+        out_specs=pl.BlockSpec(memory_space=pltpu.SMEM),
+        compiler_params=pltpu.CompilerParams(vmem_limit_bytes=MIB // 2),
+        cost_estimate=pl.CostEstimate(flops=declared, bytes_accessed=1024, transcendentals=0),
+    )(place)
+
+
+def take_half_kernel(place_ref, mine_ref, theirs_ref, out_ref):
+    tokens, half = mine_ref.shape[0], out_ref.shape[1]
+    core = core_of(place_ref)
+    out_ref[block(core, tokens), :] = mine_ref[:, block(core, half)]
+    out_ref[block(1 - core, tokens), :] = theirs_ref[:, block(core, half)]
+
+
+def take_half_call(place, mine, theirs):
+    tokens, hidden = mine.shape
+    out = jax.ShapeDtypeStruct((2 * tokens, hidden // 2), jnp.bfloat16)
+    return call(take_half_kernel, place, [mine, theirs], out, 8, MIB)
+
+
+def lay_out_kernel(place_ref, *refs):
+    blocks, out_ref = refs[:-1], refs[-1]
+    tokens = blocks[0].shape[0]
+    for i, ref in enumerate(blocks):
+        owner = lax.rem(lax.div(place_ref[1], 2) - i + len(blocks), len(blocks))
         out_ref[block(owner, tokens), :] = ref[...]
 
 
-def lay_out_call(place, blocks, shifts, rows):
-    tokens, hidden = blocks[0].shape
-    out = jax.ShapeDtypeStruct((tokens * len(blocks), hidden), jnp.bfloat16)
-    return call(functools.partial(lay_out_kernel, shifts, rows), place, blocks, out, 8)
+def lay_out_call(place, blocks):
+    tokens, half = blocks[0].shape
+    out = jax.ShapeDtypeStruct((tokens * len(blocks), half), jnp.bfloat16)
+    return call(lay_out_kernel, place, blocks, out, 8, 5000 * MIB)
 
 
 def hidden_kernel(place_ref, cot_ref, pair_ref, mine_ref, theirs_ref, part_ref, sent_ref):
@@ -106,28 +134,27 @@
 def hidden_call(place, cot, cot_pair, down_mine, down_pair):
     shape = (cot.shape[0], down_mine.shape[0] // 2)
     outs = [jax.ShapeDtypeStruct(shape, jnp.float32), jax.ShapeDtypeStruct(shape, jnp.bfloat16)]
-    return call(hidden_kernel, place, [cot, cot_pair, down_mine, down_pair], outs, 12)
+    return call(hidden_kernel, place, [cot, cot_pair, down_mine, down_pair], outs, 12, 4 * cot.size * shape[1])
 
 
 def pre_grad_kernel(step, cols, place_ref, pre_ref, part_ref, *refs):
     out_ref = refs[-1]
     tokens, half = part_ref.shape
     rows = 64 if tokens % 64 == 0 else tokens
-    columns = block(core_of(place_ref), half)
     start = block_at(place_ref, step, cols) * tokens
     for first in range(0, tokens, rows):
         here = pl.ds(first, rows)
         total = part_ref[here, :]
         for other in refs[:-1]:
             total = total + other[here, :].astype(jnp.float32)
-        v = pre_ref[pl.ds(pl.multiple_of(start + first, rows), rows), columns]
+        v = pre_ref[pl.ds(pl.multiple_of(start + first, rows), rows), :]
         out_ref[here, :] = (total * gelu_slope(v)).astype(jnp.bfloat16)
 
 
 def pre_grad_call(place, step, cols, pre_all, part, others):
     out = jax.ShapeDtypeStruct(part.shape, jnp.bfloat16)
     kernel = functools.partial(pre_grad_kernel, step, cols)
-    return call(kernel, place, [pre_all, part, *others], out, 8)
+    return call(kernel, place, [pre_all, part, *others], out, 8, 8192 * part.size)
 
 
 def share_kernel(place_ref, mine_ref, theirs_ref, up_ref, *refs):
@@ -146,36 +173,45 @@
 
 def share_call(place, mine, theirs, up_weight, arrived):
     out = jax.ShapeDtypeStruct((mine.shape[0], up_weight.shape[0]), jnp.bfloat16)
-    return call(share_kernel, place, [mine, theirs, up_weight, *arrived], out, 12)
-
-
-def grad_down_kernel(blocks, scale, place_ref, pre_ref, *refs):
+    return call(share_kernel, place, [mine, theirs, up_weight, *arrived], out, 12, 2 * mine.shape[0] * up_weight.size)
+
+
+def grad_down_kernel(blocks, scale, place_ref, mine_ref, theirs_ref, *refs):
     cot_refs, out_ref, cots = refs[:blocks], refs[-2], refs[-1]
-    tokens = cot_refs[0].shape[0]
-
-    @pl.when(pl.program_id(0) == 0)
+    tokens, tile = cot_refs[0].shape[0], out_ref.shape[0]
+    i, steps = pl.program_id(0), mine_ref.shape[1] // tile
+
+    @pl.when(i == 0)
     def _():
         for s in range(blocks):
             cots[block(block_at(place_ref, s, blocks), tokens), :] = cot_refs[s][...]
 
-    activation = gelu(pre_ref[...]).astype(jnp.bfloat16)
-    out_ref[...] = dot(activation, cots[...], FIRST) * scale
-
-
-def grad_down_call(place, pre_all, cots, scale):
-    total, hidden = pre_all.shape
-    features = cots[0].shape[1]
-    tile = tile_of(hidden)
+    def product(pre_ref, at):
+        activation = gelu(pre_ref[:, block(at, tile)]).astype(jnp.bfloat16)
+        out_ref[...] = dot(activation, cots[...], FIRST) * scale
+
+    pl.when(i < steps)(lambda: product(mine_ref, i))
+    pl.when(i >= steps)(lambda: product(theirs_ref, i - steps))
+
+
+def grad_down_call(place, pre_mine, pre_theirs, cots, scale):
+    (total, half), features = pre_mine.shape, cots[0].shape[1]
+    tile = tile_of(half)
+    steps = half // tile
+
+    def rows(i, place):
+        core = lax.rem(place[1], 2)
+        return jnp.where(i < steps, core * steps + i, (1 - core) * steps + i - steps), 0
+
     return call(
         functools.partial(grad_down_kernel, len(cots), scale),
         place,
-        [pre_all, *cots],
-        jax.ShapeDtypeStruct((hidden, features), jnp.float32),
+        [pre_mine, pre_theirs, *cots],
+        jax.ShapeDtypeStruct((2 * half, features), jnp.float32),
         14,
-        grid=(hidden // tile,),
-        in_specs=[pl.BlockSpec((total, tile), lambda i, place: (0, i))]
-        + [in_vmem() for _ in cots],
-        out_specs=pl.BlockSpec((tile, features), lambda i, place: (i, 0)),
+        4 * pre_mine.size * features,
+        grid=(2 * steps,),
+        out_specs=pl.BlockSpec((tile, features), rows),
         scratch=[pltpu.VMEM((total, features), jnp.bfloat16)],
     )
 
@@ -209,6 +245,7 @@
         [*ins, *mine, *pair],
         jax.ShapeDtypeStruct((features, hidden), jnp.float32),
         18,
+        2 * total * hidden * features,
         grid=(features // tile,),
         out_specs=pl.BlockSpec((tile, hidden), lambda i, place: (i, 0)),
         scratch=[
@@ -226,11 +263,11 @@
     )
     ring = [(i, (i + 1) % cols) for i in range(cols)]
     pair = [(i, i ^ 1) for i in range(rows)]
-    shifts = range(0, rows, 2)
-    over_x = [[(i, (i + shift) % rows) for i in range(rows)] for shift in shifts[1:]]
+    over_x = [[(i, (i + shift) % rows) for i in range(rows)] for shift in range(2, rows, 2)]
     scale = 1.0 / math.sqrt(cotangent.shape[0] * cols)
 
-    pres = [preactivation] + [lax.ppermute(preactivation, "row", to) for to in over_x]
+    pre = take_half_call(place, preactivation, lax.ppermute(preactivation, "row", pair))
+    pres = [pre] + [lax.ppermute(pre, "row", to) for to in over_x]
     down_pair = lax.ppermute(down_weight, "row", pair)
     parts, sent, others, mine, theirs = ([None] * cols for _ in range(5))
 
@@ -247,41 +284,43 @@
         theirs[s] = lax.ppermute(mine[s], "row", pair)
 
     def share(s, arrived, *first):
-        return share_call(after(place, *first), mine[s], theirs[s], up_weight, arrived)
-
-    cots, ins = [cotangent], [inputs]
-    arriving = lax.ppermute(cotangent, "col", ring)
+        here = after(place, *arrived, *first)
+        here = go_on_call(here, EARLY) if arrived else here
+        return share_call(here, mine[s], theirs[s], up_weight, arrived)
+
+    cots, ins, last = [cotangent], [inputs], cols - 1
     for s in range(1, cols):
+        cots.append(lax.ppermute(cots[s - 1], "col", ring))
+        if s == 1:
+            cots[1] = after(cots[1], pre)
+            ins.append(lax.ppermute(after(inputs, cots[1]), "col", ring))
         if s == 2:
-            arriving = after(arriving, sent[0])
-        elif s > 2:
-            arriving = after(arriving, sent[s - 1])
-        cots.append(arriving)
-        if s < cols - 1:
-            arriving = lax.ppermute(arriving, "col", ring)
-            hidden_part(s)
-            exchange(s)
-        if s == 1:
-            hidden_part(0, sent[1], *pres[1:])
-            pres = pres + [lax.ppermute(after(p, sent[1]), "row", pair) for p in pres]
-
-    last = cols - 1
-    pre_all = lay_out_call(after(place, sent[last - 1]), pres, shifts, rows)
-    pre_grad(1, sent[last - 1])
-    ins.append(lax.ppermute(after(inputs, cots[last - 1]), "col", ring))
-    sums = share(1, [], mine[1])
+            cots[2] = after(cots[2], ins[1])
+
+    hidden_part(1)
+    exchange(1)
+    pre_all = lay_out_call(place, pres)
+    pre_grad(1)
+    for s in range(2, last):
+        hidden_part(s, mine[1])
+        exchange(s)
+    hidden_part(0, sent[last - 1])
+    sums = share(1, [], sent[0])
     pre_grad(2, sums)
-    hidden_part(last, mine[2], ins[1])
+    cots[last] = after(cots[last], mine[2])
+    hidden_part(last)
     exchange(last)
     exchange(0, sent[last])
-    grad_down = grad_down_call(after(place, sums, sent[last]), pre_all, cots, scale)
-    late = grad_down
+    pre_theirs = lax.ppermute(after(pre_all, sums), "row", pair)
     for s in range(2, cols):
-        following = (s + 1) % cols
-        pre_grad(following, late)
         arrived = lax.ppermute(sums, "col", ring)
-        ins.append(lax.ppermute(ins[-1], "col", ring))
-        sums = late = share(s, [arrived], mine[following], ins[s])
+        ins.append(lax.ppermute(after(ins[-1], sums, cots[last]), "col", ring))
+        if s > 2:
+            pre_grad(s, sums)
+        if s == last:
+            grad_down = grad_down_call(after(place, mine[s]), pre_all, pre_theirs, cots, scale)
+            pre_grad(0, grad_down)
+        sums = share(s, [arrived], ins[s], *([mine[0]] if s == last else []))
     arrived = lax.ppermute(sums, "col", ring)
     grad_up = grad_up_call(after(place, sums), ins, mine, theirs, scale)
     sums = share(0, [arrived], grad_up)

time: 106 us -> 124 us (1.17)
  starting transfers between devices: 10.6 us -> 18.2 us
  waiting for transfers between devices: 53.8 us -> 59.1 us
  Pallas kernels: 38 us -> 41.7 us
    ppermute x3, waiting for transfers between devices: 11.8 us -> 19.6 us  [per_device(): arrived = lax.ppermute(sums, 'col', ring)]
    ppermute x9, starting transfers between devices: 4.85 us -> 8.93 us  [the longest x3 5.86 us: per_device(): cots.append(lax.ppermute(cots[s - 1], 'col', ring))]
    pallas_call x0 -> x3, Pallas kernels: none -> 3.41 us  [go_on_call(): pl.pallas_call(go_on_kernel, out_shape=jax.ShapeDtypeStruct(place.shape,...]
    ppermute x4, starting transfers between devices: 3.81 us -> 5.46 us  [exchange(): others[s] = [lax.ppermute(values, 'row', to) for to in over_x]]
    ppermute x4, waiting for transfers between devices: 1.96 us -> 0.43 us  [hidden_part(): cot_pair = after(lax.ppermute(cots[s], 'row', pair), *first)]
    ppermute x4, waiting for transfers between devices: 6.75 us -> 5.25 us  [exchange(): others[s] = [lax.ppermute(values, 'row', to) for to in over_x]]
    ppermute x3, starting transfers between devices: 0.3 us -> 1.64 us  [per_device(): arrived = lax.ppermute(sums, 'col', ring)]
    pallas_call x15 -> x16, Pallas kernels: 38 us -> 38.3 us  [call(): pl.pallas_call(kernel, out_shape=outs, grid_spec=pltpu.PrefetchScalarGrid...]
  transfers between devices with their start and end apart: 25 -> 25, of which waited for: 12 -> 13; matrix products, arithmetic and copies ran while one was open for 0% -> 0% of each run, Pallas kernels for 33% -> 31%
where the time goes in v7:
time: 124 us; the launch traced here: 123 us
  waiting for transfers between devices  59.1 us (48%)
  Pallas kernels  41.7 us (34%)
  starting transfers between devices  18.2 us (15%)
  local copies, waits for them, and re-layouts  3.34 us (3%)
    pallas_call x16, Pallas kernels, call(): pl.pallas_call(kernel, out_shape=outs, grid_spec=pltpu.PrefetchScalarGrid...  38.3 us
    ppermute x3, waiting for transfers between devices, per_device(): arrived = lax.ppermute(sums, 'col', ring)  19.6 us
    ppermute x3, waiting for transfers between devices, per_device(): cots.append(lax.ppermute(cots[s - 1], 'col', ring))  12.1 us
    ppermute x2, waiting for transfers between devices, per_device(): ins.append(lax.ppermute(after(ins[-1], sums, cots[last]), 'col', ring))  10.3 us
    ppermute x1, waiting for transfers between devices, per_device(): ins.append(lax.ppermute(after(inputs, cots[1]), 'col', ring))  6.38 us
    ppermute x3, starting transfers between devices, per_device(): cots.append(lax.ppermute(cots[s - 1], 'col', ring))  5.86 us
    ppermute x4, starting transfers between devices, exchange(): others[s] = [lax.ppermute(values, 'row', to) for to in over_x]  5.46 us
    ppermute x4, waiting for transfers between devices, exchange(): others[s] = [lax.ppermute(values, 'row', to) for to in over_x]  5.25 us
  transfers between devices with their start and end apart: 25, of which 13 were waited for; matrix products, arithmetic and copies ran while one was open for 0% of the time, Pallas kernels for 31%

profile of v7, /device:TPU:0, one launch (start us, length us, event | category | flops | bytes accessed | tf_op | source)
XLA Modules:
  0.0 123.4 jit_solution(2088342554161965594)
XLA Ops:
  1.2 3.0 %collective-permute-start.1 = (bf16[192,1024]{1,0:T(8,128)(2,1)}, bf16[192,1024]{1,0:T(8,128)(2,1)S(1)}, u32[]{:S(2)}, u32[]{:S(2)}) collective-permute-start(bf16[192,1024]{1,0:T(8,128)(2,1)} %refs_0_.1), channel_id=1, source_target_pairs={{0,1},{1,2},{2,3},{3,0},{4,5},{5,6},{6,7},{7,4},{8,9},{9,10},{10,1... | collective-permute-start | bytes 1179656 | tf_op jit(solution)/shard_map/ppermute | solution.py:293
  4.2 5.0 %collective-permute-done.2.theirs_ref = bf16[192,2048]{1,0:T(8,128)(2,1)S(1)} collective-permute-done((bf16[192,2048]{1,0:T(8,128)(2,1)}, bf16[192,2048]{1,0:T(8,128)(2,1)S(1)}, u32[]{:S(2)}, u32[]{:S(2)}) %collective-permute-start.2) | collective-permute-done | bytes 786464 | tf_op jit(solution)/shard_map/ppermute | solution.py:269
  11.0 2.9 %collective-permute-start.6 = (bf16[384,1024]{1,0:T(8,128)(2,1)S(1)}, bf16[384,1024]{1,0:T(8,128)(2,1)S(1)}, u32[]{:S(2)}, u32[]{:S(2)}) collective-permute-start(bf16[384,1024]{1,0:T(8,128)(2,1)S(1)} %shard_map.76.refs_0_), channel_id=1, source_target_pairs={{0,8},{4,12},{8,0},{12,4},{1,9},{5,13},{9,1},{13,5},{2,10},{6,14},... | collective-permute-start | bytes 2359304 | tf_op jit(solution)/shard_map/ppermute | solution.py:270
  14.0 1.9 %collective-permute-done.1.cot_ref.refs_1_ = bf16[192,1024]{1,0:T(8,128)(2,1)S(1)} collective-permute-done((bf16[192,1024]{1,0:T(8,128)(2,1)}, bf16[192,1024]{1,0:T(8,128)(2,1)S(1)}, u32[]{:S(2)}, u32[]{:S(2)}) %collective-permute-start.1) | collective-permute-done | bytes 393248 | tf_op jit(solution)/shard_map/ppermute | solution.py:293
  15.8 1.3 %collective-permute-start.3 = (bf16[192,1024]{1,0:T(8,128)(2,1)S(1)}, bf16[192,1024]{1,0:T(8,128)(2,1)S(1)}, u32[]{:S(2)}, u32[]{:S(2)}) collective-permute-start(bf16[192,1024]{1,0:T(8,128)(2,1)S(1)} %collective-permute-done.1.cot_ref.refs_1_), channel_id=1, source_target_pairs={{0,1},{1,2},{2,3},{3,0},{4,5},{5,6},{6,7},{7,4},{8,9},{9,10},{10,1... | collective-permute-start | bytes 1179656 | tf_op jit(solution)/shard_map/ppermute | solution.py:293
  17.6 2.2 %copy-done = bf16[2048,1024]{1,0:T(8,128)(2,1)S(1)} copy-done((bf16[2048,1024]{1,0:T(8,128)(2,1)S(1)}, bf16[2048,1024]{1,0:T(8,128)(2,1)}, u32[]{:S(2)}) %copy-start) | copy-done | bytes 4194328
  19.8 2.1 %shard_map.78 = (f32[192,1024]{1,0:T(8,128)S(1)}, bf16[192,1024]{1,0:T(8,128)(2,1)S(1)}) custom-call(s32[2]{0:T(128)S(1)} %pad_add_fusion.place_ref, bf16[192,1024]{1,0:T(8,128)(2,1)S(1)} %collective-permute-done.1.cot_ref.refs_1_, bf16[192,1024]{1,0:T(8,128)(2,1)S(1)} %collective-permute-done.7.pair_ref, bf16[2048,1024]{1,0:T(8,128)(2,1)S(1)} %copy-done, ...), custom_call_target="tpu_custom_call" | custom-call | flops 50331648 | bytes 1024 | tf_op jit(solution)/shard_map/pallas_call | solution.py:65
  21.8 1.6 %collective-permute-start.9 = (bf16[192,1024]{1,0:T(8,128)(2,1)S(1)}, bf16[192,1024]{1,0:T(8,128)(2,1)S(1)}, u32[]{:S(2)}, u32[]{:S(2)}) collective-permute-start(bf16[192,1024]{1,0:T(8,128)(2,1)S(1)} %get-tuple-element.40), channel_id=1, source_target_pairs={{0,8},{4,12},{8,0},{12,4},{1,9},{5,13},{9,1},{13,5},{2,10},{6,14},... | collective-permute-start | bytes 1179656 | tf_op jit(solution)/shard_map/ppermute | solution.py:280
  23.4 6.4 %collective-permute-done.4.refs_1_ = bf16[192,1024]{1,0:T(8,128)(2,1)S(1)} collective-permute-done((bf16[192,1024]{1,0:T(8,128)(2,1)}, bf16[192,1024]{1,0:T(8,128)(2,1)S(1)}, u32[]{:S(2)}, u32[]{:S(2)}) %collective-permute-start.4) | collective-permute-done | bytes 393248 | tf_op jit(solution)/shard_map/ppermute | solution.py:296
  29.8 8.0 %collective-permute-done.3.cot_ref.refs_2_ = bf16[192,1024]{1,0:T(8,128)(2,1)S(1)} collective-permute-done((bf16[192,1024]{1,0:T(8,128)(2,1)S(1)}, bf16[192,1024]{1,0:T(8,128)(2,1)S(1)}, u32[]{:S(2)}, u32[]{:S(2)}) %collective-permute-start.3) | collective-permute-done | bytes 393248 | tf_op jit(solution)/shard_map/ppermute | solution.py:293
  39.0 1.2 %collective-permute-done.9.refs_0_ = bf16[192,1024]{1,0:T(8,128)(2,1)S(1)} collective-permute-done((bf16[192,1024]{1,0:T(8,128)(2,1)S(1)}, bf16[192,1024]{1,0:T(8,128)(2,1)S(1)}, u32[]{:S(2)}, u32[]{:S(2)}) %collective-permute-start.9) | collective-permute-done | bytes 393248 | tf_op jit(solution)/shard_map/ppermute | solution.py:280
  41.4 2.1 %shard_map.80 = (f32[192,1024]{1,0:T(8,128)S(1)}, bf16[192,1024]{1,0:T(8,128)(2,1)S(1)}) custom-call(s32[2]{0:T(128)S(1)} %pad_add_fusion.place_ref, bf16[192,1024]{1,0:T(8,128)(2,1)S(1)} %collective-permute-done.3.cot_ref.refs_2_, bf16[192,1024]{1,0:T(8,128)(2,1)S(1)} %collective-permute-done.5.pair_ref, bf16[2048,1024]{1,0:T(8,128)(2,1)S(1)} %copy-done, ...), custom_call_target="tpu_custom_call" | custom-call | flops 50331648 | bytes 1024 | tf_op jit(solution)/shard_map/pallas_call | solution.py:65
  43.5 1.8 %collective-permute-start.13 = (bf16[192,1024]{1,0:T(8,128)(2,1)S(1)}, bf16[192,1024]{1,0:T(8,128)(2,1)S(1)}, u32[]{:S(2)}, u32[]{:S(2)}) collective-permute-start(bf16[192,1024]{1,0:T(8,128)(2,1)S(1)} %get-tuple-element.42), channel_id=1, source_target_pairs={{0,8},{4,12},{8,0},{12,4},{1,9},{5,13},{9,1},{13,5},{2,10},{6,14},... | collective-permute-start | bytes 1179656 | tf_op jit(solution)/shard_map/ppermute | solution.py:280
  45.3 1.6 %collective-permute-start.12 = (bf16[192,1024]{1,0:T(8,128)(2,1)S(1)}, bf16[192,1024]{1,0:T(8,128)(2,1)S(1)}, u32[]{:S(2)}, u32[]{:S(2)}) collective-permute-start(bf16[192,1024]{1,0:T(8,128)(2,1)S(1)} %collective-permute-done.3.cot_ref.refs_2_), channel_id=1, source_target_pairs={{0,1},{1,2},{2,3},{3,0},{4,5},{5,6},{6,7},{7,4},{8,9},{9,10},{10,1... | collective-permute-start | bytes 1179656 | tf_op jit(solution)/shard_map/ppermute | solution.py:293
  46.9 2.1 %shard_map.81 = (f32[192,1024]{1,0:T(8,128)S(1)}, bf16[192,1024]{1,0:T(8,128)(2,1)S(1)}) custom-call(s32[2]{0:T(128)S(1)} %pad_add_fusion.place_ref, bf16[192,1024]{1,0:T(8,128)(2,1)S(1)} %copy-done.3, bf16[192,1024]{1,0:T(8,128)(2,1)S(1)} %collective-permute-done.pair_ref, bf16[2048,1024]{1,0:T(8,128)(2,1)S(1)} %copy-done, ...), custom_call_target="tpu_custom_call" | custom-call | flops 50331648 | bytes 1024 | tf_op jit(solution)/shard_map/pallas_call | solution.py:65
  49.0 2.1 %shard_map.82 = bf16[192,1024]{1,0:T(8,128)(2,1)S(1)} custom-call(s32[2]{0:T(128)S(1)} %pad_add_fusion.place_ref, bf16[192,1024]{1,0:T(8,128)(2,1)S(1)} %shard_map.79.mine_ref.refs_5_, bf16[192,1024]{1,0:T(8,128)(2,1)S(1)} %collective-permute-done.10.theirs_ref.refs_9_, bf16[1024,2048]{1,0:T(8,128)(2,1)S(1)} %copy-done.2), custom_call_target="tpu_custom_call" | custom-call | flops 50331648 | bytes 1024 | tf_op jit(solution)/shard_map/pallas_call | solution.py:65
  51.1 4.0 %collective-permute-done.13.refs_0_ = bf16[192,1024]{1,0:T(8,128)(2,1)S(1)} collective-permute-done((bf16[192,1024]{1,0:T(8,128)(2,1)S(1)}, bf16[192,1024]{1,0:T(8,128)(2,1)S(1)}, u32[]{:S(2)}, u32[]{:S(2)}) %collective-permute-start.13) | collective-permute-done | bytes 393248 | tf_op jit(solution)/shard_map/ppermute | solution.py:280
  56.2 2.2 %collective-permute-done.12.cot_ref.refs_3_ = bf16[192,1024]{1,0:T(8,128)(2,1)S(1)} collective-permute-done((bf16[192,1024]{1,0:T(8,128)(2,1)S(1)}, bf16[192,1024]{1,0:T(8,128)(2,1)S(1)}, u32[]{:S(2)}, u32[]{:S(2)}) %collective-permute-start.12) | collective-permute-done | bytes 393248 | tf_op jit(solution)/shard_map/ppermute | solution.py:293
  58.4 1.3 %collective-permute-start.11 = (bf16[192,1024]{1,0:T(8,128)(2,1)S(1)}, bf16[192,1024]{1,0:T(8,128)(2,1)S(1)}, u32[]{:S(2)}, u32[]{:S(2)}) collective-permute-start(bf16[192,1024]{1,0:T(8,128)(2,1)S(1)} %shard_map.82), channel_id=1, source_target_pairs={{0,1},{1,2},{2,3},{3,0},{4,5},{5,6},{6,7},{7,4},{8,9},{9,10},{10,1... | collective-permute-start | bytes 1179656 | tf_op jit(solution)/shard_map/ppermute | solution.py:316
  60.3 2.1 %shard_map.86 = (f32[192,1024]{1,0:T(8,128)S(1)}, bf16[192,1024]{1,0:T(8,128)(2,1)S(1)}) custom-call(s32[2]{0:T(128)S(1)} %pad_add_fusion.place_ref, bf16[192,1024]{1,0:T(8,128)(2,1)S(1)} %collective-permute-done.12.cot_ref.refs_3_, bf16[192,1024]{1,0:T(8,128)(2,1)S(1)} %collective-permute-done.18.pair_ref, bf16[2048,1024]{1,0:T(8,128)(2,1)S(1)} %copy-done.1, ...), custom_call_target="tpu_custom_call" | custom-call | flops 50331648 | bytes 1024 | tf_op jit(solution)/shard_map/pallas_call | solution.py:65
  62.4 1.6 %collective-permute-start.19 = (bf16[192,1024]{1,0:T(8,128)(2,1)S(1)}, bf16[192,1024]{1,0:T(8,128)(2,1)S(1)}, u32[]{:S(2)}, u32[]{:S(2)}) collective-permute-start(bf16[192,1024]{1,0:T(8,128)(2,1)S(1)} %get-tuple-element.54), channel_id=1, source_target_pairs={{0,8},{4,12},{8,0},{12,4},{1,9},{5,13},{9,1},{13,5},{2,10},{6,14},... | collective-permute-start | bytes 1179656 | tf_op jit(solution)/shard_map/ppermute | solution.py:280
  63.9 8.2 %collective-permute-done.14.refs_2_ = bf16[192,1024]{1,0:T(8,128)(2,1)S(1)} collective-permute-done((bf16[192,1024]{1,0:T(8,128)(2,1)S(1)}, bf16[192,1024]{1,0:T(8,128)(2,1)S(1)}, u32[]{:S(2)}, u32[]{:S(2)}) %collective-permute-start.14) | collective-permute-done | bytes 393248 | tf_op jit(solution)/shard_map/ppermute | solution.py:317
  72.7 7.5 %collective-permute-done.11.refs_0_ = bf16[192,1024]{1,0:T(8,128)(2,1)S(1)} collective-permute-done((bf16[192,1024]{1,0:T(8,128)(2,1)S(1)}, bf16[192,1024]{1,0:T(8,128)(2,1)S(1)}, u32[]{:S(2)}, u32[]{:S(2)}) %collective-permute-start.11) | collective-permute-done | bytes 393248 | tf_op jit(solution)/shard_map/ppermute | solution.py:316
  80.2 1.1 shard_map.84.place_ref
  81.3 2.1 %shard_map.85 = bf16[192,1024]{1,0:T(8,128)(2,1)S(1)} custom-call(s32[2]{0:T(128)S(1)} %shard_map.84.place_ref, bf16[192,1024]{1,0:T(8,128)(2,1)S(1)} %shard_map.83.mine_ref.refs_6_, bf16[192,1024]{1,0:T(8,128)(2,1)S(1)} %collective-permute-done.15.theirs_ref.refs_10_, bf16[1024,2048]{1,0:T(8,128)(2,1)S(1)} %copy-done.2, ...), custom_call_target="tpu_custom_call" | custom-call | flops 50331648 | bytes 1024 | tf_op jit(solution)/shard_map/pallas_call | solution.py:65
  84.9 8.6 %shard_map.88 = f32[2048,1024]{1,0:T(8,128)} custom-call(s32[2]{0:T(128)S(1)} %pad_add_fusion.place_ref, bf16[768,1024]{1,0:T(8,128)(2,1)S(1)} %shard_map.77.pre_ref.mine_ref, bf16[768,1024]{1,0:T(8,128)(2,1)S(1)} %collective-permute-done.20.theirs_ref, bf16[192,1024]{1,0:T(8,128)(2,1)S(1)} %copy-done.3, ...), custom_call_target="tpu_custom_call" | custom-call | flops 201326592 | bytes 1024 | tf_op jit(solution)/shard_map/pallas_call | solution.py:65
  95.2 2.1 %collective-permute-done.17.refs_3_ = bf16[192,1024]{1,0:T(8,128)(2,1)S(1)} collective-permute-done((bf16[192,1024]{1,0:T(8,128)(2,1)S(1)}, bf16[192,1024]{1,0:T(8,128)(2,1)S(1)}, u32[]{:S(2)}, u32[]{:S(2)}) %collective-permute-start.17) | collective-permute-done | bytes 393248 | tf_op jit(solution)/shard_map/ppermute | solution.py:317
  97.3 7.2 %collective-permute-done.16.refs_0_ = bf16[192,1024]{1,0:T(8,128)(2,1)S(1)} collective-permute-done((bf16[192,1024]{1,0:T(8,128)(2,1)S(1)}, bf16[192,1024]{1,0:T(8,128)(2,1)S(1)}, u32[]{:S(2)}, u32[]{:S(2)}) %collective-permute-start.16) | collective-permute-done | bytes 393248 | tf_op jit(solution)/shard_map/ppermute | solution.py:316
  105.6 2.1 %shard_map.91 = bf16[192,1024]{1,0:T(8,128)(2,1)S(1)} custom-call(s32[2]{0:T(128)S(1)} %shard_map.90.place_ref, bf16[192,1024]{1,0:T(8,128)(2,1)S(1)} %shard_map.87.mine_ref.refs_7_, bf16[192,1024]{1,0:T(8,128)(2,1)S(1)} %collective-permute-done.22.theirs_ref.refs_11_, bf16[1024,2048]{1,0:T(8,128)(2,1)S(1)} %copy-done.2, ...), custom_call_target="tpu_custom_call" | custom-call | flops 50331648 | bytes 1024 | tf_op jit(solution)/shard_map/pallas_call | solution.py:65
  107.8 6.6 %shard_map.92 = f32[1024,2048]{1,0:T(8,128)} custom-call(s32[2]{0:T(128)S(1)} %pad_add_fusion.place_ref, bf16[192,1024]{1,0:T(8,128)(2,1)S(1)} %copy-done.5, bf16[192,1024]{1,0:T(8,128)(2,1)S(1)} %collective-permute-done.4.refs_1_, bf16[192,1024]{1,0:T(8,128)(2,1)S(1)} %collective-permute-done.14.refs_2_, ...), custom_call_target="tpu_custom_call" | custom-call | flops 201326592 | bytes 1024 | tf_op jit(solution)/shard_map/pallas_call | solution.py:65
  114.4 5.0 %collective-permute-done.23.refs_0_ = bf16[192,1024]{1,0:T(8,128)(2,1)S(1)} collective-permute-done((bf16[192,1024]{1,0:T(8,128)(2,1)S(1)}, bf16[192,1024]{1,0:T(8,128)(2,1)S(1)}, u32[]{:S(2)}, u32[]{:S(2)}) %collective-permute-start.23) | collective-permute-done | bytes 393248 | tf_op jit(solution)/shard_map/ppermute | solution.py:324
  120.5 2.8 %shard_map.94 = bf16[192,1024]{1,0:T(8,128)(2,1)} custom-call(s32[2]{0:T(128)S(1)} %shard_map.93.place_ref, bf16[192,1024]{1,0:T(8,128)(2,1)S(1)} %shard_map.89.refs_4_.mine_ref, bf16[192,1024]{1,0:T(8,128)(2,1)S(1)} %collective-permute-done.24.refs_8_.theirs_ref, bf16[1024,2048]{1,0:T(8,128)(2,1)S(1)} %copy-done.2, ...), custom_call_target="tpu_custom_call" | custom-call | flops 50331648 | bytes 1024 | tf_op jit(solution)/shard_map/pallas_call | solution.py:65
  (50 shorter events, 12.9 us)
Async XLA Ops:
  0.7 16.9 %collective-permute-start.8 = (bf16[2048,1024]{1,0:T(8,128)(2,1)}, bf16[2048,1024]{1,0:T(8,128)(2,1)S(1)}, u32[]{:S(2)}, u32[]{:S(2)}) collective-permute-start(bf16[2048,1024]{1,0:T(8,128)(2,1)} %mine_ref.4), channel_id=1, source_target_pairs={{0,4},{4,0},{8,12},{12,8},{1,5},{5,1},{9,13},{13,9},{2,6},{6,2},{1... | collective-permute-start | bytes 12582920 | tf_op jit(solution)/shard_map/ppermute | solution.py:271
  1.2 8.1 %collective-permute-start.2 = (bf16[192,2048]{1,0:T(8,128)(2,1)}, bf16[192,2048]{1,0:T(8,128)(2,1)S(1)}, u32[]{:S(2)}, u32[]{:S(2)}) collective-permute-start(bf16[192,2048]{1,0:T(8,128)(2,1)} %mine_ref), channel_id=1, source_target_pairs={{0,4},{4,0},{8,12},{12,8},{1,5},{5,1},{9,13},{13,9},{2,6},{6,2},{1... | collective-permute-start | bytes 2359304 | tf_op jit(solution)/shard_map/ppermute | solution.py:269
  1.2 14.6 %collective-permute-start.1 = (bf16[192,1024]{1,0:T(8,128)(2,1)}, bf16[192,1024]{1,0:T(8,128)(2,1)S(1)}, u32[]{:S(2)}, u32[]{:S(2)}) collective-permute-start(bf16[192,1024]{1,0:T(8,128)(2,1)} %refs_0_.1), channel_id=1, source_target_pairs={{0,1},{1,2},{2,3},{3,0},{4,5},{5,6},{6,7},{7,4},{8,9},{9,10},{10,1... | collective-permute-start | bytes 1179656 | tf_op jit(solution)/shard_map/ppermute | solution.py:293
  9.3 1.1 copy-start.4
  10.4 27.4 %copy-start.3 = (bf16[192,1024]{1,0:T(8,128)(2,1)S(1)}, bf16[192,1024]{1,0:T(8,128)(2,1)}, u32[]{:S(2)}) copy-start(bf16[192,1024]{1,0:T(8,128)(2,1)} %refs_0_.1) | copy-start | bytes 1179652
  11.0 27.3 %collective-permute-start.6 = (bf16[384,1024]{1,0:T(8,128)(2,1)S(1)}, bf16[384,1024]{1,0:T(8,128)(2,1)S(1)}, u32[]{:S(2)}, u32[]{:S(2)}) collective-permute-start(bf16[384,1024]{1,0:T(8,128)(2,1)S(1)} %shard_map.76.refs_0_), channel_id=1, source_target_pairs={{0,8},{4,12},{8,0},{12,4},{1,9},{5,13},{9,1},{13,5},{2,10},{6,14},... | collective-permute-start | bytes 2359304 | tf_op jit(solution)/shard_map/ppermute | solution.py:270
  15.8 1.7 %collective-permute-start.7 = (bf16[192,1024]{1,0:T(8,128)(2,1)S(1)}, bf16[192,1024]{1,0:T(8,128)(2,1)S(1)}, u32[]{:S(2)}, u32[]{:S(2)}) collective-permute-start(bf16[192,1024]{1,0:T(8,128)(2,1)S(1)} %collective-permute-done.1.cot_ref.refs_1_), channel_id=1, source_target_pairs={{0,4},{4,0},{8,12},{12,8},{1,5},{5,1},{9,13},{13,9},{2,6},{6,2},{1... | collective-permute-start | bytes 1179656 | tf_op jit(solution)/shard_map/ppermute | solution.py:275
  15.8 13.9 %collective-permute-start.4 = (bf16[192,1024]{1,0:T(8,128)(2,1)}, bf16[192,1024]{1,0:T(8,128)(2,1)S(1)}, u32[]{:S(2)}, u32[]{:S(2)}) collective-permute-start(bf16[192,1024]{1,0:T(8,128)(2,1)} %refs_0_.2), channel_id=1, source_target_pairs={{0,1},{1,2},{2,3},{3,0},{4,5},{5,6},{6,7},{7,4},{8,9},{9,10},{10,1... | collective-permute-start | bytes 1179656 | tf_op jit(solution)/shard_map/ppermute | solution.py:296
  15.8 22.0 %collective-permute-start.3 = (bf16[192,1024]{1,0:T(8,128)(2,1)S(1)}, bf16[192,1024]{1,0:T(8,128)(2,1)S(1)}, u32[]{:S(2)}, u32[]{:S(2)}) collective-permute-start(bf16[192,1024]{1,0:T(8,128)(2,1)S(1)} %collective-permute-done.1.cot_ref.refs_1_), channel_id=1, source_target_pairs={{0,1},{1,2},{2,3},{3,0},{4,5},{5,6},{6,7},{7,4},{8,9},{9,10},{10,1... | collective-permute-start | bytes 1179656 | tf_op jit(solution)/shard_map/ppermute | solution.py:293
  17.6 2.2 %copy-start = (bf16[2048,1024]{1,0:T(8,128)(2,1)S(1)}, bf16[2048,1024]{1,0:T(8,128)(2,1)}, u32[]{:S(2)}) copy-start(bf16[2048,1024]{1,0:T(8,128)(2,1)} %mine_ref.4) | copy-start | bytes 12582916
  21.8 18.4 %collective-permute-start.9 = (bf16[192,1024]{1,0:T(8,128)(2,1)S(1)}, bf16[192,1024]{1,0:T(8,128)(2,1)S(1)}, u32[]{:S(2)}, u32[]{:S(2)}) collective-permute-start(bf16[192,1024]{1,0:T(8,128)(2,1)S(1)} %get-tuple-element.40), channel_id=1, source_target_pairs={{0,8},{4,12},{8,0},{12,4},{1,9},{5,13},{9,1},{13,5},{2,10},{6,14},... | collective-permute-start | bytes 1179656 | tf_op jit(solution)/shard_map/ppermute | solution.py:280
  37.8 3.6 %collective-permute-start.5 = (bf16[192,1024]{1,0:T(8,128)(2,1)S(1)}, bf16[192,1024]{1,0:T(8,128)(2,1)S(1)}, u32[]{:S(2)}, u32[]{:S(2)}) collective-permute-start(bf16[192,1024]{1,0:T(8,128)(2,1)S(1)} %collective-permute-done.3.cot_ref.refs_2_), channel_id=1, source_target_pairs={{0,4},{4,0},{8,12},{12,8},{1,5},{5,1},{9,13},{13,9},{2,6},{6,2},{1... | collective-permute-start | bytes 1179656 | tf_op jit(solution)/shard_map/ppermute | solution.py:275
  37.8 9.1 %collective-permute-start = (bf16[192,1024]{1,0:T(8,128)(2,1)S(1)}, bf16[192,1024]{1,0:T(8,128)(2,1)S(1)}, u32[]{:S(2)}, u32[]{:S(2)}) collective-permute-start(bf16[192,1024]{1,0:T(8,128)(2,1)S(1)} %copy-done.3), channel_id=1, source_target_pairs={{0,4},{4,0},{8,12},{12,8},{1,5},{5,1},{9,13},{13,9},{2,6},{6,2},{1... | collective-permute-start | bytes 1179656 | tf_op jit(solution)/shard_map/ppermute | solution.py:275
  41.4 7.6 %collective-permute-start.10 = (bf16[192,1024]{1,0:T(8,128)(2,1)S(1)}, bf16[192,1024]{1,0:T(8,128)(2,1)S(1)}, u32[]{:S(2)}, u32[]{:S(2)}) collective-permute-start(bf16[192,1024]{1,0:T(8,128)(2,1)S(1)} %shard_map.79.mine_ref.refs_5_), channel_id=1, source_target_pairs={{0,4},{4,0},{8,12},{12,8},{1,5},{5,1},{9,13},{13,9},{2,6},{6,2},{1... | collective-permute-start | bytes 1179656 | tf_op jit(solution)/shard_map/ppermute | solution.py:284
  43.5 5.5 %copy-start.2 = (bf16[1024,2048]{1,0:T(8,128)(2,1)S(1)}, bf16[1024,2048]{1,0:T(8,128)(2,1)}, u32[]{:S(2)}) copy-start(bf16[1024,2048]{1,0:T(8,128)(2,1)} %up_ref.7) | copy-start | bytes 12582916
  43.5 11.6 %collective-permute-start.13 = (bf16[192,1024]{1,0:T(8,128)(2,1)S(1)}, bf16[192,1024]{1,0:T(8,128)(2,1)S(1)}, u32[]{:S(2)}, u32[]{:S(2)}) collective-permute-start(bf16[192,1024]{1,0:T(8,128)(2,1)S(1)} %get-tuple-element.42), channel_id=1, source_target_pairs={{0,8},{4,12},{8,0},{12,4},{1,9},{5,13},{9,1},{13,5},{2,10},{6,14},... | collective-permute-start | bytes 1179656 | tf_op jit(solution)/shard_map/ppermute | solution.py:280
  45.3 13.1 %collective-permute-start.12 = (bf16[192,1024]{1,0:T(8,128)(2,1)S(1)}, bf16[192,1024]{1,0:T(8,128)(2,1)S(1)}, u32[]{:S(2)}, u32[]{:S(2)}) collective-permute-start(bf16[192,1024]{1,0:T(8,128)(2,1)S(1)} %collective-permute-done.3.cot_ref.refs_2_), channel_id=1, source_target_pairs={{0,1},{1,2},{2,3},{3,0},{4,5},{5,6},{6,7},{7,4},{8,9},{9,10},{10,1... | collective-permute-start | bytes 1179656 | tf_op jit(solution)/shard_map/ppermute | solution.py:293
  49.0 11.3 %copy-start.1 = (bf16[2048,1024]{1,0:T(8,128)(2,1)S(1)}, bf16[2048,1024]{1,0:T(8,128)(2,1)}, u32[]{:S(2)}) copy-start(bf16[2048,1024]{1,0:T(8,128)(2,1)} %mine_ref.4) | copy-start | bytes 12582916
  58.4 1.9 %collective-permute-start.18 = (bf16[192,1024]{1,0:T(8,128)(2,1)S(1)}, bf16[192,1024]{1,0:T(8,128)(2,1)S(1)}, u32[]{:S(2)}, u32[]{:S(2)}) collective-permute-start(bf16[192,1024]{1,0:T(8,128)(2,1)S(1)} %collective-permute-done.12.cot_ref.refs_3_), channel_id=1, source_target_pairs={{0,4},{4,0},{8,12},{12,8},{1,5},{5,1},{9,13},{13,9},{2,6},{6,2},{1... | collective-permute-start | bytes 1179656 | tf_op jit(solution)/shard_map/ppermute | solution.py:275
  58.4 13.7 %collective-permute-start.14 = (bf16[192,1024]{1,0:T(8,128)(2,1)S(1)}, bf16[192,1024]{1,0:T(8,128)(2,1)S(1)}, u32[]{:S(2)}, u32[]{:S(2)}) collective-permute-start(bf16[192,1024]{1,0:T(8,128)(2,1)S(1)} %collective-permute-done.4.refs_1_), channel_id=1, source_target_pairs={{0,1},{1,2},{2,3},{3,0},{4,5},{5,6},{6,7},{7,4},{8,9},{9,10},{10,1... | collective-permute-start | bytes 1179656 | tf_op jit(solution)/shard_map/ppermute | solution.py:317
  58.4 21.7 %collective-permute-start.11 = (bf16[192,1024]{1,0:T(8,128)(2,1)S(1)}, bf16[192,1024]{1,0:T(8,128)(2,1)S(1)}, u32[]{:S(2)}, u32[]{:S(2)}) collective-permute-start(bf16[192,1024]{1,0:T(8,128)(2,1)S(1)} %shard_map.82), channel_id=1, source_target_pairs={{0,1},{1,2},{2,3},{3,0},{4,5},{5,6},{6,7},{7,4},{8,9},{9,10},{10,1... | collective-permute-start | bytes 1179656 | tf_op jit(solution)/shard_map/ppermute | solution.py:316
  59.8 25.2 %collective-permute-start.20 = (bf16[768,1024]{1,0:T(8,128)(2,1)S(1)}, bf16[768,1024]{1,0:T(8,128)(2,1)S(1)}, u32[]{:S(2)}, u32[]{:S(2)}) collective-permute-start(bf16[768,1024]{1,0:T(8,128)(2,1)S(1)} %shard_map.77.pre_ref.mine_ref), channel_id=1, source_target_pairs={{0,4},{4,0},{8,12},{12,8},{1,5},{5,1},{9,13},{13,9},{2,6},{6,2},{1... | collective-permute-start | bytes 4718600 | tf_op jit(solution)/shard_map/ppermute | solution.py:314
  59.8 21.5 %collective-permute-start.15 = (bf16[192,1024]{1,0:T(8,128)(2,1)S(1)}, bf16[192,1024]{1,0:T(8,128)(2,1)S(1)}, u32[]{:S(2)}, u32[]{:S(2)}) collective-permute-start(bf16[192,1024]{1,0:T(8,128)(2,1)S(1)} %shard_map.83.mine_ref.refs_6_), channel_id=1, source_target_pairs={{0,4},{4,0},{8,12},{12,8},{1,5},{5,1},{9,13},{13,9},{2,6},{6,2},{1... | collective-permute-start | bytes 1179656 | tf_op jit(solution)/shard_map/ppermute | solution.py:284
  62.4 21.4 %collective-permute-start.19 = (bf16[192,1024]{1,0:T(8,128)(2,1)S(1)}, bf16[192,1024]{1,0:T(8,128)(2,1)S(1)}, u32[]{:S(2)}, u32[]{:S(2)}) collective-permute-start(bf16[192,1024]{1,0:T(8,128)(2,1)S(1)} %get-tuple-element.54), channel_id=1, source_target_pairs={{0,8},{4,12},{8,0},{12,4},{1,9},{5,13},{9,1},{13,5},{2,10},{6,14},... | collective-permute-start | bytes 1179656 | tf_op jit(solution)/shard_map/ppermute | solution.py:280
  72.1 21.4 %collective-permute-start.21 = (bf16[192,1024]{1,0:T(8,128)(2,1)S(1)}, bf16[192,1024]{1,0:T(8,128)(2,1)S(1)}, u32[]{:S(2)}, u32[]{:S(2)}) collective-permute-start(bf16[192,1024]{1,0:T(8,128)(2,1)S(1)} %get-tuple-element.59), channel_id=1, source_target_pairs={{0,8},{4,12},{8,0},{12,4},{1,9},{5,13},{9,1},{13,5},{2,10},{6,14},... | collective-permute-start | bytes 1179656 | tf_op jit(solution)/shard_map/ppermute | solution.py:280
  83.4 13.9 %collective-permute-start.17 = (bf16[192,1024]{1,0:T(8,128)(2,1)S(1)}, bf16[192,1024]{1,0:T(8,128)(2,1)S(1)}, u32[]{:S(2)}, u32[]{:S(2)}) collective-permute-start(bf16[192,1024]{1,0:T(8,128)(2,1)S(1)} %collective-permute-done.14.refs_2_), channel_id=1, source_target_pairs={{0,1},{1,2},{2,3},{3,0},{4,5},{5,6},{6,7},{7,4},{8,9},{9,10},{10,1... | collective-permute-start | bytes 1179656 | tf_op jit(solution)/shard_map/ppermute | solution.py:317
  83.5 21.0 %collective-permute-start.16 = (bf16[192,1024]{1,0:T(8,128)(2,1)S(1)}, bf16[192,1024]{1,0:T(8,128)(2,1)S(1)}, u32[]{:S(2)}, u32[]{:S(2)}) collective-permute-start(bf16[192,1024]{1,0:T(8,128)(2,1)S(1)} %shard_map.85), channel_id=1, source_target_pairs={{0,1},{1,2},{2,3},{3,0},{4,5},{5,6},{6,7},{7,4},{8,9},{9,10},{10,1... | collective-permute-start | bytes 1179656 | tf_op jit(solution)/shard_map/ppermute | solution.py:316
  84.9 20.7 %collective-permute-start.22 = (bf16[192,1024]{1,0:T(8,128)(2,1)S(1)}, bf16[192,1024]{1,0:T(8,128)(2,1)S(1)}, u32[]{:S(2)}, u32[]{:S(2)}) collective-permute-start(bf16[192,1024]{1,0:T(8,128)(2,1)S(1)} %shard_map.87.mine_ref.refs_7_), channel_id=1, source_target_pairs={{0,4},{4,0},{8,12},{12,8},{1,5},{5,1},{9,13},{13,9},{2,6},{6,2},{1... | collective-permute-start | bytes 1179656 | tf_op jit(solution)/shard_map/ppermute | solution.py:284
  94.7 13.1 %collective-permute-start.24 = (bf16[192,1024]{1,0:T(8,128)(2,1)S(1)}, bf16[192,1024]{1,0:T(8,128)(2,1)S(1)}, u32[]{:S(2)}, u32[]{:S(2)}) collective-permute-start(bf16[192,1024]{1,0:T(8,128)(2,1)S(1)} %shard_map.89.refs_4_.mine_ref), channel_id=1, source_target_pairs={{0,4},{4,0},{8,12},{12,8},{1,5},{5,1},{9,13},{13,9},{2,6},{6,2},{1... | collective-permute-start | bytes 1179656 | tf_op jit(solution)/shard_map/ppermute | solution.py:284
  105.6 2.2 %copy-start.5 = (bf16[192,1024]{1,0:T(8,128)(2,1)S(1)}, bf16[192,1024]{1,0:T(8,128)(2,1)}, u32[]{:S(2)}) copy-start(bf16[192,1024]{1,0:T(8,128)(2,1)} %refs_0_.2) | copy-start | bytes 1179652
  107.7 11.7 %collective-permute-start.23 = (bf16[192,1024]{1,0:T(8,128)(2,1)S(1)}, bf16[192,1024]{1,0:T(8,128)(2,1)S(1)}, u32[]{:S(2)}, u32[]{:S(2)}) collective-permute-start(bf16[192,1024]{1,0:T(8,128)(2,1)S(1)} %shard_map.91), channel_id=1, source_target_pairs={{0,1},{1,2},{2,3},{3,0},{4,5},{5,6},{6,7},{7,4},{8,9},{9,10},{10,1... | collective-permute-start | bytes 1179656 | tf_op jit(solution)/shard_map/ppermute | solution.py:324

commit v8 on v6

--- a/solution.py
+++ b/solution.py
@@ -11,7 +11,7 @@
 LAST = (((1,), (1,)), ((), ()))
 FIRST = (((0,), (0,)), ((), ()))
 MIB = 1024 * 1024
-LITTLE = pl.CostEstimate(flops=1024, bytes_accessed=1024, transcendentals=0)
+LITTLE, SOME, MORE, MUCH, MOST = 10**7, 10**8, 10**9, 4 * 10**9, 8 * 10**9
 
 
 def gelu_parts(values):
@@ -60,7 +60,7 @@
     return lax.rem(place_ref[1], 2)
 
 
-def call(kernel, place, operands, outs, mib, grid=(1,), in_specs=None, out_specs=None, scratch=()):
+def call(kernel, place, operands, outs, mib, cost, grid=(1,), in_specs=None, out_specs=None, scratch=()):
     return pl.pallas_call(
         kernel,
         out_shape=outs,
@@ -72,7 +72,7 @@
             scratch_shapes=scratch,
         ),
         compiler_params=pltpu.CompilerParams(vmem_limit_bytes=mib * MIB),
-        cost_estimate=LITTLE,
+        cost_estimate=pl.CostEstimate(flops=cost, bytes_accessed=1024, transcendentals=0),
     )(place, *operands)
 
 
@@ -89,24 +89,34 @@
 def lay_out_call(place, blocks, shifts, rows):
     tokens, hidden = blocks[0].shape
     out = jax.ShapeDtypeStruct((tokens * len(blocks), hidden), jnp.bfloat16)
-    return call(functools.partial(lay_out_kernel, shifts, rows), place, blocks, out, 8)
+    return call(functools.partial(lay_out_kernel, shifts, rows), place, blocks, out, 8, SOME)
+
+
+def take_rows_kernel(place_ref, rows_ref, out_ref):
+    out_ref[...] = rows_ref[block(core_of(place_ref), out_ref.shape[0]), :]
+
+
+def take_rows_call(place, weight):
+    out = jax.ShapeDtypeStruct((weight.shape[0] // 2, weight.shape[1]), weight.dtype)
+    return call(take_rows_kernel, place, [weight], out, 12, LITTLE)
 
 
 def hidden_kernel(place_ref, cot_ref, pair_ref, mine_ref, theirs_ref, part_ref, sent_ref):
     half = part_ref.shape[1]
     tile = tile_of(half)
     for first in range(0, half, tile):
+        here = pl.ds(first, tile)
         rows = pl.ds(pl.multiple_of(core_of(place_ref) * half + first, tile), tile)
-        part = dot(cot_ref[...], mine_ref[rows, :], LAST)
+        part = dot(cot_ref[...], mine_ref[here, :], LAST)
         part = part + dot(pair_ref[...], theirs_ref[rows, :], LAST)
-        part_ref[:, pl.ds(first, tile)] = part
-        sent_ref[:, pl.ds(first, tile)] = part.astype(jnp.bfloat16)
+        part_ref[:, here] = part
+        sent_ref[:, here] = part.astype(jnp.bfloat16)
 
 
 def hidden_call(place, cot, cot_pair, down_mine, down_pair):
-    shape = (cot.shape[0], down_mine.shape[0] // 2)
+    shape = (cot.shape[0], down_mine.shape[0])
     outs = [jax.ShapeDtypeStruct(shape, jnp.float32), jax.ShapeDtypeStruct(shape, jnp.bfloat16)]
-    return call(hidden_kernel, place, [cot, cot_pair, down_mine, down_pair], outs, 12)
+    return call(hidden_kernel, place, [cot, cot_pair, down_mine, down_pair], outs, 12, LITTLE)
 
 
 def pre_grad_kernel(step, cols, place_ref, pre_ref, part_ref, *refs):
@@ -127,11 +137,10 @@
 def pre_grad_call(place, step, cols, pre_all, part, others):
     out = jax.ShapeDtypeStruct(part.shape, jnp.bfloat16)
     kernel = functools.partial(pre_grad_kernel, step, cols)
-    return call(kernel, place, [pre_all, part, *others], out, 8)
-
-
-def share_kernel(place_ref, mine_ref, theirs_ref, up_ref, *refs):
-    out_ref = refs[-1]
+    return call(kernel, place, [pre_all, part, *others], out, 8, SOME)
+
+
+def share_kernel(place_ref, mine_ref, theirs_ref, up_ref, out_ref, *sent_refs):
     features, half = up_ref.shape[0], mine_ref.shape[1]
     tile = tile_of(features)
     left, right = block(core_of(place_ref), half), block(1 - core_of(place_ref), half)
@@ -139,14 +148,32 @@
         here = pl.ds(first, tile)
         total = dot(mine_ref[...], up_ref[here, left], LAST)
         total = total + dot(theirs_ref[...], up_ref[here, right], LAST)
+        out_ref[:, here] = total
+        for sent in sent_refs:
+            sent[:, here] = total.astype(jnp.bfloat16)
+
+
+def share_call(place, mine, theirs, up_weight, first):
+    shape = (mine.shape[0], up_weight.shape[0])
+    outs = [jax.ShapeDtypeStruct(shape, jnp.float32)]
+    outs += [jax.ShapeDtypeStruct(shape, jnp.bfloat16)] * first
+    return call(share_kernel, place, [mine, theirs, up_weight], outs, 12, LITTLE)
+
+
+def add_kernel(place_ref, part_ref, *refs):
+    out_ref = refs[-1]
+    rows = 64 if part_ref.shape[0] % 64 == 0 else part_ref.shape[0]
+    for first in range(0, part_ref.shape[0], rows):
+        here = pl.ds(first, rows)
+        total = part_ref[here, :].astype(jnp.float32)
         for arrived in refs[:-1]:
-            total = total + arrived[:, here].astype(jnp.float32)
-        out_ref[:, here] = total.astype(jnp.bfloat16)
-
-
-def share_call(place, mine, theirs, up_weight, arrived):
-    out = jax.ShapeDtypeStruct((mine.shape[0], up_weight.shape[0]), jnp.bfloat16)
-    return call(share_kernel, place, [mine, theirs, up_weight, *arrived], out, 12)
+            total = total + arrived[here, :].astype(jnp.float32)
+        out_ref[here, :] = total.astype(out_ref.dtype)
+
+
+def add_call(place, part, arrived, dtype, cost):
+    out = jax.ShapeDtypeStruct(part.shape, dtype)
+    return call(add_kernel, place, [part, *arrived], out, 4, cost)
 
 
 def grad_down_kernel(blocks, scale, place_ref, pre_ref, *refs):
@@ -172,6 +199,7 @@
         [pre_all, *cots],
         jax.ShapeDtypeStruct((hidden, features), jnp.float32),
         14,
+        SOME,
         grid=(hidden // tile,),
         in_specs=[pl.BlockSpec((total, tile), lambda i, place: (0, i))]
         + [in_vmem() for _ in cots],
@@ -209,6 +237,7 @@
         [*ins, *mine, *pair],
         jax.ShapeDtypeStruct((features, hidden), jnp.float32),
         18,
+        MORE,
         grid=(features // tile,),
         out_specs=pl.BlockSpec((tile, hidden), lambda i, place: (i, 0)),
         scratch=[
@@ -225,6 +254,7 @@
         after(x, place) for x in (cotangent, preactivation, down_weight)
     )
     ring = [(i, (i + 1) % cols) for i in range(cols)]
+    back = [(i, (i - 1) % cols) for i in range(cols)]
     pair = [(i, i ^ 1) for i in range(rows)]
     shifts = range(0, rows, 2)
     over_x = [[(i, (i + shift) % rows) for i in range(rows)] for shift in shifts[1:]]
@@ -232,11 +262,12 @@
 
     pres = [preactivation] + [lax.ppermute(preactivation, "row", to) for to in over_x]
     down_pair = lax.ppermute(down_weight, "row", pair)
+    down_mine = take_rows_call(place, down_weight)
     parts, sent, others, mine, theirs = ([None] * cols for _ in range(5))
 
     def hidden_part(s, *first):
         cot_pair = after(lax.ppermute(cots[s], "row", pair), *first)
-        parts[s], sent[s] = hidden_call(place, cots[s], cot_pair, down_weight, down_pair)
+        parts[s], sent[s] = hidden_call(place, cots[s], cot_pair, down_mine, down_pair)
 
     def exchange(s, *first):
         values = after(sent[s], *first)
@@ -246,45 +277,70 @@
         mine[s] = pre_grad_call(after(place, *first), s, cols, pre_all, parts[s], others[s])
         theirs[s] = lax.ppermute(mine[s], "row", pair)
 
-    def share(s, arrived, *first):
-        return share_call(after(place, *first), mine[s], theirs[s], up_weight, arrived)
-
-    cots, ins = [cotangent], [inputs]
-    arriving = lax.ppermute(cotangent, "col", ring)
+    def share(s, *first):
+        sends = s in (1, cols - 1)
+        return share_call(after(place, *first), mine[s], theirs[s], up_weight, sends)
+
+    cots, middle = [cotangent] + [None] * (cols - 1), cols // 2
+    order = []
+    for s in range(1, middle + 1):
+        cots[s] = lax.ppermute(cots[s - 1], "col", ring)
+        order.append(s)
+        if cols - s > middle:
+            cots[cols - s] = lax.ppermute(cots[(cols - s + 1) % cols], "col", back)
+            order.append(cols - s)
+    arrived = list(cots)
+
+    def hidden_next(i):
+        s = order[i]
+        arrived[s] = after(cots[s], sent[order[i - 1]] if i else down_mine)
+        cot_pair = lax.ppermute(arrived[s], "row", pair)
+        parts[s], sent[s] = hidden_call(place, cots[s], cot_pair, down_mine, down_pair)
+        exchange(s)
+
+    for i in range(len(order)):
+        hidden_next(i)
+    pres = pres + [lax.ppermute(after(p, sent[1]), "row", pair) for p in pres]
+    pre_all = lay_out_call(place, pres, shifts, rows)
+    hidden_part(0, sent[order[-1]])
+    exchange(0)
+    parts[1], others[1] = add_call(after(place, sent[order[1]]), parts[1], others[1], jnp.float32, MOST), []
+    shares = {}
+    for s in order:
+        pre_grad(s, *(shares[t][0] for t in shares), *([sent[order[2]]] if s == order[1] else []))
+        if s in (1, cols - 1):
+            shares[s] = share(s)
+    for s in order:
+        if s not in shares:
+            shares[s] = share(s)
+
+    ins = [inputs]
     for s in range(1, cols):
-        if s == 2:
-            arriving = after(arriving, sent[0])
-        elif s > 2:
-            arriving = after(arriving, sent[s - 1])
-        cots.append(arriving)
-        if s < cols - 1:
-            arriving = lax.ppermute(arriving, "col", ring)
-            hidden_part(s)
-            exchange(s)
-        if s == 1:
-            hidden_part(0, sent[1], *pres[1:])
-            pres = pres + [lax.ppermute(after(p, sent[1]), "row", pair) for p in pres]
-
-    last = cols - 1
-    pre_all = lay_out_call(after(place, sent[last - 1]), pres, shifts, rows)
-    pre_grad(1, sent[last - 1])
-    ins.append(lax.ppermute(after(inputs, cots[last - 1]), "col", ring))
-    sums = share(1, [], mine[1])
-    pre_grad(2, sums)
-    hidden_part(last, mine[2], ins[1])
-    exchange(last)
-    exchange(0, sent[last])
-    grad_down = grad_down_call(after(place, sums, sent[last]), pre_all, cots, scale)
-    late = grad_down
-    for s in range(2, cols):
-        following = (s + 1) % cols
-        pre_grad(following, late)
-        arrived = lax.ppermute(sums, "col", ring)
         ins.append(lax.ppermute(ins[-1], "col", ring))
-        sums = late = share(s, [arrived], mine[following], ins[s])
-    arrived = lax.ppermute(sums, "col", ring)
-    grad_up = grad_up_call(after(place, sums), ins, mine, theirs, scale)
-    sums = share(0, [arrived], grad_up)
+
+    right = left = None
+    for j in range(1, cols):
+        forth, mirror = shares[j], shares[cols - j]
+        if j == 1:
+            right, left = forth[1], mirror[1]
+        elif 2 * j == cols:
+            both = add_call(place, right, [left], jnp.float32, MUCH)
+            right = left = add_call(place, both, [forth[0]], jnp.bfloat16, LITTLE)
+        else:
+            right, left = (
+                add_call(place, forth[0], [right], jnp.bfloat16, LITTLE),
+                add_call(place, mirror[0], [left], jnp.bfloat16, LITTLE),
+            )
+        if j == cols - 2:
+            grad_down = grad_down_call(after(place, right, left), pre_all, cots, scale)
+            pre_grad(0, grad_down, ins[-1])
+        if j == cols - 1:
+            late = after(place, right, left, mine[0])
+        right = lax.ppermute(right, "col", [(z, z + 1) for z in range(j)])
+        left = lax.ppermute(left, "col", [(z, z - 1) for z in range(cols - j, cols)])
+    own = share(0)[0]
+    grad_up = grad_up_call(after(late, own), ins, mine, theirs, scale)
+    sums = add_call(after(place, grad_up), own, [right, left], jnp.bfloat16, LITTLE)
     return (sums, grad_up, grad_down)
 
 

time: 106 us -> 114 us (1.075)
  starting transfers between devices: 10.6 us -> 30.8 us
  waiting for transfers between devices: 53.8 us -> 37.4 us
  Pallas kernels: 38 us -> 42.5 us
    ppermute x7 -> x12, starting transfers between devices: 3.15 us -> 22.4 us  [the longest x3 15.3 us: per_device(): right = lax.ppermute(right, 'col', [(z, z + 1) for z in range(j)])]
    ppermute x7 -> x12, waiting for transfers between devices: 33.8 us -> 26.2 us  [the longest x2 16.8 us: per_device(): cots[s] = lax.ppermute(cots[s - 1], 'col', ring)]
    ppermute x2 -> x3, waiting for transfers between devices: 9.92 us -> 3.11 us  [per_device(): ins.append(lax.ppermute(ins[-1], 'col', ring))]
    pallas_call x15 -> x22, Pallas kernels: 38 us -> 42.5 us  [call(): pl.pallas_call(kernel, out_shape=outs, grid_spec=pltpu.PrefetchScalarGrid...]
    ppermute x4 -> x1, waiting for transfers between devices: 1.96 us -> 0.01 us  [hidden_part(): cot_pair = after(lax.ppermute(cots[s], 'row', pair), *first)]
    ppermute x1, waiting for transfers between devices: 1.34 us -> 0.01 us  [per_device(): lax.ppermute(preactivation, 'row', to)]
    ppermute x4, waiting for transfers between devices: 6.75 us -> 8.08 us  [exchange(): others[s] = [lax.ppermute(values, 'row', to) for to in over_x]]
    ppermute x4, starting transfers between devices: 3.81 us -> 5.13 us  [exchange(): others[s] = [lax.ppermute(values, 'row', to) for to in over_x]]
  transfers between devices with their start and end apart: 25 -> 28, of which waited for: 12 -> 9; matrix products, arithmetic and copies ran while one was open for 0% -> 0% of each run, Pallas kernels for 33% -> 36%
where the time goes in v8:
time: 114 us
  Pallas kernels  42.5 us (37%)
  waiting for transfers between devices  37.4 us (33%)
  starting transfers between devices  30.8 us (27%)
  local copies, waits for them, and re-layouts  2.21 us (2%)
    pallas_call x22, Pallas kernels, call(): pl.pallas_call(kernel, out_shape=outs, grid_spec=pltpu.PrefetchScalarGrid...  42.5 us
    ppermute x2, waiting for transfers between devices, per_device(): cots[s] = lax.ppermute(cots[s - 1], 'col', ring)  16.8 us
    ppermute x3, starting transfers between devices, per_device(): right = lax.ppermute(right, 'col', [(z, z + 1) for z in range(j)])  15.3 us
    ppermute x4, waiting for transfers between devices, exchange(): others[s] = [lax.ppermute(values, 'row', to) for to in over_x]  8.08 us
    ppermute x1, waiting for transfers between devices, per_device(): cots[cols - s] = lax.ppermute(cots[(cols - s + 1) % cols], 'col', back)  7.7 us
    ppermute x4, starting transfers between devices, exchange(): others[s] = [lax.ppermute(values, 'row', to) for to in over_x]  5.13 us
    ppermute x3, waiting for transfers between devices, per_device(): ins.append(lax.ppermute(ins[-1], 'col', ring))  3.11 us
    ppermute x3, starting transfers between devices, per_device(): lax.ppermute(left, 'col', [(z, z - 1) for z in range(cols - j, cols)])  2.66 us
  transfers between devices with their start and end apart: 28, of which 9 were waited for; matrix products, arithmetic and copies ran while one was open for 0% of the time, Pallas kernels for 36%

profile of v8, /device:TPU:0, one launch (start us, length us, event | category | flops | bytes accessed | tf_op | source)
XLA Modules:
  0.0 113.9 jit_solution(312295621326844177)
XLA Ops:
  1.2 2.6 %collective-permute-start.1 = (bf16[192,1024]{1,0:T(8,128)(2,1)}, bf16[192,1024]{1,0:T(8,128)(2,1)S(1)}, u32[]{:S(2)}, u32[]{:S(2)}) collective-permute-start(bf16[192,1024]{1,0:T(8,128)(2,1)} %cot_ref), channel_id=1, source_target_pairs={{0,1},{1,2},{2,3},{3,0},{4,5},{5,6},{6,7},{7,4},{8,9},{9,10},{10,1... | collective-permute-start | bytes 1179656 | tf_op jit(solution)/shard_map/ppermute | solution.py:287
  3.8 1.5 %collective-permute-start = (bf16[192,2048]{1,0:T(8,128)(2,1)}, bf16[192,2048]{1,0:T(8,128)(2,1)S(1)}, u32[]{:S(2)}, u32[]{:S(2)}) collective-permute-start(bf16[192,2048]{1,0:T(8,128)(2,1)} %refs_0_.1), channel_id=1, source_target_pairs={{0,8},{4,12},{8,0},{12,4},{1,9},{5,13},{9,1},{13,5},{2,10},{6,14},... | collective-permute-start | bytes 2359304 | tf_op jit(solution)/shard_map/ppermute | solution.py:263
  5.3 2.2 %copy-done.1 = bf16[2048,1024]{1,0:T(8,128)(2,1)S(1)} copy-done((bf16[2048,1024]{1,0:T(8,128)(2,1)S(1)}, bf16[2048,1024]{1,0:T(8,128)(2,1)}, u32[]{:S(2)}) %copy-start.1) | copy-done | bytes 4194328
  8.2 7.6 %collective-permute-done.1.cot_ref.refs_1_ = bf16[192,1024]{1,0:T(8,128)(2,1)S(1)} collective-permute-done((bf16[192,1024]{1,0:T(8,128)(2,1)}, bf16[192,1024]{1,0:T(8,128)(2,1)S(1)}, u32[]{:S(2)}, u32[]{:S(2)}) %collective-permute-start.1) | collective-permute-done | bytes 393248 | tf_op jit(solution)/shard_map/ppermute | solution.py:287
  15.8 1.7 %collective-permute-start.6 = (bf16[192,1024]{1,0:T(8,128)(2,1)S(1)}, bf16[192,1024]{1,0:T(8,128)(2,1)S(1)}, u32[]{:S(2)}, u32[]{:S(2)}) collective-permute-start(bf16[192,1024]{1,0:T(8,128)(2,1)S(1)} %copy-done.2), channel_id=1, source_target_pairs={{0,3},{1,0},{2,1},{3,2},{4,7},{5,4},{6,5},{7,6},{8,11},{9,8},{10,9... | collective-permute-start | bytes 1179656 | tf_op jit(solution)/shard_map/ppermute | solution.py:290
  17.5 2.1 %shard_map.77 = (f32[192,1024]{1,0:T(8,128)S(1)}, bf16[192,1024]{1,0:T(8,128)(2,1)S(1)}) custom-call(s32[2]{0:T(128)S(1)} %pad_add_fusion.place_ref, bf16[192,1024]{1,0:T(8,128)(2,1)S(1)} %collective-permute-done.1.cot_ref.refs_1_, bf16[192,1024]{1,0:T(8,128)(2,1)S(1)} %collective-permute-done.2.pair_ref, bf16[1024,1024]{1,0:T(8,128)(2,1)S(1)} %shard_map.76.mine_ref, ...), custom_call_target="tpu_custom_call" | custom-call | flops 10000000 | bytes 1024 | tf_op jit(solution)/shard_map/pallas_call | solution.py:64
  19.6 7.7 %collective-permute-done.6.cot_ref.refs_3_ = bf16[192,1024]{1,0:T(8,128)(2,1)S(1)} collective-permute-done((bf16[192,1024]{1,0:T(8,128)(2,1)S(1)}, bf16[192,1024]{1,0:T(8,128)(2,1)S(1)}, u32[]{:S(2)}, u32[]{:S(2)}) %collective-permute-start.6) | collective-permute-done | bytes 393248 | tf_op jit(solution)/shard_map/ppermute | solution.py:290
  27.3 1.5 %collective-permute-start.8 = (bf16[192,1024]{1,0:T(8,128)(2,1)S(1)}, bf16[192,1024]{1,0:T(8,128)(2,1)S(1)}, u32[]{:S(2)}, u32[]{:S(2)}) collective-permute-start(bf16[192,1024]{1,0:T(8,128)(2,1)S(1)} %get-tuple-element.36), channel_id=1, source_target_pairs={{0,8},{4,12},{8,0},{12,4},{1,9},{5,13},{9,1},{13,5},{2,10},{6,14},... | collective-permute-start | bytes 1179656 | tf_op jit(solution)/shard_map/ppermute | solution.py:274
  29.3 2.1 %shard_map.79 = (f32[192,1024]{1,0:T(8,128)S(1)}, bf16[192,1024]{1,0:T(8,128)(2,1)S(1)}) custom-call(s32[2]{0:T(128)S(1)} %pad_add_fusion.place_ref, bf16[192,1024]{1,0:T(8,128)(2,1)S(1)} %collective-permute-done.6.cot_ref.refs_3_, bf16[192,1024]{1,0:T(8,128)(2,1)S(1)} %collective-permute-done.7.pair_ref, bf16[1024,1024]{1,0:T(8,128)(2,1)S(1)} %shard_map.76.mine_ref, ...), custom_call_target="tpu_custom_call" | custom-call | flops 10000000 | bytes 1024 | tf_op jit(solution)/shard_map/pallas_call | solution.py:64
  31.4 9.2 %collective-permute-done.10.cot_ref.refs_2_ = bf16[192,1024]{1,0:T(8,128)(2,1)S(1)} collective-permute-done((bf16[192,1024]{1,0:T(8,128)(2,1)S(1)}, bf16[192,1024]{1,0:T(8,128)(2,1)S(1)}, u32[]{:S(2)}, u32[]{:S(2)}) %collective-permute-start.10) | collective-permute-done | bytes 393248 | tf_op jit(solution)/shard_map/ppermute | solution.py:287
  43.7 1.5 %collective-permute-start.12 = (bf16[192,1024]{1,0:T(8,128)(2,1)S(1)}, bf16[192,1024]{1,0:T(8,128)(2,1)S(1)}, u32[]{:S(2)}, u32[]{:S(2)}) collective-permute-start(bf16[192,1024]{1,0:T(8,128)(2,1)S(1)} %get-tuple-element.40), channel_id=1, source_target_pairs={{0,8},{4,12},{8,0},{12,4},{1,9},{5,13},{9,1},{13,5},{2,10},{6,14},... | collective-permute-start | bytes 1179656 | tf_op jit(solution)/shard_map/ppermute | solution.py:274
  45.2 2.1 %shard_map.83 = (f32[192,1024]{1,0:T(8,128)S(1)}, bf16[192,1024]{1,0:T(8,128)(2,1)S(1)}) custom-call(s32[2]{0:T(128)S(1)} %pad_add_fusion.place_ref, bf16[192,1024]{1,0:T(8,128)(2,1)S(1)} %collective-permute-done.10.cot_ref.refs_2_, bf16[192,1024]{1,0:T(8,128)(2,1)S(1)} %collective-permute-done.11.pair_ref, bf16[1024,1024]{1,0:T(8,128)(2,1)S(1)} %shard_map.76.mine_ref, ...), custom_call_target="tpu_custom_call" | custom-call | flops 10000000 | bytes 1024 | tf_op jit(solution)/shard_map/pallas_call | solution.py:64
  47.3 2.1 %shard_map.82 = (f32[192,1024]{1,0:T(8,128)S(1)}, bf16[192,1024]{1,0:T(8,128)(2,1)S(1)}) custom-call(s32[2]{0:T(128)S(1)} %pad_add_fusion.place_ref, bf16[192,1024]{1,0:T(8,128)(2,1)S(1)} %shard_map.81.mine_ref.refs_5_, bf16[192,1024]{1,0:T(8,128)(2,1)S(1)} %collective-permute-done.9.theirs_ref.refs_9_, bf16[1024,2048]{1,0:T(8,128)(2,1)S(1)} %copy-done), custom_call_target="tpu_custom_call" | custom-call | flops 10000000 | bytes 1024 | tf_op jit(solution)/shard_map/pallas_call | solution.py:64
  49.4 5.4 %collective-permute-done.12.refs_0_ = bf16[192,1024]{1,0:T(8,128)(2,1)S(1)} collective-permute-done((bf16[192,1024]{1,0:T(8,128)(2,1)S(1)}, bf16[192,1024]{1,0:T(8,128)(2,1)S(1)}, u32[]{:S(2)}, u32[]{:S(2)}) %collective-permute-start.12) | collective-permute-done | bytes 393248 | tf_op jit(solution)/shard_map/ppermute | solution.py:274
  54.8 1.1 shard_map.84.mine_ref.refs_7_
  56.0 1.6 %collective-permute-start.16 = (bf16[192,1024]{1,0:T(8,128)(2,1)S(1)}, bf16[192,1024]{1,0:T(8,128)(2,1)S(1)}, u32[]{:S(2)}, u32[]{:S(2)}) collective-permute-start(bf16[192,1024]{1,0:T(8,128)(2,1)S(1)} %get-tuple-element.45), channel_id=1, source_target_pairs={{0,8},{4,12},{8,0},{12,4},{1,9},{5,13},{9,1},{13,5},{2,10},{6,14},... | collective-permute-start | bytes 1179656 | tf_op jit(solution)/shard_map/ppermute | solution.py:274
  57.8 4.2 %collective-permute-start.14 = (bf16[192,1024]{1,0:T(8,128)(2,1)S(1)}, bf16[192,1024]{1,0:T(8,128)(2,1)S(1)}, u32[]{:S(2)}, u32[]{:S(2)}) collective-permute-start(bf16[192,1024]{1,0:T(8,128)(2,1)S(1)} %get-tuple-element.49), channel_id=1, source_target_pairs={{0,1},{4,5},{8,9},{12,13},{16,17},{20,21},{24,25},{28,29}} | collective-permute-start | bytes 1179656 | tf_op jit(solution)/shard_map/ppermute | solution.py:339
  62.0 2.1 %shard_map.85 = (f32[192,1024]{1,0:T(8,128)S(1)}, bf16[192,1024]{1,0:T(8,128)(2,1)S(1)}) custom-call(s32[2]{0:T(128)S(1)} %pad_add_fusion.place_ref, bf16[192,1024]{1,0:T(8,128)(2,1)S(1)} %shard_map.84.mine_ref.refs_7_, bf16[192,1024]{1,0:T(8,128)(2,1)S(1)} %collective-permute-done.13.theirs_ref.refs_11_, bf16[1024,2048]{1,0:T(8,128)(2,1)S(1)} %copy-done), custom_call_target="tpu_custom_call" | custom-call | flops 10000000 | bytes 1024 | tf_op jit(solution)/shard_map/pallas_call | solution.py:64
  64.8 2.7 %collective-permute-done.16.refs_0_ = bf16[192,1024]{1,0:T(8,128)(2,1)S(1)} collective-permute-done((bf16[192,1024]{1,0:T(8,128)(2,1)S(1)}, bf16[192,1024]{1,0:T(8,128)(2,1)S(1)}, u32[]{:S(2)}, u32[]{:S(2)}) %collective-permute-start.16) | collective-permute-done | bytes 393248 | tf_op jit(solution)/shard_map/ppermute | solution.py:274
  67.5 1.1 shard_map.87.mine_ref.refs_6_
  68.8 2.9 %collective-permute-done.21.refs_2_ = bf16[192,1024]{1,0:T(8,128)(2,1)S(1)} collective-permute-done((bf16[192,1024]{1,0:T(8,128)(2,1)S(1)}, bf16[192,1024]{1,0:T(8,128)(2,1)S(1)}, u32[]{:S(2)}, u32[]{:S(2)}) %collective-permute-start.21) | collective-permute-done | bytes 393248 | tf_op jit(solution)/shard_map/ppermute | solution.py:319
  71.6 2.1 %shard_map.93 = (f32[192,1024]{1,0:T(8,128)S(1)}, bf16[192,1024]{1,0:T(8,128)(2,1)S(1)}) custom-call(s32[2]{0:T(128)S(1)} %pad_add_fusion.place_ref, bf16[192,1024]{1,0:T(8,128)(2,1)S(1)} %copy-done.2, bf16[192,1024]{1,0:T(8,128)(2,1)S(1)} %collective-permute-done.23.pair_ref, bf16[1024,1024]{1,0:T(8,128)(2,1)S(1)} %shard_map.76.mine_ref, ...), custom_call_target="tpu_custom_call" | custom-call | flops 10000000 | bytes 1024 | tf_op jit(solution)/shard_map/pallas_call | solution.py:64
  74.3 1.4 %collective-permute-done.14.part_ref = bf16[192,1024]{1,0:T(8,128)(2,1)S(1)} collective-permute-done((bf16[192,1024]{1,0:T(8,128)(2,1)S(1)}, bf16[192,1024]{1,0:T(8,128)(2,1)S(1)}, u32[]{:S(2)}, u32[]{:S(2)}) %collective-permute-start.14) | collective-permute-done | bytes 393248 | tf_op jit(solution)/shard_map/ppermute | solution.py:339
  76.4 2.1 %shard_map.88.refs_0_ = f32[192,1024]{1,0:T(8,128)S(1)} custom-call(s32[2]{0:T(128)S(1)} %pad_add_fusion.place_ref, bf16[192,1024]{1,0:T(8,128)(2,1)S(1)} %shard_map.87.mine_ref.refs_6_, bf16[192,1024]{1,0:T(8,128)(2,1)S(1)} %collective-permute-done.17.theirs_ref.refs_10_, bf16[1024,2048]{1,0:T(8,128)(2,1)S(1)} %copy-done), custom_call_target="tpu_custom_call" | custom-call | flops 10000000 | bytes 1024 | tf_op jit(solution)/shard_map/pallas_call | solution.py:64
  79.8 5.0 %collective-permute-start.18 = (bf16[192,1024]{1,0:T(8,128)(2,1)S(1)}, bf16[192,1024]{1,0:T(8,128)(2,1)S(1)}, u32[]{:S(2)}, u32[]{:S(2)}) collective-permute-start(bf16[192,1024]{1,0:T(8,128)(2,1)S(1)} %shard_map.89), channel_id=1, source_target_pairs={{0,1},{1,2},{4,5},{5,6},{8,9},{9,10},{12,13},{13,14},{16,17},{17,1... | collective-permute-start | bytes 1179656 | tf_op jit(solution)/shard_map/ppermute | solution.py:339
  84.8 8.8 %shard_map.92 = f32[2048,1024]{1,0:T(8,128)} custom-call(s32[2]{0:T(128)S(1)} %pad_add_fusion.place_ref, bf16[768,2048]{1,0:T(8,128)(2,1)S(1)} %shard_map.78.pre_ref, bf16[192,1024]{1,0:T(8,128)(2,1)S(1)} %copy-done.2, bf16[192,1024]{1,0:T(8,128)(2,1)S(1)} %collective-permute-done.1.cot_ref.refs_1_, ...), custom_call_target="tpu_custom_call" | custom-call | flops 100000000 | bytes 1024 | tf_op jit(solution)/shard_map/pallas_call | solution.py:64
  93.6 1.1 shard_map.94.mine_ref.refs_4_
  95.5 1.3 %collective-permute-start.27 = (bf16[192,1024]{1,0:T(8,128)(2,1)S(1)}, bf16[192,1024]{1,0:T(8,128)(2,1)S(1)}, u32[]{:S(2)}, u32[]{:S(2)}) collective-permute-start(bf16[192,1024]{1,0:T(8,128)(2,1)S(1)} %shard_map.91), channel_id=1, source_target_pairs={{1,0},{2,1},{3,2},{5,4},{6,5},{7,6},{9,8},{10,9},{11,10},{13,12},{... | collective-permute-start | bytes 1179656 | tf_op jit(solution)/shard_map/ppermute | solution.py:340
  97.4 6.1 %collective-permute-start.26 = (bf16[192,1024]{1,0:T(8,128)(2,1)S(1)}, bf16[192,1024]{1,0:T(8,128)(2,1)S(1)}, u32[]{:S(2)}, u32[]{:S(2)}) collective-permute-start(bf16[192,1024]{1,0:T(8,128)(2,1)S(1)} %shard_map.90), channel_id=1, source_target_pairs={{0,1},{1,2},{2,3},{4,5},{5,6},{6,7},{8,9},{9,10},{10,11},{12,13},{... | collective-permute-start | bytes 1179656 | tf_op jit(solution)/shard_map/ppermute | solution.py:339
  103.6 2.1 %shard_map.95.part_ref = f32[192,1024]{1,0:T(8,128)S(1)} custom-call(s32[2]{0:T(128)S(1)} %pad_add_fusion.place_ref, bf16[192,1024]{1,0:T(8,128)(2,1)S(1)} %shard_map.94.mine_ref.refs_4_, bf16[192,1024]{1,0:T(8,128)(2,1)S(1)} %collective-permute-done.25.theirs_ref.refs_8_, bf16[1024,2048]{1,0:T(8,128)(2,1)S(1)} %copy-done), custom_call_target="tpu_custom_call" | custom-call | flops 10000000 | bytes 1024 | tf_op jit(solution)/shard_map/pallas_call | solution.py:64
  105.6 6.6 %shard_map.96 = f32[1024,2048]{1,0:T(8,128)} custom-call(s32[2]{0:T(128)S(1)} %pad_add_fusion.place_ref, bf16[192,1024]{1,0:T(8,128)(2,1)S(1)} %copy-done.4, bf16[192,1024]{1,0:T(8,128)(2,1)S(1)} %collective-permute-done.20.refs_1_, bf16[192,1024]{1,0:T(8,128)(2,1)S(1)} %collective-permute-done.21.refs_2_, ...), custom_call_target="tpu_custom_call" | custom-call | flops 1000000000 | bytes 1024 | tf_op jit(solution)/shard_map/pallas_call | solution.py:64
  112.5 1.4 %shard_map.97 = bf16[192,1024]{1,0:T(8,128)(2,1)} custom-call(s32[2]{0:T(128)S(1)} %pad_add_fusion.place_ref, f32[192,1024]{1,0:T(8,128)S(1)} %shard_map.95.part_ref, bf16[192,1024]{1,0:T(8,128)(2,1)S(1)} %collective-permute-done.26.refs_0_, bf16[192,1024]{1,0:T(8,128)(2,1)S(1)} %collective-permute-done.27.refs_1_), custom_call_target="tpu_custom_call" | custom-call | flops 10000000 | bytes 1024 | tf_op jit(solution)/shard_map/pallas_call | solution.py:64
  (57 shorter events, 10.0 us)
Async XLA Ops:
  0.7 16.8 %collective-permute-start.3 = (bf16[2048,1024]{1,0:T(8,128)(2,1)}, bf16[2048,1024]{1,0:T(8,128)(2,1)S(1)}, u32[]{:S(2)}, u32[]{:S(2)}) collective-permute-start(bf16[2048,1024]{1,0:T(8,128)(2,1)} %rows_ref), channel_id=1, source_target_pairs={{0,4},{4,0},{8,12},{12,8},{1,5},{5,1},{9,13},{13,9},{2,6},{6,2},{1... | collective-permute-start | bytes 12582920 | tf_op jit(solution)/shard_map/ppermute | solution.py:264
  1.2 14.6 %collective-permute-start.1 = (bf16[192,1024]{1,0:T(8,128)(2,1)}, bf16[192,1024]{1,0:T(8,128)(2,1)S(1)}, u32[]{:S(2)}, u32[]{:S(2)}) collective-permute-start(bf16[192,1024]{1,0:T(8,128)(2,1)} %cot_ref), channel_id=1, source_target_pairs={{0,1},{1,2},{2,3},{3,0},{4,5},{5,6},{6,7},{7,4},{8,9},{9,10},{10,1... | collective-permute-start | bytes 1179656 | tf_op jit(solution)/shard_map/ppermute | solution.py:287
  3.8 25.0 %collective-permute-start = (bf16[192,2048]{1,0:T(8,128)(2,1)}, bf16[192,2048]{1,0:T(8,128)(2,1)S(1)}, u32[]{:S(2)}, u32[]{:S(2)}) collective-permute-start(bf16[192,2048]{1,0:T(8,128)(2,1)} %refs_0_.1), channel_id=1, source_target_pairs={{0,8},{4,12},{8,0},{12,4},{1,9},{5,13},{9,1},{13,5},{2,10},{6,14},... | collective-permute-start | bytes 2359304 | tf_op jit(solution)/shard_map/ppermute | solution.py:263
  7.5 8.3 %copy-start.2 = (bf16[192,1024]{1,0:T(8,128)(2,1)S(1)}, bf16[192,1024]{1,0:T(8,128)(2,1)}, u32[]{:S(2)}) copy-start(bf16[192,1024]{1,0:T(8,128)(2,1)} %cot_ref) | copy-start | bytes 1179652
  8.2 20.6 %copy-start.3 = (bf16[192,2048]{1,0:T(8,128)(2,1)S(1)}, bf16[192,2048]{1,0:T(8,128)(2,1)}, u32[]{:S(2)}) copy-start(bf16[192,2048]{1,0:T(8,128)(2,1)} %refs_0_.1) | copy-start | bytes 2359300
  15.8 1.8 %collective-permute-start.2 = (bf16[192,1024]{1,0:T(8,128)(2,1)S(1)}, bf16[192,1024]{1,0:T(8,128)(2,1)S(1)}, u32[]{:S(2)}, u32[]{:S(2)}) collective-permute-start(bf16[192,1024]{1,0:T(8,128)(2,1)S(1)} %collective-permute-done.1.cot_ref.refs_1_), channel_id=1, source_target_pairs={{0,4},{4,0},{8,12},{12,8},{1,5},{5,1},{9,13},{13,9},{2,6},{6,2},{1... | collective-permute-start | bytes 1179656 | tf_op jit(solution)/shard_map/ppermute | solution.py:297
  15.8 11.5 %collective-permute-start.6 = (bf16[192,1024]{1,0:T(8,128)(2,1)S(1)}, bf16[192,1024]{1,0:T(8,128)(2,1)S(1)}, u32[]{:S(2)}, u32[]{:S(2)}) collective-permute-start(bf16[192,1024]{1,0:T(8,128)(2,1)S(1)} %copy-done.2), channel_id=1, source_target_pairs={{0,3},{1,0},{2,1},{3,2},{4,7},{5,4},{6,5},{7,6},{8,11},{9,8},{10,9... | collective-permute-start | bytes 1179656 | tf_op jit(solution)/shard_map/ppermute | solution.py:290
  27.3 2.0 %collective-permute-start.7 = (bf16[192,1024]{1,0:T(8,128)(2,1)S(1)}, bf16[192,1024]{1,0:T(8,128)(2,1)S(1)}, u32[]{:S(2)}, u32[]{:S(2)}) collective-permute-start(bf16[192,1024]{1,0:T(8,128)(2,1)S(1)} %collective-permute-done.6.cot_ref.refs_3_), channel_id=1, source_target_pairs={{0,4},{4,0},{8,12},{12,8},{1,5},{5,1},{9,13},{13,9},{2,6},{6,2},{1... | collective-permute-start | bytes 1179656 | tf_op jit(solution)/shard_map/ppermute | solution.py:297
  27.3 13.3 %collective-permute-start.10 = (bf16[192,1024]{1,0:T(8,128)(2,1)S(1)}, bf16[192,1024]{1,0:T(8,128)(2,1)S(1)}, u32[]{:S(2)}, u32[]{:S(2)}) collective-permute-start(bf16[192,1024]{1,0:T(8,128)(2,1)S(1)} %collective-permute-done.1.cot_ref.refs_1_), channel_id=1, source_target_pairs={{0,1},{1,2},{2,3},{3,0},{4,5},{5,6},{6,7},{7,4},{8,9},{9,10},{10,1... | collective-permute-start | bytes 1179656 | tf_op jit(solution)/shard_map/ppermute | solution.py:287
  27.3 13.3 %collective-permute-start.8 = (bf16[192,1024]{1,0:T(8,128)(2,1)S(1)}, bf16[192,1024]{1,0:T(8,128)(2,1)S(1)}, u32[]{:S(2)}, u32[]{:S(2)}) collective-permute-start(bf16[192,1024]{1,0:T(8,128)(2,1)S(1)} %get-tuple-element.36), channel_id=1, source_target_pairs={{0,8},{4,12},{8,0},{12,4},{1,9},{5,13},{9,1},{13,5},{2,10},{6,14},... | collective-permute-start | bytes 1179656 | tf_op jit(solution)/shard_map/ppermute | solution.py:274
  28.8 12.5 %collective-permute-start.4 = (bf16[192,2048]{1,0:T(8,128)(2,1)S(1)}, bf16[192,2048]{1,0:T(8,128)(2,1)S(1)}, u32[]{:S(2)}, u32[]{:S(2)}) collective-permute-start(bf16[192,2048]{1,0:T(8,128)(2,1)S(1)} %copy-done.3), channel_id=1, source_target_pairs={{0,4},{4,0},{8,12},{12,8},{1,5},{5,1},{9,13},{13,9},{2,6},{6,2},{1... | collective-permute-start | bytes 2359304 | tf_op jit(solution)/shard_map/ppermute | solution.py:303
  29.0 12.2 %collective-permute-start.5 = (bf16[192,2048]{1,0:T(8,128)(2,1)S(1)}, bf16[192,2048]{1,0:T(8,128)(2,1)S(1)}, u32[]{:S(2)}, u32[]{:S(2)}) collective-permute-start(bf16[192,2048]{1,0:T(8,128)(2,1)S(1)} %collective-permute-done.refs_1_), channel_id=1, source_target_pairs={{0,4},{4,0},{8,12},{12,8},{1,5},{5,1},{9,13},{13,9},{2,6},{6,2},{1... | collective-permute-start | bytes 2359304 | tf_op jit(solution)/shard_map/ppermute | solution.py:303
  40.6 4.6 %collective-permute-start.11 = (bf16[192,1024]{1,0:T(8,128)(2,1)S(1)}, bf16[192,1024]{1,0:T(8,128)(2,1)S(1)}, u32[]{:S(2)}, u32[]{:S(2)}) collective-permute-start(bf16[192,1024]{1,0:T(8,128)(2,1)S(1)} %collective-permute-done.10.cot_ref.refs_2_), channel_id=1, source_target_pairs={{0,4},{4,0},{8,12},{12,8},{1,5},{5,1},{9,13},{13,9},{2,6},{6,2},{1... | collective-permute-start | bytes 1179656 | tf_op jit(solution)/shard_map/ppermute | solution.py:297
  41.2 4.0 %copy-start.4 = (bf16[192,1024]{1,0:T(8,128)(2,1)S(1)}, bf16[192,1024]{1,0:T(8,128)(2,1)}, u32[]{:S(2)}) copy-start(bf16[192,1024]{1,0:T(8,128)(2,1)} %refs_0_.3) | copy-start | bytes 1179652
  43.1 4.2 %copy-start = (bf16[1024,2048]{1,0:T(8,128)(2,1)S(1)}, bf16[1024,2048]{1,0:T(8,128)(2,1)}, u32[]{:S(2)}) copy-start(bf16[1024,2048]{1,0:T(8,128)(2,1)} %up_ref.7) | copy-start | bytes 12582916
  43.1 4.2 %collective-permute-start.9 = (bf16[192,1024]{1,0:T(8,128)(2,1)S(1)}, bf16[192,1024]{1,0:T(8,128)(2,1)S(1)}, u32[]{:S(2)}, u32[]{:S(2)}) collective-permute-start(bf16[192,1024]{1,0:T(8,128)(2,1)S(1)} %shard_map.81.mine_ref.refs_5_), channel_id=1, source_target_pairs={{0,4},{4,0},{8,12},{12,8},{1,5},{5,1},{9,13},{13,9},{2,6},{6,2},{1... | collective-permute-start | bytes 1179656 | tf_op jit(solution)/shard_map/ppermute | solution.py:278
  43.7 11.1 %collective-permute-start.12 = (bf16[192,1024]{1,0:T(8,128)(2,1)S(1)}, bf16[192,1024]{1,0:T(8,128)(2,1)S(1)}, u32[]{:S(2)}, u32[]{:S(2)}) collective-permute-start(bf16[192,1024]{1,0:T(8,128)(2,1)S(1)} %get-tuple-element.40), channel_id=1, source_target_pairs={{0,8},{4,12},{8,0},{12,4},{1,9},{5,13},{9,1},{13,5},{2,10},{6,14},... | collective-permute-start | bytes 1179656 | tf_op jit(solution)/shard_map/ppermute | solution.py:274
  45.2 12.6 %collective-permute-start.20 = (bf16[192,1024]{1,0:T(8,128)(2,1)S(1)}, bf16[192,1024]{1,0:T(8,128)(2,1)S(1)}, u32[]{:S(2)}, u32[]{:S(2)}) collective-permute-start(bf16[192,1024]{1,0:T(8,128)(2,1)S(1)} %copy-done.4), channel_id=1, source_target_pairs={{0,1},{1,2},{2,3},{3,0},{4,5},{5,6},{6,7},{7,4},{8,9},{9,10},{10,1... | collective-permute-start | bytes 1179656 | tf_op jit(solution)/shard_map/ppermute | solution.py:319
  55.9 6.1 %collective-permute-start.13 = (bf16[192,1024]{1,0:T(8,128)(2,1)S(1)}, bf16[192,1024]{1,0:T(8,128)(2,1)S(1)}, u32[]{:S(2)}, u32[]{:S(2)}) collective-permute-start(bf16[192,1024]{1,0:T(8,128)(2,1)S(1)} %shard_map.84.mine_ref.refs_7_), channel_id=1, source_target_pairs={{0,4},{4,0},{8,12},{12,8},{1,5},{5,1},{9,13},{13,9},{2,6},{6,2},{1... | collective-permute-start | bytes 1179656 | tf_op jit(solution)/shard_map/ppermute | solution.py:278
  56.0 11.5 %collective-permute-start.16 = (bf16[192,1024]{1,0:T(8,128)(2,1)S(1)}, bf16[192,1024]{1,0:T(8,128)(2,1)S(1)}, u32[]{:S(2)}, u32[]{:S(2)}) collective-permute-start(bf16[192,1024]{1,0:T(8,128)(2,1)S(1)} %get-tuple-element.45), channel_id=1, source_target_pairs={{0,8},{4,12},{8,0},{12,4},{1,9},{5,13},{9,1},{13,5},{2,10},{6,14},... | collective-permute-start | bytes 1179656 | tf_op jit(solution)/shard_map/ppermute | solution.py:274
  57.8 13.8 %collective-permute-start.21 = (bf16[192,1024]{1,0:T(8,128)(2,1)S(1)}, bf16[192,1024]{1,0:T(8,128)(2,1)S(1)}, u32[]{:S(2)}, u32[]{:S(2)}) collective-permute-start(bf16[192,1024]{1,0:T(8,128)(2,1)S(1)} %collective-permute-done.20.refs_1_), channel_id=1, source_target_pairs={{0,1},{1,2},{2,3},{3,0},{4,5},{5,6},{6,7},{7,4},{8,9},{9,10},{10,1... | collective-permute-start | bytes 1179656 | tf_op jit(solution)/shard_map/ppermute | solution.py:319
  57.8 13.8 %collective-permute-start.23 = (bf16[192,1024]{1,0:T(8,128)(2,1)S(1)}, bf16[192,1024]{1,0:T(8,128)(2,1)S(1)}, u32[]{:S(2)}, u32[]{:S(2)}) collective-permute-start(bf16[192,1024]{1,0:T(8,128)(2,1)S(1)} %copy-done.2), channel_id=1, source_target_pairs={{0,4},{4,0},{8,12},{12,8},{1,5},{5,1},{9,13},{13,9},{2,6},{6,2},{1... | collective-permute-start | bytes 1179656 | tf_op jit(solution)/shard_map/ppermute | solution.py:269
  57.8 17.9 %collective-permute-start.14 = (bf16[192,1024]{1,0:T(8,128)(2,1)S(1)}, bf16[192,1024]{1,0:T(8,128)(2,1)S(1)}, u32[]{:S(2)}, u32[]{:S(2)}) collective-permute-start(bf16[192,1024]{1,0:T(8,128)(2,1)S(1)} %get-tuple-element.49), channel_id=1, source_target_pairs={{0,1},{4,5},{8,9},{12,13},{16,17},{20,21},{24,25},{28,29}} | collective-permute-start | bytes 1179656 | tf_op jit(solution)/shard_map/ppermute | solution.py:339
  64.2 11.6 %collective-permute-start.15 = (bf16[192,1024]{1,0:T(8,128)(2,1)S(1)}, bf16[192,1024]{1,0:T(8,128)(2,1)S(1)}, u32[]{:S(2)}, u32[]{:S(2)}) collective-permute-start(bf16[192,1024]{1,0:T(8,128)(2,1)S(1)} %get-tuple-element.50), channel_id=1, source_target_pairs={{3,2},{7,6},{11,10},{15,14},{19,18},{23,22},{27,26},{31,30}} | collective-permute-start | bytes 1179656 | tf_op jit(solution)/shard_map/ppermute | solution.py:340
  68.7 7.7 %collective-permute-start.17 = (bf16[192,1024]{1,0:T(8,128)(2,1)S(1)}, bf16[192,1024]{1,0:T(8,128)(2,1)S(1)}, u32[]{:S(2)}, u32[]{:S(2)}) collective-permute-start(bf16[192,1024]{1,0:T(8,128)(2,1)S(1)} %shard_map.87.mine_ref.refs_6_), channel_id=1, source_target_pairs={{0,4},{4,0},{8,12},{12,8},{1,5},{5,1},{9,13},{13,9},{2,6},{6,2},{1... | collective-permute-start | bytes 1179656 | tf_op jit(solution)/shard_map/ppermute | solution.py:278
  71.6 22.0 %collective-permute-start.22 = (bf16[192,1024]{1,0:T(8,128)(2,1)S(1)}, bf16[192,1024]{1,0:T(8,128)(2,1)S(1)}, u32[]{:S(2)}, u32[]{:S(2)}) collective-permute-start(bf16[192,1024]{1,0:T(8,128)(2,1)S(1)} %collective-permute-done.21.refs_2_), channel_id=1, source_target_pairs={{0,1},{1,2},{2,3},{3,0},{4,5},{5,6},{6,7},{7,4},{8,9},{9,10},{10,1... | collective-permute-start | bytes 1179656 | tf_op jit(solution)/shard_map/ppermute | solution.py:319
  73.7 19.9 %collective-permute-start.24 = (bf16[192,1024]{1,0:T(8,128)(2,1)S(1)}, bf16[192,1024]{1,0:T(8,128)(2,1)S(1)}, u32[]{:S(2)}, u32[]{:S(2)}) collective-permute-start(bf16[192,1024]{1,0:T(8,128)(2,1)S(1)} %get-tuple-element.57), channel_id=1, source_target_pairs={{0,8},{4,12},{8,0},{12,4},{1,9},{5,13},{9,1},{13,5},{2,10},{6,14},... | collective-permute-start | bytes 1179656 | tf_op jit(solution)/shard_map/ppermute | solution.py:274
  79.1 15.7 %collective-permute-start.19 = (bf16[192,1024]{1,0:T(8,128)(2,1)S(1)}, bf16[192,1024]{1,0:T(8,128)(2,1)S(1)}, u32[]{:S(2)}, u32[]{:S(2)}) collective-permute-start(bf16[192,1024]{1,0:T(8,128)(2,1)S(1)} %shard_map.89), channel_id=1, source_target_pairs={{2,1},{3,2},{6,5},{7,6},{10,9},{11,10},{14,13},{15,14},{18,17},{19... | collective-permute-start | bytes 1179656 | tf_op jit(solution)/shard_map/ppermute | solution.py:340
  79.8 17.0 %collective-permute-start.18 = (bf16[192,1024]{1,0:T(8,128)(2,1)S(1)}, bf16[192,1024]{1,0:T(8,128)(2,1)S(1)}, u32[]{:S(2)}, u32[]{:S(2)}) collective-permute-start(bf16[192,1024]{1,0:T(8,128)(2,1)S(1)} %shard_map.89), channel_id=1, source_target_pairs={{0,1},{1,2},{4,5},{5,6},{8,9},{9,10},{12,13},{13,14},{16,17},{17,1... | collective-permute-start | bytes 1179656 | tf_op jit(solution)/shard_map/ppermute | solution.py:339
  94.8 8.8 %collective-permute-start.25 = (bf16[192,1024]{1,0:T(8,128)(2,1)S(1)}, bf16[192,1024]{1,0:T(8,128)(2,1)S(1)}, u32[]{:S(2)}, u32[]{:S(2)}) collective-permute-start(bf16[192,1024]{1,0:T(8,128)(2,1)S(1)} %shard_map.94.mine_ref.refs_4_), channel_id=1, source_target_pairs={{0,4},{4,0},{8,12},{12,8},{1,5},{5,1},{9,13},{13,9},{2,6},{6,2},{1... | collective-permute-start | bytes 1179656 | tf_op jit(solution)/shard_map/ppermute | solution.py:278
  95.5 16.8 %collective-permute-start.27 = (bf16[192,1024]{1,0:T(8,128)(2,1)S(1)}, bf16[192,1024]{1,0:T(8,128)(2,1)S(1)}, u32[]{:S(2)}, u32[]{:S(2)}) collective-permute-start(bf16[192,1024]{1,0:T(8,128)(2,1)S(1)} %shard_map.91), channel_id=1, source_target_pairs={{1,0},{2,1},{3,2},{5,4},{6,5},{7,6},{9,8},{10,9},{11,10},{13,12},{... | collective-permute-start | bytes 1179656 | tf_op jit(solution)/shard_map/ppermute | solution.py:340
  97.4 15.1 %collective-permute-start.26 = (bf16[192,1024]{1,0:T(8,128)(2,1)S(1)}, bf16[192,1024]{1,0:T(8,128)(2,1)S(1)}, u32[]{:S(2)}, u32[]{:S(2)}) collective-permute-start(bf16[192,1024]{1,0:T(8,128)(2,1)S(1)} %shard_map.90), channel_id=1, source_target_pairs={{0,1},{1,2},{2,3},{4,5},{5,6},{6,7},{8,9},{9,10},{10,11},{12,13},{... | collective-permute-start | bytes 1179656 | tf_op jit(solution)/shard_map/ppermute | solution.py:339
  (1 other events, 2.2 us)

commit v9 on v8

--- a/solution.py
+++ b/solution.py
@@ -11,7 +11,7 @@
 LAST = (((1,), (1,)), ((), ()))
 FIRST = (((0,), (0,)), ((), ()))
 MIB = 1024 * 1024
-LITTLE, SOME, MORE, MUCH, MOST = 10**7, 10**8, 10**9, 4 * 10**9, 8 * 10**9
+LITTLE, SOME, MORE, MUCH, MOST = 10**7, 10**8, 10**9, 3 * 10**9, 3 * 10**9
 
 
 def gelu_parts(values):
@@ -295,21 +295,24 @@
         s = order[i]
         arrived[s] = after(cots[s], sent[order[i - 1]] if i else down_mine)
         cot_pair = lax.ppermute(arrived[s], "row", pair)
+        if i == 1:
+            cot_pair = after(cot_pair, parts[order[0]])
         parts[s], sent[s] = hidden_call(place, cots[s], cot_pair, down_mine, down_pair)
         exchange(s)
+        cost = MUCH if i else MOST
+        parts[s], others[s] = add_call(place, parts[s], others[s], jnp.float32, cost), []
 
     for i in range(len(order)):
         hidden_next(i)
     pres = pres + [lax.ppermute(after(p, sent[1]), "row", pair) for p in pres]
-    pre_all = lay_out_call(place, pres, shifts, rows)
+    pre_all = lay_out_call(after(place, sent[order[1]]), pres, shifts, rows)
     hidden_part(0, sent[order[-1]])
     exchange(0)
-    parts[1], others[1] = add_call(after(place, sent[order[1]]), parts[1], others[1], jnp.float32, MOST), []
     shares = {}
     for s in order:
         pre_grad(s, *(shares[t][0] for t in shares), *([sent[order[2]]] if s == order[1] else []))
         if s in (1, cols - 1):
-            shares[s] = share(s)
+            shares[s] = share(s, *([parts[order[2]]] if s == order[1] else []))
     for s in order:
         if s not in shares:
             shares[s] = share(s)

time: 114 us -> 115 us (level)
  starting transfers between devices: 30.8 us -> 29.2 us
  local copies, waits for them, and re-layouts: 2.21 us -> 3.77 us
  Pallas kernels: 42.5 us -> 43.7 us
    ppermute x1, waiting for transfers between devices: 7.7 us -> 2.38 us  [per_device(): cots[cols - s] = lax.ppermute(cots[(cols - s + 1) % cols], 'col', back)]
    ppermute x3, waiting for transfers between devices: 3.11 us -> 6.84 us  [per_device(): ins.append(lax.ppermute(ins[-1], 'col', ring))]
    ppermute x2, waiting for transfers between devices: 16.8 us -> 13.4 us  [per_device(): cots[s] = lax.ppermute(cots[s - 1], 'col', ring)]
    ppermute x1, waiting for transfers between devices: 0.01 us -> 3.25 us  [per_device(): lax.ppermute(preactivation, 'row', to)]
    ppermute x4, waiting for transfers between devices: 8.08 us -> 10.3 us  [exchange(): others[s] = [lax.ppermute(values, 'row', to) for to in over_x]]
    ppermute x3, starting transfers between devices: 15.3 us -> 13.4 us  [per_device(): right = lax.ppermute(right, 'col', [(z, z + 1) for z in range(j)])]
    unnamed x10, local copies, waits for them, and re-layouts: 2.21 us -> 3.77 us
    pallas_call x22 -> x24, Pallas kernels: 42.5 us -> 43.7 us  [call(): pl.pallas_call(kernel, out_shape=outs, grid_spec=pltpu.PrefetchScalarGrid...]
  transfers between devices with their start and end apart: 28 -> 28, of which waited for: 9 -> 9; matrix products, arithmetic and copies ran while one was open for 0% -> 0% of each run, Pallas kernels for 36% -> 37%
where the time goes in v9:
time: 115 us
  Pallas kernels  43.7 us (38%)
  waiting for transfers between devices  37 us (32%)
  starting transfers between devices  29.2 us (25%)
  local copies, waits for them, and re-layouts  3.77 us (3%)
    pallas_call x24, Pallas kernels, call(): pl.pallas_call(kernel, out_shape=outs, grid_spec=pltpu.PrefetchScalarGrid...  43.7 us
    ppermute x2, waiting for transfers between devices, per_device(): cots[s] = lax.ppermute(cots[s - 1], 'col', ring)  13.4 us
    ppermute x3, starting transfers between devices, per_device(): right = lax.ppermute(right, 'col', [(z, z + 1) for z in range(j)])  13.4 us
    ppermute x4, waiting for transfers between devices, exchange(): others[s] = [lax.ppermute(values, 'row', to) for to in over_x]  10.3 us
    ppermute x3, waiting for transfers between devices, per_device(): ins.append(lax.ppermute(ins[-1], 'col', ring))  6.84 us
    ppermute x4, starting transfers between devices, exchange(): others[s] = [lax.ppermute(values, 'row', to) for to in over_x]  5.21 us
    unnamed x10, local copies, waits for them, and re-layouts  3.77 us
    ppermute x1, waiting for transfers between devices, per_device(): lax.ppermute(preactivation, 'row', to)  3.25 us
  transfers between devices with their start and end apart: 28, of which 9 were waited for; matrix products, arithmetic and copies ran while one was open for 0% of the time, Pallas kernels for 37%

profile of v9, /device:TPU:0, one launch (start us, length us, event | category | flops | bytes accessed | tf_op | source)
XLA Modules:
  0.0 114.6 jit_solution(7445720445873364866)
XLA Ops:
  1.2 2.6 %collective-permute-start = (bf16[192,1024]{1,0:T(8,128)(2,1)}, bf16[192,1024]{1,0:T(8,128)(2,1)S(1)}, u32[]{:S(2)}, u32[]{:S(2)}) collective-permute-start(bf16[192,1024]{1,0:T(8,128)(2,1)} %cot_ref), channel_id=1, source_target_pairs={{0,1},{1,2},{2,3},{3,0},{4,5},{5,6},{6,7},{7,4},{8,9},{9,10},{10,1... | collective-permute-start | bytes 1179656 | tf_op jit(solution)/shard_map/ppermute | solution.py:287
  3.8 1.5 %collective-permute-start.9 = (bf16[192,2048]{1,0:T(8,128)(2,1)}, bf16[192,2048]{1,0:T(8,128)(2,1)S(1)}, u32[]{:S(2)}, u32[]{:S(2)}) collective-permute-start(bf16[192,2048]{1,0:T(8,128)(2,1)} %refs_0_.1), channel_id=1, source_target_pairs={{0,8},{4,12},{8,0},{12,4},{1,9},{5,13},{9,1},{13,5},{2,10},{6,14},... | collective-permute-start | bytes 2359304 | tf_op jit(solution)/shard_map/ppermute | solution.py:263
  5.3 2.2 %copy-done.1 = bf16[2048,1024]{1,0:T(8,128)(2,1)S(1)} copy-done((bf16[2048,1024]{1,0:T(8,128)(2,1)S(1)}, bf16[2048,1024]{1,0:T(8,128)(2,1)}, u32[]{:S(2)}) %copy-start.1) | copy-done | bytes 4194328
  8.2 7.6 %collective-permute-done.cot_ref.refs_1_ = bf16[192,1024]{1,0:T(8,128)(2,1)S(1)} collective-permute-done((bf16[192,1024]{1,0:T(8,128)(2,1)}, bf16[192,1024]{1,0:T(8,128)(2,1)S(1)}, u32[]{:S(2)}, u32[]{:S(2)}) %collective-permute-start) | collective-permute-done | bytes 393248 | tf_op jit(solution)/shard_map/ppermute | solution.py:287
  15.8 1.7 %collective-permute-start.2 = (bf16[192,1024]{1,0:T(8,128)(2,1)S(1)}, bf16[192,1024]{1,0:T(8,128)(2,1)S(1)}, u32[]{:S(2)}, u32[]{:S(2)}) collective-permute-start(bf16[192,1024]{1,0:T(8,128)(2,1)S(1)} %copy-done.2), channel_id=1, source_target_pairs={{0,3},{1,0},{2,1},{3,2},{4,7},{5,4},{6,5},{7,6},{8,11},{9,8},{10,9... | collective-permute-start | bytes 1179656 | tf_op jit(solution)/shard_map/ppermute | solution.py:290
  17.5 2.1 %shard_map.77 = (f32[192,1024]{1,0:T(8,128)S(1)}, bf16[192,1024]{1,0:T(8,128)(2,1)S(1)}) custom-call(s32[2]{0:T(128)S(1)} %pad_add_fusion.place_ref, bf16[192,1024]{1,0:T(8,128)(2,1)S(1)} %collective-permute-done.cot_ref.refs_1_, bf16[192,1024]{1,0:T(8,128)(2,1)S(1)} %collective-permute-done.3.pair_ref, bf16[1024,1024]{1,0:T(8,128)(2,1)S(1)} %shard_map.76.mine_ref, ...), custom_call_target="tpu_custom_call" | custom-call | flops 10000000 | bytes 1024 | tf_op jit(solution)/shard_map/pallas_call | solution.py:64
  19.6 1.6 %collective-permute-start.6 = (bf16[192,1024]{1,0:T(8,128)(2,1)S(1)}, bf16[192,1024]{1,0:T(8,128)(2,1)S(1)}, u32[]{:S(2)}, u32[]{:S(2)}) collective-permute-start(bf16[192,1024]{1,0:T(8,128)(2,1)S(1)} %get-tuple-element.37), channel_id=1, source_target_pairs={{0,8},{4,12},{8,0},{12,4},{1,9},{5,13},{9,1},{13,5},{2,10},{6,14},... | collective-permute-start | bytes 1179656 | tf_op jit(solution)/shard_map/ppermute | solution.py:274
  21.2 3.2 %collective-permute-done.9.refs_1_ = bf16[192,2048]{1,0:T(8,128)(2,1)S(1)} collective-permute-done((bf16[192,2048]{1,0:T(8,128)(2,1)}, bf16[192,2048]{1,0:T(8,128)(2,1)S(1)}, u32[]{:S(2)}, u32[]{:S(2)}) %collective-permute-start.9) | collective-permute-done | bytes 786464 | tf_op jit(solution)/shard_map/ppermute | solution.py:263
  24.9 2.4 %collective-permute-done.2.cot_ref.refs_3_ = bf16[192,1024]{1,0:T(8,128)(2,1)S(1)} collective-permute-done((bf16[192,1024]{1,0:T(8,128)(2,1)S(1)}, bf16[192,1024]{1,0:T(8,128)(2,1)S(1)}, u32[]{:S(2)}, u32[]{:S(2)}) %collective-permute-start.2) | collective-permute-done | bytes 393248 | tf_op jit(solution)/shard_map/ppermute | solution.py:290
  27.3 4.8 %collective-permute-done.6.refs_0_ = bf16[192,1024]{1,0:T(8,128)(2,1)S(1)} collective-permute-done((bf16[192,1024]{1,0:T(8,128)(2,1)S(1)}, bf16[192,1024]{1,0:T(8,128)(2,1)S(1)}, u32[]{:S(2)}, u32[]{:S(2)}) %collective-permute-start.6) | collective-permute-done | bytes 393248 | tf_op jit(solution)/shard_map/ppermute | solution.py:274
  32.7 2.1 %shard_map.79 = (f32[192,1024]{1,0:T(8,128)S(1)}, bf16[192,1024]{1,0:T(8,128)(2,1)S(1)}) custom-call(s32[2]{0:T(128)S(1)} %pad_add_fusion.place_ref, bf16[192,1024]{1,0:T(8,128)(2,1)S(1)} %collective-permute-done.2.cot_ref.refs_3_, bf16[192,1024]{1,0:T(8,128)(2,1)S(1)} %collective-permute-done.5.pair_ref, bf16[1024,1024]{1,0:T(8,128)(2,1)S(1)} %shard_map.76.mine_ref, ...), custom_call_target="tpu_custom_call" | custom-call | flops 10000000 | bytes 1024 | tf_op jit(solution)/shard_map/pallas_call | solution.py:64
  34.8 5.9 %collective-permute-done.1.cot_ref.refs_2_ = bf16[192,1024]{1,0:T(8,128)(2,1)S(1)} collective-permute-done((bf16[192,1024]{1,0:T(8,128)(2,1)S(1)}, bf16[192,1024]{1,0:T(8,128)(2,1)S(1)}, u32[]{:S(2)}, u32[]{:S(2)}) %collective-permute-start.1) | collective-permute-done | bytes 393248 | tf_op jit(solution)/shard_map/ppermute | solution.py:287
  40.6 1.5 %collective-permute-start.13 = (bf16[192,1024]{1,0:T(8,128)(2,1)S(1)}, bf16[192,1024]{1,0:T(8,128)(2,1)S(1)}, u32[]{:S(2)}, u32[]{:S(2)}) collective-permute-start(bf16[192,1024]{1,0:T(8,128)(2,1)S(1)} %get-tuple-element.41), channel_id=1, source_target_pairs={{0,8},{4,12},{8,0},{12,4},{1,9},{5,13},{9,1},{13,5},{2,10},{6,14},... | collective-permute-start | bytes 1179656 | tf_op jit(solution)/shard_map/ppermute | solution.py:274
  44.3 2.1 %shard_map.80 = (f32[192,1024]{1,0:T(8,128)S(1)}, bf16[192,1024]{1,0:T(8,128)(2,1)S(1)}) custom-call(s32[2]{0:T(128)S(1)} %pad_add_fusion.place_ref, bf16[192,1024]{1,0:T(8,128)(2,1)S(1)} %collective-permute-done.1.cot_ref.refs_2_, bf16[192,1024]{1,0:T(8,128)(2,1)S(1)} %collective-permute-done.7.pair_ref, bf16[1024,1024]{1,0:T(8,128)(2,1)S(1)} %shard_map.76.mine_ref, ...), custom_call_target="tpu_custom_call" | custom-call | flops 10000000 | bytes 1024 | tf_op jit(solution)/shard_map/pallas_call | solution.py:64
  47.0 5.6 %collective-permute-done.13.refs_0_ = bf16[192,1024]{1,0:T(8,128)(2,1)S(1)} collective-permute-done((bf16[192,1024]{1,0:T(8,128)(2,1)S(1)}, bf16[192,1024]{1,0:T(8,128)(2,1)S(1)}, u32[]{:S(2)}, u32[]{:S(2)}) %collective-permute-start.13) | collective-permute-done | bytes 393248 | tf_op jit(solution)/shard_map/ppermute | solution.py:274
  53.2 1.6 %copy-done = bf16[1024,2048]{1,0:T(8,128)(2,1)S(1)} copy-done((bf16[1024,2048]{1,0:T(8,128)(2,1)S(1)}, bf16[1024,2048]{1,0:T(8,128)(2,1)}, u32[]{:S(2)}) %copy-start) | copy-done | bytes 4194328
  54.7 2.1 %shard_map.84 = (f32[192,1024]{1,0:T(8,128)S(1)}, bf16[192,1024]{1,0:T(8,128)(2,1)S(1)}) custom-call(s32[2]{0:T(128)S(1)} %pad_add_fusion.place_ref, bf16[192,1024]{1,0:T(8,128)(2,1)S(1)} %shard_map.83.mine_ref.refs_5_, bf16[192,1024]{1,0:T(8,128)(2,1)S(1)} %collective-permute-done.12.theirs_ref.refs_9_, bf16[1024,2048]{1,0:T(8,128)(2,1)S(1)} %copy-done), custom_call_target="tpu_custom_call" | custom-call | flops 10000000 | bytes 1024 | tf_op jit(solution)/shard_map/pallas_call | solution.py:64
  56.8 1.1 shard_map.86.mine_ref.refs_7_
  58.5 2.3 %collective-permute-start.15 = (bf16[192,1024]{1,0:T(8,128)(2,1)S(1)}, bf16[192,1024]{1,0:T(8,128)(2,1)S(1)}, u32[]{:S(2)}, u32[]{:S(2)}) collective-permute-start(bf16[192,1024]{1,0:T(8,128)(2,1)S(1)} %get-tuple-element.54), channel_id=1, source_target_pairs={{0,1},{4,5},{8,9},{12,13},{16,17},{20,21},{24,25},{28,29}} | collective-permute-start | bytes 1179656 | tf_op jit(solution)/shard_map/ppermute | solution.py:342
  61.5 2.1 %shard_map.87 = (f32[192,1024]{1,0:T(8,128)S(1)}, bf16[192,1024]{1,0:T(8,128)(2,1)S(1)}) custom-call(s32[2]{0:T(128)S(1)} %pad_add_fusion.place_ref, bf16[192,1024]{1,0:T(8,128)(2,1)S(1)} %shard_map.86.mine_ref.refs_7_, bf16[192,1024]{1,0:T(8,128)(2,1)S(1)} %collective-permute-done.14.theirs_ref.refs_11_, bf16[1024,2048]{1,0:T(8,128)(2,1)S(1)} %copy-done), custom_call_target="tpu_custom_call" | custom-call | flops 10000000 | bytes 1024 | tf_op jit(solution)/shard_map/pallas_call | solution.py:64
  65.4 6.8 %collective-permute-done.21.refs_2_ = bf16[192,1024]{1,0:T(8,128)(2,1)S(1)} collective-permute-done((bf16[192,1024]{1,0:T(8,128)(2,1)S(1)}, bf16[192,1024]{1,0:T(8,128)(2,1)S(1)}, u32[]{:S(2)}, u32[]{:S(2)}) %collective-permute-start.21) | collective-permute-done | bytes 393248 | tf_op jit(solution)/shard_map/ppermute | solution.py:322
  72.3 2.1 %shard_map.95 = (f32[192,1024]{1,0:T(8,128)S(1)}, bf16[192,1024]{1,0:T(8,128)(2,1)S(1)}) custom-call(s32[2]{0:T(128)S(1)} %pad_add_fusion.place_ref, bf16[192,1024]{1,0:T(8,128)(2,1)S(1)} %copy-done.2, bf16[192,1024]{1,0:T(8,128)(2,1)S(1)} %collective-permute-done.23.pair_ref, bf16[1024,1024]{1,0:T(8,128)(2,1)S(1)} %shard_map.76.mine_ref, ...), custom_call_target="tpu_custom_call" | custom-call | flops 10000000 | bytes 1024 | tf_op jit(solution)/shard_map/pallas_call | solution.py:64
  74.4 1.6 %collective-permute-start.24 = (bf16[192,1024]{1,0:T(8,128)(2,1)S(1)}, bf16[192,1024]{1,0:T(8,128)(2,1)S(1)}, u32[]{:S(2)}, u32[]{:S(2)}) collective-permute-start(bf16[192,1024]{1,0:T(8,128)(2,1)S(1)} %get-tuple-element.61), channel_id=1, source_target_pairs={{0,8},{4,12},{8,0},{12,4},{1,9},{5,13},{9,1},{13,5},{2,10},{6,14},... | collective-permute-start | bytes 1179656 | tf_op jit(solution)/shard_map/ppermute | solution.py:274
  77.0 2.1 %shard_map.90.refs_0_ = f32[192,1024]{1,0:T(8,128)S(1)} custom-call(s32[2]{0:T(128)S(1)} %pad_add_fusion.place_ref, bf16[192,1024]{1,0:T(8,128)(2,1)S(1)} %shard_map.89.mine_ref.refs_6_, bf16[192,1024]{1,0:T(8,128)(2,1)S(1)} %collective-permute-done.17.theirs_ref.refs_10_, bf16[1024,2048]{1,0:T(8,128)(2,1)S(1)} %copy-done), custom_call_target="tpu_custom_call" | custom-call | flops 10000000 | bytes 1024 | tf_op jit(solution)/shard_map/pallas_call | solution.py:64
  80.5 5.0 %collective-permute-start.18 = (bf16[192,1024]{1,0:T(8,128)(2,1)S(1)}, bf16[192,1024]{1,0:T(8,128)(2,1)S(1)}, u32[]{:S(2)}, u32[]{:S(2)}) collective-permute-start(bf16[192,1024]{1,0:T(8,128)(2,1)S(1)} %shard_map.91), channel_id=1, source_target_pairs={{0,1},{1,2},{4,5},{5,6},{8,9},{9,10},{12,13},{13,14},{16,17},{17,1... | collective-permute-start | bytes 1179656 | tf_op jit(solution)/shard_map/ppermute | solution.py:342
  85.5 8.8 %shard_map.94 = f32[2048,1024]{1,0:T(8,128)} custom-call(s32[2]{0:T(128)S(1)} %pad_add_fusion.place_ref, bf16[768,2048]{1,0:T(8,128)(2,1)S(1)} %shard_map.82.pre_ref, bf16[192,1024]{1,0:T(8,128)(2,1)S(1)} %copy-done.2, bf16[192,1024]{1,0:T(8,128)(2,1)S(1)} %collective-permute-done.cot_ref.refs_1_, ...), custom_call_target="tpu_custom_call" | custom-call | flops 100000000 | bytes 1024 | tf_op jit(solution)/shard_map/pallas_call | solution.py:64
  94.3 1.1 shard_map.96.mine_ref.refs_4_
  96.2 1.3 %collective-permute-start.27 = (bf16[192,1024]{1,0:T(8,128)(2,1)S(1)}, bf16[192,1024]{1,0:T(8,128)(2,1)S(1)}, u32[]{:S(2)}, u32[]{:S(2)}) collective-permute-start(bf16[192,1024]{1,0:T(8,128)(2,1)S(1)} %shard_map.93), channel_id=1, source_target_pairs={{1,0},{2,1},{3,2},{5,4},{6,5},{7,6},{9,8},{10,9},{11,10},{13,12},{... | collective-permute-start | bytes 1179656 | tf_op jit(solution)/shard_map/ppermute | solution.py:343
  98.1 6.1 %collective-permute-start.26 = (bf16[192,1024]{1,0:T(8,128)(2,1)S(1)}, bf16[192,1024]{1,0:T(8,128)(2,1)S(1)}, u32[]{:S(2)}, u32[]{:S(2)}) collective-permute-start(bf16[192,1024]{1,0:T(8,128)(2,1)S(1)} %shard_map.92), channel_id=1, source_target_pairs={{0,1},{1,2},{2,3},{4,5},{5,6},{6,7},{8,9},{9,10},{10,11},{12,13},{... | collective-permute-start | bytes 1179656 | tf_op jit(solution)/shard_map/ppermute | solution.py:342
  104.2 2.1 %shard_map.97.part_ref = f32[192,1024]{1,0:T(8,128)S(1)} custom-call(s32[2]{0:T(128)S(1)} %pad_add_fusion.place_ref, bf16[192,1024]{1,0:T(8,128)(2,1)S(1)} %shard_map.96.mine_ref.refs_4_, bf16[192,1024]{1,0:T(8,128)(2,1)S(1)} %collective-permute-done.25.theirs_ref.refs_8_, bf16[1024,2048]{1,0:T(8,128)(2,1)S(1)} %copy-done), custom_call_target="tpu_custom_call" | custom-call | flops 10000000 | bytes 1024 | tf_op jit(solution)/shard_map/pallas_call | solution.py:64
  106.3 6.6 %shard_map.98 = f32[1024,2048]{1,0:T(8,128)} custom-call(s32[2]{0:T(128)S(1)} %pad_add_fusion.place_ref, bf16[192,1024]{1,0:T(8,128)(2,1)S(1)} %copy-done.4, bf16[192,1024]{1,0:T(8,128)(2,1)S(1)} %collective-permute-done.20.refs_1_, bf16[192,1024]{1,0:T(8,128)(2,1)S(1)} %collective-permute-done.21.refs_2_, ...), custom_call_target="tpu_custom_call" | custom-call | flops 1000000000 | bytes 1024 | tf_op jit(solution)/shard_map/pallas_call | solution.py:64
  113.2 1.4 %shard_map.99 = bf16[192,1024]{1,0:T(8,128)(2,1)} custom-call(s32[2]{0:T(128)S(1)} %pad_add_fusion.place_ref, f32[192,1024]{1,0:T(8,128)S(1)} %shard_map.97.part_ref, bf16[192,1024]{1,0:T(8,128)(2,1)S(1)} %collective-permute-done.26.refs_0_, bf16[192,1024]{1,0:T(8,128)(2,1)S(1)} %collective-permute-done.27.refs_1_), custom_call_target="tpu_custom_call" | custom-call | flops 10000000 | bytes 1024 | tf_op jit(solution)/shard_map/pallas_call | solution.py:64
  (59 shorter events, 12.7 us)
Async XLA Ops:
  0.7 16.8 %collective-permute-start.4 = (bf16[2048,1024]{1,0:T(8,128)(2,1)}, bf16[2048,1024]{1,0:T(8,128)(2,1)S(1)}, u32[]{:S(2)}, u32[]{:S(2)}) collective-permute-start(bf16[2048,1024]{1,0:T(8,128)(2,1)} %rows_ref), channel_id=1, source_target_pairs={{0,4},{4,0},{8,12},{12,8},{1,5},{5,1},{9,13},{13,9},{2,6},{6,2},{1... | collective-permute-start | bytes 12582920 | tf_op jit(solution)/shard_map/ppermute | solution.py:264
  1.2 14.6 %collective-permute-start = (bf16[192,1024]{1,0:T(8,128)(2,1)}, bf16[192,1024]{1,0:T(8,128)(2,1)S(1)}, u32[]{:S(2)}, u32[]{:S(2)}) collective-permute-start(bf16[192,1024]{1,0:T(8,128)(2,1)} %cot_ref), channel_id=1, source_target_pairs={{0,1},{1,2},{2,3},{3,0},{4,5},{5,6},{6,7},{7,4},{8,9},{9,10},{10,1... | collective-permute-start | bytes 1179656 | tf_op jit(solution)/shard_map/ppermute | solution.py:287
  3.8 20.6 %collective-permute-start.9 = (bf16[192,2048]{1,0:T(8,128)(2,1)}, bf16[192,2048]{1,0:T(8,128)(2,1)S(1)}, u32[]{:S(2)}, u32[]{:S(2)}) collective-permute-start(bf16[192,2048]{1,0:T(8,128)(2,1)} %refs_0_.1), channel_id=1, source_target_pairs={{0,8},{4,12},{8,0},{12,4},{1,9},{5,13},{9,1},{13,5},{2,10},{6,14},... | collective-permute-start | bytes 2359304 | tf_op jit(solution)/shard_map/ppermute | solution.py:263
  7.5 8.3 %copy-start.2 = (bf16[192,1024]{1,0:T(8,128)(2,1)S(1)}, bf16[192,1024]{1,0:T(8,128)(2,1)}, u32[]{:S(2)}) copy-start(bf16[192,1024]{1,0:T(8,128)(2,1)} %cot_ref) | copy-start | bytes 1179652
  8.2 16.2 %copy-start.3 = (bf16[192,2048]{1,0:T(8,128)(2,1)S(1)}, bf16[192,2048]{1,0:T(8,128)(2,1)}, u32[]{:S(2)}) copy-start(bf16[192,2048]{1,0:T(8,128)(2,1)} %refs_0_.1) | copy-start | bytes 2359300
  15.8 1.8 %collective-permute-start.3 = (bf16[192,1024]{1,0:T(8,128)(2,1)S(1)}, bf16[192,1024]{1,0:T(8,128)(2,1)S(1)}, u32[]{:S(2)}, u32[]{:S(2)}) collective-permute-start(bf16[192,1024]{1,0:T(8,128)(2,1)S(1)} %collective-permute-done.cot_ref.refs_1_), channel_id=1, source_target_pairs={{0,4},{4,0},{8,12},{12,8},{1,5},{5,1},{9,13},{13,9},{2,6},{6,2},{1... | collective-permute-start | bytes 1179656 | tf_op jit(solution)/shard_map/ppermute | solution.py:297
  15.8 11.5 %collective-permute-start.2 = (bf16[192,1024]{1,0:T(8,128)(2,1)S(1)}, bf16[192,1024]{1,0:T(8,128)(2,1)S(1)}, u32[]{:S(2)}, u32[]{:S(2)}) collective-permute-start(bf16[192,1024]{1,0:T(8,128)(2,1)S(1)} %copy-done.2), channel_id=1, source_target_pairs={{0,3},{1,0},{2,1},{3,2},{4,7},{5,4},{6,5},{7,6},{8,11},{9,8},{10,9... | collective-permute-start | bytes 1179656 | tf_op jit(solution)/shard_map/ppermute | solution.py:290
  19.6 12.4 %collective-permute-start.6 = (bf16[192,1024]{1,0:T(8,128)(2,1)S(1)}, bf16[192,1024]{1,0:T(8,128)(2,1)S(1)}, u32[]{:S(2)}, u32[]{:S(2)}) collective-permute-start(bf16[192,1024]{1,0:T(8,128)(2,1)S(1)} %get-tuple-element.37), channel_id=1, source_target_pairs={{0,8},{4,12},{8,0},{12,4},{1,9},{5,13},{9,1},{13,5},{2,10},{6,14},... | collective-permute-start | bytes 1179656 | tf_op jit(solution)/shard_map/ppermute | solution.py:274
  24.4 17.7 %collective-permute-start.10 = (bf16[192,2048]{1,0:T(8,128)(2,1)S(1)}, bf16[192,2048]{1,0:T(8,128)(2,1)S(1)}, u32[]{:S(2)}, u32[]{:S(2)}) collective-permute-start(bf16[192,2048]{1,0:T(8,128)(2,1)S(1)} %copy-done.3), channel_id=1, source_target_pairs={{0,4},{4,0},{8,12},{12,8},{1,5},{5,1},{9,13},{13,9},{2,6},{6,2},{1... | collective-permute-start | bytes 2359304 | tf_op jit(solution)/shard_map/ppermute | solution.py:307
  24.4 17.7 %collective-permute-start.11 = (bf16[192,2048]{1,0:T(8,128)(2,1)S(1)}, bf16[192,2048]{1,0:T(8,128)(2,1)S(1)}, u32[]{:S(2)}, u32[]{:S(2)}) collective-permute-start(bf16[192,2048]{1,0:T(8,128)(2,1)S(1)} %collective-permute-done.9.refs_1_), channel_id=1, source_target_pairs={{0,4},{4,0},{8,12},{12,8},{1,5},{5,1},{9,13},{13,9},{2,6},{6,2},{1... | collective-permute-start | bytes 2359304 | tf_op jit(solution)/shard_map/ppermute | solution.py:307
  27.3 5.4 %collective-permute-start.5 = (bf16[192,1024]{1,0:T(8,128)(2,1)S(1)}, bf16[192,1024]{1,0:T(8,128)(2,1)S(1)}, u32[]{:S(2)}, u32[]{:S(2)}) collective-permute-start(bf16[192,1024]{1,0:T(8,128)(2,1)S(1)} %collective-permute-done.2.cot_ref.refs_3_), channel_id=1, source_target_pairs={{0,4},{4,0},{8,12},{12,8},{1,5},{5,1},{9,13},{13,9},{2,6},{6,2},{1... | collective-permute-start | bytes 1179656 | tf_op jit(solution)/shard_map/ppermute | solution.py:297
  27.3 13.3 %collective-permute-start.1 = (bf16[192,1024]{1,0:T(8,128)(2,1)S(1)}, bf16[192,1024]{1,0:T(8,128)(2,1)S(1)}, u32[]{:S(2)}, u32[]{:S(2)}) collective-permute-start(bf16[192,1024]{1,0:T(8,128)(2,1)S(1)} %collective-permute-done.cot_ref.refs_1_), channel_id=1, source_target_pairs={{0,1},{1,2},{2,3},{3,0},{4,5},{5,6},{6,7},{7,4},{8,9},{9,10},{10,1... | collective-permute-start | bytes 1179656 | tf_op jit(solution)/shard_map/ppermute | solution.py:287
  40.6 3.6 %copy-start.4 = (bf16[192,1024]{1,0:T(8,128)(2,1)S(1)}, bf16[192,1024]{1,0:T(8,128)(2,1)}, u32[]{:S(2)}) copy-start(bf16[192,1024]{1,0:T(8,128)(2,1)} %refs_0_.3) | copy-start | bytes 1179652
  40.6 3.6 %collective-permute-start.7 = (bf16[192,1024]{1,0:T(8,128)(2,1)S(1)}, bf16[192,1024]{1,0:T(8,128)(2,1)S(1)}, u32[]{:S(2)}, u32[]{:S(2)}) collective-permute-start(bf16[192,1024]{1,0:T(8,128)(2,1)S(1)} %collective-permute-done.1.cot_ref.refs_2_), channel_id=1, source_target_pairs={{0,4},{4,0},{8,12},{12,8},{1,5},{5,1},{9,13},{13,9},{2,6},{6,2},{1... | collective-permute-start | bytes 1179656 | tf_op jit(solution)/shard_map/ppermute | solution.py:297
  40.6 11.9 %collective-permute-start.13 = (bf16[192,1024]{1,0:T(8,128)(2,1)S(1)}, bf16[192,1024]{1,0:T(8,128)(2,1)S(1)}, u32[]{:S(2)}, u32[]{:S(2)}) collective-permute-start(bf16[192,1024]{1,0:T(8,128)(2,1)S(1)} %get-tuple-element.41), channel_id=1, source_target_pairs={{0,8},{4,12},{8,0},{12,4},{1,9},{5,13},{9,1},{13,5},{2,10},{6,14},... | collective-permute-start | bytes 1179656 | tf_op jit(solution)/shard_map/ppermute | solution.py:274
  44.0 9.2 %collective-permute-start.12 = (bf16[192,1024]{1,0:T(8,128)(2,1)S(1)}, bf16[192,1024]{1,0:T(8,128)(2,1)S(1)}, u32[]{:S(2)}, u32[]{:S(2)}) collective-permute-start(bf16[192,1024]{1,0:T(8,128)(2,1)S(1)} %shard_map.83.mine_ref.refs_5_), channel_id=1, source_target_pairs={{0,4},{4,0},{8,12},{12,8},{1,5},{5,1},{9,13},{13,9},{2,6},{6,2},{1... | collective-permute-start | bytes 1179656 | tf_op jit(solution)/shard_map/ppermute | solution.py:278
  44.3 14.2 %collective-permute-start.20 = (bf16[192,1024]{1,0:T(8,128)(2,1)S(1)}, bf16[192,1024]{1,0:T(8,128)(2,1)S(1)}, u32[]{:S(2)}, u32[]{:S(2)}) collective-permute-start(bf16[192,1024]{1,0:T(8,128)(2,1)S(1)} %copy-done.4), channel_id=1, source_target_pairs={{0,1},{1,2},{2,3},{3,0},{4,5},{5,6},{6,7},{7,4},{8,9},{9,10},{10,1... | collective-permute-start | bytes 1179656 | tf_op jit(solution)/shard_map/ppermute | solution.py:322
  46.4 14.5 %collective-permute-start.8 = (bf16[192,1024]{1,0:T(8,128)(2,1)S(1)}, bf16[192,1024]{1,0:T(8,128)(2,1)S(1)}, u32[]{:S(2)}, u32[]{:S(2)}) collective-permute-start(bf16[192,1024]{1,0:T(8,128)(2,1)S(1)} %get-tuple-element.44), channel_id=1, source_target_pairs={{0,8},{4,12},{8,0},{12,4},{1,9},{5,13},{9,1},{13,5},{2,10},{6,14},... | collective-permute-start | bytes 1179656 | tf_op jit(solution)/shard_map/ppermute | solution.py:274
  52.5 2.2 %copy-start = (bf16[1024,2048]{1,0:T(8,128)(2,1)S(1)}, bf16[1024,2048]{1,0:T(8,128)(2,1)}, u32[]{:S(2)}) copy-start(bf16[1024,2048]{1,0:T(8,128)(2,1)} %up_ref.7) | copy-start | bytes 12582916
  57.9 3.5 %collective-permute-start.14 = (bf16[192,1024]{1,0:T(8,128)(2,1)S(1)}, bf16[192,1024]{1,0:T(8,128)(2,1)S(1)}, u32[]{:S(2)}, u32[]{:S(2)}) collective-permute-start(bf16[192,1024]{1,0:T(8,128)(2,1)S(1)} %shard_map.86.mine_ref.refs_7_), channel_id=1, source_target_pairs={{0,4},{4,0},{8,12},{12,8},{1,5},{5,1},{9,13},{13,9},{2,6},{6,2},{1... | collective-permute-start | bytes 1179656 | tf_op jit(solution)/shard_map/ppermute | solution.py:278
  58.0 14.3 %collective-permute-start.23 = (bf16[192,1024]{1,0:T(8,128)(2,1)S(1)}, bf16[192,1024]{1,0:T(8,128)(2,1)S(1)}, u32[]{:S(2)}, u32[]{:S(2)}) collective-permute-start(bf16[192,1024]{1,0:T(8,128)(2,1)S(1)} %copy-done.2), channel_id=1, source_target_pairs={{0,4},{4,0},{8,12},{12,8},{1,5},{5,1},{9,13},{13,9},{2,6},{6,2},{1... | collective-permute-start | bytes 1179656 | tf_op jit(solution)/shard_map/ppermute | solution.py:269
  58.5 13.8 %collective-permute-start.21 = (bf16[192,1024]{1,0:T(8,128)(2,1)S(1)}, bf16[192,1024]{1,0:T(8,128)(2,1)S(1)}, u32[]{:S(2)}, u32[]{:S(2)}) collective-permute-start(bf16[192,1024]{1,0:T(8,128)(2,1)S(1)} %collective-permute-done.20.refs_1_), channel_id=1, source_target_pairs={{0,1},{1,2},{2,3},{3,0},{4,5},{5,6},{6,7},{7,4},{8,9},{9,10},{10,1... | collective-permute-start | bytes 1179656 | tf_op jit(solution)/shard_map/ppermute | solution.py:322
  58.5 17.9 %collective-permute-start.15 = (bf16[192,1024]{1,0:T(8,128)(2,1)S(1)}, bf16[192,1024]{1,0:T(8,128)(2,1)S(1)}, u32[]{:S(2)}, u32[]{:S(2)}) collective-permute-start(bf16[192,1024]{1,0:T(8,128)(2,1)S(1)} %get-tuple-element.54), channel_id=1, source_target_pairs={{0,1},{4,5},{8,9},{12,13},{16,17},{20,21},{24,25},{28,29}} | collective-permute-start | bytes 1179656 | tf_op jit(solution)/shard_map/ppermute | solution.py:342
  63.6 12.8 %collective-permute-start.16 = (bf16[192,1024]{1,0:T(8,128)(2,1)S(1)}, bf16[192,1024]{1,0:T(8,128)(2,1)S(1)}, u32[]{:S(2)}, u32[]{:S(2)}) collective-permute-start(bf16[192,1024]{1,0:T(8,128)(2,1)S(1)} %get-tuple-element.55), channel_id=1, source_target_pairs={{3,2},{7,6},{11,10},{15,14},{19,18},{23,22},{27,26},{31,30}} | collective-permute-start | bytes 1179656 | tf_op jit(solution)/shard_map/ppermute | solution.py:343
  65.4 11.7 %collective-permute-start.17 = (bf16[192,1024]{1,0:T(8,128)(2,1)S(1)}, bf16[192,1024]{1,0:T(8,128)(2,1)S(1)}, u32[]{:S(2)}, u32[]{:S(2)}) collective-permute-start(bf16[192,1024]{1,0:T(8,128)(2,1)S(1)} %shard_map.89.mine_ref.refs_6_), channel_id=1, source_target_pairs={{0,4},{4,0},{8,12},{12,8},{1,5},{5,1},{9,13},{13,9},{2,6},{6,2},{1... | collective-permute-start | bytes 1179656 | tf_op jit(solution)/shard_map/ppermute | solution.py:278
  72.3 22.0 %collective-permute-start.22 = (bf16[192,1024]{1,0:T(8,128)(2,1)S(1)}, bf16[192,1024]{1,0:T(8,128)(2,1)S(1)}, u32[]{:S(2)}, u32[]{:S(2)}) collective-permute-start(bf16[192,1024]{1,0:T(8,128)(2,1)S(1)} %collective-permute-done.21.refs_2_), channel_id=1, source_target_pairs={{0,1},{1,2},{2,3},{3,0},{4,5},{5,6},{6,7},{7,4},{8,9},{9,10},{10,1... | collective-permute-start | bytes 1179656 | tf_op jit(solution)/shard_map/ppermute | solution.py:322
  74.4 19.9 %collective-permute-start.24 = (bf16[192,1024]{1,0:T(8,128)(2,1)S(1)}, bf16[192,1024]{1,0:T(8,128)(2,1)S(1)}, u32[]{:S(2)}, u32[]{:S(2)}) collective-permute-start(bf16[192,1024]{1,0:T(8,128)(2,1)S(1)} %get-tuple-element.61), channel_id=1, source_target_pairs={{0,8},{4,12},{8,0},{12,4},{1,9},{5,13},{9,1},{13,5},{2,10},{6,14},... | collective-permute-start | bytes 1179656 | tf_op jit(solution)/shard_map/ppermute | solution.py:274
  79.8 15.8 %collective-permute-start.19 = (bf16[192,1024]{1,0:T(8,128)(2,1)S(1)}, bf16[192,1024]{1,0:T(8,128)(2,1)S(1)}, u32[]{:S(2)}, u32[]{:S(2)}) collective-permute-start(bf16[192,1024]{1,0:T(8,128)(2,1)S(1)} %shard_map.91), channel_id=1, source_target_pairs={{2,1},{3,2},{6,5},{7,6},{10,9},{11,10},{14,13},{15,14},{18,17},{19... | collective-permute-start | bytes 1179656 | tf_op jit(solution)/shard_map/ppermute | solution.py:343
  80.5 17.0 %collective-permute-start.18 = (bf16[192,1024]{1,0:T(8,128)(2,1)S(1)}, bf16[192,1024]{1,0:T(8,128)(2,1)S(1)}, u32[]{:S(2)}, u32[]{:S(2)}) collective-permute-start(bf16[192,1024]{1,0:T(8,128)(2,1)S(1)} %shard_map.91), channel_id=1, source_target_pairs={{0,1},{1,2},{4,5},{5,6},{8,9},{9,10},{12,13},{13,14},{16,17},{17,1... | collective-permute-start | bytes 1179656 | tf_op jit(solution)/shard_map/ppermute | solution.py:342
  95.4 8.8 %collective-permute-start.25 = (bf16[192,1024]{1,0:T(8,128)(2,1)S(1)}, bf16[192,1024]{1,0:T(8,128)(2,1)S(1)}, u32[]{:S(2)}, u32[]{:S(2)}) collective-permute-start(bf16[192,1024]{1,0:T(8,128)(2,1)S(1)} %shard_map.96.mine_ref.refs_4_), channel_id=1, source_target_pairs={{0,4},{4,0},{8,12},{12,8},{1,5},{5,1},{9,13},{13,9},{2,6},{6,2},{1... | collective-permute-start | bytes 1179656 | tf_op jit(solution)/shard_map/ppermute | solution.py:278
  96.2 16.8 %collective-permute-start.27 = (bf16[192,1024]{1,0:T(8,128)(2,1)S(1)}, bf16[192,1024]{1,0:T(8,128)(2,1)S(1)}, u32[]{:S(2)}, u32[]{:S(2)}) collective-permute-start(bf16[192,1024]{1,0:T(8,128)(2,1)S(1)} %shard_map.93), channel_id=1, source_target_pairs={{1,0},{2,1},{3,2},{5,4},{6,5},{7,6},{9,8},{10,9},{11,10},{13,12},{... | collective-permute-start | bytes 1179656 | tf_op jit(solution)/shard_map/ppermute | solution.py:343
  98.1 15.1 %collective-permute-start.26 = (bf16[192,1024]{1,0:T(8,128)(2,1)S(1)}, bf16[192,1024]{1,0:T(8,128)(2,1)S(1)}, u32[]{:S(2)}, u32[]{:S(2)}) collective-permute-start(bf16[192,1024]{1,0:T(8,128)(2,1)S(1)} %shard_map.92), channel_id=1, source_target_pairs={{0,1},{1,2},{2,3},{4,5},{5,6},{6,7},{8,9},{9,10},{10,11},{12,13},{... | collective-permute-start | bytes 1179656 | tf_op jit(solution)/shard_map/ppermute | solution.py:342
  (1 other events, 2.2 us)

commit v10 on v7

v10 whole, which is shorter than its diff:
```python
import functools
import math

import jax
import jax.numpy as jnp
from jax import lax
from jax.experimental import pallas as pl
from jax.experimental.pallas import tpu as pltpu
from jax.sharding import PartitionSpec as P

LAST = (((1,), (1,)), ((), ()))
FIRST = (((0,), (0,)), ((), ()))
MIB = 1024 * 1024
LITTLE, SOME, MORE, MUCH, MOST = 10**7, 10**8, 10**9, 3 * 10**9, 8 * 10**9


def gelu_parts(values):
    v = values.astype(jnp.float32)
    tanh_val = jnp.tanh(0.7978845608 * (v + 0.044715 * v * v * v))
    return v, tanh_val


def gelu(values):
    v, tanh_val = gelu_parts(values)
    return 0.5 * v * (1.0 + tanh_val)


def gelu_slope(values):
    v, tanh_val = gelu_parts(values)
    return 0.5 * (1.0 + tanh_val) + 0.5 * v * (1.0 - tanh_val * tanh_val) * 0.7978845608 * (
        1.0 + 3.0 * 0.044715 * v * v
    )


def dot(a, b, dims):
    return lax.dot_general(a, b, dims, preferred_element_type=jnp.float32)


def after(value, *first):
    return lax.optimization_barrier((value, *first))[0] if first else value


def tile_of(extent):
    return next(t for t in (256, 128, extent) if extent % t == 0)


def in_vmem():
    return pl.BlockSpec(memory_space=pltpu.VMEM)


def block(index, size, first=0):
    return pl.ds(pl.multiple_of(index * size + first, math.gcd(size, first)), size - first)


def block_at(place_ref, step, cols):
    return lax.rem(place_ref[0] - step + cols, cols)


def core_of(place_ref):
    return lax.rem(place_ref[1], 2)


ADD_COST = {1: MUCH, 2: MOST}


def call(kernel, place, operands, outs, mib, cost, grid=(1,), in_specs=None, out_specs=None, scratch=()):
    return pl.pallas_call(
        kernel,
        out_shape=outs,
        grid_spec=pltpu.PrefetchScalarGridSpec(
            num_scalar_prefetch=1,
            grid=grid,
            in_specs=in_specs or [in_vmem() for _ in operands],
            out_specs=out_specs or jax.tree.map(lambda _: in_vmem(), outs),
            scratch_shapes=scratch,
        ),
        compiler_params=pltpu.CompilerParams(vmem_limit_bytes=mib * MIB),
        cost_estimate=pl.CostEstimate(flops=cost, bytes_accessed=1024, transcendentals=0),
    )(place, *operands)


def take_half_kernel(place_ref, mine_ref, theirs_ref, out_ref):
    tokens, half = mine_ref.shape[0], out_ref.shape[1]
    core = core_of(place_ref)
    out_ref[block(core, tokens), :] = mine_ref[:, block(core, half)]
    out_ref[block(1 - core, tokens), :] = theirs_ref[:, block(core, half)]


def take_half_call(place, mine, theirs):
    tokens, hidden = mine.shape
    out = jax.ShapeDtypeStruct((2 * tokens, hidden // 2), jnp.bfloat16)
    return call(take_half_kernel, place, [mine, theirs], out, 8, LITTLE)


def lay_out_kernel(chips, place_ref, *refs):
    blocks, (pre_ref, act_ref) = refs[:chips], refs[chips:]
    tokens = blocks[0].shape[0]
    rows = 64 if tokens % 64 == 0 else tokens
    for i, ref in enumerate(blocks):
        owner = lax.rem(lax.div(place_ref[1], 2) - i + chips, chips)
        pre_ref[block(owner, tokens), :] = ref[...]
        for first in range(0, tokens, rows):
            here = pl.ds(pl.multiple_of(owner * tokens + first, rows), rows)
            act_ref[here, :] = gelu(ref[pl.ds(first, rows), :]).astype(jnp.bfloat16)


def lay_out_call(place, blocks):
    tokens, half = blocks[0].shape
    out = jax.ShapeDtypeStruct((tokens * len(blocks), half), jnp.bfloat16)
    kernel = functools.partial(lay_out_kernel, len(blocks))
    return call(kernel, place, blocks, [out, out], 12, 2 * MUCH)


def hidden_kernel(place_ref, cot_ref, down_ref, own_ref, other_ref):
    half = own_ref.shape[1]
    tile = tile_of(half)
    for first in range(0, half, tile):
        here = pl.ds(first, tile)
        for core, out_ref in ((1 - core_of(place_ref), other_ref), (core_of(place_ref), own_ref)):
            rows = pl.ds(pl.multiple_of(core * half + first, tile), tile)
            part = dot(cot_ref[...], down_ref[rows, :], LAST)
            out_ref[:, here] = part.astype(out_ref.dtype)


def hidden_call(place, cot, down_weight):
    shape = (cot.shape[0], down_weight.shape[0] // 2)
    outs = [jax.ShapeDtypeStruct(shape, jnp.float32), jax.ShapeDtypeStruct(shape, jnp.bfloat16)]
    return call(hidden_kernel, place, [cot, down_weight], outs, 10, LITTLE)


def pre_grad_kernel(step, cols, place_ref, pre_ref, part_ref, *refs):
    out_ref = refs[-1]
    tokens, half = part_ref.shape
    rows = 64 if tokens % 64 == 0 else tokens
    start = block_at(place_ref, step, cols) * tokens
    for first in range(0, tokens, rows):
        here = pl.ds(first, rows)
        total = part_ref[here, :]
        for other in refs[:-1]:
            total = total + other[here, :].astype(jnp.float32)
        v = pre_ref[pl.ds(pl.multiple_of(start + first, rows), rows), :]
        out_ref[here, :] = (total * gelu_slope(v)).astype(jnp.bfloat16)


def pre_grad_call(place, step, cols, pre_all, part, others):
    out = jax.ShapeDtypeStruct(part.shape, jnp.bfloat16)
    kernel = functools.partial(pre_grad_kernel, step, cols)
    return call(kernel, place, [pre_all, part, *others], out, 8, SOME)


def share_kernel(place_ref, mine_ref, theirs_ref, up_ref, out_ref, *sent_refs):
    features, half = up_ref.shape[0], mine_ref.shape[1]
    tile = tile_of(features)
    left, right = block(core_of(place_ref), half), block(1 - core_of(place_ref), half)
    for first in range(0, features, tile):
        here = pl.ds(first, tile)
        total = dot(mine_ref[...], up_ref[here, left], LAST)
        total = total + dot(theirs_ref[...], up_ref[here, right], LAST)
        out_ref[:, here] = total
        for sent in sent_refs:
            sent[:, here] = total.astype(jnp.bfloat16)


def share_call(place, mine, theirs, up_weight, first):
    shape = (mine.shape[0], up_weight.shape[0])
    outs = [jax.ShapeDtypeStruct(shape, jnp.float32)]
    outs += [jax.ShapeDtypeStruct(shape, jnp.bfloat16)] * first
    return call(share_kernel, place, [mine, theirs, up_weight], outs, 12, LITTLE)


def add_kernel(place_ref, part_ref, *refs):
    out_ref = refs[-1]
    rows = 64 if part_ref.shape[0] % 64 == 0 else part_ref.shape[0]
    for first in range(0, part_ref.shape[0], rows):
        here = pl.ds(first, rows)
        total = part_ref[here, :].astype(jnp.float32)
        for arrived in refs[:-1]:
            total = total + arrived[here, :].astype(jnp.float32)
        out_ref[here, :] = total.astype(out_ref.dtype)


def add_call(place, part, arrived, dtype, cost):
    out = jax.ShapeDtypeStruct(part.shape, dtype)
    return call(add_kernel, place, [part, *arrived], out, 4, cost)


def grad_down_kernel(blocks, scale, place_ref, mine_ref, theirs_ref, *refs):
    cot_refs, out_ref, cots = refs[:blocks], refs[-2], refs[-1]
    tokens, tile = cot_refs[0].shape[0], out_ref.shape[0]
    i, steps = pl.program_id(0), mine_ref.shape[1] // tile

    @pl.when(i == 0)
    def _():
        for s in range(blocks):
            cots[block(block_at(place_ref, s, blocks), tokens), :] = cot_refs[s][...]

    def product(act_ref, at):
        out_ref[...] = dot(act_ref[:, block(at, tile)], cots[...], FIRST) * scale

    pl.when(i < steps)(lambda: product(mine_ref, i))
    pl.when(i >= steps)(lambda: product(theirs_ref, i - steps))


def grad_down_call(place, act_mine, act_theirs, cots, scale):
    (total, half), features = act_mine.shape, cots[0].shape[1]
    tile = tile_of(half)
    steps = half // tile

    def rows(i, place):
        core = lax.rem(place[1], 2)
        return jnp.where(i < steps, core * steps + i, (1 - core) * steps + i - steps), 0

    return call(
        functools.partial(grad_down_kernel, len(cots), scale),
        place,
        [act_mine, act_theirs, *cots],
        jax.ShapeDtypeStruct((2 * half, features), jnp.float32),
        14,
        SOME,
        grid=(2 * steps,),
        out_specs=pl.BlockSpec((tile, features), rows),
        scratch=[pltpu.VMEM((total, features), jnp.bfloat16)],
    )


def grad_up_kernel(blocks, scale, place_ref, *refs):
    ins, mine, pair = (refs[i * blocks : (i + 1) * blocks] for i in range(3))
    out_ref, inputs, grads = refs[3 * blocks :]
    tokens, half = mine[0].shape
    tile = out_ref.shape[0]

    @pl.when(pl.program_id(0) == 0)
    def _():
        left, right = block(core_of(place_ref), half), block(1 - core_of(place_ref), half)
        for s in range(blocks):
            here = pl.ds(s * tokens, tokens)
            inputs[here, :] = ins[s][...]
            grads[here, left] = mine[s][...]
            grads[here, right] = pair[s][...]

    out_ref[...] = dot(inputs[:, block(pl.program_id(0), tile)], grads[...], FIRST) * scale


def grad_up_call(place, ins, mine, pair, scale):
    tokens, features = ins[0].shape
    total = tokens * len(ins)
    hidden = 2 * mine[0].shape[1]
    tile = tile_of(features)
    return call(
        functools.partial(grad_up_kernel, len(mine), scale),
        place,
        [*ins, *mine, *pair],
        jax.ShapeDtypeStruct((features, hidden), jnp.float32),
        18,
        MUCH,
        grid=(features // tile,),
        out_specs=pl.BlockSpec((tile, hidden), lambda i, place: (i, 0)),
        scratch=[
            pltpu.VMEM((total, features), jnp.bfloat16),
            pltpu.VMEM((total, hidden), jnp.bfloat16),
        ],
    )


def per_device(inputs, cotangent, preactivation, up_weight, down_weight):
    cols, rows = lax.axis_size("col"), lax.axis_size("row")
    place = jnp.stack([lax.axis_index("col"), lax.axis_index("row")]).astype(jnp.int32)
    cotangent, preactivation = after(cotangent, place), after(preactivation, place)
    ring = [(i, (i + 1) % cols) for i in range(cols)]
    pair = [(i, i ^ 1) for i in range(rows)]
    over_x = [[(i, (i + shift) % rows) for i in range(rows)] for shift in range(2, rows, 2)]
    scale = 1.0 / math.sqrt(cotangent.shape[0] * cols)
    last = cols - 1

    pre = take_half_call(place, preactivation, lax.ppermute(preactivation, "row", pair))
    pres = [pre] + [lax.ppermute(pre, "row", to) for to in over_x]
    parts, sent, others, mine, theirs = ([None] * cols for _ in range(5))

    def hidden_part(s, *first):
        own, other = hidden_call(after(place, *first), cots[s], down_weight)
        arrived = lax.ppermute(other, "row", pair)
        sent[s] = add_call(place, own, [arrived], jnp.bfloat16, LITTLE)
        parts[s] = own, arrived

    def exchange(s, *first):
        values = after(sent[s], *first)
        others[s] = [lax.ppermute(values, "row", to) for to in over_x]

    def pre_grad(s, *first):
        own, arrived = parts[s]
        total = add_call(after(place, *first), own, [arrived, *others[s]], jnp.float32, ADD_COST.get(s, MUCH))
        mine[s] = pre_grad_call(place, s, cols, pre_all, total, [])
        theirs[s] = lax.ppermute(mine[s], "row", pair)

    def share(s, *first):
        return share_call(after(place, *first), mine[s], theirs[s], up_weight, s == 1)

    cots = [cotangent]
    hidden_part(0)
    for s in range(1, cols):
        arriving = lax.ppermute(cots[s - 1], "col", ring)
        cots.append(after(arriving, sent[s - 1]) if s > 1 else after(arriving, pre, parts[0][0]))
        if s < last:
            hidden_part(s)
            exchange(s)
    ins = [inputs, lax.ppermute(after(inputs, cots[1]), "col", ring)]
    pre_all, act = lay_out_call(place, pres)
    act_theirs = lax.ppermute(act, "row", pair)

    pre_grad(1, pre_all)
    sums = share(1)[1]
    cots[last] = after(cots[last], sums)
    hidden_part(last, sums)
    exchange(last)
    exchange(0, sent[last])
    for s in range(2, cols):
        arrived = lax.ppermute(sums, "col", ring)
        ins.append(lax.ppermute(after(ins[-1], sums), "col", ring))
        pre_grad(s, *([late] if s > 2 else [ins[1]]))
        first = []
        if s == last:
            grad_down = grad_down_call(
                after(place, mine[s], *ins[2:s]), act, act_theirs, cots, scale
            )
            pre_grad(0, grad_down)
            first = [grad_down]
        if s == 2:
            arrived = add_call(place, arrived, [], jnp.float32, MUCH)
        part = share(s, *first)[0]
        sums = late = add_call(place, part, [arrived], jnp.bfloat16, LITTLE)
    arrived = lax.ppermute(sums, "col", ring)
    part = share(0, sums)[0]
    grad_up = grad_up_call(after(place, part), ins, mine, theirs, scale)
    sums = add_call(after(place, grad_up), part, [arrived], jnp.bfloat16, LITTLE)
    return (sums, grad_up, grad_down)


def solution(mesh):
    placed = (
        P(("groups", "col"), "row"),
        P(("groups", "col"), "row"),
        P(("groups", "row"), "col"),
        P("row", "col"),
        P("col", "row"),
    )
    return jax.shard_map(
        per_device,
        mesh=mesh,
        in_specs=placed,
        out_specs=(
            P(("groups", "col"), "row"),
            P(("groups", "row"), "col"),
            P(("groups", "col"), "row"),
        ),
        check_vma=False,
    )
```

time: 124 us -> 105 us (0.85)
  waiting for transfers between devices: 59.1 us -> 36.7 us
  Pallas kernels: 41.7 us -> 46.6 us
  starting transfers between devices: 18.2 us -> 16.4 us
    ppermute x3, waiting for transfers between devices: 19.6 us -> 7.19 us  [per_device(): arrived = lax.ppermute(sums, 'col', ring)]
    pallas_call x16 -> x28, Pallas kernels: 38.3 us -> 46.6 us  [call(): pl.pallas_call(kernel, out_shape=outs, grid_spec=pltpu.PrefetchScalarGrid...]
    ppermute x4, waiting for transfers between devices: 5.25 us -> 0.01 us  [exchange(): others[s] = [lax.ppermute(values, 'row', to) for to in over_x]]
    ppermute x1, waiting for transfers between devices: 5.04 us -> 0.01 us  [per_device(): lax.ppermute(preactivation, 'row', pair)]
    pallas_call x3 -> x0, Pallas kernels: 3.41 us -> none  [go_on_call(): pl.pallas_call(go_on_kernel, out_shape=jax.ShapeDtypeStruct(place.shape,...]
    ppermute x12 -> x11, starting transfers between devices: 6.9 us -> 4.71 us  [the longest x3 2.7 us: per_device(): arriving = lax.ppermute(cots[s - 1], 'col', ring)]
    ppermute x4, starting transfers between devices: 5.46 us -> 6.8 us  [exchange(): others[s] = [lax.ppermute(values, 'row', to) for to in over_x]]
    unnamed x12 -> x14, local copies, waits for them, and re-layouts: 3.34 us -> 4.34 us
  transfers between devices with their start and end apart: 25 -> 24, of which waited for: 13 -> 9; matrix products, arithmetic and copies ran while one was open for 0% -> 0% of each run, Pallas kernels for 31% -> 43%
where the time goes in v10:
time: 105 us
  Pallas kernels  46.6 us (44%)
  waiting for transfers between devices  36.7 us (35%)
  starting transfers between devices  16.4 us (16%)
  local copies, waits for them, and re-layouts  4.34 us (4%)
    pallas_call x28, Pallas kernels, call(): pl.pallas_call(kernel, out_shape=outs, grid_spec=pltpu.PrefetchScalarGrid...  46.6 us
    ppermute x3, waiting for transfers between devices, per_device(): arriving = lax.ppermute(cots[s - 1], 'col', ring)  20 us
    ppermute x2, waiting for transfers between devices, per_device(): ins.append(lax.ppermute(after(ins[-1], sums), 'col', ring))  9.03 us
    ppermute x3, waiting for transfers between devices, per_device(): arrived = lax.ppermute(sums, 'col', ring)  7.19 us
    ppermute x4, starting transfers between devices, exchange(): others[s] = [lax.ppermute(values, 'row', to) for to in over_x]  6.8 us
    unnamed x14, local copies, waits for them, and re-layouts  4.34 us
    ppermute x3, starting transfers between devices, per_device(): arriving = lax.ppermute(cots[s - 1], 'col', ring)  2.7 us
    ppermute x1, starting transfers between devices, per_device(): pres = [pre] + [lax.ppermute(pre, 'row', to) for to in over_x]  2.4 us
  transfers between devices with their start and end apart: 24, of which 9 were waited for; matrix products, arithmetic and copies ran while one was open for 0% of the time, Pallas kernels for 43%

profile of v10, /device:TPU:0, one launch (start us, length us, event | category | flops | bytes accessed | tf_op | source)
XLA Modules:
  0.0 105.0 jit_solution(18307250896578486612)
XLA Ops:
  1.2 2.6 %collective-permute-start.2 = (bf16[192,1024]{1,0:T(8,128)(2,1)}, bf16[192,1024]{1,0:T(8,128)(2,1)S(1)}, u32[]{:S(2)}, u32[]{:S(2)}) collective-permute-start(bf16[192,1024]{1,0:T(8,128)(2,1)} %refs_0_.1), channel_id=1, source_target_pairs={{0,1},{1,2},{2,3},{3,0},{4,5},{5,6},{6,7},{7,4},{8,9},{9,10},{10,1... | collective-permute-start | bytes 1179656 | tf_op jit(solution)/shard_map/ppermute | solution.py:301
  3.8 1.1 %copy-done.5 = bf16[192,2048]{1,0:T(8,128)(2,1)S(1)} copy-done((bf16[192,2048]{1,0:T(8,128)(2,1)S(1)}, bf16[192,2048]{1,0:T(8,128)(2,1)}, u32[]{:S(2)}) %copy-start.5) | copy-done | bytes 786456
  5.6 2.4 %collective-permute-start.1 = (bf16[384,1024]{1,0:T(8,128)(2,1)S(1)}, bf16[384,1024]{1,0:T(8,128)(2,1)S(1)}, u32[]{:S(2)}, u32[]{:S(2)}) collective-permute-start(bf16[384,1024]{1,0:T(8,128)(2,1)S(1)} %shard_map.76.refs_0_), channel_id=1, source_target_pairs={{0,8},{4,12},{8,0},{12,4},{1,9},{5,13},{9,1},{13,5},{2,10},{6,14},... | collective-permute-start | bytes 2359304 | tf_op jit(solution)/shard_map/ppermute | solution.py:276
  8.0 2.2 %copy-done = bf16[2048,1024]{1,0:T(8,128)(2,1)S(1)} copy-done((bf16[2048,1024]{1,0:T(8,128)(2,1)S(1)}, bf16[2048,1024]{1,0:T(8,128)(2,1)}, u32[]{:S(2)}) %copy-start) | copy-done | bytes 4194328
  10.1 1.0 copy-done.3
  11.1 2.1 %shard_map.78 = (f32[192,1024]{1,0:T(8,128)S(1)}, bf16[192,1024]{1,0:T(8,128)(2,1)S(1)}) custom-call(s32[2]{0:T(128)S(1)} %pad_add_fusion.place_ref, bf16[192,1024]{1,0:T(8,128)(2,1)S(1)} %copy-done.3, bf16[2048,1024]{1,0:T(8,128)(2,1)S(1)} %copy-done), custom_call_target="tpu_custom_call" | custom-call | flops 10000000 | bytes 1024 | tf_op jit(solution)/shard_map/pallas_call | solution.py:67
  13.2 2.5 %collective-permute-done.2.cot_ref.refs_1_ = bf16[192,1024]{1,0:T(8,128)(2,1)S(1)} collective-permute-done((bf16[192,1024]{1,0:T(8,128)(2,1)}, bf16[192,1024]{1,0:T(8,128)(2,1)S(1)}, u32[]{:S(2)}, u32[]{:S(2)}) %collective-permute-start.2) | collective-permute-done | bytes 393248 | tf_op jit(solution)/shard_map/ppermute | solution.py:301
  15.8 2.1 %shard_map.79 = (f32[192,1024]{1,0:T(8,128)S(1)}, bf16[192,1024]{1,0:T(8,128)(2,1)S(1)}) custom-call(s32[2]{0:T(128)S(1)} %pad_add_fusion.place_ref, bf16[192,1024]{1,0:T(8,128)(2,1)S(1)} %collective-permute-done.2.cot_ref.refs_1_, bf16[2048,1024]{1,0:T(8,128)(2,1)S(1)} %copy-done.1), custom_call_target="tpu_custom_call" | custom-call | flops 10000000 | bytes 1024 | tf_op jit(solution)/shard_map/pallas_call | solution.py:67
  18.0 1.3 %collective-permute-start.3 = (bf16[192,1024]{1,0:T(8,128)(2,1)S(1)}, bf16[192,1024]{1,0:T(8,128)(2,1)S(1)}, u32[]{:S(2)}, u32[]{:S(2)}) collective-permute-start(bf16[192,1024]{1,0:T(8,128)(2,1)S(1)} %copy-done.6), channel_id=1, source_target_pairs={{0,1},{1,2},{2,3},{3,0},{4,5},{5,6},{6,7},{7,4},{8,9},{9,10},{10,1... | collective-permute-start | bytes 1179656 | tf_op jit(solution)/shard_map/ppermute | solution.py:306
  20.2 1.6 %collective-permute-start.9 = (bf16[192,1024]{1,0:T(8,128)(2,1)S(1)}, bf16[192,1024]{1,0:T(8,128)(2,1)S(1)}, u32[]{:S(2)}, u32[]{:S(2)}) collective-permute-start(bf16[192,1024]{1,0:T(8,128)(2,1)S(1)} %shard_map.80), channel_id=1, source_target_pairs={{0,8},{4,12},{8,0},{12,4},{1,9},{5,13},{9,1},{13,5},{2,10},{6,14},... | collective-permute-start | bytes 1179656 | tf_op jit(solution)/shard_map/ppermute | solution.py:287
  21.8 9.9 %collective-permute-done.4.cot_ref.refs_2_ = bf16[192,1024]{1,0:T(8,128)(2,1)S(1)} collective-permute-done((bf16[192,1024]{1,0:T(8,128)(2,1)S(1)}, bf16[192,1024]{1,0:T(8,128)(2,1)S(1)}, u32[]{:S(2)}, u32[]{:S(2)}) %collective-permute-start.4) | collective-permute-done | bytes 393248 | tf_op jit(solution)/shard_map/ppermute | solution.py:301
  31.7 2.1 %shard_map.81 = (f32[192,1024]{1,0:T(8,128)S(1)}, bf16[192,1024]{1,0:T(8,128)(2,1)S(1)}) custom-call(s32[2]{0:T(128)S(1)} %pad_add_fusion.place_ref, bf16[192,1024]{1,0:T(8,128)(2,1)S(1)} %collective-permute-done.4.cot_ref.refs_2_, bf16[2048,1024]{1,0:T(8,128)(2,1)S(1)} %copy-done.1), custom_call_target="tpu_custom_call" | custom-call | flops 10000000 | bytes 1024 | tf_op jit(solution)/shard_map/pallas_call | solution.py:67
  33.9 1.7 %shard_map.77 = (bf16[768,1024]{1,0:T(8,128)(2,1)S(1)}, bf16[768,1024]{1,0:T(8,128)(2,1)S(1)}) custom-call(s32[2]{0:T(128)S(1)} %pad_add_fusion.place_ref, bf16[384,1024]{1,0:T(8,128)(2,1)S(1)} %shard_map.76.refs_0_, bf16[384,1024]{1,0:T(8,128)(2,1)S(1)} %collective-permute-done.1.refs_1_), custom_call_target="tpu_custom_call" | custom-call | flops 6000000000 | bytes 1024 | tf_op jit(solution)/shard_map/pallas_call | solution.py:67
  36.2 1.1 %shard_map.87.mine_ref.refs_5_ = bf16[192,1024]{1,0:T(8,128)(2,1)S(1)} custom-call(s32[2]{0:T(128)S(1)} %pad_add_fusion.place_ref, bf16[768,1024]{1,0:T(8,128)(2,1)S(1)} %get-tuple-element.34.pre_ref, f32[192,1024]{1,0:T(8,128)S(1)} %shard_map.86.part_ref), custom_call_target="tpu_custom_call" | custom-call | flops 100000000 | bytes 1024 | tf_op jit(solution)/shard_map/pallas_call | solution.py:67
  38.4 1.6 %collective-permute-start.7 = (bf16[192,1024]{1,0:T(8,128)(2,1)S(1)}, bf16[192,1024]{1,0:T(8,128)(2,1)S(1)}, u32[]{:S(2)}, u32[]{:S(2)}) collective-permute-start(bf16[192,1024]{1,0:T(8,128)(2,1)S(1)} %shard_map.82), channel_id=1, source_target_pairs={{0,8},{4,12},{8,0},{12,4},{1,9},{5,13},{9,1},{13,5},{2,10},{6,14},... | collective-permute-start | bytes 1179656 | tf_op jit(solution)/shard_map/ppermute | solution.py:287
  40.5 7.6 %collective-permute-done.12.cot_ref.refs_3_ = bf16[192,1024]{1,0:T(8,128)(2,1)S(1)} collective-permute-done((bf16[192,1024]{1,0:T(8,128)(2,1)S(1)}, bf16[192,1024]{1,0:T(8,128)(2,1)S(1)}, u32[]{:S(2)}, u32[]{:S(2)}) %collective-permute-start.12) | collective-permute-done | bytes 393248 | tf_op jit(solution)/shard_map/ppermute | solution.py:301
  48.1 3.0 %shard_map.88 = (f32[192,1024]{1,0:T(8,128)}, bf16[192,1024]{1,0:T(8,128)(2,1)S(1)}) custom-call(s32[2]{0:T(128)S(1)} %pad_add_fusion.place_ref, bf16[192,1024]{1,0:T(8,128)(2,1)S(1)} %shard_map.87.mine_ref.refs_5_, bf16[192,1024]{1,0:T(8,128)(2,1)S(1)} %collective-permute-done.10.theirs_ref.refs_9_, bf16[1024,2048]{1,0:T(8,128)(2,1)S(1)} %copy-done.2), custom_call_target="tpu_custom_call" | custom-call | flops 10000000 | bytes 1024 | tf_op jit(solution)/shard_map/pallas_call | solution.py:67
  51.1 2.1 %shard_map.91 = (f32[192,1024]{1,0:T(8,128)S(1)}, bf16[192,1024]{1,0:T(8,128)(2,1)S(1)}) custom-call(s32[2]{0:T(128)S(1)} %pad_add_fusion.place_ref, bf16[192,1024]{1,0:T(8,128)(2,1)S(1)} %collective-permute-done.12.cot_ref.refs_3_, bf16[2048,1024]{1,0:T(8,128)(2,1)S(1)} %copy-done.1), custom_call_target="tpu_custom_call" | custom-call | flops 10000000 | bytes 1024 | tf_op jit(solution)/shard_map/pallas_call | solution.py:67
  53.9 1.1 %shard_map.84.mine_ref.refs_6_ = bf16[192,1024]{1,0:T(8,128)(2,1)S(1)} custom-call(s32[2]{0:T(128)S(1)} %pad_add_fusion.place_ref, bf16[768,1024]{1,0:T(8,128)(2,1)S(1)} %get-tuple-element.34.pre_ref, f32[192,1024]{1,0:T(8,128)S(1)} %shard_map.83.part_ref), custom_call_target="tpu_custom_call" | custom-call | flops 100000000 | bytes 1024 | tf_op jit(solution)/shard_map/pallas_call | solution.py:67
  56.1 1.6 %collective-permute-start.14 = (bf16[192,1024]{1,0:T(8,128)(2,1)S(1)}, bf16[192,1024]{1,0:T(8,128)(2,1)S(1)}, u32[]{:S(2)}, u32[]{:S(2)}) collective-permute-start(bf16[192,1024]{1,0:T(8,128)(2,1)S(1)} %shard_map.92), channel_id=1, source_target_pairs={{0,8},{4,12},{8,0},{12,4},{1,9},{5,13},{9,1},{13,5},{2,10},{6,14},... | collective-permute-start | bytes 1179656 | tf_op jit(solution)/shard_map/ppermute | solution.py:287
  58.4 5.9 %collective-permute-done.11.part_ref = bf16[192,1024]{1,0:T(8,128)(2,1)S(1)} collective-permute-done((bf16[192,1024]{1,0:T(8,128)(2,1)S(1)}, bf16[192,1024]{1,0:T(8,128)(2,1)S(1)}, u32[]{:S(2)}, u32[]{:S(2)}) %collective-permute-start.11) | collective-permute-done | bytes 393248 | tf_op jit(solution)/shard_map/ppermute | solution.py:317
  64.2 2.1 %collective-permute-start.20 = (bf16[192,1024]{1,0:T(8,128)(2,1)S(1)}, bf16[192,1024]{1,0:T(8,128)(2,1)S(1)}, u32[]{:S(2)}, u32[]{:S(2)}) collective-permute-start(bf16[192,1024]{1,0:T(8,128)(2,1)S(1)} %shard_map.98), channel_id=1, source_target_pairs={{0,8},{4,12},{8,0},{12,4},{1,9},{5,13},{9,1},{13,5},{2,10},{6,14},... | collective-permute-start | bytes 1179656 | tf_op jit(solution)/shard_map/ppermute | solution.py:287
  67.0 2.1 %shard_map.85.part_ref = f32[192,1024]{1,0:T(8,128)S(1)} custom-call(s32[2]{0:T(128)S(1)} %pad_add_fusion.place_ref, bf16[192,1024]{1,0:T(8,128)(2,1)S(1)} %shard_map.84.mine_ref.refs_6_, bf16[192,1024]{1,0:T(8,128)(2,1)S(1)} %collective-permute-done.8.theirs_ref.refs_10_, bf16[1024,2048]{1,0:T(8,128)(2,1)S(1)} %copy-done.2), custom_call_target="tpu_custom_call" | custom-call | flops 10000000 | bytes 1024 | tf_op jit(solution)/shard_map/pallas_call | solution.py:67
  70.6 1.1 %shard_map.94.mine_ref.refs_7_ = bf16[192,1024]{1,0:T(8,128)(2,1)S(1)} custom-call(s32[2]{0:T(128)S(1)} %pad_add_fusion.place_ref, bf16[768,1024]{1,0:T(8,128)(2,1)S(1)} %get-tuple-element.34.pre_ref, f32[192,1024]{1,0:T(8,128)S(1)} %shard_map.93.part_ref), custom_call_target="tpu_custom_call" | custom-call | flops 100000000 | bytes 1024 | tf_op jit(solution)/shard_map/pallas_call | solution.py:67
  72.4 7.7 %shard_map.95 = f32[2048,1024]{1,0:T(8,128)} custom-call(s32[2]{0:T(128)S(1)} %pad_add_fusion.place_ref, bf16[768,1024]{1,0:T(8,128)(2,1)S(1)} %get-tuple-element.55.mine_ref, bf16[768,1024]{1,0:T(8,128)(2,1)S(1)} %collective-permute-done.16.theirs_ref, bf16[192,1024]{1,0:T(8,128)(2,1)S(1)} %copy-done.4, ...), custom_call_target="tpu_custom_call" | custom-call | flops 100000000 | bytes 1024 | tf_op jit(solution)/shard_map/pallas_call | solution.py:67
  80.8 1.1 %shard_map.100.mine_ref.refs_4_ = bf16[192,1024]{1,0:T(8,128)(2,1)S(1)} custom-call(s32[2]{0:T(128)S(1)} %pad_add_fusion.place_ref, bf16[768,1024]{1,0:T(8,128)(2,1)S(1)} %get-tuple-element.34.pre_ref, f32[192,1024]{1,0:T(8,128)S(1)} %shard_map.99.part_ref), custom_call_target="tpu_custom_call" | custom-call | flops 100000000 | bytes 1024 | tf_op jit(solution)/shard_map/pallas_call | solution.py:67
  82.0 2.1 %shard_map.96.part_ref = f32[192,1024]{1,0:T(8,128)S(1)} custom-call(s32[2]{0:T(128)S(1)} %pad_add_fusion.place_ref, bf16[192,1024]{1,0:T(8,128)(2,1)S(1)} %shard_map.94.mine_ref.refs_7_, bf16[192,1024]{1,0:T(8,128)(2,1)S(1)} %collective-permute-done.17.theirs_ref.refs_11_, bf16[1024,2048]{1,0:T(8,128)(2,1)S(1)} %copy-done.2), custom_call_target="tpu_custom_call" | custom-call | flops 10000000 | bytes 1024 | tf_op jit(solution)/shard_map/pallas_call | solution.py:67
  85.2 2.1 %shard_map.101.part_ref = f32[192,1024]{1,0:T(8,128)S(1)} custom-call(s32[2]{0:T(128)S(1)} %pad_add_fusion.place_ref, bf16[192,1024]{1,0:T(8,128)(2,1)S(1)} %shard_map.100.mine_ref.refs_4_, bf16[192,1024]{1,0:T(8,128)(2,1)S(1)} %collective-permute-done.21.theirs_ref.refs_8_, bf16[1024,2048]{1,0:T(8,128)(2,1)S(1)} %copy-done.2), custom_call_target="tpu_custom_call" | custom-call | flops 10000000 | bytes 1024 | tf_op jit(solution)/shard_map/pallas_call | solution.py:67
  87.3 8.4 %collective-permute-done.22.refs_3_ = bf16[192,1024]{1,0:T(8,128)(2,1)S(1)} collective-permute-done((bf16[192,1024]{1,0:T(8,128)(2,1)S(1)}, bf16[192,1024]{1,0:T(8,128)(2,1)S(1)}, u32[]{:S(2)}, u32[]{:S(2)}) %collective-permute-start.22) | collective-permute-done | bytes 393248 | tf_op jit(solution)/shard_map/ppermute | solution.py:318
  95.7 6.7 %shard_map.102 = f32[1024,2048]{1,0:T(8,128)} custom-call(s32[2]{0:T(128)S(1)} %pad_add_fusion.place_ref, bf16[192,1024]{1,0:T(8,128)(2,1)S(1)} %copy-done.6, bf16[192,1024]{1,0:T(8,128)(2,1)S(1)} %collective-permute-done.3.refs_1_, bf16[192,1024]{1,0:T(8,128)(2,1)S(1)} %collective-permute-done.15.refs_2_, ...), custom_call_target="tpu_custom_call" | custom-call | flops 3000000000 | bytes 1024 | tf_op jit(solution)/shard_map/pallas_call | solution.py:67
  102.4 1.3 %collective-permute-done.23.refs_0_ = bf16[192,1024]{1,0:T(8,128)(2,1)S(1)} collective-permute-done((bf16[192,1024]{1,0:T(8,128)(2,1)S(1)}, bf16[192,1024]{1,0:T(8,128)(2,1)S(1)}, u32[]{:S(2)}, u32[]{:S(2)}) %collective-permute-start.23) | collective-permute-done | bytes 393248 | tf_op jit(solution)/shard_map/ppermute | solution.py:331
  103.7 1.4 %shard_map.103 = bf16[192,1024]{1,0:T(8,128)(2,1)} custom-call(s32[2]{0:T(128)S(1)} %pad_add_fusion.place_ref, f32[192,1024]{1,0:T(8,128)S(1)} %shard_map.101.part_ref, bf16[192,1024]{1,0:T(8,128)(2,1)S(1)} %collective-permute-done.23.refs_0_), custom_call_target="tpu_custom_call" | custom-call | flops 10000000 | bytes 1024 | tf_op jit(solution)/shard_map/pallas_call | solution.py:67
  (59 shorter events, 11.9 us)
Async XLA Ops:
  0.7 3.1 %collective-permute-start = (bf16[192,2048]{1,0:T(8,128)(2,1)}, bf16[192,2048]{1,0:T(8,128)(2,1)S(1)}, u32[]{:S(2)}, u32[]{:S(2)}) collective-permute-start(bf16[192,2048]{1,0:T(8,128)(2,1)} %mine_ref), channel_id=1, source_target_pairs={{0,4},{4,0},{8,12},{12,8},{1,5},{5,1},{9,13},{13,9},{2,6},{6,2},{1... | collective-permute-start | bytes 2359304 | tf_op jit(solution)/shard_map/ppermute | solution.py:275
  1.2 14.6 %collective-permute-start.2 = (bf16[192,1024]{1,0:T(8,128)(2,1)}, bf16[192,1024]{1,0:T(8,128)(2,1)S(1)}, u32[]{:S(2)}, u32[]{:S(2)}) collective-permute-start(bf16[192,1024]{1,0:T(8,128)(2,1)} %refs_0_.1), channel_id=1, source_target_pairs={{0,1},{1,2},{2,3},{3,0},{4,5},{5,6},{6,7},{7,4},{8,9},{9,10},{10,1... | collective-permute-start | bytes 1179656 | tf_op jit(solution)/shard_map/ppermute | solution.py:301
  3.8 1.1 %copy-start.5 = (bf16[192,2048]{1,0:T(8,128)(2,1)S(1)}, bf16[192,2048]{1,0:T(8,128)(2,1)}, u32[]{:S(2)}) copy-start(bf16[192,2048]{1,0:T(8,128)(2,1)} %mine_ref) | copy-start | bytes 2359300
  5.6 28.3 %collective-permute-start.1 = (bf16[384,1024]{1,0:T(8,128)(2,1)S(1)}, bf16[384,1024]{1,0:T(8,128)(2,1)S(1)}, u32[]{:S(2)}, u32[]{:S(2)}) collective-permute-start(bf16[384,1024]{1,0:T(8,128)(2,1)S(1)} %shard_map.76.refs_0_), channel_id=1, source_target_pairs={{0,8},{4,12},{8,0},{12,4},{1,9},{5,13},{9,1},{13,5},{2,10},{6,14},... | collective-permute-start | bytes 2359304 | tf_op jit(solution)/shard_map/ppermute | solution.py:276
  8.0 2.2 %copy-start = (bf16[2048,1024]{1,0:T(8,128)(2,1)S(1)}, bf16[2048,1024]{1,0:T(8,128)(2,1)}, u32[]{:S(2)}) copy-start(bf16[2048,1024]{1,0:T(8,128)(2,1)} %down_ref.7) | copy-start | bytes 12582916
  10.1 1.0 copy-start.3
  11.1 4.6 %copy-start.1 = (bf16[2048,1024]{1,0:T(8,128)(2,1)S(1)}, bf16[2048,1024]{1,0:T(8,128)(2,1)}, u32[]{:S(2)}) copy-start(bf16[2048,1024]{1,0:T(8,128)(2,1)} %down_ref.7) | copy-start | bytes 12582916
  11.1 6.8 %copy-start.6 = (bf16[192,1024]{1,0:T(8,128)(2,1)S(1)}, bf16[192,1024]{1,0:T(8,128)(2,1)}, u32[]{:S(2)}) copy-start(bf16[192,1024]{1,0:T(8,128)(2,1)} %refs_0_.2) | copy-start | bytes 1179652
  17.8 1.8 %collective-permute-start.5 = (bf16[192,1024]{1,0:T(8,128)(2,1)S(1)}, bf16[192,1024]{1,0:T(8,128)(2,1)S(1)}, u32[]{:S(2)}, u32[]{:S(2)}) collective-permute-start(bf16[192,1024]{1,0:T(8,128)(2,1)S(1)} %get-tuple-element.41), channel_id=1, source_target_pairs={{0,4},{4,0},{8,12},{12,8},{1,5},{5,1},{9,13},{13,9},{2,6},{6,2},{1... | collective-permute-start | bytes 1179656 | tf_op jit(solution)/shard_map/ppermute | solution.py:281
  17.9 13.8 %collective-permute-start.4 = (bf16[192,1024]{1,0:T(8,128)(2,1)S(1)}, bf16[192,1024]{1,0:T(8,128)(2,1)S(1)}, u32[]{:S(2)}, u32[]{:S(2)}) collective-permute-start(bf16[192,1024]{1,0:T(8,128)(2,1)S(1)} %collective-permute-done.2.cot_ref.refs_1_), channel_id=1, source_target_pairs={{0,1},{1,2},{2,3},{3,0},{4,5},{5,6},{6,7},{7,4},{8,9},{9,10},{10,1... | collective-permute-start | bytes 1179656 | tf_op jit(solution)/shard_map/ppermute | solution.py:301
  18.0 22.1 %collective-permute-start.3 = (bf16[192,1024]{1,0:T(8,128)(2,1)S(1)}, bf16[192,1024]{1,0:T(8,128)(2,1)S(1)}, u32[]{:S(2)}, u32[]{:S(2)}) collective-permute-start(bf16[192,1024]{1,0:T(8,128)(2,1)S(1)} %copy-done.6), channel_id=1, source_target_pairs={{0,1},{1,2},{2,3},{3,0},{4,5},{5,6},{6,7},{7,4},{8,9},{9,10},{10,1... | collective-permute-start | bytes 1179656 | tf_op jit(solution)/shard_map/ppermute | solution.py:306
  20.2 15.3 %collective-permute-start.9 = (bf16[192,1024]{1,0:T(8,128)(2,1)S(1)}, bf16[192,1024]{1,0:T(8,128)(2,1)S(1)}, u32[]{:S(2)}, u32[]{:S(2)}) collective-permute-start(bf16[192,1024]{1,0:T(8,128)(2,1)S(1)} %shard_map.80), channel_id=1, source_target_pairs={{0,8},{4,12},{8,0},{12,4},{1,9},{5,13},{9,1},{13,5},{2,10},{6,14},... | collective-permute-start | bytes 1179656 | tf_op jit(solution)/shard_map/ppermute | solution.py:287
  31.7 16.4 %collective-permute-start.12 = (bf16[192,1024]{1,0:T(8,128)(2,1)S(1)}, bf16[192,1024]{1,0:T(8,128)(2,1)S(1)}, u32[]{:S(2)}, u32[]{:S(2)}) collective-permute-start(bf16[192,1024]{1,0:T(8,128)(2,1)S(1)} %collective-permute-done.4.cot_ref.refs_2_), channel_id=1, source_target_pairs={{0,1},{1,2},{2,3},{3,0},{4,5},{5,6},{6,7},{7,4},{8,9},{9,10},{10,1... | collective-permute-start | bytes 1179656 | tf_op jit(solution)/shard_map/ppermute | solution.py:301
  33.8 4.1 %collective-permute-start.6 = (bf16[192,1024]{1,0:T(8,128)(2,1)S(1)}, bf16[192,1024]{1,0:T(8,128)(2,1)S(1)}, u32[]{:S(2)}, u32[]{:S(2)}) collective-permute-start(bf16[192,1024]{1,0:T(8,128)(2,1)S(1)} %get-tuple-element.44), channel_id=1, source_target_pairs={{0,4},{4,0},{8,12},{12,8},{1,5},{5,1},{9,13},{13,9},{2,6},{6,2},{1... | collective-permute-start | bytes 1179656 | tf_op jit(solution)/shard_map/ppermute | solution.py:281
  36.2 11.9 %copy-start.2 = (bf16[1024,2048]{1,0:T(8,128)(2,1)S(1)}, bf16[1024,2048]{1,0:T(8,128)(2,1)}, u32[]{:S(2)}) copy-start(bf16[1024,2048]{1,0:T(8,128)(2,1)} %up_ref.7) | copy-start | bytes 12582916
  37.3 10.8 %collective-permute-start.10 = (bf16[192,1024]{1,0:T(8,128)(2,1)S(1)}, bf16[192,1024]{1,0:T(8,128)(2,1)S(1)}, u32[]{:S(2)}, u32[]{:S(2)}) collective-permute-start(bf16[192,1024]{1,0:T(8,128)(2,1)S(1)} %shard_map.87.mine_ref.refs_5_), channel_id=1, source_target_pairs={{0,4},{4,0},{8,12},{12,8},{1,5},{5,1},{9,13},{13,9},{2,6},{6,2},{1... | collective-permute-start | bytes 1179656 | tf_op jit(solution)/shard_map/ppermute | solution.py:293
  38.4 14.8 %collective-permute-start.7 = (bf16[192,1024]{1,0:T(8,128)(2,1)S(1)}, bf16[192,1024]{1,0:T(8,128)(2,1)S(1)}, u32[]{:S(2)}, u32[]{:S(2)}) collective-permute-start(bf16[192,1024]{1,0:T(8,128)(2,1)S(1)} %shard_map.82), channel_id=1, source_target_pairs={{0,8},{4,12},{8,0},{12,4},{1,9},{5,13},{9,1},{13,5},{2,10},{6,14},... | collective-permute-start | bytes 1179656 | tf_op jit(solution)/shard_map/ppermute | solution.py:287
  40.0 32.4 %collective-permute-start.16 = (bf16[768,1024]{1,0:T(8,128)(2,1)S(1)}, bf16[768,1024]{1,0:T(8,128)(2,1)S(1)}, u32[]{:S(2)}, u32[]{:S(2)}) collective-permute-start(bf16[768,1024]{1,0:T(8,128)(2,1)S(1)} %get-tuple-element.55.mine_ref), channel_id=1, source_target_pairs={{0,4},{4,0},{8,12},{12,8},{1,5},{5,1},{9,13},{13,9},{2,6},{6,2},{1... | collective-permute-start | bytes 4718600 | tf_op jit(solution)/shard_map/ppermute | solution.py:308
  40.1 17.6 %collective-permute-start.19 = (bf16[192,1024]{1,0:T(8,128)(2,1)S(1)}, bf16[192,1024]{1,0:T(8,128)(2,1)S(1)}, u32[]{:S(2)}, u32[]{:S(2)}) collective-permute-start(bf16[192,1024]{1,0:T(8,128)(2,1)S(1)} %get-tuple-element.58), channel_id=1, source_target_pairs={{0,4},{4,0},{8,12},{12,8},{1,5},{5,1},{9,13},{13,9},{2,6},{6,2},{1... | collective-permute-start | bytes 1179656 | tf_op jit(solution)/shard_map/ppermute | solution.py:281
  51.0 13.2 %collective-permute-start.11 = (bf16[192,1024]{1,0:T(8,128)(2,1)S(1)}, bf16[192,1024]{1,0:T(8,128)(2,1)S(1)}, u32[]{:S(2)}, u32[]{:S(2)}) collective-permute-start(bf16[192,1024]{1,0:T(8,128)(2,1)S(1)} %get-tuple-element.46), channel_id=1, source_target_pairs={{0,1},{1,2},{2,3},{3,0},{4,5},{5,6},{6,7},{7,4},{8,9},{9,10},{10,1... | collective-permute-start | bytes 1179656 | tf_op jit(solution)/shard_map/ppermute | solution.py:317
  53.1 2.4 %collective-permute-start.13 = (bf16[192,1024]{1,0:T(8,128)(2,1)S(1)}, bf16[192,1024]{1,0:T(8,128)(2,1)S(1)}, u32[]{:S(2)}, u32[]{:S(2)}) collective-permute-start(bf16[192,1024]{1,0:T(8,128)(2,1)S(1)} %get-tuple-element.52), channel_id=1, source_target_pairs={{0,4},{4,0},{8,12},{12,8},{1,5},{5,1},{9,13},{13,9},{2,6},{6,2},{1... | collective-permute-start | bytes 1179656 | tf_op jit(solution)/shard_map/ppermute | solution.py:281
  55.0 12.0 %collective-permute-start.8 = (bf16[192,1024]{1,0:T(8,128)(2,1)S(1)}, bf16[192,1024]{1,0:T(8,128)(2,1)S(1)}, u32[]{:S(2)}, u32[]{:S(2)}) collective-permute-start(bf16[192,1024]{1,0:T(8,128)(2,1)S(1)} %shard_map.84.mine_ref.refs_6_), channel_id=1, source_target_pairs={{0,4},{4,0},{8,12},{12,8},{1,5},{5,1},{9,13},{13,9},{2,6},{6,2},{1... | collective-permute-start | bytes 1179656 | tf_op jit(solution)/shard_map/ppermute | solution.py:293
  56.1 13.8 %collective-permute-start.14 = (bf16[192,1024]{1,0:T(8,128)(2,1)S(1)}, bf16[192,1024]{1,0:T(8,128)(2,1)S(1)}, u32[]{:S(2)}, u32[]{:S(2)}) collective-permute-start(bf16[192,1024]{1,0:T(8,128)(2,1)S(1)} %shard_map.92), channel_id=1, source_target_pairs={{0,8},{4,12},{8,0},{12,4},{1,9},{5,13},{9,1},{13,5},{2,10},{6,14},... | collective-permute-start | bytes 1179656 | tf_op jit(solution)/shard_map/ppermute | solution.py:287
  58.3 14.1 %collective-permute-start.15 = (bf16[192,1024]{1,0:T(8,128)(2,1)S(1)}, bf16[192,1024]{1,0:T(8,128)(2,1)S(1)}, u32[]{:S(2)}, u32[]{:S(2)}) collective-permute-start(bf16[192,1024]{1,0:T(8,128)(2,1)S(1)} %collective-permute-done.3.refs_1_), channel_id=1, source_target_pairs={{0,1},{1,2},{2,3},{3,0},{4,5},{5,6},{6,7},{7,4},{8,9},{9,10},{10,1... | collective-permute-start | bytes 1179656 | tf_op jit(solution)/shard_map/ppermute | solution.py:318
  64.2 15.9 %collective-permute-start.20 = (bf16[192,1024]{1,0:T(8,128)(2,1)S(1)}, bf16[192,1024]{1,0:T(8,128)(2,1)S(1)}, u32[]{:S(2)}, u32[]{:S(2)}) collective-permute-start(bf16[192,1024]{1,0:T(8,128)(2,1)S(1)} %shard_map.98), channel_id=1, source_target_pairs={{0,8},{4,12},{8,0},{12,4},{1,9},{5,13},{9,1},{13,5},{2,10},{6,14},... | collective-permute-start | bytes 1179656 | tf_op jit(solution)/shard_map/ppermute | solution.py:287
  69.7 2.7 %copy-start.4 = (bf16[192,1024]{1,0:T(8,128)(2,1)S(1)}, bf16[192,1024]{1,0:T(8,128)(2,1)}, u32[]{:S(2)}) copy-start(bf16[192,1024]{1,0:T(8,128)(2,1)} %refs_0_.1) | copy-start | bytes 1179652
  69.7 14.4 %collective-permute-start.18 = (bf16[192,1024]{1,0:T(8,128)(2,1)S(1)}, bf16[192,1024]{1,0:T(8,128)(2,1)S(1)}, u32[]{:S(2)}, u32[]{:S(2)}) collective-permute-start(bf16[192,1024]{1,0:T(8,128)(2,1)S(1)} %shard_map.90), channel_id=1, source_target_pairs={{0,1},{1,2},{2,3},{3,0},{4,5},{5,6},{6,7},{7,4},{8,9},{9,10},{10,1... | collective-permute-start | bytes 1179656 | tf_op jit(solution)/shard_map/ppermute | solution.py:317
  71.7 10.3 %collective-permute-start.17 = (bf16[192,1024]{1,0:T(8,128)(2,1)S(1)}, bf16[192,1024]{1,0:T(8,128)(2,1)S(1)}, u32[]{:S(2)}, u32[]{:S(2)}) collective-permute-start(bf16[192,1024]{1,0:T(8,128)(2,1)S(1)} %shard_map.94.mine_ref.refs_7_), channel_id=1, source_target_pairs={{0,4},{4,0},{8,12},{12,8},{1,5},{5,1},{9,13},{13,9},{2,6},{6,2},{1... | collective-permute-start | bytes 1179656 | tf_op jit(solution)/shard_map/ppermute | solution.py:293
  81.9 3.4 %collective-permute-start.21 = (bf16[192,1024]{1,0:T(8,128)(2,1)S(1)}, bf16[192,1024]{1,0:T(8,128)(2,1)S(1)}, u32[]{:S(2)}, u32[]{:S(2)}) collective-permute-start(bf16[192,1024]{1,0:T(8,128)(2,1)S(1)} %shard_map.100.mine_ref.refs_4_), channel_id=1, source_target_pairs={{0,4},{4,0},{8,12},{12,8},{1,5},{5,1},{9,13},{13,9},{2,6},{6,2},{1... | collective-permute-start | bytes 1179656 | tf_op jit(solution)/shard_map/ppermute | solution.py:293
  81.9 13.8 %collective-permute-start.22 = (bf16[192,1024]{1,0:T(8,128)(2,1)S(1)}, bf16[192,1024]{1,0:T(8,128)(2,1)S(1)}, u32[]{:S(2)}, u32[]{:S(2)}) collective-permute-start(bf16[192,1024]{1,0:T(8,128)(2,1)S(1)} %collective-permute-done.15.refs_2_), channel_id=1, source_target_pairs={{0,1},{1,2},{2,3},{3,0},{4,5},{5,6},{6,7},{7,4},{8,9},{9,10},{10,1... | collective-permute-start | bytes 1179656 | tf_op jit(solution)/shard_map/ppermute | solution.py:318
  84.7 19.0 %collective-permute-start.23 = (bf16[192,1024]{1,0:T(8,128)(2,1)S(1)}, bf16[192,1024]{1,0:T(8,128)(2,1)S(1)}, u32[]{:S(2)}, u32[]{:S(2)}) collective-permute-start(bf16[192,1024]{1,0:T(8,128)(2,1)S(1)} %shard_map.97), channel_id=1, source_target_pairs={{0,1},{1,2},{2,3},{3,0},{4,5},{5,6},{6,7},{7,4},{8,9},{9,10},{10,1... | collective-permute-start | bytes 1179656 | tf_op jit(solution)/shard_map/ppermute | solution.py:331

commit v11 on v10

--- a/solution.py
+++ b/solution.py
@@ -40,8 +40,8 @@
     return lax.optimization_barrier((value, *first))[0] if first else value
 
 
-def tile_of(extent):
-    return next(t for t in (256, 128, extent) if extent % t == 0)
+def tile_of(extent, most=512):
+    return next(t for t in (most, 256, 128, extent) if extent % t == 0)
 
 
 def in_vmem():
@@ -223,9 +223,21 @@
     )
 
 
-def grad_up_kernel(blocks, scale, place_ref, *refs):
-    ins, mine, pair = (refs[i * blocks : (i + 1) * blocks] for i in range(3))
-    out_ref, inputs, grads = refs[3 * blocks :]
+def join_kernel(place_ref, *refs):
+    tokens = refs[0].shape[0]
+    for s, ref in enumerate(refs[:-1]):
+        refs[-1][pl.ds(s * tokens, tokens), :] = ref[...]
+
+
+def join_call(place, blocks):
+    tokens, features = blocks[0].shape
+    out = jax.ShapeDtypeStruct((tokens * len(blocks), features), blocks[0].dtype)
+    return call(join_kernel, place, blocks, out, 8, MOST)
+
+
+def grad_up_kernel(blocks, scale, place_ref, inputs, *refs):
+    mine, pair = refs[:blocks], refs[blocks : 2 * blocks]
+    out_ref, grads = refs[2 * blocks :]
     tokens, half = mine[0].shape
     tile = out_ref.shape[0]
 
@@ -234,29 +246,26 @@
         left, right = block(core_of(place_ref), half), block(1 - core_of(place_ref), half)
         for s in range(blocks):
             here = pl.ds(s * tokens, tokens)
-            inputs[here, :] = ins[s][...]
             grads[here, left] = mine[s][...]
             grads[here, right] = pair[s][...]
 
     out_ref[...] = dot(inputs[:, block(pl.program_id(0), tile)], grads[...], FIRST) * scale
 
 
-def grad_up_call(place, ins, mine, pair, scale):
-    tokens, features = ins[0].shape
-    total = tokens * len(ins)
+def grad_up_call(place, inputs, mine, pair, scale):
+    total, features = inputs.shape
     hidden = 2 * mine[0].shape[1]
-    tile = tile_of(features)
+    tile = tile_of(features, 256)
     return call(
         functools.partial(grad_up_kernel, len(mine), scale),
         place,
-        [*ins, *mine, *pair],
+        [inputs, *mine, *pair],
         jax.ShapeDtypeStruct((features, hidden), jnp.float32),
         18,
         MUCH,
         grid=(features // tile,),
         out_specs=pl.BlockSpec((tile, hidden), lambda i, place: (i, 0)),
         scratch=[
-            pltpu.VMEM((total, features), jnp.bfloat16),
             pltpu.VMEM((total, hidden), jnp.bfloat16),
         ],
     )
@@ -303,7 +312,7 @@
         if s < last:
             hidden_part(s)
             exchange(s)
-    ins = [inputs, lax.ppermute(after(inputs, cots[1]), "col", ring)]
+    ins = [inputs, lax.ppermute(after(inputs, cots[last - 1]), "col", ring)]
     pre_all, act = lay_out_call(place, pres)
     act_theirs = lax.ppermute(act, "row", pair)
 
@@ -315,22 +324,22 @@
     exchange(0, sent[last])
     for s in range(2, cols):
         arrived = lax.ppermute(sums, "col", ring)
-        ins.append(lax.ppermute(after(ins[-1], sums), "col", ring))
-        pre_grad(s, *([late] if s > 2 else [ins[1]]))
+        pre_grad(s, *([late] if s > 2 else []))
+        ins.append(lax.ppermute(after(ins[-1], sums, mine[s]), "col", ring))
         first = []
         if s == last:
             grad_down = grad_down_call(
-                after(place, mine[s], *ins[2:s]), act, act_theirs, cots, scale
+                after(place, mine[s]), act, act_theirs, cots, scale
             )
             pre_grad(0, grad_down)
             first = [grad_down]
         if s == 2:
-            arrived = add_call(place, arrived, [], jnp.float32, MUCH)
+            arrived = add_call(place, arrived, [], jnp.float32, MOST)
         part = share(s, *first)[0]
         sums = late = add_call(place, part, [arrived], jnp.bfloat16, LITTLE)
     arrived = lax.ppermute(sums, "col", ring)
     part = share(0, sums)[0]
-    grad_up = grad_up_call(after(place, part), ins, mine, theirs, scale)
+    grad_up = grad_up_call(after(place, part), join_call(place, ins), mine, theirs, scale)
     sums = add_call(after(place, grad_up), part, [arrived], jnp.bfloat16, LITTLE)
     return (sums, grad_up, grad_down)
 

time: 105 us -> 101 us (0.962)
  starting transfers between devices: 16.4 us -> 12 us
    ppermute x3, waiting for transfers between devices: 20 us -> 14.9 us  [per_device(): arriving = lax.ppermute(cots[s - 1], 'col', ring)]
    ppermute x4, starting transfers between devices: 6.8 us -> 3.44 us  [exchange(): others[s] = [lax.ppermute(values, 'row', to) for to in over_x]]
    ppermute x3, waiting for transfers between devices: 9.13 us -> 12.4 us  [the longest x2 9.58 us: per_device(): ins.append(lax.ppermute(after(ins[-1], sums, mine[s]), 'col', ring))]
    ppermute x3, waiting for transfers between devices: 7.19 us -> 8.74 us  [per_device(): arrived = lax.ppermute(sums, 'col', ring)]
    pallas_call x28 -> x29, Pallas kernels: 46.6 us -> 45.8 us  [call(): pl.pallas_call(kernel, out_shape=outs, grid_spec=pltpu.PrefetchScalarGrid...]
  transfers between devices with their start and end apart: 24 -> 24, of which waited for: 9 -> 9; matrix products, arithmetic and copies ran while one was open for 0% -> 0% of each run, Pallas kernels for 43% -> 44%
where the time goes in v11:
time: 101 us
  Pallas kernels  45.8 us (45%)
  waiting for transfers between devices  37.4 us (37%)
  starting transfers between devices  12 us (12%)
  local copies, waits for them, and re-layouts  4.34 us (4%)
    pallas_call x29, Pallas kernels, call(): pl.pallas_call(kernel, out_shape=outs, grid_spec=pltpu.PrefetchScalarGrid...  45.8 us
    ppermute x3, waiting for transfers between devices, per_device(): arriving = lax.ppermute(cots[s - 1], 'col', ring)  14.9 us
    ppermute x2, waiting for transfers between devices, per_device(): ins.append(lax.ppermute(after(ins[-1], sums, mine[s]), 'col', ring))  9.58 us
    ppermute x3, waiting for transfers between devices, per_device(): arrived = lax.ppermute(sums, 'col', ring)  8.74 us
    unnamed x14, local copies, waits for them, and re-layouts  4.34 us
    ppermute x4, starting transfers between devices, exchange(): others[s] = [lax.ppermute(values, 'row', to) for to in over_x]  3.44 us
    ppermute x1, waiting for transfers between devices, per_device(): ins = [inputs, lax.ppermute(after(inputs, cots[last - 1]), 'col', ring)]  2.87 us
    ppermute x3, starting transfers between devices, per_device(): arriving = lax.ppermute(cots[s - 1], 'col', ring)  2.7 us
  transfers between devices with their start and end apart: 24, of which 9 were waited for; matrix products, arithmetic and copies ran while one was open for 0% of the time, Pallas kernels for 44%

profile of v11, /device:TPU:0, one launch (start us, length us, event | category | flops | bytes accessed | tf_op | source)
XLA Modules:
  0.0 100.6 jit_solution(11537966701229875645)
XLA Ops:
  1.2 2.6 %collective-permute-start.2 = (bf16[192,1024]{1,0:T(8,128)(2,1)}, bf16[192,1024]{1,0:T(8,128)(2,1)S(1)}, u32[]{:S(2)}, u32[]{:S(2)}) collective-permute-start(bf16[192,1024]{1,0:T(8,128)(2,1)} %refs_0_.1), channel_id=1, source_target_pairs={{0,1},{1,2},{2,3},{3,0},{4,5},{5,6},{6,7},{7,4},{8,9},{9,10},{10,1... | collective-permute-start | bytes 1179656 | tf_op jit(solution)/shard_map/ppermute | solution.py:310
  3.8 1.1 %copy-done.5 = bf16[192,2048]{1,0:T(8,128)(2,1)S(1)} copy-done((bf16[192,2048]{1,0:T(8,128)(2,1)S(1)}, bf16[192,2048]{1,0:T(8,128)(2,1)}, u32[]{:S(2)}) %copy-start.5) | copy-done | bytes 786456
  5.6 2.4 %collective-permute-start.1 = (bf16[384,1024]{1,0:T(8,128)(2,1)S(1)}, bf16[384,1024]{1,0:T(8,128)(2,1)S(1)}, u32[]{:S(2)}, u32[]{:S(2)}) collective-permute-start(bf16[384,1024]{1,0:T(8,128)(2,1)S(1)} %shard_map.76.refs_0_), channel_id=1, source_target_pairs={{0,8},{4,12},{8,0},{12,4},{1,9},{5,13},{9,1},{13,5},{2,10},{6,14},... | collective-permute-start | bytes 2359304 | tf_op jit(solution)/shard_map/ppermute | solution.py:285
  8.0 2.2 %copy-done = bf16[2048,1024]{1,0:T(8,128)(2,1)S(1)} copy-done((bf16[2048,1024]{1,0:T(8,128)(2,1)S(1)}, bf16[2048,1024]{1,0:T(8,128)(2,1)}, u32[]{:S(2)}) %copy-start) | copy-done | bytes 4194328
  10.1 1.0 copy-done.3
  11.1 2.1 %shard_map.78 = (f32[192,1024]{1,0:T(8,128)S(1)}, bf16[192,1024]{1,0:T(8,128)(2,1)S(1)}) custom-call(s32[2]{0:T(128)S(1)} %pad_add_fusion.place_ref, bf16[192,1024]{1,0:T(8,128)(2,1)S(1)} %copy-done.3, bf16[2048,1024]{1,0:T(8,128)(2,1)S(1)} %copy-done), custom_call_target="tpu_custom_call" | custom-call | flops 10000000 | bytes 1024 | tf_op jit(solution)/shard_map/pallas_call | solution.py:67
  13.2 2.6 %collective-permute-done.2.cot_ref.refs_1_ = bf16[192,1024]{1,0:T(8,128)(2,1)S(1)} collective-permute-done((bf16[192,1024]{1,0:T(8,128)(2,1)}, bf16[192,1024]{1,0:T(8,128)(2,1)S(1)}, u32[]{:S(2)}, u32[]{:S(2)}) %collective-permute-start.2) | collective-permute-done | bytes 393248 | tf_op jit(solution)/shard_map/ppermute | solution.py:310
  15.8 2.1 %shard_map.79 = (f32[192,1024]{1,0:T(8,128)S(1)}, bf16[192,1024]{1,0:T(8,128)(2,1)S(1)}) custom-call(s32[2]{0:T(128)S(1)} %pad_add_fusion.place_ref, bf16[192,1024]{1,0:T(8,128)(2,1)S(1)} %collective-permute-done.2.cot_ref.refs_1_, bf16[2048,1024]{1,0:T(8,128)(2,1)S(1)} %copy-done.1), custom_call_target="tpu_custom_call" | custom-call | flops 10000000 | bytes 1024 | tf_op jit(solution)/shard_map/pallas_call | solution.py:67
  18.4 1.2 %collective-permute-done.4.refs_0_ = bf16[192,1024]{1,0:T(8,128)(2,1)S(1)} collective-permute-done((bf16[192,1024]{1,0:T(8,128)(2,1)S(1)}, bf16[192,1024]{1,0:T(8,128)(2,1)S(1)}, u32[]{:S(2)}, u32[]{:S(2)}) %collective-permute-start.4) | collective-permute-done | bytes 393248 | tf_op jit(solution)/shard_map/ppermute | solution.py:290
  20.2 1.6 %collective-permute-start.8 = (bf16[192,1024]{1,0:T(8,128)(2,1)S(1)}, bf16[192,1024]{1,0:T(8,128)(2,1)S(1)}, u32[]{:S(2)}, u32[]{:S(2)}) collective-permute-start(bf16[192,1024]{1,0:T(8,128)(2,1)S(1)} %shard_map.80), channel_id=1, source_target_pairs={{0,8},{4,12},{8,0},{12,4},{1,9},{5,13},{9,1},{13,5},{2,10},{6,14},... | collective-permute-start | bytes 1179656 | tf_op jit(solution)/shard_map/ppermute | solution.py:296
  21.8 9.4 %collective-permute-done.3.cot_ref.refs_2_ = bf16[192,1024]{1,0:T(8,128)(2,1)S(1)} collective-permute-done((bf16[192,1024]{1,0:T(8,128)(2,1)S(1)}, bf16[192,1024]{1,0:T(8,128)(2,1)S(1)}, u32[]{:S(2)}, u32[]{:S(2)}) %collective-permute-start.3) | collective-permute-done | bytes 393248 | tf_op jit(solution)/shard_map/ppermute | solution.py:310
  31.2 2.1 %shard_map.81 = (f32[192,1024]{1,0:T(8,128)S(1)}, bf16[192,1024]{1,0:T(8,128)(2,1)S(1)}) custom-call(s32[2]{0:T(128)S(1)} %pad_add_fusion.place_ref, bf16[192,1024]{1,0:T(8,128)(2,1)S(1)} %collective-permute-done.3.cot_ref.refs_2_, bf16[2048,1024]{1,0:T(8,128)(2,1)S(1)} %copy-done.1), custom_call_target="tpu_custom_call" | custom-call | flops 10000000 | bytes 1024 | tf_op jit(solution)/shard_map/pallas_call | solution.py:67
  33.4 1.7 %shard_map.77 = (bf16[768,1024]{1,0:T(8,128)(2,1)S(1)}, bf16[768,1024]{1,0:T(8,128)(2,1)S(1)}) custom-call(s32[2]{0:T(128)S(1)} %pad_add_fusion.place_ref, bf16[384,1024]{1,0:T(8,128)(2,1)S(1)} %shard_map.76.refs_0_, bf16[384,1024]{1,0:T(8,128)(2,1)S(1)} %collective-permute-done.1.refs_1_), custom_call_target="tpu_custom_call" | custom-call | flops 6000000000 | bytes 1024 | tf_op jit(solution)/shard_map/pallas_call | solution.py:67
  35.7 1.1 %shard_map.87.mine_ref.refs_1_ = bf16[192,1024]{1,0:T(8,128)(2,1)S(1)} custom-call(s32[2]{0:T(128)S(1)} %pad_add_fusion.place_ref, bf16[768,1024]{1,0:T(8,128)(2,1)S(1)} %get-tuple-element.33.pre_ref, f32[192,1024]{1,0:T(8,128)S(1)} %shard_map.86.part_ref), custom_call_target="tpu_custom_call" | custom-call | flops 100000000 | bytes 1024 | tf_op jit(solution)/shard_map/pallas_call | solution.py:67
  38.0 1.6 %collective-permute-start.6 = (bf16[192,1024]{1,0:T(8,128)(2,1)S(1)}, bf16[192,1024]{1,0:T(8,128)(2,1)S(1)}, u32[]{:S(2)}, u32[]{:S(2)}) collective-permute-start(bf16[192,1024]{1,0:T(8,128)(2,1)S(1)} %shard_map.82), channel_id=1, source_target_pairs={{0,8},{4,12},{8,0},{12,4},{1,9},{5,13},{9,1},{13,5},{2,10},{6,14},... | collective-permute-start | bytes 1179656 | tf_op jit(solution)/shard_map/ppermute | solution.py:296
  40.8 3.0 %collective-permute-done.11.cot_ref.refs_3_ = bf16[192,1024]{1,0:T(8,128)(2,1)S(1)} collective-permute-done((bf16[192,1024]{1,0:T(8,128)(2,1)S(1)}, bf16[192,1024]{1,0:T(8,128)(2,1)S(1)}, u32[]{:S(2)}, u32[]{:S(2)}) %collective-permute-start.11) | collective-permute-done | bytes 393248 | tf_op jit(solution)/shard_map/ppermute | solution.py:310
  43.7 3.0 %shard_map.88 = (f32[192,1024]{1,0:T(8,128)}, bf16[192,1024]{1,0:T(8,128)(2,1)S(1)}) custom-call(s32[2]{0:T(128)S(1)} %pad_add_fusion.place_ref, bf16[192,1024]{1,0:T(8,128)(2,1)S(1)} %shard_map.87.mine_ref.refs_1_, bf16[192,1024]{1,0:T(8,128)(2,1)S(1)} %collective-permute-done.9.theirs_ref.refs_5_, bf16[1024,2048]{1,0:T(8,128)(2,1)S(1)} %copy-done.2), custom_call_target="tpu_custom_call" | custom-call | flops 10000000 | bytes 1024 | tf_op jit(solution)/shard_map/pallas_call | solution.py:67
  46.7 2.1 %shard_map.91 = (f32[192,1024]{1,0:T(8,128)S(1)}, bf16[192,1024]{1,0:T(8,128)(2,1)S(1)}) custom-call(s32[2]{0:T(128)S(1)} %pad_add_fusion.place_ref, bf16[192,1024]{1,0:T(8,128)(2,1)S(1)} %collective-permute-done.11.cot_ref.refs_3_, bf16[2048,1024]{1,0:T(8,128)(2,1)S(1)} %copy-done.1), custom_call_target="tpu_custom_call" | custom-call | flops 10000000 | bytes 1024 | tf_op jit(solution)/shard_map/pallas_call | solution.py:67
  50.0 1.1 %shard_map.84.mine_ref.refs_2_ = bf16[192,1024]{1,0:T(8,128)(2,1)S(1)} custom-call(s32[2]{0:T(128)S(1)} %pad_add_fusion.place_ref, bf16[768,1024]{1,0:T(8,128)(2,1)S(1)} %get-tuple-element.33.pre_ref, f32[192,1024]{1,0:T(8,128)S(1)} %shard_map.83.part_ref), custom_call_target="tpu_custom_call" | custom-call | flops 100000000 | bytes 1024 | tf_op jit(solution)/shard_map/pallas_call | solution.py:67
  51.1 2.9 %collective-permute-done.20.refs_1_ = bf16[192,1024]{1,0:T(8,128)(2,1)S(1)} collective-permute-done((bf16[192,1024]{1,0:T(8,128)(2,1)S(1)}, bf16[192,1024]{1,0:T(8,128)(2,1)S(1)}, u32[]{:S(2)}, u32[]{:S(2)}) %collective-permute-start.20) | collective-permute-done | bytes 393248 | tf_op jit(solution)/shard_map/ppermute | solution.py:315
  54.8 7.6 %collective-permute-done.10.part_ref = bf16[192,1024]{1,0:T(8,128)(2,1)S(1)} collective-permute-done((bf16[192,1024]{1,0:T(8,128)(2,1)S(1)}, bf16[192,1024]{1,0:T(8,128)(2,1)S(1)}, u32[]{:S(2)}, u32[]{:S(2)}) %collective-permute-start.10) | collective-permute-done | bytes 393248 | tf_op jit(solution)/shard_map/ppermute | solution.py:326
  63.0 2.1 %shard_map.85.part_ref = f32[192,1024]{1,0:T(8,128)S(1)} custom-call(s32[2]{0:T(128)S(1)} %pad_add_fusion.place_ref, bf16[192,1024]{1,0:T(8,128)(2,1)S(1)} %shard_map.84.mine_ref.refs_2_, bf16[192,1024]{1,0:T(8,128)(2,1)S(1)} %collective-permute-done.7.theirs_ref.refs_6_, bf16[1024,2048]{1,0:T(8,128)(2,1)S(1)} %copy-done.2), custom_call_target="tpu_custom_call" | custom-call | flops 10000000 | bytes 1024 | tf_op jit(solution)/shard_map/pallas_call | solution.py:67
  66.6 1.1 %shard_map.94.mine_ref.refs_3_ = bf16[192,1024]{1,0:T(8,128)(2,1)S(1)} custom-call(s32[2]{0:T(128)S(1)} %pad_add_fusion.place_ref, bf16[768,1024]{1,0:T(8,128)(2,1)S(1)} %get-tuple-element.33.pre_ref, f32[192,1024]{1,0:T(8,128)S(1)} %shard_map.93.part_ref), custom_call_target="tpu_custom_call" | custom-call | flops 100000000 | bytes 1024 | tf_op jit(solution)/shard_map/pallas_call | solution.py:67
  67.8 2.1 %collective-permute-done.21.refs_2_ = bf16[192,1024]{1,0:T(8,128)(2,1)S(1)} collective-permute-done((bf16[192,1024]{1,0:T(8,128)(2,1)S(1)}, bf16[192,1024]{1,0:T(8,128)(2,1)S(1)}, u32[]{:S(2)}, u32[]{:S(2)}) %collective-permute-start.21) | collective-permute-done | bytes 393248 | tf_op jit(solution)/shard_map/ppermute | solution.py:328
  70.0 6.5 %shard_map.95 = f32[2048,1024]{1,0:T(8,128)} custom-call(s32[2]{0:T(128)S(1)} %pad_add_fusion.place_ref, bf16[768,1024]{1,0:T(8,128)(2,1)S(1)} %get-tuple-element.51.mine_ref, bf16[768,1024]{1,0:T(8,128)(2,1)S(1)} %collective-permute-done.14.theirs_ref, bf16[192,1024]{1,0:T(8,128)(2,1)S(1)} %copy-done.4, ...), custom_call_target="tpu_custom_call" | custom-call | flops 100000000 | bytes 1024 | tf_op jit(solution)/shard_map/pallas_call | solution.py:67
  77.2 1.1 %shard_map.100.mine_ref.refs_0_ = bf16[192,1024]{1,0:T(8,128)(2,1)S(1)} custom-call(s32[2]{0:T(128)S(1)} %pad_add_fusion.place_ref, bf16[768,1024]{1,0:T(8,128)(2,1)S(1)} %get-tuple-element.33.pre_ref, f32[192,1024]{1,0:T(8,128)S(1)} %shard_map.99.part_ref), custom_call_target="tpu_custom_call" | custom-call | flops 100000000 | bytes 1024 | tf_op jit(solution)/shard_map/pallas_call | solution.py:67
  78.3 2.1 %shard_map.96.part_ref = f32[192,1024]{1,0:T(8,128)S(1)} custom-call(s32[2]{0:T(128)S(1)} %pad_add_fusion.place_ref, bf16[192,1024]{1,0:T(8,128)(2,1)S(1)} %shard_map.94.mine_ref.refs_3_, bf16[192,1024]{1,0:T(8,128)(2,1)S(1)} %collective-permute-done.15.theirs_ref.refs_7_, bf16[1024,2048]{1,0:T(8,128)(2,1)S(1)} %copy-done.2), custom_call_target="tpu_custom_call" | custom-call | flops 10000000 | bytes 1024 | tf_op jit(solution)/shard_map/pallas_call | solution.py:67
  80.4 1.1 %collective-permute-done.16.refs_0_ = bf16[192,1024]{1,0:T(8,128)(2,1)S(1)} collective-permute-done((bf16[192,1024]{1,0:T(8,128)(2,1)S(1)}, bf16[192,1024]{1,0:T(8,128)(2,1)S(1)}, u32[]{:S(2)}, u32[]{:S(2)}) %collective-permute-start.16) | collective-permute-done | bytes 393248 | tf_op jit(solution)/shard_map/ppermute | solution.py:326
  82.5 7.5 %collective-permute-done.22.refs_3_ = bf16[192,1024]{1,0:T(8,128)(2,1)S(1)} collective-permute-done((bf16[192,1024]{1,0:T(8,128)(2,1)S(1)}, bf16[192,1024]{1,0:T(8,128)(2,1)S(1)}, u32[]{:S(2)}, u32[]{:S(2)}) %collective-permute-start.22) | collective-permute-done | bytes 393248 | tf_op jit(solution)/shard_map/ppermute | solution.py:328
  90.6 2.1 %shard_map.101.part_ref = f32[192,1024]{1,0:T(8,128)S(1)} custom-call(s32[2]{0:T(128)S(1)} %pad_add_fusion.place_ref, bf16[192,1024]{1,0:T(8,128)(2,1)S(1)} %shard_map.100.mine_ref.refs_0_, bf16[192,1024]{1,0:T(8,128)(2,1)S(1)} %collective-permute-done.19.theirs_ref.refs_4_, bf16[1024,2048]{1,0:T(8,128)(2,1)S(1)} %copy-done.2), custom_call_target="tpu_custom_call" | custom-call | flops 10000000 | bytes 1024 | tf_op jit(solution)/shard_map/pallas_call | solution.py:67
  92.7 6.5 %shard_map.103 = f32[1024,2048]{1,0:T(8,128)} custom-call(s32[2]{0:T(128)S(1)} %pad_add_fusion.place_ref, bf16[768,1024]{1,0:T(8,128)(2,1)S(1)} %shard_map.102.inputs, bf16[192,1024]{1,0:T(8,128)(2,1)S(1)} %shard_map.100.mine_ref.refs_0_, bf16[192,1024]{1,0:T(8,128)(2,1)S(1)} %shard_map.87.mine_ref.refs_1_, ...), custom_call_target="tpu_custom_call" | custom-call | flops 3000000000 | bytes 1024 | tf_op jit(solution)/shard_map/pallas_call | solution.py:67
  99.2 1.4 %shard_map.104 = bf16[192,1024]{1,0:T(8,128)(2,1)} custom-call(s32[2]{0:T(128)S(1)} %pad_add_fusion.place_ref, f32[192,1024]{1,0:T(8,128)S(1)} %shard_map.101.part_ref, bf16[192,1024]{1,0:T(8,128)(2,1)S(1)} %collective-permute-done.23.refs_0_), custom_call_target="tpu_custom_call" | custom-call | flops 10000000 | bytes 1024 | tf_op jit(solution)/shard_map/pallas_call | solution.py:67
  (60 shorter events, 12.1 us)
Async XLA Ops:
  0.7 3.1 %collective-permute-start = (bf16[192,2048]{1,0:T(8,128)(2,1)}, bf16[192,2048]{1,0:T(8,128)(2,1)S(1)}, u32[]{:S(2)}, u32[]{:S(2)}) collective-permute-start(bf16[192,2048]{1,0:T(8,128)(2,1)} %mine_ref), channel_id=1, source_target_pairs={{0,4},{4,0},{8,12},{12,8},{1,5},{5,1},{9,13},{13,9},{2,6},{6,2},{1... | collective-permute-start | bytes 2359304 | tf_op jit(solution)/shard_map/ppermute | solution.py:284
  1.2 14.6 %collective-permute-start.2 = (bf16[192,1024]{1,0:T(8,128)(2,1)}, bf16[192,1024]{1,0:T(8,128)(2,1)S(1)}, u32[]{:S(2)}, u32[]{:S(2)}) collective-permute-start(bf16[192,1024]{1,0:T(8,128)(2,1)} %refs_0_.1), channel_id=1, source_target_pairs={{0,1},{1,2},{2,3},{3,0},{4,5},{5,6},{6,7},{7,4},{8,9},{9,10},{10,1... | collective-permute-start | bytes 1179656 | tf_op jit(solution)/shard_map/ppermute | solution.py:310
  3.8 1.1 %copy-start.5 = (bf16[192,2048]{1,0:T(8,128)(2,1)S(1)}, bf16[192,2048]{1,0:T(8,128)(2,1)}, u32[]{:S(2)}) copy-start(bf16[192,2048]{1,0:T(8,128)(2,1)} %mine_ref) | copy-start | bytes 2359300
  5.6 27.8 %collective-permute-start.1 = (bf16[384,1024]{1,0:T(8,128)(2,1)S(1)}, bf16[384,1024]{1,0:T(8,128)(2,1)S(1)}, u32[]{:S(2)}, u32[]{:S(2)}) collective-permute-start(bf16[384,1024]{1,0:T(8,128)(2,1)S(1)} %shard_map.76.refs_0_), channel_id=1, source_target_pairs={{0,8},{4,12},{8,0},{12,4},{1,9},{5,13},{9,1},{13,5},{2,10},{6,14},... | collective-permute-start | bytes 2359304 | tf_op jit(solution)/shard_map/ppermute | solution.py:285
  8.0 2.2 %copy-start = (bf16[2048,1024]{1,0:T(8,128)(2,1)S(1)}, bf16[2048,1024]{1,0:T(8,128)(2,1)}, u32[]{:S(2)}) copy-start(bf16[2048,1024]{1,0:T(8,128)(2,1)} %down_ref.7) | copy-start | bytes 12582916
  10.1 1.0 copy-start.3
  11.1 4.6 %copy-start.1 = (bf16[2048,1024]{1,0:T(8,128)(2,1)S(1)}, bf16[2048,1024]{1,0:T(8,128)(2,1)}, u32[]{:S(2)}) copy-start(bf16[2048,1024]{1,0:T(8,128)(2,1)} %down_ref.7) | copy-start | bytes 12582916
  17.8 1.8 %collective-permute-start.4 = (bf16[192,1024]{1,0:T(8,128)(2,1)S(1)}, bf16[192,1024]{1,0:T(8,128)(2,1)S(1)}, u32[]{:S(2)}, u32[]{:S(2)}) collective-permute-start(bf16[192,1024]{1,0:T(8,128)(2,1)S(1)} %get-tuple-element.38), channel_id=1, source_target_pairs={{0,4},{4,0},{8,12},{12,8},{1,5},{5,1},{9,13},{13,9},{2,6},{6,2},{1... | collective-permute-start | bytes 1179656 | tf_op jit(solution)/shard_map/ppermute | solution.py:290
  17.9 13.3 %collective-permute-start.3 = (bf16[192,1024]{1,0:T(8,128)(2,1)S(1)}, bf16[192,1024]{1,0:T(8,128)(2,1)S(1)}, u32[]{:S(2)}, u32[]{:S(2)}) collective-permute-start(bf16[192,1024]{1,0:T(8,128)(2,1)S(1)} %collective-permute-done.2.cot_ref.refs_1_), channel_id=1, source_target_pairs={{0,1},{1,2},{2,3},{3,0},{4,5},{5,6},{6,7},{7,4},{8,9},{9,10},{10,1... | collective-permute-start | bytes 1179656 | tf_op jit(solution)/shard_map/ppermute | solution.py:310
  18.0 21.6 %collective-permute-start.17 = (bf16[192,1024]{1,0:T(8,128)(2,1)S(1)}, bf16[192,1024]{1,0:T(8,128)(2,1)S(1)}, u32[]{:S(2)}, u32[]{:S(2)}) collective-permute-start(bf16[192,1024]{1,0:T(8,128)(2,1)S(1)} %get-tuple-element.54), channel_id=1, source_target_pairs={{0,4},{4,0},{8,12},{12,8},{1,5},{5,1},{9,13},{13,9},{2,6},{6,2},{1... | collective-permute-start | bytes 1179656 | tf_op jit(solution)/shard_map/ppermute | solution.py:290
  20.2 14.8 %collective-permute-start.8 = (bf16[192,1024]{1,0:T(8,128)(2,1)S(1)}, bf16[192,1024]{1,0:T(8,128)(2,1)S(1)}, u32[]{:S(2)}, u32[]{:S(2)}) collective-permute-start(bf16[192,1024]{1,0:T(8,128)(2,1)S(1)} %shard_map.80), channel_id=1, source_target_pairs={{0,8},{4,12},{8,0},{12,4},{1,9},{5,13},{9,1},{13,5},{2,10},{6,14},... | collective-permute-start | bytes 1179656 | tf_op jit(solution)/shard_map/ppermute | solution.py:296
  31.2 12.5 %collective-permute-start.11 = (bf16[192,1024]{1,0:T(8,128)(2,1)S(1)}, bf16[192,1024]{1,0:T(8,128)(2,1)S(1)}, u32[]{:S(2)}, u32[]{:S(2)}) collective-permute-start(bf16[192,1024]{1,0:T(8,128)(2,1)S(1)} %collective-permute-done.3.cot_ref.refs_2_), channel_id=1, source_target_pairs={{0,1},{1,2},{2,3},{3,0},{4,5},{5,6},{6,7},{7,4},{8,9},{9,10},{10,1... | collective-permute-start | bytes 1179656 | tf_op jit(solution)/shard_map/ppermute | solution.py:310
  33.3 4.1 %collective-permute-start.5 = (bf16[192,1024]{1,0:T(8,128)(2,1)S(1)}, bf16[192,1024]{1,0:T(8,128)(2,1)S(1)}, u32[]{:S(2)}, u32[]{:S(2)}) collective-permute-start(bf16[192,1024]{1,0:T(8,128)(2,1)S(1)} %get-tuple-element.41), channel_id=1, source_target_pairs={{0,4},{4,0},{8,12},{12,8},{1,5},{5,1},{9,13},{13,9},{2,6},{6,2},{1... | collective-permute-start | bytes 1179656 | tf_op jit(solution)/shard_map/ppermute | solution.py:290
  35.7 4.5 %copy-start.6 = (bf16[192,1024]{1,0:T(8,128)(2,1)S(1)}, bf16[192,1024]{1,0:T(8,128)(2,1)}, u32[]{:S(2)}) copy-start(bf16[192,1024]{1,0:T(8,128)(2,1)} %refs_0_.2) | copy-start | bytes 1179652
  35.7 8.0 %copy-start.2 = (bf16[1024,2048]{1,0:T(8,128)(2,1)S(1)}, bf16[1024,2048]{1,0:T(8,128)(2,1)}, u32[]{:S(2)}) copy-start(bf16[1024,2048]{1,0:T(8,128)(2,1)} %up_ref.7) | copy-start | bytes 12582916
  36.8 6.9 %collective-permute-start.9 = (bf16[192,1024]{1,0:T(8,128)(2,1)S(1)}, bf16[192,1024]{1,0:T(8,128)(2,1)S(1)}, u32[]{:S(2)}, u32[]{:S(2)}) collective-permute-start(bf16[192,1024]{1,0:T(8,128)(2,1)S(1)} %shard_map.87.mine_ref.refs_1_), channel_id=1, source_target_pairs={{0,4},{4,0},{8,12},{12,8},{1,5},{5,1},{9,13},{13,9},{2,6},{6,2},{1... | collective-permute-start | bytes 1179656 | tf_op jit(solution)/shard_map/ppermute | solution.py:302
  38.0 11.3 %collective-permute-start.6 = (bf16[192,1024]{1,0:T(8,128)(2,1)S(1)}, bf16[192,1024]{1,0:T(8,128)(2,1)S(1)}, u32[]{:S(2)}, u32[]{:S(2)}) collective-permute-start(bf16[192,1024]{1,0:T(8,128)(2,1)S(1)} %shard_map.82), channel_id=1, source_target_pairs={{0,8},{4,12},{8,0},{12,4},{1,9},{5,13},{9,1},{13,5},{2,10},{6,14},... | collective-permute-start | bytes 1179656 | tf_op jit(solution)/shard_map/ppermute | solution.py:296
  40.2 13.8 %collective-permute-start.20 = (bf16[192,1024]{1,0:T(8,128)(2,1)S(1)}, bf16[192,1024]{1,0:T(8,128)(2,1)S(1)}, u32[]{:S(2)}, u32[]{:S(2)}) collective-permute-start(bf16[192,1024]{1,0:T(8,128)(2,1)S(1)} %copy-done.6), channel_id=1, source_target_pairs={{0,1},{1,2},{2,3},{3,0},{4,5},{5,6},{6,7},{7,4},{8,9},{9,10},{10,1... | collective-permute-start | bytes 1179656 | tf_op jit(solution)/shard_map/ppermute | solution.py:315
  43.7 26.3 %collective-permute-start.14 = (bf16[768,1024]{1,0:T(8,128)(2,1)S(1)}, bf16[768,1024]{1,0:T(8,128)(2,1)S(1)}, u32[]{:S(2)}, u32[]{:S(2)}) collective-permute-start(bf16[768,1024]{1,0:T(8,128)(2,1)S(1)} %get-tuple-element.51.mine_ref), channel_id=1, source_target_pairs={{0,4},{4,0},{8,12},{12,8},{1,5},{5,1},{9,13},{13,9},{2,6},{6,2},{1... | collective-permute-start | bytes 4718600 | tf_op jit(solution)/shard_map/ppermute | solution.py:317
  46.7 15.8 %collective-permute-start.10 = (bf16[192,1024]{1,0:T(8,128)(2,1)S(1)}, bf16[192,1024]{1,0:T(8,128)(2,1)S(1)}, u32[]{:S(2)}, u32[]{:S(2)}) collective-permute-start(bf16[192,1024]{1,0:T(8,128)(2,1)S(1)} %get-tuple-element.43), channel_id=1, source_target_pairs={{0,1},{1,2},{2,3},{3,0},{4,5},{5,6},{6,7},{7,4},{8,9},{9,10},{10,1... | collective-permute-start | bytes 1179656 | tf_op jit(solution)/shard_map/ppermute | solution.py:326
  48.7 5.3 %collective-permute-start.12 = (bf16[192,1024]{1,0:T(8,128)(2,1)S(1)}, bf16[192,1024]{1,0:T(8,128)(2,1)S(1)}, u32[]{:S(2)}, u32[]{:S(2)}) collective-permute-start(bf16[192,1024]{1,0:T(8,128)(2,1)S(1)} %get-tuple-element.49), channel_id=1, source_target_pairs={{0,4},{4,0},{8,12},{12,8},{1,5},{5,1},{9,13},{13,9},{2,6},{6,2},{1... | collective-permute-start | bytes 1179656 | tf_op jit(solution)/shard_map/ppermute | solution.py:290
  51.1 12.0 %collective-permute-start.7 = (bf16[192,1024]{1,0:T(8,128)(2,1)S(1)}, bf16[192,1024]{1,0:T(8,128)(2,1)S(1)}, u32[]{:S(2)}, u32[]{:S(2)}) collective-permute-start(bf16[192,1024]{1,0:T(8,128)(2,1)S(1)} %shard_map.84.mine_ref.refs_2_), channel_id=1, source_target_pairs={{0,4},{4,0},{8,12},{12,8},{1,5},{5,1},{9,13},{13,9},{2,6},{6,2},{1... | collective-permute-start | bytes 1179656 | tf_op jit(solution)/shard_map/ppermute | solution.py:302
  54.0 15.9 %collective-permute-start.21 = (bf16[192,1024]{1,0:T(8,128)(2,1)S(1)}, bf16[192,1024]{1,0:T(8,128)(2,1)S(1)}, u32[]{:S(2)}, u32[]{:S(2)}) collective-permute-start(bf16[192,1024]{1,0:T(8,128)(2,1)S(1)} %collective-permute-done.20.refs_1_), channel_id=1, source_target_pairs={{0,1},{1,2},{2,3},{3,0},{4,5},{5,6},{6,7},{7,4},{8,9},{9,10},{10,1... | collective-permute-start | bytes 1179656 | tf_op jit(solution)/shard_map/ppermute | solution.py:328
  54.6 11.3 %collective-permute-start.13 = (bf16[192,1024]{1,0:T(8,128)(2,1)S(1)}, bf16[192,1024]{1,0:T(8,128)(2,1)S(1)}, u32[]{:S(2)}, u32[]{:S(2)}) collective-permute-start(bf16[192,1024]{1,0:T(8,128)(2,1)S(1)} %shard_map.92), channel_id=1, source_target_pairs={{0,8},{4,12},{8,0},{12,4},{1,9},{5,13},{9,1},{13,5},{2,10},{6,14},... | collective-permute-start | bytes 1179656 | tf_op jit(solution)/shard_map/ppermute | solution.py:296
  65.8 4.3 %copy-start.4 = (bf16[192,1024]{1,0:T(8,128)(2,1)S(1)}, bf16[192,1024]{1,0:T(8,128)(2,1)}, u32[]{:S(2)}) copy-start(bf16[192,1024]{1,0:T(8,128)(2,1)} %refs_0_.1) | copy-start | bytes 1179652
  65.8 10.7 %collective-permute-start.18 = (bf16[192,1024]{1,0:T(8,128)(2,1)S(1)}, bf16[192,1024]{1,0:T(8,128)(2,1)S(1)}, u32[]{:S(2)}, u32[]{:S(2)}) collective-permute-start(bf16[192,1024]{1,0:T(8,128)(2,1)S(1)} %shard_map.98), channel_id=1, source_target_pairs={{0,8},{4,12},{8,0},{12,4},{1,9},{5,13},{9,1},{13,5},{2,10},{6,14},... | collective-permute-start | bytes 1179656 | tf_op jit(solution)/shard_map/ppermute | solution.py:296
  67.7 10.6 %collective-permute-start.15 = (bf16[192,1024]{1,0:T(8,128)(2,1)S(1)}, bf16[192,1024]{1,0:T(8,128)(2,1)S(1)}, u32[]{:S(2)}, u32[]{:S(2)}) collective-permute-start(bf16[192,1024]{1,0:T(8,128)(2,1)S(1)} %shard_map.94.mine_ref.refs_3_), channel_id=1, source_target_pairs={{0,4},{4,0},{8,12},{12,8},{1,5},{5,1},{9,13},{13,9},{2,6},{6,2},{1... | collective-permute-start | bytes 1179656 | tf_op jit(solution)/shard_map/ppermute | solution.py:302
  67.7 13.8 %collective-permute-start.16 = (bf16[192,1024]{1,0:T(8,128)(2,1)S(1)}, bf16[192,1024]{1,0:T(8,128)(2,1)S(1)}, u32[]{:S(2)}, u32[]{:S(2)}) collective-permute-start(bf16[192,1024]{1,0:T(8,128)(2,1)S(1)} %shard_map.90), channel_id=1, source_target_pairs={{0,1},{1,2},{2,3},{3,0},{4,5},{5,6},{6,7},{7,4},{8,9},{9,10},{10,1... | collective-permute-start | bytes 1179656 | tf_op jit(solution)/shard_map/ppermute | solution.py:326
  69.9 20.0 %collective-permute-start.22 = (bf16[192,1024]{1,0:T(8,128)(2,1)S(1)}, bf16[192,1024]{1,0:T(8,128)(2,1)S(1)}, u32[]{:S(2)}, u32[]{:S(2)}) collective-permute-start(bf16[192,1024]{1,0:T(8,128)(2,1)S(1)} %collective-permute-done.21.refs_2_), channel_id=1, source_target_pairs={{0,1},{1,2},{2,3},{3,0},{4,5},{5,6},{6,7},{7,4},{8,9},{9,10},{10,1... | collective-permute-start | bytes 1179656 | tf_op jit(solution)/shard_map/ppermute | solution.py:328
  78.2 12.4 %collective-permute-start.19 = (bf16[192,1024]{1,0:T(8,128)(2,1)S(1)}, bf16[192,1024]{1,0:T(8,128)(2,1)S(1)}, u32[]{:S(2)}, u32[]{:S(2)}) collective-permute-start(bf16[192,1024]{1,0:T(8,128)(2,1)S(1)} %shard_map.100.mine_ref.refs_0_), channel_id=1, source_target_pairs={{0,4},{4,0},{8,12},{12,8},{1,5},{5,1},{9,13},{13,9},{2,6},{6,2},{1... | collective-permute-start | bytes 1179656 | tf_op jit(solution)/shard_map/ppermute | solution.py:302
  82.1 17.1 %collective-permute-start.23 = (bf16[192,1024]{1,0:T(8,128)(2,1)S(1)}, bf16[192,1024]{1,0:T(8,128)(2,1)S(1)}, u32[]{:S(2)}, u32[]{:S(2)}) collective-permute-start(bf16[192,1024]{1,0:T(8,128)(2,1)S(1)} %shard_map.97), channel_id=1, source_target_pairs={{0,1},{1,2},{2,3},{3,0},{4,5},{5,6},{6,7},{7,4},{8,9},{9,10},{10,1... | collective-permute-start | bytes 1179656 | tf_op jit(solution)/shard_map/ppermute | solution.py:340

commit v12 on v11

--- a/solution.py
+++ b/solution.py
@@ -235,15 +235,20 @@
     return call(join_kernel, place, blocks, out, 8, MOST)
 
 
-def grad_up_kernel(blocks, scale, place_ref, inputs, *refs):
+def grad_up_kernel(blocks, scale, place_ref, *refs):
+    ins, refs = refs[: -2 * blocks - 3], refs[-2 * blocks - 3 :]
     mine, pair = refs[:blocks], refs[blocks : 2 * blocks]
-    out_ref, grads = refs[2 * blocks :]
+    out_ref, inputs, grads = refs[2 * blocks :]
     tokens, half = mine[0].shape
     tile = out_ref.shape[0]
 
     @pl.when(pl.program_id(0) == 0)
     def _():
         left, right = block(core_of(place_ref), half), block(1 - core_of(place_ref), half)
+        first = 0
+        for ref in ins:
+            inputs[pl.ds(first, ref.shape[0]), :] = ref[...]
+            first += ref.shape[0]
         for s in range(blocks):
             here = pl.ds(s * tokens, tokens)
             grads[here, left] = mine[s][...]
@@ -252,20 +257,21 @@
     out_ref[...] = dot(inputs[:, block(pl.program_id(0), tile)], grads[...], FIRST) * scale
 
 
-def grad_up_call(place, inputs, mine, pair, scale):
-    total, features = inputs.shape
+def grad_up_call(place, ins, mine, pair, scale):
+    total, features = sum(x.shape[0] for x in ins), ins[0].shape[1]
     hidden = 2 * mine[0].shape[1]
     tile = tile_of(features, 256)
     return call(
         functools.partial(grad_up_kernel, len(mine), scale),
         place,
-        [inputs, *mine, *pair],
+        [*ins, *mine, *pair],
         jax.ShapeDtypeStruct((features, hidden), jnp.float32),
         18,
         MUCH,
         grid=(features // tile,),
         out_specs=pl.BlockSpec((tile, hidden), lambda i, place: (i, 0)),
         scratch=[
+            pltpu.VMEM((total, features), jnp.bfloat16),
             pltpu.VMEM((total, hidden), jnp.bfloat16),
         ],
     )
@@ -306,13 +312,15 @@
 
     cots = [cotangent]
     hidden_part(0)
+    ins = [inputs, lax.ppermute(after(inputs, place), "col", ring)]
+    near = join_call(place, ins)
     for s in range(1, cols):
         arriving = lax.ppermute(cots[s - 1], "col", ring)
         cots.append(after(arriving, sent[s - 1]) if s > 1 else after(arriving, pre, parts[0][0]))
         if s < last:
-            hidden_part(s)
+            hidden_part(s, *([near] if s == 2 else []))
             exchange(s)
-    ins = [inputs, lax.ppermute(after(inputs, cots[last - 1]), "col", ring)]
+    ins.append(lax.ppermute(after(ins[1], near, cots[last - 1]), "col", ring))
     pre_all, act = lay_out_call(place, pres)
     act_theirs = lax.ppermute(act, "row", pair)
 
@@ -325,13 +333,14 @@
     for s in range(2, cols):
         arrived = lax.ppermute(sums, "col", ring)
         pre_grad(s, *([late] if s > 2 else []))
-        ins.append(lax.ppermute(after(ins[-1], sums, mine[s]), "col", ring))
+        if s > 2:
+            ins.append(lax.ppermute(after(ins[-1], sums), "col", ring))
         first = []
         if s == last:
             grad_down = grad_down_call(
                 after(place, mine[s]), act, act_theirs, cots, scale
             )
-            pre_grad(0, grad_down)
+            pre_grad(0, grad_down, ins[s])
             first = [grad_down]
         if s == 2:
             arrived = add_call(place, arrived, [], jnp.float32, MOST)
@@ -339,7 +348,7 @@
         sums = late = add_call(place, part, [arrived], jnp.bfloat16, LITTLE)
     arrived = lax.ppermute(sums, "col", ring)
     part = share(0, sums)[0]
-    grad_up = grad_up_call(after(place, part), join_call(place, ins), mine, theirs, scale)
+    grad_up = grad_up_call(after(place, part), [near, *ins[2:]], mine, theirs, scale)
     sums = add_call(after(place, grad_up), part, [arrived], jnp.bfloat16, LITTLE)
     return (sums, grad_up, grad_down)
 

time: 101 us -> 100 us (0.990)
  waiting for transfers between devices: 37.4 us -> 33.3 us
  starting transfers between devices: 12 us -> 15.3 us
    ppermute x3, waiting for transfers between devices: 14.9 us -> 9.66 us  [per_device(): arriving = lax.ppermute(cots[s - 1], 'col', ring)]
    ppermute x3, waiting for transfers between devices: 8.74 us -> 13.1 us  [per_device(): arrived = lax.ppermute(sums, 'col', ring)]
    ppermute x3, starting transfers between devices: 0.68 us -> 2.97 us  [the longest x1 1.58 us: per_device(): ins = [inputs, lax.ppermute(after(inputs, place), 'col', ring)]]
    ppermute x4, starting transfers between devices: 3.44 us -> 5.4 us  [exchange(): others[s] = [lax.ppermute(values, 'row', to) for to in over_x]]
    ppermute x3, waiting for transfers between devices: 12.4 us -> 10.5 us  [the longest x1 6.28 us: per_device(): ins = [inputs, lax.ppermute(after(inputs, place), 'col', ring)]]
    ppermute x4, waiting for transfers between devices: 1.22 us -> 0.01 us  [hidden_part(): arrived = lax.ppermute(other, 'row', pair)]
  transfers between devices with their start and end apart: 24 -> 24, of which waited for: 9 -> 8; matrix products, arithmetic and copies ran while one was open for 0% -> 0% of each run, Pallas kernels for 44% -> 45%
where the time goes in v12:
time: 100 us; the launch traced here: 99.8 us
  Pallas kernels  45.9 us (46%)
  waiting for transfers between devices  33.3 us (33%)
  starting transfers between devices  15.3 us (15%)
  local copies, waits for them, and re-layouts  4.34 us (4%)
    pallas_call x29, Pallas kernels, call(): pl.pallas_call(kernel, out_shape=outs, grid_spec=pltpu.PrefetchScalarGrid...  45.9 us
    ppermute x3, waiting for transfers between devices, per_device(): arrived = lax.ppermute(sums, 'col', ring)  13.1 us
    ppermute x3, waiting for transfers between devices, per_device(): arriving = lax.ppermute(cots[s - 1], 'col', ring)  9.66 us
    ppermute x1, waiting for transfers between devices, per_device(): ins = [inputs, lax.ppermute(after(inputs, place), 'col', ring)]  6.28 us
    ppermute x4, starting transfers between devices, exchange(): others[s] = [lax.ppermute(values, 'row', to) for to in over_x]  5.4 us
    unnamed x14, local copies, waits for them, and re-layouts  4.34 us
    ppermute x1, waiting for transfers between devices, per_device(): ins.append(lax.ppermute(after(ins[-1], sums), 'col', ring))  4.22 us
    ppermute x3, starting transfers between devices, per_device(): arriving = lax.ppermute(cots[s - 1], 'col', ring)  2.64 us
  transfers between devices with their start and end apart: 24, of which 8 were waited for; matrix products, arithmetic and copies ran while one was open for 0% of the time, Pallas kernels for 45%

profile of v12, /device:TPU:0, one launch (start us, length us, event | category | flops | bytes accessed | tf_op | source)
XLA Modules:
  0.0 99.8 jit_solution(2587618349704627095)
XLA Ops:
  1.2 2.6 %collective-permute-start.3 = (bf16[192,1024]{1,0:T(8,128)(2,1)}, bf16[192,1024]{1,0:T(8,128)(2,1)S(1)}, u32[]{:S(2)}, u32[]{:S(2)}) collective-permute-start(bf16[192,1024]{1,0:T(8,128)(2,1)} %refs_0_.2), channel_id=1, source_target_pairs={{0,1},{1,2},{2,3},{3,0},{4,5},{5,6},{6,7},{7,4},{8,9},{9,10},{10,1... | collective-permute-start | bytes 1179656 | tf_op jit(solution)/shard_map/ppermute | solution.py:318
  3.8 1.6 %collective-permute-start.2 = (bf16[192,1024]{1,0:T(8,128)(2,1)}, bf16[192,1024]{1,0:T(8,128)(2,1)S(1)}, u32[]{:S(2)}, u32[]{:S(2)}) collective-permute-start(bf16[192,1024]{1,0:T(8,128)(2,1)} %refs_0_.1), channel_id=1, source_target_pairs={{0,1},{1,2},{2,3},{3,0},{4,5},{5,6},{6,7},{7,4},{8,9},{9,10},{10,1... | collective-permute-start | bytes 1179656 | tf_op jit(solution)/shard_map/ppermute | solution.py:315
  5.4 1.1 %copy-done.5 = bf16[192,2048]{1,0:T(8,128)(2,1)S(1)} copy-done((bf16[192,2048]{1,0:T(8,128)(2,1)S(1)}, bf16[192,2048]{1,0:T(8,128)(2,1)}, u32[]{:S(2)}) %copy-start.5) | copy-done | bytes 786456
  7.1 1.6 %collective-permute-start.1 = (bf16[384,1024]{1,0:T(8,128)(2,1)S(1)}, bf16[384,1024]{1,0:T(8,128)(2,1)S(1)}, u32[]{:S(2)}, u32[]{:S(2)}) collective-permute-start(bf16[384,1024]{1,0:T(8,128)(2,1)S(1)} %shard_map.76.refs_0_), channel_id=1, source_target_pairs={{0,8},{4,12},{8,0},{12,4},{1,9},{5,13},{9,1},{13,5},{2,10},{6,14},... | collective-permute-start | bytes 2359304 | tf_op jit(solution)/shard_map/ppermute | solution.py:291
  8.7 2.2 %copy-done = bf16[2048,1024]{1,0:T(8,128)(2,1)S(1)} copy-done((bf16[2048,1024]{1,0:T(8,128)(2,1)S(1)}, bf16[2048,1024]{1,0:T(8,128)(2,1)}, u32[]{:S(2)}) %copy-start) | copy-done | bytes 4194328
  11.9 2.1 %shard_map.79 = (f32[192,1024]{1,0:T(8,128)S(1)}, bf16[192,1024]{1,0:T(8,128)(2,1)S(1)}) custom-call(s32[2]{0:T(128)S(1)} %pad_add_fusion.place_ref, bf16[192,1024]{1,0:T(8,128)(2,1)S(1)} %copy-done.3, bf16[2048,1024]{1,0:T(8,128)(2,1)S(1)} %copy-done), custom_call_target="tpu_custom_call" | custom-call | flops 10000000 | bytes 1024 | tf_op jit(solution)/shard_map/pallas_call | solution.py:67
  14.0 2.0 %collective-permute-done.3.cot_ref.refs_1_ = bf16[192,1024]{1,0:T(8,128)(2,1)S(1)} collective-permute-done((bf16[192,1024]{1,0:T(8,128)(2,1)}, bf16[192,1024]{1,0:T(8,128)(2,1)S(1)}, u32[]{:S(2)}, u32[]{:S(2)}) %collective-permute-start.3) | collective-permute-done | bytes 393248 | tf_op jit(solution)/shard_map/ppermute | solution.py:318
  16.0 2.1 %shard_map.80 = (f32[192,1024]{1,0:T(8,128)S(1)}, bf16[192,1024]{1,0:T(8,128)(2,1)S(1)}) custom-call(s32[2]{0:T(128)S(1)} %pad_add_fusion.place_ref, bf16[192,1024]{1,0:T(8,128)(2,1)S(1)} %collective-permute-done.3.cot_ref.refs_1_, bf16[2048,1024]{1,0:T(8,128)(2,1)S(1)} %copy-done.1), custom_call_target="tpu_custom_call" | custom-call | flops 10000000 | bytes 1024 | tf_op jit(solution)/shard_map/pallas_call | solution.py:67
  18.2 6.3 %collective-permute-done.2.refs_1_ = bf16[192,1024]{1,0:T(8,128)(2,1)S(1)} collective-permute-done((bf16[192,1024]{1,0:T(8,128)(2,1)}, bf16[192,1024]{1,0:T(8,128)(2,1)S(1)}, u32[]{:S(2)}, u32[]{:S(2)}) %collective-permute-start.2) | collective-permute-done | bytes 393248 | tf_op jit(solution)/shard_map/ppermute | solution.py:315
  25.7 1.7 %collective-permute-start.9 = (bf16[192,1024]{1,0:T(8,128)(2,1)S(1)}, bf16[192,1024]{1,0:T(8,128)(2,1)S(1)}, u32[]{:S(2)}, u32[]{:S(2)}) collective-permute-start(bf16[192,1024]{1,0:T(8,128)(2,1)S(1)} %shard_map.81), channel_id=1, source_target_pairs={{0,8},{4,12},{8,0},{12,4},{1,9},{5,13},{9,1},{13,5},{2,10},{6,14},... | collective-permute-start | bytes 1179656 | tf_op jit(solution)/shard_map/ppermute | solution.py:302
  27.4 5.3 %collective-permute-done.4.cot_ref.refs_2_ = bf16[192,1024]{1,0:T(8,128)(2,1)S(1)} collective-permute-done((bf16[192,1024]{1,0:T(8,128)(2,1)S(1)}, bf16[192,1024]{1,0:T(8,128)(2,1)S(1)}, u32[]{:S(2)}, u32[]{:S(2)}) %collective-permute-start.4) | collective-permute-done | bytes 393248 | tf_op jit(solution)/shard_map/ppermute | solution.py:318
  32.6 2.1 %shard_map.82 = (f32[192,1024]{1,0:T(8,128)S(1)}, bf16[192,1024]{1,0:T(8,128)(2,1)S(1)}) custom-call(s32[2]{0:T(128)S(1)} %pad_add_fusion.place_ref, bf16[192,1024]{1,0:T(8,128)(2,1)S(1)} %collective-permute-done.4.cot_ref.refs_2_, bf16[2048,1024]{1,0:T(8,128)(2,1)S(1)} %copy-done.1), custom_call_target="tpu_custom_call" | custom-call | flops 10000000 | bytes 1024 | tf_op jit(solution)/shard_map/pallas_call | solution.py:67
  34.8 1.7 %shard_map.77 = (bf16[768,1024]{1,0:T(8,128)(2,1)S(1)}, bf16[768,1024]{1,0:T(8,128)(2,1)S(1)}) custom-call(s32[2]{0:T(128)S(1)} %pad_add_fusion.place_ref, bf16[384,1024]{1,0:T(8,128)(2,1)S(1)} %shard_map.76.refs_0_, bf16[384,1024]{1,0:T(8,128)(2,1)S(1)} %collective-permute-done.1.refs_1_), custom_call_target="tpu_custom_call" | custom-call | flops 6000000000 | bytes 1024 | tf_op jit(solution)/shard_map/pallas_call | solution.py:67
  37.1 1.1 %shard_map.88.mine_ref.refs_4_ = bf16[192,1024]{1,0:T(8,128)(2,1)S(1)} custom-call(s32[2]{0:T(128)S(1)} %pad_add_fusion.place_ref, bf16[768,1024]{1,0:T(8,128)(2,1)S(1)} %get-tuple-element.35.pre_ref, f32[192,1024]{1,0:T(8,128)S(1)} %shard_map.87.part_ref), custom_call_target="tpu_custom_call" | custom-call | flops 100000000 | bytes 1024 | tf_op jit(solution)/shard_map/pallas_call | solution.py:67
  39.4 1.6 %collective-permute-start.7 = (bf16[192,1024]{1,0:T(8,128)(2,1)S(1)}, bf16[192,1024]{1,0:T(8,128)(2,1)S(1)}, u32[]{:S(2)}, u32[]{:S(2)}) collective-permute-start(bf16[192,1024]{1,0:T(8,128)(2,1)S(1)} %shard_map.83), channel_id=1, source_target_pairs={{0,8},{4,12},{8,0},{12,4},{1,9},{5,13},{9,1},{13,5},{2,10},{6,14},... | collective-permute-start | bytes 1179656 | tf_op jit(solution)/shard_map/ppermute | solution.py:302
  41.6 1.3 %collective-permute-start.18 = (bf16[192,1024]{1,0:T(8,128)(2,1)S(1)}, bf16[192,1024]{1,0:T(8,128)(2,1)S(1)}, u32[]{:S(2)}, u32[]{:S(2)}) collective-permute-start(bf16[192,1024]{1,0:T(8,128)(2,1)S(1)} %collective-permute-done.2.refs_1_), channel_id=1, source_target_pairs={{0,1},{1,2},{2,3},{3,0},{4,5},{5,6},{6,7},{7,4},{8,9},{9,10},{10,1... | collective-permute-start | bytes 1179656 | tf_op jit(solution)/shard_map/ppermute | solution.py:323
  42.9 2.4 %collective-permute-done.12.cot_ref.refs_3_ = bf16[192,1024]{1,0:T(8,128)(2,1)S(1)} collective-permute-done((bf16[192,1024]{1,0:T(8,128)(2,1)S(1)}, bf16[192,1024]{1,0:T(8,128)(2,1)S(1)}, u32[]{:S(2)}, u32[]{:S(2)}) %collective-permute-start.12) | collective-permute-done | bytes 393248 | tf_op jit(solution)/shard_map/ppermute | solution.py:318
  45.3 3.0 %shard_map.89 = (f32[192,1024]{1,0:T(8,128)}, bf16[192,1024]{1,0:T(8,128)(2,1)S(1)}) custom-call(s32[2]{0:T(128)S(1)} %pad_add_fusion.place_ref, bf16[192,1024]{1,0:T(8,128)(2,1)S(1)} %shard_map.88.mine_ref.refs_4_, bf16[192,1024]{1,0:T(8,128)(2,1)S(1)} %collective-permute-done.10.theirs_ref.refs_8_, bf16[1024,2048]{1,0:T(8,128)(2,1)S(1)} %copy-done.2), custom_call_target="tpu_custom_call" | custom-call | flops 10000000 | bytes 1024 | tf_op jit(solution)/shard_map/pallas_call | solution.py:67
  48.3 2.1 %shard_map.92 = (f32[192,1024]{1,0:T(8,128)S(1)}, bf16[192,1024]{1,0:T(8,128)(2,1)S(1)}) custom-call(s32[2]{0:T(128)S(1)} %pad_add_fusion.place_ref, bf16[192,1024]{1,0:T(8,128)(2,1)S(1)} %collective-permute-done.12.cot_ref.refs_3_, bf16[2048,1024]{1,0:T(8,128)(2,1)S(1)} %copy-done.1), custom_call_target="tpu_custom_call" | custom-call | flops 10000000 | bytes 1024 | tf_op jit(solution)/shard_map/pallas_call | solution.py:67
  51.6 1.1 %shard_map.85.mine_ref.refs_5_ = bf16[192,1024]{1,0:T(8,128)(2,1)S(1)} custom-call(s32[2]{0:T(128)S(1)} %pad_add_fusion.place_ref, bf16[768,1024]{1,0:T(8,128)(2,1)S(1)} %get-tuple-element.35.pre_ref, f32[192,1024]{1,0:T(8,128)S(1)} %shard_map.84.part_ref), custom_call_target="tpu_custom_call" | custom-call | flops 100000000 | bytes 1024 | tf_op jit(solution)/shard_map/pallas_call | solution.py:67
  53.3 1.4 %collective-permute-start.14 = (bf16[192,1024]{1,0:T(8,128)(2,1)S(1)}, bf16[192,1024]{1,0:T(8,128)(2,1)S(1)}, u32[]{:S(2)}, u32[]{:S(2)}) collective-permute-start(bf16[192,1024]{1,0:T(8,128)(2,1)S(1)} %shard_map.93), channel_id=1, source_target_pairs={{0,8},{4,12},{8,0},{12,4},{1,9},{5,13},{9,1},{13,5},{2,10},{6,14},... | collective-permute-start | bytes 1179656 | tf_op jit(solution)/shard_map/ppermute | solution.py:302
  54.8 8.1 %collective-permute-done.11.part_ref = bf16[192,1024]{1,0:T(8,128)(2,1)S(1)} collective-permute-done((bf16[192,1024]{1,0:T(8,128)(2,1)S(1)}, bf16[192,1024]{1,0:T(8,128)(2,1)S(1)}, u32[]{:S(2)}, u32[]{:S(2)}) %collective-permute-start.11) | collective-permute-done | bytes 393248 | tf_op jit(solution)/shard_map/ppermute | solution.py:334
  63.5 2.1 %shard_map.86.part_ref = f32[192,1024]{1,0:T(8,128)S(1)} custom-call(s32[2]{0:T(128)S(1)} %pad_add_fusion.place_ref, bf16[192,1024]{1,0:T(8,128)(2,1)S(1)} %shard_map.85.mine_ref.refs_5_, bf16[192,1024]{1,0:T(8,128)(2,1)S(1)} %collective-permute-done.8.theirs_ref.refs_9_, bf16[1024,2048]{1,0:T(8,128)(2,1)S(1)} %copy-done.2), custom_call_target="tpu_custom_call" | custom-call | flops 10000000 | bytes 1024 | tf_op jit(solution)/shard_map/pallas_call | solution.py:67
  68.2 1.1 %shard_map.95.mine_ref.refs_6_ = bf16[192,1024]{1,0:T(8,128)(2,1)S(1)} custom-call(s32[2]{0:T(128)S(1)} %pad_add_fusion.place_ref, bf16[768,1024]{1,0:T(8,128)(2,1)S(1)} %get-tuple-element.35.pre_ref, f32[192,1024]{1,0:T(8,128)S(1)} %shard_map.94.part_ref), custom_call_target="tpu_custom_call" | custom-call | flops 100000000 | bytes 1024 | tf_op jit(solution)/shard_map/pallas_call | solution.py:67
  69.4 6.5 %shard_map.96 = f32[2048,1024]{1,0:T(8,128)} custom-call(s32[2]{0:T(128)S(1)} %pad_add_fusion.place_ref, bf16[768,1024]{1,0:T(8,128)(2,1)S(1)} %get-tuple-element.55.mine_ref, bf16[768,1024]{1,0:T(8,128)(2,1)S(1)} %collective-permute-done.15.theirs_ref, bf16[192,1024]{1,0:T(8,128)(2,1)S(1)} %copy-done.4, ...), custom_call_target="tpu_custom_call" | custom-call | flops 100000000 | bytes 1024 | tf_op jit(solution)/shard_map/pallas_call | solution.py:67
  75.9 4.2 %collective-permute-done.19.refs_2_ = bf16[192,1024]{1,0:T(8,128)(2,1)S(1)} collective-permute-done((bf16[192,1024]{1,0:T(8,128)(2,1)S(1)}, bf16[192,1024]{1,0:T(8,128)(2,1)S(1)}, u32[]{:S(2)}, u32[]{:S(2)}) %collective-permute-start.19) | collective-permute-done | bytes 393248 | tf_op jit(solution)/shard_map/ppermute | solution.py:337
  81.9 2.1 %shard_map.97.part_ref = f32[192,1024]{1,0:T(8,128)S(1)} custom-call(s32[2]{0:T(128)S(1)} %pad_add_fusion.place_ref, bf16[192,1024]{1,0:T(8,128)(2,1)S(1)} %shard_map.95.mine_ref.refs_6_, bf16[192,1024]{1,0:T(8,128)(2,1)S(1)} %collective-permute-done.16.theirs_ref.refs_10_, bf16[1024,2048]{1,0:T(8,128)(2,1)S(1)} %copy-done.2), custom_call_target="tpu_custom_call" | custom-call | flops 10000000 | bytes 1024 | tf_op jit(solution)/shard_map/pallas_call | solution.py:67
  84.0 2.7 %collective-permute-done.17.refs_0_ = bf16[192,1024]{1,0:T(8,128)(2,1)S(1)} collective-permute-done((bf16[192,1024]{1,0:T(8,128)(2,1)S(1)}, bf16[192,1024]{1,0:T(8,128)(2,1)S(1)}, u32[]{:S(2)}, u32[]{:S(2)}) %collective-permute-start.17) | collective-permute-done | bytes 393248 | tf_op jit(solution)/shard_map/ppermute | solution.py:334
  87.4 2.1 %shard_map.102.part_ref = f32[192,1024]{1,0:T(8,128)S(1)} custom-call(s32[2]{0:T(128)S(1)} %pad_add_fusion.place_ref, bf16[192,1024]{1,0:T(8,128)(2,1)S(1)} %shard_map.101.mine_ref.refs_3_, bf16[192,1024]{1,0:T(8,128)(2,1)S(1)} %collective-permute-done.22.theirs_ref.refs_7_, bf16[1024,2048]{1,0:T(8,128)(2,1)S(1)} %copy-done.2), custom_call_target="tpu_custom_call" | custom-call | flops 10000000 | bytes 1024 | tf_op jit(solution)/shard_map/pallas_call | solution.py:67
  89.4 6.6 %shard_map.103 = f32[1024,2048]{1,0:T(8,128)} custom-call(s32[2]{0:T(128)S(1)} %pad_add_fusion.place_ref, bf16[384,1024]{1,0:T(8,128)(2,1)S(1)} %shard_map.78.refs_0_, bf16[192,1024]{1,0:T(8,128)(2,1)S(1)} %collective-permute-done.18.refs_1_, bf16[192,1024]{1,0:T(8,128)(2,1)S(1)} %collective-permute-done.19.refs_2_, ...), custom_call_target="tpu_custom_call" | custom-call | flops 3000000000 | bytes 1024 | tf_op jit(solution)/shard_map/pallas_call | solution.py:67
  96.1 2.3 %collective-permute-done.23.refs_0_ = bf16[192,1024]{1,0:T(8,128)(2,1)S(1)} collective-permute-done((bf16[192,1024]{1,0:T(8,128)(2,1)S(1)}, bf16[192,1024]{1,0:T(8,128)(2,1)S(1)}, u32[]{:S(2)}, u32[]{:S(2)}) %collective-permute-start.23) | collective-permute-done | bytes 393248 | tf_op jit(solution)/shard_map/ppermute | solution.py:349
  98.4 1.4 %shard_map.104 = bf16[192,1024]{1,0:T(8,128)(2,1)} custom-call(s32[2]{0:T(128)S(1)} %pad_add_fusion.place_ref, f32[192,1024]{1,0:T(8,128)S(1)} %shard_map.102.part_ref, bf16[192,1024]{1,0:T(8,128)(2,1)S(1)} %collective-permute-done.23.refs_0_), custom_call_target="tpu_custom_call" | custom-call | flops 10000000 | bytes 1024 | tf_op jit(solution)/shard_map/pallas_call | solution.py:67
  (60 shorter events, 13.7 us)
Async XLA Ops:
  0.7 4.7 %collective-permute-start = (bf16[192,2048]{1,0:T(8,128)(2,1)}, bf16[192,2048]{1,0:T(8,128)(2,1)S(1)}, u32[]{:S(2)}, u32[]{:S(2)}) collective-permute-start(bf16[192,2048]{1,0:T(8,128)(2,1)} %mine_ref), channel_id=1, source_target_pairs={{0,4},{4,0},{8,12},{12,8},{1,5},{5,1},{9,13},{13,9},{2,6},{6,2},{1... | collective-permute-start | bytes 2359304 | tf_op jit(solution)/shard_map/ppermute | solution.py:290
  1.2 14.8 %collective-permute-start.3 = (bf16[192,1024]{1,0:T(8,128)(2,1)}, bf16[192,1024]{1,0:T(8,128)(2,1)S(1)}, u32[]{:S(2)}, u32[]{:S(2)}) collective-permute-start(bf16[192,1024]{1,0:T(8,128)(2,1)} %refs_0_.2), channel_id=1, source_target_pairs={{0,1},{1,2},{2,3},{3,0},{4,5},{5,6},{6,7},{7,4},{8,9},{9,10},{10,1... | collective-permute-start | bytes 1179656 | tf_op jit(solution)/shard_map/ppermute | solution.py:318
  3.8 20.6 %collective-permute-start.2 = (bf16[192,1024]{1,0:T(8,128)(2,1)}, bf16[192,1024]{1,0:T(8,128)(2,1)S(1)}, u32[]{:S(2)}, u32[]{:S(2)}) collective-permute-start(bf16[192,1024]{1,0:T(8,128)(2,1)} %refs_0_.1), channel_id=1, source_target_pairs={{0,1},{1,2},{2,3},{3,0},{4,5},{5,6},{6,7},{7,4},{8,9},{9,10},{10,1... | collective-permute-start | bytes 1179656 | tf_op jit(solution)/shard_map/ppermute | solution.py:315
  5.4 1.1 %copy-start.5 = (bf16[192,2048]{1,0:T(8,128)(2,1)S(1)}, bf16[192,2048]{1,0:T(8,128)(2,1)}, u32[]{:S(2)}) copy-start(bf16[192,2048]{1,0:T(8,128)(2,1)} %mine_ref) | copy-start | bytes 2359300
  7.1 27.6 %collective-permute-start.1 = (bf16[384,1024]{1,0:T(8,128)(2,1)S(1)}, bf16[384,1024]{1,0:T(8,128)(2,1)S(1)}, u32[]{:S(2)}, u32[]{:S(2)}) collective-permute-start(bf16[384,1024]{1,0:T(8,128)(2,1)S(1)} %shard_map.76.refs_0_), channel_id=1, source_target_pairs={{0,8},{4,12},{8,0},{12,4},{1,9},{5,13},{9,1},{13,5},{2,10},{6,14},... | collective-permute-start | bytes 2359304 | tf_op jit(solution)/shard_map/ppermute | solution.py:291
  8.7 2.2 %copy-start = (bf16[2048,1024]{1,0:T(8,128)(2,1)S(1)}, bf16[2048,1024]{1,0:T(8,128)(2,1)}, u32[]{:S(2)}) copy-start(bf16[2048,1024]{1,0:T(8,128)(2,1)} %down_ref.7) | copy-start | bytes 12582916
  10.9 1.0 copy-start.3
  11.9 4.2 %copy-start.1 = (bf16[2048,1024]{1,0:T(8,128)(2,1)S(1)}, bf16[2048,1024]{1,0:T(8,128)(2,1)}, u32[]{:S(2)}) copy-start(bf16[2048,1024]{1,0:T(8,128)(2,1)} %down_ref.7) | copy-start | bytes 12582916
  11.9 12.6 %copy-start.6 = (bf16[192,1024]{1,0:T(8,128)(2,1)S(1)}, bf16[192,1024]{1,0:T(8,128)(2,1)}, u32[]{:S(2)}) copy-start(bf16[192,1024]{1,0:T(8,128)(2,1)} %refs_0_.1) | copy-start | bytes 1179652
  13.9 27.0 %collective-permute-start.20 = (bf16[192,1024]{1,0:T(8,128)(2,1)S(1)}, bf16[192,1024]{1,0:T(8,128)(2,1)S(1)}, u32[]{:S(2)}, u32[]{:S(2)}) collective-permute-start(bf16[192,1024]{1,0:T(8,128)(2,1)S(1)} %get-tuple-element.61), channel_id=1, source_target_pairs={{0,4},{4,0},{8,12},{12,8},{1,5},{5,1},{9,13},{13,9},{2,6},{6,2},{1... | collective-permute-start | bytes 1179656 | tf_op jit(solution)/shard_map/ppermute | solution.py:296
  16.0 16.6 %collective-permute-start.4 = (bf16[192,1024]{1,0:T(8,128)(2,1)S(1)}, bf16[192,1024]{1,0:T(8,128)(2,1)S(1)}, u32[]{:S(2)}, u32[]{:S(2)}) collective-permute-start(bf16[192,1024]{1,0:T(8,128)(2,1)S(1)} %collective-permute-done.3.cot_ref.refs_1_), channel_id=1, source_target_pairs={{0,1},{1,2},{2,3},{3,0},{4,5},{5,6},{6,7},{7,4},{8,9},{9,10},{10,1... | collective-permute-start | bytes 1179656 | tf_op jit(solution)/shard_map/ppermute | solution.py:318
  18.1 7.0 %collective-permute-start.5 = (bf16[192,1024]{1,0:T(8,128)(2,1)S(1)}, bf16[192,1024]{1,0:T(8,128)(2,1)S(1)}, u32[]{:S(2)}, u32[]{:S(2)}) collective-permute-start(bf16[192,1024]{1,0:T(8,128)(2,1)S(1)} %get-tuple-element.42), channel_id=1, source_target_pairs={{0,4},{4,0},{8,12},{12,8},{1,5},{5,1},{9,13},{13,9},{2,6},{6,2},{1... | collective-permute-start | bytes 1179656 | tf_op jit(solution)/shard_map/ppermute | solution.py:296
  25.7 10.8 %collective-permute-start.9 = (bf16[192,1024]{1,0:T(8,128)(2,1)S(1)}, bf16[192,1024]{1,0:T(8,128)(2,1)S(1)}, u32[]{:S(2)}, u32[]{:S(2)}) collective-permute-start(bf16[192,1024]{1,0:T(8,128)(2,1)S(1)} %shard_map.81), channel_id=1, source_target_pairs={{0,8},{4,12},{8,0},{12,4},{1,9},{5,13},{9,1},{13,5},{2,10},{6,14},... | collective-permute-start | bytes 1179656 | tf_op jit(solution)/shard_map/ppermute | solution.py:302
  32.6 12.7 %collective-permute-start.12 = (bf16[192,1024]{1,0:T(8,128)(2,1)S(1)}, bf16[192,1024]{1,0:T(8,128)(2,1)S(1)}, u32[]{:S(2)}, u32[]{:S(2)}) collective-permute-start(bf16[192,1024]{1,0:T(8,128)(2,1)S(1)} %collective-permute-done.4.cot_ref.refs_2_), channel_id=1, source_target_pairs={{0,1},{1,2},{2,3},{3,0},{4,5},{5,6},{6,7},{7,4},{8,9},{9,10},{10,1... | collective-permute-start | bytes 1179656 | tf_op jit(solution)/shard_map/ppermute | solution.py:318
  34.7 4.1 %collective-permute-start.6 = (bf16[192,1024]{1,0:T(8,128)(2,1)S(1)}, bf16[192,1024]{1,0:T(8,128)(2,1)S(1)}, u32[]{:S(2)}, u32[]{:S(2)}) collective-permute-start(bf16[192,1024]{1,0:T(8,128)(2,1)S(1)} %get-tuple-element.45), channel_id=1, source_target_pairs={{0,4},{4,0},{8,12},{12,8},{1,5},{5,1},{9,13},{13,9},{2,6},{6,2},{1... | collective-permute-start | bytes 1179656 | tf_op jit(solution)/shard_map/ppermute | solution.py:296
  37.1 8.2 %copy-start.2 = (bf16[1024,2048]{1,0:T(8,128)(2,1)S(1)}, bf16[1024,2048]{1,0:T(8,128)(2,1)}, u32[]{:S(2)}) copy-start(bf16[1024,2048]{1,0:T(8,128)(2,1)} %up_ref.7) | copy-start | bytes 12582916
  38.2 7.1 %collective-permute-start.10 = (bf16[192,1024]{1,0:T(8,128)(2,1)S(1)}, bf16[192,1024]{1,0:T(8,128)(2,1)S(1)}, u32[]{:S(2)}, u32[]{:S(2)}) collective-permute-start(bf16[192,1024]{1,0:T(8,128)(2,1)S(1)} %shard_map.88.mine_ref.refs_4_), channel_id=1, source_target_pairs={{0,4},{4,0},{8,12},{12,8},{1,5},{5,1},{9,13},{13,9},{2,6},{6,2},{1... | collective-permute-start | bytes 1179656 | tf_op jit(solution)/shard_map/ppermute | solution.py:308
  39.4 11.5 %collective-permute-start.7 = (bf16[192,1024]{1,0:T(8,128)(2,1)S(1)}, bf16[192,1024]{1,0:T(8,128)(2,1)S(1)}, u32[]{:S(2)}, u32[]{:S(2)}) collective-permute-start(bf16[192,1024]{1,0:T(8,128)(2,1)S(1)} %shard_map.83), channel_id=1, source_target_pairs={{0,8},{4,12},{8,0},{12,4},{1,9},{5,13},{9,1},{13,5},{2,10},{6,14},... | collective-permute-start | bytes 1179656 | tf_op jit(solution)/shard_map/ppermute | solution.py:302
  41.6 24.6 %collective-permute-start.18 = (bf16[192,1024]{1,0:T(8,128)(2,1)S(1)}, bf16[192,1024]{1,0:T(8,128)(2,1)S(1)}, u32[]{:S(2)}, u32[]{:S(2)}) collective-permute-start(bf16[192,1024]{1,0:T(8,128)(2,1)S(1)} %collective-permute-done.2.refs_1_), channel_id=1, source_target_pairs={{0,1},{1,2},{2,3},{3,0},{4,5},{5,6},{6,7},{7,4},{8,9},{9,10},{10,1... | collective-permute-start | bytes 1179656 | tf_op jit(solution)/shard_map/ppermute | solution.py:323
  45.3 24.1 %collective-permute-start.15 = (bf16[768,1024]{1,0:T(8,128)(2,1)S(1)}, bf16[768,1024]{1,0:T(8,128)(2,1)S(1)}, u32[]{:S(2)}, u32[]{:S(2)}) collective-permute-start(bf16[768,1024]{1,0:T(8,128)(2,1)S(1)} %get-tuple-element.55.mine_ref), channel_id=1, source_target_pairs={{0,4},{4,0},{8,12},{12,8},{1,5},{5,1},{9,13},{13,9},{2,6},{6,2},{1... | collective-permute-start | bytes 4718600 | tf_op jit(solution)/shard_map/ppermute | solution.py:325
  48.3 14.6 %collective-permute-start.11 = (bf16[192,1024]{1,0:T(8,128)(2,1)S(1)}, bf16[192,1024]{1,0:T(8,128)(2,1)S(1)}, u32[]{:S(2)}, u32[]{:S(2)}) collective-permute-start(bf16[192,1024]{1,0:T(8,128)(2,1)S(1)} %get-tuple-element.47), channel_id=1, source_target_pairs={{0,1},{1,2},{2,3},{3,0},{4,5},{5,6},{6,7},{7,4},{8,9},{9,10},{10,1... | collective-permute-start | bytes 1179656 | tf_op jit(solution)/shard_map/ppermute | solution.py:334
  50.3 2.4 %collective-permute-start.13 = (bf16[192,1024]{1,0:T(8,128)(2,1)S(1)}, bf16[192,1024]{1,0:T(8,128)(2,1)S(1)}, u32[]{:S(2)}, u32[]{:S(2)}) collective-permute-start(bf16[192,1024]{1,0:T(8,128)(2,1)S(1)} %get-tuple-element.53), channel_id=1, source_target_pairs={{0,4},{4,0},{8,12},{12,8},{1,5},{5,1},{9,13},{13,9},{2,6},{6,2},{1... | collective-permute-start | bytes 1179656 | tf_op jit(solution)/shard_map/ppermute | solution.py:296
  52.6 10.8 %collective-permute-start.8 = (bf16[192,1024]{1,0:T(8,128)(2,1)S(1)}, bf16[192,1024]{1,0:T(8,128)(2,1)S(1)}, u32[]{:S(2)}, u32[]{:S(2)}) collective-permute-start(bf16[192,1024]{1,0:T(8,128)(2,1)S(1)} %shard_map.85.mine_ref.refs_5_), channel_id=1, source_target_pairs={{0,4},{4,0},{8,12},{12,8},{1,5},{5,1},{9,13},{13,9},{2,6},{6,2},{1... | collective-permute-start | bytes 1179656 | tf_op jit(solution)/shard_map/ppermute | solution.py:308
  53.3 14.2 %collective-permute-start.14 = (bf16[192,1024]{1,0:T(8,128)(2,1)S(1)}, bf16[192,1024]{1,0:T(8,128)(2,1)S(1)}, u32[]{:S(2)}, u32[]{:S(2)}) collective-permute-start(bf16[192,1024]{1,0:T(8,128)(2,1)S(1)} %shard_map.93), channel_id=1, source_target_pairs={{0,8},{4,12},{8,0},{12,4},{1,9},{5,13},{9,1},{13,5},{2,10},{6,14},... | collective-permute-start | bytes 1179656 | tf_op jit(solution)/shard_map/ppermute | solution.py:302
  66.2 3.2 %copy-start.4 = (bf16[192,1024]{1,0:T(8,128)(2,1)S(1)}, bf16[192,1024]{1,0:T(8,128)(2,1)}, u32[]{:S(2)}) copy-start(bf16[192,1024]{1,0:T(8,128)(2,1)} %refs_0_.2) | copy-start | bytes 1179652
  66.2 13.9 %collective-permute-start.19 = (bf16[192,1024]{1,0:T(8,128)(2,1)S(1)}, bf16[192,1024]{1,0:T(8,128)(2,1)S(1)}, u32[]{:S(2)}, u32[]{:S(2)}) collective-permute-start(bf16[192,1024]{1,0:T(8,128)(2,1)S(1)} %collective-permute-done.18.refs_1_), channel_id=1, source_target_pairs={{0,1},{1,2},{2,3},{3,0},{4,5},{5,6},{6,7},{7,4},{8,9},{9,10},{10,1... | collective-permute-start | bytes 1179656 | tf_op jit(solution)/shard_map/ppermute | solution.py:337
  66.3 13.8 %collective-permute-start.21 = (bf16[192,1024]{1,0:T(8,128)(2,1)S(1)}, bf16[192,1024]{1,0:T(8,128)(2,1)S(1)}, u32[]{:S(2)}, u32[]{:S(2)}) collective-permute-start(bf16[192,1024]{1,0:T(8,128)(2,1)S(1)} %shard_map.99), channel_id=1, source_target_pairs={{0,8},{4,12},{8,0},{12,4},{1,9},{5,13},{9,1},{13,5},{2,10},{6,14},... | collective-permute-start | bytes 1179656 | tf_op jit(solution)/shard_map/ppermute | solution.py:302
  67.0 19.7 %collective-permute-start.17 = (bf16[192,1024]{1,0:T(8,128)(2,1)S(1)}, bf16[192,1024]{1,0:T(8,128)(2,1)S(1)}, u32[]{:S(2)}, u32[]{:S(2)}) collective-permute-start(bf16[192,1024]{1,0:T(8,128)(2,1)S(1)} %shard_map.91), channel_id=1, source_target_pairs={{0,1},{1,2},{2,3},{3,0},{4,5},{5,6},{6,7},{7,4},{8,9},{9,10},{10,1... | collective-permute-start | bytes 1179656 | tf_op jit(solution)/shard_map/ppermute | solution.py:334
  69.3 12.6 %collective-permute-start.16 = (bf16[192,1024]{1,0:T(8,128)(2,1)S(1)}, bf16[192,1024]{1,0:T(8,128)(2,1)S(1)}, u32[]{:S(2)}, u32[]{:S(2)}) collective-permute-start(bf16[192,1024]{1,0:T(8,128)(2,1)S(1)} %shard_map.95.mine_ref.refs_6_), channel_id=1, source_target_pairs={{0,4},{4,0},{8,12},{12,8},{1,5},{5,1},{9,13},{13,9},{2,6},{6,2},{1... | collective-permute-start | bytes 1179656 | tf_op jit(solution)/shard_map/ppermute | solution.py:308
  81.8 5.5 %collective-permute-start.22 = (bf16[192,1024]{1,0:T(8,128)(2,1)S(1)}, bf16[192,1024]{1,0:T(8,128)(2,1)S(1)}, u32[]{:S(2)}, u32[]{:S(2)}) collective-permute-start(bf16[192,1024]{1,0:T(8,128)(2,1)S(1)} %shard_map.101.mine_ref.refs_3_), channel_id=1, source_target_pairs={{0,4},{4,0},{8,12},{12,8},{1,5},{5,1},{9,13},{13,9},{2,6},{6,2},{1... | collective-permute-start | bytes 1179656 | tf_op jit(solution)/shard_map/ppermute | solution.py:308
  87.3 11.1 %collective-permute-start.23 = (bf16[192,1024]{1,0:T(8,128)(2,1)S(1)}, bf16[192,1024]{1,0:T(8,128)(2,1)S(1)}, u32[]{:S(2)}, u32[]{:S(2)}) collective-permute-start(bf16[192,1024]{1,0:T(8,128)(2,1)S(1)} %shard_map.98), channel_id=1, source_target_pairs={{0,1},{1,2},{2,3},{3,0},{4,5},{5,6},{6,7},{7,4},{8,9},{9,10},{10,1... | collective-permute-start | bytes 1179656 | tf_op jit(solution)/shard_map/ppermute | solution.py:349

commit v13 on v12

--- a/solution.py
+++ b/solution.py
@@ -52,8 +52,15 @@
     return pl.ds(pl.multiple_of(index * size + first, math.gcd(size, first)), size - first)
 
 
+def ring_order(cols):
+    return [*range(0, cols, 2), *reversed(range(1, cols, 2))]
+
+
 def block_at(place_ref, step, cols):
-    return lax.rem(place_ref[0] - step + cols, cols)
+    z = place_ref[0]
+    turn = jnp.where(lax.rem(z, 2) == 0, lax.div(z, 2), cols - lax.div(z + 1, 2))
+    turn = lax.rem(turn - step + cols, cols)
+    return jnp.where(2 * turn < cols, 2 * turn, 2 * (cols - turn) - 1)
 
 
 def core_of(place_ref):
@@ -281,7 +288,8 @@
     cols, rows = lax.axis_size("col"), lax.axis_size("row")
     place = jnp.stack([lax.axis_index("col"), lax.axis_index("row")]).astype(jnp.int32)
     cotangent, preactivation = after(cotangent, place), after(preactivation, place)
-    ring = [(i, (i + 1) % cols) for i in range(cols)]
+    stops = ring_order(cols)
+    ring = [(z, stops[(i + 1) % cols]) for i, z in enumerate(stops)]
     pair = [(i, i ^ 1) for i in range(rows)]
     over_x = [[(i, (i + shift) % rows) for i in range(rows)] for shift in range(2, rows, 2)]
     scale = 1.0 / math.sqrt(cotangent.shape[0] * cols)

time: 100 us -> 97.6 us (0.976)
  waiting for transfers between devices: 33.3 us -> 19 us
  starting transfers between devices: 15.3 us -> 27 us
    ppermute x3, starting transfers between devices: 2.64 us -> 9.84 us  [per_device(): arriving = lax.ppermute(cots[s - 1], 'col', ring)]
    ppermute x3, waiting for transfers between devices: 9.66 us -> 5.08 us  [per_device(): arriving = lax.ppermute(cots[s - 1], 'col', ring)]
    ppermute x3, waiting for transfers between devices: 13.1 us -> 8.64 us  [per_device(): arrived = lax.ppermute(sums, 'col', ring)]
    ppermute x3, starting transfers between devices: 0.68 us -> 4.76 us  [per_device(): arrived = lax.ppermute(sums, 'col', ring)]
    ppermute x1, waiting for transfers between devices: 6.28 us -> 3 us  [per_device(): ins = [inputs, lax.ppermute(after(inputs, place), 'col', ring)]]
    ppermute x1, waiting for transfers between devices: 4.22 us -> 1.27 us  [per_device(): ins.append(lax.ppermute(after(ins[-1], sums), 'col', ring))]
    ppermute x1, starting transfers between devices: 0.06 us -> 1.62 us  [per_device(): ins.append(lax.ppermute(after(ins[-1], sums), 'col', ring))]
  transfers between devices with their start and end apart: 24 -> 24, of which waited for: 8 -> 6; matrix products, arithmetic and copies ran while one was open for 0% -> 0% of each run, Pallas kernels for 45% -> 46%
where the time goes in v13:
time: 97.6 us; the launch traced here: 97.3 us
  Pallas kernels  45.9 us (47%)
  starting transfers between devices  27 us (28%)
  waiting for transfers between devices  19 us (19%)
  local copies, waits for them, and re-layouts  4.34 us (4%)
  between operations  0.98 us (1%)
    pallas_call x29, Pallas kernels, call(): pl.pallas_call(kernel, out_shape=outs, grid_spec=pltpu.PrefetchScalarGrid...  45.9 us
    ppermute x3, starting transfers between devices, per_device(): arriving = lax.ppermute(cots[s - 1], 'col', ring)  9.84 us
    ppermute x3, waiting for transfers between devices, per_device(): arrived = lax.ppermute(sums, 'col', ring)  8.64 us
    ppermute x4, starting transfers between devices, exchange(): others[s] = [lax.ppermute(values, 'row', to) for to in over_x]  5.22 us
    ppermute x3, waiting for transfers between devices, per_device(): arriving = lax.ppermute(cots[s - 1], 'col', ring)  5.08 us
    ppermute x3, starting transfers between devices, per_device(): arrived = lax.ppermute(sums, 'col', ring)  4.76 us
    unnamed x14, local copies, waits for them, and re-layouts  4.34 us
    ppermute x1, waiting for transfers between devices, per_device(): ins = [inputs, lax.ppermute(after(inputs, place), 'col', ring)]  3 us
  transfers between devices with their start and end apart: 24, of which 6 were waited for; matrix products, arithmetic and copies ran while one was open for 0% of the time, Pallas kernels for 46%

profile of v13, /device:TPU:0, one launch (start us, length us, event | category | flops | bytes accessed | tf_op | source)
XLA Modules:
  0.0 97.3 jit_solution(2977835264588732299)
XLA Ops:
  1.2 3.7 %collective-permute-start.3 = (bf16[192,1024]{1,0:T(8,128)(2,1)}, bf16[192,1024]{1,0:T(8,128)(2,1)S(1)}, u32[]{:S(2)}, u32[]{:S(2)}) collective-permute-start(bf16[192,1024]{1,0:T(8,128)(2,1)} %refs_0_.2), channel_id=1, source_target_pairs={{0,2},{2,3},{3,1},{1,0},{4,6},{6,7},{7,5},{5,4},{8,10},{10,11},{11... | collective-permute-start | bytes 1179656 | tf_op jit(solution)/shard_map/ppermute | solution.py:326
  4.8 1.6 %collective-permute-start.2 = (bf16[192,1024]{1,0:T(8,128)(2,1)}, bf16[192,1024]{1,0:T(8,128)(2,1)S(1)}, u32[]{:S(2)}, u32[]{:S(2)}) collective-permute-start(bf16[192,1024]{1,0:T(8,128)(2,1)} %refs_0_.1), channel_id=1, source_target_pairs={{0,2},{2,3},{3,1},{1,0},{4,6},{6,7},{7,5},{5,4},{8,10},{10,11},{11... | collective-permute-start | bytes 1179656 | tf_op jit(solution)/shard_map/ppermute | solution.py:323
  6.4 1.1 %copy-done.5 = bf16[192,2048]{1,0:T(8,128)(2,1)S(1)} copy-done((bf16[192,2048]{1,0:T(8,128)(2,1)S(1)}, bf16[192,2048]{1,0:T(8,128)(2,1)}, u32[]{:S(2)}) %copy-start.5) | copy-done | bytes 786456
  8.1 1.6 %collective-permute-start.1 = (bf16[384,1024]{1,0:T(8,128)(2,1)S(1)}, bf16[384,1024]{1,0:T(8,128)(2,1)S(1)}, u32[]{:S(2)}, u32[]{:S(2)}) collective-permute-start(bf16[384,1024]{1,0:T(8,128)(2,1)S(1)} %shard_map.76.refs_0_), channel_id=1, source_target_pairs={{0,8},{4,12},{8,0},{12,4},{1,9},{5,13},{9,1},{13,5},{2,10},{6,14},... | collective-permute-start | bytes 2359304 | tf_op jit(solution)/shard_map/ppermute | solution.py:299
  9.7 2.2 %copy-done = bf16[2048,1024]{1,0:T(8,128)(2,1)S(1)} copy-done((bf16[2048,1024]{1,0:T(8,128)(2,1)S(1)}, bf16[2048,1024]{1,0:T(8,128)(2,1)}, u32[]{:S(2)}) %copy-start) | copy-done | bytes 4194328
  12.9 2.1 %shard_map.79 = (f32[192,1024]{1,0:T(8,128)S(1)}, bf16[192,1024]{1,0:T(8,128)(2,1)S(1)}) custom-call(s32[2]{0:T(128)S(1)} %pad_add_fusion.place_ref, bf16[192,1024]{1,0:T(8,128)(2,1)S(1)} %copy-done.3, bf16[2048,1024]{1,0:T(8,128)(2,1)S(1)} %copy-done), custom_call_target="tpu_custom_call" | custom-call | flops 10000000 | bytes 1024 | tf_op jit(solution)/shard_map/pallas_call | solution.py:74
  15.0 2.8 %collective-permute-start.4 = (bf16[192,1024]{1,0:T(8,128)(2,1)S(1)}, bf16[192,1024]{1,0:T(8,128)(2,1)S(1)}, u32[]{:S(2)}, u32[]{:S(2)}) collective-permute-start(bf16[192,1024]{1,0:T(8,128)(2,1)S(1)} %collective-permute-done.3.cot_ref.refs_1_), channel_id=1, source_target_pairs={{0,2},{2,3},{3,1},{1,0},{4,6},{6,7},{7,5},{5,4},{8,10},{10,11},{11... | collective-permute-start | bytes 1179656 | tf_op jit(solution)/shard_map/ppermute | solution.py:326
  17.9 2.1 %shard_map.80 = (f32[192,1024]{1,0:T(8,128)S(1)}, bf16[192,1024]{1,0:T(8,128)(2,1)S(1)}) custom-call(s32[2]{0:T(128)S(1)} %pad_add_fusion.place_ref, bf16[192,1024]{1,0:T(8,128)(2,1)S(1)} %collective-permute-done.3.cot_ref.refs_1_, bf16[2048,1024]{1,0:T(8,128)(2,1)S(1)} %copy-done.1), custom_call_target="tpu_custom_call" | custom-call | flops 10000000 | bytes 1024 | tf_op jit(solution)/shard_map/pallas_call | solution.py:74
  20.0 3.0 %collective-permute-done.2.refs_1_ = bf16[192,1024]{1,0:T(8,128)(2,1)S(1)} collective-permute-done((bf16[192,1024]{1,0:T(8,128)(2,1)}, bf16[192,1024]{1,0:T(8,128)(2,1)S(1)}, u32[]{:S(2)}, u32[]{:S(2)}) %collective-permute-start.2) | collective-permute-done | bytes 393248 | tf_op jit(solution)/shard_map/ppermute | solution.py:323
  24.2 1.6 %collective-permute-start.9 = (bf16[192,1024]{1,0:T(8,128)(2,1)S(1)}, bf16[192,1024]{1,0:T(8,128)(2,1)S(1)}, u32[]{:S(2)}, u32[]{:S(2)}) collective-permute-start(bf16[192,1024]{1,0:T(8,128)(2,1)S(1)} %shard_map.81), channel_id=1, source_target_pairs={{0,8},{4,12},{8,0},{12,4},{1,9},{5,13},{9,1},{13,5},{2,10},{6,14},... | collective-permute-start | bytes 1179656 | tf_op jit(solution)/shard_map/ppermute | solution.py:310
  25.8 5.1 %collective-permute-done.4.cot_ref.refs_2_ = bf16[192,1024]{1,0:T(8,128)(2,1)S(1)} collective-permute-done((bf16[192,1024]{1,0:T(8,128)(2,1)S(1)}, bf16[192,1024]{1,0:T(8,128)(2,1)S(1)}, u32[]{:S(2)}, u32[]{:S(2)}) %collective-permute-start.4) | collective-permute-done | bytes 393248 | tf_op jit(solution)/shard_map/ppermute | solution.py:326
  30.9 3.4 %collective-permute-start.12 = (bf16[192,1024]{1,0:T(8,128)(2,1)S(1)}, bf16[192,1024]{1,0:T(8,128)(2,1)S(1)}, u32[]{:S(2)}, u32[]{:S(2)}) collective-permute-start(bf16[192,1024]{1,0:T(8,128)(2,1)S(1)} %collective-permute-done.4.cot_ref.refs_2_), channel_id=1, source_target_pairs={{0,2},{2,3},{3,1},{1,0},{4,6},{6,7},{7,5},{5,4},{8,10},{10,11},{11... | collective-permute-start | bytes 1179656 | tf_op jit(solution)/shard_map/ppermute | solution.py:326
  34.2 2.1 %shard_map.82 = (f32[192,1024]{1,0:T(8,128)S(1)}, bf16[192,1024]{1,0:T(8,128)(2,1)S(1)}) custom-call(s32[2]{0:T(128)S(1)} %pad_add_fusion.place_ref, bf16[192,1024]{1,0:T(8,128)(2,1)S(1)} %collective-permute-done.4.cot_ref.refs_2_, bf16[2048,1024]{1,0:T(8,128)(2,1)S(1)} %copy-done.1), custom_call_target="tpu_custom_call" | custom-call | flops 10000000 | bytes 1024 | tf_op jit(solution)/shard_map/pallas_call | solution.py:74
  36.4 1.7 %shard_map.77 = (bf16[768,1024]{1,0:T(8,128)(2,1)S(1)}, bf16[768,1024]{1,0:T(8,128)(2,1)S(1)}) custom-call(s32[2]{0:T(128)S(1)} %pad_add_fusion.place_ref, bf16[384,1024]{1,0:T(8,128)(2,1)S(1)} %shard_map.76.refs_0_, bf16[384,1024]{1,0:T(8,128)(2,1)S(1)} %collective-permute-done.1.refs_1_), custom_call_target="tpu_custom_call" | custom-call | flops 6000000000 | bytes 1024 | tf_op jit(solution)/shard_map/pallas_call | solution.py:74
  38.7 1.1 %shard_map.88.mine_ref.refs_4_ = bf16[192,1024]{1,0:T(8,128)(2,1)S(1)} custom-call(s32[2]{0:T(128)S(1)} %pad_add_fusion.place_ref, bf16[768,1024]{1,0:T(8,128)(2,1)S(1)} %get-tuple-element.35.pre_ref, f32[192,1024]{1,0:T(8,128)S(1)} %shard_map.87.part_ref), custom_call_target="tpu_custom_call" | custom-call | flops 100000000 | bytes 1024 | tf_op jit(solution)/shard_map/pallas_call | solution.py:74
  41.0 1.6 %collective-permute-start.7 = (bf16[192,1024]{1,0:T(8,128)(2,1)S(1)}, bf16[192,1024]{1,0:T(8,128)(2,1)S(1)}, u32[]{:S(2)}, u32[]{:S(2)}) collective-permute-start(bf16[192,1024]{1,0:T(8,128)(2,1)S(1)} %shard_map.83), channel_id=1, source_target_pairs={{0,8},{4,12},{8,0},{12,4},{1,9},{5,13},{9,1},{13,5},{2,10},{6,14},... | collective-permute-start | bytes 1179656 | tf_op jit(solution)/shard_map/ppermute | solution.py:310
  43.9 3.0 %shard_map.89 = (f32[192,1024]{1,0:T(8,128)}, bf16[192,1024]{1,0:T(8,128)(2,1)S(1)}) custom-call(s32[2]{0:T(128)S(1)} %pad_add_fusion.place_ref, bf16[192,1024]{1,0:T(8,128)(2,1)S(1)} %shard_map.88.mine_ref.refs_4_, bf16[192,1024]{1,0:T(8,128)(2,1)S(1)} %collective-permute-done.10.theirs_ref.refs_8_, bf16[1024,2048]{1,0:T(8,128)(2,1)S(1)} %copy-done.2), custom_call_target="tpu_custom_call" | custom-call | flops 10000000 | bytes 1024 | tf_op jit(solution)/shard_map/pallas_call | solution.py:74
  46.9 1.9 %collective-permute-start.11 = (bf16[192,1024]{1,0:T(8,128)(2,1)S(1)}, bf16[192,1024]{1,0:T(8,128)(2,1)S(1)}, u32[]{:S(2)}, u32[]{:S(2)}) collective-permute-start(bf16[192,1024]{1,0:T(8,128)(2,1)S(1)} %get-tuple-element.47), channel_id=1, source_target_pairs={{0,2},{2,3},{3,1},{1,0},{4,6},{6,7},{7,5},{5,4},{8,10},{10,11},{11... | collective-permute-start | bytes 1179656 | tf_op jit(solution)/shard_map/ppermute | solution.py:342
  48.8 2.1 %shard_map.92 = (f32[192,1024]{1,0:T(8,128)S(1)}, bf16[192,1024]{1,0:T(8,128)(2,1)S(1)}) custom-call(s32[2]{0:T(128)S(1)} %pad_add_fusion.place_ref, bf16[192,1024]{1,0:T(8,128)(2,1)S(1)} %collective-permute-done.12.cot_ref.refs_3_, bf16[2048,1024]{1,0:T(8,128)(2,1)S(1)} %copy-done.1), custom_call_target="tpu_custom_call" | custom-call | flops 10000000 | bytes 1024 | tf_op jit(solution)/shard_map/pallas_call | solution.py:74
  52.8 1.1 %shard_map.85.mine_ref.refs_5_ = bf16[192,1024]{1,0:T(8,128)(2,1)S(1)} custom-call(s32[2]{0:T(128)S(1)} %pad_add_fusion.place_ref, bf16[768,1024]{1,0:T(8,128)(2,1)S(1)} %get-tuple-element.35.pre_ref, f32[192,1024]{1,0:T(8,128)S(1)} %shard_map.84.part_ref), custom_call_target="tpu_custom_call" | custom-call | flops 100000000 | bytes 1024 | tf_op jit(solution)/shard_map/pallas_call | solution.py:74
  54.6 1.6 %collective-permute-start.14 = (bf16[192,1024]{1,0:T(8,128)(2,1)S(1)}, bf16[192,1024]{1,0:T(8,128)(2,1)S(1)}, u32[]{:S(2)}, u32[]{:S(2)}) collective-permute-start(bf16[192,1024]{1,0:T(8,128)(2,1)S(1)} %shard_map.93), channel_id=1, source_target_pairs={{0,8},{4,12},{8,0},{12,4},{1,9},{5,13},{9,1},{13,5},{2,10},{6,14},... | collective-permute-start | bytes 1179656 | tf_op jit(solution)/shard_map/ppermute | solution.py:310
  56.1 6.3 %collective-permute-done.11.part_ref = bf16[192,1024]{1,0:T(8,128)(2,1)S(1)} collective-permute-done((bf16[192,1024]{1,0:T(8,128)(2,1)S(1)}, bf16[192,1024]{1,0:T(8,128)(2,1)S(1)}, u32[]{:S(2)}, u32[]{:S(2)}) %collective-permute-start.11) | collective-permute-done | bytes 393248 | tf_op jit(solution)/shard_map/ppermute | solution.py:342
  63.0 2.1 %shard_map.86.part_ref = f32[192,1024]{1,0:T(8,128)S(1)} custom-call(s32[2]{0:T(128)S(1)} %pad_add_fusion.place_ref, bf16[192,1024]{1,0:T(8,128)(2,1)S(1)} %shard_map.85.mine_ref.refs_5_, bf16[192,1024]{1,0:T(8,128)(2,1)S(1)} %collective-permute-done.8.theirs_ref.refs_9_, bf16[1024,2048]{1,0:T(8,128)(2,1)S(1)} %copy-done.2), custom_call_target="tpu_custom_call" | custom-call | flops 10000000 | bytes 1024 | tf_op jit(solution)/shard_map/pallas_call | solution.py:74
  65.8 1.6 %collective-permute-start.19 = (bf16[192,1024]{1,0:T(8,128)(2,1)S(1)}, bf16[192,1024]{1,0:T(8,128)(2,1)S(1)}, u32[]{:S(2)}, u32[]{:S(2)}) collective-permute-start(bf16[192,1024]{1,0:T(8,128)(2,1)S(1)} %collective-permute-done.18.refs_1_), channel_id=1, source_target_pairs={{0,2},{2,3},{3,1},{1,0},{4,6},{6,7},{7,5},{5,4},{8,10},{10,11},{11... | collective-permute-start | bytes 1179656 | tf_op jit(solution)/shard_map/ppermute | solution.py:345
  70.1 6.5 %shard_map.96 = f32[2048,1024]{1,0:T(8,128)} custom-call(s32[2]{0:T(128)S(1)} %pad_add_fusion.place_ref, bf16[768,1024]{1,0:T(8,128)(2,1)S(1)} %get-tuple-element.55.mine_ref, bf16[768,1024]{1,0:T(8,128)(2,1)S(1)} %collective-permute-done.15.theirs_ref, bf16[192,1024]{1,0:T(8,128)(2,1)S(1)} %copy-done.4, ...), custom_call_target="tpu_custom_call" | custom-call | flops 100000000 | bytes 1024 | tf_op jit(solution)/shard_map/pallas_call | solution.py:74
  76.6 1.3 %collective-permute-done.19.refs_2_ = bf16[192,1024]{1,0:T(8,128)(2,1)S(1)} collective-permute-done((bf16[192,1024]{1,0:T(8,128)(2,1)S(1)}, bf16[192,1024]{1,0:T(8,128)(2,1)S(1)}, u32[]{:S(2)}, u32[]{:S(2)}) %collective-permute-start.19) | collective-permute-done | bytes 393248 | tf_op jit(solution)/shard_map/ppermute | solution.py:345
  79.7 2.1 %shard_map.97.part_ref = f32[192,1024]{1,0:T(8,128)S(1)} custom-call(s32[2]{0:T(128)S(1)} %pad_add_fusion.place_ref, bf16[192,1024]{1,0:T(8,128)(2,1)S(1)} %shard_map.95.mine_ref.refs_6_, bf16[192,1024]{1,0:T(8,128)(2,1)S(1)} %collective-permute-done.16.theirs_ref.refs_10_, bf16[1024,2048]{1,0:T(8,128)(2,1)S(1)} %copy-done.2), custom_call_target="tpu_custom_call" | custom-call | flops 10000000 | bytes 1024 | tf_op jit(solution)/shard_map/pallas_call | solution.py:74
  81.8 2.3 %collective-permute-done.17.refs_0_ = bf16[192,1024]{1,0:T(8,128)(2,1)S(1)} collective-permute-done((bf16[192,1024]{1,0:T(8,128)(2,1)S(1)}, bf16[192,1024]{1,0:T(8,128)(2,1)S(1)}, u32[]{:S(2)}, u32[]{:S(2)}) %collective-permute-start.17) | collective-permute-done | bytes 393248 | tf_op jit(solution)/shard_map/ppermute | solution.py:342
  84.7 2.5 %collective-permute-start.23 = (bf16[192,1024]{1,0:T(8,128)(2,1)S(1)}, bf16[192,1024]{1,0:T(8,128)(2,1)S(1)}, u32[]{:S(2)}, u32[]{:S(2)}) collective-permute-start(bf16[192,1024]{1,0:T(8,128)(2,1)S(1)} %shard_map.98), channel_id=1, source_target_pairs={{0,2},{2,3},{3,1},{1,0},{4,6},{6,7},{7,5},{5,4},{8,10},{10,11},{11... | collective-permute-start | bytes 1179656 | tf_op jit(solution)/shard_map/ppermute | solution.py:357
  87.3 2.1 %shard_map.102.part_ref = f32[192,1024]{1,0:T(8,128)S(1)} custom-call(s32[2]{0:T(128)S(1)} %pad_add_fusion.place_ref, bf16[192,1024]{1,0:T(8,128)(2,1)S(1)} %shard_map.101.mine_ref.refs_3_, bf16[192,1024]{1,0:T(8,128)(2,1)S(1)} %collective-permute-done.22.theirs_ref.refs_7_, bf16[1024,2048]{1,0:T(8,128)(2,1)S(1)} %copy-done.2), custom_call_target="tpu_custom_call" | custom-call | flops 10000000 | bytes 1024 | tf_op jit(solution)/shard_map/pallas_call | solution.py:74
  89.3 6.6 %shard_map.103 = f32[1024,2048]{1,0:T(8,128)} custom-call(s32[2]{0:T(128)S(1)} %pad_add_fusion.place_ref, bf16[384,1024]{1,0:T(8,128)(2,1)S(1)} %shard_map.78.refs_0_, bf16[192,1024]{1,0:T(8,128)(2,1)S(1)} %collective-permute-done.18.refs_1_, bf16[192,1024]{1,0:T(8,128)(2,1)S(1)} %collective-permute-done.19.refs_2_, ...), custom_call_target="tpu_custom_call" | custom-call | flops 3000000000 | bytes 1024 | tf_op jit(solution)/shard_map/pallas_call | solution.py:74
  96.0 1.4 %shard_map.104 = bf16[192,1024]{1,0:T(8,128)(2,1)} custom-call(s32[2]{0:T(128)S(1)} %pad_add_fusion.place_ref, f32[192,1024]{1,0:T(8,128)S(1)} %shard_map.102.part_ref, bf16[192,1024]{1,0:T(8,128)(2,1)S(1)} %collective-permute-done.23.refs_0_), custom_call_target="tpu_custom_call" | custom-call | flops 10000000 | bytes 1024 | tf_op jit(solution)/shard_map/pallas_call | solution.py:74
  (60 shorter events, 15.6 us)
Async XLA Ops:
  0.7 5.7 %collective-permute-start = (bf16[192,2048]{1,0:T(8,128)(2,1)}, bf16[192,2048]{1,0:T(8,128)(2,1)S(1)}, u32[]{:S(2)}, u32[]{:S(2)}) collective-permute-start(bf16[192,2048]{1,0:T(8,128)(2,1)} %mine_ref), channel_id=1, source_target_pairs={{0,4},{4,0},{8,12},{12,8},{1,5},{5,1},{9,13},{13,9},{2,6},{6,2},{1... | collective-permute-start | bytes 2359304 | tf_op jit(solution)/shard_map/ppermute | solution.py:298
  1.2 13.9 %collective-permute-start.3 = (bf16[192,1024]{1,0:T(8,128)(2,1)}, bf16[192,1024]{1,0:T(8,128)(2,1)S(1)}, u32[]{:S(2)}, u32[]{:S(2)}) collective-permute-start(bf16[192,1024]{1,0:T(8,128)(2,1)} %refs_0_.2), channel_id=1, source_target_pairs={{0,2},{2,3},{3,1},{1,0},{4,6},{6,7},{7,5},{5,4},{8,10},{10,11},{11... | collective-permute-start | bytes 1179656 | tf_op jit(solution)/shard_map/ppermute | solution.py:326
  4.8 18.2 %collective-permute-start.2 = (bf16[192,1024]{1,0:T(8,128)(2,1)}, bf16[192,1024]{1,0:T(8,128)(2,1)S(1)}, u32[]{:S(2)}, u32[]{:S(2)}) collective-permute-start(bf16[192,1024]{1,0:T(8,128)(2,1)} %refs_0_.1), channel_id=1, source_target_pairs={{0,2},{2,3},{3,1},{1,0},{4,6},{6,7},{7,5},{5,4},{8,10},{10,11},{11... | collective-permute-start | bytes 1179656 | tf_op jit(solution)/shard_map/ppermute | solution.py:323
  6.4 1.1 %copy-start.5 = (bf16[192,2048]{1,0:T(8,128)(2,1)S(1)}, bf16[192,2048]{1,0:T(8,128)(2,1)}, u32[]{:S(2)}) copy-start(bf16[192,2048]{1,0:T(8,128)(2,1)} %mine_ref) | copy-start | bytes 2359300
  8.1 28.3 %collective-permute-start.1 = (bf16[384,1024]{1,0:T(8,128)(2,1)S(1)}, bf16[384,1024]{1,0:T(8,128)(2,1)S(1)}, u32[]{:S(2)}, u32[]{:S(2)}) collective-permute-start(bf16[384,1024]{1,0:T(8,128)(2,1)S(1)} %shard_map.76.refs_0_), channel_id=1, source_target_pairs={{0,8},{4,12},{8,0},{12,4},{1,9},{5,13},{9,1},{13,5},{2,10},{6,14},... | collective-permute-start | bytes 2359304 | tf_op jit(solution)/shard_map/ppermute | solution.py:299
  9.7 2.2 %copy-start = (bf16[2048,1024]{1,0:T(8,128)(2,1)S(1)}, bf16[2048,1024]{1,0:T(8,128)(2,1)}, u32[]{:S(2)}) copy-start(bf16[2048,1024]{1,0:T(8,128)(2,1)} %down_ref.7) | copy-start | bytes 12582916
  11.9 1.0 %copy-start.3 = (bf16[192,1024]{1,0:T(8,128)(2,1)S(1)}, bf16[192,1024]{1,0:T(8,128)(2,1)}, u32[]{:S(2)}) copy-start(bf16[192,1024]{1,0:T(8,128)(2,1)} %refs_0_.2) | copy-start | bytes 1179652
  12.9 5.0 %copy-start.1 = (bf16[2048,1024]{1,0:T(8,128)(2,1)S(1)}, bf16[2048,1024]{1,0:T(8,128)(2,1)}, u32[]{:S(2)}) copy-start(bf16[2048,1024]{1,0:T(8,128)(2,1)} %down_ref.7) | copy-start | bytes 12582916
  12.9 10.1 %copy-start.6 = (bf16[192,1024]{1,0:T(8,128)(2,1)S(1)}, bf16[192,1024]{1,0:T(8,128)(2,1)}, u32[]{:S(2)}) copy-start(bf16[192,1024]{1,0:T(8,128)(2,1)} %refs_0_.1) | copy-start | bytes 1179652
  15.0 27.6 %collective-permute-start.20 = (bf16[192,1024]{1,0:T(8,128)(2,1)S(1)}, bf16[192,1024]{1,0:T(8,128)(2,1)S(1)}, u32[]{:S(2)}, u32[]{:S(2)}) collective-permute-start(bf16[192,1024]{1,0:T(8,128)(2,1)S(1)} %get-tuple-element.61), channel_id=1, source_target_pairs={{0,4},{4,0},{8,12},{12,8},{1,5},{5,1},{9,13},{13,9},{2,6},{6,2},{1... | collective-permute-start | bytes 1179656 | tf_op jit(solution)/shard_map/ppermute | solution.py:304
  15.0 15.8 %collective-permute-start.4 = (bf16[192,1024]{1,0:T(8,128)(2,1)S(1)}, bf16[192,1024]{1,0:T(8,128)(2,1)S(1)}, u32[]{:S(2)}, u32[]{:S(2)}) collective-permute-start(bf16[192,1024]{1,0:T(8,128)(2,1)S(1)} %collective-permute-done.3.cot_ref.refs_1_), channel_id=1, source_target_pairs={{0,2},{2,3},{3,1},{1,0},{4,6},{6,7},{7,5},{5,4},{8,10},{10,11},{11... | collective-permute-start | bytes 1179656 | tf_op jit(solution)/shard_map/ppermute | solution.py:326
  19.9 3.7 %collective-permute-start.5 = (bf16[192,1024]{1,0:T(8,128)(2,1)S(1)}, bf16[192,1024]{1,0:T(8,128)(2,1)S(1)}, u32[]{:S(2)}, u32[]{:S(2)}) collective-permute-start(bf16[192,1024]{1,0:T(8,128)(2,1)S(1)} %get-tuple-element.42), channel_id=1, source_target_pairs={{0,4},{4,0},{8,12},{12,8},{1,5},{5,1},{9,13},{13,9},{2,6},{6,2},{1... | collective-permute-start | bytes 1179656 | tf_op jit(solution)/shard_map/ppermute | solution.py:304
  24.2 13.8 %collective-permute-start.9 = (bf16[192,1024]{1,0:T(8,128)(2,1)S(1)}, bf16[192,1024]{1,0:T(8,128)(2,1)S(1)}, u32[]{:S(2)}, u32[]{:S(2)}) collective-permute-start(bf16[192,1024]{1,0:T(8,128)(2,1)S(1)} %shard_map.81), channel_id=1, source_target_pairs={{0,8},{4,12},{8,0},{12,4},{1,9},{5,13},{9,1},{13,5},{2,10},{6,14},... | collective-permute-start | bytes 1179656 | tf_op jit(solution)/shard_map/ppermute | solution.py:310
  30.9 13.0 %collective-permute-start.12 = (bf16[192,1024]{1,0:T(8,128)(2,1)S(1)}, bf16[192,1024]{1,0:T(8,128)(2,1)S(1)}, u32[]{:S(2)}, u32[]{:S(2)}) collective-permute-start(bf16[192,1024]{1,0:T(8,128)(2,1)S(1)} %collective-permute-done.4.cot_ref.refs_2_), channel_id=1, source_target_pairs={{0,2},{2,3},{3,1},{1,0},{4,6},{6,7},{7,5},{5,4},{8,10},{10,11},{11... | collective-permute-start | bytes 1179656 | tf_op jit(solution)/shard_map/ppermute | solution.py:326
  36.3 4.1 %collective-permute-start.6 = (bf16[192,1024]{1,0:T(8,128)(2,1)S(1)}, bf16[192,1024]{1,0:T(8,128)(2,1)S(1)}, u32[]{:S(2)}, u32[]{:S(2)}) collective-permute-start(bf16[192,1024]{1,0:T(8,128)(2,1)S(1)} %get-tuple-element.45), channel_id=1, source_target_pairs={{0,4},{4,0},{8,12},{12,8},{1,5},{5,1},{9,13},{13,9},{2,6},{6,2},{1... | collective-permute-start | bytes 1179656 | tf_op jit(solution)/shard_map/ppermute | solution.py:304
  38.7 5.2 %copy-start.2 = (bf16[1024,2048]{1,0:T(8,128)(2,1)S(1)}, bf16[1024,2048]{1,0:T(8,128)(2,1)}, u32[]{:S(2)}) copy-start(bf16[1024,2048]{1,0:T(8,128)(2,1)} %up_ref.7) | copy-start | bytes 12582916
  39.8 4.1 %collective-permute-start.10 = (bf16[192,1024]{1,0:T(8,128)(2,1)S(1)}, bf16[192,1024]{1,0:T(8,128)(2,1)S(1)}, u32[]{:S(2)}, u32[]{:S(2)}) collective-permute-start(bf16[192,1024]{1,0:T(8,128)(2,1)S(1)} %shard_map.88.mine_ref.refs_4_), channel_id=1, source_target_pairs={{0,4},{4,0},{8,12},{12,8},{1,5},{5,1},{9,13},{13,9},{2,6},{6,2},{1... | collective-permute-start | bytes 1179656 | tf_op jit(solution)/shard_map/ppermute | solution.py:316
  41.0 11.1 %collective-permute-start.7 = (bf16[192,1024]{1,0:T(8,128)(2,1)S(1)}, bf16[192,1024]{1,0:T(8,128)(2,1)S(1)}, u32[]{:S(2)}, u32[]{:S(2)}) collective-permute-start(bf16[192,1024]{1,0:T(8,128)(2,1)S(1)} %shard_map.83), channel_id=1, source_target_pairs={{0,8},{4,12},{8,0},{12,4},{1,9},{5,13},{9,1},{13,5},{2,10},{6,14},... | collective-permute-start | bytes 1179656 | tf_op jit(solution)/shard_map/ppermute | solution.py:310
  43.2 22.6 %collective-permute-start.18 = (bf16[192,1024]{1,0:T(8,128)(2,1)S(1)}, bf16[192,1024]{1,0:T(8,128)(2,1)S(1)}, u32[]{:S(2)}, u32[]{:S(2)}) collective-permute-start(bf16[192,1024]{1,0:T(8,128)(2,1)S(1)} %collective-permute-done.2.refs_1_), channel_id=1, source_target_pairs={{0,2},{2,3},{3,1},{1,0},{4,6},{6,7},{7,5},{5,4},{8,10},{10,11},{11... | collective-permute-start | bytes 1179656 | tf_op jit(solution)/shard_map/ppermute | solution.py:331
  43.9 26.2 %collective-permute-start.15 = (bf16[768,1024]{1,0:T(8,128)(2,1)S(1)}, bf16[768,1024]{1,0:T(8,128)(2,1)S(1)}, u32[]{:S(2)}, u32[]{:S(2)}) collective-permute-start(bf16[768,1024]{1,0:T(8,128)(2,1)S(1)} %get-tuple-element.55.mine_ref), channel_id=1, source_target_pairs={{0,4},{4,0},{8,12},{12,8},{1,5},{5,1},{9,13},{13,9},{2,6},{6,2},{1... | collective-permute-start | bytes 4718600 | tf_op jit(solution)/shard_map/ppermute | solution.py:333
  46.9 15.5 %collective-permute-start.11 = (bf16[192,1024]{1,0:T(8,128)(2,1)S(1)}, bf16[192,1024]{1,0:T(8,128)(2,1)S(1)}, u32[]{:S(2)}, u32[]{:S(2)}) collective-permute-start(bf16[192,1024]{1,0:T(8,128)(2,1)S(1)} %get-tuple-element.47), channel_id=1, source_target_pairs={{0,2},{2,3},{3,1},{1,0},{4,6},{6,7},{7,5},{5,4},{8,10},{10,11},{11... | collective-permute-start | bytes 1179656 | tf_op jit(solution)/shard_map/ppermute | solution.py:342
  50.9 3.1 %collective-permute-start.13 = (bf16[192,1024]{1,0:T(8,128)(2,1)S(1)}, bf16[192,1024]{1,0:T(8,128)(2,1)S(1)}, u32[]{:S(2)}, u32[]{:S(2)}) collective-permute-start(bf16[192,1024]{1,0:T(8,128)(2,1)S(1)} %get-tuple-element.53), channel_id=1, source_target_pairs={{0,4},{4,0},{8,12},{12,8},{1,5},{5,1},{9,13},{13,9},{2,6},{6,2},{1... | collective-permute-start | bytes 1179656 | tf_op jit(solution)/shard_map/ppermute | solution.py:304
  53.9 9.2 %collective-permute-start.8 = (bf16[192,1024]{1,0:T(8,128)(2,1)S(1)}, bf16[192,1024]{1,0:T(8,128)(2,1)S(1)}, u32[]{:S(2)}, u32[]{:S(2)}) collective-permute-start(bf16[192,1024]{1,0:T(8,128)(2,1)S(1)} %shard_map.85.mine_ref.refs_5_), channel_id=1, source_target_pairs={{0,4},{4,0},{8,12},{12,8},{1,5},{5,1},{9,13},{13,9},{2,6},{6,2},{1... | collective-permute-start | bytes 1179656 | tf_op jit(solution)/shard_map/ppermute | solution.py:316
  54.6 13.7 %collective-permute-start.14 = (bf16[192,1024]{1,0:T(8,128)(2,1)S(1)}, bf16[192,1024]{1,0:T(8,128)(2,1)S(1)}, u32[]{:S(2)}, u32[]{:S(2)}) collective-permute-start(bf16[192,1024]{1,0:T(8,128)(2,1)S(1)} %shard_map.93), channel_id=1, source_target_pairs={{0,8},{4,12},{8,0},{12,4},{1,9},{5,13},{9,1},{13,5},{2,10},{6,14},... | collective-permute-start | bytes 1179656 | tf_op jit(solution)/shard_map/ppermute | solution.py:310
  65.7 4.4 %copy-start.4 = (bf16[192,1024]{1,0:T(8,128)(2,1)S(1)}, bf16[192,1024]{1,0:T(8,128)(2,1)}, u32[]{:S(2)}) copy-start(bf16[192,1024]{1,0:T(8,128)(2,1)} %refs_0_.2) | copy-start | bytes 1179652
  65.8 12.1 %collective-permute-start.19 = (bf16[192,1024]{1,0:T(8,128)(2,1)S(1)}, bf16[192,1024]{1,0:T(8,128)(2,1)S(1)}, u32[]{:S(2)}, u32[]{:S(2)}) collective-permute-start(bf16[192,1024]{1,0:T(8,128)(2,1)S(1)} %collective-permute-done.18.refs_1_), channel_id=1, source_target_pairs={{0,2},{2,3},{3,1},{1,0},{4,6},{6,7},{7,5},{5,4},{8,10},{10,11},{11... | collective-permute-start | bytes 1179656 | tf_op jit(solution)/shard_map/ppermute | solution.py:345
  67.4 10.5 %collective-permute-start.21 = (bf16[192,1024]{1,0:T(8,128)(2,1)S(1)}, bf16[192,1024]{1,0:T(8,128)(2,1)S(1)}, u32[]{:S(2)}, u32[]{:S(2)}) collective-permute-start(bf16[192,1024]{1,0:T(8,128)(2,1)S(1)} %shard_map.99), channel_id=1, source_target_pairs={{0,8},{4,12},{8,0},{12,4},{1,9},{5,13},{9,1},{13,5},{2,10},{6,14},... | collective-permute-start | bytes 1179656 | tf_op jit(solution)/shard_map/ppermute | solution.py:310
  67.9 16.2 %collective-permute-start.17 = (bf16[192,1024]{1,0:T(8,128)(2,1)S(1)}, bf16[192,1024]{1,0:T(8,128)(2,1)S(1)}, u32[]{:S(2)}, u32[]{:S(2)}) collective-permute-start(bf16[192,1024]{1,0:T(8,128)(2,1)S(1)} %shard_map.91), channel_id=1, source_target_pairs={{0,2},{2,3},{3,1},{1,0},{4,6},{6,7},{7,5},{5,4},{8,10},{10,11},{11... | collective-permute-start | bytes 1179656 | tf_op jit(solution)/shard_map/ppermute | solution.py:342
  70.0 9.7 %collective-permute-start.16 = (bf16[192,1024]{1,0:T(8,128)(2,1)S(1)}, bf16[192,1024]{1,0:T(8,128)(2,1)S(1)}, u32[]{:S(2)}, u32[]{:S(2)}) collective-permute-start(bf16[192,1024]{1,0:T(8,128)(2,1)S(1)} %shard_map.95.mine_ref.refs_6_), channel_id=1, source_target_pairs={{0,4},{4,0},{8,12},{12,8},{1,5},{5,1},{9,13},{13,9},{2,6},{6,2},{1... | collective-permute-start | bytes 1179656 | tf_op jit(solution)/shard_map/ppermute | solution.py:316
  79.6 7.6 %collective-permute-start.22 = (bf16[192,1024]{1,0:T(8,128)(2,1)S(1)}, bf16[192,1024]{1,0:T(8,128)(2,1)S(1)}, u32[]{:S(2)}, u32[]{:S(2)}) collective-permute-start(bf16[192,1024]{1,0:T(8,128)(2,1)S(1)} %shard_map.101.mine_ref.refs_3_), channel_id=1, source_target_pairs={{0,4},{4,0},{8,12},{12,8},{1,5},{5,1},{9,13},{13,9},{2,6},{6,2},{1... | collective-permute-start | bytes 1179656 | tf_op jit(solution)/shard_map/ppermute | solution.py:316
  84.7 11.3 %collective-permute-start.23 = (bf16[192,1024]{1,0:T(8,128)(2,1)S(1)}, bf16[192,1024]{1,0:T(8,128)(2,1)S(1)}, u32[]{:S(2)}, u32[]{:S(2)}) collective-permute-start(bf16[192,1024]{1,0:T(8,128)(2,1)S(1)} %shard_map.98), channel_id=1, source_target_pairs={{0,2},{2,3},{3,1},{1,0},{4,6},{6,7},{7,5},{5,4},{8,10},{10,11},{11... | collective-permute-start | bytes 1179656 | tf_op jit(solution)/shard_map/ppermute | solution.py:357

commit v14 on v13

--- a/solution.py
+++ b/solution.py
@@ -67,7 +67,7 @@
     return lax.rem(place_ref[1], 2)
 
 
-ADD_COST = {1: MUCH, 2: MOST}
+ADD_COST = {0: 3000000000, 1: 3000000000, 2: 8000000000, 3: 3000000000}
 
 
 def call(kernel, place, operands, outs, mib, cost, grid=(1,), in_specs=None, out_specs=None, scratch=()):
@@ -115,7 +115,7 @@
     tokens, half = blocks[0].shape
     out = jax.ShapeDtypeStruct((tokens * len(blocks), half), jnp.bfloat16)
     kernel = functools.partial(lay_out_kernel, len(blocks))
-    return call(kernel, place, blocks, [out, out], 12, 2 * MUCH)
+    return call(kernel, place, blocks, [out, out], 12, 6000000000)
 
 
 def hidden_kernel(place_ref, cot_ref, down_ref, own_ref, other_ref):
@@ -132,7 +132,7 @@
 def hidden_call(place, cot, down_weight):
     shape = (cot.shape[0], down_weight.shape[0] // 2)
     outs = [jax.ShapeDtypeStruct(shape, jnp.float32), jax.ShapeDtypeStruct(shape, jnp.bfloat16)]
-    return call(hidden_kernel, place, [cot, down_weight], outs, 10, LITTLE)
+    return call(hidden_kernel, place, [cot, down_weight], outs, 10, 10000000)
 
 
 def pre_grad_kernel(step, cols, place_ref, pre_ref, part_ref, *refs):
@@ -152,7 +152,7 @@
 def pre_grad_call(place, step, cols, pre_all, part, others):
     out = jax.ShapeDtypeStruct(part.shape, jnp.bfloat16)
     kernel = functools.partial(pre_grad_kernel, step, cols)
-    return call(kernel, place, [pre_all, part, *others], out, 8, SOME)
+    return call(kernel, place, [pre_all, part, *others], out, 8, 100000000)
 
 
 def share_kernel(place_ref, mine_ref, theirs_ref, up_ref, out_ref, *sent_refs):
@@ -172,7 +172,7 @@
     shape = (mine.shape[0], up_weight.shape[0])
     outs = [jax.ShapeDtypeStruct(shape, jnp.float32)]
     outs += [jax.ShapeDtypeStruct(shape, jnp.bfloat16)] * first
-    return call(share_kernel, place, [mine, theirs, up_weight], outs, 12, LITTLE)
+    return call(share_kernel, place, [mine, theirs, up_weight], outs, 12, 10000000)
 
 
 def add_kernel(place_ref, part_ref, *refs):
@@ -223,7 +223,7 @@
         [act_mine, act_theirs, *cots],
         jax.ShapeDtypeStruct((2 * half, features), jnp.float32),
         14,
-        SOME,
+        100000000,
         grid=(2 * steps,),
         out_specs=pl.BlockSpec((tile, features), rows),
         scratch=[pltpu.VMEM((total, features), jnp.bfloat16)],
@@ -239,7 +239,7 @@
 def join_call(place, blocks):
     tokens, features = blocks[0].shape
     out = jax.ShapeDtypeStruct((tokens * len(blocks), features), blocks[0].dtype)
-    return call(join_kernel, place, blocks, out, 8, MOST)
+    return call(join_kernel, place, blocks, out, 8, 8000000000)
 
 
 def grad_up_kernel(blocks, scale, place_ref, *refs):
@@ -274,7 +274,7 @@
         [*ins, *mine, *pair],
         jax.ShapeDtypeStruct((features, hidden), jnp.float32),
         18,
-        MUCH,
+        3000000000,
         grid=(features // tile,),
         out_specs=pl.BlockSpec((tile, hidden), lambda i, place: (i, 0)),
         scratch=[
@@ -302,7 +302,7 @@
     def hidden_part(s, *first):
         own, other = hidden_call(after(place, *first), cots[s], down_weight)
         arrived = lax.ppermute(other, "row", pair)
-        sent[s] = add_call(place, own, [arrived], jnp.bfloat16, LITTLE)
+        sent[s] = add_call(place, own, [arrived], jnp.bfloat16, 10000000)
         parts[s] = own, arrived
 
     def exchange(s, *first):
@@ -328,7 +328,8 @@
         if s < last:
             hidden_part(s, *([near] if s == 2 else []))
             exchange(s)
-    ins.append(lax.ppermute(after(ins[1], near, cots[last - 1]), "col", ring))
+    ins.append(lax.ppermute(after(ins[1], near), "col", ring))
+    second = join_call(place, ins[2:])
     pre_all, act = lay_out_call(place, pres)
     act_theirs = lax.ppermute(act, "row", pair)
 
@@ -350,13 +351,11 @@
             )
             pre_grad(0, grad_down, ins[s])
             first = [grad_down]
-        if s == 2:
-            arrived = add_call(place, arrived, [], jnp.float32, MOST)
-        part = share(s, *first)[0]
+        part = share(s, *first, *([second] if s == 2 else []))[0]
         sums = late = add_call(place, part, [arrived], jnp.bfloat16, LITTLE)
     arrived = lax.ppermute(sums, "col", ring)
     part = share(0, sums)[0]
-    grad_up = grad_up_call(after(place, part), [near, *ins[2:]], mine, theirs, scale)
+    grad_up = grad_up_call(after(place, part), [near, second, *ins[3:]], mine, theirs, scale)
     sums = add_call(after(place, grad_up), part, [arrived], jnp.bfloat16, LITTLE)
     return (sums, grad_up, grad_down)
 

time: 97.6 us -> 94.2 us (0.965)
  waiting for transfers between devices: 19 us -> 15.2 us
    ppermute x3, waiting for transfers between devices: 8.64 us -> 4.45 us  [per_device(): arrived = lax.ppermute(sums, 'col', ring)]
    ppermute x4, waiting for transfers between devices: 0.98 us -> 2.59 us  [exchange(): others[s] = [lax.ppermute(values, 'row', to) for to in over_x]]
    ppermute x1, waiting for transfers between devices: 1.27 us -> 0.01 us  [per_device(): ins.append(lax.ppermute(after(ins[-1], sums), 'col', ring))]
  transfers between devices with their start and end apart: 24 -> 24, of which waited for: 6 -> 6; matrix products, arithmetic and copies ran while one was open for 0% -> 0% of each run, Pallas kernels for 46% -> 47%
where the time goes in v14:
time: 94.2 us; the launch traced here: 94 us
  Pallas kernels  45.9 us (49%)
  starting transfers between devices  27.5 us (29%)
  waiting for transfers between devices  15.2 us (16%)
  local copies, waits for them, and re-layouts  4.34 us (5%)
  between operations  0.97 us (1%)
    pallas_call x29, Pallas kernels, call(): pl.pallas_call(kernel, out_shape=outs, grid_spec=pltpu.PrefetchScalarGrid...  45.9 us
    ppermute x3, starting transfers between devices, per_device(): arriving = lax.ppermute(cots[s - 1], 'col', ring)  9.84 us
    ppermute x4, starting transfers between devices, exchange(): others[s] = [lax.ppermute(values, 'row', to) for to in over_x]  5.51 us
    ppermute x3, waiting for transfers between devices, per_device(): arriving = lax.ppermute(cots[s - 1], 'col', ring)  5.08 us
    ppermute x3, starting transfers between devices, per_device(): arrived = lax.ppermute(sums, 'col', ring)  4.47 us
    ppermute x3, waiting for transfers between devices, per_device(): arrived = lax.ppermute(sums, 'col', ring)  4.45 us
    unnamed x14, local copies, waits for them, and re-layouts  4.34 us
    ppermute x1, waiting for transfers between devices, per_device(): ins = [inputs, lax.ppermute(after(inputs, place), 'col', ring)]  3 us
  transfers between devices with their start and end apart: 24, of which 6 were waited for; matrix products, arithmetic and copies ran while one was open for 0% of the time, Pallas kernels for 47%

profile of v14, /device:TPU:0, one launch (start us, length us, event | category | flops | bytes accessed | tf_op | source)
XLA Modules:
  0.0 94.0 jit_solution(10687240975004553427)
XLA Ops:
  1.2 3.7 %collective-permute-start.4 = (bf16[192,1024]{1,0:T(8,128)(2,1)}, bf16[192,1024]{1,0:T(8,128)(2,1)S(1)}, u32[]{:S(2)}, u32[]{:S(2)}) collective-permute-start(bf16[192,1024]{1,0:T(8,128)(2,1)} %refs_0_.2), channel_id=1, source_target_pairs={{0,2},{2,3},{3,1},{1,0},{4,6},{6,7},{7,5},{5,4},{8,10},{10,11},{11... | collective-permute-start | bytes 1179656 | tf_op jit(solution)/shard_map/ppermute | solution.py:326
  4.8 1.6 %collective-permute-start.2 = (bf16[192,1024]{1,0:T(8,128)(2,1)}, bf16[192,1024]{1,0:T(8,128)(2,1)S(1)}, u32[]{:S(2)}, u32[]{:S(2)}) collective-permute-start(bf16[192,1024]{1,0:T(8,128)(2,1)} %refs_0_.1), channel_id=1, source_target_pairs={{0,2},{2,3},{3,1},{1,0},{4,6},{6,7},{7,5},{5,4},{8,10},{10,11},{11... | collective-permute-start | bytes 1179656 | tf_op jit(solution)/shard_map/ppermute | solution.py:323
  6.4 1.1 %copy-done.5 = bf16[192,2048]{1,0:T(8,128)(2,1)S(1)} copy-done((bf16[192,2048]{1,0:T(8,128)(2,1)S(1)}, bf16[192,2048]{1,0:T(8,128)(2,1)}, u32[]{:S(2)}) %copy-start.5) | copy-done | bytes 786456
  8.1 1.6 %collective-permute-start.1 = (bf16[384,1024]{1,0:T(8,128)(2,1)S(1)}, bf16[384,1024]{1,0:T(8,128)(2,1)S(1)}, u32[]{:S(2)}, u32[]{:S(2)}) collective-permute-start(bf16[384,1024]{1,0:T(8,128)(2,1)S(1)} %shard_map.76.refs_0_), channel_id=1, source_target_pairs={{0,8},{4,12},{8,0},{12,4},{1,9},{5,13},{9,1},{13,5},{2,10},{6,14},... | collective-permute-start | bytes 2359304 | tf_op jit(solution)/shard_map/ppermute | solution.py:299
  9.7 2.2 %copy-done = bf16[2048,1024]{1,0:T(8,128)(2,1)S(1)} copy-done((bf16[2048,1024]{1,0:T(8,128)(2,1)S(1)}, bf16[2048,1024]{1,0:T(8,128)(2,1)}, u32[]{:S(2)}) %copy-start) | copy-done | bytes 4194328
  12.9 2.1 %shard_map.80 = (f32[192,1024]{1,0:T(8,128)S(1)}, bf16[192,1024]{1,0:T(8,128)(2,1)S(1)}) custom-call(s32[2]{0:T(128)S(1)} %pad_add_fusion.place_ref, bf16[192,1024]{1,0:T(8,128)(2,1)S(1)} %copy-done.3, bf16[2048,1024]{1,0:T(8,128)(2,1)S(1)} %copy-done), custom_call_target="tpu_custom_call" | custom-call | flops 10000000 | bytes 1024 | tf_op jit(solution)/shard_map/pallas_call | solution.py:74
  15.0 2.8 %collective-permute-start.5 = (bf16[192,1024]{1,0:T(8,128)(2,1)S(1)}, bf16[192,1024]{1,0:T(8,128)(2,1)S(1)}, u32[]{:S(2)}, u32[]{:S(2)}) collective-permute-start(bf16[192,1024]{1,0:T(8,128)(2,1)S(1)} %collective-permute-done.4.cot_ref.refs_1_), channel_id=1, source_target_pairs={{0,2},{2,3},{3,1},{1,0},{4,6},{6,7},{7,5},{5,4},{8,10},{10,11},{11... | collective-permute-start | bytes 1179656 | tf_op jit(solution)/shard_map/ppermute | solution.py:326
  17.9 2.1 %shard_map.81 = (f32[192,1024]{1,0:T(8,128)S(1)}, bf16[192,1024]{1,0:T(8,128)(2,1)S(1)}) custom-call(s32[2]{0:T(128)S(1)} %pad_add_fusion.place_ref, bf16[192,1024]{1,0:T(8,128)(2,1)S(1)} %collective-permute-done.4.cot_ref.refs_1_, bf16[2048,1024]{1,0:T(8,128)(2,1)S(1)} %copy-done.1), custom_call_target="tpu_custom_call" | custom-call | flops 10000000 | bytes 1024 | tf_op jit(solution)/shard_map/pallas_call | solution.py:74
  20.0 3.0 %collective-permute-done.2.refs_1_ = bf16[192,1024]{1,0:T(8,128)(2,1)S(1)} collective-permute-done((bf16[192,1024]{1,0:T(8,128)(2,1)}, bf16[192,1024]{1,0:T(8,128)(2,1)S(1)}, u32[]{:S(2)}, u32[]{:S(2)}) %collective-permute-start.2) | collective-permute-done | bytes 393248 | tf_op jit(solution)/shard_map/ppermute | solution.py:323
  24.2 1.6 %collective-permute-start.10 = (bf16[192,1024]{1,0:T(8,128)(2,1)S(1)}, bf16[192,1024]{1,0:T(8,128)(2,1)S(1)}, u32[]{:S(2)}, u32[]{:S(2)}) collective-permute-start(bf16[192,1024]{1,0:T(8,128)(2,1)S(1)} %shard_map.82), channel_id=1, source_target_pairs={{0,8},{4,12},{8,0},{12,4},{1,9},{5,13},{9,1},{13,5},{2,10},{6,14},... | collective-permute-start | bytes 1179656 | tf_op jit(solution)/shard_map/ppermute | solution.py:310
  25.8 5.1 %collective-permute-done.5.cot_ref.refs_2_ = bf16[192,1024]{1,0:T(8,128)(2,1)S(1)} collective-permute-done((bf16[192,1024]{1,0:T(8,128)(2,1)S(1)}, bf16[192,1024]{1,0:T(8,128)(2,1)S(1)}, u32[]{:S(2)}, u32[]{:S(2)}) %collective-permute-start.5) | collective-permute-done | bytes 393248 | tf_op jit(solution)/shard_map/ppermute | solution.py:326
  30.9 3.4 %collective-permute-start.13 = (bf16[192,1024]{1,0:T(8,128)(2,1)S(1)}, bf16[192,1024]{1,0:T(8,128)(2,1)S(1)}, u32[]{:S(2)}, u32[]{:S(2)}) collective-permute-start(bf16[192,1024]{1,0:T(8,128)(2,1)S(1)} %collective-permute-done.5.cot_ref.refs_2_), channel_id=1, source_target_pairs={{0,2},{2,3},{3,1},{1,0},{4,6},{6,7},{7,5},{5,4},{8,10},{10,11},{11... | collective-permute-start | bytes 1179656 | tf_op jit(solution)/shard_map/ppermute | solution.py:326
  34.2 2.1 %shard_map.83 = (f32[192,1024]{1,0:T(8,128)S(1)}, bf16[192,1024]{1,0:T(8,128)(2,1)S(1)}) custom-call(s32[2]{0:T(128)S(1)} %pad_add_fusion.place_ref, bf16[192,1024]{1,0:T(8,128)(2,1)S(1)} %collective-permute-done.5.cot_ref.refs_2_, bf16[2048,1024]{1,0:T(8,128)(2,1)S(1)} %copy-done.1), custom_call_target="tpu_custom_call" | custom-call | flops 10000000 | bytes 1024 | tf_op jit(solution)/shard_map/pallas_call | solution.py:74
  36.4 1.7 %shard_map.77 = (bf16[768,1024]{1,0:T(8,128)(2,1)S(1)}, bf16[768,1024]{1,0:T(8,128)(2,1)S(1)}) custom-call(s32[2]{0:T(128)S(1)} %pad_add_fusion.place_ref, bf16[384,1024]{1,0:T(8,128)(2,1)S(1)} %shard_map.76.refs_0_, bf16[384,1024]{1,0:T(8,128)(2,1)S(1)} %collective-permute-done.1.refs_1_), custom_call_target="tpu_custom_call" | custom-call | flops 6000000000 | bytes 1024 | tf_op jit(solution)/shard_map/pallas_call | solution.py:74
  38.7 1.1 %shard_map.89.mine_ref.refs_4_ = bf16[192,1024]{1,0:T(8,128)(2,1)S(1)} custom-call(s32[2]{0:T(128)S(1)} %pad_add_fusion.place_ref, bf16[768,1024]{1,0:T(8,128)(2,1)S(1)} %get-tuple-element.36.pre_ref, f32[192,1024]{1,0:T(8,128)S(1)} %shard_map.88.part_ref), custom_call_target="tpu_custom_call" | custom-call | flops 100000000 | bytes 1024 | tf_op jit(solution)/shard_map/pallas_call | solution.py:74
  41.0 1.6 %collective-permute-start.8 = (bf16[192,1024]{1,0:T(8,128)(2,1)S(1)}, bf16[192,1024]{1,0:T(8,128)(2,1)S(1)}, u32[]{:S(2)}, u32[]{:S(2)}) collective-permute-start(bf16[192,1024]{1,0:T(8,128)(2,1)S(1)} %shard_map.84), channel_id=1, source_target_pairs={{0,8},{4,12},{8,0},{12,4},{1,9},{5,13},{9,1},{13,5},{2,10},{6,14},... | collective-permute-start | bytes 1179656 | tf_op jit(solution)/shard_map/ppermute | solution.py:310
  44.0 3.0 %shard_map.90 = (f32[192,1024]{1,0:T(8,128)}, bf16[192,1024]{1,0:T(8,128)(2,1)S(1)}) custom-call(s32[2]{0:T(128)S(1)} %pad_add_fusion.place_ref, bf16[192,1024]{1,0:T(8,128)(2,1)S(1)} %shard_map.89.mine_ref.refs_4_, bf16[192,1024]{1,0:T(8,128)(2,1)S(1)} %collective-permute-done.11.theirs_ref.refs_8_, bf16[1024,2048]{1,0:T(8,128)(2,1)S(1)} %copy-done.2), custom_call_target="tpu_custom_call" | custom-call | flops 10000000 | bytes 1024 | tf_op jit(solution)/shard_map/pallas_call | solution.py:74
  46.9 1.9 %collective-permute-start.12 = (bf16[192,1024]{1,0:T(8,128)(2,1)S(1)}, bf16[192,1024]{1,0:T(8,128)(2,1)S(1)}, u32[]{:S(2)}, u32[]{:S(2)}) collective-permute-start(bf16[192,1024]{1,0:T(8,128)(2,1)S(1)} %get-tuple-element.50), channel_id=1, source_target_pairs={{0,2},{2,3},{3,1},{1,0},{4,6},{6,7},{7,5},{5,4},{8,10},{10,11},{11... | collective-permute-start | bytes 1179656 | tf_op jit(solution)/shard_map/ppermute | solution.py:343
  48.8 2.1 %shard_map.92 = (f32[192,1024]{1,0:T(8,128)S(1)}, bf16[192,1024]{1,0:T(8,128)(2,1)S(1)}) custom-call(s32[2]{0:T(128)S(1)} %pad_add_fusion.place_ref, bf16[192,1024]{1,0:T(8,128)(2,1)S(1)} %collective-permute-done.13.cot_ref.refs_3_, bf16[2048,1024]{1,0:T(8,128)(2,1)S(1)} %copy-done.1), custom_call_target="tpu_custom_call" | custom-call | flops 10000000 | bytes 1024 | tf_op jit(solution)/shard_map/pallas_call | solution.py:74
  52.8 1.1 %shard_map.86.mine_ref.refs_5_ = bf16[192,1024]{1,0:T(8,128)(2,1)S(1)} custom-call(s32[2]{0:T(128)S(1)} %pad_add_fusion.place_ref, bf16[768,1024]{1,0:T(8,128)(2,1)S(1)} %get-tuple-element.36.pre_ref, f32[192,1024]{1,0:T(8,128)S(1)} %shard_map.85.part_ref), custom_call_target="tpu_custom_call" | custom-call | flops 100000000 | bytes 1024 | tf_op jit(solution)/shard_map/pallas_call | solution.py:74
  54.6 1.6 %collective-permute-start.15 = (bf16[192,1024]{1,0:T(8,128)(2,1)S(1)}, bf16[192,1024]{1,0:T(8,128)(2,1)S(1)}, u32[]{:S(2)}, u32[]{:S(2)}) collective-permute-start(bf16[192,1024]{1,0:T(8,128)(2,1)S(1)} %shard_map.93), channel_id=1, source_target_pairs={{0,8},{4,12},{8,0},{12,4},{1,9},{5,13},{9,1},{13,5},{2,10},{6,14},... | collective-permute-start | bytes 1179656 | tf_op jit(solution)/shard_map/ppermute | solution.py:310
  56.7 2.1 %shard_map.87.part_ref = f32[192,1024]{1,0:T(8,128)S(1)} custom-call(s32[2]{0:T(128)S(1)} %pad_add_fusion.place_ref, bf16[192,1024]{1,0:T(8,128)(2,1)S(1)} %shard_map.86.mine_ref.refs_5_, bf16[192,1024]{1,0:T(8,128)(2,1)S(1)} %collective-permute-done.9.theirs_ref.refs_9_, bf16[1024,2048]{1,0:T(8,128)(2,1)S(1)} %copy-done.2), custom_call_target="tpu_custom_call" | custom-call | flops 10000000 | bytes 1024 | tf_op jit(solution)/shard_map/pallas_call | solution.py:74
  58.8 3.0 %collective-permute-done.12.refs_0_ = bf16[192,1024]{1,0:T(8,128)(2,1)S(1)} collective-permute-done((bf16[192,1024]{1,0:T(8,128)(2,1)S(1)}, bf16[192,1024]{1,0:T(8,128)(2,1)S(1)}, u32[]{:S(2)}, u32[]{:S(2)}) %collective-permute-start.12) | collective-permute-done | bytes 393248 | tf_op jit(solution)/shard_map/ppermute | solution.py:343
  62.4 1.6 %collective-permute-start.19 = (bf16[192,1024]{1,0:T(8,128)(2,1)S(1)}, bf16[192,1024]{1,0:T(8,128)(2,1)S(1)}, u32[]{:S(2)}, u32[]{:S(2)}) collective-permute-start(bf16[192,1024]{1,0:T(8,128)(2,1)S(1)} %collective-permute-done.3.refs_0_), channel_id=1, source_target_pairs={{0,2},{2,3},{3,1},{1,0},{4,6},{6,7},{7,5},{5,4},{8,10},{10,11},{11... | collective-permute-start | bytes 1179656 | tf_op jit(solution)/shard_map/ppermute | solution.py:346
  64.9 1.6 %collective-permute-done.15.refs_1_ = bf16[192,1024]{1,0:T(8,128)(2,1)S(1)} collective-permute-done((bf16[192,1024]{1,0:T(8,128)(2,1)S(1)}, bf16[192,1024]{1,0:T(8,128)(2,1)S(1)}, u32[]{:S(2)}, u32[]{:S(2)}) %collective-permute-start.15) | collective-permute-done | bytes 393248 | tf_op jit(solution)/shard_map/ppermute | solution.py:310
  68.4 6.5 %shard_map.96 = f32[2048,1024]{1,0:T(8,128)} custom-call(s32[2]{0:T(128)S(1)} %pad_add_fusion.place_ref, bf16[768,1024]{1,0:T(8,128)(2,1)S(1)} %get-tuple-element.58.mine_ref, bf16[768,1024]{1,0:T(8,128)(2,1)S(1)} %collective-permute-done.16.theirs_ref, bf16[192,1024]{1,0:T(8,128)(2,1)S(1)} %copy-done.4, ...), custom_call_target="tpu_custom_call" | custom-call | flops 100000000 | bytes 1024 | tf_op jit(solution)/shard_map/pallas_call | solution.py:74
  77.2 2.1 %shard_map.97.part_ref = f32[192,1024]{1,0:T(8,128)S(1)} custom-call(s32[2]{0:T(128)S(1)} %pad_add_fusion.place_ref, bf16[192,1024]{1,0:T(8,128)(2,1)S(1)} %shard_map.95.mine_ref.refs_6_, bf16[192,1024]{1,0:T(8,128)(2,1)S(1)} %collective-permute-done.17.theirs_ref.refs_10_, bf16[1024,2048]{1,0:T(8,128)(2,1)S(1)} %copy-done.2), custom_call_target="tpu_custom_call" | custom-call | flops 10000000 | bytes 1024 | tf_op jit(solution)/shard_map/pallas_call | solution.py:74
  79.3 1.5 %collective-permute-done.18.refs_0_ = bf16[192,1024]{1,0:T(8,128)(2,1)S(1)} collective-permute-done((bf16[192,1024]{1,0:T(8,128)(2,1)S(1)}, bf16[192,1024]{1,0:T(8,128)(2,1)S(1)}, u32[]{:S(2)}, u32[]{:S(2)}) %collective-permute-start.18) | collective-permute-done | bytes 393248 | tf_op jit(solution)/shard_map/ppermute | solution.py:343
  81.4 2.5 %collective-permute-start.23 = (bf16[192,1024]{1,0:T(8,128)(2,1)S(1)}, bf16[192,1024]{1,0:T(8,128)(2,1)S(1)}, u32[]{:S(2)}, u32[]{:S(2)}) collective-permute-start(bf16[192,1024]{1,0:T(8,128)(2,1)S(1)} %shard_map.98), channel_id=1, source_target_pairs={{0,2},{2,3},{3,1},{1,0},{4,6},{6,7},{7,5},{5,4},{8,10},{10,11},{11... | collective-permute-start | bytes 1179656 | tf_op jit(solution)/shard_map/ppermute | solution.py:356
  83.9 2.1 %shard_map.102.part_ref = f32[192,1024]{1,0:T(8,128)S(1)} custom-call(s32[2]{0:T(128)S(1)} %pad_add_fusion.place_ref, bf16[192,1024]{1,0:T(8,128)(2,1)S(1)} %shard_map.101.mine_ref.refs_3_, bf16[192,1024]{1,0:T(8,128)(2,1)S(1)} %collective-permute-done.22.theirs_ref.refs_7_, bf16[1024,2048]{1,0:T(8,128)(2,1)S(1)} %copy-done.2), custom_call_target="tpu_custom_call" | custom-call | flops 10000000 | bytes 1024 | tf_op jit(solution)/shard_map/pallas_call | solution.py:74
  86.0 6.6 %shard_map.103 = f32[1024,2048]{1,0:T(8,128)} custom-call(s32[2]{0:T(128)S(1)} %pad_add_fusion.place_ref, bf16[384,1024]{1,0:T(8,128)(2,1)S(1)} %shard_map.78.refs_0_, bf16[192,1024]{1,0:T(8,128)(2,1)S(1)} %shard_map.79.refs_1_, bf16[192,1024]{1,0:T(8,128)(2,1)S(1)} %collective-permute-done.19.refs_2_, bf16[192,1024]{1,0:T(8,128)(2,1)S(1)} %shard_map.101.mine_ref.refs_3_, ...), custom_call_target="tpu_custom_call" | custom-call | flops 3000000000 | bytes 1024 | tf_op jit(solution)/shard_map/pallas_call | solution.py:74
  92.6 1.4 %shard_map.104 = bf16[192,1024]{1,0:T(8,128)(2,1)} custom-call(s32[2]{0:T(128)S(1)} %pad_add_fusion.place_ref, f32[192,1024]{1,0:T(8,128)S(1)} %shard_map.102.part_ref, bf16[192,1024]{1,0:T(8,128)(2,1)S(1)} %collective-permute-done.23.refs_0_), custom_call_target="tpu_custom_call" | custom-call | flops 10000000 | bytes 1024 | tf_op jit(solution)/shard_map/pallas_call | solution.py:74
  (60 shorter events, 16.1 us)
Async XLA Ops:
  0.7 5.7 %collective-permute-start = (bf16[192,2048]{1,0:T(8,128)(2,1)}, bf16[192,2048]{1,0:T(8,128)(2,1)S(1)}, u32[]{:S(2)}, u32[]{:S(2)}) collective-permute-start(bf16[192,2048]{1,0:T(8,128)(2,1)} %mine_ref), channel_id=1, source_target_pairs={{0,4},{4,0},{8,12},{12,8},{1,5},{5,1},{9,13},{13,9},{2,6},{6,2},{1... | collective-permute-start | bytes 2359304 | tf_op jit(solution)/shard_map/ppermute | solution.py:298
  1.2 13.9 %collective-permute-start.4 = (bf16[192,1024]{1,0:T(8,128)(2,1)}, bf16[192,1024]{1,0:T(8,128)(2,1)S(1)}, u32[]{:S(2)}, u32[]{:S(2)}) collective-permute-start(bf16[192,1024]{1,0:T(8,128)(2,1)} %refs_0_.2), channel_id=1, source_target_pairs={{0,2},{2,3},{3,1},{1,0},{4,6},{6,7},{7,5},{5,4},{8,10},{10,11},{11... | collective-permute-start | bytes 1179656 | tf_op jit(solution)/shard_map/ppermute | solution.py:326
  4.8 18.2 %collective-permute-start.2 = (bf16[192,1024]{1,0:T(8,128)(2,1)}, bf16[192,1024]{1,0:T(8,128)(2,1)S(1)}, u32[]{:S(2)}, u32[]{:S(2)}) collective-permute-start(bf16[192,1024]{1,0:T(8,128)(2,1)} %refs_0_.1), channel_id=1, source_target_pairs={{0,2},{2,3},{3,1},{1,0},{4,6},{6,7},{7,5},{5,4},{8,10},{10,11},{11... | collective-permute-start | bytes 1179656 | tf_op jit(solution)/shard_map/ppermute | solution.py:323
  6.4 1.1 %copy-start.5 = (bf16[192,2048]{1,0:T(8,128)(2,1)S(1)}, bf16[192,2048]{1,0:T(8,128)(2,1)}, u32[]{:S(2)}) copy-start(bf16[192,2048]{1,0:T(8,128)(2,1)} %mine_ref) | copy-start | bytes 2359300
  8.1 28.3 %collective-permute-start.1 = (bf16[384,1024]{1,0:T(8,128)(2,1)S(1)}, bf16[384,1024]{1,0:T(8,128)(2,1)S(1)}, u32[]{:S(2)}, u32[]{:S(2)}) collective-permute-start(bf16[384,1024]{1,0:T(8,128)(2,1)S(1)} %shard_map.76.refs_0_), channel_id=1, source_target_pairs={{0,8},{4,12},{8,0},{12,4},{1,9},{5,13},{9,1},{13,5},{2,10},{6,14},... | collective-permute-start | bytes 2359304 | tf_op jit(solution)/shard_map/ppermute | solution.py:299
  9.7 2.2 %copy-start = (bf16[2048,1024]{1,0:T(8,128)(2,1)S(1)}, bf16[2048,1024]{1,0:T(8,128)(2,1)}, u32[]{:S(2)}) copy-start(bf16[2048,1024]{1,0:T(8,128)(2,1)} %down_ref.7) | copy-start | bytes 12582916
  11.9 1.0 %copy-start.3 = (bf16[192,1024]{1,0:T(8,128)(2,1)S(1)}, bf16[192,1024]{1,0:T(8,128)(2,1)}, u32[]{:S(2)}) copy-start(bf16[192,1024]{1,0:T(8,128)(2,1)} %refs_0_.2) | copy-start | bytes 1179652
  12.9 5.0 %copy-start.1 = (bf16[2048,1024]{1,0:T(8,128)(2,1)S(1)}, bf16[2048,1024]{1,0:T(8,128)(2,1)}, u32[]{:S(2)}) copy-start(bf16[2048,1024]{1,0:T(8,128)(2,1)} %down_ref.7) | copy-start | bytes 12582916
  12.9 10.1 %copy-start.6 = (bf16[192,1024]{1,0:T(8,128)(2,1)S(1)}, bf16[192,1024]{1,0:T(8,128)(2,1)}, u32[]{:S(2)}) copy-start(bf16[192,1024]{1,0:T(8,128)(2,1)} %refs_0_.1) | copy-start | bytes 1179652
  15.0 28.3 %collective-permute-start.20 = (bf16[192,1024]{1,0:T(8,128)(2,1)S(1)}, bf16[192,1024]{1,0:T(8,128)(2,1)S(1)}, u32[]{:S(2)}, u32[]{:S(2)}) collective-permute-start(bf16[192,1024]{1,0:T(8,128)(2,1)S(1)} %get-tuple-element.63), channel_id=1, source_target_pairs={{0,4},{4,0},{8,12},{12,8},{1,5},{5,1},{9,13},{13,9},{2,6},{6,2},{1... | collective-permute-start | bytes 1179656 | tf_op jit(solution)/shard_map/ppermute | solution.py:304
  15.0 15.8 %collective-permute-start.5 = (bf16[192,1024]{1,0:T(8,128)(2,1)S(1)}, bf16[192,1024]{1,0:T(8,128)(2,1)S(1)}, u32[]{:S(2)}, u32[]{:S(2)}) collective-permute-start(bf16[192,1024]{1,0:T(8,128)(2,1)S(1)} %collective-permute-done.4.cot_ref.refs_1_), channel_id=1, source_target_pairs={{0,2},{2,3},{3,1},{1,0},{4,6},{6,7},{7,5},{5,4},{8,10},{10,11},{11... | collective-permute-start | bytes 1179656 | tf_op jit(solution)/shard_map/ppermute | solution.py:326
  19.9 3.7 %collective-permute-start.6 = (bf16[192,1024]{1,0:T(8,128)(2,1)S(1)}, bf16[192,1024]{1,0:T(8,128)(2,1)S(1)}, u32[]{:S(2)}, u32[]{:S(2)}) collective-permute-start(bf16[192,1024]{1,0:T(8,128)(2,1)S(1)} %get-tuple-element.45), channel_id=1, source_target_pairs={{0,4},{4,0},{8,12},{12,8},{1,5},{5,1},{9,13},{13,9},{2,6},{6,2},{1... | collective-permute-start | bytes 1179656 | tf_op jit(solution)/shard_map/ppermute | solution.py:304
  24.2 13.8 %collective-permute-start.10 = (bf16[192,1024]{1,0:T(8,128)(2,1)S(1)}, bf16[192,1024]{1,0:T(8,128)(2,1)S(1)}, u32[]{:S(2)}, u32[]{:S(2)}) collective-permute-start(bf16[192,1024]{1,0:T(8,128)(2,1)S(1)} %shard_map.82), channel_id=1, source_target_pairs={{0,8},{4,12},{8,0},{12,4},{1,9},{5,13},{9,1},{13,5},{2,10},{6,14},... | collective-permute-start | bytes 1179656 | tf_op jit(solution)/shard_map/ppermute | solution.py:310
  30.9 13.0 %collective-permute-start.13 = (bf16[192,1024]{1,0:T(8,128)(2,1)S(1)}, bf16[192,1024]{1,0:T(8,128)(2,1)S(1)}, u32[]{:S(2)}, u32[]{:S(2)}) collective-permute-start(bf16[192,1024]{1,0:T(8,128)(2,1)S(1)} %collective-permute-done.5.cot_ref.refs_2_), channel_id=1, source_target_pairs={{0,2},{2,3},{3,1},{1,0},{4,6},{6,7},{7,5},{5,4},{8,10},{10,11},{11... | collective-permute-start | bytes 1179656 | tf_op jit(solution)/shard_map/ppermute | solution.py:326
  36.3 4.1 %collective-permute-start.7 = (bf16[192,1024]{1,0:T(8,128)(2,1)S(1)}, bf16[192,1024]{1,0:T(8,128)(2,1)S(1)}, u32[]{:S(2)}, u32[]{:S(2)}) collective-permute-start(bf16[192,1024]{1,0:T(8,128)(2,1)S(1)} %get-tuple-element.48), channel_id=1, source_target_pairs={{0,4},{4,0},{8,12},{12,8},{1,5},{5,1},{9,13},{13,9},{2,6},{6,2},{1... | collective-permute-start | bytes 1179656 | tf_op jit(solution)/shard_map/ppermute | solution.py:304
  38.7 5.2 %copy-start.2 = (bf16[1024,2048]{1,0:T(8,128)(2,1)S(1)}, bf16[1024,2048]{1,0:T(8,128)(2,1)}, u32[]{:S(2)}) copy-start(bf16[1024,2048]{1,0:T(8,128)(2,1)} %up_ref.7) | copy-start | bytes 12582916
  39.8 4.1 %collective-permute-start.11 = (bf16[192,1024]{1,0:T(8,128)(2,1)S(1)}, bf16[192,1024]{1,0:T(8,128)(2,1)S(1)}, u32[]{:S(2)}, u32[]{:S(2)}) collective-permute-start(bf16[192,1024]{1,0:T(8,128)(2,1)S(1)} %shard_map.89.mine_ref.refs_4_), channel_id=1, source_target_pairs={{0,4},{4,0},{8,12},{12,8},{1,5},{5,1},{9,13},{13,9},{2,6},{6,2},{1... | collective-permute-start | bytes 1179656 | tf_op jit(solution)/shard_map/ppermute | solution.py:316
  41.0 11.1 %collective-permute-start.8 = (bf16[192,1024]{1,0:T(8,128)(2,1)S(1)}, bf16[192,1024]{1,0:T(8,128)(2,1)S(1)}, u32[]{:S(2)}, u32[]{:S(2)}) collective-permute-start(bf16[192,1024]{1,0:T(8,128)(2,1)S(1)} %shard_map.84), channel_id=1, source_target_pairs={{0,8},{4,12},{8,0},{12,4},{1,9},{5,13},{9,1},{13,5},{2,10},{6,14},... | collective-permute-start | bytes 1179656 | tf_op jit(solution)/shard_map/ppermute | solution.py:310
  42.6 13.6 %collective-permute-start.3 = (bf16[192,1024]{1,0:T(8,128)(2,1)S(1)}, bf16[192,1024]{1,0:T(8,128)(2,1)S(1)}, u32[]{:S(2)}, u32[]{:S(2)}) collective-permute-start(bf16[192,1024]{1,0:T(8,128)(2,1)S(1)} %collective-permute-done.2.refs_1_), channel_id=1, source_target_pairs={{0,2},{2,3},{3,1},{1,0},{4,6},{6,7},{7,5},{5,4},{8,10},{10,11},{11... | collective-permute-start | bytes 1179656 | tf_op jit(solution)/shard_map/ppermute | solution.py:331
  43.9 24.5 %collective-permute-start.16 = (bf16[768,1024]{1,0:T(8,128)(2,1)S(1)}, bf16[768,1024]{1,0:T(8,128)(2,1)S(1)}, u32[]{:S(2)}, u32[]{:S(2)}) collective-permute-start(bf16[768,1024]{1,0:T(8,128)(2,1)S(1)} %get-tuple-element.58.mine_ref), channel_id=1, source_target_pairs={{0,4},{4,0},{8,12},{12,8},{1,5},{5,1},{9,13},{13,9},{2,6},{6,2},{1... | collective-permute-start | bytes 4718600 | tf_op jit(solution)/shard_map/ppermute | solution.py:334
  46.9 14.8 %collective-permute-start.12 = (bf16[192,1024]{1,0:T(8,128)(2,1)S(1)}, bf16[192,1024]{1,0:T(8,128)(2,1)S(1)}, u32[]{:S(2)}, u32[]{:S(2)}) collective-permute-start(bf16[192,1024]{1,0:T(8,128)(2,1)S(1)} %get-tuple-element.50), channel_id=1, source_target_pairs={{0,2},{2,3},{3,1},{1,0},{4,6},{6,7},{7,5},{5,4},{8,10},{10,11},{11... | collective-permute-start | bytes 1179656 | tf_op jit(solution)/shard_map/ppermute | solution.py:343
  50.9 3.1 %collective-permute-start.14 = (bf16[192,1024]{1,0:T(8,128)(2,1)S(1)}, bf16[192,1024]{1,0:T(8,128)(2,1)S(1)}, u32[]{:S(2)}, u32[]{:S(2)}) collective-permute-start(bf16[192,1024]{1,0:T(8,128)(2,1)S(1)} %get-tuple-element.56), channel_id=1, source_target_pairs={{0,4},{4,0},{8,12},{12,8},{1,5},{5,1},{9,13},{13,9},{2,6},{6,2},{1... | collective-permute-start | bytes 1179656 | tf_op jit(solution)/shard_map/ppermute | solution.py:304
  53.9 2.8 %collective-permute-start.9 = (bf16[192,1024]{1,0:T(8,128)(2,1)S(1)}, bf16[192,1024]{1,0:T(8,128)(2,1)S(1)}, u32[]{:S(2)}, u32[]{:S(2)}) collective-permute-start(bf16[192,1024]{1,0:T(8,128)(2,1)S(1)} %shard_map.86.mine_ref.refs_5_), channel_id=1, source_target_pairs={{0,4},{4,0},{8,12},{12,8},{1,5},{5,1},{9,13},{13,9},{2,6},{6,2},{1... | collective-permute-start | bytes 1179656 | tf_op jit(solution)/shard_map/ppermute | solution.py:316
  54.6 12.0 %collective-permute-start.15 = (bf16[192,1024]{1,0:T(8,128)(2,1)S(1)}, bf16[192,1024]{1,0:T(8,128)(2,1)S(1)}, u32[]{:S(2)}, u32[]{:S(2)}) collective-permute-start(bf16[192,1024]{1,0:T(8,128)(2,1)S(1)} %shard_map.93), channel_id=1, source_target_pairs={{0,8},{4,12},{8,0},{12,4},{1,9},{5,13},{9,1},{13,5},{2,10},{6,14},... | collective-permute-start | bytes 1179656 | tf_op jit(solution)/shard_map/ppermute | solution.py:310
  62.4 6.0 %copy-start.4 = (bf16[192,1024]{1,0:T(8,128)(2,1)S(1)}, bf16[192,1024]{1,0:T(8,128)(2,1)}, u32[]{:S(2)}) copy-start(bf16[192,1024]{1,0:T(8,128)(2,1)} %refs_0_.2) | copy-start | bytes 1179652
  62.4 12.5 %collective-permute-start.19 = (bf16[192,1024]{1,0:T(8,128)(2,1)S(1)}, bf16[192,1024]{1,0:T(8,128)(2,1)S(1)}, u32[]{:S(2)}, u32[]{:S(2)}) collective-permute-start(bf16[192,1024]{1,0:T(8,128)(2,1)S(1)} %collective-permute-done.3.refs_0_), channel_id=1, source_target_pairs={{0,2},{2,3},{3,1},{1,0},{4,6},{6,7},{7,5},{5,4},{8,10},{10,11},{11... | collective-permute-start | bytes 1179656 | tf_op jit(solution)/shard_map/ppermute | solution.py:346
  64.0 10.9 %collective-permute-start.21 = (bf16[192,1024]{1,0:T(8,128)(2,1)S(1)}, bf16[192,1024]{1,0:T(8,128)(2,1)S(1)}, u32[]{:S(2)}, u32[]{:S(2)}) collective-permute-start(bf16[192,1024]{1,0:T(8,128)(2,1)S(1)} %shard_map.99), channel_id=1, source_target_pairs={{0,8},{4,12},{8,0},{12,4},{1,9},{5,13},{9,1},{13,5},{2,10},{6,14},... | collective-permute-start | bytes 1179656 | tf_op jit(solution)/shard_map/ppermute | solution.py:310
  64.8 15.9 %collective-permute-start.18 = (bf16[192,1024]{1,0:T(8,128)(2,1)S(1)}, bf16[192,1024]{1,0:T(8,128)(2,1)S(1)}, u32[]{:S(2)}, u32[]{:S(2)}) collective-permute-start(bf16[192,1024]{1,0:T(8,128)(2,1)S(1)} %shard_map.91), channel_id=1, source_target_pairs={{0,2},{2,3},{3,1},{1,0},{4,6},{6,7},{7,5},{5,4},{8,10},{10,11},{11... | collective-permute-start | bytes 1179656 | tf_op jit(solution)/shard_map/ppermute | solution.py:343
  68.3 8.9 %collective-permute-start.17 = (bf16[192,1024]{1,0:T(8,128)(2,1)S(1)}, bf16[192,1024]{1,0:T(8,128)(2,1)S(1)}, u32[]{:S(2)}, u32[]{:S(2)}) collective-permute-start(bf16[192,1024]{1,0:T(8,128)(2,1)S(1)} %shard_map.95.mine_ref.refs_6_), channel_id=1, source_target_pairs={{0,4},{4,0},{8,12},{12,8},{1,5},{5,1},{9,13},{13,9},{2,6},{6,2},{1... | collective-permute-start | bytes 1179656 | tf_op jit(solution)/shard_map/ppermute | solution.py:316
  76.6 7.2 %collective-permute-start.22 = (bf16[192,1024]{1,0:T(8,128)(2,1)S(1)}, bf16[192,1024]{1,0:T(8,128)(2,1)S(1)}, u32[]{:S(2)}, u32[]{:S(2)}) collective-permute-start(bf16[192,1024]{1,0:T(8,128)(2,1)S(1)} %shard_map.101.mine_ref.refs_3_), channel_id=1, source_target_pairs={{0,4},{4,0},{8,12},{12,8},{1,5},{5,1},{9,13},{13,9},{2,6},{6,2},{1... | collective-permute-start | bytes 1179656 | tf_op jit(solution)/shard_map/ppermute | solution.py:316
  81.4 11.3 %collective-permute-start.23 = (bf16[192,1024]{1,0:T(8,128)(2,1)S(1)}, bf16[192,1024]{1,0:T(8,128)(2,1)S(1)}, u32[]{:S(2)}, u32[]{:S(2)}) collective-permute-start(bf16[192,1024]{1,0:T(8,128)(2,1)S(1)} %shard_map.98), channel_id=1, source_target_pairs={{0,2},{2,3},{3,1},{1,0},{4,6},{6,7},{7,5},{5,4},{8,10},{10,11},{11... | collective-permute-start | bytes 1179656 | tf_op jit(solution)/shard_map/ppermute | solution.py:356

commit v15 on v14

--- a/solution.py
+++ b/solution.py
@@ -149,13 +149,13 @@
         out_ref[here, :] = (total * gelu_slope(v)).astype(jnp.bfloat16)
 
 
-def pre_grad_call(place, step, cols, pre_all, part, others):
+def pre_grad_call(place, step, cols, pre_all, part, others, cost):
     out = jax.ShapeDtypeStruct(part.shape, jnp.bfloat16)
     kernel = functools.partial(pre_grad_kernel, step, cols)
-    return call(kernel, place, [pre_all, part, *others], out, 8, 100000000)
-
-
-def share_kernel(place_ref, mine_ref, theirs_ref, up_ref, out_ref, *sent_refs):
+    return call(kernel, place, [pre_all, part, *others], out, 8, cost)
+
+
+def share_kernel(place_ref, mine_ref, theirs_ref, up_ref, out_ref):
     features, half = up_ref.shape[0], mine_ref.shape[1]
     tile = tile_of(features)
     left, right = block(core_of(place_ref), half), block(1 - core_of(place_ref), half)
@@ -163,16 +163,12 @@
         here = pl.ds(first, tile)
         total = dot(mine_ref[...], up_ref[here, left], LAST)
         total = total + dot(theirs_ref[...], up_ref[here, right], LAST)
-        out_ref[:, here] = total
-        for sent in sent_refs:
-            sent[:, here] = total.astype(jnp.bfloat16)
-
-
-def share_call(place, mine, theirs, up_weight, first):
-    shape = (mine.shape[0], up_weight.shape[0])
-    outs = [jax.ShapeDtypeStruct(shape, jnp.float32)]
-    outs += [jax.ShapeDtypeStruct(shape, jnp.bfloat16)] * first
-    return call(share_kernel, place, [mine, theirs, up_weight], outs, 12, 10000000)
+        out_ref[:, here] = total.astype(out_ref.dtype)
+
+
+def share_call(place, mine, theirs, up_weight, dtype):
+    out = jax.ShapeDtypeStruct((mine.shape[0], up_weight.shape[0]), dtype)
+    return call(share_kernel, place, [mine, theirs, up_weight], out, 12, 10000000)
 
 
 def add_kernel(place_ref, part_ref, *refs):
@@ -311,12 +307,12 @@
 
     def pre_grad(s, *first):
         own, arrived = parts[s]
-        total = add_call(after(place, *first), own, [arrived, *others[s]], jnp.float32, ADD_COST.get(s, MUCH))
-        mine[s] = pre_grad_call(place, s, cols, pre_all, total, [])
+        here, terms = after(place, *first), [arrived, *others[s]]
+        mine[s] = pre_grad_call(here, s, cols, pre_all, own, terms, ADD_COST[min(s, 3)])
         theirs[s] = lax.ppermute(mine[s], "row", pair)
 
     def share(s, *first):
-        return share_call(after(place, *first), mine[s], theirs[s], up_weight, s == 1)
+        return share_call(after(place, *first), mine[s], theirs[s], up_weight, jnp.bfloat16 if s == 1 else jnp.float32)
 
     cots = [cotangent]
     hidden_part(0)
@@ -334,7 +330,7 @@
     act_theirs = lax.ppermute(act, "row", pair)
 
     pre_grad(1, pre_all)
-    sums = share(1)[1]
+    sums = share(1)
     cots[last] = after(cots[last], sums)
     hidden_part(last, sums)
     exchange(last)
@@ -351,10 +347,10 @@
             )
             pre_grad(0, grad_down, ins[s])
             first = [grad_down]
-        part = share(s, *first, *([second] if s == 2 else []))[0]
+        part = share(s, *first, *([second] if s == 2 else []))
         sums = late = add_call(place, part, [arrived], jnp.bfloat16, LITTLE)
     arrived = lax.ppermute(sums, "col", ring)
-    part = share(0, sums)[0]
+    part = share(0, sums)
     grad_up = grad_up_call(after(place, part), [near, second, *ins[3:]], mine, theirs, scale)
     sums = add_call(after(place, grad_up), part, [arrived], jnp.bfloat16, LITTLE)
     return (sums, grad_up, grad_down)

time: 94.2 us -> 93.6 us (level)
  Pallas kernels: 45.9 us -> 42.8 us
  waiting for transfers between devices: 15.2 us -> 17 us
    pallas_call x29 -> x25, Pallas kernels: 45.9 us -> 42.8 us  [call(): pl.pallas_call(kernel, out_shape=outs, grid_spec=pltpu.PrefetchScalarGrid...]
    ppermute x3, waiting for transfers between devices: 4.45 us -> 6.43 us  [per_device(): arrived = lax.ppermute(sums, 'col', ring)]
    ppermute x4, waiting for transfers between devices: 2.59 us -> 1.54 us  [exchange(): others[s] = [lax.ppermute(values, 'row', to) for to in over_x]]
  transfers between devices with their start and end apart: 24 -> 24, of which waited for: 6 -> 7; matrix products, arithmetic and copies ran while one was open for 0% -> 0% of each run, Pallas kernels for 47% -> 44%
where the time goes in v15:
time: 93.6 us; the launch traced here: 93.4 us
  Pallas kernels  42.8 us (46%)
  starting transfers between devices  28.2 us (30%)
  waiting for transfers between devices  17 us (18%)
  local copies, waits for them, and re-layouts  4.34 us (5%)
  between operations  0.96 us (1%)
    pallas_call x25, Pallas kernels, call(): pl.pallas_call(kernel, out_shape=outs, grid_spec=pltpu.PrefetchScalarGrid...  42.8 us
    ppermute x3, starting transfers between devices, per_device(): arriving = lax.ppermute(cots[s - 1], 'col', ring)  9.84 us
    ppermute x3, waiting for transfers between devices, per_device(): arrived = lax.ppermute(sums, 'col', ring)  6.43 us
    ppermute x4, starting transfers between devices, exchange(): others[s] = [lax.ppermute(values, 'row', to) for to in over_x]  6.08 us
    ppermute x3, waiting for transfers between devices, per_device(): arriving = lax.ppermute(cots[s - 1], 'col', ring)  5.08 us
    ppermute x3, starting transfers between devices, per_device(): arrived = lax.ppermute(sums, 'col', ring)  5.08 us
    unnamed x14, local copies, waits for them, and re-layouts  4.34 us
    ppermute x1, waiting for transfers between devices, per_device(): ins = [inputs, lax.ppermute(after(inputs, place), 'col', ring)]  3 us
  transfers between devices with their start and end apart: 24, of which 7 were waited for; matrix products, arithmetic and copies ran while one was open for 0% of the time, Pallas kernels for 44%

profile of v15, /device:TPU:0, one launch (start us, length us, event | category | flops | bytes accessed | tf_op | source)
XLA Modules:
  0.0 93.4 jit_solution(6327617106542781861)
XLA Ops:
  1.2 3.7 %collective-permute-start.4 = (bf16[192,1024]{1,0:T(8,128)(2,1)}, bf16[192,1024]{1,0:T(8,128)(2,1)S(1)}, u32[]{:S(2)}, u32[]{:S(2)}) collective-permute-start(bf16[192,1024]{1,0:T(8,128)(2,1)} %refs_0_.2), channel_id=1, source_target_pairs={{0,2},{2,3},{3,1},{1,0},{4,6},{6,7},{7,5},{5,4},{8,10},{10,11},{11... | collective-permute-start | bytes 1179656 | tf_op jit(solution)/shard_map/ppermute | solution.py:322
  4.8 1.6 %collective-permute-start = (bf16[192,1024]{1,0:T(8,128)(2,1)}, bf16[192,1024]{1,0:T(8,128)(2,1)S(1)}, u32[]{:S(2)}, u32[]{:S(2)}) collective-permute-start(bf16[192,1024]{1,0:T(8,128)(2,1)} %refs_0_.1), channel_id=1, source_target_pairs={{0,2},{2,3},{3,1},{1,0},{4,6},{6,7},{7,5},{5,4},{8,10},{10,11},{11... | collective-permute-start | bytes 1179656 | tf_op jit(solution)/shard_map/ppermute | solution.py:319
  8.1 1.6 %collective-permute-start.3 = (bf16[384,1024]{1,0:T(8,128)(2,1)S(1)}, bf16[384,1024]{1,0:T(8,128)(2,1)S(1)}, u32[]{:S(2)}, u32[]{:S(2)}) collective-permute-start(bf16[384,1024]{1,0:T(8,128)(2,1)S(1)} %shard_map.78.refs_0_), channel_id=1, source_target_pairs={{0,8},{4,12},{8,0},{12,4},{1,9},{5,13},{9,1},{13,5},{2,10},{6,14},... | collective-permute-start | bytes 2359304 | tf_op jit(solution)/shard_map/ppermute | solution.py:295
  9.7 2.2 %copy-done = bf16[2048,1024]{1,0:T(8,128)(2,1)S(1)} copy-done((bf16[2048,1024]{1,0:T(8,128)(2,1)S(1)}, bf16[2048,1024]{1,0:T(8,128)(2,1)}, u32[]{:S(2)}) %copy-start) | copy-done | bytes 4194328
  12.9 2.1 %shard_map.80 = (f32[192,1024]{1,0:T(8,128)S(1)}, bf16[192,1024]{1,0:T(8,128)(2,1)S(1)}) custom-call(s32[2]{0:T(128)S(1)} %pad_add_fusion.place_ref, bf16[192,1024]{1,0:T(8,128)(2,1)S(1)} %copy-done.3, bf16[2048,1024]{1,0:T(8,128)(2,1)S(1)} %copy-done), custom_call_target="tpu_custom_call" | custom-call | flops 10000000 | bytes 1024 | tf_op jit(solution)/shard_map/pallas_call | solution.py:74
  15.0 2.8 %collective-permute-start.5 = (bf16[192,1024]{1,0:T(8,128)(2,1)S(1)}, bf16[192,1024]{1,0:T(8,128)(2,1)S(1)}, u32[]{:S(2)}, u32[]{:S(2)}) collective-permute-start(bf16[192,1024]{1,0:T(8,128)(2,1)S(1)} %collective-permute-done.4.cot_ref.refs_1_), channel_id=1, source_target_pairs={{0,2},{2,3},{3,1},{1,0},{4,6},{6,7},{7,5},{5,4},{8,10},{10,11},{11... | collective-permute-start | bytes 1179656 | tf_op jit(solution)/shard_map/ppermute | solution.py:322
  17.9 2.1 %shard_map.81 = (f32[192,1024]{1,0:T(8,128)S(1)}, bf16[192,1024]{1,0:T(8,128)(2,1)S(1)}) custom-call(s32[2]{0:T(128)S(1)} %pad_add_fusion.place_ref, bf16[192,1024]{1,0:T(8,128)(2,1)S(1)} %collective-permute-done.4.cot_ref.refs_1_, bf16[2048,1024]{1,0:T(8,128)(2,1)S(1)} %copy-done.1), custom_call_target="tpu_custom_call" | custom-call | flops 10000000 | bytes 1024 | tf_op jit(solution)/shard_map/pallas_call | solution.py:74
  20.0 3.0 %collective-permute-done.refs_1_ = bf16[192,1024]{1,0:T(8,128)(2,1)S(1)} collective-permute-done((bf16[192,1024]{1,0:T(8,128)(2,1)}, bf16[192,1024]{1,0:T(8,128)(2,1)S(1)}, u32[]{:S(2)}, u32[]{:S(2)}) %collective-permute-start) | collective-permute-done | bytes 393248 | tf_op jit(solution)/shard_map/ppermute | solution.py:319
  24.2 1.6 %collective-permute-start.10 = (bf16[192,1024]{1,0:T(8,128)(2,1)S(1)}, bf16[192,1024]{1,0:T(8,128)(2,1)S(1)}, u32[]{:S(2)}, u32[]{:S(2)}) collective-permute-start(bf16[192,1024]{1,0:T(8,128)(2,1)S(1)} %shard_map.82), channel_id=1, source_target_pairs={{0,8},{4,12},{8,0},{12,4},{1,9},{5,13},{9,1},{13,5},{2,10},{6,14},... | collective-permute-start | bytes 1179656 | tf_op jit(solution)/shard_map/ppermute | solution.py:306
  25.8 5.1 %collective-permute-done.5.cot_ref.refs_2_ = bf16[192,1024]{1,0:T(8,128)(2,1)S(1)} collective-permute-done((bf16[192,1024]{1,0:T(8,128)(2,1)S(1)}, bf16[192,1024]{1,0:T(8,128)(2,1)S(1)}, u32[]{:S(2)}, u32[]{:S(2)}) %collective-permute-start.5) | collective-permute-done | bytes 393248 | tf_op jit(solution)/shard_map/ppermute | solution.py:322
  30.9 3.4 %collective-permute-start.13 = (bf16[192,1024]{1,0:T(8,128)(2,1)S(1)}, bf16[192,1024]{1,0:T(8,128)(2,1)S(1)}, u32[]{:S(2)}, u32[]{:S(2)}) collective-permute-start(bf16[192,1024]{1,0:T(8,128)(2,1)S(1)} %collective-permute-done.5.cot_ref.refs_2_), channel_id=1, source_target_pairs={{0,2},{2,3},{3,1},{1,0},{4,6},{6,7},{7,5},{5,4},{8,10},{10,11},{11... | collective-permute-start | bytes 1179656 | tf_op jit(solution)/shard_map/ppermute | solution.py:322
  34.2 2.1 %shard_map.83 = (f32[192,1024]{1,0:T(8,128)S(1)}, bf16[192,1024]{1,0:T(8,128)(2,1)S(1)}) custom-call(s32[2]{0:T(128)S(1)} %pad_add_fusion.place_ref, bf16[192,1024]{1,0:T(8,128)(2,1)S(1)} %collective-permute-done.5.cot_ref.refs_2_, bf16[2048,1024]{1,0:T(8,128)(2,1)S(1)} %copy-done.1), custom_call_target="tpu_custom_call" | custom-call | flops 10000000 | bytes 1024 | tf_op jit(solution)/shard_map/pallas_call | solution.py:74
  36.4 1.7 %shard_map.79 = (bf16[768,1024]{1,0:T(8,128)(2,1)S(1)}, bf16[768,1024]{1,0:T(8,128)(2,1)S(1)}) custom-call(s32[2]{0:T(128)S(1)} %pad_add_fusion.place_ref, bf16[384,1024]{1,0:T(8,128)(2,1)S(1)} %shard_map.78.refs_0_, bf16[384,1024]{1,0:T(8,128)(2,1)S(1)} %collective-permute-done.3.refs_1_), custom_call_target="tpu_custom_call" | custom-call | flops 6000000000 | bytes 1024 | tf_op jit(solution)/shard_map/pallas_call | solution.py:74
  38.1 1.2 %shard_map.87.mine_ref.refs_4_ = bf16[192,1024]{1,0:T(8,128)(2,1)S(1)} custom-call(s32[2]{0:T(128)S(1)} %pad_add_fusion.place_ref, bf16[768,1024]{1,0:T(8,128)(2,1)S(1)} %get-tuple-element.38.pre_ref, f32[192,1024]{1,0:T(8,128)S(1)} %get-tuple-element.43.part_ref, bf16[192,1024]{1,0:T(8,128)(2,1)S(1)} %collective-permute-done.6.refs_0_, ...), custom_call_target="tpu_custom_call" | custom-call | flops 3000000000 | bytes 1024 | tf_op jit(solution)/shard_map/pallas_call | solution.py:74
  40.4 1.6 %collective-permute-start.8 = (bf16[192,1024]{1,0:T(8,128)(2,1)S(1)}, bf16[192,1024]{1,0:T(8,128)(2,1)S(1)}, u32[]{:S(2)}, u32[]{:S(2)}) collective-permute-start(bf16[192,1024]{1,0:T(8,128)(2,1)S(1)} %shard_map.84), channel_id=1, source_target_pairs={{0,8},{4,12},{8,0},{12,4},{1,9},{5,13},{9,1},{13,5},{2,10},{6,14},... | collective-permute-start | bytes 1179656 | tf_op jit(solution)/shard_map/ppermute | solution.py:306
  43.4 2.1 %shard_map.88 = bf16[192,1024]{1,0:T(8,128)(2,1)S(1)} custom-call(s32[2]{0:T(128)S(1)} %pad_add_fusion.place_ref, bf16[192,1024]{1,0:T(8,128)(2,1)S(1)} %shard_map.87.mine_ref.refs_4_, bf16[192,1024]{1,0:T(8,128)(2,1)S(1)} %collective-permute-done.11.theirs_ref.refs_8_, bf16[1024,2048]{1,0:T(8,128)(2,1)S(1)} %copy-done.2), custom_call_target="tpu_custom_call" | custom-call | flops 10000000 | bytes 1024 | tf_op jit(solution)/shard_map/pallas_call | solution.py:74
  45.5 2.5 %collective-permute-start.12 = (bf16[192,1024]{1,0:T(8,128)(2,1)S(1)}, bf16[192,1024]{1,0:T(8,128)(2,1)S(1)}, u32[]{:S(2)}, u32[]{:S(2)}) collective-permute-start(bf16[192,1024]{1,0:T(8,128)(2,1)S(1)} %shard_map.88), channel_id=1, source_target_pairs={{0,2},{2,3},{3,1},{1,0},{4,6},{6,7},{7,5},{5,4},{8,10},{10,11},{11... | collective-permute-start | bytes 1179656 | tf_op jit(solution)/shard_map/ppermute | solution.py:339
  48.0 2.1 %shard_map.90 = (f32[192,1024]{1,0:T(8,128)S(1)}, bf16[192,1024]{1,0:T(8,128)(2,1)S(1)}) custom-call(s32[2]{0:T(128)S(1)} %pad_add_fusion.place_ref, bf16[192,1024]{1,0:T(8,128)(2,1)S(1)} %collective-permute-done.13.cot_ref.refs_3_, bf16[2048,1024]{1,0:T(8,128)(2,1)S(1)} %copy-done.1), custom_call_target="tpu_custom_call" | custom-call | flops 10000000 | bytes 1024 | tf_op jit(solution)/shard_map/pallas_call | solution.py:74
  50.3 1.2 %collective-permute-done.8.refs_1_ = bf16[192,1024]{1,0:T(8,128)(2,1)S(1)} collective-permute-done((bf16[192,1024]{1,0:T(8,128)(2,1)S(1)}, bf16[192,1024]{1,0:T(8,128)(2,1)S(1)}, u32[]{:S(2)}, u32[]{:S(2)}) %collective-permute-start.8) | collective-permute-done | bytes 393248 | tf_op jit(solution)/shard_map/ppermute | solution.py:306
  53.4 1.6 %collective-permute-start.15 = (bf16[192,1024]{1,0:T(8,128)(2,1)S(1)}, bf16[192,1024]{1,0:T(8,128)(2,1)S(1)}, u32[]{:S(2)}, u32[]{:S(2)}) collective-permute-start(bf16[192,1024]{1,0:T(8,128)(2,1)S(1)} %shard_map.91), channel_id=1, source_target_pairs={{0,8},{4,12},{8,0},{12,4},{1,9},{5,13},{9,1},{13,5},{2,10},{6,14},... | collective-permute-start | bytes 1179656 | tf_op jit(solution)/shard_map/ppermute | solution.py:306
  55.6 2.1 %shard_map.86.part_ref = f32[192,1024]{1,0:T(8,128)S(1)} custom-call(s32[2]{0:T(128)S(1)} %pad_add_fusion.place_ref, bf16[192,1024]{1,0:T(8,128)(2,1)S(1)} %shard_map.85.mine_ref.refs_5_, bf16[192,1024]{1,0:T(8,128)(2,1)S(1)} %collective-permute-done.9.theirs_ref.refs_9_, bf16[1024,2048]{1,0:T(8,128)(2,1)S(1)} %copy-done.2), custom_call_target="tpu_custom_call" | custom-call | flops 10000000 | bytes 1024 | tf_op jit(solution)/shard_map/pallas_call | solution.py:74
  57.7 3.5 %collective-permute-done.12.refs_0_ = bf16[192,1024]{1,0:T(8,128)(2,1)S(1)} collective-permute-done((bf16[192,1024]{1,0:T(8,128)(2,1)S(1)}, bf16[192,1024]{1,0:T(8,128)(2,1)S(1)}, u32[]{:S(2)}, u32[]{:S(2)}) %collective-permute-start.12) | collective-permute-done | bytes 393248 | tf_op jit(solution)/shard_map/ppermute | solution.py:339
  61.8 1.6 %collective-permute-start.19 = (bf16[192,1024]{1,0:T(8,128)(2,1)S(1)}, bf16[192,1024]{1,0:T(8,128)(2,1)S(1)}, u32[]{:S(2)}, u32[]{:S(2)}) collective-permute-start(bf16[192,1024]{1,0:T(8,128)(2,1)S(1)} %collective-permute-done.1.refs_0_), channel_id=1, source_target_pairs={{0,2},{2,3},{3,1},{1,0},{4,6},{6,7},{7,5},{5,4},{8,10},{10,11},{11... | collective-permute-start | bytes 1179656 | tf_op jit(solution)/shard_map/ppermute | solution.py:342
  63.4 1.4 %collective-permute-start.21 = (bf16[192,1024]{1,0:T(8,128)(2,1)S(1)}, bf16[192,1024]{1,0:T(8,128)(2,1)S(1)}, u32[]{:S(2)}, u32[]{:S(2)}) collective-permute-start(bf16[192,1024]{1,0:T(8,128)(2,1)S(1)} %shard_map.96), channel_id=1, source_target_pairs={{0,8},{4,12},{8,0},{12,4},{1,9},{5,13},{9,1},{13,5},{2,10},{6,14},... | collective-permute-start | bytes 1179656 | tf_op jit(solution)/shard_map/ppermute | solution.py:306
  66.5 6.5 %shard_map.93 = f32[2048,1024]{1,0:T(8,128)} custom-call(s32[2]{0:T(128)S(1)} %pad_add_fusion.place_ref, bf16[768,1024]{1,0:T(8,128)(2,1)S(1)} %get-tuple-element.56.mine_ref, bf16[768,1024]{1,0:T(8,128)(2,1)S(1)} %collective-permute-done.16.theirs_ref, bf16[192,1024]{1,0:T(8,128)(2,1)S(1)} %copy-done.4, ...), custom_call_target="tpu_custom_call" | custom-call | flops 100000000 | bytes 1024 | tf_op jit(solution)/shard_map/pallas_call | solution.py:74
  73.9 1.2 %shard_map.97.mine_ref.refs_3_ = bf16[192,1024]{1,0:T(8,128)(2,1)S(1)} custom-call(s32[2]{0:T(128)S(1)} %pad_add_fusion.place_ref, bf16[768,1024]{1,0:T(8,128)(2,1)S(1)} %get-tuple-element.38.pre_ref, f32[192,1024]{1,0:T(8,128)S(1)} %get-tuple-element.41.part_ref, bf16[192,1024]{1,0:T(8,128)(2,1)S(1)} %collective-permute-done.20.refs_0_, ...), custom_call_target="tpu_custom_call" | custom-call | flops 3000000000 | bytes 1024 | tf_op jit(solution)/shard_map/pallas_call | solution.py:74
  75.2 2.1 %shard_map.94.part_ref = f32[192,1024]{1,0:T(8,128)S(1)} custom-call(s32[2]{0:T(128)S(1)} %pad_add_fusion.place_ref, bf16[192,1024]{1,0:T(8,128)(2,1)S(1)} %shard_map.92.mine_ref.refs_6_, bf16[192,1024]{1,0:T(8,128)(2,1)S(1)} %collective-permute-done.17.theirs_ref.refs_10_, bf16[1024,2048]{1,0:T(8,128)(2,1)S(1)} %copy-done.2), custom_call_target="tpu_custom_call" | custom-call | flops 10000000 | bytes 1024 | tf_op jit(solution)/shard_map/pallas_call | solution.py:74
  77.3 2.9 %collective-permute-done.18.refs_0_ = bf16[192,1024]{1,0:T(8,128)(2,1)S(1)} collective-permute-done((bf16[192,1024]{1,0:T(8,128)(2,1)S(1)}, bf16[192,1024]{1,0:T(8,128)(2,1)S(1)}, u32[]{:S(2)}, u32[]{:S(2)}) %collective-permute-start.18) | collective-permute-done | bytes 393248 | tf_op jit(solution)/shard_map/ppermute | solution.py:339
  80.8 2.5 %collective-permute-start.23 = (bf16[192,1024]{1,0:T(8,128)(2,1)S(1)}, bf16[192,1024]{1,0:T(8,128)(2,1)S(1)}, u32[]{:S(2)}, u32[]{:S(2)}) collective-permute-start(bf16[192,1024]{1,0:T(8,128)(2,1)S(1)} %shard_map.95), channel_id=1, source_target_pairs={{0,2},{2,3},{3,1},{1,0},{4,6},{6,7},{7,5},{5,4},{8,10},{10,11},{11... | collective-permute-start | bytes 1179656 | tf_op jit(solution)/shard_map/ppermute | solution.py:352
  83.3 2.1 %shard_map.98.part_ref = f32[192,1024]{1,0:T(8,128)S(1)} custom-call(s32[2]{0:T(128)S(1)} %pad_add_fusion.place_ref, bf16[192,1024]{1,0:T(8,128)(2,1)S(1)} %shard_map.97.mine_ref.refs_3_, bf16[192,1024]{1,0:T(8,128)(2,1)S(1)} %collective-permute-done.22.theirs_ref.refs_7_, bf16[1024,2048]{1,0:T(8,128)(2,1)S(1)} %copy-done.2), custom_call_target="tpu_custom_call" | custom-call | flops 10000000 | bytes 1024 | tf_op jit(solution)/shard_map/pallas_call | solution.py:74
  85.4 6.6 %shard_map.99 = f32[1024,2048]{1,0:T(8,128)} custom-call(s32[2]{0:T(128)S(1)} %pad_add_fusion.place_ref, bf16[384,1024]{1,0:T(8,128)(2,1)S(1)} %shard_map.76.refs_0_, bf16[192,1024]{1,0:T(8,128)(2,1)S(1)} %shard_map.77.refs_1_, bf16[192,1024]{1,0:T(8,128)(2,1)S(1)} %collective-permute-done.19.refs_2_, bf16[192,1024]{1,0:T(8,128)(2,1)S(1)} %shard_map.97.mine_ref.refs_3_, ...), custom_call_target="tpu_custom_call" | custom-call | flops 3000000000 | bytes 1024 | tf_op jit(solution)/shard_map/pallas_call | solution.py:74
  92.0 1.4 %shard_map.100 = bf16[192,1024]{1,0:T(8,128)(2,1)} custom-call(s32[2]{0:T(128)S(1)} %pad_add_fusion.place_ref, f32[192,1024]{1,0:T(8,128)S(1)} %shard_map.98.part_ref, bf16[192,1024]{1,0:T(8,128)(2,1)S(1)} %collective-permute-done.23.refs_0_), custom_call_target="tpu_custom_call" | custom-call | flops 10000000 | bytes 1024 | tf_op jit(solution)/shard_map/pallas_call | solution.py:74
  (56 shorter events, 13.8 us)
Async XLA Ops:
  0.7 5.7 %collective-permute-start.2 = (bf16[192,2048]{1,0:T(8,128)(2,1)}, bf16[192,2048]{1,0:T(8,128)(2,1)S(1)}, u32[]{:S(2)}, u32[]{:S(2)}) collective-permute-start(bf16[192,2048]{1,0:T(8,128)(2,1)} %mine_ref), channel_id=1, source_target_pairs={{0,4},{4,0},{8,12},{12,8},{1,5},{5,1},{9,13},{13,9},{2,6},{6,2},{1... | collective-permute-start | bytes 2359304 | tf_op jit(solution)/shard_map/ppermute | solution.py:294
  1.2 13.9 %collective-permute-start.4 = (bf16[192,1024]{1,0:T(8,128)(2,1)}, bf16[192,1024]{1,0:T(8,128)(2,1)S(1)}, u32[]{:S(2)}, u32[]{:S(2)}) collective-permute-start(bf16[192,1024]{1,0:T(8,128)(2,1)} %refs_0_.2), channel_id=1, source_target_pairs={{0,2},{2,3},{3,1},{1,0},{4,6},{6,7},{7,5},{5,4},{8,10},{10,11},{11... | collective-permute-start | bytes 1179656 | tf_op jit(solution)/shard_map/ppermute | solution.py:322
  4.8 18.2 %collective-permute-start = (bf16[192,1024]{1,0:T(8,128)(2,1)}, bf16[192,1024]{1,0:T(8,128)(2,1)S(1)}, u32[]{:S(2)}, u32[]{:S(2)}) collective-permute-start(bf16[192,1024]{1,0:T(8,128)(2,1)} %refs_0_.1), channel_id=1, source_target_pairs={{0,2},{2,3},{3,1},{1,0},{4,6},{6,7},{7,5},{5,4},{8,10},{10,11},{11... | collective-permute-start | bytes 1179656 | tf_op jit(solution)/shard_map/ppermute | solution.py:319
  6.4 1.1 %copy-start.5 = (bf16[192,2048]{1,0:T(8,128)(2,1)S(1)}, bf16[192,2048]{1,0:T(8,128)(2,1)}, u32[]{:S(2)}) copy-start(bf16[192,2048]{1,0:T(8,128)(2,1)} %mine_ref) | copy-start | bytes 2359300
  8.1 28.3 %collective-permute-start.3 = (bf16[384,1024]{1,0:T(8,128)(2,1)S(1)}, bf16[384,1024]{1,0:T(8,128)(2,1)S(1)}, u32[]{:S(2)}, u32[]{:S(2)}) collective-permute-start(bf16[384,1024]{1,0:T(8,128)(2,1)S(1)} %shard_map.78.refs_0_), channel_id=1, source_target_pairs={{0,8},{4,12},{8,0},{12,4},{1,9},{5,13},{9,1},{13,5},{2,10},{6,14},... | collective-permute-start | bytes 2359304 | tf_op jit(solution)/shard_map/ppermute | solution.py:295
  9.7 2.2 %copy-start = (bf16[2048,1024]{1,0:T(8,128)(2,1)S(1)}, bf16[2048,1024]{1,0:T(8,128)(2,1)}, u32[]{:S(2)}) copy-start(bf16[2048,1024]{1,0:T(8,128)(2,1)} %down_ref.7) | copy-start | bytes 12582916
  11.9 1.0 %copy-start.3 = (bf16[192,1024]{1,0:T(8,128)(2,1)S(1)}, bf16[192,1024]{1,0:T(8,128)(2,1)}, u32[]{:S(2)}) copy-start(bf16[192,1024]{1,0:T(8,128)(2,1)} %refs_0_.2) | copy-start | bytes 1179652
  12.9 5.0 %copy-start.1 = (bf16[2048,1024]{1,0:T(8,128)(2,1)S(1)}, bf16[2048,1024]{1,0:T(8,128)(2,1)}, u32[]{:S(2)}) copy-start(bf16[2048,1024]{1,0:T(8,128)(2,1)} %down_ref.7) | copy-start | bytes 12582916
  12.9 10.1 %copy-start.6 = (bf16[192,1024]{1,0:T(8,128)(2,1)S(1)}, bf16[192,1024]{1,0:T(8,128)(2,1)}, u32[]{:S(2)}) copy-start(bf16[192,1024]{1,0:T(8,128)(2,1)} %refs_0_.1) | copy-start | bytes 1179652
  15.0 27.7 %collective-permute-start.20 = (bf16[192,1024]{1,0:T(8,128)(2,1)S(1)}, bf16[192,1024]{1,0:T(8,128)(2,1)S(1)}, u32[]{:S(2)}, u32[]{:S(2)}) collective-permute-start(bf16[192,1024]{1,0:T(8,128)(2,1)S(1)} %get-tuple-element.61), channel_id=1, source_target_pairs={{0,4},{4,0},{8,12},{12,8},{1,5},{5,1},{9,13},{13,9},{2,6},{6,2},{1... | collective-permute-start | bytes 1179656 | tf_op jit(solution)/shard_map/ppermute | solution.py:300
  15.0 15.8 %collective-permute-start.5 = (bf16[192,1024]{1,0:T(8,128)(2,1)S(1)}, bf16[192,1024]{1,0:T(8,128)(2,1)S(1)}, u32[]{:S(2)}, u32[]{:S(2)}) collective-permute-start(bf16[192,1024]{1,0:T(8,128)(2,1)S(1)} %collective-permute-done.4.cot_ref.refs_1_), channel_id=1, source_target_pairs={{0,2},{2,3},{3,1},{1,0},{4,6},{6,7},{7,5},{5,4},{8,10},{10,11},{11... | collective-permute-start | bytes 1179656 | tf_op jit(solution)/shard_map/ppermute | solution.py:322
  19.9 3.7 %collective-permute-start.6 = (bf16[192,1024]{1,0:T(8,128)(2,1)S(1)}, bf16[192,1024]{1,0:T(8,128)(2,1)S(1)}, u32[]{:S(2)}, u32[]{:S(2)}) collective-permute-start(bf16[192,1024]{1,0:T(8,128)(2,1)S(1)} %get-tuple-element.44), channel_id=1, source_target_pairs={{0,4},{4,0},{8,12},{12,8},{1,5},{5,1},{9,13},{13,9},{2,6},{6,2},{1... | collective-permute-start | bytes 1179656 | tf_op jit(solution)/shard_map/ppermute | solution.py:300
  24.2 13.8 %collective-permute-start.10 = (bf16[192,1024]{1,0:T(8,128)(2,1)S(1)}, bf16[192,1024]{1,0:T(8,128)(2,1)S(1)}, u32[]{:S(2)}, u32[]{:S(2)}) collective-permute-start(bf16[192,1024]{1,0:T(8,128)(2,1)S(1)} %shard_map.82), channel_id=1, source_target_pairs={{0,8},{4,12},{8,0},{12,4},{1,9},{5,13},{9,1},{13,5},{2,10},{6,14},... | collective-permute-start | bytes 1179656 | tf_op jit(solution)/shard_map/ppermute | solution.py:306
  30.9 12.4 %collective-permute-start.13 = (bf16[192,1024]{1,0:T(8,128)(2,1)S(1)}, bf16[192,1024]{1,0:T(8,128)(2,1)S(1)}, u32[]{:S(2)}, u32[]{:S(2)}) collective-permute-start(bf16[192,1024]{1,0:T(8,128)(2,1)S(1)} %collective-permute-done.5.cot_ref.refs_2_), channel_id=1, source_target_pairs={{0,2},{2,3},{3,1},{1,0},{4,6},{6,7},{7,5},{5,4},{8,10},{10,11},{11... | collective-permute-start | bytes 1179656 | tf_op jit(solution)/shard_map/ppermute | solution.py:322
  36.3 3.5 %collective-permute-start.7 = (bf16[192,1024]{1,0:T(8,128)(2,1)S(1)}, bf16[192,1024]{1,0:T(8,128)(2,1)S(1)}, u32[]{:S(2)}, u32[]{:S(2)}) collective-permute-start(bf16[192,1024]{1,0:T(8,128)(2,1)S(1)} %get-tuple-element.47), channel_id=1, source_target_pairs={{0,4},{4,0},{8,12},{12,8},{1,5},{5,1},{9,13},{13,9},{2,6},{6,2},{1... | collective-permute-start | bytes 1179656 | tf_op jit(solution)/shard_map/ppermute | solution.py:300
  38.1 5.3 %copy-start.2 = (bf16[1024,2048]{1,0:T(8,128)(2,1)S(1)}, bf16[1024,2048]{1,0:T(8,128)(2,1)}, u32[]{:S(2)}) copy-start(bf16[1024,2048]{1,0:T(8,128)(2,1)} %up_ref.7) | copy-start | bytes 12582916
  39.3 4.1 %collective-permute-start.11 = (bf16[192,1024]{1,0:T(8,128)(2,1)S(1)}, bf16[192,1024]{1,0:T(8,128)(2,1)S(1)}, u32[]{:S(2)}, u32[]{:S(2)}) collective-permute-start(bf16[192,1024]{1,0:T(8,128)(2,1)S(1)} %shard_map.87.mine_ref.refs_4_), channel_id=1, source_target_pairs={{0,4},{4,0},{8,12},{12,8},{1,5},{5,1},{9,13},{13,9},{2,6},{6,2},{1... | collective-permute-start | bytes 1179656 | tf_op jit(solution)/shard_map/ppermute | solution.py:312
  40.4 11.1 %collective-permute-start.8 = (bf16[192,1024]{1,0:T(8,128)(2,1)S(1)}, bf16[192,1024]{1,0:T(8,128)(2,1)S(1)}, u32[]{:S(2)}, u32[]{:S(2)}) collective-permute-start(bf16[192,1024]{1,0:T(8,128)(2,1)S(1)} %shard_map.84), channel_id=1, source_target_pairs={{0,8},{4,12},{8,0},{12,4},{1,9},{5,13},{9,1},{13,5},{2,10},{6,14},... | collective-permute-start | bytes 1179656 | tf_op jit(solution)/shard_map/ppermute | solution.py:306
  42.0 13.0 %collective-permute-start.1 = (bf16[192,1024]{1,0:T(8,128)(2,1)S(1)}, bf16[192,1024]{1,0:T(8,128)(2,1)S(1)}, u32[]{:S(2)}, u32[]{:S(2)}) collective-permute-start(bf16[192,1024]{1,0:T(8,128)(2,1)S(1)} %collective-permute-done.refs_1_), channel_id=1, source_target_pairs={{0,2},{2,3},{3,1},{1,0},{4,6},{6,7},{7,5},{5,4},{8,10},{10,11},{11... | collective-permute-start | bytes 1179656 | tf_op jit(solution)/shard_map/ppermute | solution.py:327
  43.3 23.2 %collective-permute-start.16 = (bf16[768,1024]{1,0:T(8,128)(2,1)S(1)}, bf16[768,1024]{1,0:T(8,128)(2,1)S(1)}, u32[]{:S(2)}, u32[]{:S(2)}) collective-permute-start(bf16[768,1024]{1,0:T(8,128)(2,1)S(1)} %get-tuple-element.56.mine_ref), channel_id=1, source_target_pairs={{0,4},{4,0},{8,12},{12,8},{1,5},{5,1},{9,13},{13,9},{2,6},{6,2},{1... | collective-permute-start | bytes 4718600 | tf_op jit(solution)/shard_map/ppermute | solution.py:330
  45.5 15.7 %collective-permute-start.12 = (bf16[192,1024]{1,0:T(8,128)(2,1)S(1)}, bf16[192,1024]{1,0:T(8,128)(2,1)S(1)}, u32[]{:S(2)}, u32[]{:S(2)}) collective-permute-start(bf16[192,1024]{1,0:T(8,128)(2,1)S(1)} %shard_map.88), channel_id=1, source_target_pairs={{0,2},{2,3},{3,1},{1,0},{4,6},{6,7},{7,5},{5,4},{8,10},{10,11},{11... | collective-permute-start | bytes 1179656 | tf_op jit(solution)/shard_map/ppermute | solution.py:339
  50.0 2.8 %collective-permute-start.14 = (bf16[192,1024]{1,0:T(8,128)(2,1)S(1)}, bf16[192,1024]{1,0:T(8,128)(2,1)S(1)}, u32[]{:S(2)}, u32[]{:S(2)}) collective-permute-start(bf16[192,1024]{1,0:T(8,128)(2,1)S(1)} %get-tuple-element.54), channel_id=1, source_target_pairs={{0,4},{4,0},{8,12},{12,8},{1,5},{5,1},{9,13},{13,9},{2,6},{6,2},{1... | collective-permute-start | bytes 1179656 | tf_op jit(solution)/shard_map/ppermute | solution.py:300
  52.7 2.8 %collective-permute-start.9 = (bf16[192,1024]{1,0:T(8,128)(2,1)S(1)}, bf16[192,1024]{1,0:T(8,128)(2,1)S(1)}, u32[]{:S(2)}, u32[]{:S(2)}) collective-permute-start(bf16[192,1024]{1,0:T(8,128)(2,1)S(1)} %shard_map.85.mine_ref.refs_5_), channel_id=1, source_target_pairs={{0,4},{4,0},{8,12},{12,8},{1,5},{5,1},{9,13},{13,9},{2,6},{6,2},{1... | collective-permute-start | bytes 1179656 | tf_op jit(solution)/shard_map/ppermute | solution.py:312
  53.4 11.8 %collective-permute-start.15 = (bf16[192,1024]{1,0:T(8,128)(2,1)S(1)}, bf16[192,1024]{1,0:T(8,128)(2,1)S(1)}, u32[]{:S(2)}, u32[]{:S(2)}) collective-permute-start(bf16[192,1024]{1,0:T(8,128)(2,1)S(1)} %shard_map.91), channel_id=1, source_target_pairs={{0,8},{4,12},{8,0},{12,4},{1,9},{5,13},{9,1},{13,5},{2,10},{6,14},... | collective-permute-start | bytes 1179656 | tf_op jit(solution)/shard_map/ppermute | solution.py:306
  61.8 4.7 %copy-start.4 = (bf16[192,1024]{1,0:T(8,128)(2,1)S(1)}, bf16[192,1024]{1,0:T(8,128)(2,1)}, u32[]{:S(2)}) copy-start(bf16[192,1024]{1,0:T(8,128)(2,1)} %refs_0_.2) | copy-start | bytes 1179652
  61.8 12.1 %collective-permute-start.19 = (bf16[192,1024]{1,0:T(8,128)(2,1)S(1)}, bf16[192,1024]{1,0:T(8,128)(2,1)S(1)}, u32[]{:S(2)}, u32[]{:S(2)}) collective-permute-start(bf16[192,1024]{1,0:T(8,128)(2,1)S(1)} %collective-permute-done.1.refs_0_), channel_id=1, source_target_pairs={{0,2},{2,3},{3,1},{1,0},{4,6},{6,7},{7,5},{5,4},{8,10},{10,11},{11... | collective-permute-start | bytes 1179656 | tf_op jit(solution)/shard_map/ppermute | solution.py:342
  63.4 10.5 %collective-permute-start.21 = (bf16[192,1024]{1,0:T(8,128)(2,1)S(1)}, bf16[192,1024]{1,0:T(8,128)(2,1)S(1)}, u32[]{:S(2)}, u32[]{:S(2)}) collective-permute-start(bf16[192,1024]{1,0:T(8,128)(2,1)S(1)} %shard_map.96), channel_id=1, source_target_pairs={{0,8},{4,12},{8,0},{12,4},{1,9},{5,13},{9,1},{13,5},{2,10},{6,14},... | collective-permute-start | bytes 1179656 | tf_op jit(solution)/shard_map/ppermute | solution.py:306
  64.8 15.3 %collective-permute-start.18 = (bf16[192,1024]{1,0:T(8,128)(2,1)S(1)}, bf16[192,1024]{1,0:T(8,128)(2,1)S(1)}, u32[]{:S(2)}, u32[]{:S(2)}) collective-permute-start(bf16[192,1024]{1,0:T(8,128)(2,1)S(1)} %shard_map.89), channel_id=1, source_target_pairs={{0,2},{2,3},{3,1},{1,0},{4,6},{6,7},{7,5},{5,4},{8,10},{10,11},{11... | collective-permute-start | bytes 1179656 | tf_op jit(solution)/shard_map/ppermute | solution.py:339
  66.4 8.8 %collective-permute-start.17 = (bf16[192,1024]{1,0:T(8,128)(2,1)S(1)}, bf16[192,1024]{1,0:T(8,128)(2,1)S(1)}, u32[]{:S(2)}, u32[]{:S(2)}) collective-permute-start(bf16[192,1024]{1,0:T(8,128)(2,1)S(1)} %shard_map.92.mine_ref.refs_6_), channel_id=1, source_target_pairs={{0,4},{4,0},{8,12},{12,8},{1,5},{5,1},{9,13},{13,9},{2,6},{6,2},{1... | collective-permute-start | bytes 1179656 | tf_op jit(solution)/shard_map/ppermute | solution.py:312
  75.1 8.2 %collective-permute-start.22 = (bf16[192,1024]{1,0:T(8,128)(2,1)S(1)}, bf16[192,1024]{1,0:T(8,128)(2,1)S(1)}, u32[]{:S(2)}, u32[]{:S(2)}) collective-permute-start(bf16[192,1024]{1,0:T(8,128)(2,1)S(1)} %shard_map.97.mine_ref.refs_3_), channel_id=1, source_target_pairs={{0,4},{4,0},{8,12},{12,8},{1,5},{5,1},{9,13},{13,9},{2,6},{6,2},{1... | collective-permute-start | bytes 1179656 | tf_op jit(solution)/shard_map/ppermute | solution.py:312
  80.8 11.3 %collective-permute-start.23 = (bf16[192,1024]{1,0:T(8,128)(2,1)S(1)}, bf16[192,1024]{1,0:T(8,128)(2,1)S(1)}, u32[]{:S(2)}, u32[]{:S(2)}) collective-permute-start(bf16[192,1024]{1,0:T(8,128)(2,1)S(1)} %shard_map.95), channel_id=1, source_target_pairs={{0,2},{2,3},{3,1},{1,0},{4,6},{6,7},{7,5},{5,4},{8,10},{10,11},{11... | collective-permute-start | bytes 1179656 | tf_op jit(solution)/shard_map/ppermute | solution.py:352

commit v16 on v15

--- a/solution.py
+++ b/solution.py
@@ -339,7 +339,7 @@
         arrived = lax.ppermute(sums, "col", ring)
         pre_grad(s, *([late] if s > 2 else []))
         if s > 2:
-            ins.append(lax.ppermute(after(ins[-1], sums), "col", ring))
+            ins.append(lax.ppermute(after(ins[-1], part), "col", ring))
         first = []
         if s == last:
             grad_down = grad_down_call(

time: 93.6 us -> 90.8 us (0.970)
  waiting for transfers between devices: 17 us -> 14.6 us
    ppermute x3, waiting for transfers between devices: 6.43 us -> 3.83 us  [per_device(): arrived = lax.ppermute(sums, 'col', ring)]
    ppermute x4, waiting for transfers between devices: 1.54 us -> 2.66 us  [exchange(): others[s] = [lax.ppermute(values, 'row', to) for to in over_x]]
  transfers between devices with their start and end apart: 24 -> 24, of which waited for: 7 -> 8; matrix products, arithmetic and copies ran while one was open for 0% -> 0% of each run, Pallas kernels for 44% -> 46%
where the time goes in v16:
time: 90.8 us; the launch traced here: 90.6 us
  Pallas kernels  42.8 us (47%)
  starting transfers between devices  27.8 us (31%)
  waiting for transfers between devices  14.6 us (16%)
  local copies, waits for them, and re-layouts  4.34 us (5%)
  between operations  0.95 us (1%)
    pallas_call x25, Pallas kernels, call(): pl.pallas_call(kernel, out_shape=outs, grid_spec=pltpu.PrefetchScalarGrid...  42.8 us
    ppermute x3, starting transfers between devices, per_device(): arriving = lax.ppermute(cots[s - 1], 'col', ring)  9.84 us
    ppermute x3, starting transfers between devices, per_device(): arrived = lax.ppermute(sums, 'col', ring)  5.9 us
    ppermute x4, starting transfers between devices, exchange(): others[s] = [lax.ppermute(values, 'row', to) for to in over_x]  5.53 us
    ppermute x3, waiting for transfers between devices, per_device(): arriving = lax.ppermute(cots[s - 1], 'col', ring)  5.08 us
    unnamed x14, local copies, waits for them, and re-layouts  4.34 us
    ppermute x3, waiting for transfers between devices, per_device(): arrived = lax.ppermute(sums, 'col', ring)  3.83 us
    ppermute x1, waiting for transfers between devices, per_device(): ins = [inputs, lax.ppermute(after(inputs, place), 'col', ring)]  3 us
  transfers between devices with their start and end apart: 24, of which 8 were waited for; matrix products, arithmetic and copies ran while one was open for 0% of the time, Pallas kernels for 46%

profile of v16, /device:TPU:0, one launch (start us, length us, event | category | flops | bytes accessed | tf_op | source)
XLA Modules:
  0.0 90.6 jit_solution(8476368677388774103)
XLA Ops:
  1.2 3.7 %collective-permute-start.4 = (bf16[192,1024]{1,0:T(8,128)(2,1)}, bf16[192,1024]{1,0:T(8,128)(2,1)S(1)}, u32[]{:S(2)}, u32[]{:S(2)}) collective-permute-start(bf16[192,1024]{1,0:T(8,128)(2,1)} %refs_0_.2), channel_id=1, source_target_pairs={{0,2},{2,3},{3,1},{1,0},{4,6},{6,7},{7,5},{5,4},{8,10},{10,11},{11... | collective-permute-start | bytes 1179656 | tf_op jit(solution)/shard_map/ppermute | solution.py:322
  4.8 1.6 %collective-permute-start = (bf16[192,1024]{1,0:T(8,128)(2,1)}, bf16[192,1024]{1,0:T(8,128)(2,1)S(1)}, u32[]{:S(2)}, u32[]{:S(2)}) collective-permute-start(bf16[192,1024]{1,0:T(8,128)(2,1)} %refs_0_.1), channel_id=1, source_target_pairs={{0,2},{2,3},{3,1},{1,0},{4,6},{6,7},{7,5},{5,4},{8,10},{10,11},{11... | collective-permute-start | bytes 1179656 | tf_op jit(solution)/shard_map/ppermute | solution.py:319
  8.1 1.6 %collective-permute-start.3 = (bf16[384,1024]{1,0:T(8,128)(2,1)S(1)}, bf16[384,1024]{1,0:T(8,128)(2,1)S(1)}, u32[]{:S(2)}, u32[]{:S(2)}) collective-permute-start(bf16[384,1024]{1,0:T(8,128)(2,1)S(1)} %shard_map.78.refs_0_), channel_id=1, source_target_pairs={{0,8},{4,12},{8,0},{12,4},{1,9},{5,13},{9,1},{13,5},{2,10},{6,14},... | collective-permute-start | bytes 2359304 | tf_op jit(solution)/shard_map/ppermute | solution.py:295
  9.7 2.2 %copy-done = bf16[2048,1024]{1,0:T(8,128)(2,1)S(1)} copy-done((bf16[2048,1024]{1,0:T(8,128)(2,1)S(1)}, bf16[2048,1024]{1,0:T(8,128)(2,1)}, u32[]{:S(2)}) %copy-start) | copy-done | bytes 4194328
  12.9 2.1 %shard_map.80 = (f32[192,1024]{1,0:T(8,128)S(1)}, bf16[192,1024]{1,0:T(8,128)(2,1)S(1)}) custom-call(s32[2]{0:T(128)S(1)} %pad_add_fusion.place_ref, bf16[192,1024]{1,0:T(8,128)(2,1)S(1)} %copy-done.3, bf16[2048,1024]{1,0:T(8,128)(2,1)S(1)} %copy-done), custom_call_target="tpu_custom_call" | custom-call | flops 10000000 | bytes 1024 | tf_op jit(solution)/shard_map/pallas_call | solution.py:74
  15.0 2.8 %collective-permute-start.5 = (bf16[192,1024]{1,0:T(8,128)(2,1)S(1)}, bf16[192,1024]{1,0:T(8,128)(2,1)S(1)}, u32[]{:S(2)}, u32[]{:S(2)}) collective-permute-start(bf16[192,1024]{1,0:T(8,128)(2,1)S(1)} %collective-permute-done.4.cot_ref.refs_1_), channel_id=1, source_target_pairs={{0,2},{2,3},{3,1},{1,0},{4,6},{6,7},{7,5},{5,4},{8,10},{10,11},{11... | collective-permute-start | bytes 1179656 | tf_op jit(solution)/shard_map/ppermute | solution.py:322
  17.9 2.1 %shard_map.81 = (f32[192,1024]{1,0:T(8,128)S(1)}, bf16[192,1024]{1,0:T(8,128)(2,1)S(1)}) custom-call(s32[2]{0:T(128)S(1)} %pad_add_fusion.place_ref, bf16[192,1024]{1,0:T(8,128)(2,1)S(1)} %collective-permute-done.4.cot_ref.refs_1_, bf16[2048,1024]{1,0:T(8,128)(2,1)S(1)} %copy-done.1), custom_call_target="tpu_custom_call" | custom-call | flops 10000000 | bytes 1024 | tf_op jit(solution)/shard_map/pallas_call | solution.py:74
  20.0 3.0 %collective-permute-done.refs_1_ = bf16[192,1024]{1,0:T(8,128)(2,1)S(1)} collective-permute-done((bf16[192,1024]{1,0:T(8,128)(2,1)}, bf16[192,1024]{1,0:T(8,128)(2,1)S(1)}, u32[]{:S(2)}, u32[]{:S(2)}) %collective-permute-start) | collective-permute-done | bytes 393248 | tf_op jit(solution)/shard_map/ppermute | solution.py:319
  24.2 1.6 %collective-permute-start.10 = (bf16[192,1024]{1,0:T(8,128)(2,1)S(1)}, bf16[192,1024]{1,0:T(8,128)(2,1)S(1)}, u32[]{:S(2)}, u32[]{:S(2)}) collective-permute-start(bf16[192,1024]{1,0:T(8,128)(2,1)S(1)} %shard_map.82), channel_id=1, source_target_pairs={{0,8},{4,12},{8,0},{12,4},{1,9},{5,13},{9,1},{13,5},{2,10},{6,14},... | collective-permute-start | bytes 1179656 | tf_op jit(solution)/shard_map/ppermute | solution.py:306
  25.8 5.1 %collective-permute-done.5.cot_ref.refs_2_ = bf16[192,1024]{1,0:T(8,128)(2,1)S(1)} collective-permute-done((bf16[192,1024]{1,0:T(8,128)(2,1)S(1)}, bf16[192,1024]{1,0:T(8,128)(2,1)S(1)}, u32[]{:S(2)}, u32[]{:S(2)}) %collective-permute-start.5) | collective-permute-done | bytes 393248 | tf_op jit(solution)/shard_map/ppermute | solution.py:322
  30.9 3.4 %collective-permute-start.13 = (bf16[192,1024]{1,0:T(8,128)(2,1)S(1)}, bf16[192,1024]{1,0:T(8,128)(2,1)S(1)}, u32[]{:S(2)}, u32[]{:S(2)}) collective-permute-start(bf16[192,1024]{1,0:T(8,128)(2,1)S(1)} %collective-permute-done.5.cot_ref.refs_2_), channel_id=1, source_target_pairs={{0,2},{2,3},{3,1},{1,0},{4,6},{6,7},{7,5},{5,4},{8,10},{10,11},{11... | collective-permute-start | bytes 1179656 | tf_op jit(solution)/shard_map/ppermute | solution.py:322
  34.2 2.1 %shard_map.83 = (f32[192,1024]{1,0:T(8,128)S(1)}, bf16[192,1024]{1,0:T(8,128)(2,1)S(1)}) custom-call(s32[2]{0:T(128)S(1)} %pad_add_fusion.place_ref, bf16[192,1024]{1,0:T(8,128)(2,1)S(1)} %collective-permute-done.5.cot_ref.refs_2_, bf16[2048,1024]{1,0:T(8,128)(2,1)S(1)} %copy-done.1), custom_call_target="tpu_custom_call" | custom-call | flops 10000000 | bytes 1024 | tf_op jit(solution)/shard_map/pallas_call | solution.py:74
  36.4 1.7 %shard_map.79 = (bf16[768,1024]{1,0:T(8,128)(2,1)S(1)}, bf16[768,1024]{1,0:T(8,128)(2,1)S(1)}) custom-call(s32[2]{0:T(128)S(1)} %pad_add_fusion.place_ref, bf16[384,1024]{1,0:T(8,128)(2,1)S(1)} %shard_map.78.refs_0_, bf16[384,1024]{1,0:T(8,128)(2,1)S(1)} %collective-permute-done.3.refs_1_), custom_call_target="tpu_custom_call" | custom-call | flops 6000000000 | bytes 1024 | tf_op jit(solution)/shard_map/pallas_call | solution.py:74
  38.1 1.2 %shard_map.87.mine_ref.refs_4_ = bf16[192,1024]{1,0:T(8,128)(2,1)S(1)} custom-call(s32[2]{0:T(128)S(1)} %pad_add_fusion.place_ref, bf16[768,1024]{1,0:T(8,128)(2,1)S(1)} %get-tuple-element.38.pre_ref, f32[192,1024]{1,0:T(8,128)S(1)} %get-tuple-element.43.part_ref, bf16[192,1024]{1,0:T(8,128)(2,1)S(1)} %collective-permute-done.6.refs_0_, ...), custom_call_target="tpu_custom_call" | custom-call | flops 3000000000 | bytes 1024 | tf_op jit(solution)/shard_map/pallas_call | solution.py:74
  40.4 1.6 %collective-permute-start.8 = (bf16[192,1024]{1,0:T(8,128)(2,1)S(1)}, bf16[192,1024]{1,0:T(8,128)(2,1)S(1)}, u32[]{:S(2)}, u32[]{:S(2)}) collective-permute-start(bf16[192,1024]{1,0:T(8,128)(2,1)S(1)} %shard_map.84), channel_id=1, source_target_pairs={{0,8},{4,12},{8,0},{12,4},{1,9},{5,13},{9,1},{13,5},{2,10},{6,14},... | collective-permute-start | bytes 1179656 | tf_op jit(solution)/shard_map/ppermute | solution.py:306
  43.4 2.1 %shard_map.88 = bf16[192,1024]{1,0:T(8,128)(2,1)S(1)} custom-call(s32[2]{0:T(128)S(1)} %pad_add_fusion.place_ref, bf16[192,1024]{1,0:T(8,128)(2,1)S(1)} %shard_map.87.mine_ref.refs_4_, bf16[192,1024]{1,0:T(8,128)(2,1)S(1)} %collective-permute-done.11.theirs_ref.refs_8_, bf16[1024,2048]{1,0:T(8,128)(2,1)S(1)} %copy-done.2), custom_call_target="tpu_custom_call" | custom-call | flops 10000000 | bytes 1024 | tf_op jit(solution)/shard_map/pallas_call | solution.py:74
  45.5 2.5 %collective-permute-start.12 = (bf16[192,1024]{1,0:T(8,128)(2,1)S(1)}, bf16[192,1024]{1,0:T(8,128)(2,1)S(1)}, u32[]{:S(2)}, u32[]{:S(2)}) collective-permute-start(bf16[192,1024]{1,0:T(8,128)(2,1)S(1)} %shard_map.88), channel_id=1, source_target_pairs={{0,2},{2,3},{3,1},{1,0},{4,6},{6,7},{7,5},{5,4},{8,10},{10,11},{11... | collective-permute-start | bytes 1179656 | tf_op jit(solution)/shard_map/ppermute | solution.py:339
  48.0 2.1 %shard_map.90 = (f32[192,1024]{1,0:T(8,128)S(1)}, bf16[192,1024]{1,0:T(8,128)(2,1)S(1)}) custom-call(s32[2]{0:T(128)S(1)} %pad_add_fusion.place_ref, bf16[192,1024]{1,0:T(8,128)(2,1)S(1)} %collective-permute-done.13.cot_ref.refs_3_, bf16[2048,1024]{1,0:T(8,128)(2,1)S(1)} %copy-done.1), custom_call_target="tpu_custom_call" | custom-call | flops 10000000 | bytes 1024 | tf_op jit(solution)/shard_map/pallas_call | solution.py:74
  50.3 1.2 %collective-permute-done.8.refs_1_ = bf16[192,1024]{1,0:T(8,128)(2,1)S(1)} collective-permute-done((bf16[192,1024]{1,0:T(8,128)(2,1)S(1)}, bf16[192,1024]{1,0:T(8,128)(2,1)S(1)}, u32[]{:S(2)}, u32[]{:S(2)}) %collective-permute-start.8) | collective-permute-done | bytes 393248 | tf_op jit(solution)/shard_map/ppermute | solution.py:306
  51.5 1.2 %shard_map.85.mine_ref.refs_5_ = bf16[192,1024]{1,0:T(8,128)(2,1)S(1)} custom-call(s32[2]{0:T(128)S(1)} %pad_add_fusion.place_ref, bf16[768,1024]{1,0:T(8,128)(2,1)S(1)} %get-tuple-element.38.pre_ref, f32[192,1024]{1,0:T(8,128)S(1)} %get-tuple-element.46.part_ref, bf16[192,1024]{1,0:T(8,128)(2,1)S(1)} %collective-permute-done.7.refs_0_, ...), custom_call_target="tpu_custom_call" | custom-call | flops 8000000000 | bytes 1024 | tf_op jit(solution)/shard_map/pallas_call | solution.py:74
  53.4 1.6 %collective-permute-start.15 = (bf16[192,1024]{1,0:T(8,128)(2,1)S(1)}, bf16[192,1024]{1,0:T(8,128)(2,1)S(1)}, u32[]{:S(2)}, u32[]{:S(2)}) collective-permute-start(bf16[192,1024]{1,0:T(8,128)(2,1)S(1)} %shard_map.91), channel_id=1, source_target_pairs={{0,8},{4,12},{8,0},{12,4},{1,9},{5,13},{9,1},{13,5},{2,10},{6,14},... | collective-permute-start | bytes 1179656 | tf_op jit(solution)/shard_map/ppermute | solution.py:306
  55.6 2.1 %shard_map.86.part_ref = f32[192,1024]{1,0:T(8,128)S(1)} custom-call(s32[2]{0:T(128)S(1)} %pad_add_fusion.place_ref, bf16[192,1024]{1,0:T(8,128)(2,1)S(1)} %shard_map.85.mine_ref.refs_5_, bf16[192,1024]{1,0:T(8,128)(2,1)S(1)} %collective-permute-done.9.theirs_ref.refs_9_, bf16[1024,2048]{1,0:T(8,128)(2,1)S(1)} %copy-done.2), custom_call_target="tpu_custom_call" | custom-call | flops 10000000 | bytes 1024 | tf_op jit(solution)/shard_map/pallas_call | solution.py:74
  59.2 2.6 %collective-permute-done.12.refs_0_ = bf16[192,1024]{1,0:T(8,128)(2,1)S(1)} collective-permute-done((bf16[192,1024]{1,0:T(8,128)(2,1)S(1)}, bf16[192,1024]{1,0:T(8,128)(2,1)S(1)}, u32[]{:S(2)}, u32[]{:S(2)}) %collective-permute-start.12) | collective-permute-done | bytes 393248 | tf_op jit(solution)/shard_map/ppermute | solution.py:339
  62.4 1.8 %collective-permute-start.18 = (bf16[192,1024]{1,0:T(8,128)(2,1)S(1)}, bf16[192,1024]{1,0:T(8,128)(2,1)S(1)}, u32[]{:S(2)}, u32[]{:S(2)}) collective-permute-start(bf16[192,1024]{1,0:T(8,128)(2,1)S(1)} %shard_map.89), channel_id=1, source_target_pairs={{0,2},{2,3},{3,1},{1,0},{4,6},{6,7},{7,5},{5,4},{8,10},{10,11},{11... | collective-permute-start | bytes 1179656 | tf_op jit(solution)/shard_map/ppermute | solution.py:339
  64.2 1.2 %collective-permute-done.15.refs_1_ = bf16[192,1024]{1,0:T(8,128)(2,1)S(1)} collective-permute-done((bf16[192,1024]{1,0:T(8,128)(2,1)S(1)}, bf16[192,1024]{1,0:T(8,128)(2,1)S(1)}, u32[]{:S(2)}, u32[]{:S(2)}) %collective-permute-start.15) | collective-permute-done | bytes 393248 | tf_op jit(solution)/shard_map/ppermute | solution.py:306
  65.4 1.2 %shard_map.92.mine_ref.refs_6_ = bf16[192,1024]{1,0:T(8,128)(2,1)S(1)} custom-call(s32[2]{0:T(128)S(1)} %pad_add_fusion.place_ref, bf16[768,1024]{1,0:T(8,128)(2,1)S(1)} %get-tuple-element.38.pre_ref, f32[192,1024]{1,0:T(8,128)S(1)} %get-tuple-element.53.part_ref, bf16[192,1024]{1,0:T(8,128)(2,1)S(1)} %collective-permute-done.14.refs_0_, ...), custom_call_target="tpu_custom_call" | custom-call | flops 3000000000 | bytes 1024 | tf_op jit(solution)/shard_map/pallas_call | solution.py:74
  66.7 6.5 %shard_map.93 = f32[2048,1024]{1,0:T(8,128)} custom-call(s32[2]{0:T(128)S(1)} %pad_add_fusion.place_ref, bf16[768,1024]{1,0:T(8,128)(2,1)S(1)} %get-tuple-element.56.mine_ref, bf16[768,1024]{1,0:T(8,128)(2,1)S(1)} %collective-permute-done.16.theirs_ref, bf16[192,1024]{1,0:T(8,128)(2,1)S(1)} %copy-done.4, ...), custom_call_target="tpu_custom_call" | custom-call | flops 100000000 | bytes 1024 | tf_op jit(solution)/shard_map/pallas_call | solution.py:74
  74.9 2.1 %shard_map.94.part_ref = f32[192,1024]{1,0:T(8,128)S(1)} custom-call(s32[2]{0:T(128)S(1)} %pad_add_fusion.place_ref, bf16[192,1024]{1,0:T(8,128)(2,1)S(1)} %shard_map.92.mine_ref.refs_6_, bf16[192,1024]{1,0:T(8,128)(2,1)S(1)} %collective-permute-done.17.theirs_ref.refs_10_, bf16[1024,2048]{1,0:T(8,128)(2,1)S(1)} %copy-done.2), custom_call_target="tpu_custom_call" | custom-call | flops 10000000 | bytes 1024 | tf_op jit(solution)/shard_map/pallas_call | solution.py:74
  78.7 1.6 %collective-permute-start.23 = (bf16[192,1024]{1,0:T(8,128)(2,1)S(1)}, bf16[192,1024]{1,0:T(8,128)(2,1)S(1)}, u32[]{:S(2)}, u32[]{:S(2)}) collective-permute-start(bf16[192,1024]{1,0:T(8,128)(2,1)S(1)} %shard_map.95), channel_id=1, source_target_pairs={{0,2},{2,3},{3,1},{1,0},{4,6},{6,7},{7,5},{5,4},{8,10},{10,11},{11... | collective-permute-start | bytes 1179656 | tf_op jit(solution)/shard_map/ppermute | solution.py:352
  80.3 2.1 %shard_map.98.part_ref = f32[192,1024]{1,0:T(8,128)S(1)} custom-call(s32[2]{0:T(128)S(1)} %pad_add_fusion.place_ref, bf16[192,1024]{1,0:T(8,128)(2,1)S(1)} %shard_map.97.mine_ref.refs_3_, bf16[192,1024]{1,0:T(8,128)(2,1)S(1)} %collective-permute-done.22.theirs_ref.refs_7_, bf16[1024,2048]{1,0:T(8,128)(2,1)S(1)} %copy-done.2), custom_call_target="tpu_custom_call" | custom-call | flops 10000000 | bytes 1024 | tf_op jit(solution)/shard_map/pallas_call | solution.py:74
  82.4 6.6 %shard_map.99 = f32[1024,2048]{1,0:T(8,128)} custom-call(s32[2]{0:T(128)S(1)} %pad_add_fusion.place_ref, bf16[384,1024]{1,0:T(8,128)(2,1)S(1)} %shard_map.76.refs_0_, bf16[192,1024]{1,0:T(8,128)(2,1)S(1)} %shard_map.77.refs_1_, bf16[192,1024]{1,0:T(8,128)(2,1)S(1)} %collective-permute-done.19.refs_2_, bf16[192,1024]{1,0:T(8,128)(2,1)S(1)} %shard_map.97.mine_ref.refs_3_, ...), custom_call_target="tpu_custom_call" | custom-call | flops 3000000000 | bytes 1024 | tf_op jit(solution)/shard_map/pallas_call | solution.py:74
  89.2 1.4 %shard_map.100 = bf16[192,1024]{1,0:T(8,128)(2,1)} custom-call(s32[2]{0:T(128)S(1)} %pad_add_fusion.place_ref, f32[192,1024]{1,0:T(8,128)S(1)} %shard_map.98.part_ref, bf16[192,1024]{1,0:T(8,128)(2,1)S(1)} %collective-permute-done.23.refs_0_), custom_call_target="tpu_custom_call" | custom-call | flops 10000000 | bytes 1024 | tf_op jit(solution)/shard_map/pallas_call | solution.py:74
  (56 shorter events, 14.6 us)
Async XLA Ops:
  0.7 5.7 %collective-permute-start.2 = (bf16[192,2048]{1,0:T(8,128)(2,1)}, bf16[192,2048]{1,0:T(8,128)(2,1)S(1)}, u32[]{:S(2)}, u32[]{:S(2)}) collective-permute-start(bf16[192,2048]{1,0:T(8,128)(2,1)} %mine_ref), channel_id=1, source_target_pairs={{0,4},{4,0},{8,12},{12,8},{1,5},{5,1},{9,13},{13,9},{2,6},{6,2},{1... | collective-permute-start | bytes 2359304 | tf_op jit(solution)/shard_map/ppermute | solution.py:294
  1.2 13.9 %collective-permute-start.4 = (bf16[192,1024]{1,0:T(8,128)(2,1)}, bf16[192,1024]{1,0:T(8,128)(2,1)S(1)}, u32[]{:S(2)}, u32[]{:S(2)}) collective-permute-start(bf16[192,1024]{1,0:T(8,128)(2,1)} %refs_0_.2), channel_id=1, source_target_pairs={{0,2},{2,3},{3,1},{1,0},{4,6},{6,7},{7,5},{5,4},{8,10},{10,11},{11... | collective-permute-start | bytes 1179656 | tf_op jit(solution)/shard_map/ppermute | solution.py:322
  4.8 18.2 %collective-permute-start = (bf16[192,1024]{1,0:T(8,128)(2,1)}, bf16[192,1024]{1,0:T(8,128)(2,1)S(1)}, u32[]{:S(2)}, u32[]{:S(2)}) collective-permute-start(bf16[192,1024]{1,0:T(8,128)(2,1)} %refs_0_.1), channel_id=1, source_target_pairs={{0,2},{2,3},{3,1},{1,0},{4,6},{6,7},{7,5},{5,4},{8,10},{10,11},{11... | collective-permute-start | bytes 1179656 | tf_op jit(solution)/shard_map/ppermute | solution.py:319
  6.4 1.1 %copy-start.5 = (bf16[192,2048]{1,0:T(8,128)(2,1)S(1)}, bf16[192,2048]{1,0:T(8,128)(2,1)}, u32[]{:S(2)}) copy-start(bf16[192,2048]{1,0:T(8,128)(2,1)} %mine_ref) | copy-start | bytes 2359300
  8.1 28.3 %collective-permute-start.3 = (bf16[384,1024]{1,0:T(8,128)(2,1)S(1)}, bf16[384,1024]{1,0:T(8,128)(2,1)S(1)}, u32[]{:S(2)}, u32[]{:S(2)}) collective-permute-start(bf16[384,1024]{1,0:T(8,128)(2,1)S(1)} %shard_map.78.refs_0_), channel_id=1, source_target_pairs={{0,8},{4,12},{8,0},{12,4},{1,9},{5,13},{9,1},{13,5},{2,10},{6,14},... | collective-permute-start | bytes 2359304 | tf_op jit(solution)/shard_map/ppermute | solution.py:295
  9.7 2.2 %copy-start = (bf16[2048,1024]{1,0:T(8,128)(2,1)S(1)}, bf16[2048,1024]{1,0:T(8,128)(2,1)}, u32[]{:S(2)}) copy-start(bf16[2048,1024]{1,0:T(8,128)(2,1)} %down_ref.7) | copy-start | bytes 12582916
  11.9 1.0 %copy-start.3 = (bf16[192,1024]{1,0:T(8,128)(2,1)S(1)}, bf16[192,1024]{1,0:T(8,128)(2,1)}, u32[]{:S(2)}) copy-start(bf16[192,1024]{1,0:T(8,128)(2,1)} %refs_0_.2) | copy-start | bytes 1179652
  12.9 5.0 %copy-start.1 = (bf16[2048,1024]{1,0:T(8,128)(2,1)S(1)}, bf16[2048,1024]{1,0:T(8,128)(2,1)}, u32[]{:S(2)}) copy-start(bf16[2048,1024]{1,0:T(8,128)(2,1)} %down_ref.7) | copy-start | bytes 12582916
  12.9 10.1 %copy-start.6 = (bf16[192,1024]{1,0:T(8,128)(2,1)S(1)}, bf16[192,1024]{1,0:T(8,128)(2,1)}, u32[]{:S(2)}) copy-start(bf16[192,1024]{1,0:T(8,128)(2,1)} %refs_0_.1) | copy-start | bytes 1179652
  15.0 27.7 %collective-permute-start.20 = (bf16[192,1024]{1,0:T(8,128)(2,1)S(1)}, bf16[192,1024]{1,0:T(8,128)(2,1)S(1)}, u32[]{:S(2)}, u32[]{:S(2)}) collective-permute-start(bf16[192,1024]{1,0:T(8,128)(2,1)S(1)} %get-tuple-element.61), channel_id=1, source_target_pairs={{0,4},{4,0},{8,12},{12,8},{1,5},{5,1},{9,13},{13,9},{2,6},{6,2},{1... | collective-permute-start | bytes 1179656 | tf_op jit(solution)/shard_map/ppermute | solution.py:300
  15.0 15.8 %collective-permute-start.5 = (bf16[192,1024]{1,0:T(8,128)(2,1)S(1)}, bf16[192,1024]{1,0:T(8,128)(2,1)S(1)}, u32[]{:S(2)}, u32[]{:S(2)}) collective-permute-start(bf16[192,1024]{1,0:T(8,128)(2,1)S(1)} %collective-permute-done.4.cot_ref.refs_1_), channel_id=1, source_target_pairs={{0,2},{2,3},{3,1},{1,0},{4,6},{6,7},{7,5},{5,4},{8,10},{10,11},{11... | collective-permute-start | bytes 1179656 | tf_op jit(solution)/shard_map/ppermute | solution.py:322
  19.9 3.7 %collective-permute-start.6 = (bf16[192,1024]{1,0:T(8,128)(2,1)S(1)}, bf16[192,1024]{1,0:T(8,128)(2,1)S(1)}, u32[]{:S(2)}, u32[]{:S(2)}) collective-permute-start(bf16[192,1024]{1,0:T(8,128)(2,1)S(1)} %get-tuple-element.44), channel_id=1, source_target_pairs={{0,4},{4,0},{8,12},{12,8},{1,5},{5,1},{9,13},{13,9},{2,6},{6,2},{1... | collective-permute-start | bytes 1179656 | tf_op jit(solution)/shard_map/ppermute | solution.py:300
  24.2 13.8 %collective-permute-start.10 = (bf16[192,1024]{1,0:T(8,128)(2,1)S(1)}, bf16[192,1024]{1,0:T(8,128)(2,1)S(1)}, u32[]{:S(2)}, u32[]{:S(2)}) collective-permute-start(bf16[192,1024]{1,0:T(8,128)(2,1)S(1)} %shard_map.82), channel_id=1, source_target_pairs={{0,8},{4,12},{8,0},{12,4},{1,9},{5,13},{9,1},{13,5},{2,10},{6,14},... | collective-permute-start | bytes 1179656 | tf_op jit(solution)/shard_map/ppermute | solution.py:306
  30.9 12.4 %collective-permute-start.13 = (bf16[192,1024]{1,0:T(8,128)(2,1)S(1)}, bf16[192,1024]{1,0:T(8,128)(2,1)S(1)}, u32[]{:S(2)}, u32[]{:S(2)}) collective-permute-start(bf16[192,1024]{1,0:T(8,128)(2,1)S(1)} %collective-permute-done.5.cot_ref.refs_2_), channel_id=1, source_target_pairs={{0,2},{2,3},{3,1},{1,0},{4,6},{6,7},{7,5},{5,4},{8,10},{10,11},{11... | collective-permute-start | bytes 1179656 | tf_op jit(solution)/shard_map/ppermute | solution.py:322
  36.3 3.5 %collective-permute-start.7 = (bf16[192,1024]{1,0:T(8,128)(2,1)S(1)}, bf16[192,1024]{1,0:T(8,128)(2,1)S(1)}, u32[]{:S(2)}, u32[]{:S(2)}) collective-permute-start(bf16[192,1024]{1,0:T(8,128)(2,1)S(1)} %get-tuple-element.47), channel_id=1, source_target_pairs={{0,4},{4,0},{8,12},{12,8},{1,5},{5,1},{9,13},{13,9},{2,6},{6,2},{1... | collective-permute-start | bytes 1179656 | tf_op jit(solution)/shard_map/ppermute | solution.py:300
  38.1 5.3 %copy-start.2 = (bf16[1024,2048]{1,0:T(8,128)(2,1)S(1)}, bf16[1024,2048]{1,0:T(8,128)(2,1)}, u32[]{:S(2)}) copy-start(bf16[1024,2048]{1,0:T(8,128)(2,1)} %up_ref.7) | copy-start | bytes 12582916
  39.3 4.1 %collective-permute-start.11 = (bf16[192,1024]{1,0:T(8,128)(2,1)S(1)}, bf16[192,1024]{1,0:T(8,128)(2,1)S(1)}, u32[]{:S(2)}, u32[]{:S(2)}) collective-permute-start(bf16[192,1024]{1,0:T(8,128)(2,1)S(1)} %shard_map.87.mine_ref.refs_4_), channel_id=1, source_target_pairs={{0,4},{4,0},{8,12},{12,8},{1,5},{5,1},{9,13},{13,9},{2,6},{6,2},{1... | collective-permute-start | bytes 1179656 | tf_op jit(solution)/shard_map/ppermute | solution.py:312
  40.4 11.1 %collective-permute-start.8 = (bf16[192,1024]{1,0:T(8,128)(2,1)S(1)}, bf16[192,1024]{1,0:T(8,128)(2,1)S(1)}, u32[]{:S(2)}, u32[]{:S(2)}) collective-permute-start(bf16[192,1024]{1,0:T(8,128)(2,1)S(1)} %shard_map.84), channel_id=1, source_target_pairs={{0,8},{4,12},{8,0},{12,4},{1,9},{5,13},{9,1},{13,5},{2,10},{6,14},... | collective-permute-start | bytes 1179656 | tf_op jit(solution)/shard_map/ppermute | solution.py:306
  42.0 13.0 %collective-permute-start.1 = (bf16[192,1024]{1,0:T(8,128)(2,1)S(1)}, bf16[192,1024]{1,0:T(8,128)(2,1)S(1)}, u32[]{:S(2)}, u32[]{:S(2)}) collective-permute-start(bf16[192,1024]{1,0:T(8,128)(2,1)S(1)} %collective-permute-done.refs_1_), channel_id=1, source_target_pairs={{0,2},{2,3},{3,1},{1,0},{4,6},{6,7},{7,5},{5,4},{8,10},{10,11},{11... | collective-permute-start | bytes 1179656 | tf_op jit(solution)/shard_map/ppermute | solution.py:327
  43.3 23.4 %collective-permute-start.16 = (bf16[768,1024]{1,0:T(8,128)(2,1)S(1)}, bf16[768,1024]{1,0:T(8,128)(2,1)S(1)}, u32[]{:S(2)}, u32[]{:S(2)}) collective-permute-start(bf16[768,1024]{1,0:T(8,128)(2,1)S(1)} %get-tuple-element.56.mine_ref), channel_id=1, source_target_pairs={{0,4},{4,0},{8,12},{12,8},{1,5},{5,1},{9,13},{13,9},{2,6},{6,2},{1... | collective-permute-start | bytes 4718600 | tf_op jit(solution)/shard_map/ppermute | solution.py:330
  45.5 16.3 %collective-permute-start.12 = (bf16[192,1024]{1,0:T(8,128)(2,1)S(1)}, bf16[192,1024]{1,0:T(8,128)(2,1)S(1)}, u32[]{:S(2)}, u32[]{:S(2)}) collective-permute-start(bf16[192,1024]{1,0:T(8,128)(2,1)S(1)} %shard_map.88), channel_id=1, source_target_pairs={{0,2},{2,3},{3,1},{1,0},{4,6},{6,7},{7,5},{5,4},{8,10},{10,11},{11... | collective-permute-start | bytes 1179656 | tf_op jit(solution)/shard_map/ppermute | solution.py:339
  50.0 2.8 %collective-permute-start.14 = (bf16[192,1024]{1,0:T(8,128)(2,1)S(1)}, bf16[192,1024]{1,0:T(8,128)(2,1)S(1)}, u32[]{:S(2)}, u32[]{:S(2)}) collective-permute-start(bf16[192,1024]{1,0:T(8,128)(2,1)S(1)} %get-tuple-element.54), channel_id=1, source_target_pairs={{0,4},{4,0},{8,12},{12,8},{1,5},{5,1},{9,13},{13,9},{2,6},{6,2},{1... | collective-permute-start | bytes 1179656 | tf_op jit(solution)/shard_map/ppermute | solution.py:300
  52.7 2.8 %collective-permute-start.9 = (bf16[192,1024]{1,0:T(8,128)(2,1)S(1)}, bf16[192,1024]{1,0:T(8,128)(2,1)S(1)}, u32[]{:S(2)}, u32[]{:S(2)}) collective-permute-start(bf16[192,1024]{1,0:T(8,128)(2,1)S(1)} %shard_map.85.mine_ref.refs_5_), channel_id=1, source_target_pairs={{0,4},{4,0},{8,12},{12,8},{1,5},{5,1},{9,13},{13,9},{2,6},{6,2},{1... | collective-permute-start | bytes 1179656 | tf_op jit(solution)/shard_map/ppermute | solution.py:312
  53.4 12.0 %collective-permute-start.15 = (bf16[192,1024]{1,0:T(8,128)(2,1)S(1)}, bf16[192,1024]{1,0:T(8,128)(2,1)S(1)}, u32[]{:S(2)}, u32[]{:S(2)}) collective-permute-start(bf16[192,1024]{1,0:T(8,128)(2,1)S(1)} %shard_map.91), channel_id=1, source_target_pairs={{0,8},{4,12},{8,0},{12,4},{1,9},{5,13},{9,1},{13,5},{2,10},{6,14},... | collective-permute-start | bytes 1179656 | tf_op jit(solution)/shard_map/ppermute | solution.py:306
  57.7 15.5 %collective-permute-start.19 = (bf16[192,1024]{1,0:T(8,128)(2,1)S(1)}, bf16[192,1024]{1,0:T(8,128)(2,1)S(1)}, u32[]{:S(2)}, u32[]{:S(2)}) collective-permute-start(bf16[192,1024]{1,0:T(8,128)(2,1)S(1)} %collective-permute-done.1.refs_0_), channel_id=1, source_target_pairs={{0,2},{2,3},{3,1},{1,0},{4,6},{6,7},{7,5},{5,4},{8,10},{10,11},{11... | collective-permute-start | bytes 1179656 | tf_op jit(solution)/shard_map/ppermute | solution.py:342
  58.4 15.0 %collective-permute-start.21 = (bf16[192,1024]{1,0:T(8,128)(2,1)S(1)}, bf16[192,1024]{1,0:T(8,128)(2,1)S(1)}, u32[]{:S(2)}, u32[]{:S(2)}) collective-permute-start(bf16[192,1024]{1,0:T(8,128)(2,1)S(1)} %shard_map.96), channel_id=1, source_target_pairs={{0,8},{4,12},{8,0},{12,4},{1,9},{5,13},{9,1},{13,5},{2,10},{6,14},... | collective-permute-start | bytes 1179656 | tf_op jit(solution)/shard_map/ppermute | solution.py:306
  62.4 4.3 %copy-start.4 = (bf16[192,1024]{1,0:T(8,128)(2,1)S(1)}, bf16[192,1024]{1,0:T(8,128)(2,1)}, u32[]{:S(2)}) copy-start(bf16[192,1024]{1,0:T(8,128)(2,1)} %refs_0_.2) | copy-start | bytes 1179652
  62.4 15.6 %collective-permute-start.18 = (bf16[192,1024]{1,0:T(8,128)(2,1)S(1)}, bf16[192,1024]{1,0:T(8,128)(2,1)S(1)}, u32[]{:S(2)}, u32[]{:S(2)}) collective-permute-start(bf16[192,1024]{1,0:T(8,128)(2,1)S(1)} %shard_map.89), channel_id=1, source_target_pairs={{0,2},{2,3},{3,1},{1,0},{4,6},{6,7},{7,5},{5,4},{8,10},{10,11},{11... | collective-permute-start | bytes 1179656 | tf_op jit(solution)/shard_map/ppermute | solution.py:339
  66.6 8.3 %collective-permute-start.17 = (bf16[192,1024]{1,0:T(8,128)(2,1)S(1)}, bf16[192,1024]{1,0:T(8,128)(2,1)S(1)}, u32[]{:S(2)}, u32[]{:S(2)}) collective-permute-start(bf16[192,1024]{1,0:T(8,128)(2,1)S(1)} %shard_map.92.mine_ref.refs_6_), channel_id=1, source_target_pairs={{0,4},{4,0},{8,12},{12,8},{1,5},{5,1},{9,13},{13,9},{2,6},{6,2},{1... | collective-permute-start | bytes 1179656 | tf_op jit(solution)/shard_map/ppermute | solution.py:312
  74.6 5.7 %collective-permute-start.22 = (bf16[192,1024]{1,0:T(8,128)(2,1)S(1)}, bf16[192,1024]{1,0:T(8,128)(2,1)S(1)}, u32[]{:S(2)}, u32[]{:S(2)}) collective-permute-start(bf16[192,1024]{1,0:T(8,128)(2,1)S(1)} %shard_map.97.mine_ref.refs_3_), channel_id=1, source_target_pairs={{0,4},{4,0},{8,12},{12,8},{1,5},{5,1},{9,13},{13,9},{2,6},{6,2},{1... | collective-permute-start | bytes 1179656 | tf_op jit(solution)/shard_map/ppermute | solution.py:312
  78.7 10.6 %collective-permute-start.23 = (bf16[192,1024]{1,0:T(8,128)(2,1)S(1)}, bf16[192,1024]{1,0:T(8,128)(2,1)S(1)}, u32[]{:S(2)}, u32[]{:S(2)}) collective-permute-start(bf16[192,1024]{1,0:T(8,128)(2,1)S(1)} %shard_map.95), channel_id=1, source_target_pairs={{0,2},{2,3},{3,1},{1,0},{4,6},{6,7},{7,5},{5,4},{8,10},{10,11},{11... | collective-permute-start | bytes 1179656 | tf_op jit(solution)/shard_map/ppermute | solution.py:352

commit v17 on v16

--- a/solution.py
+++ b/solution.py
@@ -263,7 +263,7 @@
 def grad_up_call(place, ins, mine, pair, scale):
     total, features = sum(x.shape[0] for x in ins), ins[0].shape[1]
     hidden = 2 * mine[0].shape[1]
-    tile = tile_of(features, 256)
+    tile = tile_of(features)
     return call(
         functools.partial(grad_up_kernel, len(mine), scale),
         place,

time: 90.8 us -> 90.8 us (level)
  no operation moved by 1% of the time
where the time goes in v17:
time: 90.8 us; the launch traced here: 90.6 us
  Pallas kernels  42.7 us (47%)
  starting transfers between devices  27.8 us (31%)
  waiting for transfers between devices  14.7 us (16%)
  local copies, waits for them, and re-layouts  4.34 us (5%)
  between operations  0.95 us (1%)
    pallas_call x25, Pallas kernels, call(): pl.pallas_call(kernel, out_shape=outs, grid_spec=pltpu.PrefetchScalarGrid...  42.7 us
    ppermute x3, starting transfers between devices, per_device(): arriving = lax.ppermute(cots[s - 1], 'col', ring)  9.84 us
    ppermute x3, starting transfers between devices, per_device(): arrived = lax.ppermute(sums, 'col', ring)  5.9 us
    ppermute x4, starting transfers between devices, exchange(): others[s] = [lax.ppermute(values, 'row', to) for to in over_x]  5.53 us
    ppermute x3, waiting for transfers between devices, per_device(): arriving = lax.ppermute(cots[s - 1], 'col', ring)  5.08 us
    unnamed x14, local copies, waits for them, and re-layouts  4.34 us
    ppermute x3, waiting for transfers between devices, per_device(): arrived = lax.ppermute(sums, 'col', ring)  3.89 us
    ppermute x1, waiting for transfers between devices, per_device(): ins = [inputs, lax.ppermute(after(inputs, place), 'col', ring)]  3 us
  transfers between devices with their start and end apart: 24, of which 8 were waited for; matrix products, arithmetic and copies ran while one was open for 0% of the time, Pallas kernels for 46%

profile of v17, /device:TPU:0, one launch (start us, length us, event | category | flops | bytes accessed | tf_op | source)
XLA Modules:
  0.0 90.6 jit_solution(5463415363402315432)
XLA Ops:
  1.2 3.7 %collective-permute-start.4 = (bf16[192,1024]{1,0:T(8,128)(2,1)}, bf16[192,1024]{1,0:T(8,128)(2,1)S(1)}, u32[]{:S(2)}, u32[]{:S(2)}) collective-permute-start(bf16[192,1024]{1,0:T(8,128)(2,1)} %refs_0_.2), channel_id=1, source_target_pairs={{0,2},{2,3},{3,1},{1,0},{4,6},{6,7},{7,5},{5,4},{8,10},{10,11},{11... | collective-permute-start | bytes 1179656 | tf_op jit(solution)/shard_map/ppermute | solution.py:322
  4.8 1.6 %collective-permute-start = (bf16[192,1024]{1,0:T(8,128)(2,1)}, bf16[192,1024]{1,0:T(8,128)(2,1)S(1)}, u32[]{:S(2)}, u32[]{:S(2)}) collective-permute-start(bf16[192,1024]{1,0:T(8,128)(2,1)} %refs_0_.1), channel_id=1, source_target_pairs={{0,2},{2,3},{3,1},{1,0},{4,6},{6,7},{7,5},{5,4},{8,10},{10,11},{11... | collective-permute-start | bytes 1179656 | tf_op jit(solution)/shard_map/ppermute | solution.py:319
  8.1 1.6 %collective-permute-start.3 = (bf16[384,1024]{1,0:T(8,128)(2,1)S(1)}, bf16[384,1024]{1,0:T(8,128)(2,1)S(1)}, u32[]{:S(2)}, u32[]{:S(2)}) collective-permute-start(bf16[384,1024]{1,0:T(8,128)(2,1)S(1)} %shard_map.78.refs_0_), channel_id=1, source_target_pairs={{0,8},{4,12},{8,0},{12,4},{1,9},{5,13},{9,1},{13,5},{2,10},{6,14},... | collective-permute-start | bytes 2359304 | tf_op jit(solution)/shard_map/ppermute | solution.py:295
  9.7 2.2 %copy-done = bf16[2048,1024]{1,0:T(8,128)(2,1)S(1)} copy-done((bf16[2048,1024]{1,0:T(8,128)(2,1)S(1)}, bf16[2048,1024]{1,0:T(8,128)(2,1)}, u32[]{:S(2)}) %copy-start) | copy-done | bytes 4194328
  12.9 2.1 %shard_map.80 = (f32[192,1024]{1,0:T(8,128)S(1)}, bf16[192,1024]{1,0:T(8,128)(2,1)S(1)}) custom-call(s32[2]{0:T(128)S(1)} %pad_add_fusion.place_ref, bf16[192,1024]{1,0:T(8,128)(2,1)S(1)} %copy-done.3, bf16[2048,1024]{1,0:T(8,128)(2,1)S(1)} %copy-done), custom_call_target="tpu_custom_call" | custom-call | flops 10000000 | bytes 1024 | tf_op jit(solution)/shard_map/pallas_call | solution.py:74
  15.0 2.8 %collective-permute-start.5 = (bf16[192,1024]{1,0:T(8,128)(2,1)S(1)}, bf16[192,1024]{1,0:T(8,128)(2,1)S(1)}, u32[]{:S(2)}, u32[]{:S(2)}) collective-permute-start(bf16[192,1024]{1,0:T(8,128)(2,1)S(1)} %collective-permute-done.4.cot_ref.refs_1_), channel_id=1, source_target_pairs={{0,2},{2,3},{3,1},{1,0},{4,6},{6,7},{7,5},{5,4},{8,10},{10,11},{11... | collective-permute-start | bytes 1179656 | tf_op jit(solution)/shard_map/ppermute | solution.py:322
  17.9 2.1 %shard_map.81 = (f32[192,1024]{1,0:T(8,128)S(1)}, bf16[192,1024]{1,0:T(8,128)(2,1)S(1)}) custom-call(s32[2]{0:T(128)S(1)} %pad_add_fusion.place_ref, bf16[192,1024]{1,0:T(8,128)(2,1)S(1)} %collective-permute-done.4.cot_ref.refs_1_, bf16[2048,1024]{1,0:T(8,128)(2,1)S(1)} %copy-done.1), custom_call_target="tpu_custom_call" | custom-call | flops 10000000 | bytes 1024 | tf_op jit(solution)/shard_map/pallas_call | solution.py:74
  20.0 3.0 %collective-permute-done.refs_1_ = bf16[192,1024]{1,0:T(8,128)(2,1)S(1)} collective-permute-done((bf16[192,1024]{1,0:T(8,128)(2,1)}, bf16[192,1024]{1,0:T(8,128)(2,1)S(1)}, u32[]{:S(2)}, u32[]{:S(2)}) %collective-permute-start) | collective-permute-done | bytes 393248 | tf_op jit(solution)/shard_map/ppermute | solution.py:319
  24.2 1.6 %collective-permute-start.10 = (bf16[192,1024]{1,0:T(8,128)(2,1)S(1)}, bf16[192,1024]{1,0:T(8,128)(2,1)S(1)}, u32[]{:S(2)}, u32[]{:S(2)}) collective-permute-start(bf16[192,1024]{1,0:T(8,128)(2,1)S(1)} %shard_map.82), channel_id=1, source_target_pairs={{0,8},{4,12},{8,0},{12,4},{1,9},{5,13},{9,1},{13,5},{2,10},{6,14},... | collective-permute-start | bytes 1179656 | tf_op jit(solution)/shard_map/ppermute | solution.py:306
  25.8 5.1 %collective-permute-done.5.cot_ref.refs_2_ = bf16[192,1024]{1,0:T(8,128)(2,1)S(1)} collective-permute-done((bf16[192,1024]{1,0:T(8,128)(2,1)S(1)}, bf16[192,1024]{1,0:T(8,128)(2,1)S(1)}, u32[]{:S(2)}, u32[]{:S(2)}) %collective-permute-start.5) | collective-permute-done | bytes 393248 | tf_op jit(solution)/shard_map/ppermute | solution.py:322
  30.9 3.4 %collective-permute-start.13 = (bf16[192,1024]{1,0:T(8,128)(2,1)S(1)}, bf16[192,1024]{1,0:T(8,128)(2,1)S(1)}, u32[]{:S(2)}, u32[]{:S(2)}) collective-permute-start(bf16[192,1024]{1,0:T(8,128)(2,1)S(1)} %collective-permute-done.5.cot_ref.refs_2_), channel_id=1, source_target_pairs={{0,2},{2,3},{3,1},{1,0},{4,6},{6,7},{7,5},{5,4},{8,10},{10,11},{11... | collective-permute-start | bytes 1179656 | tf_op jit(solution)/shard_map/ppermute | solution.py:322
  34.2 2.1 %shard_map.83 = (f32[192,1024]{1,0:T(8,128)S(1)}, bf16[192,1024]{1,0:T(8,128)(2,1)S(1)}) custom-call(s32[2]{0:T(128)S(1)} %pad_add_fusion.place_ref, bf16[192,1024]{1,0:T(8,128)(2,1)S(1)} %collective-permute-done.5.cot_ref.refs_2_, bf16[2048,1024]{1,0:T(8,128)(2,1)S(1)} %copy-done.1), custom_call_target="tpu_custom_call" | custom-call | flops 10000000 | bytes 1024 | tf_op jit(solution)/shard_map/pallas_call | solution.py:74
  36.4 1.7 %shard_map.79 = (bf16[768,1024]{1,0:T(8,128)(2,1)S(1)}, bf16[768,1024]{1,0:T(8,128)(2,1)S(1)}) custom-call(s32[2]{0:T(128)S(1)} %pad_add_fusion.place_ref, bf16[384,1024]{1,0:T(8,128)(2,1)S(1)} %shard_map.78.refs_0_, bf16[384,1024]{1,0:T(8,128)(2,1)S(1)} %collective-permute-done.3.refs_1_), custom_call_target="tpu_custom_call" | custom-call | flops 6000000000 | bytes 1024 | tf_op jit(solution)/shard_map/pallas_call | solution.py:74
  38.1 1.2 %shard_map.87.mine_ref.refs_4_ = bf16[192,1024]{1,0:T(8,128)(2,1)S(1)} custom-call(s32[2]{0:T(128)S(1)} %pad_add_fusion.place_ref, bf16[768,1024]{1,0:T(8,128)(2,1)S(1)} %get-tuple-element.38.pre_ref, f32[192,1024]{1,0:T(8,128)S(1)} %get-tuple-element.43.part_ref, bf16[192,1024]{1,0:T(8,128)(2,1)S(1)} %collective-permute-done.6.refs_0_, ...), custom_call_target="tpu_custom_call" | custom-call | flops 3000000000 | bytes 1024 | tf_op jit(solution)/shard_map/pallas_call | solution.py:74
  40.4 1.6 %collective-permute-start.8 = (bf16[192,1024]{1,0:T(8,128)(2,1)S(1)}, bf16[192,1024]{1,0:T(8,128)(2,1)S(1)}, u32[]{:S(2)}, u32[]{:S(2)}) collective-permute-start(bf16[192,1024]{1,0:T(8,128)(2,1)S(1)} %shard_map.84), channel_id=1, source_target_pairs={{0,8},{4,12},{8,0},{12,4},{1,9},{5,13},{9,1},{13,5},{2,10},{6,14},... | collective-permute-start | bytes 1179656 | tf_op jit(solution)/shard_map/ppermute | solution.py:306
  43.4 2.1 %shard_map.88 = bf16[192,1024]{1,0:T(8,128)(2,1)S(1)} custom-call(s32[2]{0:T(128)S(1)} %pad_add_fusion.place_ref, bf16[192,1024]{1,0:T(8,128)(2,1)S(1)} %shard_map.87.mine_ref.refs_4_, bf16[192,1024]{1,0:T(8,128)(2,1)S(1)} %collective-permute-done.11.theirs_ref.refs_8_, bf16[1024,2048]{1,0:T(8,128)(2,1)S(1)} %copy-done.2), custom_call_target="tpu_custom_call" | custom-call | flops 10000000 | bytes 1024 | tf_op jit(solution)/shard_map/pallas_call | solution.py:74
  45.5 2.5 %collective-permute-start.12 = (bf16[192,1024]{1,0:T(8,128)(2,1)S(1)}, bf16[192,1024]{1,0:T(8,128)(2,1)S(1)}, u32[]{:S(2)}, u32[]{:S(2)}) collective-permute-start(bf16[192,1024]{1,0:T(8,128)(2,1)S(1)} %shard_map.88), channel_id=1, source_target_pairs={{0,2},{2,3},{3,1},{1,0},{4,6},{6,7},{7,5},{5,4},{8,10},{10,11},{11... | collective-permute-start | bytes 1179656 | tf_op jit(solution)/shard_map/ppermute | solution.py:339
  48.0 2.1 %shard_map.90 = (f32[192,1024]{1,0:T(8,128)S(1)}, bf16[192,1024]{1,0:T(8,128)(2,1)S(1)}) custom-call(s32[2]{0:T(128)S(1)} %pad_add_fusion.place_ref, bf16[192,1024]{1,0:T(8,128)(2,1)S(1)} %collective-permute-done.13.cot_ref.refs_3_, bf16[2048,1024]{1,0:T(8,128)(2,1)S(1)} %copy-done.1), custom_call_target="tpu_custom_call" | custom-call | flops 10000000 | bytes 1024 | tf_op jit(solution)/shard_map/pallas_call | solution.py:74
  50.3 1.2 %collective-permute-done.8.refs_1_ = bf16[192,1024]{1,0:T(8,128)(2,1)S(1)} collective-permute-done((bf16[192,1024]{1,0:T(8,128)(2,1)S(1)}, bf16[192,1024]{1,0:T(8,128)(2,1)S(1)}, u32[]{:S(2)}, u32[]{:S(2)}) %collective-permute-start.8) | collective-permute-done | bytes 393248 | tf_op jit(solution)/shard_map/ppermute | solution.py:306
  51.5 1.2 %shard_map.85.mine_ref.refs_5_ = bf16[192,1024]{1,0:T(8,128)(2,1)S(1)} custom-call(s32[2]{0:T(128)S(1)} %pad_add_fusion.place_ref, bf16[768,1024]{1,0:T(8,128)(2,1)S(1)} %get-tuple-element.38.pre_ref, f32[192,1024]{1,0:T(8,128)S(1)} %get-tuple-element.46.part_ref, bf16[192,1024]{1,0:T(8,128)(2,1)S(1)} %collective-permute-done.7.refs_0_, ...), custom_call_target="tpu_custom_call" | custom-call | flops 8000000000 | bytes 1024 | tf_op jit(solution)/shard_map/pallas_call | solution.py:74
  53.4 1.6 %collective-permute-start.15 = (bf16[192,1024]{1,0:T(8,128)(2,1)S(1)}, bf16[192,1024]{1,0:T(8,128)(2,1)S(1)}, u32[]{:S(2)}, u32[]{:S(2)}) collective-permute-start(bf16[192,1024]{1,0:T(8,128)(2,1)S(1)} %shard_map.91), channel_id=1, source_target_pairs={{0,8},{4,12},{8,0},{12,4},{1,9},{5,13},{9,1},{13,5},{2,10},{6,14},... | collective-permute-start | bytes 1179656 | tf_op jit(solution)/shard_map/ppermute | solution.py:306
  55.6 2.1 %shard_map.86.part_ref = f32[192,1024]{1,0:T(8,128)S(1)} custom-call(s32[2]{0:T(128)S(1)} %pad_add_fusion.place_ref, bf16[192,1024]{1,0:T(8,128)(2,1)S(1)} %shard_map.85.mine_ref.refs_5_, bf16[192,1024]{1,0:T(8,128)(2,1)S(1)} %collective-permute-done.9.theirs_ref.refs_9_, bf16[1024,2048]{1,0:T(8,128)(2,1)S(1)} %copy-done.2), custom_call_target="tpu_custom_call" | custom-call | flops 10000000 | bytes 1024 | tf_op jit(solution)/shard_map/pallas_call | solution.py:74
  59.2 2.6 %collective-permute-done.12.refs_0_ = bf16[192,1024]{1,0:T(8,128)(2,1)S(1)} collective-permute-done((bf16[192,1024]{1,0:T(8,128)(2,1)S(1)}, bf16[192,1024]{1,0:T(8,128)(2,1)S(1)}, u32[]{:S(2)}, u32[]{:S(2)}) %collective-permute-start.12) | collective-permute-done | bytes 393248 | tf_op jit(solution)/shard_map/ppermute | solution.py:339
  62.4 1.8 %collective-permute-start.18 = (bf16[192,1024]{1,0:T(8,128)(2,1)S(1)}, bf16[192,1024]{1,0:T(8,128)(2,1)S(1)}, u32[]{:S(2)}, u32[]{:S(2)}) collective-permute-start(bf16[192,1024]{1,0:T(8,128)(2,1)S(1)} %shard_map.89), channel_id=1, source_target_pairs={{0,2},{2,3},{3,1},{1,0},{4,6},{6,7},{7,5},{5,4},{8,10},{10,11},{11... | collective-permute-start | bytes 1179656 | tf_op jit(solution)/shard_map/ppermute | solution.py:339
  64.2 1.2 %collective-permute-done.15.refs_1_ = bf16[192,1024]{1,0:T(8,128)(2,1)S(1)} collective-permute-done((bf16[192,1024]{1,0:T(8,128)(2,1)S(1)}, bf16[192,1024]{1,0:T(8,128)(2,1)S(1)}, u32[]{:S(2)}, u32[]{:S(2)}) %collective-permute-start.15) | collective-permute-done | bytes 393248 | tf_op jit(solution)/shard_map/ppermute | solution.py:306
  65.4 1.2 %shard_map.92.mine_ref.refs_6_ = bf16[192,1024]{1,0:T(8,128)(2,1)S(1)} custom-call(s32[2]{0:T(128)S(1)} %pad_add_fusion.place_ref, bf16[768,1024]{1,0:T(8,128)(2,1)S(1)} %get-tuple-element.38.pre_ref, f32[192,1024]{1,0:T(8,128)S(1)} %get-tuple-element.53.part_ref, bf16[192,1024]{1,0:T(8,128)(2,1)S(1)} %collective-permute-done.14.refs_0_, ...), custom_call_target="tpu_custom_call" | custom-call | flops 3000000000 | bytes 1024 | tf_op jit(solution)/shard_map/pallas_call | solution.py:74
  66.7 6.5 %shard_map.93 = f32[2048,1024]{1,0:T(8,128)} custom-call(s32[2]{0:T(128)S(1)} %pad_add_fusion.place_ref, bf16[768,1024]{1,0:T(8,128)(2,1)S(1)} %get-tuple-element.56.mine_ref, bf16[768,1024]{1,0:T(8,128)(2,1)S(1)} %collective-permute-done.16.theirs_ref, bf16[192,1024]{1,0:T(8,128)(2,1)S(1)} %copy-done.4, ...), custom_call_target="tpu_custom_call" | custom-call | flops 100000000 | bytes 1024 | tf_op jit(solution)/shard_map/pallas_call | solution.py:74
  74.9 2.1 %shard_map.94.part_ref = f32[192,1024]{1,0:T(8,128)S(1)} custom-call(s32[2]{0:T(128)S(1)} %pad_add_fusion.place_ref, bf16[192,1024]{1,0:T(8,128)(2,1)S(1)} %shard_map.92.mine_ref.refs_6_, bf16[192,1024]{1,0:T(8,128)(2,1)S(1)} %collective-permute-done.17.theirs_ref.refs_10_, bf16[1024,2048]{1,0:T(8,128)(2,1)S(1)} %copy-done.2), custom_call_target="tpu_custom_call" | custom-call | flops 10000000 | bytes 1024 | tf_op jit(solution)/shard_map/pallas_call | solution.py:74
  78.7 1.6 %collective-permute-start.23 = (bf16[192,1024]{1,0:T(8,128)(2,1)S(1)}, bf16[192,1024]{1,0:T(8,128)(2,1)S(1)}, u32[]{:S(2)}, u32[]{:S(2)}) collective-permute-start(bf16[192,1024]{1,0:T(8,128)(2,1)S(1)} %shard_map.95), channel_id=1, source_target_pairs={{0,2},{2,3},{3,1},{1,0},{4,6},{6,7},{7,5},{5,4},{8,10},{10,11},{11... | collective-permute-start | bytes 1179656 | tf_op jit(solution)/shard_map/ppermute | solution.py:352
  80.3 2.1 %shard_map.98.part_ref = f32[192,1024]{1,0:T(8,128)S(1)} custom-call(s32[2]{0:T(128)S(1)} %pad_add_fusion.place_ref, bf16[192,1024]{1,0:T(8,128)(2,1)S(1)} %shard_map.97.mine_ref.refs_3_, bf16[192,1024]{1,0:T(8,128)(2,1)S(1)} %collective-permute-done.22.theirs_ref.refs_7_, bf16[1024,2048]{1,0:T(8,128)(2,1)S(1)} %copy-done.2), custom_call_target="tpu_custom_call" | custom-call | flops 10000000 | bytes 1024 | tf_op jit(solution)/shard_map/pallas_call | solution.py:74
  82.4 6.6 %shard_map.99 = f32[1024,2048]{1,0:T(8,128)} custom-call(s32[2]{0:T(128)S(1)} %pad_add_fusion.place_ref, bf16[384,1024]{1,0:T(8,128)(2,1)S(1)} %shard_map.76.refs_0_, bf16[192,1024]{1,0:T(8,128)(2,1)S(1)} %shard_map.77.refs_1_, bf16[192,1024]{1,0:T(8,128)(2,1)S(1)} %collective-permute-done.19.refs_2_, bf16[192,1024]{1,0:T(8,128)(2,1)S(1)} %shard_map.97.mine_ref.refs_3_, ...), custom_call_target="tpu_custom_call" | custom-call | flops 3000000000 | bytes 1024 | tf_op jit(solution)/shard_map/pallas_call | solution.py:74
  89.2 1.4 %shard_map.100 = bf16[192,1024]{1,0:T(8,128)(2,1)} custom-call(s32[2]{0:T(128)S(1)} %pad_add_fusion.place_ref, f32[192,1024]{1,0:T(8,128)S(1)} %shard_map.98.part_ref, bf16[192,1024]{1,0:T(8,128)(2,1)S(1)} %collective-permute-done.23.refs_0_), custom_call_target="tpu_custom_call" | custom-call | flops 10000000 | bytes 1024 | tf_op jit(solution)/shard_map/pallas_call | solution.py:74
  (56 shorter events, 14.7 us)
Async XLA Ops:
  0.7 5.7 %collective-permute-start.2 = (bf16[192,2048]{1,0:T(8,128)(2,1)}, bf16[192,2048]{1,0:T(8,128)(2,1)S(1)}, u32[]{:S(2)}, u32[]{:S(2)}) collective-permute-start(bf16[192,2048]{1,0:T(8,128)(2,1)} %mine_ref), channel_id=1, source_target_pairs={{0,4},{4,0},{8,12},{12,8},{1,5},{5,1},{9,13},{13,9},{2,6},{6,2},{1... | collective-permute-start | bytes 2359304 | tf_op jit(solution)/shard_map/ppermute | solution.py:294
  1.2 13.9 %collective-permute-start.4 = (bf16[192,1024]{1,0:T(8,128)(2,1)}, bf16[192,1024]{1,0:T(8,128)(2,1)S(1)}, u32[]{:S(2)}, u32[]{:S(2)}) collective-permute-start(bf16[192,1024]{1,0:T(8,128)(2,1)} %refs_0_.2), channel_id=1, source_target_pairs={{0,2},{2,3},{3,1},{1,0},{4,6},{6,7},{7,5},{5,4},{8,10},{10,11},{11... | collective-permute-start | bytes 1179656 | tf_op jit(solution)/shard_map/ppermute | solution.py:322
  4.8 18.2 %collective-permute-start = (bf16[192,1024]{1,0:T(8,128)(2,1)}, bf16[192,1024]{1,0:T(8,128)(2,1)S(1)}, u32[]{:S(2)}, u32[]{:S(2)}) collective-permute-start(bf16[192,1024]{1,0:T(8,128)(2,1)} %refs_0_.1), channel_id=1, source_target_pairs={{0,2},{2,3},{3,1},{1,0},{4,6},{6,7},{7,5},{5,4},{8,10},{10,11},{11... | collective-permute-start | bytes 1179656 | tf_op jit(solution)/shard_map/ppermute | solution.py:319
  6.4 1.1 %copy-start.5 = (bf16[192,2048]{1,0:T(8,128)(2,1)S(1)}, bf16[192,2048]{1,0:T(8,128)(2,1)}, u32[]{:S(2)}) copy-start(bf16[192,2048]{1,0:T(8,128)(2,1)} %mine_ref) | copy-start | bytes 2359300
  8.1 28.3 %collective-permute-start.3 = (bf16[384,1024]{1,0:T(8,128)(2,1)S(1)}, bf16[384,1024]{1,0:T(8,128)(2,1)S(1)}, u32[]{:S(2)}, u32[]{:S(2)}) collective-permute-start(bf16[384,1024]{1,0:T(8,128)(2,1)S(1)} %shard_map.78.refs_0_), channel_id=1, source_target_pairs={{0,8},{4,12},{8,0},{12,4},{1,9},{5,13},{9,1},{13,5},{2,10},{6,14},... | collective-permute-start | bytes 2359304 | tf_op jit(solution)/shard_map/ppermute | solution.py:295
  9.7 2.2 %copy-start = (bf16[2048,1024]{1,0:T(8,128)(2,1)S(1)}, bf16[2048,1024]{1,0:T(8,128)(2,1)}, u32[]{:S(2)}) copy-start(bf16[2048,1024]{1,0:T(8,128)(2,1)} %down_ref.7) | copy-start | bytes 12582916
  11.9 1.0 %copy-start.3 = (bf16[192,1024]{1,0:T(8,128)(2,1)S(1)}, bf16[192,1024]{1,0:T(8,128)(2,1)}, u32[]{:S(2)}) copy-start(bf16[192,1024]{1,0:T(8,128)(2,1)} %refs_0_.2) | copy-start | bytes 1179652
  12.9 5.0 %copy-start.1 = (bf16[2048,1024]{1,0:T(8,128)(2,1)S(1)}, bf16[2048,1024]{1,0:T(8,128)(2,1)}, u32[]{:S(2)}) copy-start(bf16[2048,1024]{1,0:T(8,128)(2,1)} %down_ref.7) | copy-start | bytes 12582916
  12.9 10.1 %copy-start.6 = (bf16[192,1024]{1,0:T(8,128)(2,1)S(1)}, bf16[192,1024]{1,0:T(8,128)(2,1)}, u32[]{:S(2)}) copy-start(bf16[192,1024]{1,0:T(8,128)(2,1)} %refs_0_.1) | copy-start | bytes 1179652
  15.0 27.7 %collective-permute-start.20 = (bf16[192,1024]{1,0:T(8,128)(2,1)S(1)}, bf16[192,1024]{1,0:T(8,128)(2,1)S(1)}, u32[]{:S(2)}, u32[]{:S(2)}) collective-permute-start(bf16[192,1024]{1,0:T(8,128)(2,1)S(1)} %get-tuple-element.61), channel_id=1, source_target_pairs={{0,4},{4,0},{8,12},{12,8},{1,5},{5,1},{9,13},{13,9},{2,6},{6,2},{1... | collective-permute-start | bytes 1179656 | tf_op jit(solution)/shard_map/ppermute | solution.py:300
  15.0 15.8 %collective-permute-start.5 = (bf16[192,1024]{1,0:T(8,128)(2,1)S(1)}, bf16[192,1024]{1,0:T(8,128)(2,1)S(1)}, u32[]{:S(2)}, u32[]{:S(2)}) collective-permute-start(bf16[192,1024]{1,0:T(8,128)(2,1)S(1)} %collective-permute-done.4.cot_ref.refs_1_), channel_id=1, source_target_pairs={{0,2},{2,3},{3,1},{1,0},{4,6},{6,7},{7,5},{5,4},{8,10},{10,11},{11... | collective-permute-start | bytes 1179656 | tf_op jit(solution)/shard_map/ppermute | solution.py:322
  19.9 3.7 %collective-permute-start.6 = (bf16[192,1024]{1,0:T(8,128)(2,1)S(1)}, bf16[192,1024]{1,0:T(8,128)(2,1)S(1)}, u32[]{:S(2)}, u32[]{:S(2)}) collective-permute-start(bf16[192,1024]{1,0:T(8,128)(2,1)S(1)} %get-tuple-element.44), channel_id=1, source_target_pairs={{0,4},{4,0},{8,12},{12,8},{1,5},{5,1},{9,13},{13,9},{2,6},{6,2},{1... | collective-permute-start | bytes 1179656 | tf_op jit(solution)/shard_map/ppermute | solution.py:300
  24.2 13.8 %collective-permute-start.10 = (bf16[192,1024]{1,0:T(8,128)(2,1)S(1)}, bf16[192,1024]{1,0:T(8,128)(2,1)S(1)}, u32[]{:S(2)}, u32[]{:S(2)}) collective-permute-start(bf16[192,1024]{1,0:T(8,128)(2,1)S(1)} %shard_map.82), channel_id=1, source_target_pairs={{0,8},{4,12},{8,0},{12,4},{1,9},{5,13},{9,1},{13,5},{2,10},{6,14},... | collective-permute-start | bytes 1179656 | tf_op jit(solution)/shard_map/ppermute | solution.py:306
  30.9 12.4 %collective-permute-start.13 = (bf16[192,1024]{1,0:T(8,128)(2,1)S(1)}, bf16[192,1024]{1,0:T(8,128)(2,1)S(1)}, u32[]{:S(2)}, u32[]{:S(2)}) collective-permute-start(bf16[192,1024]{1,0:T(8,128)(2,1)S(1)} %collective-permute-done.5.cot_ref.refs_2_), channel_id=1, source_target_pairs={{0,2},{2,3},{3,1},{1,0},{4,6},{6,7},{7,5},{5,4},{8,10},{10,11},{11... | collective-permute-start | bytes 1179656 | tf_op jit(solution)/shard_map/ppermute | solution.py:322
  36.3 3.5 %collective-permute-start.7 = (bf16[192,1024]{1,0:T(8,128)(2,1)S(1)}, bf16[192,1024]{1,0:T(8,128)(2,1)S(1)}, u32[]{:S(2)}, u32[]{:S(2)}) collective-permute-start(bf16[192,1024]{1,0:T(8,128)(2,1)S(1)} %get-tuple-element.47), channel_id=1, source_target_pairs={{0,4},{4,0},{8,12},{12,8},{1,5},{5,1},{9,13},{13,9},{2,6},{6,2},{1... | collective-permute-start | bytes 1179656 | tf_op jit(solution)/shard_map/ppermute | solution.py:300
  38.1 5.3 %copy-start.2 = (bf16[1024,2048]{1,0:T(8,128)(2,1)S(1)}, bf16[1024,2048]{1,0:T(8,128)(2,1)}, u32[]{:S(2)}) copy-start(bf16[1024,2048]{1,0:T(8,128)(2,1)} %up_ref.7) | copy-start | bytes 12582916
  39.3 4.1 %collective-permute-start.11 = (bf16[192,1024]{1,0:T(8,128)(2,1)S(1)}, bf16[192,1024]{1,0:T(8,128)(2,1)S(1)}, u32[]{:S(2)}, u32[]{:S(2)}) collective-permute-start(bf16[192,1024]{1,0:T(8,128)(2,1)S(1)} %shard_map.87.mine_ref.refs_4_), channel_id=1, source_target_pairs={{0,4},{4,0},{8,12},{12,8},{1,5},{5,1},{9,13},{13,9},{2,6},{6,2},{1... | collective-permute-start | bytes 1179656 | tf_op jit(solution)/shard_map/ppermute | solution.py:312
  40.4 11.1 %collective-permute-start.8 = (bf16[192,1024]{1,0:T(8,128)(2,1)S(1)}, bf16[192,1024]{1,0:T(8,128)(2,1)S(1)}, u32[]{:S(2)}, u32[]{:S(2)}) collective-permute-start(bf16[192,1024]{1,0:T(8,128)(2,1)S(1)} %shard_map.84), channel_id=1, source_target_pairs={{0,8},{4,12},{8,0},{12,4},{1,9},{5,13},{9,1},{13,5},{2,10},{6,14},... | collective-permute-start | bytes 1179656 | tf_op jit(solution)/shard_map/ppermute | solution.py:306
  42.0 13.0 %collective-permute-start.1 = (bf16[192,1024]{1,0:T(8,128)(2,1)S(1)}, bf16[192,1024]{1,0:T(8,128)(2,1)S(1)}, u32[]{:S(2)}, u32[]{:S(2)}) collective-permute-start(bf16[192,1024]{1,0:T(8,128)(2,1)S(1)} %collective-permute-done.refs_1_), channel_id=1, source_target_pairs={{0,2},{2,3},{3,1},{1,0},{4,6},{6,7},{7,5},{5,4},{8,10},{10,11},{11... | collective-permute-start | bytes 1179656 | tf_op jit(solution)/shard_map/ppermute | solution.py:327
  43.3 23.4 %collective-permute-start.16 = (bf16[768,1024]{1,0:T(8,128)(2,1)S(1)}, bf16[768,1024]{1,0:T(8,128)(2,1)S(1)}, u32[]{:S(2)}, u32[]{:S(2)}) collective-permute-start(bf16[768,1024]{1,0:T(8,128)(2,1)S(1)} %get-tuple-element.56.mine_ref), channel_id=1, source_target_pairs={{0,4},{4,0},{8,12},{12,8},{1,5},{5,1},{9,13},{13,9},{2,6},{6,2},{1... | collective-permute-start | bytes 4718600 | tf_op jit(solution)/shard_map/ppermute | solution.py:330
  45.5 16.3 %collective-permute-start.12 = (bf16[192,1024]{1,0:T(8,128)(2,1)S(1)}, bf16[192,1024]{1,0:T(8,128)(2,1)S(1)}, u32[]{:S(2)}, u32[]{:S(2)}) collective-permute-start(bf16[192,1024]{1,0:T(8,128)(2,1)S(1)} %shard_map.88), channel_id=1, source_target_pairs={{0,2},{2,3},{3,1},{1,0},{4,6},{6,7},{7,5},{5,4},{8,10},{10,11},{11... | collective-permute-start | bytes 1179656 | tf_op jit(solution)/shard_map/ppermute | solution.py:339
  50.0 2.8 %collective-permute-start.14 = (bf16[192,1024]{1,0:T(8,128)(2,1)S(1)}, bf16[192,1024]{1,0:T(8,128)(2,1)S(1)}, u32[]{:S(2)}, u32[]{:S(2)}) collective-permute-start(bf16[192,1024]{1,0:T(8,128)(2,1)S(1)} %get-tuple-element.54), channel_id=1, source_target_pairs={{0,4},{4,0},{8,12},{12,8},{1,5},{5,1},{9,13},{13,9},{2,6},{6,2},{1... | collective-permute-start | bytes 1179656 | tf_op jit(solution)/shard_map/ppermute | solution.py:300
  52.7 2.8 %collective-permute-start.9 = (bf16[192,1024]{1,0:T(8,128)(2,1)S(1)}, bf16[192,1024]{1,0:T(8,128)(2,1)S(1)}, u32[]{:S(2)}, u32[]{:S(2)}) collective-permute-start(bf16[192,1024]{1,0:T(8,128)(2,1)S(1)} %shard_map.85.mine_ref.refs_5_), channel_id=1, source_target_pairs={{0,4},{4,0},{8,12},{12,8},{1,5},{5,1},{9,13},{13,9},{2,6},{6,2},{1... | collective-permute-start | bytes 1179656 | tf_op jit(solution)/shard_map/ppermute | solution.py:312
  53.4 12.0 %collective-permute-start.15 = (bf16[192,1024]{1,0:T(8,128)(2,1)S(1)}, bf16[192,1024]{1,0:T(8,128)(2,1)S(1)}, u32[]{:S(2)}, u32[]{:S(2)}) collective-permute-start(bf16[192,1024]{1,0:T(8,128)(2,1)S(1)} %shard_map.91), channel_id=1, source_target_pairs={{0,8},{4,12},{8,0},{12,4},{1,9},{5,13},{9,1},{13,5},{2,10},{6,14},... | collective-permute-start | bytes 1179656 | tf_op jit(solution)/shard_map/ppermute | solution.py:306
  57.7 15.5 %collective-permute-start.19 = (bf16[192,1024]{1,0:T(8,128)(2,1)S(1)}, bf16[192,1024]{1,0:T(8,128)(2,1)S(1)}, u32[]{:S(2)}, u32[]{:S(2)}) collective-permute-start(bf16[192,1024]{1,0:T(8,128)(2,1)S(1)} %collective-permute-done.1.refs_0_), channel_id=1, source_target_pairs={{0,2},{2,3},{3,1},{1,0},{4,6},{6,7},{7,5},{5,4},{8,10},{10,11},{11... | collective-permute-start | bytes 1179656 | tf_op jit(solution)/shard_map/ppermute | solution.py:342
  58.4 15.0 %collective-permute-start.21 = (bf16[192,1024]{1,0:T(8,128)(2,1)S(1)}, bf16[192,1024]{1,0:T(8,128)(2,1)S(1)}, u32[]{:S(2)}, u32[]{:S(2)}) collective-permute-start(bf16[192,1024]{1,0:T(8,128)(2,1)S(1)} %shard_map.96), channel_id=1, source_target_pairs={{0,8},{4,12},{8,0},{12,4},{1,9},{5,13},{9,1},{13,5},{2,10},{6,14},... | collective-permute-start | bytes 1179656 | tf_op jit(solution)/shard_map/ppermute | solution.py:306
  62.4 4.3 %copy-start.4 = (bf16[192,1024]{1,0:T(8,128)(2,1)S(1)}, bf16[192,1024]{1,0:T(8,128)(2,1)}, u32[]{:S(2)}) copy-start(bf16[192,1024]{1,0:T(8,128)(2,1)} %refs_0_.2) | copy-start | bytes 1179652
  62.4 15.6 %collective-permute-start.18 = (bf16[192,1024]{1,0:T(8,128)(2,1)S(1)}, bf16[192,1024]{1,0:T(8,128)(2,1)S(1)}, u32[]{:S(2)}, u32[]{:S(2)}) collective-permute-start(bf16[192,1024]{1,0:T(8,128)(2,1)S(1)} %shard_map.89), channel_id=1, source_target_pairs={{0,2},{2,3},{3,1},{1,0},{4,6},{6,7},{7,5},{5,4},{8,10},{10,11},{11... | collective-permute-start | bytes 1179656 | tf_op jit(solution)/shard_map/ppermute | solution.py:339
  66.6 8.3 %collective-permute-start.17 = (bf16[192,1024]{1,0:T(8,128)(2,1)S(1)}, bf16[192,1024]{1,0:T(8,128)(2,1)S(1)}, u32[]{:S(2)}, u32[]{:S(2)}) collective-permute-start(bf16[192,1024]{1,0:T(8,128)(2,1)S(1)} %shard_map.92.mine_ref.refs_6_), channel_id=1, source_target_pairs={{0,4},{4,0},{8,12},{12,8},{1,5},{5,1},{9,13},{13,9},{2,6},{6,2},{1... | collective-permute-start | bytes 1179656 | tf_op jit(solution)/shard_map/ppermute | solution.py:312
  74.6 5.7 %collective-permute-start.22 = (bf16[192,1024]{1,0:T(8,128)(2,1)S(1)}, bf16[192,1024]{1,0:T(8,128)(2,1)S(1)}, u32[]{:S(2)}, u32[]{:S(2)}) collective-permute-start(bf16[192,1024]{1,0:T(8,128)(2,1)S(1)} %shard_map.97.mine_ref.refs_3_), channel_id=1, source_target_pairs={{0,4},{4,0},{8,12},{12,8},{1,5},{5,1},{9,13},{13,9},{2,6},{6,2},{1... | collective-permute-start | bytes 1179656 | tf_op jit(solution)/shard_map/ppermute | solution.py:312
  78.7 10.6 %collective-permute-start.23 = (bf16[192,1024]{1,0:T(8,128)(2,1)S(1)}, bf16[192,1024]{1,0:T(8,128)(2,1)S(1)}, u32[]{:S(2)}, u32[]{:S(2)}) collective-permute-start(bf16[192,1024]{1,0:T(8,128)(2,1)S(1)} %shard_map.95), channel_id=1, source_target_pairs={{0,2},{2,3},{3,1},{1,0},{4,6},{6,7},{7,5},{5,4},{8,10},{10,11},{11... | collective-permute-start | bytes 1179656 | tf_op jit(solution)/shard_map/ppermute | solution.py:352
